TPU v7x, 32 devices: a whole 2x2x4 slice. The times are simulated.
32 devices in a mesh: parts: 2 (over x), dp: 16 (over z, y, core).
Axes of the slice: x: 2, y: 2, z: 4, core: 2. Of those that a mesh axis runs over, the one named last changes fastest.
Arguments:
- activations: bfloat16 [4096, 8192], P(('parts', 'dp')), parts along dimension 0, may hold values from -6 to 6
- out_grads: bfloat16 [4096, 28672], P(('parts', 'dp')), parts along dimension 0, may hold values from -6 to 6
- in_basis: bfloat16 [8192, 64], P('dp'), may hold values from -0.0625 to 0.0625
- out_basis: bfloat16 [28672, 64], P('dp'), may hold values from -0.03125 to 0.03125
- preconditioner: bfloat16 [4096, 4096], P('dp'), may hold values from -0.09375 to 0.09375
- queries: bfloat16 [128, 4096], P('dp'), may hold values from -6 to 6
Outputs:
- scores: float32 [4, 128], P('parts', 'dp'), parts along dimension 0
There are 2 independent parts, one for each index of `parts`. A program takes and returns all parts, laid end to end along the dimension named above; an argument that names none is the same for every part. Nothing has to cross between parts.
All inputs are finite; a program needn't handle non-finite values.
Results may differ from a plain program's by a relative error of at most 0.0061.
Values may be sent and summed in bfloat16 or wider, within the bound.
No kernel may reach another device: no remote copies, remote signals or barrier semaphores. Data moves between devices by JAX's collectives and lax.ppermute only.
A program may use at most 64 MiB of HBM per device.

v0:
```python
import math

import jax
import jax.numpy as jnp
from jax import lax
from jax.sharding import PartitionSpec as P

LEN = 1024


def project_rows(left, piece):
    return jnp.dot(left, piece, preferred_element_type=jnp.float32)


def local(activations, out_grads, in_basis, out_basis, preconditioner, queries):
    rows = activations.shape[0]
    rank = in_basis.shape[1]
    act_proj = project_rows(activations, lax.all_gather(in_basis, "dp", axis=0, tiled=True)).astype(
        jnp.bfloat16
    )
    grad_proj = project_rows(out_grads, lax.all_gather(out_basis, "dp", axis=0, tiled=True)).astype(
        jnp.bfloat16
    )
    partial_value = lax.dot_general(
        grad_proj, act_proj, (((0,), (0,)), ((), ())), preferred_element_type=jnp.float32
    )
    partial_value = partial_value.reshape(1, rank * rank) * (1.0 / math.sqrt(LEN))
    split = LEN // rows
    gathered = lax.all_gather(partial_value, "dp", axis=0, tiled=True)
    features = gathered.reshape(-1, split, rank * rank).sum(axis=1).astype(jnp.bfloat16)
    conditioned = lax.dot_general(
        features, preconditioner, (((1,), (1,)), ((), ())), preferred_element_type=jnp.float32
    ).astype(jnp.bfloat16)
    scores = lax.dot_general(
        lax.all_gather(conditioned, "dp", axis=1, tiled=True),
        queries,
        (((1,), (1,)), ((), ())),
        preferred_element_type=jnp.float32,
    )
    return scores * (1.0 / rank)


def solution(mesh):
    return jax.shard_map(
        local,
        mesh=mesh,
        in_specs=(
            P(("parts", "dp"), None),
            P(("parts", "dp"), None),
            P("dp", None),
            P("dp", None),
            P("dp", None),
            P("dp", None),
        ),
        out_specs=P("parts", "dp"),
        check_vma=False,
    )
```

profile of v0, /device:TPU:0, one launch (start us, length us, event | category | flops | bytes accessed | tf_op | source)
XLA Modules:
  0.0 152.5 jit_solution(11675698065579341991)
XLA Ops:
  6.5 0.0 copy-start
  6.5 0.0 all-gather.6.cloned.1.call-start
  6.5 0.7 all-gather.6.cloned.1.call-update
  7.3 0.0 all-gather.4.cloned.1.call-start
  7.3 0.7 all-gather.4.cloned.1.call-update
  8.0 41.0 %all-gather.6.cloned.1.call-done = bf16[8192,64]{0,1:T(8,128)(2,1)} async-done(((bf16[512,64]{0,1:T(8,128)(2,1)}), bf16[8192,64]{0,1:T(8,128)(2,1)}) %all-gather.6.cloned.1.call-update) | async-done | bytes 1048592 | tf_op jit(solution)/shard_map/all_gather | solution.py:18
  49.1 0.0 copy-done
  49.1 1.9 %convolution_convert_fusion = bf16[128,64]{1,0:T(8,128)(2,1)S(1)} fusion(bf16[128,8192]{1,0:T(8,128)(2,1)S(1)} %copy-done, bf16[8192,64]{0,1:T(8,128)(2,1)} %all-gather.6.cloned.1.call-done), kind=kOutput, calls=%fused_computation | convolution fusion | flops 134225920 | bytes 3162112 | tf_op jit(solution)/shard_map/dot_general | solution.py:12
  51.0 0.0 copy-start.1
  51.0 47.5 %all-gather.4.cloned.1.call-done = bf16[28672,64]{0,1:T(8,128)(2,1)} async-done(((bf16[1792,64]{0,1:T(8,128)(2,1)}), bf16[28672,64]{0,1:T(8,128)(2,1)}) %all-gather.4.cloned.1.call-update) | async-done | bytes 3670032 | tf_op jit(solution)/shard_map/all_gather | solution.py:21
  98.5 6.3 %fusion.1 = f32[64,64]{1,0:T(8,128)S(1)} fusion(bf16[128,64]{1,0:T(8,128)(2,1)S(1)} %convolution_convert_fusion, bf16[128,28672]{1,0:T(8,128)(2,1)} %param.7, bf16[28672,64]{0,1:T(8,128)(2,1)} %all-gather.4.cloned.1.call-done), kind=kOutput, calls=%fused_computation.3 | convolution fusion | flops 470822912 | bytes 11042816 | tf_op jit(solution)/shard_map/dot_general | solution.py:24
  104.9 0.1 reshape.19
  105.0 20.1 %all-gather = f32[16,1,4096]{2,1,0:T(1,128)S(1)} all-gather(f32[1,1,4096]{2,1,0:T(1,128)S(1)} %reshape.19), channel_id=1, replica_groups=mesh['parts'=2,'dp'=16] {'dp'}, dimensions={0}, use_global_device_ids=true | all-gather | bytes 278528 | tf_op jit(solution)/shard_map/all_gather | solution.py:29
  125.0 0.2 bitcast_reduce_fusion
  125.3 2.2 %convolution_convert_fusion.2 = bf16[2,256]{1,0:T(2,128)(2,1)S(1)} fusion(bf16[256,4096]{1,0:T(8,128)(2,1)} %param.10, bf16[2,4096]{1,0:T(2,128)(2,1)S(1)} %bitcast_reduce_fusion), kind=kOutput, calls=%fused_computation.4 | convolution fusion | flops 4194816 | bytes 2114560 | tf_op jit(solution)/shard_map/dot_general | solution.py:31
  127.5 17.4 %all_gather.15 = bf16[2,4096]{1,0:T(2,128)(2,1)S(1)} all-gather(bf16[2,256]{1,0:T(2,128)(2,1)S(1)} %convolution_convert_fusion.2), channel_id=1, replica_groups=mesh['parts'=2,'dp'=16] {'dp'}, dimensions={1}, use_global_device_ids=true | all-gather | bytes 17408 | tf_op jit(solution)/shard_map/all_gather | solution.py:35
  144.9 0.0 copy-done.1
  144.9 0.7 convolution_multiply_fusion
Async XLA Ops:
  6.5 42.5 %copy-start = (bf16[128,8192]{1,0:T(8,128)(2,1)S(1)}, bf16[128,8192]{1,0:T(8,128)(2,1)}, u32[]{:S(2)}) copy-start(bf16[128,8192]{1,0:T(8,128)(2,1)} %param.6) | copy-start | bytes 6291460
  6.5 42.5 %all-gather.6.cloned.1.call-start = ((), (), s32[]{:S(2)}) async-start(), calls=%async_computation.1 | async-start | bytes 1114112 | tf_op jit(solution)/shard_map/all_gather | solution.py:18
  7.3 91.3 %all-gather.4.cloned.1.call-start = ((), (), s32[]{:S(2)}) async-start(), calls=%async_computation | async-start | bytes 3899392 | tf_op jit(solution)/shard_map/all_gather | solution.py:21
  51.0 94.0 %copy-start.1 = (bf16[8,4096]{1,0:T(8,128)(2,1)S(1)}, bf16[8,4096]{1,0:T(8,128)(2,1)}, u32[]{:S(2)}) copy-start(bf16[8,4096]{1,0:T(8,128)(2,1)} %param.11) | copy-start | bytes 196612
Sparse Core Ops, SparseCore 0:
  9.5 39.4 all-gather.5
  51.2 47.2 all-gather.3
where the time goes:
time: 153 us; the launch traced here: 152 us
  waiting for transfers between devices  90 us (59%)
  blocking collectives  37.5 us (25%)
  between operations  13.4 us (9%)
  matrix products  11.2 us (7%)
    all_gather x1, waiting for transfers between devices, local(): lax.all_gather(out_basis, 'dp', axis=0, tiled=True)  47.5 us
    all_gather x1, waiting for transfers between devices, local(): lax.all_gather(in_basis, 'dp', axis=0, tiled=True)  41 us
    all_gather x1, blocking collectives, local(): gathered = lax.all_gather(partial_value, 'dp', axis=0, tiled=True)  20.1 us
    all_gather x1, blocking collectives, local(): lax.all_gather(conditioned, 'dp', axis=1, tiled=True)  17.4 us
    dot_general x1, matrix products, local(): lax.dot_general(grad_proj, act_proj, (((0,), (0,)), ((), ())), preferred_...  6.33 us
  transfers between devices with their start and end apart: 2, of which 2 were waited for; matrix products, arithmetic and copies ran while one was open for 1% of the time, Pallas kernels for 0%

commit v1 on v0

v1 whole, which is shorter than its diff:
```python
import functools
import math

import jax
import jax.numpy as jnp
from jax import lax
from jax.experimental import pallas as pl
from jax.experimental.pallas import tpu as pltpu
from jax.sharding import PartitionSpec as P

LEN = 1024
NT = (((1,), (1,)), ((), ()))
TN = (((0,), (0,)), ((), ()))


def dot(a, b, dims):
    return lax.dot_general(a, b, dims, preferred_element_type=jnp.float32)


def factors(n):
    rest = n // 2
    inner = 1
    while inner * inner * 4 <= rest:
        inner *= 2
    return rest // inner, inner, 2


def shift(x, sizes, steps):
    pairs = []
    for a in range(sizes[0]):
        for b in range(sizes[1]):
            for c in range(sizes[2]):
                to = [(i + s) % m for i, s, m in zip((a, b, c), steps, sizes)]
                pairs.append(
                    ((a * sizes[1] + b) * sizes[2] + c, (to[0] * sizes[1] + to[1]) * sizes[2] + to[2])
                )
    return lax.ppermute(x, "dp", pairs)


def owner(sizes, steps):
    me = lax.axis_index("dp")
    c = lax.rem(me, sizes[2])
    b = lax.rem(me // sizes[2], sizes[1])
    a = me // (sizes[1] * sizes[2])
    a, b, c = (lax.rem(i + m - s, m) for i, s, m in zip((a, b, c), steps, sizes))
    return (a * sizes[1] + b) * sizes[2] + c


def project_kernel(sizes, steps, width, carry, *refs):
    count = len(steps)
    act, grad = refs[:2]
    pieces = refs[2 : 2 + count]
    refs = refs[2 + count :]
    if carry:
        a_in, g_in = refs[:2]
        refs = refs[2:]
    a_out, g_out, a_buf, g_buf, sems = refs
    g_width = pieces[0].shape[1] - width
    copies = []
    for i, step in enumerate(steps):
        index = owner(sizes, step)
        a_copy = pltpu.make_async_copy(
            act.at[:, pl.ds(pl.multiple_of(index * width, 128), width)], a_buf.at[i], sems.at[0, i]
        )
        g_copy = pltpu.make_async_copy(
            grad.at[:, pl.ds(pl.multiple_of(index * g_width, 128), g_width)], g_buf.at[i], sems.at[1, i]
        )
        a_copy.start()
        g_copy.start()
        copies.append((a_copy, g_copy))
    if carry:
        a_sum, g_sum = a_in[...], g_in[...]
    else:
        a_sum = g_sum = jnp.zeros(a_out.shape, jnp.float32)
    for i, (a_copy, g_copy) in enumerate(copies):
        a_copy.wait()
        a_sum += dot(a_buf[i], pieces[i][:, :width], NT)
        g_copy.wait()
        g_sum += dot(g_buf[i], pieces[i][:, width:], NT)
    a_out[...] = a_sum
    g_out[...] = g_sum


def project(act, grad, pieces, steps, sizes, width, rank, carry=None):
    rows = act.shape[0]
    count = len(pieces)
    g_width = pieces[0].shape[1] - width
    vmem = pl.BlockSpec(memory_space=pltpu.VMEM)
    hbm = pl.BlockSpec(memory_space=pl.ANY)
    total = jax.ShapeDtypeStruct((rows, rank), jnp.float32)
    carried = () if carry is None else carry
    return pl.pallas_call(
        functools.partial(project_kernel, sizes, steps, width, carry is not None),
        out_shape=(total, total),
        in_specs=[hbm, hbm] + [vmem] * (count + len(carried)),
        out_specs=(vmem, vmem),
        scratch_shapes=[
            pltpu.VMEM((count, rows, width), act.dtype),
            pltpu.VMEM((count, rows, g_width), act.dtype),
            pltpu.SemaphoreType.DMA((2, count)),
        ],
        compiler_params=pltpu.CompilerParams(vmem_limit_bytes=32 * 2**20),
        cost_estimate=pl.CostEstimate(
            flops=2 * count * rows * rank * (width + g_width),
            bytes_accessed=count * (rows + rank) * (width + g_width) * 2,
            transcendentals=0,
        ),
    )(act, grad, *pieces, *carried)


def projections(activations, out_grads, in_basis, out_basis, sizes):
    width, rank = in_basis.shape
    run = functools.partial(project, activations, out_grads, sizes=sizes, width=width, rank=rank)
    own = jnp.concatenate([in_basis.T, out_basis.T], axis=1)
    level = [((a, 0, 0), own if a == 0 else shift(own, sizes, (a, 0, 0))) for a in range(sizes[0])]
    level2 = [((s[0], b, 0), shift(x, sizes, (0, b, 0))) for b in range(1, sizes[1]) for s, x in level]
    level3 = [((s[0], s[1], 1), shift(x, sizes, (0, 0, 1))) for s, x in level + level2]
    carry = None
    for group in (level, level2, level3):
        steps, pieces = zip(*group)
        carry = run(pieces=pieces, steps=steps, carry=carry)
    return carry


def spread(x, sizes, one_level):
    return [
        (s, x if s == (0, 0, 0) else shift(x, sizes, s))
        for s in one_level
    ]


def local(activations, out_grads, in_basis, out_basis, preconditioner, queries):
    rows = activations.shape[0]
    width, rank = in_basis.shape
    n = activations.shape[1] // width
    sizes = factors(n)
    split = LEN // rows
    act_sum, grad_sum = projections(activations, out_grads, in_basis, out_basis, sizes)
    raw = dot(grad_sum.astype(jnp.bfloat16), act_sum.astype(jnp.bfloat16), TN)
    raw = raw.reshape(1, rank * rank) * (1.0 / math.sqrt(LEN))
    group = sizes[1] * sizes[2]
    inner = [(0, b, c) for b in range(sizes[1]) for c in range(sizes[2])]
    outer = [(a, 0, 0) for a in range(sizes[0])]
    summed = sum(x for _, x in spread(raw, sizes, inner))
    blocks = spread(summed, sizes, outer)
    sequences = n // split
    rows_of = lax.broadcasted_iota(jnp.int32, (sequences, 1), 0)
    features = sum(
        jnp.where(owner(sizes, s) // split == rows_of, x, 0.0) for s, x in blocks
    ).astype(jnp.bfloat16)
    conditioned = dot(features, preconditioner, NT).astype(jnp.bfloat16)
    out = preconditioner.shape[0]
    steps = [(a, b, c) for a, _, _ in outer for _, b, c in inner]
    terms = [
        dot(x, lax.dynamic_slice_in_dim(queries, owner(sizes, s) * out, out, axis=1), NT)
        for s, x in spread(conditioned, sizes, steps)
    ]
    return sum(terms) * (1.0 / rank)


def local_gathered(activations, out_grads, in_basis, out_basis, preconditioner, queries):
    rows = activations.shape[0]
    rank = in_basis.shape[1]
    act_proj = jnp.dot(
        activations,
        lax.all_gather(in_basis, "dp", axis=0, tiled=True),
        preferred_element_type=jnp.float32,
    ).astype(jnp.bfloat16)
    grad_proj = jnp.dot(
        out_grads,
        lax.all_gather(out_basis, "dp", axis=0, tiled=True),
        preferred_element_type=jnp.float32,
    ).astype(jnp.bfloat16)
    raw = dot(grad_proj, act_proj, TN).reshape(1, rank * rank) * (1.0 / math.sqrt(LEN))
    gathered = lax.all_gather(raw, "dp", axis=0, tiled=True)
    features = gathered.reshape(-1, LEN // rows, rank * rank).sum(axis=1).astype(jnp.bfloat16)
    conditioned = dot(features, preconditioner, NT).astype(jnp.bfloat16)
    scores = dot(lax.all_gather(conditioned, "dp", axis=1, tiled=True), queries, NT)
    return scores * (1.0 / rank)


def solution(mesh):
    n = mesh.shape["dp"]

    def body(activations, out_grads, in_basis, out_basis, preconditioner, queries):
        aligned = in_basis.shape[0] % 128 == 0 and out_basis.shape[0] % 128 == 0
        regular = aligned and (LEN // activations.shape[0]) % (factors(n)[1] * 2) == 0
        form = local if regular else local_gathered
        return form(activations, out_grads, in_basis, out_basis, preconditioner, queries)

    return jax.shard_map(
        body,
        mesh=mesh,
        in_specs=(
            P(("parts", "dp"), None),
            P(("parts", "dp"), None),
            P("dp", None),
            P("dp", None),
            P("dp", None),
            P("dp", None),
        ),
        out_specs=P("parts", "dp"),
        check_vma=False,
    )
```

time: 153 us -> 102 us (0.67)
  waiting for transfers between devices: 90 us -> 28.9 us
  starting transfers between devices: 0.04 us -> 49.4 us
  blocking collectives: 37.5 us -> 0 us
  between operations: 13.4 us -> 0.14 us
  Pallas kernels: 0 us -> 11 us
  local copies, waits for them, and re-layouts: 0.11 us -> 8.1 us
  matrix products: 11.2 us -> 3.28 us
    all_gather x2 -> x0, waiting for transfers between devices: 88.6 us -> none  [the longest x1 47.5 us: local(): lax.all_gather(out_basis, 'dp', axis=0, tiled=True)]
    ppermute x0 -> x36, starting transfers between devices: none -> 49.4 us  [shift(): return lax.ppermute(x, 'dp', pairs)]
    all_gather x2 -> x0, blocking collectives: 37.5 us -> none  [the longest x1 20.1 us: local(): gathered = lax.all_gather(partial_value, 'dp', axis=0, tiled=True)]
    ppermute x0 -> x36, waiting for transfers between devices: none -> 28.9 us  [shift(): return lax.ppermute(x, 'dp', pairs)]
    pallas_call x0 -> x3, Pallas kernels: none -> 11 us  [project(): pl.pallas_call(functools.partial(project_kernel, sizes, steps, width, car...]
    dot_general x4 -> x18, matrix products: 11.2 us -> 3.28 us  [dot(): return lax.dot_general(a, b, dims, preferred_element_type=jnp.float32)]
    unnamed x5 -> x16, local copies, waits for them, and re-layouts: 0.11 us -> 8.02 us
  transfers between devices with their start and end apart: 2 -> 36, of which waited for: 2 -> 11; matrix products, arithmetic and copies ran while one was open for 1% -> 2% of each run, Pallas kernels for 0% -> 6%
where the time goes in v1:
time: 102 us
  starting transfers between devices  49.4 us (48%)
  waiting for transfers between devices  28.9 us (28%)
  Pallas kernels  11 us (11%)
  local copies, waits for them, and re-layouts  8.1 us (8%)
  matrix products  3.28 us (3%)
  other arithmetic  1.16 us (1%)
    ppermute x36, starting transfers between devices, shift(): return lax.ppermute(x, 'dp', pairs)  49.4 us
    ppermute x36, waiting for transfers between devices, shift(): return lax.ppermute(x, 'dp', pairs)  28.9 us
    pallas_call x3, Pallas kernels, project(): pl.pallas_call(functools.partial(project_kernel, sizes, steps, width, car...  11 us
    unnamed x16, local copies, waits for them, and re-layouts  8.02 us
    dot_general x18, matrix products, dot(): return lax.dot_general(a, b, dims, preferred_element_type=jnp.float32)  3.28 us
  transfers between devices with their start and end apart: 36, of which 11 were waited for; matrix products, arithmetic and copies ran while one was open for 2% of the time, Pallas kernels for 6%

profile of v1, /device:TPU:0, one launch (start us, length us, event | category | flops | bytes accessed | tf_op | source)
XLA Modules:
  0.0 102.0 jit_solution(18316121021089145231)
XLA Ops:
  1.1 4.1 %collective-permute-start.3 = (bf16[64,2304]{1,0:T(8,128)(2,1)S(1)}, bf16[64,2304]{1,0:T(8,128)(2,1)S(1)}, u32[]{:S(2)}, u32[]{:S(2)}) collective-permute-start(bf16[64,2304]{1,0:T(8,128)(2,1)S(1)} %pad_maximum_fusion.refs_2_), channel_id=1, source_target_pairs={{0,8},{1,9},{2,10},{3,11},{4,12},{5,13},{6,14},{7,15},{8,0},{9,1},... | collective-permute-start | bytes 884744 | tf_op jit(solution)/shard_map/ppermute | solution.py:37
  7.3 1.5 %collective-permute-start.7 = (bf16[64,2304]{1,0:T(8,128)(2,1)S(1)}, bf16[64,2304]{1,0:T(8,128)(2,1)}, u32[]{:S(2)}, u32[]{:S(2)}) collective-permute-start(bf16[64,2304]{1,0:T(8,128)(2,1)S(1)} %pad_maximum_fusion.refs_2_), channel_id=1, source_target_pairs={{0,2},{1,3},{2,0},{3,1},{4,6},{5,7},{6,4},{7,5},{8,10},{9,11},{10,... | collective-permute-start | bytes 884744 | tf_op jit(solution)/shard_map/ppermute | solution.py:37
  8.8 11.5 %collective-permute-done.3.refs_4_ = bf16[64,2304]{1,0:T(8,128)(2,1)S(1)} collective-permute-done((bf16[64,2304]{1,0:T(8,128)(2,1)S(1)}, bf16[64,2304]{1,0:T(8,128)(2,1)S(1)}, u32[]{:S(2)}, u32[]{:S(2)}) %collective-permute-start.3) | collective-permute-done | bytes 294944 | tf_op jit(solution)/shard_map/ppermute | solution.py:37
  20.3 7.3 %collective-permute-start.11 = (bf16[64,2304]{1,0:T(8,128)(2,1)S(1)}, bf16[64,2304]{1,0:T(8,128)(2,1)}, u32[]{:S(2)}, u32[]{:S(2)}) collective-permute-start(bf16[64,2304]{1,0:T(8,128)(2,1)S(1)} %collective-permute-done.3.refs_4_), channel_id=1, source_target_pairs={{0,2},{1,3},{2,0},{3,1},{4,6},{5,7},{6,4},{7,5},{8,10},{9,11},{10,... | collective-permute-start | bytes 884744 | tf_op jit(solution)/shard_map/ppermute | solution.py:37
  27.7 2.0 %collective-permute-start.9 = (bf16[64,2304]{1,0:T(8,128)(2,1)S(1)}, bf16[64,2304]{1,0:T(8,128)(2,1)}, u32[]{:S(2)}, u32[]{:S(2)}) collective-permute-start(bf16[64,2304]{1,0:T(8,128)(2,1)S(1)} %collective-permute-done.1.refs_3_), channel_id=1, source_target_pairs={{0,2},{1,3},{2,0},{3,1},{4,6},{5,7},{6,4},{7,5},{8,10},{9,11},{10,... | collective-permute-start | bytes 884744 | tf_op jit(solution)/shard_map/ppermute | solution.py:37
  31.6 2.5 %collective-permute-done.11.refs_4_ = bf16[64,2304]{1,0:T(8,128)(2,1)} collective-permute-done((bf16[64,2304]{1,0:T(8,128)(2,1)S(1)}, bf16[64,2304]{1,0:T(8,128)(2,1)}, u32[]{:S(2)}, u32[]{:S(2)}) %collective-permute-start.11) | collective-permute-done | bytes 294944 | tf_op jit(solution)/shard_map/ppermute | solution.py:37
  34.1 3.2 %collective-permute-done.13.refs_5_ = bf16[64,2304]{1,0:T(8,128)(2,1)} collective-permute-done((bf16[64,2304]{1,0:T(8,128)(2,1)}, bf16[64,2304]{1,0:T(8,128)(2,1)}, u32[]{:S(2)}, u32[]{:S(2)}) %collective-permute-start.13) | collective-permute-done | bytes 294944 | tf_op jit(solution)/shard_map/ppermute | solution.py:37
  37.2 3.2 %collective-permute-done.9.refs_3_ = bf16[64,2304]{1,0:T(8,128)(2,1)} collective-permute-done((bf16[64,2304]{1,0:T(8,128)(2,1)S(1)}, bf16[64,2304]{1,0:T(8,128)(2,1)}, u32[]{:S(2)}, u32[]{:S(2)}) %collective-permute-start.9) | collective-permute-done | bytes 294944 | tf_op jit(solution)/shard_map/ppermute | solution.py:37
  41.0 3.1 %copy-done.1 = bf16[128,28672]{1,0:T(8,128)(2,1)S(1)} copy-done((bf16[128,28672]{1,0:T(8,128)(2,1)S(1)}, bf16[128,28672]{1,0:T(8,128)(2,1)}, u32[]{:S(2)}) %copy-start.1) | copy-done | bytes 7340056
  44.0 1.6 %copy-done.2 = bf16[128,8192]{1,0:T(8,128)(2,1)S(1)} copy-done((bf16[128,8192]{1,0:T(8,128)(2,1)S(1)}, bf16[128,8192]{1,0:T(8,128)(2,1)}, u32[]{:S(2)}) %copy-start.2) | copy-done | bytes 2097176
  47.6 2.9 %shard_map.64 = (f32[128,64]{1,0:T(8,128)S(1)}, f32[128,64]{1,0:T(8,128)S(1)}) custom-call(bf16[128,8192]{1,0:T(8,128)(2,1)S(1)} %copy-done.2, bf16[128,28672]{1,0:T(8,128)(2,1)S(1)} %copy-done.1, bf16[64,2304]{1,0:T(8,128)(2,1)S(1)} %pad_maximum_fusion.refs_2_, bf16[64,2304]{1,0:T(8,128)(2,1)S(1)} %copy-done.6, bf16[64,2304]{1,0:T(8,128)(2,1)S(1)} %copy-done.4, ...), custom_call_target="tpu_custom_call" | custom-call | flops 150994944 | bytes 3538944 | tf_op jit(solution)/shard_map/pallas_call | solution.py:92
  50.5 3.1 %shard_map.65 = (f32[128,64]{1,0:T(8,128)S(1)}, f32[128,64]{1,0:T(8,128)S(1)}) custom-call(bf16[128,8192]{1,0:T(8,128)(2,1)S(1)} %copy-done.2, bf16[128,28672]{1,0:T(8,128)(2,1)S(1)} %copy-done.1, bf16[64,2304]{1,0:T(8,128)(2,1)} %collective-permute-done.7.refs_2_, bf16[64,2304]{1,0:T(8,128)(2,1)} %collective-permute-done.9.refs_3_, ...), custom_call_target="tpu_custom_call" | custom-call | flops 150994944 | bytes 3538944 | tf_op jit(solution)/shard_map/pallas_call | solution.py:92
  53.7 5.0 %shard_map.66 = (f32[128,64]{1,0:T(8,128)S(1)}, f32[128,64]{1,0:T(8,128)S(1)}) custom-call(bf16[128,8192]{1,0:T(8,128)(2,1)S(1)} %copy-done.2, bf16[128,28672]{1,0:T(8,128)(2,1)S(1)} %copy-done.1, bf16[64,2304]{1,0:T(8,128)(2,1)S(1)} %collective-permute-done.refs_2_, bf16[64,2304]{1,0:T(8,128)(2,1)S(1)} %collective-permute-done.2.refs_3_, ...), custom_call_target="tpu_custom_call" | custom-call | flops 301989888 | bytes 7077888 | tf_op jit(solution)/shard_map/pallas_call | solution.py:92
  59.5 1.5 %collective-permute-start.16 = (f32[1,4096]{1,0:T(1,128)S(1)}, f32[1,4096]{1,0:T(1,128)S(1)}, u32[]{:S(2)}, u32[]{:S(2)}) collective-permute-start(f32[1,4096]{1,0:T(1,128)S(1)} %mul.136), channel_id=1, source_target_pairs={{0,2},{1,3},{2,0},{3,1},{4,6},{5,7},{6,4},{7,5},{8,10},{9,11},{10,... | collective-permute-start | bytes 49160 | tf_op jit(solution)/shard_map/ppermute | solution.py:37
  61.0 2.2 %collective-permute-done.16 = f32[1,4096]{1,0:T(1,128)S(1)} collective-permute-done((f32[1,4096]{1,0:T(1,128)S(1)}, f32[1,4096]{1,0:T(1,128)S(1)}, u32[]{:S(2)}, u32[]{:S(2)}) %collective-permute-start.16) | collective-permute-done | bytes 16416 | tf_op jit(solution)/shard_map/ppermute | solution.py:37
  64.3 7.0 %collective-permute-start.18 = (f32[1,4096]{1,0:T(1,128)S(1)}, f32[1,4096]{1,0:T(1,128)S(1)}, u32[]{:S(2)}, u32[]{:S(2)}) collective-permute-start(f32[1,4096]{1,0:T(1,128)S(1)} %add_add_fusion), channel_id=1, source_target_pairs={{0,4},{1,5},{2,6},{3,7},{4,8},{5,9},{6,10},{7,11},{8,12},{9,13},{1... | collective-permute-start | bytes 49160 | tf_op jit(solution)/shard_map/ppermute | solution.py:37
  71.3 3.4 %collective-permute-start.19 = (f32[1,4096]{1,0:T(1,128)S(1)}, f32[1,4096]{1,0:T(1,128)S(1)}, u32[]{:S(2)}, u32[]{:S(2)}) collective-permute-start(f32[1,4096]{1,0:T(1,128)S(1)} %add_add_fusion), channel_id=1, source_target_pairs={{0,8},{1,9},{2,10},{3,11},{4,12},{5,13},{6,14},{7,15},{8,0},{9,1},... | collective-permute-start | bytes 49160 | tf_op jit(solution)/shard_map/ppermute | solution.py:37
  76.4 2.0 %collective-permute-done.20 = f32[1,4096]{1,0:T(1,128)S(1)} collective-permute-done((f32[1,4096]{1,0:T(1,128)S(1)}, f32[1,4096]{1,0:T(1,128)S(1)}, u32[]{:S(2)}, u32[]{:S(2)}) %collective-permute-start.20) | collective-permute-done | bytes 16416 | tf_op jit(solution)/shard_map/ppermute | solution.py:37
  80.6 2.6 %collective-permute-start.26 = (bf16[2,256]{1,0:T(2,128)(2,1)S(1)}, bf16[2,256]{1,0:T(2,128)(2,1)S(1)}, u32[]{:S(2)}, u32[]{:S(2)}) collective-permute-start(bf16[2,256]{1,0:T(2,128)(2,1)S(1)} %convolution_convert_fusion), channel_id=1, source_target_pairs={{0,6},{1,7},{2,4},{3,5},{4,10},{5,11},{6,8},{7,9},{8,14},{9,15},{1... | collective-permute-start | bytes 3080 | tf_op jit(solution)/shard_map/ppermute | solution.py:37
  83.3 1.9 %collective-permute-start.27 = (bf16[2,256]{1,0:T(2,128)(2,1)S(1)}, bf16[2,256]{1,0:T(2,128)(2,1)S(1)}, u32[]{:S(2)}, u32[]{:S(2)}) collective-permute-start(bf16[2,256]{1,0:T(2,128)(2,1)S(1)} %convolution_convert_fusion), channel_id=1, source_target_pairs={{0,7},{1,6},{2,5},{3,4},{4,11},{5,10},{6,9},{7,8},{8,15},{9,14},{1... | collective-permute-start | bytes 3080 | tf_op jit(solution)/shard_map/ppermute | solution.py:37
  87.8 1.8 %collective-permute-start.30 = (bf16[2,256]{1,0:T(2,128)(2,1)S(1)}, bf16[2,256]{1,0:T(2,128)(2,1)S(1)}, u32[]{:S(2)}, u32[]{:S(2)}) collective-permute-start(bf16[2,256]{1,0:T(2,128)(2,1)S(1)} %convolution_convert_fusion), channel_id=1, source_target_pairs={{0,10},{1,11},{2,8},{3,9},{4,14},{5,15},{6,12},{7,13},{8,2},{9,3},... | collective-permute-start | bytes 3080 | tf_op jit(solution)/shard_map/ppermute | solution.py:37
  89.8 2.1 %collective-permute-start.31 = (bf16[2,256]{1,0:T(2,128)(2,1)S(1)}, bf16[2,256]{1,0:T(2,128)(2,1)S(1)}, u32[]{:S(2)}, u32[]{:S(2)}) collective-permute-start(bf16[2,256]{1,0:T(2,128)(2,1)S(1)} %convolution_convert_fusion), channel_id=1, source_target_pairs={{0,11},{1,10},{2,9},{3,8},{4,15},{5,14},{6,13},{7,12},{8,3},{9,2},... | collective-permute-start | bytes 3080 | tf_op jit(solution)/shard_map/ppermute | solution.py:37
  92.0 2.0 %collective-permute-start.32 = (bf16[2,256]{1,0:T(2,128)(2,1)S(1)}, bf16[2,256]{1,0:T(2,128)(2,1)S(1)}, u32[]{:S(2)}, u32[]{:S(2)}) collective-permute-start(bf16[2,256]{1,0:T(2,128)(2,1)S(1)} %convolution_convert_fusion), channel_id=1, source_target_pairs={{0,12},{1,13},{2,14},{3,15},{4,0},{5,1},{6,2},{7,3},{8,4},{9,5},{1... | collective-permute-start | bytes 3080 | tf_op jit(solution)/shard_map/ppermute | solution.py:37
  94.2 1.9 %collective-permute-start.34 = (bf16[2,256]{1,0:T(2,128)(2,1)S(1)}, bf16[2,256]{1,0:T(2,128)(2,1)S(1)}, u32[]{:S(2)}, u32[]{:S(2)}) collective-permute-start(bf16[2,256]{1,0:T(2,128)(2,1)S(1)} %convolution_convert_fusion), channel_id=1, source_target_pairs={{0,14},{1,15},{2,12},{3,13},{4,2},{5,3},{6,0},{7,1},{8,6},{9,7},{1... | collective-permute-start | bytes 3080 | tf_op jit(solution)/shard_map/ppermute | solution.py:37
  (90 shorter events, 22.6 us)
Async XLA Ops:
  1.1 19.2 %collective-permute-start.3 = (bf16[64,2304]{1,0:T(8,128)(2,1)S(1)}, bf16[64,2304]{1,0:T(8,128)(2,1)S(1)}, u32[]{:S(2)}, u32[]{:S(2)}) collective-permute-start(bf16[64,2304]{1,0:T(8,128)(2,1)S(1)} %pad_maximum_fusion.refs_2_), channel_id=1, source_target_pairs={{0,8},{1,9},{2,10},{3,11},{4,12},{5,13},{6,14},{7,15},{8,0},{9,1},... | collective-permute-start | bytes 884744 | tf_op jit(solution)/shard_map/ppermute | solution.py:37
  5.2 22.4 %collective-permute-start.5 = (bf16[64,2304]{1,0:T(8,128)(2,1)S(1)}, bf16[64,2304]{1,0:T(8,128)(2,1)}, u32[]{:S(2)}, u32[]{:S(2)}) collective-permute-start(bf16[64,2304]{1,0:T(8,128)(2,1)S(1)} %pad_maximum_fusion.refs_2_), channel_id=1, source_target_pairs={{0,12},{1,13},{2,14},{3,15},{4,0},{5,1},{6,2},{7,3},{8,4},{9,5},{1... | collective-permute-start | bytes 884744 | tf_op jit(solution)/shard_map/ppermute | solution.py:37
  6.6 21.1 %collective-permute-start.1 = (bf16[64,2304]{1,0:T(8,128)(2,1)S(1)}, bf16[64,2304]{1,0:T(8,128)(2,1)S(1)}, u32[]{:S(2)}, u32[]{:S(2)}) collective-permute-start(bf16[64,2304]{1,0:T(8,128)(2,1)S(1)} %pad_maximum_fusion.refs_2_), channel_id=1, source_target_pairs={{0,4},{1,5},{2,6},{3,7},{4,8},{5,9},{6,10},{7,11},{8,12},{9,13},{1... | collective-permute-start | bytes 884744 | tf_op jit(solution)/shard_map/ppermute | solution.py:37
  7.3 22.4 %collective-permute-start.7 = (bf16[64,2304]{1,0:T(8,128)(2,1)S(1)}, bf16[64,2304]{1,0:T(8,128)(2,1)}, u32[]{:S(2)}, u32[]{:S(2)}) collective-permute-start(bf16[64,2304]{1,0:T(8,128)(2,1)S(1)} %pad_maximum_fusion.refs_2_), channel_id=1, source_target_pairs={{0,2},{1,3},{2,0},{3,1},{4,6},{5,7},{6,4},{7,5},{8,10},{9,11},{10,... | collective-permute-start | bytes 884744 | tf_op jit(solution)/shard_map/ppermute | solution.py:37
  8.8 21.6 %collective-permute-start = (bf16[64,2304]{1,0:T(8,128)(2,1)S(1)}, bf16[64,2304]{1,0:T(8,128)(2,1)S(1)}, u32[]{:S(2)}, u32[]{:S(2)}) collective-permute-start(bf16[64,2304]{1,0:T(8,128)(2,1)S(1)} %pad_maximum_fusion.refs_2_), channel_id=1, source_target_pairs={{0,1},{1,0},{2,3},{3,2},{4,5},{5,4},{6,7},{7,6},{8,9},{9,8},{10,11... | collective-permute-start | bytes 884744 | tf_op jit(solution)/shard_map/ppermute | solution.py:37
  20.3 13.8 %collective-permute-start.11 = (bf16[64,2304]{1,0:T(8,128)(2,1)S(1)}, bf16[64,2304]{1,0:T(8,128)(2,1)}, u32[]{:S(2)}, u32[]{:S(2)}) collective-permute-start(bf16[64,2304]{1,0:T(8,128)(2,1)S(1)} %collective-permute-done.3.refs_4_), channel_id=1, source_target_pairs={{0,2},{1,3},{2,0},{3,1},{4,6},{5,7},{6,4},{7,5},{8,10},{9,11},{10,... | collective-permute-start | bytes 884744 | tf_op jit(solution)/shard_map/ppermute | solution.py:37
  27.6 9.6 %collective-permute-start.13 = (bf16[64,2304]{1,0:T(8,128)(2,1)}, bf16[64,2304]{1,0:T(8,128)(2,1)}, u32[]{:S(2)}, u32[]{:S(2)}) collective-permute-start(bf16[64,2304]{1,0:T(8,128)(2,1)} %collective-permute-done.5.refs_5_), channel_id=1, source_target_pairs={{0,2},{1,3},{2,0},{3,1},{4,6},{5,7},{6,4},{7,5},{8,10},{9,11},{10,... | collective-permute-start | bytes 884744 | tf_op jit(solution)/shard_map/ppermute | solution.py:37
  27.7 12.7 %collective-permute-start.9 = (bf16[64,2304]{1,0:T(8,128)(2,1)S(1)}, bf16[64,2304]{1,0:T(8,128)(2,1)}, u32[]{:S(2)}, u32[]{:S(2)}) collective-permute-start(bf16[64,2304]{1,0:T(8,128)(2,1)S(1)} %collective-permute-done.1.refs_3_), channel_id=1, source_target_pairs={{0,2},{1,3},{2,0},{3,1},{4,6},{5,7},{6,4},{7,5},{8,10},{9,11},{10,... | collective-permute-start | bytes 884744 | tf_op jit(solution)/shard_map/ppermute | solution.py:37
  29.7 10.7 %collective-permute-start.2 = (bf16[64,2304]{1,0:T(8,128)(2,1)S(1)}, bf16[64,2304]{1,0:T(8,128)(2,1)S(1)}, u32[]{:S(2)}, u32[]{:S(2)}) collective-permute-start(bf16[64,2304]{1,0:T(8,128)(2,1)S(1)} %collective-permute-done.1.refs_3_), channel_id=1, source_target_pairs={{0,1},{1,0},{2,3},{3,2},{4,5},{5,4},{6,7},{7,6},{8,9},{9,8},{10,11... | collective-permute-start | bytes 884744 | tf_op jit(solution)/shard_map/ppermute | solution.py:37
  30.4 10.5 %collective-permute-start.4 = (bf16[64,2304]{1,0:T(8,128)(2,1)S(1)}, bf16[64,2304]{1,0:T(8,128)(2,1)S(1)}, u32[]{:S(2)}, u32[]{:S(2)}) collective-permute-start(bf16[64,2304]{1,0:T(8,128)(2,1)S(1)} %collective-permute-done.3.refs_4_), channel_id=1, source_target_pairs={{0,1},{1,0},{2,3},{3,2},{4,5},{5,4},{6,7},{7,6},{8,9},{9,8},{10,11... | collective-permute-start | bytes 884744 | tf_op jit(solution)/shard_map/ppermute | solution.py:37
  34.1 19.6 %collective-permute-start.6 = (bf16[64,2304]{1,0:T(8,128)(2,1)}, bf16[64,2304]{1,0:T(8,128)(2,1)}, u32[]{:S(2)}, u32[]{:S(2)}) collective-permute-start(bf16[64,2304]{1,0:T(8,128)(2,1)} %collective-permute-done.5.refs_5_), channel_id=1, source_target_pairs={{0,1},{1,0},{2,3},{3,2},{4,5},{5,4},{6,7},{7,6},{8,9},{9,8},{10,11... | collective-permute-start | bytes 884744 | tf_op jit(solution)/shard_map/ppermute | solution.py:37
  37.2 16.4 %collective-permute-start.8 = (bf16[64,2304]{1,0:T(8,128)(2,1)}, bf16[64,2304]{1,0:T(8,128)(2,1)}, u32[]{:S(2)}, u32[]{:S(2)}) collective-permute-start(bf16[64,2304]{1,0:T(8,128)(2,1)} %collective-permute-done.7.refs_2_), channel_id=1, source_target_pairs={{0,1},{1,0},{2,3},{3,2},{4,5},{5,4},{6,7},{7,6},{8,9},{9,8},{10,11... | collective-permute-start | bytes 884744 | tf_op jit(solution)/shard_map/ppermute | solution.py:37
  40.4 13.3 %collective-permute-start.10 = (bf16[64,2304]{1,0:T(8,128)(2,1)}, bf16[64,2304]{1,0:T(8,128)(2,1)}, u32[]{:S(2)}, u32[]{:S(2)}) collective-permute-start(bf16[64,2304]{1,0:T(8,128)(2,1)} %collective-permute-done.9.refs_3_), channel_id=1, source_target_pairs={{0,1},{1,0},{2,3},{3,2},{4,5},{5,4},{6,7},{7,6},{8,9},{9,8},{10,11... | collective-permute-start | bytes 884744 | tf_op jit(solution)/shard_map/ppermute | solution.py:37
  40.4 13.3 %collective-permute-start.12 = (bf16[64,2304]{1,0:T(8,128)(2,1)}, bf16[64,2304]{1,0:T(8,128)(2,1)}, u32[]{:S(2)}, u32[]{:S(2)}) collective-permute-start(bf16[64,2304]{1,0:T(8,128)(2,1)} %collective-permute-done.11.refs_4_), channel_id=1, source_target_pairs={{0,1},{1,0},{2,3},{3,2},{4,5},{5,4},{6,7},{7,6},{8,9},{9,8},{10,11... | collective-permute-start | bytes 884744 | tf_op jit(solution)/shard_map/ppermute | solution.py:37
  40.9 12.8 %collective-permute-start.14 = (bf16[64,2304]{1,0:T(8,128)(2,1)}, bf16[64,2304]{1,0:T(8,128)(2,1)}, u32[]{:S(2)}, u32[]{:S(2)}) collective-permute-start(bf16[64,2304]{1,0:T(8,128)(2,1)} %collective-permute-done.13.refs_5_), channel_id=1, source_target_pairs={{0,1},{1,0},{2,3},{3,2},{4,5},{5,4},{6,7},{7,6},{8,9},{9,8},{10,11... | collective-permute-start | bytes 884744 | tf_op jit(solution)/shard_map/ppermute | solution.py:37
  64.3 11.5 %collective-permute-start.18 = (f32[1,4096]{1,0:T(1,128)S(1)}, f32[1,4096]{1,0:T(1,128)S(1)}, u32[]{:S(2)}, u32[]{:S(2)}) collective-permute-start(f32[1,4096]{1,0:T(1,128)S(1)} %add_add_fusion), channel_id=1, source_target_pairs={{0,4},{1,5},{2,6},{3,7},{4,8},{5,9},{6,10},{7,11},{8,12},{9,13},{1... | collective-permute-start | bytes 49160 | tf_op jit(solution)/shard_map/ppermute | solution.py:37
  79.8 8.0 %collective-permute-start.25 = (bf16[2,256]{1,0:T(2,128)(2,1)S(1)}, bf16[2,256]{1,0:T(2,128)(2,1)S(1)}, u32[]{:S(2)}, u32[]{:S(2)}) collective-permute-start(bf16[2,256]{1,0:T(2,128)(2,1)S(1)} %convolution_convert_fusion), channel_id=1, source_target_pairs={{0,5},{1,4},{2,7},{3,6},{4,9},{5,8},{6,11},{7,10},{8,13},{9,12},{1... | collective-permute-start | bytes 3080 | tf_op jit(solution)/shard_map/ppermute | solution.py:37
  80.6 9.2 %collective-permute-start.26 = (bf16[2,256]{1,0:T(2,128)(2,1)S(1)}, bf16[2,256]{1,0:T(2,128)(2,1)S(1)}, u32[]{:S(2)}, u32[]{:S(2)}) collective-permute-start(bf16[2,256]{1,0:T(2,128)(2,1)S(1)} %convolution_convert_fusion), channel_id=1, source_target_pairs={{0,6},{1,7},{2,4},{3,5},{4,10},{5,11},{6,8},{7,9},{8,14},{9,15},{1... | collective-permute-start | bytes 3080 | tf_op jit(solution)/shard_map/ppermute | solution.py:37
  83.3 8.7 %collective-permute-start.27 = (bf16[2,256]{1,0:T(2,128)(2,1)S(1)}, bf16[2,256]{1,0:T(2,128)(2,1)S(1)}, u32[]{:S(2)}, u32[]{:S(2)}) collective-permute-start(bf16[2,256]{1,0:T(2,128)(2,1)S(1)} %convolution_convert_fusion), channel_id=1, source_target_pairs={{0,7},{1,6},{2,5},{3,4},{4,11},{5,10},{6,9},{7,8},{8,15},{9,14},{1... | collective-permute-start | bytes 3080 | tf_op jit(solution)/shard_map/ppermute | solution.py:37
  85.3 8.8 %collective-permute-start.28 = (bf16[2,256]{1,0:T(2,128)(2,1)S(1)}, bf16[2,256]{1,0:T(2,128)(2,1)S(1)}, u32[]{:S(2)}, u32[]{:S(2)}) collective-permute-start(bf16[2,256]{1,0:T(2,128)(2,1)S(1)} %convolution_convert_fusion), channel_id=1, source_target_pairs={{0,8},{1,9},{2,10},{3,11},{4,12},{5,13},{6,14},{7,15},{8,0},{9,1},... | collective-permute-start | bytes 3080 | tf_op jit(solution)/shard_map/ppermute | solution.py:37
  86.3 7.9 %collective-permute-start.29 = (bf16[2,256]{1,0:T(2,128)(2,1)S(1)}, bf16[2,256]{1,0:T(2,128)(2,1)S(1)}, u32[]{:S(2)}, u32[]{:S(2)}) collective-permute-start(bf16[2,256]{1,0:T(2,128)(2,1)S(1)} %convolution_convert_fusion), channel_id=1, source_target_pairs={{0,9},{1,8},{2,11},{3,10},{4,13},{5,12},{6,15},{7,14},{8,1},{9,0},... | collective-permute-start | bytes 3080 | tf_op jit(solution)/shard_map/ppermute | solution.py:37
  87.8 8.4 %collective-permute-start.30 = (bf16[2,256]{1,0:T(2,128)(2,1)S(1)}, bf16[2,256]{1,0:T(2,128)(2,1)S(1)}, u32[]{:S(2)}, u32[]{:S(2)}) collective-permute-start(bf16[2,256]{1,0:T(2,128)(2,1)S(1)} %convolution_convert_fusion), channel_id=1, source_target_pairs={{0,10},{1,11},{2,8},{3,9},{4,14},{5,15},{6,12},{7,13},{8,2},{9,3},... | collective-permute-start | bytes 3080 | tf_op jit(solution)/shard_map/ppermute | solution.py:37
  89.8 8.0 %collective-permute-start.31 = (bf16[2,256]{1,0:T(2,128)(2,1)S(1)}, bf16[2,256]{1,0:T(2,128)(2,1)S(1)}, u32[]{:S(2)}, u32[]{:S(2)}) collective-permute-start(bf16[2,256]{1,0:T(2,128)(2,1)S(1)} %convolution_convert_fusion), channel_id=1, source_target_pairs={{0,11},{1,10},{2,9},{3,8},{4,15},{5,14},{6,13},{7,12},{8,3},{9,2},... | collective-permute-start | bytes 3080 | tf_op jit(solution)/shard_map/ppermute | solution.py:37
  92.0 7.4 %collective-permute-start.32 = (bf16[2,256]{1,0:T(2,128)(2,1)S(1)}, bf16[2,256]{1,0:T(2,128)(2,1)S(1)}, u32[]{:S(2)}, u32[]{:S(2)}) collective-permute-start(bf16[2,256]{1,0:T(2,128)(2,1)S(1)} %convolution_convert_fusion), channel_id=1, source_target_pairs={{0,12},{1,13},{2,14},{3,15},{4,0},{5,1},{6,2},{7,3},{8,4},{9,5},{1... | collective-permute-start | bytes 3080 | tf_op jit(solution)/shard_map/ppermute | solution.py:37
  (20 other events, 164.1 us)

commit v2 on v0

v2 whole, which is shorter than its diff:
```python
import functools
import math

import jax
import jax.numpy as jnp
from jax import lax
from jax.experimental import pallas as pl
from jax.experimental.pallas import tpu as pltpu
from jax.sharding import PartitionSpec as P

LEN = 1024
NT = (((1,), (1,)), ((), ()))
TN = (((0,), (0,)), ((), ()))


def dot(a, b, dims):
    return lax.dot_general(a, b, dims, preferred_element_type=jnp.float32)


def chip_at(place, chips):
    half = chips // 2
    return jnp.where(place < half, 2 * place, 2 * (chips - 1 - place) + 1)


def block_at(offset, chips):
    me = lax.axis_index("dp")
    chip = me >> 1
    z, y = chip >> 1, chip & 1
    place = jnp.where(y == 0, z, chips - 1 - z)
    return chip_at((place - offset) & (chips - 1), chips) * 2 + (me & 1)


def ring(x, step, chips):
    half = chips // 2
    chip = [2 * p if p < half else 2 * (chips - 1 - p) + 1 for p in range(chips)]
    pairs = [
        (chip[p] * 2 + c, chip[(p + step) % chips] * 2 + c) for p in range(chips) for c in range(2)
    ]
    return lax.ppermute(x, "dp", pairs)


def swap(x, bit, n):
    return lax.ppermute(x, "dp", [(i, i ^ bit) for i in range(n)])


def project_kernel(chips, offsets, halves, carry, *refs):
    tokens, refs = refs[:4], refs[4:]
    blocks = []
    for half in halves:
        blocks.append(refs[: 1 + half])
        refs = refs[1 + half :]
    if carry:
        carried, refs = refs[0], refs[1:]
    out, a_buf, g_buf, b_buf, sems = refs
    rows = tokens[0].shape[0]
    a_width, g_width = a_buf.shape[2], g_buf.shape[2]
    rank = b_buf.shape[1]
    copies = []
    for i, (offset, parts) in enumerate(zip(offsets, blocks)):
        index = block_at(offset, chips)
        mine = []
        for core in range(2):
            for which, (buf, width) in enumerate(((a_buf, a_width), (g_buf, g_width))):
                mine.append(
                    pltpu.make_async_copy(
                        tokens[2 * which + core].at[:, pl.ds(pl.multiple_of(index * width, 128), width)],
                        buf.at[i, pl.ds(core * rows, rows)],
                        sems.at[i, 2 * which + core],
                    )
                )
        for k, part in enumerate(parts):
            size = rank // len(parts)
            mine.append(
                pltpu.make_async_copy(part, b_buf.at[i, pl.ds(k * size, size)], sems.at[i, 4 + k])
            )
        for copy in mine:
            copy.start()
        copies.append(mine)
    if carry:
        a_sum, g_sum = carried[:, :rank], carried[:, rank:]
    else:
        a_sum = g_sum = jnp.zeros((2 * rows, rank), jnp.float32)
    for i, mine in enumerate(copies):
        for copy in mine:
            copy.wait()
        a_sum += dot(a_buf[i], b_buf[i, :, :a_width], NT)
        g_sum += dot(g_buf[i], b_buf[i, :, a_width:], NT)
    out[:, :rank] = a_sum
    out[:, rank:] = g_sum


def project(tokens, blocks, offsets, chips, a_width, carry=None):
    rows = tokens[0].shape[0]
    count = len(offsets)
    blocks = [b if isinstance(b, tuple) else (b,) for b in blocks]
    halves = [len(b) - 1 for b in blocks]
    flat = [x for b in blocks for x in b]
    width = flat[0].shape[1]
    rank = sum(x.shape[0] for x in blocks[0])
    vmem = pl.BlockSpec(memory_space=pltpu.VMEM)
    anywhere = pl.BlockSpec(memory_space=pl.ANY)
    carried = () if carry is None else (carry,)
    return pl.pallas_call(
        functools.partial(project_kernel, chips, offsets, halves, carry is not None),
        out_shape=jax.ShapeDtypeStruct((2 * rows, 2 * rank), jnp.float32),
        in_specs=[anywhere] * (4 + len(flat)) + [vmem] * len(carried),
        out_specs=vmem,
        scratch_shapes=[
            pltpu.VMEM((count, 2 * rows, a_width), jnp.bfloat16),
            pltpu.VMEM((count, 2 * rows, width - a_width), jnp.bfloat16),
            pltpu.VMEM((count, rank, width), jnp.bfloat16),
            pltpu.SemaphoreType.DMA((count, 6)),
        ],
        compiler_params=pltpu.CompilerParams(vmem_limit_bytes=24 * 2**20),
        cost_estimate=pl.CostEstimate(
            flops=4 * count * rows * rank * width,
            bytes_accessed=count * (2 * rows + rank) * width * 2,
            transcendentals=0,
        ),
    )(*tokens, *flat, *carried)


def ordered_kernel(count, x, out):
    me = lax.axis_index("dp")
    width = x.shape[1] // count
    for j in range(count):
        out[:, j * width : (j + 1) * width] = x[:, pl.ds(pl.multiple_of((me ^ j) * width, 128), width)]


def local(activations, out_grads, in_basis, out_basis, preconditioner, queries):
    rows = activations.shape[0]
    a_width, rank = in_basis.shape
    n = activations.shape[1] // a_width
    chips = n // 2
    split = LEN // rows
    me = lax.axis_index("dp")

    own = jnp.concatenate([in_basis.T, out_basis.T], axis=1)
    up, down = [own], [own]
    for _ in range(chips // 2 - 1):
        up.append(ring(up[-1], 1, chips))
        down.append(ring(down[-1], -1, chips))
    tokens = (activations, swap(activations, 1, n), out_grads, swap(out_grads, 1, n))
    preconditioner_2 = swap(preconditioner, 1, n)

    run = functools.partial(project, tokens, chips=chips, a_width=a_width)
    early, offsets = [own], [0]
    for i in range(1, chips // 2 - 1):
        early += [up[i], down[i]]
        offsets += [i, -i]
    last = chips // 2 - 1
    total = run(early, offsets)
    total, up_last, down_last = lax.optimization_barrier((total, up[last], down[last]))
    half = rank // 2
    far = (ring(up_last[:half], 1, chips), ring(down_last[half:], -1, chips))
    total = run([up_last, down_last], [last, -last], carry=total)
    total = run([far], [chips // 2], carry=total)
    theirs = swap(total, 1, n)
    total = (total + jnp.concatenate([theirs[rows:], theirs[:rows]], axis=0)).astype(jnp.bfloat16)

    raw = dot(total[:, rank:], total[:, :rank], TN)
    raw = raw.reshape(1, rank * rank) * (1.0 / math.sqrt(LEN))
    bit = 2
    while bit < n:
        other = swap(raw, bit, n)
        if bit < split:
            raw = raw + other
        else:
            raw = jnp.where(
                (me & bit) == 0,
                jnp.concatenate([raw, other], axis=0),
                jnp.concatenate([other, raw], axis=0),
            )
        bit *= 2
    features = raw.astype(jnp.bfloat16)

    conditioned = jnp.concatenate(
        [dot(features, m, NT) for m in (preconditioner, preconditioner_2)], axis=1
    ).astype(jnp.bfloat16)
    bit = 2
    while bit < n:
        conditioned = jnp.concatenate([conditioned, swap(conditioned, bit, n)], axis=1)
        bit *= 2
    arranged = pl.pallas_call(
        functools.partial(ordered_kernel, n),
        out_shape=jax.ShapeDtypeStruct(queries.shape, queries.dtype),
    )(queries)
    return dot(conditioned, arranged, NT) * (1.0 / rank)


def local_gathered(activations, out_grads, in_basis, out_basis, preconditioner, queries):
    rows = activations.shape[0]
    rank = in_basis.shape[1]
    act_proj = jnp.dot(
        activations,
        lax.all_gather(in_basis, "dp", axis=0, tiled=True),
        preferred_element_type=jnp.float32,
    ).astype(jnp.bfloat16)
    grad_proj = jnp.dot(
        out_grads,
        lax.all_gather(out_basis, "dp", axis=0, tiled=True),
        preferred_element_type=jnp.float32,
    ).astype(jnp.bfloat16)
    raw = dot(grad_proj, act_proj, TN).reshape(1, rank * rank) * (1.0 / math.sqrt(LEN))
    gathered = lax.all_gather(raw, "dp", axis=0, tiled=True)
    features = gathered.reshape(-1, LEN // rows, rank * rank).sum(axis=1).astype(jnp.bfloat16)
    conditioned = dot(features, preconditioner, NT).astype(jnp.bfloat16)
    scores = dot(lax.all_gather(conditioned, "dp", axis=1, tiled=True), queries, NT)
    return scores * (1.0 / rank)


def power_of_two(x):
    return x > 0 and x & (x - 1) == 0


def solution(mesh):
    n = mesh.shape["dp"]

    def body(activations, out_grads, in_basis, out_basis, preconditioner, queries):
        aligned = all(x.shape[0] % 128 == 0 for x in (in_basis, out_basis, preconditioner))
        split = LEN // activations.shape[0]
        regular = aligned and n >= 8 and power_of_two(n) and power_of_two(split) and 4 <= split <= n
        form = local if regular else local_gathered
        return form(activations, out_grads, in_basis, out_basis, preconditioner, queries)

    return jax.shard_map(
        body,
        mesh=mesh,
        in_specs=(
            P(("parts", "dp"), None),
            P(("parts", "dp"), None),
            P("dp", None),
            P("dp", None),
            P("dp", None),
            P("dp", None),
        ),
        out_specs=P("parts", "dp"),
        check_vma=False,
    )
```

time: 153 us -> 69.9 us (0.46)
  waiting for transfers between devices: 90 us -> 30.2 us
  blocking collectives: 37.5 us -> 0 us
  starting transfers between devices: 0.04 us -> 19.7 us
  between operations: 13.4 us -> 0.14 us
  Pallas kernels: 0 us -> 8.95 us
  matrix products: 11.2 us -> 4.71 us
  local copies, waits for them, and re-layouts: 0.11 us -> 4.83 us
    all_gather x2 -> x0, waiting for transfers between devices: 88.6 us -> none  [the longest x1 47.5 us: local(): lax.all_gather(out_basis, 'dp', axis=0, tiled=True)]
    all_gather x2 -> x0, blocking collectives: 37.5 us -> none  [the longest x1 20.1 us: local(): gathered = lax.all_gather(partial_value, 'dp', axis=0, tiled=True)]
    ppermute x0 -> x18, waiting for transfers between devices: none -> 30.2 us  [the longest x8 15.9 us: ring(): return lax.ppermute(x, 'dp', pairs)]
    ppermute x0 -> x18, starting transfers between devices: none -> 19.7 us  [the longest x10 10.4 us: swap(): return lax.ppermute(x, 'dp', [(i, i ^ bit) for i in range(n)])]
    pallas_call x0 -> x4, Pallas kernels: none -> 8.95 us  [the longest x3 7.48 us: project(): pl.pallas_call(functools.partial(project_kernel, chips, offsets, halves,...]
    dot_general x4, matrix products: 11.2 us -> 4.71 us  [dot(): return lax.dot_general(a, b, dims, preferred_element_type=jnp.float32)]
    unnamed x5 -> x8, local copies, waits for them, and re-layouts: 0.11 us -> 4.7 us
  transfers between devices with their start and end apart: 2 -> 18, of which waited for: 2 -> 11; matrix products, arithmetic and copies ran while one was open for 1% -> 3% of each run, Pallas kernels for 0% -> 13%
where the time goes in v2:
time: 69.9 us; the launch traced here: 69.5 us
  waiting for transfers between devices  30.2 us (43%)
  starting transfers between devices  19.7 us (28%)
  Pallas kernels  8.95 us (13%)
  local copies, waits for them, and re-layouts  4.83 us (7%)
  matrix products  4.71 us (7%)
  other arithmetic  1.05 us (2%)
    ppermute x8, waiting for transfers between devices, ring(): return lax.ppermute(x, 'dp', pairs)  15.9 us
    ppermute x10, waiting for transfers between devices, swap(): return lax.ppermute(x, 'dp', [(i, i ^ bit) for i in range(n)])  14.3 us
    ppermute x10, starting transfers between devices, swap(): return lax.ppermute(x, 'dp', [(i, i ^ bit) for i in range(n)])  10.4 us
    ppermute x8, starting transfers between devices, ring(): return lax.ppermute(x, 'dp', pairs)  9.27 us
    pallas_call x3, Pallas kernels, project(): pl.pallas_call(functools.partial(project_kernel, chips, offsets, halves,...  7.48 us
    dot_general x4, matrix products, dot(): return lax.dot_general(a, b, dims, preferred_element_type=jnp.float32)  4.71 us
    unnamed x8, local copies, waits for them, and re-layouts  4.7 us
    pallas_call x1, Pallas kernels, local(): pl.pallas_call(functools.partial(ordered_kernel, n), out_shape=jax.ShapeD...  1.47 us
  transfers between devices with their start and end apart: 18, of which 11 were waited for; matrix products, arithmetic and copies ran while one was open for 3% of the time, Pallas kernels for 13%

profile of v2, /device:TPU:0, one launch (start us, length us, event | category | flops | bytes accessed | tf_op | source)
XLA Modules:
  0.0 69.5 jit_solution(11601848832553716649)
XLA Ops:
  1.5 3.1 %collective-permute-start.2 = (bf16[64,2304]{1,0:T(8,128)(2,1)S(1)}, bf16[64,2304]{1,0:T(8,128)(2,1)S(1)}, u32[]{:S(2)}, u32[]{:S(2)}) collective-permute-start(bf16[64,2304]{1,0:T(8,128)(2,1)S(1)} %pad_maximum_fusion.refs_4_), channel_id=1, source_target_pairs={{0,4},{1,5},{4,8},{5,9},{8,12},{9,13},{12,14},{13,15},{14,10},{15,... | collective-permute-start | bytes 884744 | tf_op jit(solution)/shard_map/ppermute | solution.py:39
  4.6 7.1 %collective-permute-done.2.refs_5_ = bf16[64,2304]{1,0:T(8,128)(2,1)S(1)} collective-permute-done((bf16[64,2304]{1,0:T(8,128)(2,1)S(1)}, bf16[64,2304]{1,0:T(8,128)(2,1)S(1)}, u32[]{:S(2)}, u32[]{:S(2)}) %collective-permute-start.2) | collective-permute-done | bytes 294944 | tf_op jit(solution)/shard_map/ppermute | solution.py:39
  11.7 1.8 %collective-permute-start.4 = (bf16[64,2304]{1,0:T(8,128)(2,1)S(1)}, bf16[64,2304]{1,0:T(8,128)(2,1)S(1)}, u32[]{:S(2)}, u32[]{:S(2)}) collective-permute-start(bf16[64,2304]{1,0:T(8,128)(2,1)S(1)} %collective-permute-done.2.refs_5_), channel_id=1, source_target_pairs={{0,4},{1,5},{4,8},{5,9},{8,12},{9,13},{12,14},{13,15},{14,10},{15,... | collective-permute-start | bytes 884744 | tf_op jit(solution)/shard_map/ppermute | solution.py:39
  13.7 6.4 %collective-permute-done.4.refs_7_ = bf16[64,2304]{1,0:T(8,128)(2,1)S(1)} collective-permute-done((bf16[64,2304]{1,0:T(8,128)(2,1)S(1)}, bf16[64,2304]{1,0:T(8,128)(2,1)S(1)}, u32[]{:S(2)}, u32[]{:S(2)}) %collective-permute-start.4) | collective-permute-done | bytes 294944 | tf_op jit(solution)/shard_map/ppermute | solution.py:39
  20.1 1.5 %collective-permute-start.6 = (bf16[64,2304]{1,0:T(8,128)(2,1)S(1)}, bf16[64,2304]{1,0:T(8,128)(2,1)S(1)}, u32[]{:S(2)}, u32[]{:S(2)}) collective-permute-start(bf16[64,2304]{1,0:T(8,128)(2,1)S(1)} %collective-permute-done.4.refs_7_), channel_id=1, source_target_pairs={{0,4},{1,5},{4,8},{5,9},{8,12},{9,13},{12,14},{13,15},{14,10},{15,... | collective-permute-start | bytes 884744 | tf_op jit(solution)/shard_map/ppermute | solution.py:39
  22.1 3.1 %copy-done = bf16[128,28672]{1,0:T(8,128)(2,1)S(1)} copy-done((bf16[128,28672]{1,0:T(8,128)(2,1)S(1)}, bf16[128,28672]{1,0:T(8,128)(2,1)}, u32[]{:S(2)}) %copy-start) | copy-done | bytes 7340056
  25.2 1.6 %copy-done.1 = bf16[128,8192]{1,0:T(8,128)(2,1)S(1)} copy-done((bf16[128,8192]{1,0:T(8,128)(2,1)S(1)}, bf16[128,8192]{1,0:T(8,128)(2,1)}, u32[]{:S(2)}) %copy-start.1) | copy-done | bytes 2097176
  26.8 4.3 %shard_map.64.refs_6_ = f32[256,128]{1,0:T(8,128)S(1)} custom-call(bf16[128,8192]{1,0:T(8,128)(2,1)S(1)} %copy-done.1, bf16[128,8192]{1,0:T(8,128)(2,1)S(1)} %collective-permute-done.refs_1_, bf16[128,28672]{1,0:T(8,128)(2,1)S(1)} %copy-done, bf16[128,28672]{1,0:T(8,128)(2,1)S(1)} %collective-permute-done.1.refs_3_, ...), custom_call_target="tpu_custom_call" | custom-call | flops 377487360 | bytes 7372800 | tf_op jit(solution)/shard_map/pallas_call | solution.py:103
  31.1 1.5 %collective-permute-start.8 = (bf16[32,2304]{1,0:T(8,128)(2,1)S(1)}, bf16[32,2304]{1,0:T(8,128)(2,1)S(1)}, u32[]{:S(2)}, u32[]{:S(2)}) collective-permute-start(bf16[32,2304]{1,0:T(8,128)(2,1)S(1)} %slice.18), channel_id=1, source_target_pairs={{0,4},{1,5},{4,8},{5,9},{8,12},{9,13},{12,14},{13,15},{14,10},{15,... | collective-permute-start | bytes 442376 | tf_op jit(solution)/shard_map/ppermute | solution.py:39
  33.2 2.1 %shard_map.65.refs_6_ = f32[256,128]{1,0:T(8,128)S(1)} custom-call(bf16[128,8192]{1,0:T(8,128)(2,1)S(1)} %copy-done.1, bf16[128,8192]{1,0:T(8,128)(2,1)S(1)} %collective-permute-done.refs_1_, bf16[128,28672]{1,0:T(8,128)(2,1)S(1)} %copy-done, bf16[128,28672]{1,0:T(8,128)(2,1)S(1)} %collective-permute-done.1.refs_3_, ...), custom_call_target="tpu_custom_call" | custom-call | flops 150994944 | bytes 2949120 | tf_op jit(solution)/shard_map/pallas_call | solution.py:103
  36.3 1.5 %collective-permute-done.9.refs_5_ = bf16[32,2304]{1,0:T(8,128)(2,1)S(1)} collective-permute-done((bf16[32,2304]{1,0:T(8,128)(2,1)S(1)}, bf16[32,2304]{1,0:T(8,128)(2,1)S(1)}, u32[]{:S(2)}, u32[]{:S(2)}) %collective-permute-start.9) | collective-permute-done | bytes 147488 | tf_op jit(solution)/shard_map/ppermute | solution.py:39
  41.3 3.2 %collective-permute-done.11 = f32[1,4096]{1,0:T(1,128)S(1)} collective-permute-done((f32[1,4096]{1,0:T(1,128)S(1)}, f32[1,4096]{1,0:T(1,128)S(1)}, u32[]{:S(2)}, u32[]{:S(2)}) %collective-permute-start.11) | collective-permute-done | bytes 16416 | tf_op jit(solution)/shard_map/ppermute | solution.py:43
  44.6 1.6 %collective-permute-start.12 = (f32[1,4096]{1,0:T(1,128)S(1)}, f32[1,4096]{1,0:T(1,128)S(1)}, u32[]{:S(2)}, u32[]{:S(2)}) collective-permute-start(f32[1,4096]{1,0:T(1,128)S(1)} %add.10), channel_id=1, source_target_pairs={{0,4},{1,5},{2,6},{3,7},{4,0},{5,1},{6,2},{7,3},{8,12},{9,13},{10,... | collective-permute-start | bytes 49160 | tf_op jit(solution)/shard_map/ppermute | solution.py:43
  46.2 2.2 %collective-permute-done.12 = f32[1,4096]{1,0:T(1,128)S(1)} collective-permute-done((f32[1,4096]{1,0:T(1,128)S(1)}, f32[1,4096]{1,0:T(1,128)S(1)}, u32[]{:S(2)}, u32[]{:S(2)}) %collective-permute-start.12) | collective-permute-done | bytes 16416 | tf_op jit(solution)/shard_map/ppermute | solution.py:43
  48.4 2.7 %collective-permute-start.13 = (bf16[1,4096]{1,0:T(2,128)(2,1)S(1)}, bf16[1,4096]{1,0:T(2,128)(2,1)S(1)}, u32[]{:S(2)}, u32[]{:S(2)}) collective-permute-start(bf16[1,4096]{1,0:T(2,128)(2,1)S(1)} %add.11), channel_id=1, source_target_pairs={{0,8},{1,9},{2,10},{3,11},{4,12},{5,13},{6,14},{7,15},{8,0},{9,1},... | collective-permute-start | bytes 24584 | tf_op jit(solution)/shard_map/ppermute | solution.py:43
  51.0 2.0 %collective-permute-done.13 = bf16[1,4096]{1,0:T(2,128)(2,1)S(1)} collective-permute-done((bf16[1,4096]{1,0:T(2,128)(2,1)S(1)}, bf16[1,4096]{1,0:T(2,128)(2,1)S(1)}, u32[]{:S(2)}, u32[]{:S(2)}) %collective-permute-start.13) | collective-permute-done | bytes 8224 | tf_op jit(solution)/shard_map/ppermute | solution.py:43
  53.7 2.3 %constant_dynamic-update-slice_fusion.3 = (bf16[2,4096]{1,0:T(2,128)(2,1)S(1)}, bf16[2,256]{1,0:T(2,128)(2,1)S(1)}) fusion(bf16[2,4096]{1,0:T(2,128)(2,1)S(1)} %get-tuple-element.13, bf16[256,4096]{1,0:T(8,128)(2,1)} %collective-permute-done.14, bf16[1,4096]{1,0:T(2,128)(2,1)S(1)} %collective-permute-done.13, bf16[1,4096]{1,0:T(2,128)(2,1)S(1)} %add.11, ...), kind=kOutput, calls=%fused_computation.14 | convolution fusion | flops 4268544 | bytes 2131969 | tf_op jit(solution)/shard_map/dot_general | solution.py:17
  56.6 1.5 %shard_map.67 = bf16[8,4096]{1,0:T(8,128)(2,1)} custom-call(bf16[8,4096]{1,0:T(8,128)(2,1)} %x.1), custom_call_target="tpu_custom_call" | custom-call | tf_op jit(solution)/shard_map/pallas_call | solution.py:184
  58.1 1.6 %collective-permute-done.15 = bf16[2,512]{1,0:T(2,128)(2,1)S(1)} collective-permute-done((bf16[2,512]{1,0:T(2,128)(2,1)S(1)}, bf16[2,512]{1,0:T(2,128)(2,1)S(1)}, u32[]{:S(2)}, u32[]{:S(2)}) %collective-permute-start.15) | collective-permute-done | bytes 2080 | tf_op jit(solution)/shard_map/ppermute | solution.py:43
  59.7 1.6 %collective-permute-start.16 = (bf16[2,1024]{1,0:T(2,128)(2,1)S(1)}, bf16[2,1024]{1,0:T(2,128)(2,1)S(1)}, u32[]{:S(2)}, u32[]{:S(2)}) collective-permute-start(bf16[2,1024]{1,0:T(2,128)(2,1)S(1)} %pad_maximum_fusion.2), channel_id=1, source_target_pairs={{0,4},{1,5},{2,6},{3,7},{4,0},{5,1},{6,2},{7,3},{8,12},{9,13},{10,... | collective-permute-start | bytes 12296 | tf_op jit(solution)/shard_map/ppermute | solution.py:43
  61.3 2.0 %collective-permute-done.16 = bf16[2,1024]{1,0:T(2,128)(2,1)S(1)} collective-permute-done((bf16[2,1024]{1,0:T(2,128)(2,1)S(1)}, bf16[2,1024]{1,0:T(2,128)(2,1)S(1)}, u32[]{:S(2)}, u32[]{:S(2)}) %collective-permute-start.16) | collective-permute-done | bytes 4128 | tf_op jit(solution)/shard_map/ppermute | solution.py:43
  63.4 2.7 %collective-permute-start.17 = (bf16[2,2048]{1,0:T(2,128)(2,1)S(1)}, bf16[2,2048]{1,0:T(2,128)(2,1)S(1)}, u32[]{:S(2)}, u32[]{:S(2)}) collective-permute-start(bf16[2,2048]{1,0:T(2,128)(2,1)S(1)} %pad_maximum_fusion.1), channel_id=1, source_target_pairs={{0,8},{1,9},{2,10},{3,11},{4,12},{5,13},{6,14},{7,15},{8,0},{9,1},... | collective-permute-start | bytes 24584 | tf_op jit(solution)/shard_map/ppermute | solution.py:43
  66.0 1.9 %collective-permute-done.17 = bf16[2,2048]{1,0:T(2,128)(2,1)S(1)} collective-permute-done((bf16[2,2048]{1,0:T(2,128)(2,1)S(1)}, bf16[2,2048]{1,0:T(2,128)(2,1)S(1)}, u32[]{:S(2)}, u32[]{:S(2)}) %collective-permute-start.17) | collective-permute-done | bytes 8224 | tf_op jit(solution)/shard_map/ppermute | solution.py:43
  68.0 1.6 %convolution_multiply_fusion.1 = f32[2,8]{1,0:T(2,128)} fusion(bf16[2,4096]{1,0:T(2,128)(2,1)S(1)} %constant_dynamic-update-slice_fusion, bf16[8,4096]{1,0:T(8,128)(2,1)} %shard_map.67), kind=kOutput, calls=%fused_computation.3 | convolution fusion | flops 131088 | bytes 81984 | tf_op jit(solution)/shard_map/dot_general | solution.py:17
  (40 shorter events, 8.7 us)
Async XLA Ops:
  0.0 22.1 %collective-permute-start.1 = (bf16[128,28672]{1,0:T(8,128)(2,1)}, bf16[128,28672]{1,0:T(8,128)(2,1)S(1)}, u32[]{:S(2)}, u32[]{:S(2)}) collective-permute-start(bf16[128,28672]{1,0:T(8,128)(2,1)} %refs_2_.5), channel_id=1, source_target_pairs={{0,1},{1,0},{2,3},{3,2},{4,5},{5,4},{6,7},{7,6},{8,9},{9,8},{10,11... | collective-permute-start | bytes 22020104 | tf_op jit(solution)/shard_map/ppermute | solution.py:43
  0.5 21.6 %collective-permute-start = (bf16[128,8192]{1,0:T(8,128)(2,1)}, bf16[128,8192]{1,0:T(8,128)(2,1)S(1)}, u32[]{:S(2)}, u32[]{:S(2)}) collective-permute-start(bf16[128,8192]{1,0:T(8,128)(2,1)} %refs_0_.5), channel_id=1, source_target_pairs={{0,1},{1,0},{2,3},{3,2},{4,5},{5,4},{6,7},{7,6},{8,9},{9,8},{10,11... | collective-permute-start | bytes 6291464 | tf_op jit(solution)/shard_map/ppermute | solution.py:43
  1.5 10.2 %collective-permute-start.2 = (bf16[64,2304]{1,0:T(8,128)(2,1)S(1)}, bf16[64,2304]{1,0:T(8,128)(2,1)S(1)}, u32[]{:S(2)}, u32[]{:S(2)}) collective-permute-start(bf16[64,2304]{1,0:T(8,128)(2,1)S(1)} %pad_maximum_fusion.refs_4_), channel_id=1, source_target_pairs={{0,4},{1,5},{4,8},{5,9},{8,12},{9,13},{12,14},{13,15},{14,10},{15,... | collective-permute-start | bytes 884744 | tf_op jit(solution)/shard_map/ppermute | solution.py:39
  4.6 8.9 %collective-permute-start.3 = (bf16[64,2304]{1,0:T(8,128)(2,1)S(1)}, bf16[64,2304]{1,0:T(8,128)(2,1)S(1)}, u32[]{:S(2)}, u32[]{:S(2)}) collective-permute-start(bf16[64,2304]{1,0:T(8,128)(2,1)S(1)} %pad_maximum_fusion.refs_4_), channel_id=1, source_target_pairs={{0,2},{1,3},{4,0},{5,1},{8,4},{9,5},{12,8},{13,9},{14,12},{15,13},... | collective-permute-start | bytes 884744 | tf_op jit(solution)/shard_map/ppermute | solution.py:39
  4.6 49.2 %collective-permute-start.14 = (bf16[256,4096]{1,0:T(8,128)(2,1)}, bf16[256,4096]{1,0:T(8,128)(2,1)}, u32[]{:S(2)}, u32[]{:S(2)}) collective-permute-start(bf16[256,4096]{1,0:T(8,128)(2,1)} %param.10), channel_id=1, source_target_pairs={{0,1},{1,0},{2,3},{3,2},{4,5},{5,4},{6,7},{7,6},{8,9},{9,8},{10,11... | collective-permute-start | bytes 6291464 | tf_op jit(solution)/shard_map/ppermute | solution.py:43
  11.7 8.4 %collective-permute-start.4 = (bf16[64,2304]{1,0:T(8,128)(2,1)S(1)}, bf16[64,2304]{1,0:T(8,128)(2,1)S(1)}, u32[]{:S(2)}, u32[]{:S(2)}) collective-permute-start(bf16[64,2304]{1,0:T(8,128)(2,1)S(1)} %collective-permute-done.2.refs_5_), channel_id=1, source_target_pairs={{0,4},{1,5},{4,8},{5,9},{8,12},{9,13},{12,14},{13,15},{14,10},{15,... | collective-permute-start | bytes 884744 | tf_op jit(solution)/shard_map/ppermute | solution.py:39
  13.5 8.1 %collective-permute-start.5 = (bf16[64,2304]{1,0:T(8,128)(2,1)S(1)}, bf16[64,2304]{1,0:T(8,128)(2,1)S(1)}, u32[]{:S(2)}, u32[]{:S(2)}) collective-permute-start(bf16[64,2304]{1,0:T(8,128)(2,1)S(1)} %collective-permute-done.3.refs_6_), channel_id=1, source_target_pairs={{0,2},{1,3},{4,0},{5,1},{8,4},{9,5},{12,8},{13,9},{14,12},{15,13},... | collective-permute-start | bytes 884744 | tf_op jit(solution)/shard_map/ppermute | solution.py:39
  20.1 11.0 %collective-permute-start.6 = (bf16[64,2304]{1,0:T(8,128)(2,1)S(1)}, bf16[64,2304]{1,0:T(8,128)(2,1)S(1)}, u32[]{:S(2)}, u32[]{:S(2)}) collective-permute-start(bf16[64,2304]{1,0:T(8,128)(2,1)S(1)} %collective-permute-done.4.refs_7_), channel_id=1, source_target_pairs={{0,4},{1,5},{4,8},{5,9},{8,12},{9,13},{12,14},{13,15},{14,10},{15,... | collective-permute-start | bytes 884744 | tf_op jit(solution)/shard_map/ppermute | solution.py:39
  21.5 9.5 %collective-permute-start.7 = (bf16[64,2304]{1,0:T(8,128)(2,1)S(1)}, bf16[64,2304]{1,0:T(8,128)(2,1)S(1)}, u32[]{:S(2)}, u32[]{:S(2)}) collective-permute-start(bf16[64,2304]{1,0:T(8,128)(2,1)S(1)} %collective-permute-done.5.refs_8_), channel_id=1, source_target_pairs={{0,2},{1,3},{4,0},{5,1},{8,4},{9,5},{12,8},{13,9},{14,12},{15,13},... | collective-permute-start | bytes 884744 | tf_op jit(solution)/shard_map/ppermute | solution.py:39
  22.1 3.1 %copy-start = (bf16[128,28672]{1,0:T(8,128)(2,1)S(1)}, bf16[128,28672]{1,0:T(8,128)(2,1)}, u32[]{:S(2)}) copy-start(bf16[128,28672]{1,0:T(8,128)(2,1)} %refs_2_.5) | copy-start | bytes 22020100
  25.2 1.6 %copy-start.1 = (bf16[128,8192]{1,0:T(8,128)(2,1)S(1)}, bf16[128,8192]{1,0:T(8,128)(2,1)}, u32[]{:S(2)}) copy-start(bf16[128,8192]{1,0:T(8,128)(2,1)} %refs_0_.5) | copy-start | bytes 6291460
  31.1 5.2 %collective-permute-start.8 = (bf16[32,2304]{1,0:T(8,128)(2,1)S(1)}, bf16[32,2304]{1,0:T(8,128)(2,1)S(1)}, u32[]{:S(2)}, u32[]{:S(2)}) collective-permute-start(bf16[32,2304]{1,0:T(8,128)(2,1)S(1)} %slice.18), channel_id=1, source_target_pairs={{0,4},{1,5},{4,8},{5,9},{8,12},{9,13},{12,14},{13,15},{14,10},{15,... | collective-permute-start | bytes 442376 | tf_op jit(solution)/shard_map/ppermute | solution.py:39
  32.6 5.2 %collective-permute-start.9 = (bf16[32,2304]{1,0:T(8,128)(2,1)S(1)}, bf16[32,2304]{1,0:T(8,128)(2,1)S(1)}, u32[]{:S(2)}, u32[]{:S(2)}) collective-permute-start(bf16[32,2304]{1,0:T(8,128)(2,1)S(1)} %slice.19), channel_id=1, source_target_pairs={{0,2},{1,3},{4,0},{5,1},{8,4},{9,5},{12,8},{13,9},{14,12},{15,13},... | collective-permute-start | bytes 442376 | tf_op jit(solution)/shard_map/ppermute | solution.py:39
  35.4 17.7 %copy-start.2 = (bf16[256,4096]{1,0:T(8,128)(2,1)S(1)}, bf16[256,4096]{1,0:T(8,128)(2,1)}, u32[]{:S(2)}) copy-start(bf16[256,4096]{1,0:T(8,128)(2,1)} %param.10) | copy-start | bytes 6291460
  38.9 1.4 %collective-permute-start.10 = (f32[256,128]{1,0:T(8,128)S(1)}, f32[256,128]{1,0:T(8,128)S(1)}, u32[]{:S(2)}, u32[]{:S(2)}) collective-permute-start(f32[256,128]{1,0:T(8,128)S(1)} %shard_map.66), channel_id=1, source_target_pairs={{0,1},{1,0},{2,3},{3,2},{4,5},{5,4},{6,7},{7,6},{8,9},{9,8},{10,11... | collective-permute-start | bytes 393224 | tf_op jit(solution)/shard_map/ppermute | solution.py:43
  40.7 3.8 %collective-permute-start.11 = (f32[1,4096]{1,0:T(1,128)S(1)}, f32[1,4096]{1,0:T(1,128)S(1)}, u32[]{:S(2)}, u32[]{:S(2)}) collective-permute-start(f32[1,4096]{1,0:T(1,128)S(1)} %mul.22), channel_id=1, source_target_pairs={{0,2},{1,3},{2,0},{3,1},{4,6},{5,7},{6,4},{7,5},{8,10},{9,11},{10,... | collective-permute-start | bytes 49160 | tf_op jit(solution)/shard_map/ppermute | solution.py:43
  44.6 3.8 %collective-permute-start.12 = (f32[1,4096]{1,0:T(1,128)S(1)}, f32[1,4096]{1,0:T(1,128)S(1)}, u32[]{:S(2)}, u32[]{:S(2)}) collective-permute-start(f32[1,4096]{1,0:T(1,128)S(1)} %add.10), channel_id=1, source_target_pairs={{0,4},{1,5},{2,6},{3,7},{4,0},{5,1},{6,2},{7,3},{8,12},{9,13},{10,... | collective-permute-start | bytes 49160 | tf_op jit(solution)/shard_map/ppermute | solution.py:43
  48.4 4.7 %collective-permute-start.13 = (bf16[1,4096]{1,0:T(2,128)(2,1)S(1)}, bf16[1,4096]{1,0:T(2,128)(2,1)S(1)}, u32[]{:S(2)}, u32[]{:S(2)}) collective-permute-start(bf16[1,4096]{1,0:T(2,128)(2,1)S(1)} %add.11), channel_id=1, source_target_pairs={{0,8},{1,9},{2,10},{3,11},{4,12},{5,13},{6,14},{7,15},{8,0},{9,1},... | collective-permute-start | bytes 24584 | tf_op jit(solution)/shard_map/ppermute | solution.py:43
  56.0 3.7 %collective-permute-start.15 = (bf16[2,512]{1,0:T(2,128)(2,1)S(1)}, bf16[2,512]{1,0:T(2,128)(2,1)S(1)}, u32[]{:S(2)}, u32[]{:S(2)}) collective-permute-start(bf16[2,512]{1,0:T(2,128)(2,1)S(1)} %pad_maximum_fusion.3), channel_id=1, source_target_pairs={{0,2},{1,3},{2,0},{3,1},{4,6},{5,7},{6,4},{7,5},{8,10},{9,11},{10,... | collective-permute-start | bytes 6152 | tf_op jit(solution)/shard_map/ppermute | solution.py:43
  59.7 3.7 %collective-permute-start.16 = (bf16[2,1024]{1,0:T(2,128)(2,1)S(1)}, bf16[2,1024]{1,0:T(2,128)(2,1)S(1)}, u32[]{:S(2)}, u32[]{:S(2)}) collective-permute-start(bf16[2,1024]{1,0:T(2,128)(2,1)S(1)} %pad_maximum_fusion.2), channel_id=1, source_target_pairs={{0,4},{1,5},{2,6},{3,7},{4,0},{5,1},{6,2},{7,3},{8,12},{9,13},{10,... | collective-permute-start | bytes 12296 | tf_op jit(solution)/shard_map/ppermute | solution.py:43
  63.4 4.6 %collective-permute-start.17 = (bf16[2,2048]{1,0:T(2,128)(2,1)S(1)}, bf16[2,2048]{1,0:T(2,128)(2,1)S(1)}, u32[]{:S(2)}, u32[]{:S(2)}) collective-permute-start(bf16[2,2048]{1,0:T(2,128)(2,1)S(1)} %pad_maximum_fusion.1), channel_id=1, source_target_pairs={{0,8},{1,9},{2,10},{3,11},{4,12},{5,13},{6,14},{7,15},{8,0},{9,1},... | collective-permute-start | bytes 24584 | tf_op jit(solution)/shard_map/ppermute | solution.py:43

commit v3 on v0

v3 whole, which is shorter than its diff:
```python
import functools
import math

import jax
import jax.numpy as jnp
from jax import lax
from jax.experimental import pallas as pl
from jax.experimental.pallas import tpu as pltpu
from jax.sharding import PartitionSpec as P

LEN = 1024
LIMIT = 48
NT = (((1,), (1,)), ((), ()))
TN = (((0,), (0,)), ((), ()))
VMEM = pl.BlockSpec(memory_space=pltpu.VMEM)
HBM = pl.BlockSpec(memory_space=pltpu.HBM)


def dot(a, b, dims):
    return lax.dot_general(a, b, dims, preferred_element_type=jnp.float32)


def chip_behind(offset, chips):
    chip = lax.axis_index("dp") >> 1
    z, y = chip >> 1, chip & 1
    place = (jnp.where(y == 0, z, chips - 1 - z) - offset) & (chips - 1)
    return jnp.where(place < chips // 2, 2 * place, 2 * (chips - 1 - place) + 1)


def ring(x, step, chips):
    half = chips // 2
    chip = [2 * p if p < half else 2 * (chips - 1 - p) + 1 for p in range(chips)]
    pairs = [
        (chip[p] * 2 + c, chip[(p + step) % chips] * 2 + c) for p in range(chips) for c in range(2)
    ]
    return lax.ppermute(x, "dp", pairs)


def swap(x, bit, n):
    return lax.ppermute(x, "dp", [(i, i ^ bit) for i in range(n)])


def project_kernel(chips, offsets, widths, carry, fetch, *refs):
    tokens, refs = refs[:4], refs[4:]
    blocks, refs = refs[: 2 * len(offsets)], refs[2 * len(offsets) :]
    if carry:
        carried, refs = refs[0], refs[1:]
    out, refs = refs[0], refs[1:]
    if fetch is not None:
        fetched, refs = refs[0], refs[1:]
    buf, sems = refs
    rows = tokens[0].shape[0]
    rank, cut = blocks[0].shape
    a_width, g_width = widths
    core = lax.axis_index("dp") & 1
    copies = []
    for i, offset in enumerate(offsets + ([] if fetch is None else [fetch])):
        index = chip_behind(offset, chips) * 2 + core
        to = buf.at[i] if i < len(offsets) else fetched
        for k, ref in enumerate(tokens):
            width, start = (a_width, 0) if k < 2 else (g_width, a_width)
            copies.append(
                pltpu.make_async_copy(
                    ref.at[:, pl.ds(pl.multiple_of(index * width, 128), width)],
                    to.at[pl.ds(k % 2 * rows, rows), pl.ds(start, width)],
                    sems.at[i, k],
                )
            )
    for copy in copies:
        copy.start()
    if carry:
        a_sum, g_sum = carried[:, :rank], carried[:, rank:]
    else:
        a_sum = g_sum = jnp.zeros((out.shape[0], rank), jnp.float32)
    for i in range(len(offsets)):
        for copy in copies[4 * i : 4 * i + 4]:
            copy.wait()
        a_sum += dot(buf[i, :, :a_width], blocks[2 * i][:, :a_width], NT)
        g_sum += dot(buf[i, :, a_width:cut], blocks[2 * i][:, a_width:], NT)
        g_sum += dot(buf[i, :, cut:], blocks[2 * i + 1][...], NT)
    out[:, :rank] = a_sum
    out[:, rank:] = g_sum
    for copy in copies[4 * len(offsets) :]:
        copy.wait()


def project(tokens, blocks, offsets, widths, chips, carry=None, fetch=None):
    rows = tokens[0].shape[0]
    count = len(offsets)
    rank = blocks[0][0].shape[0]
    width = sum(widths)
    flat = [x for block in blocks for x in block]
    carried = () if carry is None else (carry,)
    out_shape = [jax.ShapeDtypeStruct((2 * rows, 2 * rank), jnp.float32)]
    if fetch is not None:
        out_shape.append(jax.ShapeDtypeStruct((2 * rows, width), tokens[0].dtype))
    return pl.pallas_call(
        functools.partial(project_kernel, chips, offsets, widths, carry is not None, fetch),
        out_shape=out_shape,
        in_specs=[HBM] * 4 + [VMEM] * (len(flat) + len(carried)),
        out_specs=[VMEM] * len(out_shape),
        scratch_shapes=[
            pltpu.VMEM((count, 2 * rows, width), tokens[0].dtype),
            pltpu.SemaphoreType.DMA((count + 1, 4)),
        ],
        compiler_params=pltpu.CompilerParams(vmem_limit_bytes=LIMIT * 2**20),
        cost_estimate=pl.CostEstimate(
            flops=4 * count * rows * rank * width,
            bytes_accessed=count * (2 * rows + rank) * width * 2,
            transcendentals=0,
        ),
    )(*tokens, *flat, *carried)


def finish_kernel(a_width, tokens, first, second, carried, out):
    rank, cut = first.shape
    out[:, :rank] = carried[:, :rank] + dot(tokens[:, :a_width], first[:, :a_width], NT)
    out[:, rank:] = (
        carried[:, rank:]
        + dot(tokens[:, a_width:cut], first[:, a_width:], NT)
        + dot(tokens[:, cut:], second[...], NT)
    )


def finish(tokens, block, a_width, carry):
    return pl.pallas_call(
        functools.partial(finish_kernel, a_width),
        out_shape=jax.ShapeDtypeStruct(carry.shape, carry.dtype),
        in_specs=[VMEM] * 4,
        out_specs=VMEM,
        compiler_params=pltpu.CompilerParams(vmem_limit_bytes=16 * 2**20),
    )(tokens, *block, carry)


def to_all(x, groups):
    copies = jnp.broadcast_to(x[None], (len(groups[0]),) + x.shape)
    return lax.all_to_all(copies, "dp", 0, 0, axis_index_groups=groups, tiled=True)


def local(activations, out_grads, in_basis, out_basis, preconditioner, queries):
    rows = activations.shape[0]
    a_width, rank = in_basis.shape
    n = activations.shape[1] // a_width
    chips = n // 2
    split = LEN // rows

    width = a_width + out_basis.shape[0]
    cut = width // 256 * 128
    in_rows, out_rows = in_basis.T, out_basis.T
    own = (
        jnp.concatenate([in_rows, out_rows[:, : cut - a_width]], axis=1),
        out_rows[:, cut - a_width :],
    )
    up, down = [own], [own]
    for _ in range(chips // 2 - 1):
        up.append(tuple(ring(x, 1, chips) for x in up[-1]))
        down.append(tuple(ring(x, -1, chips) for x in down[-1]))
    tokens = (activations, swap(activations, 1, n), out_grads, swap(out_grads, 1, n))

    widths = (a_width, width - a_width)
    run = functools.partial(project, tokens, widths=widths, chips=chips)
    (total,) = run([own, up[1], down[1]], [0, 1, -1])
    total, far_up, far_down = lax.optimization_barrier((total, up[-1][0], down[-1][1]))
    far = (ring(far_up, 1, chips), ring(far_down, -1, chips))
    for i in range(2, chips // 2 - 1):
        (total,) = run([up[i], down[i]], [i, -i], carry=total)
    i = chips // 2 - 1
    total, far_tokens = run([up[i], down[i]], [i, -i], carry=total, fetch=chips // 2)
    total = finish(far_tokens, far, a_width, total)
    theirs = swap(total, 1, n)
    total = (total + jnp.concatenate([theirs[rows:], theirs[:rows]], axis=0)).astype(jnp.bfloat16)

    raw = dot(total[:, rank:], total[:, :rank], TN)
    raw = raw.reshape(1, rank * rank) * (1.0 / math.sqrt(LEN))
    planes = [[2 * i + c for i in range(chips)] for c in range(2)]
    raw = to_all(raw, planes).reshape(-1, split // 2, rank * rank)
    features = raw.sum(axis=1).astype(jnp.bfloat16)

    conditioned = dot(features, preconditioner, NT).astype(jnp.bfloat16)
    conditioned = to_all(conditioned, [list(range(n))])
    conditioned = conditioned.transpose(1, 0, 2).reshape(-1, queries.shape[1])
    return dot(conditioned, queries, NT) * (1.0 / rank)


def local_gathered(activations, out_grads, in_basis, out_basis, preconditioner, queries):
    rows = activations.shape[0]
    rank = in_basis.shape[1]
    act_proj = jnp.dot(
        activations,
        lax.all_gather(in_basis, "dp", axis=0, tiled=True),
        preferred_element_type=jnp.float32,
    ).astype(jnp.bfloat16)
    grad_proj = jnp.dot(
        out_grads,
        lax.all_gather(out_basis, "dp", axis=0, tiled=True),
        preferred_element_type=jnp.float32,
    ).astype(jnp.bfloat16)
    raw = dot(grad_proj, act_proj, TN).reshape(1, rank * rank) * (1.0 / math.sqrt(LEN))
    gathered = lax.all_gather(raw, "dp", axis=0, tiled=True)
    features = gathered.reshape(-1, LEN // rows, rank * rank).sum(axis=1).astype(jnp.bfloat16)
    conditioned = dot(features, preconditioner, NT).astype(jnp.bfloat16)
    scores = dot(lax.all_gather(conditioned, "dp", axis=1, tiled=True), queries, NT)
    return scores * (1.0 / rank)


def power_of_two(x):
    return x > 0 and x & (x - 1) == 0


def solution(mesh):
    n = mesh.shape["dp"]

    def body(activations, out_grads, in_basis, out_basis, preconditioner, queries):
        aligned = all(x.shape[0] % 128 == 0 for x in (in_basis, out_basis, preconditioner))
        split = LEN // activations.shape[0]
        regular = aligned and n >= 8 and power_of_two(n) and power_of_two(split) and 4 <= split <= n
        form = local if regular else local_gathered
        return form(activations, out_grads, in_basis, out_basis, preconditioner, queries)

    return jax.shard_map(
        body,
        mesh=mesh,
        in_specs=(
            P(("parts", "dp"), None),
            P(("parts", "dp"), None),
            P("dp", None),
            P("dp", None),
            P("dp", None),
            P("dp", None),
        ),
        out_specs=P("parts", "dp"),
        check_vma=False,
    )
```

time: 153 us -> 63.4 us (0.41)
  waiting for transfers between devices: 90 us -> 7.38 us
  starting transfers between devices: 0.04 us -> 18.9 us
  blocking collectives: 37.5 us -> 21.8 us
  between operations: 13.4 us -> 0.18 us
  matrix products: 11.2 us -> 1.61 us
  Pallas kernels: 0 us -> 8.17 us
  local copies, waits for them, and re-layouts: 0.11 us -> 3.74 us
    all_gather x2 -> x0, waiting for transfers between devices: 88.6 us -> none  [the longest x1 47.5 us: local(): lax.all_gather(out_basis, 'dp', axis=0, tiled=True)]
    all_gather x2 -> x0, blocking collectives: 37.5 us -> none  [the longest x1 20.1 us: local(): gathered = lax.all_gather(partial_value, 'dp', axis=0, tiled=True)]
    all_to_all x0 -> x2, blocking collectives: none -> 21.8 us  [to_all(): lax.all_to_all(copies, 'dp', 0, 0, axis_index_groups=groups, tiled=True)]
    ppermute x0 -> x17, starting transfers between devices: none -> 18.9 us  [the longest x14 18.3 us: ring(): return lax.ppermute(x, 'dp', pairs)]
    dot_general x4 -> x3, matrix products: 11.2 us -> 1.61 us  [dot(): return lax.dot_general(a, b, dims, preferred_element_type=jnp.float32)]
    pallas_call x0 -> x4, Pallas kernels: none -> 8.17 us  [the longest x3 7.66 us: project(): pl.pallas_call(functools.partial(project_kernel, chips, offsets, widths,...]
    ppermute x0 -> x17, waiting for transfers between devices: none -> 7.38 us  [the longest x14 6.04 us: ring(): return lax.ppermute(x, 'dp', pairs)]
    slice x0 -> x3, local copies, waits for them, and re-layouts: none -> 1.93 us  [the longest x1 1 us: local(): out_rows[:, :cut - a_width]]
  transfers between devices with their start and end apart: 2 -> 17, of which waited for: 2 -> 8; matrix products, arithmetic and copies ran while one was open for 1% -> 4% of each run, Pallas kernels for 0% -> 12%
where the time goes in v3:
time: 63.4 us; the launch traced here: 63 us
  blocking collectives  21.8 us (34%)
  starting transfers between devices  18.9 us (30%)
  Pallas kernels  8.17 us (13%)
  waiting for transfers between devices  7.38 us (12%)
  local copies, waits for them, and re-layouts  3.74 us (6%)
  matrix products  1.61 us (3%)
  other arithmetic  1.26 us (2%)
    all_to_all x2, blocking collectives, to_all(): lax.all_to_all(copies, 'dp', 0, 0, axis_index_groups=groups, tiled=True)  21.8 us
    ppermute x14, starting transfers between devices, ring(): return lax.ppermute(x, 'dp', pairs)  18.3 us
    pallas_call x3, Pallas kernels, project(): pl.pallas_call(functools.partial(project_kernel, chips, offsets, widths,...  7.66 us
    ppermute x14, waiting for transfers between devices, ring(): return lax.ppermute(x, 'dp', pairs)  6.04 us
    dot_general x3, matrix products, dot(): return lax.dot_general(a, b, dims, preferred_element_type=jnp.float32)  1.61 us
    unnamed x6, local copies, waits for them, and re-layouts  1.6 us
    ppermute x3, waiting for transfers between devices, swap(): return lax.ppermute(x, 'dp', [(i, i ^ bit) for i in range(n)])  1.34 us
  transfers between devices with their start and end apart: 17, of which 8 were waited for; matrix products, arithmetic and copies ran while one was open for 4% of the time, Pallas kernels for 12%

profile of v3, /device:TPU:0, one launch (start us, length us, event | category | flops | bytes accessed | tf_op | source)
XLA Modules:
  0.0 63.0 jit_solution(13993165106100294436)
XLA Ops:
  0.5 1.0 %slice.24 = bf16[64,640]{1,0:T(8,128)(2,1)S(1)} slice(bf16[64,1792]{1,0:T(8,128)(2,1)} %bitcast.9), slice={[0:64], [0:640]} | slice | bytes 163840 | tf_op jit(solution)/shard_map/slice | solution.py:151
  2.4 3.1 %collective-permute-start.2 = (bf16[64,1152]{1,0:T(8,128)(2,1)S(1)}, bf16[64,1152]{1,0:T(8,128)(2,1)S(1)}, u32[]{:S(2)}, u32[]{:S(2)}) collective-permute-start(bf16[64,1152]{1,0:T(8,128)(2,1)S(1)} %pad_maximum_fusion.refs_4_), channel_id=1, source_target_pairs={{0,4},{1,5},{4,8},{5,9},{8,12},{9,13},{12,14},{13,15},{14,10},{15,... | collective-permute-start | bytes 442376 | tf_op jit(solution)/shard_map/ppermute | solution.py:36
  5.5 0.9 %slice.25.refs_5_ = bf16[64,1152]{1,0:T(8,128)(2,1)S(1)} slice(bf16[64,1792]{1,0:T(8,128)(2,1)} %bitcast.10), slice={[0:64], [640:1792]} | slice | bytes 294912 | tf_op jit(solution)/shard_map/slice | solution.py:152
  6.4 2.0 %collective-permute-start.11 = (bf16[64,1152]{1,0:T(8,128)(2,1)S(1)}, bf16[64,1152]{1,0:T(8,128)(2,1)S(1)}, u32[]{:S(2)}, u32[]{:S(2)}) collective-permute-start(bf16[64,1152]{1,0:T(8,128)(2,1)S(1)} %slice.25.refs_5_), channel_id=1, source_target_pairs={{0,2},{1,3},{4,0},{5,1},{8,4},{9,5},{12,8},{13,9},{14,12},{15,13},... | collective-permute-start | bytes 442376 | tf_op jit(solution)/shard_map/ppermute | solution.py:36
  8.4 1.0 %collective-permute-done.2.refs_6_ = bf16[64,1152]{1,0:T(8,128)(2,1)S(1)} collective-permute-done((bf16[64,1152]{1,0:T(8,128)(2,1)S(1)}, bf16[64,1152]{1,0:T(8,128)(2,1)S(1)}, u32[]{:S(2)}, u32[]{:S(2)}) %collective-permute-start.2) | collective-permute-done | bytes 147488 | tf_op jit(solution)/shard_map/ppermute | solution.py:36
  9.4 1.8 %collective-permute-start.5 = (bf16[64,1152]{1,0:T(8,128)(2,1)S(1)}, bf16[64,1152]{1,0:T(8,128)(2,1)S(1)}, u32[]{:S(2)}, u32[]{:S(2)}) collective-permute-start(bf16[64,1152]{1,0:T(8,128)(2,1)S(1)} %slice.25.refs_5_), channel_id=1, source_target_pairs={{0,4},{1,5},{4,8},{5,9},{8,12},{9,13},{12,14},{13,15},{14,10},{15,... | collective-permute-start | bytes 442376 | tf_op jit(solution)/shard_map/ppermute | solution.py:36
  11.2 1.1 %collective-permute-done.8.refs_8_ = bf16[64,1152]{1,0:T(8,128)(2,1)S(1)} collective-permute-done((bf16[64,1152]{1,0:T(8,128)(2,1)S(1)}, bf16[64,1152]{1,0:T(8,128)(2,1)S(1)}, u32[]{:S(2)}, u32[]{:S(2)}) %collective-permute-start.8) | collective-permute-done | bytes 147488 | tf_op jit(solution)/shard_map/ppermute | solution.py:36
  12.2 1.6 %collective-permute-start.3 = (bf16[64,1152]{1,0:T(8,128)(2,1)S(1)}, bf16[64,1152]{1,0:T(8,128)(2,1)S(1)}, u32[]{:S(2)}, u32[]{:S(2)}) collective-permute-start(bf16[64,1152]{1,0:T(8,128)(2,1)S(1)} %collective-permute-done.2.refs_6_), channel_id=1, source_target_pairs={{0,4},{1,5},{4,8},{5,9},{8,12},{9,13},{12,14},{13,15},{14,10},{15,... | collective-permute-start | bytes 442376 | tf_op jit(solution)/shard_map/ppermute | solution.py:36
  14.3 1.8 %collective-permute-done.5.refs_7_ = bf16[64,1152]{1,0:T(8,128)(2,1)S(1)} collective-permute-done((bf16[64,1152]{1,0:T(8,128)(2,1)S(1)}, bf16[64,1152]{1,0:T(8,128)(2,1)S(1)}, u32[]{:S(2)}, u32[]{:S(2)}) %collective-permute-start.5) | collective-permute-done | bytes 147488 | tf_op jit(solution)/shard_map/ppermute | solution.py:36
  16.1 1.4 %collective-permute-start.9 = (bf16[64,1152]{1,0:T(8,128)(2,1)S(1)}, bf16[64,1152]{1,0:T(8,128)(2,1)S(1)}, u32[]{:S(2)}, u32[]{:S(2)}) collective-permute-start(bf16[64,1152]{1,0:T(8,128)(2,1)S(1)} %collective-permute-done.8.refs_8_), channel_id=1, source_target_pairs={{0,2},{1,3},{4,0},{5,1},{8,4},{9,5},{12,8},{13,9},{14,12},{15,13},... | collective-permute-start | bytes 442376 | tf_op jit(solution)/shard_map/ppermute | solution.py:36
  17.7 1.5 %collective-permute-start.6 = (bf16[64,1152]{1,0:T(8,128)(2,1)S(1)}, bf16[64,1152]{1,0:T(8,128)(2,1)S(1)}, u32[]{:S(2)}, u32[]{:S(2)}) collective-permute-start(bf16[64,1152]{1,0:T(8,128)(2,1)S(1)} %collective-permute-done.5.refs_7_), channel_id=1, source_target_pairs={{0,4},{1,5},{4,8},{5,9},{8,12},{9,13},{12,14},{13,15},{14,10},{15,... | collective-permute-start | bytes 442376 | tf_op jit(solution)/shard_map/ppermute | solution.py:36
  19.2 1.0 %collective-permute-done.12.refs_7_ = bf16[64,1152]{1,0:T(8,128)(2,1)S(1)} collective-permute-done((bf16[64,1152]{1,0:T(8,128)(2,1)S(1)}, bf16[64,1152]{1,0:T(8,128)(2,1)S(1)}, u32[]{:S(2)}, u32[]{:S(2)}) %collective-permute-start.12) | collective-permute-done | bytes 147488 | tf_op jit(solution)/shard_map/ppermute | solution.py:36
  20.2 1.6 %collective-permute-start.4 = (bf16[64,1152]{1,0:T(8,128)(2,1)S(1)}, bf16[64,1152]{1,0:T(8,128)(2,1)S(1)}, u32[]{:S(2)}, u32[]{:S(2)}) collective-permute-start(bf16[64,1152]{1,0:T(8,128)(2,1)S(1)} %collective-permute-done.3.refs_4_), channel_id=1, source_target_pairs={{0,4},{1,5},{4,8},{5,9},{8,12},{9,13},{12,14},{13,15},{14,10},{15,... | collective-permute-start | bytes 442376 | tf_op jit(solution)/shard_map/ppermute | solution.py:36
  21.7 0.9 %collective-permute-start.13 = (bf16[64,1152]{1,0:T(8,128)(2,1)S(1)}, bf16[64,1152]{1,0:T(8,128)(2,1)S(1)}, u32[]{:S(2)}, u32[]{:S(2)}) collective-permute-start(bf16[64,1152]{1,0:T(8,128)(2,1)S(1)} %collective-permute-done.12.refs_7_), channel_id=1, source_target_pairs={{0,2},{1,3},{4,0},{5,1},{8,4},{9,5},{12,8},{13,9},{14,12},{15,13},... | collective-permute-start | bytes 442376 | tf_op jit(solution)/shard_map/ppermute | solution.py:36
  23.5 1.1 %collective-permute-start.10 = (bf16[64,1152]{1,0:T(8,128)(2,1)S(1)}, bf16[64,1152]{1,0:T(8,128)(2,1)S(1)}, u32[]{:S(2)}, u32[]{:S(2)}) collective-permute-start(bf16[64,1152]{1,0:T(8,128)(2,1)S(1)} %collective-permute-done.9.refs_6_), channel_id=1, source_target_pairs={{0,2},{1,3},{4,0},{5,1},{8,4},{9,5},{12,8},{13,9},{14,12},{15,13},... | collective-permute-start | bytes 442376 | tf_op jit(solution)/shard_map/ppermute | solution.py:36
  24.6 0.9 %collective-permute-start.7 = (bf16[64,1152]{1,0:T(8,128)(2,1)S(1)}, bf16[64,1152]{1,0:T(8,128)(2,1)S(1)}, u32[]{:S(2)}, u32[]{:S(2)}) collective-permute-start(bf16[64,1152]{1,0:T(8,128)(2,1)S(1)} %collective-permute-done.6.refs_5_), channel_id=1, source_target_pairs={{0,4},{1,5},{4,8},{5,9},{8,12},{9,13},{12,14},{13,15},{14,10},{15,... | collective-permute-start | bytes 442376 | tf_op jit(solution)/shard_map/ppermute | solution.py:36
  25.6 1.6 %copy-done.1 = bf16[128,8192]{1,0:T(8,128)(2,1)S(1)} copy-done((bf16[128,8192]{1,0:T(8,128)(2,1)S(1)}, bf16[128,8192]{1,0:T(8,128)(2,1)}, u32[]{:S(2)}) %copy-start.1) | copy-done | bytes 2097176
  27.1 2.9 %shard_map.64.refs_8_ = f32[256,128]{1,0:T(8,128)S(1)} custom-call(bf16[128,8192]{1,0:T(8,128)(2,1)S(1)} %copy-done.1, bf16[128,8192]{1,0:T(8,128)(2,1)S(1)} %collective-permute-done.refs_1_, bf16[128,28672]{1,0:T(8,128)(2,1)} %refs_2_.5, bf16[128,28672]{1,0:T(8,128)(2,1)} %collective-permute-done.1.refs_3_, bf16[64,1152]{1,0:T(8,128)(2,1)S(1)} %pad_maximum_fusion.refs_4_, ...), custom_call_target="tpu_custom_call" | custom-call | flops 226492416 | bytes 4423680 | tf_op jit(solution)/shard_map/pallas_call | solution.py:97
  30.1 1.2 %collective-permute-start.14 = (bf16[64,1152]{1,0:T(8,128)(2,1)S(1)}, bf16[64,1152]{1,0:T(8,128)(2,1)S(1)}, u32[]{:S(2)}, u32[]{:S(2)}) collective-permute-start(bf16[64,1152]{1,0:T(8,128)(2,1)S(1)} %collective-permute-done.4.refs_4_), channel_id=1, source_target_pairs={{0,4},{1,5},{4,8},{5,9},{8,12},{9,13},{12,14},{13,15},{14,10},{15,... | collective-permute-start | bytes 442376 | tf_op jit(solution)/shard_map/ppermute | solution.py:36
  32.2 2.3 %shard_map.65.refs_8_ = f32[256,128]{1,0:T(8,128)S(1)} custom-call(bf16[128,8192]{1,0:T(8,128)(2,1)S(1)} %copy-done.1, bf16[128,8192]{1,0:T(8,128)(2,1)S(1)} %collective-permute-done.refs_1_, bf16[128,28672]{1,0:T(8,128)(2,1)} %refs_2_.5, bf16[128,28672]{1,0:T(8,128)(2,1)} %collective-permute-done.1.refs_3_, ...), custom_call_target="tpu_custom_call" | custom-call | flops 150994944 | bytes 2949120 | tf_op jit(solution)/shard_map/pallas_call | solution.py:97
  34.5 2.4 %shard_map.66 = (f32[256,128]{1,0:T(8,128)S(1)}, bf16[256,2304]{1,0:T(8,128)(2,1)S(1)}) custom-call(bf16[128,8192]{1,0:T(8,128)(2,1)S(1)} %copy-done.1, bf16[128,8192]{1,0:T(8,128)(2,1)S(1)} %collective-permute-done.refs_1_, bf16[128,28672]{1,0:T(8,128)(2,1)} %refs_2_.5, bf16[128,28672]{1,0:T(8,128)(2,1)} %collective-permute-done.1.refs_3_, ...), custom_call_target="tpu_custom_call" | custom-call | flops 150994944 | bytes 2949120 | tf_op jit(solution)/shard_map/pallas_call | solution.py:97
  37.6 1.3 %collective-permute-done.16 = f32[256,128]{1,0:T(8,128)S(1)} collective-permute-done((f32[256,128]{1,0:T(8,128)S(1)}, f32[256,128]{1,0:T(8,128)S(1)}, u32[]{:S(2)}, u32[]{:S(2)}) %collective-permute-start.16) | collective-permute-done | bytes 131104 | tf_op jit(solution)/shard_map/ppermute | solution.py:40
  39.4 12.7 %all_to_all.10 = f32[8,1,4096]{2,1,0:T(1,128)S(1)} all-to-all(f32[8,1,4096]{2,1,0:T(1,128)S(1)} %broadcast_in_dim.4), channel_id=1, replica_groups={{0,2,4,6,8,10,12,14},{1,3,5,7,9,11,13,15},{16,18,20,22,24,26,28,30},{17..., dimensions={0} | all-to-all | bytes 262144 | tf_op jit(solution)/shard_map/all_to_all | solution.py:137
  53.2 9.1 %all_to_all.11 = bf16[16,2,256]{2,1,0:T(2,128)(2,1)S(1)} all-to-all(bf16[16,2,256]{2,1,0:T(2,128)(2,1)S(1)} %broadcast_in_dim.5), channel_id=1, replica_groups={{0,1,2,3,4,5,6,7,8,9,10,11,12,13,14,15},{16,17,18,19,20,21,22,23,24,25,..., dimensions={0} | all-to-all | bytes 32768 | tf_op jit(solution)/shard_map/all_to_all | solution.py:137
  (36 shorter events, 6.6 us)
Async XLA Ops:
  0.0 52.6 %copy-start = (bf16[256,4096]{1,0:T(8,128)(2,1)S(1)}, bf16[256,4096]{1,0:T(8,128)(2,1)}, u32[]{:S(2)}) copy-start(bf16[256,4096]{1,0:T(8,128)(2,1)} %param.10) | copy-start | bytes 6291460
  0.0 25.5 %collective-permute-start.1 = (bf16[128,28672]{1,0:T(8,128)(2,1)}, bf16[128,28672]{1,0:T(8,128)(2,1)}, u32[]{:S(2)}, u32[]{:S(2)}) collective-permute-start(bf16[128,28672]{1,0:T(8,128)(2,1)} %refs_2_.5), channel_id=1, source_target_pairs={{0,1},{1,0},{2,3},{3,2},{4,5},{5,4},{6,7},{7,6},{8,9},{9,8},{10,11... | collective-permute-start | bytes 22020104 | tf_op jit(solution)/shard_map/ppermute | solution.py:40
  0.5 24.2 %collective-permute-start = (bf16[128,8192]{1,0:T(8,128)(2,1)}, bf16[128,8192]{1,0:T(8,128)(2,1)S(1)}, u32[]{:S(2)}, u32[]{:S(2)}) collective-permute-start(bf16[128,8192]{1,0:T(8,128)(2,1)} %refs_0_.5), channel_id=1, source_target_pairs={{0,1},{1,0},{2,3},{3,2},{4,5},{5,4},{6,7},{7,6},{8,9},{9,8},{10,11... | collective-permute-start | bytes 6291464 | tf_op jit(solution)/shard_map/ppermute | solution.py:40
  2.4 7.0 %collective-permute-start.2 = (bf16[64,1152]{1,0:T(8,128)(2,1)S(1)}, bf16[64,1152]{1,0:T(8,128)(2,1)S(1)}, u32[]{:S(2)}, u32[]{:S(2)}) collective-permute-start(bf16[64,1152]{1,0:T(8,128)(2,1)S(1)} %pad_maximum_fusion.refs_4_), channel_id=1, source_target_pairs={{0,4},{1,5},{4,8},{5,9},{8,12},{9,13},{12,14},{13,15},{14,10},{15,... | collective-permute-start | bytes 442376 | tf_op jit(solution)/shard_map/ppermute | solution.py:36
  5.5 6.8 %collective-permute-start.8 = (bf16[64,1152]{1,0:T(8,128)(2,1)S(1)}, bf16[64,1152]{1,0:T(8,128)(2,1)S(1)}, u32[]{:S(2)}, u32[]{:S(2)}) collective-permute-start(bf16[64,1152]{1,0:T(8,128)(2,1)S(1)} %pad_maximum_fusion.refs_4_), channel_id=1, source_target_pairs={{0,2},{1,3},{4,0},{5,1},{8,4},{9,5},{12,8},{13,9},{14,12},{15,13},... | collective-permute-start | bytes 442376 | tf_op jit(solution)/shard_map/ppermute | solution.py:36
  6.4 7.7 %collective-permute-start.11 = (bf16[64,1152]{1,0:T(8,128)(2,1)S(1)}, bf16[64,1152]{1,0:T(8,128)(2,1)S(1)}, u32[]{:S(2)}, u32[]{:S(2)}) collective-permute-start(bf16[64,1152]{1,0:T(8,128)(2,1)S(1)} %slice.25.refs_5_), channel_id=1, source_target_pairs={{0,2},{1,3},{4,0},{5,1},{8,4},{9,5},{12,8},{13,9},{14,12},{15,13},... | collective-permute-start | bytes 442376 | tf_op jit(solution)/shard_map/ppermute | solution.py:36
  9.4 6.7 %collective-permute-start.5 = (bf16[64,1152]{1,0:T(8,128)(2,1)S(1)}, bf16[64,1152]{1,0:T(8,128)(2,1)S(1)}, u32[]{:S(2)}, u32[]{:S(2)}) collective-permute-start(bf16[64,1152]{1,0:T(8,128)(2,1)S(1)} %slice.25.refs_5_), channel_id=1, source_target_pairs={{0,4},{1,5},{4,8},{5,9},{8,12},{9,13},{12,14},{13,15},{14,10},{15,... | collective-permute-start | bytes 442376 | tf_op jit(solution)/shard_map/ppermute | solution.py:36
  12.2 5.5 %collective-permute-start.3 = (bf16[64,1152]{1,0:T(8,128)(2,1)S(1)}, bf16[64,1152]{1,0:T(8,128)(2,1)S(1)}, u32[]{:S(2)}, u32[]{:S(2)}) collective-permute-start(bf16[64,1152]{1,0:T(8,128)(2,1)S(1)} %collective-permute-done.2.refs_6_), channel_id=1, source_target_pairs={{0,4},{1,5},{4,8},{5,9},{8,12},{9,13},{12,14},{13,15},{14,10},{15,... | collective-permute-start | bytes 442376 | tf_op jit(solution)/shard_map/ppermute | solution.py:36
  14.0 6.1 %collective-permute-start.12 = (bf16[64,1152]{1,0:T(8,128)(2,1)S(1)}, bf16[64,1152]{1,0:T(8,128)(2,1)S(1)}, u32[]{:S(2)}, u32[]{:S(2)}) collective-permute-start(bf16[64,1152]{1,0:T(8,128)(2,1)S(1)} %collective-permute-done.11.refs_9_), channel_id=1, source_target_pairs={{0,2},{1,3},{4,0},{5,1},{8,4},{9,5},{12,8},{13,9},{14,12},{15,13},... | collective-permute-start | bytes 442376 | tf_op jit(solution)/shard_map/ppermute | solution.py:36
  16.1 5.6 %collective-permute-start.9 = (bf16[64,1152]{1,0:T(8,128)(2,1)S(1)}, bf16[64,1152]{1,0:T(8,128)(2,1)S(1)}, u32[]{:S(2)}, u32[]{:S(2)}) collective-permute-start(bf16[64,1152]{1,0:T(8,128)(2,1)S(1)} %collective-permute-done.8.refs_8_), channel_id=1, source_target_pairs={{0,2},{1,3},{4,0},{5,1},{8,4},{9,5},{12,8},{13,9},{14,12},{15,13},... | collective-permute-start | bytes 442376 | tf_op jit(solution)/shard_map/ppermute | solution.py:36
  17.7 5.8 %collective-permute-start.6 = (bf16[64,1152]{1,0:T(8,128)(2,1)S(1)}, bf16[64,1152]{1,0:T(8,128)(2,1)S(1)}, u32[]{:S(2)}, u32[]{:S(2)}) collective-permute-start(bf16[64,1152]{1,0:T(8,128)(2,1)S(1)} %collective-permute-done.5.refs_7_), channel_id=1, source_target_pairs={{0,4},{1,5},{4,8},{5,9},{8,12},{9,13},{12,14},{13,15},{14,10},{15,... | collective-permute-start | bytes 442376 | tf_op jit(solution)/shard_map/ppermute | solution.py:36
  20.2 9.9 %collective-permute-start.4 = (bf16[64,1152]{1,0:T(8,128)(2,1)S(1)}, bf16[64,1152]{1,0:T(8,128)(2,1)S(1)}, u32[]{:S(2)}, u32[]{:S(2)}) collective-permute-start(bf16[64,1152]{1,0:T(8,128)(2,1)S(1)} %collective-permute-done.3.refs_4_), channel_id=1, source_target_pairs={{0,4},{1,5},{4,8},{5,9},{8,12},{9,13},{12,14},{13,15},{14,10},{15,... | collective-permute-start | bytes 442376 | tf_op jit(solution)/shard_map/ppermute | solution.py:36
  21.7 8.4 %collective-permute-start.13 = (bf16[64,1152]{1,0:T(8,128)(2,1)S(1)}, bf16[64,1152]{1,0:T(8,128)(2,1)S(1)}, u32[]{:S(2)}, u32[]{:S(2)}) collective-permute-start(bf16[64,1152]{1,0:T(8,128)(2,1)S(1)} %collective-permute-done.12.refs_7_), channel_id=1, source_target_pairs={{0,2},{1,3},{4,0},{5,1},{8,4},{9,5},{12,8},{13,9},{14,12},{15,13},... | collective-permute-start | bytes 442376 | tf_op jit(solution)/shard_map/ppermute | solution.py:36
  23.5 11.0 %collective-permute-start.10 = (bf16[64,1152]{1,0:T(8,128)(2,1)S(1)}, bf16[64,1152]{1,0:T(8,128)(2,1)S(1)}, u32[]{:S(2)}, u32[]{:S(2)}) collective-permute-start(bf16[64,1152]{1,0:T(8,128)(2,1)S(1)} %collective-permute-done.9.refs_6_), channel_id=1, source_target_pairs={{0,2},{1,3},{4,0},{5,1},{8,4},{9,5},{12,8},{13,9},{14,12},{15,13},... | collective-permute-start | bytes 442376 | tf_op jit(solution)/shard_map/ppermute | solution.py:36
  24.6 9.9 %collective-permute-start.7 = (bf16[64,1152]{1,0:T(8,128)(2,1)S(1)}, bf16[64,1152]{1,0:T(8,128)(2,1)S(1)}, u32[]{:S(2)}, u32[]{:S(2)}) collective-permute-start(bf16[64,1152]{1,0:T(8,128)(2,1)S(1)} %collective-permute-done.6.refs_5_), channel_id=1, source_target_pairs={{0,4},{1,5},{4,8},{5,9},{8,12},{9,13},{12,14},{13,15},{14,10},{15,... | collective-permute-start | bytes 442376 | tf_op jit(solution)/shard_map/ppermute | solution.py:36
  25.6 1.6 %copy-start.1 = (bf16[128,8192]{1,0:T(8,128)(2,1)S(1)}, bf16[128,8192]{1,0:T(8,128)(2,1)}, u32[]{:S(2)}) copy-start(bf16[128,8192]{1,0:T(8,128)(2,1)} %refs_0_.5) | copy-start | bytes 6291460
  30.1 6.9 %collective-permute-start.14 = (bf16[64,1152]{1,0:T(8,128)(2,1)S(1)}, bf16[64,1152]{1,0:T(8,128)(2,1)S(1)}, u32[]{:S(2)}, u32[]{:S(2)}) collective-permute-start(bf16[64,1152]{1,0:T(8,128)(2,1)S(1)} %collective-permute-done.4.refs_4_), channel_id=1, source_target_pairs={{0,4},{1,5},{4,8},{5,9},{8,12},{9,13},{12,14},{13,15},{14,10},{15,... | collective-permute-start | bytes 442376 | tf_op jit(solution)/shard_map/ppermute | solution.py:36
  31.3 5.6 %collective-permute-start.15 = (bf16[64,1152]{1,0:T(8,128)(2,1)S(1)}, bf16[64,1152]{1,0:T(8,128)(2,1)S(1)}, u32[]{:S(2)}, u32[]{:S(2)}) collective-permute-start(bf16[64,1152]{1,0:T(8,128)(2,1)S(1)} %collective-permute-done.13.refs_7_), channel_id=1, source_target_pairs={{0,2},{1,3},{4,0},{5,1},{8,4},{9,5},{12,8},{13,9},{14,12},{15,13},... | collective-permute-start | bytes 442376 | tf_op jit(solution)/shard_map/ppermute | solution.py:36
  37.5 24.8 %copy-start.2 = (bf16[8,4096]{1,0:T(8,128)(2,1)S(1)}, bf16[8,4096]{1,0:T(8,128)(2,1)}, u32[]{:S(2)}) copy-start(bf16[8,4096]{1,0:T(8,128)(2,1)} %param.11) | copy-start | bytes 196612
  37.5 1.4 %collective-permute-start.16 = (f32[256,128]{1,0:T(8,128)S(1)}, f32[256,128]{1,0:T(8,128)S(1)}, u32[]{:S(2)}, u32[]{:S(2)}) collective-permute-start(f32[256,128]{1,0:T(8,128)S(1)} %shard_map.67), channel_id=1, source_target_pairs={{0,1},{1,0},{2,3},{3,2},{4,5},{5,4},{6,7},{7,6},{8,9},{9,8},{10,11... | collective-permute-start | bytes 393224 | tf_op jit(solution)/shard_map/ppermute | solution.py:40

commit v4 on v3

--- a/solution.py
+++ b/solution.py
@@ -151,11 +151,16 @@
         jnp.concatenate([in_rows, out_rows[:, : cut - a_width]], axis=1),
         out_rows[:, cut - a_width :],
     )
+    activations_2 = swap(activations, 1, n)
+    out_grads_2 = swap(out_grads, 1, n)
     up, down = [own], [own]
-    for _ in range(chips // 2 - 1):
+    for i in range(chips // 2 - 1):
+        if i == 1:
+            first, activations_2 = lax.optimization_barrier((up[-1][0], activations_2))
+            up[-1] = (first, up[-1][1])
         up.append(tuple(ring(x, 1, chips) for x in up[-1]))
         down.append(tuple(ring(x, -1, chips) for x in down[-1]))
-    tokens = (activations, swap(activations, 1, n), out_grads, swap(out_grads, 1, n))
+    tokens = (activations, activations_2, out_grads, out_grads_2)
 
     widths = (a_width, width - a_width)
     run = functools.partial(project, tokens, widths=widths, chips=chips)
@@ -171,10 +176,11 @@
     total = (total + jnp.concatenate([theirs[rows:], theirs[:rows]], axis=0)).astype(jnp.bfloat16)
 
     raw = dot(total[:, rank:], total[:, :rank], TN)
-    raw = raw.reshape(1, rank * rank) * (1.0 / math.sqrt(LEN))
+    raw = (raw * (1.0 / math.sqrt(LEN))).astype(jnp.bfloat16).reshape(-1, 128)
     planes = [[2 * i + c for i in range(chips)] for c in range(2)]
-    raw = to_all(raw, planes).reshape(-1, split // 2, rank * rank)
-    features = raw.sum(axis=1).astype(jnp.bfloat16)
+    raw = to_all(raw, planes).astype(jnp.float32)
+    features = raw.reshape((-1, split // 2) + raw.shape[1:]).sum(axis=1)
+    features = features.astype(jnp.bfloat16).reshape(-1, rank * rank)
 
     conditioned = dot(features, preconditioner, NT).astype(jnp.bfloat16)
     conditioned = to_all(conditioned, [list(range(n))])

time: 63.4 us -> 61.3 us (0.967)
  blocking collectives: 21.8 us -> 20.6 us
  starting transfers between devices: 18.9 us -> 17.7 us
  waiting for transfers between devices: 7.38 us -> 8.19 us
    all_to_all x2, blocking collectives: 21.8 us -> 20.6 us  [to_all(): lax.all_to_all(copies, 'dp', 0, 0, axis_index_groups=groups, tiled=True)]
    ppermute x14, starting transfers between devices: 18.3 us -> 17.1 us  [ring(): return lax.ppermute(x, 'dp', pairs)]
    ppermute x14, waiting for transfers between devices: 6.04 us -> 6.85 us  [ring(): return lax.ppermute(x, 'dp', pairs)]
  transfers between devices with their start and end apart: 17 -> 17, of which waited for: 8 -> 7; matrix products, arithmetic and copies ran while one was open for 4% -> 5% of each run, Pallas kernels for 12% -> 13%
where the time goes in v4:
time: 61.3 us; the launch traced here: 61 us
  blocking collectives  20.6 us (34%)
  starting transfers between devices  17.7 us (29%)
  waiting for transfers between devices  8.19 us (13%)
  Pallas kernels  8.18 us (13%)
  local copies, waits for them, and re-layouts  3.66 us (6%)
  matrix products  1.61 us (3%)
  other arithmetic  0.88 us (1%)
    all_to_all x2, blocking collectives, to_all(): lax.all_to_all(copies, 'dp', 0, 0, axis_index_groups=groups, tiled=True)  20.6 us
    ppermute x14, starting transfers between devices, ring(): return lax.ppermute(x, 'dp', pairs)  17.1 us
    pallas_call x3, Pallas kernels, project(): pl.pallas_call(functools.partial(project_kernel, chips, offsets, widths,...  7.65 us
    ppermute x14, waiting for transfers between devices, ring(): return lax.ppermute(x, 'dp', pairs)  6.85 us
    dot_general x3, matrix products, dot(): return lax.dot_general(a, b, dims, preferred_element_type=jnp.float32)  1.61 us
    unnamed x6, local copies, waits for them, and re-layouts  1.6 us
    ppermute x3, waiting for transfers between devices, swap(): return lax.ppermute(x, 'dp', [(i, i ^ bit) for i in range(n)])  1.34 us
  transfers between devices with their start and end apart: 17, of which 7 were waited for; matrix products, arithmetic and copies ran while one was open for 5% of the time, Pallas kernels for 13%

profile of v4, /device:TPU:0, one launch (start us, length us, event | category | flops | bytes accessed | tf_op | source)
XLA Modules:
  0.0 61.0 jit_solution(11915851684727451966)
XLA Ops:
  0.5 1.0 %slice.24 = bf16[64,640]{1,0:T(8,128)(2,1)S(1)} slice(bf16[64,1792]{1,0:T(8,128)(2,1)} %bitcast.14), slice={[0:64], [0:640]} | slice | bytes 163840 | tf_op jit(solution)/shard_map/slice | solution.py:151
  1.5 0.9 %pad_maximum_fusion.refs_4_ = bf16[64,1152]{1,0:T(8,128)(2,1)S(1)} fusion(bf16[64,640]{1,0:T(8,128)(2,1)S(1)} %slice.24, bf16[64,512]{1,0:T(8,128)(2,1)} %bitcast.17), kind=kLoop, calls=%fused_computation.4 | loop fusion | flops 294912 | bytes 294912 | tf_op jit(solution)/shard_map/concatenate | solution.py:151
  2.4 3.1 %collective-permute-start = (bf16[64,1152]{1,0:T(8,128)(2,1)S(1)}, bf16[64,1152]{1,0:T(8,128)(2,1)S(1)}, u32[]{:S(2)}, u32[]{:S(2)}) collective-permute-start(bf16[64,1152]{1,0:T(8,128)(2,1)S(1)} %pad_maximum_fusion.refs_4_), channel_id=1, source_target_pairs={{0,4},{1,5},{4,8},{5,9},{8,12},{9,13},{12,14},{13,15},{14,10},{15,... | collective-permute-start | bytes 442376 | tf_op jit(solution)/shard_map/ppermute | solution.py:36
  5.5 0.9 %slice.25.refs_5_ = bf16[64,1152]{1,0:T(8,128)(2,1)S(1)} slice(bf16[64,1792]{1,0:T(8,128)(2,1)} %bitcast.15), slice={[0:64], [640:1792]} | slice | bytes 294912 | tf_op jit(solution)/shard_map/slice | solution.py:152
  6.4 2.0 %collective-permute-start.8 = (bf16[64,1152]{1,0:T(8,128)(2,1)S(1)}, bf16[64,1152]{1,0:T(8,128)(2,1)S(1)}, u32[]{:S(2)}, u32[]{:S(2)}) collective-permute-start(bf16[64,1152]{1,0:T(8,128)(2,1)S(1)} %pad_maximum_fusion.refs_4_), channel_id=1, source_target_pairs={{0,2},{1,3},{4,0},{5,1},{8,4},{9,5},{12,8},{13,9},{14,12},{15,13},... | collective-permute-start | bytes 442376 | tf_op jit(solution)/shard_map/ppermute | solution.py:36
  8.4 1.0 %collective-permute-done.refs_6_ = bf16[64,1152]{1,0:T(8,128)(2,1)S(1)} collective-permute-done((bf16[64,1152]{1,0:T(8,128)(2,1)S(1)}, bf16[64,1152]{1,0:T(8,128)(2,1)S(1)}, u32[]{:S(2)}, u32[]{:S(2)}) %collective-permute-start) | collective-permute-done | bytes 147488 | tf_op jit(solution)/shard_map/ppermute | solution.py:36
  9.4 1.8 %collective-permute-start.5 = (bf16[64,1152]{1,0:T(8,128)(2,1)S(1)}, bf16[64,1152]{1,0:T(8,128)(2,1)S(1)}, u32[]{:S(2)}, u32[]{:S(2)}) collective-permute-start(bf16[64,1152]{1,0:T(8,128)(2,1)S(1)} %slice.25.refs_5_), channel_id=1, source_target_pairs={{0,4},{1,5},{4,8},{5,9},{8,12},{9,13},{12,14},{13,15},{14,10},{15,... | collective-permute-start | bytes 442376 | tf_op jit(solution)/shard_map/ppermute | solution.py:36
  11.2 2.0 %collective-permute-done.11.refs_9_ = bf16[64,1152]{1,0:T(8,128)(2,1)S(1)} collective-permute-done((bf16[64,1152]{1,0:T(8,128)(2,1)S(1)}, bf16[64,1152]{1,0:T(8,128)(2,1)S(1)}, u32[]{:S(2)}, u32[]{:S(2)}) %collective-permute-start.11) | collective-permute-done | bytes 147488 | tf_op jit(solution)/shard_map/ppermute | solution.py:36
  13.2 2.0 %collective-permute-start.3 = (bf16[64,1152]{1,0:T(8,128)(2,1)S(1)}, bf16[64,1152]{1,0:T(8,128)(2,1)S(1)}, u32[]{:S(2)}, u32[]{:S(2)}) collective-permute-start(bf16[64,1152]{1,0:T(8,128)(2,1)S(1)} %collective-permute-done.refs_6_), channel_id=1, source_target_pairs={{0,4},{1,5},{4,8},{5,9},{8,12},{9,13},{12,14},{13,15},{14,10},{15,... | collective-permute-start | bytes 442376 | tf_op jit(solution)/shard_map/ppermute | solution.py:36
  15.2 1.1 %collective-permute-done.8.refs_8_ = bf16[64,1152]{1,0:T(8,128)(2,1)S(1)} collective-permute-done((bf16[64,1152]{1,0:T(8,128)(2,1)S(1)}, bf16[64,1152]{1,0:T(8,128)(2,1)S(1)}, u32[]{:S(2)}, u32[]{:S(2)}) %collective-permute-start.8) | collective-permute-done | bytes 147488 | tf_op jit(solution)/shard_map/ppermute | solution.py:36
  16.4 2.0 %collective-permute-start.6 = (bf16[64,1152]{1,0:T(8,128)(2,1)S(1)}, bf16[64,1152]{1,0:T(8,128)(2,1)S(1)}, u32[]{:S(2)}, u32[]{:S(2)}) collective-permute-start(bf16[64,1152]{1,0:T(8,128)(2,1)S(1)} %collective-permute-done.5.refs_7_), channel_id=1, source_target_pairs={{0,4},{1,5},{4,8},{5,9},{8,12},{9,13},{12,14},{13,15},{14,10},{15,... | collective-permute-start | bytes 442376 | tf_op jit(solution)/shard_map/ppermute | solution.py:36
  18.9 1.0 %collective-permute-done.3.refs_4_ = bf16[64,1152]{1,0:T(8,128)(2,1)S(1)} collective-permute-done((bf16[64,1152]{1,0:T(8,128)(2,1)S(1)}, bf16[64,1152]{1,0:T(8,128)(2,1)S(1)}, u32[]{:S(2)}, u32[]{:S(2)}) %collective-permute-start.3) | collective-permute-done | bytes 147488 | tf_op jit(solution)/shard_map/ppermute | solution.py:36
  19.9 2.0 %collective-permute-start.4 = (bf16[64,1152]{1,0:T(8,128)(2,1)S(1)}, bf16[64,1152]{1,0:T(8,128)(2,1)S(1)}, u32[]{:S(2)}, u32[]{:S(2)}) collective-permute-start(bf16[64,1152]{1,0:T(8,128)(2,1)S(1)} %collective-permute-done.3.refs_4_), channel_id=1, source_target_pairs={{0,4},{1,5},{4,8},{5,9},{8,12},{9,13},{12,14},{13,15},{14,10},{15,... | collective-permute-start | bytes 442376 | tf_op jit(solution)/shard_map/ppermute | solution.py:36
  21.9 1.2 %collective-permute-done.9.refs_6_ = bf16[64,1152]{1,0:T(8,128)(2,1)S(1)} collective-permute-done((bf16[64,1152]{1,0:T(8,128)(2,1)S(1)}, bf16[64,1152]{1,0:T(8,128)(2,1)S(1)}, u32[]{:S(2)}, u32[]{:S(2)}) %collective-permute-start.9) | collective-permute-done | bytes 147488 | tf_op jit(solution)/shard_map/ppermute | solution.py:36
  23.1 2.0 %collective-permute-start.7 = (bf16[64,1152]{1,0:T(8,128)(2,1)S(1)}, bf16[64,1152]{1,0:T(8,128)(2,1)S(1)}, u32[]{:S(2)}, u32[]{:S(2)}) collective-permute-start(bf16[64,1152]{1,0:T(8,128)(2,1)S(1)} %collective-permute-done.6.refs_5_), channel_id=1, source_target_pairs={{0,4},{1,5},{4,8},{5,9},{8,12},{9,13},{12,14},{13,15},{14,10},{15,... | collective-permute-start | bytes 442376 | tf_op jit(solution)/shard_map/ppermute | solution.py:36
  25.2 1.6 %copy-done.1 = bf16[128,8192]{1,0:T(8,128)(2,1)S(1)} copy-done((bf16[128,8192]{1,0:T(8,128)(2,1)S(1)}, bf16[128,8192]{1,0:T(8,128)(2,1)}, u32[]{:S(2)}) %copy-start.1) | copy-done | bytes 2097176
  26.8 2.9 %shard_map.64.refs_8_ = f32[256,128]{1,0:T(8,128)S(1)} custom-call(bf16[128,8192]{1,0:T(8,128)(2,1)S(1)} %copy-done.1, bf16[128,8192]{1,0:T(8,128)(2,1)S(1)} %collective-permute-done.1.refs_1_, bf16[128,28672]{1,0:T(8,128)(2,1)} %refs_2_.5, bf16[128,28672]{1,0:T(8,128)(2,1)} %collective-permute-done.2.refs_3_, bf16[64,1152]{1,0:T(8,128)(2,1)S(1)} %pad_maximum_fusion.refs_4_, ...), custom_call_target="tpu_custom_call" | custom-call | flops 226492416 | bytes 4423680 | tf_op jit(solution)/shard_map/pallas_call | solution.py:97
  29.7 1.6 %collective-permute-start.14 = (bf16[64,1152]{1,0:T(8,128)(2,1)S(1)}, bf16[64,1152]{1,0:T(8,128)(2,1)S(1)}, u32[]{:S(2)}, u32[]{:S(2)}) collective-permute-start(bf16[64,1152]{1,0:T(8,128)(2,1)S(1)} %collective-permute-done.4.refs_4_), channel_id=1, source_target_pairs={{0,4},{1,5},{4,8},{5,9},{8,12},{9,13},{12,14},{13,15},{14,10},{15,... | collective-permute-start | bytes 442376 | tf_op jit(solution)/shard_map/ppermute | solution.py:36
  31.8 2.3 %shard_map.65.refs_8_ = f32[256,128]{1,0:T(8,128)S(1)} custom-call(bf16[128,8192]{1,0:T(8,128)(2,1)S(1)} %copy-done.1, bf16[128,8192]{1,0:T(8,128)(2,1)S(1)} %collective-permute-done.1.refs_1_, bf16[128,28672]{1,0:T(8,128)(2,1)} %refs_2_.5, bf16[128,28672]{1,0:T(8,128)(2,1)} %collective-permute-done.2.refs_3_, ...), custom_call_target="tpu_custom_call" | custom-call | flops 150994944 | bytes 2949120 | tf_op jit(solution)/shard_map/pallas_call | solution.py:97
  34.2 2.4 %shard_map.66 = (f32[256,128]{1,0:T(8,128)S(1)}, bf16[256,2304]{1,0:T(8,128)(2,1)S(1)}) custom-call(bf16[128,8192]{1,0:T(8,128)(2,1)S(1)} %copy-done.1, bf16[128,8192]{1,0:T(8,128)(2,1)S(1)} %collective-permute-done.1.refs_1_, bf16[128,28672]{1,0:T(8,128)(2,1)} %refs_2_.5, bf16[128,28672]{1,0:T(8,128)(2,1)} %collective-permute-done.2.refs_3_, ...), custom_call_target="tpu_custom_call" | custom-call | flops 150994944 | bytes 2949120 | tf_op jit(solution)/shard_map/pallas_call | solution.py:97
  37.2 1.3 %collective-permute-done.16 = f32[256,128]{1,0:T(8,128)S(1)} collective-permute-done((f32[256,128]{1,0:T(8,128)S(1)}, f32[256,128]{1,0:T(8,128)S(1)}, u32[]{:S(2)}, u32[]{:S(2)}) %collective-permute-start.16) | collective-permute-done | bytes 131104 | tf_op jit(solution)/shard_map/ppermute | solution.py:40
  38.9 11.5 %all_to_all.10 = bf16[8,32,128]{2,1,0:T(8,128)(2,1)S(1)} all-to-all(bf16[8,32,128]{2,1,0:T(8,128)(2,1)S(1)} %broadcast_in_dim.14), channel_id=1, replica_groups={{0,2,4,6,8,10,12,14},{1,3,5,7,9,11,13,15},{16,18,20,22,24,26,28,30},{17..., dimensions={0} | all-to-all | bytes 131072 | tf_op jit(solution)/shard_map/all_to_all | solution.py:137
  51.2 9.1 %all_to_all.11 = bf16[16,2,256]{2,1,0:T(2,128)(2,1)S(1)} all-to-all(bf16[16,2,256]{2,1,0:T(2,128)(2,1)S(1)} %broadcast_in_dim.15), channel_id=1, replica_groups={{0,1,2,3,4,5,6,7,8,9,10,11,12,13,14,15},{16,17,18,19,20,21,22,23,24,25,..., dimensions={0} | all-to-all | bytes 32768 | tf_op jit(solution)/shard_map/all_to_all | solution.py:137
  60.3 0.7 %convolution_multiply_fusion.1 = f32[2,8]{1,0:T(2,128)} fusion(bf16[2,4096]{1,0:T(2,128)(2,1)S(1)} %bitcast.18, bf16[8,4096]{1,0:T(8,128)(2,1)S(1)} %copy-done.2), kind=kOutput, calls=%fused_computation.3 | convolution fusion | flops 131088 | bytes 81984 | tf_op jit(solution)/shard_map/dot_general | solution.py:20
  (34 shorter events, 3.2 us)
Async XLA Ops:
  0.0 50.5 %copy-start = (bf16[256,4096]{1,0:T(8,128)(2,1)S(1)}, bf16[256,4096]{1,0:T(8,128)(2,1)}, u32[]{:S(2)}) copy-start(bf16[256,4096]{1,0:T(8,128)(2,1)} %param.10) | copy-start | bytes 6291460
  0.0 25.2 %collective-permute-start.2 = (bf16[128,28672]{1,0:T(8,128)(2,1)}, bf16[128,28672]{1,0:T(8,128)(2,1)}, u32[]{:S(2)}, u32[]{:S(2)}) collective-permute-start(bf16[128,28672]{1,0:T(8,128)(2,1)} %refs_2_.5), channel_id=1, source_target_pairs={{0,1},{1,0},{2,3},{3,2},{4,5},{5,4},{6,7},{7,6},{8,9},{9,8},{10,11... | collective-permute-start | bytes 22020104 | tf_op jit(solution)/shard_map/ppermute | solution.py:40
  0.5 12.7 %collective-permute-start.1 = (bf16[128,8192]{1,0:T(8,128)(2,1)}, bf16[128,8192]{1,0:T(8,128)(2,1)S(1)}, u32[]{:S(2)}, u32[]{:S(2)}) collective-permute-start(bf16[128,8192]{1,0:T(8,128)(2,1)} %refs_0_.5), channel_id=1, source_target_pairs={{0,1},{1,0},{2,3},{3,2},{4,5},{5,4},{6,7},{7,6},{8,9},{9,8},{10,11... | collective-permute-start | bytes 6291464 | tf_op jit(solution)/shard_map/ppermute | solution.py:40
  2.4 7.0 %collective-permute-start = (bf16[64,1152]{1,0:T(8,128)(2,1)S(1)}, bf16[64,1152]{1,0:T(8,128)(2,1)S(1)}, u32[]{:S(2)}, u32[]{:S(2)}) collective-permute-start(bf16[64,1152]{1,0:T(8,128)(2,1)S(1)} %pad_maximum_fusion.refs_4_), channel_id=1, source_target_pairs={{0,4},{1,5},{4,8},{5,9},{8,12},{9,13},{12,14},{13,15},{14,10},{15,... | collective-permute-start | bytes 442376 | tf_op jit(solution)/shard_map/ppermute | solution.py:36
  6.4 6.8 %collective-permute-start.11 = (bf16[64,1152]{1,0:T(8,128)(2,1)S(1)}, bf16[64,1152]{1,0:T(8,128)(2,1)S(1)}, u32[]{:S(2)}, u32[]{:S(2)}) collective-permute-start(bf16[64,1152]{1,0:T(8,128)(2,1)S(1)} %slice.25.refs_5_), channel_id=1, source_target_pairs={{0,2},{1,3},{4,0},{5,1},{8,4},{9,5},{12,8},{13,9},{14,12},{15,13},... | collective-permute-start | bytes 442376 | tf_op jit(solution)/shard_map/ppermute | solution.py:36
  6.4 9.9 %collective-permute-start.8 = (bf16[64,1152]{1,0:T(8,128)(2,1)S(1)}, bf16[64,1152]{1,0:T(8,128)(2,1)S(1)}, u32[]{:S(2)}, u32[]{:S(2)}) collective-permute-start(bf16[64,1152]{1,0:T(8,128)(2,1)S(1)} %pad_maximum_fusion.refs_4_), channel_id=1, source_target_pairs={{0,2},{1,3},{4,0},{5,1},{8,4},{9,5},{12,8},{13,9},{14,12},{15,13},... | collective-permute-start | bytes 442376 | tf_op jit(solution)/shard_map/ppermute | solution.py:36
  9.4 7.0 %collective-permute-start.5 = (bf16[64,1152]{1,0:T(8,128)(2,1)S(1)}, bf16[64,1152]{1,0:T(8,128)(2,1)S(1)}, u32[]{:S(2)}, u32[]{:S(2)}) collective-permute-start(bf16[64,1152]{1,0:T(8,128)(2,1)S(1)} %slice.25.refs_5_), channel_id=1, source_target_pairs={{0,4},{1,5},{4,8},{5,9},{8,12},{9,13},{12,14},{13,15},{14,10},{15,... | collective-permute-start | bytes 442376 | tf_op jit(solution)/shard_map/ppermute | solution.py:36
  13.2 5.7 %collective-permute-start.12 = (bf16[64,1152]{1,0:T(8,128)(2,1)S(1)}, bf16[64,1152]{1,0:T(8,128)(2,1)S(1)}, u32[]{:S(2)}, u32[]{:S(2)}) collective-permute-start(bf16[64,1152]{1,0:T(8,128)(2,1)S(1)} %collective-permute-done.11.refs_9_), channel_id=1, source_target_pairs={{0,2},{1,3},{4,0},{5,1},{8,4},{9,5},{12,8},{13,9},{14,12},{15,13},... | collective-permute-start | bytes 442376 | tf_op jit(solution)/shard_map/ppermute | solution.py:36
  13.2 6.7 %collective-permute-start.3 = (bf16[64,1152]{1,0:T(8,128)(2,1)S(1)}, bf16[64,1152]{1,0:T(8,128)(2,1)S(1)}, u32[]{:S(2)}, u32[]{:S(2)}) collective-permute-start(bf16[64,1152]{1,0:T(8,128)(2,1)S(1)} %collective-permute-done.refs_6_), channel_id=1, source_target_pairs={{0,4},{1,5},{4,8},{5,9},{8,12},{9,13},{12,14},{13,15},{14,10},{15,... | collective-permute-start | bytes 442376 | tf_op jit(solution)/shard_map/ppermute | solution.py:36
  16.4 6.8 %collective-permute-start.9 = (bf16[64,1152]{1,0:T(8,128)(2,1)S(1)}, bf16[64,1152]{1,0:T(8,128)(2,1)S(1)}, u32[]{:S(2)}, u32[]{:S(2)}) collective-permute-start(bf16[64,1152]{1,0:T(8,128)(2,1)S(1)} %collective-permute-done.8.refs_8_), channel_id=1, source_target_pairs={{0,2},{1,3},{4,0},{5,1},{8,4},{9,5},{12,8},{13,9},{14,12},{15,13},... | collective-permute-start | bytes 442376 | tf_op jit(solution)/shard_map/ppermute | solution.py:36
  16.4 6.8 %collective-permute-start.6 = (bf16[64,1152]{1,0:T(8,128)(2,1)S(1)}, bf16[64,1152]{1,0:T(8,128)(2,1)S(1)}, u32[]{:S(2)}, u32[]{:S(2)}) collective-permute-start(bf16[64,1152]{1,0:T(8,128)(2,1)S(1)} %collective-permute-done.5.refs_7_), channel_id=1, source_target_pairs={{0,4},{1,5},{4,8},{5,9},{8,12},{9,13},{12,14},{13,15},{14,10},{15,... | collective-permute-start | bytes 442376 | tf_op jit(solution)/shard_map/ppermute | solution.py:36
  18.9 10.8 %collective-permute-start.13 = (bf16[64,1152]{1,0:T(8,128)(2,1)S(1)}, bf16[64,1152]{1,0:T(8,128)(2,1)S(1)}, u32[]{:S(2)}, u32[]{:S(2)}) collective-permute-start(bf16[64,1152]{1,0:T(8,128)(2,1)S(1)} %collective-permute-done.12.refs_7_), channel_id=1, source_target_pairs={{0,2},{1,3},{4,0},{5,1},{8,4},{9,5},{12,8},{13,9},{14,12},{15,13},... | collective-permute-start | bytes 442376 | tf_op jit(solution)/shard_map/ppermute | solution.py:36
  19.9 9.9 %collective-permute-start.4 = (bf16[64,1152]{1,0:T(8,128)(2,1)S(1)}, bf16[64,1152]{1,0:T(8,128)(2,1)S(1)}, u32[]{:S(2)}, u32[]{:S(2)}) collective-permute-start(bf16[64,1152]{1,0:T(8,128)(2,1)S(1)} %collective-permute-done.3.refs_4_), channel_id=1, source_target_pairs={{0,4},{1,5},{4,8},{5,9},{8,12},{9,13},{12,14},{13,15},{14,10},{15,... | collective-permute-start | bytes 442376 | tf_op jit(solution)/shard_map/ppermute | solution.py:36
  23.1 11.0 %collective-permute-start.10 = (bf16[64,1152]{1,0:T(8,128)(2,1)S(1)}, bf16[64,1152]{1,0:T(8,128)(2,1)S(1)}, u32[]{:S(2)}, u32[]{:S(2)}) collective-permute-start(bf16[64,1152]{1,0:T(8,128)(2,1)S(1)} %collective-permute-done.9.refs_6_), channel_id=1, source_target_pairs={{0,2},{1,3},{4,0},{5,1},{8,4},{9,5},{12,8},{13,9},{14,12},{15,13},... | collective-permute-start | bytes 442376 | tf_op jit(solution)/shard_map/ppermute | solution.py:36
  23.1 11.0 %collective-permute-start.7 = (bf16[64,1152]{1,0:T(8,128)(2,1)S(1)}, bf16[64,1152]{1,0:T(8,128)(2,1)S(1)}, u32[]{:S(2)}, u32[]{:S(2)}) collective-permute-start(bf16[64,1152]{1,0:T(8,128)(2,1)S(1)} %collective-permute-done.6.refs_5_), channel_id=1, source_target_pairs={{0,4},{1,5},{4,8},{5,9},{8,12},{9,13},{12,14},{13,15},{14,10},{15,... | collective-permute-start | bytes 442376 | tf_op jit(solution)/shard_map/ppermute | solution.py:36
  25.2 1.6 %copy-start.1 = (bf16[128,8192]{1,0:T(8,128)(2,1)S(1)}, bf16[128,8192]{1,0:T(8,128)(2,1)}, u32[]{:S(2)}) copy-start(bf16[128,8192]{1,0:T(8,128)(2,1)} %refs_0_.5) | copy-start | bytes 6291460
  29.7 6.9 %collective-permute-start.14 = (bf16[64,1152]{1,0:T(8,128)(2,1)S(1)}, bf16[64,1152]{1,0:T(8,128)(2,1)S(1)}, u32[]{:S(2)}, u32[]{:S(2)}) collective-permute-start(bf16[64,1152]{1,0:T(8,128)(2,1)S(1)} %collective-permute-done.4.refs_4_), channel_id=1, source_target_pairs={{0,4},{1,5},{4,8},{5,9},{8,12},{9,13},{12,14},{13,15},{14,10},{15,... | collective-permute-start | bytes 442376 | tf_op jit(solution)/shard_map/ppermute | solution.py:36
  31.3 5.2 %collective-permute-start.15 = (bf16[64,1152]{1,0:T(8,128)(2,1)S(1)}, bf16[64,1152]{1,0:T(8,128)(2,1)S(1)}, u32[]{:S(2)}, u32[]{:S(2)}) collective-permute-start(bf16[64,1152]{1,0:T(8,128)(2,1)S(1)} %collective-permute-done.13.refs_7_), channel_id=1, source_target_pairs={{0,2},{1,3},{4,0},{5,1},{8,4},{9,5},{12,8},{13,9},{14,12},{15,13},... | collective-permute-start | bytes 442376 | tf_op jit(solution)/shard_map/ppermute | solution.py:36
  36.6 23.7 %copy-start.2 = (bf16[8,4096]{1,0:T(8,128)(2,1)S(1)}, bf16[8,4096]{1,0:T(8,128)(2,1)}, u32[]{:S(2)}) copy-start(bf16[8,4096]{1,0:T(8,128)(2,1)} %param.11) | copy-start | bytes 196612
  37.1 1.4 %collective-permute-start.16 = (f32[256,128]{1,0:T(8,128)S(1)}, f32[256,128]{1,0:T(8,128)S(1)}, u32[]{:S(2)}, u32[]{:S(2)}) collective-permute-start(f32[256,128]{1,0:T(8,128)S(1)} %shard_map.67), channel_id=1, source_target_pairs={{0,1},{1,0},{2,3},{3,2},{4,5},{5,4},{6,7},{7,6},{8,9},{9,8},{10,11... | collective-permute-start | bytes 393224 | tf_op jit(solution)/shard_map/ppermute | solution.py:40

commit v5 on v3

--- a/solution.py
+++ b/solution.py
@@ -9,7 +9,7 @@
 from jax.sharding import PartitionSpec as P
 
 LEN = 1024
-LIMIT = 48
+LIMIT = 46
 NT = (((1,), (1,)), ((), ()))
 TN = (((0,), (0,)), ((), ()))
 VMEM = pl.BlockSpec(memory_space=pltpu.VMEM)
@@ -40,96 +40,91 @@
     return lax.ppermute(x, "dp", [(i, i ^ bit) for i in range(n)])
 
 
-def project_kernel(chips, offsets, widths, carry, fetch, *refs):
-    tokens, refs = refs[:4], refs[4:]
-    blocks, refs = refs[: 2 * len(offsets)], refs[2 * len(offsets) :]
-    if carry:
-        carried, refs = refs[0], refs[1:]
-    out, refs = refs[0], refs[1:]
-    if fetch is not None:
-        fetched, refs = refs[0], refs[1:]
-    buf, sems = refs
-    rows = tokens[0].shape[0]
-    rank, cut = blocks[0].shape
-    a_width, g_width = widths
+def gather_kernel(chips, a_width, act, grad, out, sems):
     core = lax.axis_index("dp") & 1
     copies = []
-    for i, offset in enumerate(offsets + ([] if fetch is None else [fetch])):
-        index = chip_behind(offset, chips) * 2 + core
-        to = buf.at[i] if i < len(offsets) else fetched
-        for k, ref in enumerate(tokens):
-            width, start = (a_width, 0) if k < 2 else (g_width, a_width)
+    for chip in range(chips):
+        block = 2 * chip + core
+        for k, (ref, start, stop) in enumerate(((act, 0, a_width), (grad, a_width, out.shape[2]))):
+            width = stop - start
             copies.append(
                 pltpu.make_async_copy(
-                    ref.at[:, pl.ds(pl.multiple_of(index * width, 128), width)],
-                    to.at[pl.ds(k % 2 * rows, rows), pl.ds(start, width)],
-                    sems.at[i, k],
+                    ref.at[:, pl.ds(pl.multiple_of(block * width, 128), width)],
+                    out.at[chip, :, pl.ds(start, width)],
+                    sems.at[chip, k],
                 )
             )
     for copy in copies:
         copy.start()
+    for copy in copies:
+        copy.wait()
+
+
+def gather_columns(act, grad, a_width, width, chips):
+    rows = act.shape[0]
+    return pl.pallas_call(
+        functools.partial(gather_kernel, chips, a_width),
+        out_shape=jax.ShapeDtypeStruct((chips, rows, width), act.dtype),
+        in_specs=[HBM, HBM],
+        out_specs=VMEM,
+        scratch_shapes=[pltpu.SemaphoreType.DMA((chips, 2))],
+        compiler_params=pltpu.CompilerParams(vmem_limit_bytes=LIMIT * 2**20),
+        cost_estimate=pl.CostEstimate(
+            flops=0, bytes_accessed=4 * chips * rows * width, transcendentals=0
+        ),
+    )(act, grad)
+
+
+def project_kernel(chips, offsets, a_width, carry, *refs):
+    mine, act, grad = refs[:3]
+    blocks, refs = refs[3 : 3 + 2 * len(offsets)], refs[3 + 2 * len(offsets) :]
+    out = refs[-1]
+    rank, cut = blocks[0].shape
+    width = mine.shape[2]
+    g_width = width - a_width
+    core = lax.axis_index("dp") & 1
     if carry:
-        a_sum, g_sum = carried[:, :rank], carried[:, rank:]
+        a_sum, g_sum = refs[0][:, :rank], refs[0][:, rank:]
     else:
         a_sum = g_sum = jnp.zeros((out.shape[0], rank), jnp.float32)
-    for i in range(len(offsets)):
-        for copy in copies[4 * i : 4 * i + 4]:
-            copy.wait()
-        a_sum += dot(buf[i, :, :a_width], blocks[2 * i][:, :a_width], NT)
-        g_sum += dot(buf[i, :, a_width:cut], blocks[2 * i][:, a_width:], NT)
-        g_sum += dot(buf[i, :, cut:], blocks[2 * i + 1][...], NT)
+    for i, offset in enumerate(offsets):
+        chip = chip_behind(offset, chips)
+        block = chip * 2 + core
+        a_at = pl.multiple_of(block * a_width, 128)
+        g_at = pl.multiple_of(block * g_width, 128)
+
+        def both(start, stop):
+            if stop <= a_width:
+                theirs = act[:, pl.ds(a_at + start, stop - start)]
+            else:
+                theirs = grad[:, pl.ds(g_at + start - a_width, stop - start)]
+            return jnp.concatenate([mine[chip, :, start:stop], theirs], axis=0)
+
+        a_sum += dot(both(0, a_width), blocks[2 * i][:, :a_width], NT)
+        g_sum += dot(both(a_width, cut), blocks[2 * i][:, a_width:], NT)
+        g_sum += dot(both(cut, width), blocks[2 * i + 1][...], NT)
     out[:, :rank] = a_sum
     out[:, rank:] = g_sum
-    for copy in copies[4 * len(offsets) :]:
-        copy.wait()
-
-
-def project(tokens, blocks, offsets, widths, chips, carry=None, fetch=None):
-    rows = tokens[0].shape[0]
+
+
+def project(tokens, blocks, offsets, a_width, carry=None):
+    chips, rows, width = tokens[0].shape
     count = len(offsets)
     rank = blocks[0][0].shape[0]
-    width = sum(widths)
     flat = [x for block in blocks for x in block]
     carried = () if carry is None else (carry,)
-    out_shape = [jax.ShapeDtypeStruct((2 * rows, 2 * rank), jnp.float32)]
-    if fetch is not None:
-        out_shape.append(jax.ShapeDtypeStruct((2 * rows, width), tokens[0].dtype))
     return pl.pallas_call(
-        functools.partial(project_kernel, chips, offsets, widths, carry is not None, fetch),
-        out_shape=out_shape,
-        in_specs=[HBM] * 4 + [VMEM] * (len(flat) + len(carried)),
-        out_specs=[VMEM] * len(out_shape),
-        scratch_shapes=[
-            pltpu.VMEM((count, 2 * rows, width), tokens[0].dtype),
-            pltpu.SemaphoreType.DMA((count + 1, 4)),
-        ],
-        compiler_params=pltpu.CompilerParams(vmem_limit_bytes=LIMIT * 2**20),
+        functools.partial(project_kernel, chips, offsets, a_width, carry is not None),
+        out_shape=jax.ShapeDtypeStruct((2 * rows, 2 * rank), jnp.float32),
+        in_specs=[VMEM] * (3 + len(flat) + len(carried)),
+        out_specs=VMEM,
+        compiler_params=pltpu.CompilerParams(vmem_limit_bytes=24 * 2**20),
         cost_estimate=pl.CostEstimate(
             flops=4 * count * rows * rank * width,
             bytes_accessed=count * (2 * rows + rank) * width * 2,
             transcendentals=0,
         ),
     )(*tokens, *flat, *carried)
-
-
-def finish_kernel(a_width, tokens, first, second, carried, out):
-    rank, cut = first.shape
-    out[:, :rank] = carried[:, :rank] + dot(tokens[:, :a_width], first[:, :a_width], NT)
-    out[:, rank:] = (
-        carried[:, rank:]
-        + dot(tokens[:, a_width:cut], first[:, a_width:], NT)
-        + dot(tokens[:, cut:], second[...], NT)
-    )
-
-
-def finish(tokens, block, a_width, carry):
-    return pl.pallas_call(
-        functools.partial(finish_kernel, a_width),
-        out_shape=jax.ShapeDtypeStruct(carry.shape, carry.dtype),
-        in_specs=[VMEM] * 4,
-        out_specs=VMEM,
-        compiler_params=pltpu.CompilerParams(vmem_limit_bytes=16 * 2**20),
-    )(tokens, *block, carry)
 
 
 def to_all(x, groups):
@@ -151,22 +146,27 @@
         jnp.concatenate([in_rows, out_rows[:, : cut - a_width]], axis=1),
         out_rows[:, cut - a_width :],
     )
+    activations_2 = swap(activations, 1, n)
+    out_grads_2 = swap(out_grads, 1, n)
     up, down = [own], [own]
-    for _ in range(chips // 2 - 1):
+    for i in range(chips // 2 - 1):
+        if i == 1:
+            mine = gather_columns(activations, out_grads, a_width, width, chips)
+            first, activations_2, mine = lax.optimization_barrier((up[-1][0], activations_2, mine))
+            up[-1] = (first, up[-1][1])
         up.append(tuple(ring(x, 1, chips) for x in up[-1]))
         down.append(tuple(ring(x, -1, chips) for x in down[-1]))
-    tokens = (activations, swap(activations, 1, n), out_grads, swap(out_grads, 1, n))
-
-    widths = (a_width, width - a_width)
-    run = functools.partial(project, tokens, widths=widths, chips=chips)
-    (total,) = run([own, up[1], down[1]], [0, 1, -1])
+    run = functools.partial(project, (mine, activations_2, out_grads_2), a_width=a_width)
+    near, offsets = [own], [0]
+    for i in range(1, chips // 2 - 1):
+        near += [up[i], down[i]]
+        offsets += [i, -i]
+    total = run(near, offsets)
     total, far_up, far_down = lax.optimization_barrier((total, up[-1][0], down[-1][1]))
     far = (ring(far_up, 1, chips), ring(far_down, -1, chips))
-    for i in range(2, chips // 2 - 1):
-        (total,) = run([up[i], down[i]], [i, -i], carry=total)
-    i = chips // 2 - 1
-    total, far_tokens = run([up[i], down[i]], [i, -i], carry=total, fetch=chips // 2)
-    total = finish(far_tokens, far, a_width, total)
+    last = chips // 2 - 1
+    total = run([up[last], down[last]], [last, -last], carry=total)
+    total = run([far], [chips // 2], carry=total)
     theirs = swap(total, 1, n)
     total = (total + jnp.concatenate([theirs[rows:], theirs[:rows]], axis=0)).astype(jnp.bfloat16)
 

time: 63.4 us -> 63.4 us (level)
  Pallas kernels: 8.17 us -> 10.1 us
  blocking collectives: 21.8 us -> 20 us
  starting transfers between devices: 18.9 us -> 17.7 us
  waiting for transfers between devices: 7.38 us -> 8.43 us
    pallas_call x4, Pallas kernels: 8.17 us -> 10.1 us  [the longest x3 7.89 us: project(): pl.pallas_call(functools.partial(project_kernel, chips, offsets, a_width,...]
    all_to_all x2, blocking collectives: 21.8 us -> 20 us  [to_all(): lax.all_to_all(copies, 'dp', 0, 0, axis_index_groups=groups, tiled=True)]
    ppermute x14, starting transfers between devices: 18.3 us -> 17.1 us  [ring(): return lax.ppermute(x, 'dp', pairs)]
    ppermute x14, waiting for transfers between devices: 6.04 us -> 7.09 us  [ring(): return lax.ppermute(x, 'dp', pairs)]
  transfers between devices with their start and end apart: 17 -> 17, of which waited for: 8 -> 6; matrix products, arithmetic and copies ran while one was open for 4% -> 4% of each run, Pallas kernels for 12% -> 13%
where the time goes in v5:
time: 63.4 us; the launch traced here: 63 us
  blocking collectives  20 us (32%)
  starting transfers between devices  17.7 us (28%)
  Pallas kernels  10.1 us (16%)
  waiting for transfers between devices  8.43 us (13%)
  local copies, waits for them, and re-layouts  3.74 us (6%)
  matrix products  1.61 us (3%)
  other arithmetic  1.26 us (2%)
    all_to_all x2, blocking collectives, to_all(): lax.all_to_all(copies, 'dp', 0, 0, axis_index_groups=groups, tiled=True)  20 us
    ppermute x14, starting transfers between devices, ring(): return lax.ppermute(x, 'dp', pairs)  17.1 us
    pallas_call x3, Pallas kernels, project(): pl.pallas_call(functools.partial(project_kernel, chips, offsets, a_width,...  7.89 us
    ppermute x14, waiting for transfers between devices, ring(): return lax.ppermute(x, 'dp', pairs)  7.09 us
    pallas_call x1, Pallas kernels, gather_columns(): pl.pallas_call(functools.partial(gather_kernel, chips, a_width), out_shap...  2.19 us
    dot_general x3, matrix products, dot(): return lax.dot_general(a, b, dims, preferred_element_type=jnp.float32)  1.61 us
    unnamed x6, local copies, waits for them, and re-layouts  1.6 us
    ppermute x3, waiting for transfers between devices, swap(): return lax.ppermute(x, 'dp', [(i, i ^ bit) for i in range(n)])  1.34 us
  transfers between devices with their start and end apart: 17, of which 6 were waited for; matrix products, arithmetic and copies ran while one was open for 4% of the time, Pallas kernels for 13%

profile of v5, /device:TPU:0, one launch (start us, length us, event | category | flops | bytes accessed | tf_op | source)
XLA Modules:
  0.0 63.0 jit_solution(14457198902515202816)
XLA Ops:
  0.5 1.0 %slice.24 = bf16[64,640]{1,0:T(8,128)(2,1)S(1)} slice(bf16[64,1792]{1,0:T(8,128)(2,1)} %bitcast.9), slice={[0:64], [0:640]} | slice | bytes 163840 | tf_op jit(solution)/shard_map/slice | solution.py:146
  1.5 0.9 %pad_maximum_fusion.refs_3_ = bf16[64,1152]{1,0:T(8,128)(2,1)S(1)} fusion(bf16[64,640]{1,0:T(8,128)(2,1)S(1)} %slice.24, bf16[64,512]{1,0:T(8,128)(2,1)} %bitcast.11), kind=kLoop, calls=%fused_computation.3 | loop fusion | flops 294912 | bytes 294912 | tf_op jit(solution)/shard_map/concatenate | solution.py:146
  2.4 3.1 %collective-permute-start = (bf16[64,1152]{1,0:T(8,128)(2,1)S(1)}, bf16[64,1152]{1,0:T(8,128)(2,1)S(1)}, u32[]{:S(2)}, u32[]{:S(2)}) collective-permute-start(bf16[64,1152]{1,0:T(8,128)(2,1)S(1)} %pad_maximum_fusion.refs_3_), channel_id=1, source_target_pairs={{0,4},{1,5},{4,8},{5,9},{8,12},{9,13},{12,14},{13,15},{14,10},{15,... | collective-permute-start | bytes 442376 | tf_op jit(solution)/shard_map/ppermute | solution.py:36
  5.5 0.9 %slice.25.refs_4_ = bf16[64,1152]{1,0:T(8,128)(2,1)S(1)} slice(bf16[64,1792]{1,0:T(8,128)(2,1)} %bitcast.10), slice={[0:64], [640:1792]} | slice | bytes 294912 | tf_op jit(solution)/shard_map/slice | solution.py:147
  6.4 2.0 %collective-permute-start.4 = (bf16[64,1152]{1,0:T(8,128)(2,1)S(1)}, bf16[64,1152]{1,0:T(8,128)(2,1)S(1)}, u32[]{:S(2)}, u32[]{:S(2)}) collective-permute-start(bf16[64,1152]{1,0:T(8,128)(2,1)S(1)} %pad_maximum_fusion.refs_3_), channel_id=1, source_target_pairs={{0,2},{1,3},{4,0},{5,1},{8,4},{9,5},{12,8},{13,9},{14,12},{15,13},... | collective-permute-start | bytes 442376 | tf_op jit(solution)/shard_map/ppermute | solution.py:36
  8.4 1.0 %collective-permute-done.refs_5_ = bf16[64,1152]{1,0:T(8,128)(2,1)S(1)} collective-permute-done((bf16[64,1152]{1,0:T(8,128)(2,1)S(1)}, bf16[64,1152]{1,0:T(8,128)(2,1)S(1)}, u32[]{:S(2)}, u32[]{:S(2)}) %collective-permute-start) | collective-permute-done | bytes 147488 | tf_op jit(solution)/shard_map/ppermute | solution.py:36
  9.4 1.8 %collective-permute-start.3 = (bf16[64,1152]{1,0:T(8,128)(2,1)S(1)}, bf16[64,1152]{1,0:T(8,128)(2,1)S(1)}, u32[]{:S(2)}, u32[]{:S(2)}) collective-permute-start(bf16[64,1152]{1,0:T(8,128)(2,1)S(1)} %slice.25.refs_4_), channel_id=1, source_target_pairs={{0,4},{1,5},{4,8},{5,9},{8,12},{9,13},{12,14},{13,15},{14,10},{15,... | collective-permute-start | bytes 442376 | tf_op jit(solution)/shard_map/ppermute | solution.py:36
  11.2 1.6 %copy-done.1 = bf16[128,8192]{1,0:T(8,128)(2,1)S(1)} copy-done((bf16[128,8192]{1,0:T(8,128)(2,1)S(1)}, bf16[128,8192]{1,0:T(8,128)(2,1)}, u32[]{:S(2)}) %copy-start.1) | copy-done | bytes 2097176
  12.8 2.2 %shard_map.64.refs_0_ = bf16[8,128,2304]{2,1,0:T(8,128)(2,1)S(1)} custom-call(bf16[128,8192]{1,0:T(8,128)(2,1)S(1)} %copy-done.1, bf16[128,28672]{1,0:T(8,128)(2,1)} %grad.1), custom_call_target="tpu_custom_call" | custom-call | bytes 9437184 | tf_op jit(solution)/shard_map/pallas_call | solution.py:65
  15.2 1.8 %collective-permute-start.6 = (bf16[64,1152]{1,0:T(8,128)(2,1)S(1)}, bf16[64,1152]{1,0:T(8,128)(2,1)S(1)}, u32[]{:S(2)}, u32[]{:S(2)}) collective-permute-start(bf16[64,1152]{1,0:T(8,128)(2,1)S(1)} %collective-permute-done.refs_5_), channel_id=1, source_target_pairs={{0,4},{1,5},{4,8},{5,9},{8,12},{9,13},{12,14},{13,15},{14,10},{15,... | collective-permute-start | bytes 442376 | tf_op jit(solution)/shard_map/ppermute | solution.py:36
  17.3 1.8 %collective-permute-start.7 = (bf16[64,1152]{1,0:T(8,128)(2,1)S(1)}, bf16[64,1152]{1,0:T(8,128)(2,1)S(1)}, u32[]{:S(2)}, u32[]{:S(2)}) collective-permute-start(bf16[64,1152]{1,0:T(8,128)(2,1)S(1)} %collective-permute-done.3.refs_6_), channel_id=1, source_target_pairs={{0,4},{1,5},{4,8},{5,9},{8,12},{9,13},{12,14},{13,15},{14,10},{15,... | collective-permute-start | bytes 442376 | tf_op jit(solution)/shard_map/ppermute | solution.py:36
  19.1 2.7 %collective-permute-done.9.refs_12_ = bf16[64,1152]{1,0:T(8,128)(2,1)S(1)} collective-permute-done((bf16[64,1152]{1,0:T(8,128)(2,1)S(1)}, bf16[64,1152]{1,0:T(8,128)(2,1)S(1)}, u32[]{:S(2)}, u32[]{:S(2)}) %collective-permute-start.9) | collective-permute-done | bytes 147488 | tf_op jit(solution)/shard_map/ppermute | solution.py:36
  22.0 1.8 %collective-permute-start.10 = (bf16[64,1152]{1,0:T(8,128)(2,1)S(1)}, bf16[64,1152]{1,0:T(8,128)(2,1)S(1)}, u32[]{:S(2)}, u32[]{:S(2)}) collective-permute-start(bf16[64,1152]{1,0:T(8,128)(2,1)S(1)} %collective-permute-done.6.refs_9_), channel_id=1, source_target_pairs={{0,4},{1,5},{4,8},{5,9},{8,12},{9,13},{12,14},{13,15},{14,10},{15,... | collective-permute-start | bytes 442376 | tf_op jit(solution)/shard_map/ppermute | solution.py:36
  23.8 1.1 %collective-permute-done.8.refs_11_ = bf16[64,1152]{1,0:T(8,128)(2,1)S(1)} collective-permute-done((bf16[64,1152]{1,0:T(8,128)(2,1)S(1)}, bf16[64,1152]{1,0:T(8,128)(2,1)S(1)}, u32[]{:S(2)}, u32[]{:S(2)}) %collective-permute-start.8) | collective-permute-done | bytes 147488 | tf_op jit(solution)/shard_map/ppermute | solution.py:36
  25.2 1.8 %collective-permute-start.14 = (bf16[64,1152]{1,0:T(8,128)(2,1)S(1)}, bf16[64,1152]{1,0:T(8,128)(2,1)S(1)}, u32[]{:S(2)}, u32[]{:S(2)}) collective-permute-start(bf16[64,1152]{1,0:T(8,128)(2,1)S(1)} %collective-permute-done.7.refs_10_), channel_id=1, source_target_pairs={{0,4},{1,5},{4,8},{5,9},{8,12},{9,13},{12,14},{13,15},{14,10},{15,... | collective-permute-start | bytes 442376 | tf_op jit(solution)/shard_map/ppermute | solution.py:36
  27.0 3.3 %shard_map.65.refs_7_ = f32[256,128]{1,0:T(8,128)S(1)} custom-call(bf16[8,128,2304]{2,1,0:T(8,128)(2,1)S(1)} %shard_map.64.refs_0_, bf16[128,8192]{1,0:T(8,128)(2,1)} %collective-permute-done.1.refs_1_, bf16[128,28672]{1,0:T(8,128)(2,1)S(1)} %collective-permute-done.2.refs_2_, bf16[64,1152]{1,0:T(8,128)(2,1)S(1)} %pad_maximum_fusion.refs_3_, ...), custom_call_target="tpu_custom_call" | custom-call | flops 377487360 | bytes 7372800 | tf_op jit(solution)/shard_map/pallas_call | solution.py:116
  30.4 1.6 %collective-permute-start.12 = (bf16[64,1152]{1,0:T(8,128)(2,1)S(1)}, bf16[64,1152]{1,0:T(8,128)(2,1)S(1)}, u32[]{:S(2)}, u32[]{:S(2)}) collective-permute-start(bf16[64,1152]{1,0:T(8,128)(2,1)S(1)} %collective-permute-done.10.refs_3_), channel_id=1, source_target_pairs={{0,4},{1,5},{4,8},{5,9},{8,12},{9,13},{12,14},{13,15},{14,10},{15,... | collective-permute-start | bytes 442376 | tf_op jit(solution)/shard_map/ppermute | solution.py:36
  32.4 2.4 %shard_map.66.refs_5_ = f32[256,128]{1,0:T(8,128)S(1)} custom-call(bf16[8,128,2304]{2,1,0:T(8,128)(2,1)S(1)} %shard_map.64.refs_0_, bf16[128,8192]{1,0:T(8,128)(2,1)} %collective-permute-done.1.refs_1_, bf16[128,28672]{1,0:T(8,128)(2,1)S(1)} %collective-permute-done.2.refs_2_, bf16[64,1152]{1,0:T(8,128)(2,1)S(1)} %collective-permute-done.10.refs_3_, ...), custom_call_target="tpu_custom_call" | custom-call | flops 150994944 | bytes 2949120 | tf_op jit(solution)/shard_map/pallas_call | solution.py:116
  35.6 1.6 %collective-permute-done.13.refs_4_ = bf16[64,1152]{1,0:T(8,128)(2,1)S(1)} collective-permute-done((bf16[64,1152]{1,0:T(8,128)(2,1)S(1)}, bf16[64,1152]{1,0:T(8,128)(2,1)S(1)}, u32[]{:S(2)}, u32[]{:S(2)}) %collective-permute-start.13) | collective-permute-done | bytes 147488 | tf_op jit(solution)/shard_map/ppermute | solution.py:36
  37.1 2.1 %shard_map.67 = f32[256,128]{1,0:T(8,128)S(1)} custom-call(bf16[8,128,2304]{2,1,0:T(8,128)(2,1)S(1)} %shard_map.64.refs_0_, bf16[128,8192]{1,0:T(8,128)(2,1)} %collective-permute-done.1.refs_1_, bf16[128,28672]{1,0:T(8,128)(2,1)S(1)} %collective-permute-done.2.refs_2_, bf16[64,1152]{1,0:T(8,128)(2,1)S(1)} %collective-permute-done.12.refs_3_, ...), custom_call_target="tpu_custom_call" | custom-call | flops 75497472 | bytes 1474560 | tf_op jit(solution)/shard_map/pallas_call | solution.py:116
  39.4 1.3 %collective-permute-done.16 = f32[256,128]{1,0:T(8,128)S(1)} collective-permute-done((f32[256,128]{1,0:T(8,128)S(1)}, f32[256,128]{1,0:T(8,128)S(1)}, u32[]{:S(2)}, u32[]{:S(2)}) %collective-permute-start.16) | collective-permute-done | bytes 131104 | tf_op jit(solution)/shard_map/ppermute | solution.py:40
  41.1 10.9 %all_to_all.10 = f32[8,1,4096]{2,1,0:T(1,128)S(1)} all-to-all(f32[8,1,4096]{2,1,0:T(1,128)S(1)} %broadcast_in_dim.4), channel_id=1, replica_groups={{0,2,4,6,8,10,12,14},{1,3,5,7,9,11,13,15},{16,18,20,22,24,26,28,30},{17..., dimensions={0} | all-to-all | bytes 262144 | tf_op jit(solution)/shard_map/all_to_all | solution.py:132
  53.2 9.1 %all_to_all.11 = bf16[16,2,256]{2,1,0:T(2,128)(2,1)S(1)} all-to-all(bf16[16,2,256]{2,1,0:T(2,128)(2,1)S(1)} %broadcast_in_dim.5), channel_id=1, replica_groups={{0,1,2,3,4,5,6,7,8,9,10,11,12,13,14,15},{16,17,18,19,20,21,22,23,24,25,..., dimensions={0} | all-to-all | bytes 32768 | tf_op jit(solution)/shard_map/all_to_all | solution.py:132
  62.3 0.7 %convolution_multiply_fusion.1 = f32[2,8]{1,0:T(2,128)} fusion(bf16[2,4096]{1,0:T(2,128)(2,1)S(1)} %bitcast.12, bf16[8,4096]{1,0:T(8,128)(2,1)S(1)} %copy-done.2), kind=kOutput, calls=%fused_computation.2 | convolution fusion | flops 131088 | bytes 81984 | tf_op jit(solution)/shard_map/dot_general | solution.py:20
  (36 shorter events, 4.3 us)
Async XLA Ops:
  0.0 52.5 %copy-start = (bf16[256,4096]{1,0:T(8,128)(2,1)S(1)}, bf16[256,4096]{1,0:T(8,128)(2,1)}, u32[]{:S(2)}) copy-start(bf16[256,4096]{1,0:T(8,128)(2,1)} %param.10) | copy-start | bytes 6291460
  0.0 27.0 %collective-permute-start.2 = (bf16[128,28672]{1,0:T(8,128)(2,1)}, bf16[128,28672]{1,0:T(8,128)(2,1)S(1)}, u32[]{:S(2)}, u32[]{:S(2)}) collective-permute-start(bf16[128,28672]{1,0:T(8,128)(2,1)} %grad.1), channel_id=1, source_target_pairs={{0,1},{1,0},{2,3},{3,2},{4,5},{5,4},{6,7},{7,6},{8,9},{9,8},{10,11... | collective-permute-start | bytes 22020104 | tf_op jit(solution)/shard_map/ppermute | solution.py:40
  0.5 14.8 %collective-permute-start.1 = (bf16[128,8192]{1,0:T(8,128)(2,1)}, bf16[128,8192]{1,0:T(8,128)(2,1)}, u32[]{:S(2)}, u32[]{:S(2)}) collective-permute-start(bf16[128,8192]{1,0:T(8,128)(2,1)} %act.1), channel_id=1, source_target_pairs={{0,1},{1,0},{2,3},{3,2},{4,5},{5,4},{6,7},{7,6},{8,9},{9,8},{10,11... | collective-permute-start | bytes 6291464 | tf_op jit(solution)/shard_map/ppermute | solution.py:40
  2.4 7.0 %collective-permute-start = (bf16[64,1152]{1,0:T(8,128)(2,1)S(1)}, bf16[64,1152]{1,0:T(8,128)(2,1)S(1)}, u32[]{:S(2)}, u32[]{:S(2)}) collective-permute-start(bf16[64,1152]{1,0:T(8,128)(2,1)S(1)} %pad_maximum_fusion.refs_3_), channel_id=1, source_target_pairs={{0,4},{1,5},{4,8},{5,9},{8,12},{9,13},{12,14},{13,15},{14,10},{15,... | collective-permute-start | bytes 442376 | tf_op jit(solution)/shard_map/ppermute | solution.py:36
  6.4 8.6 %collective-permute-start.5 = (bf16[64,1152]{1,0:T(8,128)(2,1)S(1)}, bf16[64,1152]{1,0:T(8,128)(2,1)S(1)}, u32[]{:S(2)}, u32[]{:S(2)}) collective-permute-start(bf16[64,1152]{1,0:T(8,128)(2,1)S(1)} %slice.25.refs_4_), channel_id=1, source_target_pairs={{0,2},{1,3},{4,0},{5,1},{8,4},{9,5},{12,8},{13,9},{14,12},{15,13},... | collective-permute-start | bytes 442376 | tf_op jit(solution)/shard_map/ppermute | solution.py:36
  6.4 10.6 %collective-permute-start.4 = (bf16[64,1152]{1,0:T(8,128)(2,1)S(1)}, bf16[64,1152]{1,0:T(8,128)(2,1)S(1)}, u32[]{:S(2)}, u32[]{:S(2)}) collective-permute-start(bf16[64,1152]{1,0:T(8,128)(2,1)S(1)} %pad_maximum_fusion.refs_3_), channel_id=1, source_target_pairs={{0,2},{1,3},{4,0},{5,1},{8,4},{9,5},{12,8},{13,9},{14,12},{15,13},... | collective-permute-start | bytes 442376 | tf_op jit(solution)/shard_map/ppermute | solution.py:36
  9.4 7.9 %collective-permute-start.3 = (bf16[64,1152]{1,0:T(8,128)(2,1)S(1)}, bf16[64,1152]{1,0:T(8,128)(2,1)S(1)}, u32[]{:S(2)}, u32[]{:S(2)}) collective-permute-start(bf16[64,1152]{1,0:T(8,128)(2,1)S(1)} %slice.25.refs_4_), channel_id=1, source_target_pairs={{0,4},{1,5},{4,8},{5,9},{8,12},{9,13},{12,14},{13,15},{14,10},{15,... | collective-permute-start | bytes 442376 | tf_op jit(solution)/shard_map/ppermute | solution.py:36
  11.2 1.6 %copy-start.1 = (bf16[128,8192]{1,0:T(8,128)(2,1)S(1)}, bf16[128,8192]{1,0:T(8,128)(2,1)}, u32[]{:S(2)}) copy-start(bf16[128,8192]{1,0:T(8,128)(2,1)} %act.1) | copy-start | bytes 6291460
  15.0 6.8 %collective-permute-start.9 = (bf16[64,1152]{1,0:T(8,128)(2,1)S(1)}, bf16[64,1152]{1,0:T(8,128)(2,1)S(1)}, u32[]{:S(2)}, u32[]{:S(2)}) collective-permute-start(bf16[64,1152]{1,0:T(8,128)(2,1)S(1)} %collective-permute-done.5.refs_8_), channel_id=1, source_target_pairs={{0,2},{1,3},{4,0},{5,1},{8,4},{9,5},{12,8},{13,9},{14,12},{15,13},... | collective-permute-start | bytes 442376 | tf_op jit(solution)/shard_map/ppermute | solution.py:36
  15.2 6.8 %collective-permute-start.6 = (bf16[64,1152]{1,0:T(8,128)(2,1)S(1)}, bf16[64,1152]{1,0:T(8,128)(2,1)S(1)}, u32[]{:S(2)}, u32[]{:S(2)}) collective-permute-start(bf16[64,1152]{1,0:T(8,128)(2,1)S(1)} %collective-permute-done.refs_5_), channel_id=1, source_target_pairs={{0,4},{1,5},{4,8},{5,9},{8,12},{9,13},{12,14},{13,15},{14,10},{15,... | collective-permute-start | bytes 442376 | tf_op jit(solution)/shard_map/ppermute | solution.py:36
  17.0 7.9 %collective-permute-start.8 = (bf16[64,1152]{1,0:T(8,128)(2,1)S(1)}, bf16[64,1152]{1,0:T(8,128)(2,1)S(1)}, u32[]{:S(2)}, u32[]{:S(2)}) collective-permute-start(bf16[64,1152]{1,0:T(8,128)(2,1)S(1)} %collective-permute-done.4.refs_7_), channel_id=1, source_target_pairs={{0,2},{1,3},{4,0},{5,1},{8,4},{9,5},{12,8},{13,9},{14,12},{15,13},... | collective-permute-start | bytes 442376 | tf_op jit(solution)/shard_map/ppermute | solution.py:36
  17.3 7.9 %collective-permute-start.7 = (bf16[64,1152]{1,0:T(8,128)(2,1)S(1)}, bf16[64,1152]{1,0:T(8,128)(2,1)S(1)}, u32[]{:S(2)}, u32[]{:S(2)}) collective-permute-start(bf16[64,1152]{1,0:T(8,128)(2,1)S(1)} %collective-permute-done.3.refs_6_), channel_id=1, source_target_pairs={{0,4},{1,5},{4,8},{5,9},{8,12},{9,13},{12,14},{13,15},{14,10},{15,... | collective-permute-start | bytes 442376 | tf_op jit(solution)/shard_map/ppermute | solution.py:36
  21.8 8.5 %collective-permute-start.11 = (bf16[64,1152]{1,0:T(8,128)(2,1)S(1)}, bf16[64,1152]{1,0:T(8,128)(2,1)S(1)}, u32[]{:S(2)}, u32[]{:S(2)}) collective-permute-start(bf16[64,1152]{1,0:T(8,128)(2,1)S(1)} %collective-permute-done.9.refs_12_), channel_id=1, source_target_pairs={{0,2},{1,3},{4,0},{5,1},{8,4},{9,5},{12,8},{13,9},{14,12},{15,13},... | collective-permute-start | bytes 442376 | tf_op jit(solution)/shard_map/ppermute | solution.py:36
  22.0 8.3 %collective-permute-start.10 = (bf16[64,1152]{1,0:T(8,128)(2,1)S(1)}, bf16[64,1152]{1,0:T(8,128)(2,1)S(1)}, u32[]{:S(2)}, u32[]{:S(2)}) collective-permute-start(bf16[64,1152]{1,0:T(8,128)(2,1)S(1)} %collective-permute-done.6.refs_9_), channel_id=1, source_target_pairs={{0,4},{1,5},{4,8},{5,9},{8,12},{9,13},{12,14},{13,15},{14,10},{15,... | collective-permute-start | bytes 442376 | tf_op jit(solution)/shard_map/ppermute | solution.py:36
  25.0 7.5 %collective-permute-start.15 = (bf16[64,1152]{1,0:T(8,128)(2,1)S(1)}, bf16[64,1152]{1,0:T(8,128)(2,1)S(1)}, u32[]{:S(2)}, u32[]{:S(2)}) collective-permute-start(bf16[64,1152]{1,0:T(8,128)(2,1)S(1)} %collective-permute-done.8.refs_11_), channel_id=1, source_target_pairs={{0,2},{1,3},{4,0},{5,1},{8,4},{9,5},{12,8},{13,9},{14,12},{15,13},... | collective-permute-start | bytes 442376 | tf_op jit(solution)/shard_map/ppermute | solution.py:36
  25.2 7.3 %collective-permute-start.14 = (bf16[64,1152]{1,0:T(8,128)(2,1)S(1)}, bf16[64,1152]{1,0:T(8,128)(2,1)S(1)}, u32[]{:S(2)}, u32[]{:S(2)}) collective-permute-start(bf16[64,1152]{1,0:T(8,128)(2,1)S(1)} %collective-permute-done.7.refs_10_), channel_id=1, source_target_pairs={{0,4},{1,5},{4,8},{5,9},{8,12},{9,13},{12,14},{13,15},{14,10},{15,... | collective-permute-start | bytes 442376 | tf_op jit(solution)/shard_map/ppermute | solution.py:36
  30.4 5.2 %collective-permute-start.12 = (bf16[64,1152]{1,0:T(8,128)(2,1)S(1)}, bf16[64,1152]{1,0:T(8,128)(2,1)S(1)}, u32[]{:S(2)}, u32[]{:S(2)}) collective-permute-start(bf16[64,1152]{1,0:T(8,128)(2,1)S(1)} %collective-permute-done.10.refs_3_), channel_id=1, source_target_pairs={{0,4},{1,5},{4,8},{5,9},{8,12},{9,13},{12,14},{13,15},{14,10},{15,... | collective-permute-start | bytes 442376 | tf_op jit(solution)/shard_map/ppermute | solution.py:36
  32.0 5.1 %collective-permute-start.13 = (bf16[64,1152]{1,0:T(8,128)(2,1)S(1)}, bf16[64,1152]{1,0:T(8,128)(2,1)S(1)}, u32[]{:S(2)}, u32[]{:S(2)}) collective-permute-start(bf16[64,1152]{1,0:T(8,128)(2,1)S(1)} %collective-permute-done.11.refs_6_), channel_id=1, source_target_pairs={{0,2},{1,3},{4,0},{5,1},{8,4},{9,5},{12,8},{13,9},{14,12},{15,13},... | collective-permute-start | bytes 442376 | tf_op jit(solution)/shard_map/ppermute | solution.py:36
  39.3 23.0 %copy-start.2 = (bf16[8,4096]{1,0:T(8,128)(2,1)S(1)}, bf16[8,4096]{1,0:T(8,128)(2,1)}, u32[]{:S(2)}) copy-start(bf16[8,4096]{1,0:T(8,128)(2,1)} %param.11) | copy-start | bytes 196612
  39.3 1.4 %collective-permute-start.16 = (f32[256,128]{1,0:T(8,128)S(1)}, f32[256,128]{1,0:T(8,128)S(1)}, u32[]{:S(2)}, u32[]{:S(2)}) collective-permute-start(f32[256,128]{1,0:T(8,128)S(1)} %shard_map.67), channel_id=1, source_target_pairs={{0,1},{1,0},{2,3},{3,2},{4,5},{5,4},{6,7},{7,6},{8,9},{9,8},{10,11... | collective-permute-start | bytes 393224 | tf_op jit(solution)/shard_map/ppermute | solution.py:40

commit v6 on v5

--- a/solution.py
+++ b/solution.py
@@ -9,7 +9,7 @@
 from jax.sharding import PartitionSpec as P
 
 LEN = 1024
-LIMIT = 46
+LIMIT = 42
 NT = (((1,), (1,)), ((), ()))
 TN = (((0,), (0,)), ((), ()))
 VMEM = pl.BlockSpec(memory_space=pltpu.VMEM)

time: 63.4 us -> 62.1 us (0.979)
  Pallas kernels: 10.1 us -> 5.31 us
  starting transfers between devices: 17.7 us -> 19 us
  waiting for transfers between devices: 8.43 us -> 9.72 us
  blocking collectives: 20 us -> 21 us
    pallas_call x3, Pallas kernels: 7.89 us -> 3.12 us  [project(): pl.pallas_call(functools.partial(project_kernel, chips, offsets, a_width,...]
    ppermute x14, waiting for transfers between devices: 7.09 us -> 8.38 us  [ring(): return lax.ppermute(x, 'dp', pairs)]
    ppermute x14, starting transfers between devices: 17.1 us -> 18.4 us  [ring(): return lax.ppermute(x, 'dp', pairs)]
    all_to_all x2, blocking collectives: 20 us -> 21 us  [to_all(): lax.all_to_all(copies, 'dp', 0, 0, axis_index_groups=groups, tiled=True)]
  transfers between devices with their start and end apart: 17 -> 17, of which waited for: 6 -> 8; matrix products, arithmetic and copies ran while one was open for 4% -> 4% of each run, Pallas kernels for 13% -> 8%
where the time goes in v6:
time: 62.1 us; the launch traced here: 61.8 us
  blocking collectives  21 us (34%)
  starting transfers between devices  19 us (31%)
  waiting for transfers between devices  9.72 us (16%)
  Pallas kernels  5.31 us (9%)
  local copies, waits for them, and re-layouts  3.74 us (6%)
  matrix products  1.61 us (3%)
  other arithmetic  1.26 us (2%)
    all_to_all x2, blocking collectives, to_all(): lax.all_to_all(copies, 'dp', 0, 0, axis_index_groups=groups, tiled=True)  21 us
    ppermute x14, starting transfers between devices, ring(): return lax.ppermute(x, 'dp', pairs)  18.4 us
    ppermute x14, waiting for transfers between devices, ring(): return lax.ppermute(x, 'dp', pairs)  8.38 us
    pallas_call x3, Pallas kernels, project(): pl.pallas_call(functools.partial(project_kernel, chips, offsets, a_width,...  3.12 us
    pallas_call x1, Pallas kernels, gather_columns(): pl.pallas_call(functools.partial(gather_kernel, chips, a_width), out_shap...  2.19 us
    dot_general x3, matrix products, dot(): return lax.dot_general(a, b, dims, preferred_element_type=jnp.float32)  1.61 us
    unnamed x6, local copies, waits for them, and re-layouts  1.6 us
    ppermute x3, waiting for transfers between devices, swap(): return lax.ppermute(x, 'dp', [(i, i ^ bit) for i in range(n)])  1.34 us
  transfers between devices with their start and end apart: 17, of which 8 were waited for; matrix products, arithmetic and copies ran while one was open for 4% of the time, Pallas kernels for 8%

profile of v6, /device:TPU:0, one launch (start us, length us, event | category | flops | bytes accessed | tf_op | source)
XLA Modules:
  0.0 61.8 jit_solution(16961988700251348511)
XLA Ops:
  0.5 1.0 %slice.24 = bf16[64,640]{1,0:T(8,128)(2,1)S(1)} slice(bf16[64,1792]{1,0:T(8,128)(2,1)} %bitcast.9), slice={[0:64], [0:640]} | slice | bytes 163840 | tf_op jit(solution)/shard_map/slice | solution.py:146
  1.5 0.9 %pad_maximum_fusion.refs_3_ = bf16[64,1152]{1,0:T(8,128)(2,1)S(1)} fusion(bf16[64,640]{1,0:T(8,128)(2,1)S(1)} %slice.24, bf16[64,512]{1,0:T(8,128)(2,1)} %bitcast.11), kind=kLoop, calls=%fused_computation.3 | loop fusion | flops 294912 | bytes 294912 | tf_op jit(solution)/shard_map/concatenate | solution.py:146
  2.4 3.1 %collective-permute-start = (bf16[64,1152]{1,0:T(8,128)(2,1)S(1)}, bf16[64,1152]{1,0:T(8,128)(2,1)S(1)}, u32[]{:S(2)}, u32[]{:S(2)}) collective-permute-start(bf16[64,1152]{1,0:T(8,128)(2,1)S(1)} %pad_maximum_fusion.refs_3_), channel_id=1, source_target_pairs={{0,4},{1,5},{4,8},{5,9},{8,12},{9,13},{12,14},{13,15},{14,10},{15,... | collective-permute-start | bytes 442376 | tf_op jit(solution)/shard_map/ppermute | solution.py:36
  5.5 0.9 %slice.25.refs_4_ = bf16[64,1152]{1,0:T(8,128)(2,1)S(1)} slice(bf16[64,1792]{1,0:T(8,128)(2,1)} %bitcast.10), slice={[0:64], [640:1792]} | slice | bytes 294912 | tf_op jit(solution)/shard_map/slice | solution.py:147
  6.4 2.0 %collective-permute-start.4 = (bf16[64,1152]{1,0:T(8,128)(2,1)S(1)}, bf16[64,1152]{1,0:T(8,128)(2,1)S(1)}, u32[]{:S(2)}, u32[]{:S(2)}) collective-permute-start(bf16[64,1152]{1,0:T(8,128)(2,1)S(1)} %pad_maximum_fusion.refs_3_), channel_id=1, source_target_pairs={{0,2},{1,3},{4,0},{5,1},{8,4},{9,5},{12,8},{13,9},{14,12},{15,13},... | collective-permute-start | bytes 442376 | tf_op jit(solution)/shard_map/ppermute | solution.py:36
  8.4 1.0 %collective-permute-done.refs_5_ = bf16[64,1152]{1,0:T(8,128)(2,1)S(1)} collective-permute-done((bf16[64,1152]{1,0:T(8,128)(2,1)S(1)}, bf16[64,1152]{1,0:T(8,128)(2,1)S(1)}, u32[]{:S(2)}, u32[]{:S(2)}) %collective-permute-start) | collective-permute-done | bytes 147488 | tf_op jit(solution)/shard_map/ppermute | solution.py:36
  9.4 1.8 %collective-permute-start.3 = (bf16[64,1152]{1,0:T(8,128)(2,1)S(1)}, bf16[64,1152]{1,0:T(8,128)(2,1)S(1)}, u32[]{:S(2)}, u32[]{:S(2)}) collective-permute-start(bf16[64,1152]{1,0:T(8,128)(2,1)S(1)} %slice.25.refs_4_), channel_id=1, source_target_pairs={{0,4},{1,5},{4,8},{5,9},{8,12},{9,13},{12,14},{13,15},{14,10},{15,... | collective-permute-start | bytes 442376 | tf_op jit(solution)/shard_map/ppermute | solution.py:36
  11.2 1.6 %copy-done.1 = bf16[128,8192]{1,0:T(8,128)(2,1)S(1)} copy-done((bf16[128,8192]{1,0:T(8,128)(2,1)S(1)}, bf16[128,8192]{1,0:T(8,128)(2,1)}, u32[]{:S(2)}) %copy-start.1) | copy-done | bytes 2097176
  12.8 2.2 %shard_map.64.refs_0_ = bf16[8,128,2304]{2,1,0:T(8,128)(2,1)S(1)} custom-call(bf16[128,8192]{1,0:T(8,128)(2,1)S(1)} %copy-done.1, bf16[128,28672]{1,0:T(8,128)(2,1)} %grad.1), custom_call_target="tpu_custom_call" | custom-call | bytes 9437184 | tf_op jit(solution)/shard_map/pallas_call | solution.py:65
  15.2 2.7 %collective-permute-start.6 = (bf16[64,1152]{1,0:T(8,128)(2,1)S(1)}, bf16[64,1152]{1,0:T(8,128)(2,1)S(1)}, u32[]{:S(2)}, u32[]{:S(2)}) collective-permute-start(bf16[64,1152]{1,0:T(8,128)(2,1)S(1)} %collective-permute-done.refs_5_), channel_id=1, source_target_pairs={{0,4},{1,5},{4,8},{5,9},{8,12},{9,13},{12,14},{13,15},{14,10},{15,... | collective-permute-start | bytes 442376 | tf_op jit(solution)/shard_map/ppermute | solution.py:36
  17.9 2.0 %collective-permute-start.7 = (bf16[64,1152]{1,0:T(8,128)(2,1)S(1)}, bf16[64,1152]{1,0:T(8,128)(2,1)S(1)}, u32[]{:S(2)}, u32[]{:S(2)}) collective-permute-start(bf16[64,1152]{1,0:T(8,128)(2,1)S(1)} %collective-permute-done.3.refs_6_), channel_id=1, source_target_pairs={{0,4},{1,5},{4,8},{5,9},{8,12},{9,13},{12,14},{13,15},{14,10},{15,... | collective-permute-start | bytes 442376 | tf_op jit(solution)/shard_map/ppermute | solution.py:36
  20.4 2.1 %collective-permute-done.6.refs_9_ = bf16[64,1152]{1,0:T(8,128)(2,1)S(1)} collective-permute-done((bf16[64,1152]{1,0:T(8,128)(2,1)S(1)}, bf16[64,1152]{1,0:T(8,128)(2,1)S(1)}, u32[]{:S(2)}, u32[]{:S(2)}) %collective-permute-start.6) | collective-permute-done | bytes 147488 | tf_op jit(solution)/shard_map/ppermute | solution.py:36
  22.5 2.1 %collective-permute-start.10 = (bf16[64,1152]{1,0:T(8,128)(2,1)S(1)}, bf16[64,1152]{1,0:T(8,128)(2,1)S(1)}, u32[]{:S(2)}, u32[]{:S(2)}) collective-permute-start(bf16[64,1152]{1,0:T(8,128)(2,1)S(1)} %collective-permute-done.6.refs_9_), channel_id=1, source_target_pairs={{0,4},{1,5},{4,8},{5,9},{8,12},{9,13},{12,14},{13,15},{14,10},{15,... | collective-permute-start | bytes 442376 | tf_op jit(solution)/shard_map/ppermute | solution.py:36
  24.6 1.0 %collective-permute-done.7.refs_10_ = bf16[64,1152]{1,0:T(8,128)(2,1)S(1)} collective-permute-done((bf16[64,1152]{1,0:T(8,128)(2,1)S(1)}, bf16[64,1152]{1,0:T(8,128)(2,1)S(1)}, u32[]{:S(2)}, u32[]{:S(2)}) %collective-permute-start.7) | collective-permute-done | bytes 147488 | tf_op jit(solution)/shard_map/ppermute | solution.py:36
  25.6 2.1 %collective-permute-start.14 = (bf16[64,1152]{1,0:T(8,128)(2,1)S(1)}, bf16[64,1152]{1,0:T(8,128)(2,1)S(1)}, u32[]{:S(2)}, u32[]{:S(2)}) collective-permute-start(bf16[64,1152]{1,0:T(8,128)(2,1)S(1)} %collective-permute-done.7.refs_10_), channel_id=1, source_target_pairs={{0,4},{1,5},{4,8},{5,9},{8,12},{9,13},{12,14},{13,15},{14,10},{15,... | collective-permute-start | bytes 442376 | tf_op jit(solution)/shard_map/ppermute | solution.py:36
  27.8 1.8 %shard_map.65.refs_7_ = f32[256,128]{1,0:T(8,128)S(1)} custom-call(bf16[8,128,2304]{2,1,0:T(8,128)(2,1)S(1)} %shard_map.64.refs_0_, bf16[128,8192]{1,0:T(8,128)(2,1)S(1)} %collective-permute-done.1.refs_1_, bf16[128,28672]{1,0:T(8,128)(2,1)S(1)} %collective-permute-done.2.refs_2_, bf16[64,1152]{1,0:T(8,128)(2,1)S(1)} %pad_maximum_fusion.refs_3_, ...), custom_call_target="tpu_custom_call" | custom-call | flops 377487360 | bytes 7372800 | tf_op jit(solution)/shard_map/pallas_call | solution.py:116
  29.5 1.8 %collective-permute-start.12 = (bf16[64,1152]{1,0:T(8,128)(2,1)S(1)}, bf16[64,1152]{1,0:T(8,128)(2,1)S(1)}, u32[]{:S(2)}, u32[]{:S(2)}) collective-permute-start(bf16[64,1152]{1,0:T(8,128)(2,1)S(1)} %collective-permute-done.10.refs_3_), channel_id=1, source_target_pairs={{0,4},{1,5},{4,8},{5,9},{8,12},{9,13},{12,14},{13,15},{14,10},{15,... | collective-permute-start | bytes 442376 | tf_op jit(solution)/shard_map/ppermute | solution.py:36
  31.6 0.8 %collective-permute-done.14.refs_4_ = bf16[64,1152]{1,0:T(8,128)(2,1)S(1)} collective-permute-done((bf16[64,1152]{1,0:T(8,128)(2,1)S(1)}, bf16[64,1152]{1,0:T(8,128)(2,1)S(1)}, u32[]{:S(2)}, u32[]{:S(2)}) %collective-permute-start.14) | collective-permute-done | bytes 147488 | tf_op jit(solution)/shard_map/ppermute | solution.py:36
  32.5 0.8 %shard_map.66.refs_5_ = f32[256,128]{1,0:T(8,128)S(1)} custom-call(bf16[8,128,2304]{2,1,0:T(8,128)(2,1)S(1)} %shard_map.64.refs_0_, bf16[128,8192]{1,0:T(8,128)(2,1)S(1)} %collective-permute-done.1.refs_1_, bf16[128,28672]{1,0:T(8,128)(2,1)S(1)} %collective-permute-done.2.refs_2_, bf16[64,1152]{1,0:T(8,128)(2,1)S(1)} %collective-permute-done.10.refs_3_, ...), custom_call_target="tpu_custom_call" | custom-call | flops 150994944 | bytes 2949120 | tf_op jit(solution)/shard_map/pallas_call | solution.py:116
  33.3 1.4 %collective-permute-done.12.refs_3_ = bf16[64,1152]{1,0:T(8,128)(2,1)S(1)} collective-permute-done((bf16[64,1152]{1,0:T(8,128)(2,1)S(1)}, bf16[64,1152]{1,0:T(8,128)(2,1)S(1)}, u32[]{:S(2)}, u32[]{:S(2)}) %collective-permute-start.12) | collective-permute-done | bytes 147488 | tf_op jit(solution)/shard_map/ppermute | solution.py:36
  34.7 1.8 %collective-permute-done.13.refs_4_ = bf16[64,1152]{1,0:T(8,128)(2,1)S(1)} collective-permute-done((bf16[64,1152]{1,0:T(8,128)(2,1)S(1)}, bf16[64,1152]{1,0:T(8,128)(2,1)S(1)}, u32[]{:S(2)}, u32[]{:S(2)}) %collective-permute-start.13) | collective-permute-done | bytes 147488 | tf_op jit(solution)/shard_map/ppermute | solution.py:36
  37.1 1.3 %collective-permute-done.16 = f32[256,128]{1,0:T(8,128)S(1)} collective-permute-done((f32[256,128]{1,0:T(8,128)S(1)}, f32[256,128]{1,0:T(8,128)S(1)}, u32[]{:S(2)}, u32[]{:S(2)}) %collective-permute-start.16) | collective-permute-done | bytes 131104 | tf_op jit(solution)/shard_map/ppermute | solution.py:40
  38.9 12.0 %all_to_all.10 = f32[8,1,4096]{2,1,0:T(1,128)S(1)} all-to-all(f32[8,1,4096]{2,1,0:T(1,128)S(1)} %broadcast_in_dim.4), channel_id=1, replica_groups={{0,2,4,6,8,10,12,14},{1,3,5,7,9,11,13,15},{16,18,20,22,24,26,28,30},{17..., dimensions={0} | all-to-all | bytes 262144 | tf_op jit(solution)/shard_map/all_to_all | solution.py:132
  52.0 9.1 %all_to_all.11 = bf16[16,2,256]{2,1,0:T(2,128)(2,1)S(1)} all-to-all(bf16[16,2,256]{2,1,0:T(2,128)(2,1)S(1)} %broadcast_in_dim.5), channel_id=1, replica_groups={{0,1,2,3,4,5,6,7,8,9,10,11,12,13,14,15},{16,17,18,19,20,21,22,23,24,25,..., dimensions={0} | all-to-all | bytes 32768 | tf_op jit(solution)/shard_map/all_to_all | solution.py:132
  (36 shorter events, 4.5 us)
Async XLA Ops:
  0.0 51.3 %copy-start = (bf16[256,4096]{1,0:T(8,128)(2,1)S(1)}, bf16[256,4096]{1,0:T(8,128)(2,1)}, u32[]{:S(2)}) copy-start(bf16[256,4096]{1,0:T(8,128)(2,1)} %param.10) | copy-start | bytes 6291460
  0.0 27.7 %collective-permute-start.2 = (bf16[128,28672]{1,0:T(8,128)(2,1)}, bf16[128,28672]{1,0:T(8,128)(2,1)S(1)}, u32[]{:S(2)}, u32[]{:S(2)}) collective-permute-start(bf16[128,28672]{1,0:T(8,128)(2,1)} %grad.1), channel_id=1, source_target_pairs={{0,1},{1,0},{2,3},{3,2},{4,5},{5,4},{6,7},{7,6},{8,9},{9,8},{10,11... | collective-permute-start | bytes 22020104 | tf_op jit(solution)/shard_map/ppermute | solution.py:40
  0.5 14.8 %collective-permute-start.1 = (bf16[128,8192]{1,0:T(8,128)(2,1)}, bf16[128,8192]{1,0:T(8,128)(2,1)S(1)}, u32[]{:S(2)}, u32[]{:S(2)}) collective-permute-start(bf16[128,8192]{1,0:T(8,128)(2,1)} %act.1), channel_id=1, source_target_pairs={{0,1},{1,0},{2,3},{3,2},{4,5},{5,4},{6,7},{7,6},{8,9},{9,8},{10,11... | collective-permute-start | bytes 6291464 | tf_op jit(solution)/shard_map/ppermute | solution.py:40
  2.4 7.0 %collective-permute-start = (bf16[64,1152]{1,0:T(8,128)(2,1)S(1)}, bf16[64,1152]{1,0:T(8,128)(2,1)S(1)}, u32[]{:S(2)}, u32[]{:S(2)}) collective-permute-start(bf16[64,1152]{1,0:T(8,128)(2,1)S(1)} %pad_maximum_fusion.refs_3_), channel_id=1, source_target_pairs={{0,4},{1,5},{4,8},{5,9},{8,12},{9,13},{12,14},{13,15},{14,10},{15,... | collective-permute-start | bytes 442376 | tf_op jit(solution)/shard_map/ppermute | solution.py:36
  6.4 8.6 %collective-permute-start.5 = (bf16[64,1152]{1,0:T(8,128)(2,1)S(1)}, bf16[64,1152]{1,0:T(8,128)(2,1)S(1)}, u32[]{:S(2)}, u32[]{:S(2)}) collective-permute-start(bf16[64,1152]{1,0:T(8,128)(2,1)S(1)} %slice.25.refs_4_), channel_id=1, source_target_pairs={{0,2},{1,3},{4,0},{5,1},{8,4},{9,5},{12,8},{13,9},{14,12},{15,13},... | collective-permute-start | bytes 442376 | tf_op jit(solution)/shard_map/ppermute | solution.py:36
  6.4 11.5 %collective-permute-start.4 = (bf16[64,1152]{1,0:T(8,128)(2,1)S(1)}, bf16[64,1152]{1,0:T(8,128)(2,1)S(1)}, u32[]{:S(2)}, u32[]{:S(2)}) collective-permute-start(bf16[64,1152]{1,0:T(8,128)(2,1)S(1)} %pad_maximum_fusion.refs_3_), channel_id=1, source_target_pairs={{0,2},{1,3},{4,0},{5,1},{8,4},{9,5},{12,8},{13,9},{14,12},{15,13},... | collective-permute-start | bytes 442376 | tf_op jit(solution)/shard_map/ppermute | solution.py:36
  9.4 8.5 %collective-permute-start.3 = (bf16[64,1152]{1,0:T(8,128)(2,1)S(1)}, bf16[64,1152]{1,0:T(8,128)(2,1)S(1)}, u32[]{:S(2)}, u32[]{:S(2)}) collective-permute-start(bf16[64,1152]{1,0:T(8,128)(2,1)S(1)} %slice.25.refs_4_), channel_id=1, source_target_pairs={{0,4},{1,5},{4,8},{5,9},{8,12},{9,13},{12,14},{13,15},{14,10},{15,... | collective-permute-start | bytes 442376 | tf_op jit(solution)/shard_map/ppermute | solution.py:36
  11.2 1.6 %copy-start.1 = (bf16[128,8192]{1,0:T(8,128)(2,1)S(1)}, bf16[128,8192]{1,0:T(8,128)(2,1)}, u32[]{:S(2)}) copy-start(bf16[128,8192]{1,0:T(8,128)(2,1)} %act.1) | copy-start | bytes 6291460
  15.0 5.2 %collective-permute-start.9 = (bf16[64,1152]{1,0:T(8,128)(2,1)S(1)}, bf16[64,1152]{1,0:T(8,128)(2,1)S(1)}, u32[]{:S(2)}, u32[]{:S(2)}) collective-permute-start(bf16[64,1152]{1,0:T(8,128)(2,1)S(1)} %collective-permute-done.5.refs_8_), channel_id=1, source_target_pairs={{0,2},{1,3},{4,0},{5,1},{8,4},{9,5},{12,8},{13,9},{14,12},{15,13},... | collective-permute-start | bytes 442376 | tf_op jit(solution)/shard_map/ppermute | solution.py:36
  15.2 7.2 %collective-permute-start.6 = (bf16[64,1152]{1,0:T(8,128)(2,1)S(1)}, bf16[64,1152]{1,0:T(8,128)(2,1)S(1)}, u32[]{:S(2)}, u32[]{:S(2)}) collective-permute-start(bf16[64,1152]{1,0:T(8,128)(2,1)S(1)} %collective-permute-done.refs_5_), channel_id=1, source_target_pairs={{0,4},{1,5},{4,8},{5,9},{8,12},{9,13},{12,14},{13,15},{14,10},{15,... | collective-permute-start | bytes 442376 | tf_op jit(solution)/shard_map/ppermute | solution.py:36
  17.9 6.7 %collective-permute-start.8 = (bf16[64,1152]{1,0:T(8,128)(2,1)S(1)}, bf16[64,1152]{1,0:T(8,128)(2,1)S(1)}, u32[]{:S(2)}, u32[]{:S(2)}) collective-permute-start(bf16[64,1152]{1,0:T(8,128)(2,1)S(1)} %collective-permute-done.4.refs_7_), channel_id=1, source_target_pairs={{0,2},{1,3},{4,0},{5,1},{8,4},{9,5},{12,8},{13,9},{14,12},{15,13},... | collective-permute-start | bytes 442376 | tf_op jit(solution)/shard_map/ppermute | solution.py:36
  17.9 7.7 %collective-permute-start.7 = (bf16[64,1152]{1,0:T(8,128)(2,1)S(1)}, bf16[64,1152]{1,0:T(8,128)(2,1)S(1)}, u32[]{:S(2)}, u32[]{:S(2)}) collective-permute-start(bf16[64,1152]{1,0:T(8,128)(2,1)S(1)} %collective-permute-done.3.refs_6_), channel_id=1, source_target_pairs={{0,4},{1,5},{4,8},{5,9},{8,12},{9,13},{12,14},{13,15},{14,10},{15,... | collective-permute-start | bytes 442376 | tf_op jit(solution)/shard_map/ppermute | solution.py:36
  20.2 9.4 %collective-permute-start.11 = (bf16[64,1152]{1,0:T(8,128)(2,1)S(1)}, bf16[64,1152]{1,0:T(8,128)(2,1)S(1)}, u32[]{:S(2)}, u32[]{:S(2)}) collective-permute-start(bf16[64,1152]{1,0:T(8,128)(2,1)S(1)} %collective-permute-done.9.refs_12_), channel_id=1, source_target_pairs={{0,2},{1,3},{4,0},{5,1},{8,4},{9,5},{12,8},{13,9},{14,12},{15,13},... | collective-permute-start | bytes 442376 | tf_op jit(solution)/shard_map/ppermute | solution.py:36
  22.5 7.1 %collective-permute-start.10 = (bf16[64,1152]{1,0:T(8,128)(2,1)S(1)}, bf16[64,1152]{1,0:T(8,128)(2,1)S(1)}, u32[]{:S(2)}, u32[]{:S(2)}) collective-permute-start(bf16[64,1152]{1,0:T(8,128)(2,1)S(1)} %collective-permute-done.6.refs_9_), channel_id=1, source_target_pairs={{0,4},{1,5},{4,8},{5,9},{8,12},{9,13},{12,14},{13,15},{14,10},{15,... | collective-permute-start | bytes 442376 | tf_op jit(solution)/shard_map/ppermute | solution.py:36
  24.6 7.0 %collective-permute-start.15 = (bf16[64,1152]{1,0:T(8,128)(2,1)S(1)}, bf16[64,1152]{1,0:T(8,128)(2,1)S(1)}, u32[]{:S(2)}, u32[]{:S(2)}) collective-permute-start(bf16[64,1152]{1,0:T(8,128)(2,1)S(1)} %collective-permute-done.8.refs_11_), channel_id=1, source_target_pairs={{0,2},{1,3},{4,0},{5,1},{8,4},{9,5},{12,8},{13,9},{14,12},{15,13},... | collective-permute-start | bytes 442376 | tf_op jit(solution)/shard_map/ppermute | solution.py:36
  25.6 6.8 %collective-permute-start.14 = (bf16[64,1152]{1,0:T(8,128)(2,1)S(1)}, bf16[64,1152]{1,0:T(8,128)(2,1)S(1)}, u32[]{:S(2)}, u32[]{:S(2)}) collective-permute-start(bf16[64,1152]{1,0:T(8,128)(2,1)S(1)} %collective-permute-done.7.refs_10_), channel_id=1, source_target_pairs={{0,4},{1,5},{4,8},{5,9},{8,12},{9,13},{12,14},{13,15},{14,10},{15,... | collective-permute-start | bytes 442376 | tf_op jit(solution)/shard_map/ppermute | solution.py:36
  29.5 5.2 %collective-permute-start.12 = (bf16[64,1152]{1,0:T(8,128)(2,1)S(1)}, bf16[64,1152]{1,0:T(8,128)(2,1)S(1)}, u32[]{:S(2)}, u32[]{:S(2)}) collective-permute-start(bf16[64,1152]{1,0:T(8,128)(2,1)S(1)} %collective-permute-done.10.refs_3_), channel_id=1, source_target_pairs={{0,4},{1,5},{4,8},{5,9},{8,12},{9,13},{12,14},{13,15},{14,10},{15,... | collective-permute-start | bytes 442376 | tf_op jit(solution)/shard_map/ppermute | solution.py:36
  31.4 5.1 %collective-permute-start.13 = (bf16[64,1152]{1,0:T(8,128)(2,1)S(1)}, bf16[64,1152]{1,0:T(8,128)(2,1)S(1)}, u32[]{:S(2)}, u32[]{:S(2)}) collective-permute-start(bf16[64,1152]{1,0:T(8,128)(2,1)S(1)} %collective-permute-done.11.refs_6_), channel_id=1, source_target_pairs={{0,2},{1,3},{4,0},{5,1},{8,4},{9,5},{12,8},{13,9},{14,12},{15,13},... | collective-permute-start | bytes 442376 | tf_op jit(solution)/shard_map/ppermute | solution.py:36
  37.0 24.0 %copy-start.2 = (bf16[8,4096]{1,0:T(8,128)(2,1)S(1)}, bf16[8,4096]{1,0:T(8,128)(2,1)}, u32[]{:S(2)}) copy-start(bf16[8,4096]{1,0:T(8,128)(2,1)} %param.11) | copy-start | bytes 196612
  37.1 1.4 %collective-permute-start.16 = (f32[256,128]{1,0:T(8,128)S(1)}, f32[256,128]{1,0:T(8,128)S(1)}, u32[]{:S(2)}, u32[]{:S(2)}) collective-permute-start(f32[256,128]{1,0:T(8,128)S(1)} %shard_map.67), channel_id=1, source_target_pairs={{0,1},{1,0},{2,3},{3,2},{4,5},{5,4},{6,7},{7,6},{8,9},{9,8},{10,11... | collective-permute-start | bytes 393224 | tf_op jit(solution)/shard_map/ppermute | solution.py:40

commit v7 on v3

--- a/solution.py
+++ b/solution.py
@@ -40,62 +40,64 @@
     return lax.ppermute(x, "dp", [(i, i ^ bit) for i in range(n)])
 
 
-def project_kernel(chips, offsets, widths, carry, fetch, *refs):
+def add_products(a_sum, g_sum, tokens, block):
+    a_block, *g_block = block
+    a_width = a_block.shape[1]
+    g_block = jnp.concatenate([ref[...] for ref in g_block], axis=0)
+    a_sum += dot(tokens[:, :a_width], a_block[...], NT)
+    g_sum += dot(tokens[:, a_width:], g_block, NT)
+    return a_sum, g_sum
+
+
+def project_kernel(chips, offsets, carry, fetch, *refs):
     tokens, refs = refs[:4], refs[4:]
     blocks, refs = refs[: 2 * len(offsets)], refs[2 * len(offsets) :]
-    if carry:
-        carried, refs = refs[0], refs[1:]
-    out, refs = refs[0], refs[1:]
-    if fetch is not None:
-        fetched, refs = refs[0], refs[1:]
-    buf, sems = refs
+    carried, refs = (refs[0], refs[1:]) if carry else (None, refs)
+    out, *fetched, buf, sems = refs
     rows = tokens[0].shape[0]
-    rank, cut = blocks[0].shape
-    a_width, g_width = widths
+    rank, a_width = blocks[0].shape
+    g_width = blocks[1].shape[1]
     core = lax.axis_index("dp") & 1
     copies = []
     for i, offset in enumerate(offsets + ([] if fetch is None else [fetch])):
         index = chip_behind(offset, chips) * 2 + core
-        to = buf.at[i] if i < len(offsets) else fetched
+        to = buf.at[i] if i < len(offsets) else fetched[0]
         for k, ref in enumerate(tokens):
-            width, start = (a_width, 0) if k < 2 else (g_width, a_width)
+            width, first = (a_width, 0) if k < 2 else (g_width, a_width)
             copies.append(
                 pltpu.make_async_copy(
                     ref.at[:, pl.ds(pl.multiple_of(index * width, 128), width)],
-                    to.at[pl.ds(k % 2 * rows, rows), pl.ds(start, width)],
+                    to.at[pl.ds(k % 2 * rows, rows), pl.ds(first, width)],
                     sems.at[i, k],
                 )
             )
     for copy in copies:
         copy.start()
     if carry:
-        a_sum, g_sum = carried[:, :rank], carried[:, rank:]
+        sums = carried[:, :rank], carried[:, rank:]
     else:
-        a_sum = g_sum = jnp.zeros((out.shape[0], rank), jnp.float32)
+        sums = (jnp.zeros((out.shape[0], rank), jnp.float32),) * 2
     for i in range(len(offsets)):
         for copy in copies[4 * i : 4 * i + 4]:
             copy.wait()
-        a_sum += dot(buf[i, :, :a_width], blocks[2 * i][:, :a_width], NT)
-        g_sum += dot(buf[i, :, a_width:cut], blocks[2 * i][:, a_width:], NT)
-        g_sum += dot(buf[i, :, cut:], blocks[2 * i + 1][...], NT)
-    out[:, :rank] = a_sum
-    out[:, rank:] = g_sum
+        sums = add_products(*sums, buf.at[i], blocks[2 * i : 2 * i + 2])
+    out[:, :rank], out[:, rank:] = sums
     for copy in copies[4 * len(offsets) :]:
         copy.wait()
 
 
-def project(tokens, blocks, offsets, widths, chips, carry=None, fetch=None):
+def project(tokens, blocks, offsets, chips, carry=None, fetch=None):
     rows = tokens[0].shape[0]
     count = len(offsets)
     rank = blocks[0][0].shape[0]
-    width = sum(widths)
+    width = sum(x.shape[1] for x in blocks[0])
     flat = [x for block in blocks for x in block]
     carried = () if carry is None else (carry,)
     out_shape = [jax.ShapeDtypeStruct((2 * rows, 2 * rank), jnp.float32)]
     if fetch is not None:
         out_shape.append(jax.ShapeDtypeStruct((2 * rows, width), tokens[0].dtype))
     return pl.pallas_call(
-        functools.partial(project_kernel, chips, offsets, widths, carry is not None, fetch),
+        functools.partial(project_kernel, chips, offsets, carry is not None, fetch),
         out_shape=out_shape,
         in_specs=[HBM] * 4 + [VMEM] * (len(flat) + len(carried)),
         out_specs=[VMEM] * len(out_shape),
@@ -112,21 +114,19 @@
     )(*tokens, *flat, *carried)
 
 
-def finish_kernel(a_width, tokens, first, second, carried, out):
-    rank, cut = first.shape
-    out[:, :rank] = carried[:, :rank] + dot(tokens[:, :a_width], first[:, :a_width], NT)
-    out[:, rank:] = (
-        carried[:, rank:]
-        + dot(tokens[:, a_width:cut], first[:, a_width:], NT)
-        + dot(tokens[:, cut:], second[...], NT)
-    )
-
-
-def finish(tokens, block, a_width, carry):
+def finish_kernel(tokens, *refs):
+    *block, carried, out = refs
+    rank = block[0].shape[0]
+    out[:, :rank], out[:, rank:] = add_products(
+        carried[:, :rank], carried[:, rank:], tokens, block
+    )
+
+
+def finish(tokens, block, carry):
     return pl.pallas_call(
-        functools.partial(finish_kernel, a_width),
+        finish_kernel,
         out_shape=jax.ShapeDtypeStruct(carry.shape, carry.dtype),
-        in_specs=[VMEM] * 4,
+        in_specs=[VMEM] * (2 + len(block)),
         out_specs=VMEM,
         compiler_params=pltpu.CompilerParams(vmem_limit_bytes=16 * 2**20),
     )(tokens, *block, carry)
@@ -144,29 +144,37 @@
     chips = n // 2
     split = LEN // rows
 
-    width = a_width + out_basis.shape[0]
-    cut = width // 256 * 128
-    in_rows, out_rows = in_basis.T, out_basis.T
-    own = (
-        jnp.concatenate([in_rows, out_rows[:, : cut - a_width]], axis=1),
-        out_rows[:, cut - a_width :],
-    )
-    up, down = [own], [own]
-    for _ in range(chips // 2 - 1):
-        up.append(tuple(ring(x, 1, chips) for x in up[-1]))
-        down.append(tuple(ring(x, -1, chips) for x in down[-1]))
-    tokens = (activations, swap(activations, 1, n), out_grads, swap(out_grads, 1, n))
-
-    widths = (a_width, width - a_width)
-    run = functools.partial(project, tokens, widths=widths, chips=chips)
-    (total,) = run([own, up[1], down[1]], [0, 1, -1])
-    total, far_up, far_down = lax.optimization_barrier((total, up[-1][0], down[-1][1]))
-    far = (ring(far_up, 1, chips), ring(far_down, -1, chips))
-    for i in range(2, chips // 2 - 1):
-        (total,) = run([up[i], down[i]], [i, -i], carry=total)
-    i = chips // 2 - 1
-    total, far_tokens = run([up[i], down[i]], [i, -i], carry=total, fetch=chips // 2)
-    total = finish(far_tokens, far, a_width, total)
+    own = (in_basis.T, out_basis.T)
+
+    def step(block, way):
+        return tuple(ring(x, way, chips) for x in block)
+
+    activations_2 = swap(activations, 1, n)
+    first, activations_2, send = lax.optimization_barrier(
+        ((step(own, 1), step(own, -1)), activations_2, out_grads)
+    )
+    tokens = (activations, activations_2, out_grads, swap(send, 1, n))
+    up, down = [own, first[0]], [own, first[1]]
+    for _ in range(chips // 2 - 2):
+        up.append(step(up[-1], 1))
+        down.append(step(down[-1], -1))
+
+    near, offsets = [own], [0]
+    for i in range(1, chips // 2 - 1):
+        near += [up[i], down[i]]
+        offsets += [i, -i]
+    (total,) = project(tokens, near, offsets, chips)
+    last = chips // 2 - 1
+    total, far_up, far_down = lax.optimization_barrier((total, up[last], down[last][1]))
+    far = (
+        ring(far_up[0], 1, chips),
+        ring(far_up[1][: rank // 2], 1, chips),
+        ring(far_down[rank // 2 :], -1, chips),
+    )
+    total, far_tokens = project(
+        tokens, [up[last], down[last]], [last, -last], chips, carry=total, fetch=chips // 2
+    )
+    total = finish(far_tokens, far, total)
     theirs = swap(total, 1, n)
     total = (total + jnp.concatenate([theirs[rows:], theirs[:rows]], axis=0)).astype(jnp.bfloat16)
 

time: 63.4 us -> 73.5 us (1.16)
  waiting for transfers between devices: 7.38 us -> 21.2 us
  starting transfers between devices: 18.9 us -> 15.9 us
  other arithmetic: 1.26 us -> 0.41 us
    ppermute x14 -> x15, waiting for transfers between devices: 6.04 us -> 19.8 us  [ring(): return lax.ppermute(x, 'dp', pairs)]
    ppermute x14 -> x15, starting transfers between devices: 18.3 us -> 15.3 us  [ring(): return lax.ppermute(x, 'dp', pairs)]
    slice x2, local copies, waits for them, and re-layouts: 1.92 us -> 0.02 us  [the longest x1 0.01 us: local(): far_down[rank // 2:]]
    unnamed x6 -> x10, local copies, waits for them, and re-layouts: 1.6 us -> 3.38 us
    concatenate x1 -> x0, other arithmetic: 0.85 us -> none  [local(): jnp.concatenate([in_rows, out_rows[:, :cut - a_width]], axis=1)]
    pallas_call x4 -> x3, Pallas kernels: 8.17 us -> 8.05 us  [the longest x2 7.54 us: project(): pl.pallas_call(functools.partial(project_kernel, chips, offsets, carry is...]
  transfers between devices with their start and end apart: 17 -> 18, of which waited for: 8 -> 6; matrix products, arithmetic and copies ran while one was open for 4% -> 0% of each run, Pallas kernels for 12% -> 10%
where the time goes in v7:
time: 73.5 us; the launch traced here: 73.2 us
  blocking collectives  22.2 us (30%)
  waiting for transfers between devices  21.2 us (29%)
  starting transfers between devices  15.9 us (22%)
  Pallas kernels  8.05 us (11%)
  local copies, waits for them, and re-layouts  3.61 us (5%)
  matrix products  1.61 us (2%)
    all_to_all x2, blocking collectives, to_all(): lax.all_to_all(copies, 'dp', 0, 0, axis_index_groups=groups, tiled=True)  22.2 us
    ppermute x15, waiting for transfers between devices, ring(): return lax.ppermute(x, 'dp', pairs)  19.8 us
    ppermute x15, starting transfers between devices, ring(): return lax.ppermute(x, 'dp', pairs)  15.3 us
    pallas_call x2, Pallas kernels, project(): pl.pallas_call(functools.partial(project_kernel, chips, offsets, carry is...  7.54 us
    unnamed x10, local copies, waits for them, and re-layouts  3.38 us
    dot_general x3, matrix products, dot(): return lax.dot_general(a, b, dims, preferred_element_type=jnp.float32)  1.61 us
  transfers between devices with their start and end apart: 18, of which 6 were waited for; matrix products, arithmetic and copies ran while one was open for 0% of the time, Pallas kernels for 10%

profile of v7, /device:TPU:0, one launch (start us, length us, event | category | flops | bytes accessed | tf_op | source)
XLA Modules:
  0.0 73.2 jit_solution(16720941588918619909)
XLA Ops:
  0.0 0.5 collective-permute-start.4
  0.5 2.6 %collective-permute-start.3 = (bf16[64,1792]{1,0:T(8,128)(2,1)}, bf16[64,1792]{1,0:T(8,128)(2,1)S(1)}, u32[]{:S(2)}, u32[]{:S(2)}) collective-permute-start(bf16[64,1792]{1,0:T(8,128)(2,1)} %bitcast.9), channel_id=1, source_target_pairs={{0,2},{1,3},{4,0},{5,1},{8,4},{9,5},{12,8},{13,9},{14,12},{15,13},... | collective-permute-start | bytes 688136 | tf_op jit(solution)/shard_map/ppermute | solution.py:36
  3.2 1.9 %collective-permute-start.2 = (bf16[64,512]{1,0:T(8,128)(2,1)}, bf16[64,512]{1,0:T(8,128)(2,1)S(1)}, u32[]{:S(2)}, u32[]{:S(2)}) collective-permute-start(bf16[64,512]{1,0:T(8,128)(2,1)} %bitcast.12), channel_id=1, source_target_pairs={{0,2},{1,3},{4,0},{5,1},{8,4},{9,5},{12,8},{13,9},{14,12},{15,13},... | collective-permute-start | bytes 196616 | tf_op jit(solution)/shard_map/ppermute | solution.py:36
  5.2 5.7 %collective-permute-done.2.refs_8_ = bf16[64,512]{1,0:T(8,128)(2,1)S(1)} collective-permute-done((bf16[64,512]{1,0:T(8,128)(2,1)}, bf16[64,512]{1,0:T(8,128)(2,1)S(1)}, u32[]{:S(2)}, u32[]{:S(2)}) %collective-permute-start.2) | collective-permute-done | bytes 65568 | tf_op jit(solution)/shard_map/ppermute | solution.py:36
  10.9 1.4 %collective-permute-done.refs_6_ = bf16[64,512]{1,0:T(8,128)(2,1)S(1)} collective-permute-done((bf16[64,512]{1,0:T(8,128)(2,1)}, bf16[64,512]{1,0:T(8,128)(2,1)S(1)}, u32[]{:S(2)}, u32[]{:S(2)}) %collective-permute-start) | collective-permute-done | bytes 65568 | tf_op jit(solution)/shard_map/ppermute | solution.py:36
  12.8 1.7 %collective-permute-start.12 = (bf16[64,1792]{1,0:T(8,128)(2,1)S(1)}, bf16[64,1792]{1,0:T(8,128)(2,1)S(1)}, u32[]{:S(2)}, u32[]{:S(2)}) collective-permute-start(bf16[64,1792]{1,0:T(8,128)(2,1)S(1)} %collective-permute-done.3.refs_9_), channel_id=1, source_target_pairs={{0,2},{1,3},{4,0},{5,1},{8,4},{9,5},{12,8},{13,9},{14,12},{15,13},... | collective-permute-start | bytes 688136 | tf_op jit(solution)/shard_map/ppermute | solution.py:36
  14.5 5.9 %collective-permute-done.8.refs_11_ = bf16[64,1792]{1,0:T(8,128)(2,1)S(1)} collective-permute-done((bf16[64,1792]{1,0:T(8,128)(2,1)S(1)}, bf16[64,1792]{1,0:T(8,128)(2,1)S(1)}, u32[]{:S(2)}, u32[]{:S(2)}) %collective-permute-start.8) | collective-permute-done | bytes 229408 | tf_op jit(solution)/shard_map/ppermute | solution.py:36
  20.8 1.7 %collective-permute-start.13 = (bf16[64,1792]{1,0:T(8,128)(2,1)S(1)}, bf16[64,1792]{1,0:T(8,128)(2,1)S(1)}, u32[]{:S(2)}, u32[]{:S(2)}) collective-permute-start(bf16[64,1792]{1,0:T(8,128)(2,1)S(1)} %collective-permute-done.12.refs_13_), channel_id=1, source_target_pairs={{0,2},{1,3},{4,0},{5,1},{8,4},{9,5},{12,8},{13,9},{14,12},{15,13},... | collective-permute-start | bytes 688136 | tf_op jit(solution)/shard_map/ppermute | solution.py:36
  22.8 1.7 %collective-permute-start.10 = (bf16[64,512]{1,0:T(8,128)(2,1)S(1)}, bf16[64,512]{1,0:T(8,128)(2,1)S(1)}, u32[]{:S(2)}, u32[]{:S(2)}) collective-permute-start(bf16[64,512]{1,0:T(8,128)(2,1)S(1)} %collective-permute-done.2.refs_8_), channel_id=1, source_target_pairs={{0,2},{1,3},{4,0},{5,1},{8,4},{9,5},{12,8},{13,9},{14,12},{15,13},... | collective-permute-start | bytes 196616 | tf_op jit(solution)/shard_map/ppermute | solution.py:36
  24.5 4.5 %collective-permute-done.6.refs_10_ = bf16[64,512]{1,0:T(8,128)(2,1)S(1)} collective-permute-done((bf16[64,512]{1,0:T(8,128)(2,1)S(1)}, bf16[64,512]{1,0:T(8,128)(2,1)S(1)}, u32[]{:S(2)}, u32[]{:S(2)}) %collective-permute-start.6) | collective-permute-done | bytes 65568 | tf_op jit(solution)/shard_map/ppermute | solution.py:36
  29.4 1.6 %copy-done.1 = bf16[128,8192]{1,0:T(8,128)(2,1)S(1)} copy-done((bf16[128,8192]{1,0:T(8,128)(2,1)S(1)}, bf16[128,8192]{1,0:T(8,128)(2,1)}, u32[]{:S(2)}) %copy-start.1) | copy-done | bytes 2097176
  30.9 0.9 %copy-done.2 = bf16[1792,64]{0,1:T(8,128)(2,1)S(1)} copy-done((bf16[1792,64]{0,1:T(8,128)(2,1)S(1)}, bf16[1792,64]{0,1:T(8,128)(2,1)}, u32[]{:S(2)}) %copy-start.2) | copy-done | bytes 229400
  31.9 0.8 %copy-done.3 = bf16[512,64]{0,1:T(8,128)(2,1)S(1)} copy-done((bf16[512,64]{0,1:T(8,128)(2,1)S(1)}, bf16[512,64]{0,1:T(8,128)(2,1)}, u32[]{:S(2)}) %copy-start.3) | copy-done | bytes 65560
  32.7 4.6 %shard_map.64.refs_8_ = f32[256,128]{1,0:T(8,128)S(1)} custom-call(bf16[128,8192]{1,0:T(8,128)(2,1)S(1)} %copy-done.1, bf16[128,8192]{1,0:T(8,128)(2,1)S(1)} %collective-permute-done.4.refs_1_, bf16[128,28672]{1,0:T(8,128)(2,1)} %refs_2_.3, bf16[128,28672]{1,0:T(8,128)(2,1)} %collective-permute-done.5.refs_3_, bf16[64,512]{1,0:T(8,128)(2,1)S(1)} %bitcast.14, ...), custom_call_target="tpu_custom_call" | custom-call | flops 377487360 | bytes 7372800 | tf_op jit(solution)/shard_map/pallas_call | solution.py:99
  37.4 1.7 %collective-permute-start.16 = (bf16[32,1792]{1,0:T(8,128)(2,1)S(1)}, bf16[32,1792]{1,0:T(8,128)(2,1)S(1)}, u32[]{:S(2)}, u32[]{:S(2)}) collective-permute-start(bf16[32,1792]{1,0:T(8,128)(2,1)S(1)} %slice.19), channel_id=1, source_target_pairs={{0,2},{1,3},{4,0},{5,1},{8,4},{9,5},{12,8},{13,9},{14,12},{15,13},... | collective-permute-start | bytes 344072 | tf_op jit(solution)/shard_map/ppermute | solution.py:36
  39.5 1.7 %collective-permute-start.11 = (bf16[64,512]{1,0:T(8,128)(2,1)S(1)}, bf16[64,512]{1,0:T(8,128)(2,1)S(1)}, u32[]{:S(2)}, u32[]{:S(2)}) collective-permute-start(bf16[64,512]{1,0:T(8,128)(2,1)S(1)} %collective-permute-done.10.refs_12_), channel_id=1, source_target_pairs={{0,2},{1,3},{4,0},{5,1},{8,4},{9,5},{12,8},{13,9},{14,12},{15,13},... | collective-permute-start | bytes 196616 | tf_op jit(solution)/shard_map/ppermute | solution.py:36
  41.5 2.2 %collective-permute-done.11.refs_6_ = bf16[64,512]{1,0:T(8,128)(2,1)S(1)} collective-permute-done((bf16[64,512]{1,0:T(8,128)(2,1)S(1)}, bf16[64,512]{1,0:T(8,128)(2,1)S(1)}, u32[]{:S(2)}, u32[]{:S(2)}) %collective-permute-start.11) | collective-permute-done | bytes 65568 | tf_op jit(solution)/shard_map/ppermute | solution.py:36
  43.8 2.9 %shard_map.65 = (f32[256,128]{1,0:T(8,128)S(1)}, bf16[256,2304]{1,0:T(8,128)(2,1)S(1)}) custom-call(bf16[128,8192]{1,0:T(8,128)(2,1)S(1)} %copy-done.1, bf16[128,8192]{1,0:T(8,128)(2,1)S(1)} %collective-permute-done.4.refs_1_, bf16[128,28672]{1,0:T(8,128)(2,1)} %refs_2_.3, bf16[128,28672]{1,0:T(8,128)(2,1)} %collective-permute-done.5.refs_3_, ...), custom_call_target="tpu_custom_call" | custom-call | flops 150994944 | bytes 2949120 | tf_op jit(solution)/shard_map/pallas_call | solution.py:99
  46.7 0.5 shard_map.66
  47.3 1.3 %collective-permute-done.17 = f32[256,128]{1,0:T(8,128)S(1)} collective-permute-done((f32[256,128]{1,0:T(8,128)S(1)}, f32[256,128]{1,0:T(8,128)S(1)}, u32[]{:S(2)}, u32[]{:S(2)}) %collective-permute-start.17) | collective-permute-done | bytes 131104 | tf_op jit(solution)/shard_map/ppermute | solution.py:40
  49.1 13.1 %all_to_all.10 = f32[8,1,4096]{2,1,0:T(1,128)S(1)} all-to-all(f32[8,1,4096]{2,1,0:T(1,128)S(1)} %broadcast_in_dim.4), channel_id=1, replica_groups={{0,2,4,6,8,10,12,14},{1,3,5,7,9,11,13,15},{16,18,20,22,24,26,28,30},{17..., dimensions={0} | all-to-all | bytes 262144 | tf_op jit(solution)/shard_map/all_to_all | solution.py:137
  62.7 0.6 convolution_convert_fusion
  63.4 9.1 %all_to_all.11 = bf16[16,2,256]{2,1,0:T(2,128)(2,1)S(1)} all-to-all(bf16[16,2,256]{2,1,0:T(2,128)(2,1)S(1)} %broadcast_in_dim.5), channel_id=1, replica_groups={{0,1,2,3,4,5,6,7,8,9,10,11,12,13,14,15},{16,17,18,19,20,21,22,23,24,25,..., dimensions={0} | all-to-all | bytes 32768 | tf_op jit(solution)/shard_map/all_to_all | solution.py:137
  72.4 0.7 convolution_multiply_fusion.1
  (40 shorter events, 3.6 us)
Async XLA Ops:
  0.0 62.7 %copy-start = (bf16[256,4096]{1,0:T(8,128)(2,1)S(1)}, bf16[256,4096]{1,0:T(8,128)(2,1)}, u32[]{:S(2)}) copy-start(bf16[256,4096]{1,0:T(8,128)(2,1)} %param.10) | copy-start | bytes 6291460
  0.0 12.3 %collective-permute-start.4 = (bf16[128,8192]{1,0:T(8,128)(2,1)}, bf16[128,8192]{1,0:T(8,128)(2,1)S(1)}, u32[]{:S(2)}, u32[]{:S(2)}) collective-permute-start(bf16[128,8192]{1,0:T(8,128)(2,1)} %refs_0_.3), channel_id=1, source_target_pairs={{0,1},{1,0},{2,3},{3,2},{4,5},{5,4},{6,7},{7,6},{8,9},{9,8},{10,11... | collective-permute-start | bytes 6291464 | tf_op jit(solution)/shard_map/ppermute | solution.py:40
  0.5 11.9 %collective-permute-start.3 = (bf16[64,1792]{1,0:T(8,128)(2,1)}, bf16[64,1792]{1,0:T(8,128)(2,1)S(1)}, u32[]{:S(2)}, u32[]{:S(2)}) collective-permute-start(bf16[64,1792]{1,0:T(8,128)(2,1)} %bitcast.9), channel_id=1, source_target_pairs={{0,2},{1,3},{4,0},{5,1},{8,4},{9,5},{12,8},{13,9},{14,12},{15,13},... | collective-permute-start | bytes 688136 | tf_op jit(solution)/shard_map/ppermute | solution.py:36
  3.0 9.3 %collective-permute-start.1 = (bf16[64,1792]{1,0:T(8,128)(2,1)}, bf16[64,1792]{1,0:T(8,128)(2,1)S(1)}, u32[]{:S(2)}, u32[]{:S(2)}) collective-permute-start(bf16[64,1792]{1,0:T(8,128)(2,1)} %bitcast.10), channel_id=1, source_target_pairs={{0,4},{1,5},{4,8},{5,9},{8,12},{9,13},{12,14},{13,15},{14,10},{15,... | collective-permute-start | bytes 688136 | tf_op jit(solution)/shard_map/ppermute | solution.py:36
  3.2 7.7 %collective-permute-start.2 = (bf16[64,512]{1,0:T(8,128)(2,1)}, bf16[64,512]{1,0:T(8,128)(2,1)S(1)}, u32[]{:S(2)}, u32[]{:S(2)}) collective-permute-start(bf16[64,512]{1,0:T(8,128)(2,1)} %bitcast.12), channel_id=1, source_target_pairs={{0,2},{1,3},{4,0},{5,1},{8,4},{9,5},{12,8},{13,9},{14,12},{15,13},... | collective-permute-start | bytes 196616 | tf_op jit(solution)/shard_map/ppermute | solution.py:36
  5.1 7.3 %collective-permute-start = (bf16[64,512]{1,0:T(8,128)(2,1)}, bf16[64,512]{1,0:T(8,128)(2,1)S(1)}, u32[]{:S(2)}, u32[]{:S(2)}) collective-permute-start(bf16[64,512]{1,0:T(8,128)(2,1)} %bitcast.13), channel_id=1, source_target_pairs={{0,4},{1,5},{4,8},{5,9},{8,12},{9,13},{12,14},{13,15},{14,10},{15,... | collective-permute-start | bytes 196616 | tf_op jit(solution)/shard_map/ppermute | solution.py:36
  12.3 17.0 %collective-permute-start.5 = (bf16[128,28672]{1,0:T(8,128)(2,1)}, bf16[128,28672]{1,0:T(8,128)(2,1)}, u32[]{:S(2)}, u32[]{:S(2)}) collective-permute-start(bf16[128,28672]{1,0:T(8,128)(2,1)} %refs_2_.3), channel_id=1, source_target_pairs={{0,1},{1,0},{2,3},{3,2},{4,5},{5,4},{6,7},{7,6},{8,9},{9,8},{10,11... | collective-permute-start | bytes 22020104 | tf_op jit(solution)/shard_map/ppermute | solution.py:40
  12.4 8.0 %collective-permute-start.8 = (bf16[64,1792]{1,0:T(8,128)(2,1)S(1)}, bf16[64,1792]{1,0:T(8,128)(2,1)S(1)}, u32[]{:S(2)}, u32[]{:S(2)}) collective-permute-start(bf16[64,1792]{1,0:T(8,128)(2,1)S(1)} %collective-permute-done.1.refs_7_), channel_id=1, source_target_pairs={{0,4},{1,5},{4,8},{5,9},{8,12},{9,13},{12,14},{13,15},{14,10},{15,... | collective-permute-start | bytes 688136 | tf_op jit(solution)/shard_map/ppermute | solution.py:36
  12.8 8.0 %collective-permute-start.12 = (bf16[64,1792]{1,0:T(8,128)(2,1)S(1)}, bf16[64,1792]{1,0:T(8,128)(2,1)S(1)}, u32[]{:S(2)}, u32[]{:S(2)}) collective-permute-start(bf16[64,1792]{1,0:T(8,128)(2,1)S(1)} %collective-permute-done.3.refs_9_), channel_id=1, source_target_pairs={{0,2},{1,3},{4,0},{5,1},{8,4},{9,5},{12,8},{13,9},{14,12},{15,13},... | collective-permute-start | bytes 688136 | tf_op jit(solution)/shard_map/ppermute | solution.py:36
  20.4 16.9 %collective-permute-start.9 = (bf16[64,1792]{1,0:T(8,128)(2,1)S(1)}, bf16[64,1792]{1,0:T(8,128)(2,1)S(1)}, u32[]{:S(2)}, u32[]{:S(2)}) collective-permute-start(bf16[64,1792]{1,0:T(8,128)(2,1)S(1)} %collective-permute-done.8.refs_11_), channel_id=1, source_target_pairs={{0,4},{1,5},{4,8},{5,9},{8,12},{9,13},{12,14},{13,15},{14,10},{15,... | collective-permute-start | bytes 688136 | tf_op jit(solution)/shard_map/ppermute | solution.py:36
  20.8 16.6 %collective-permute-start.13 = (bf16[64,1792]{1,0:T(8,128)(2,1)S(1)}, bf16[64,1792]{1,0:T(8,128)(2,1)S(1)}, u32[]{:S(2)}, u32[]{:S(2)}) collective-permute-start(bf16[64,1792]{1,0:T(8,128)(2,1)S(1)} %collective-permute-done.12.refs_13_), channel_id=1, source_target_pairs={{0,2},{1,3},{4,0},{5,1},{8,4},{9,5},{12,8},{13,9},{14,12},{15,13},... | collective-permute-start | bytes 688136 | tf_op jit(solution)/shard_map/ppermute | solution.py:36
  22.5 6.5 %collective-permute-start.6 = (bf16[64,512]{1,0:T(8,128)(2,1)S(1)}, bf16[64,512]{1,0:T(8,128)(2,1)S(1)}, u32[]{:S(2)}, u32[]{:S(2)}) collective-permute-start(bf16[64,512]{1,0:T(8,128)(2,1)S(1)} %collective-permute-done.refs_6_), channel_id=1, source_target_pairs={{0,4},{1,5},{4,8},{5,9},{8,12},{9,13},{12,14},{13,15},{14,10},{15,... | collective-permute-start | bytes 196616 | tf_op jit(solution)/shard_map/ppermute | solution.py:36
  22.8 6.5 %collective-permute-start.10 = (bf16[64,512]{1,0:T(8,128)(2,1)S(1)}, bf16[64,512]{1,0:T(8,128)(2,1)S(1)}, u32[]{:S(2)}, u32[]{:S(2)}) collective-permute-start(bf16[64,512]{1,0:T(8,128)(2,1)S(1)} %collective-permute-done.2.refs_8_), channel_id=1, source_target_pairs={{0,2},{1,3},{4,0},{5,1},{8,4},{9,5},{12,8},{13,9},{14,12},{15,13},... | collective-permute-start | bytes 196616 | tf_op jit(solution)/shard_map/ppermute | solution.py:36
  29.0 8.4 %collective-permute-start.7 = (bf16[64,512]{1,0:T(8,128)(2,1)S(1)}, bf16[64,512]{1,0:T(8,128)(2,1)S(1)}, u32[]{:S(2)}, u32[]{:S(2)}) collective-permute-start(bf16[64,512]{1,0:T(8,128)(2,1)S(1)} %collective-permute-done.6.refs_10_), channel_id=1, source_target_pairs={{0,4},{1,5},{4,8},{5,9},{8,12},{9,13},{12,14},{13,15},{14,10},{15,... | collective-permute-start | bytes 196616 | tf_op jit(solution)/shard_map/ppermute | solution.py:36
  29.3 1.6 %copy-start.1 = (bf16[128,8192]{1,0:T(8,128)(2,1)S(1)}, bf16[128,8192]{1,0:T(8,128)(2,1)}, u32[]{:S(2)}) copy-start(bf16[128,8192]{1,0:T(8,128)(2,1)} %refs_0_.3) | copy-start | bytes 6291460
  30.9 0.9 %copy-start.2 = (bf16[1792,64]{0,1:T(8,128)(2,1)S(1)}, bf16[1792,64]{0,1:T(8,128)(2,1)}, u32[]{:S(2)}) copy-start(bf16[1792,64]{0,1:T(8,128)(2,1)} %param.9) | copy-start | bytes 688132
  31.9 0.8 %copy-start.3 = (bf16[512,64]{0,1:T(8,128)(2,1)S(1)}, bf16[512,64]{0,1:T(8,128)(2,1)}, u32[]{:S(2)}) copy-start(bf16[512,64]{0,1:T(8,128)(2,1)} %param.8) | copy-start | bytes 196612
  37.4 9.3 %collective-permute-start.16 = (bf16[32,1792]{1,0:T(8,128)(2,1)S(1)}, bf16[32,1792]{1,0:T(8,128)(2,1)S(1)}, u32[]{:S(2)}, u32[]{:S(2)}) collective-permute-start(bf16[32,1792]{1,0:T(8,128)(2,1)S(1)} %slice.19), channel_id=1, source_target_pairs={{0,2},{1,3},{4,0},{5,1},{8,4},{9,5},{12,8},{13,9},{14,12},{15,13},... | collective-permute-start | bytes 344072 | tf_op jit(solution)/shard_map/ppermute | solution.py:36
  39.1 7.6 %collective-permute-start.15 = (bf16[32,1792]{1,0:T(8,128)(2,1)S(1)}, bf16[32,1792]{1,0:T(8,128)(2,1)S(1)}, u32[]{:S(2)}, u32[]{:S(2)}) collective-permute-start(bf16[32,1792]{1,0:T(8,128)(2,1)S(1)} %slice.18), channel_id=1, source_target_pairs={{0,4},{1,5},{4,8},{5,9},{8,12},{9,13},{12,14},{13,15},{14,10},{15,... | collective-permute-start | bytes 344072 | tf_op jit(solution)/shard_map/ppermute | solution.py:36
  39.5 4.3 %collective-permute-start.11 = (bf16[64,512]{1,0:T(8,128)(2,1)S(1)}, bf16[64,512]{1,0:T(8,128)(2,1)S(1)}, u32[]{:S(2)}, u32[]{:S(2)}) collective-permute-start(bf16[64,512]{1,0:T(8,128)(2,1)S(1)} %collective-permute-done.10.refs_12_), channel_id=1, source_target_pairs={{0,2},{1,3},{4,0},{5,1},{8,4},{9,5},{12,8},{13,9},{14,12},{15,13},... | collective-permute-start | bytes 196616 | tf_op jit(solution)/shard_map/ppermute | solution.py:36
  41.2 5.5 %collective-permute-start.14 = (bf16[64,512]{1,0:T(8,128)(2,1)S(1)}, bf16[64,512]{1,0:T(8,128)(2,1)S(1)}, u32[]{:S(2)}, u32[]{:S(2)}) collective-permute-start(bf16[64,512]{1,0:T(8,128)(2,1)S(1)} %collective-permute-done.7.refs_4_), channel_id=1, source_target_pairs={{0,4},{1,5},{4,8},{5,9},{8,12},{9,13},{12,14},{13,15},{14,10},{15,... | collective-permute-start | bytes 196616 | tf_op jit(solution)/shard_map/ppermute | solution.py:36
  47.2 25.2 %copy-start.4 = (bf16[8,4096]{1,0:T(8,128)(2,1)S(1)}, bf16[8,4096]{1,0:T(8,128)(2,1)}, u32[]{:S(2)}) copy-start(bf16[8,4096]{1,0:T(8,128)(2,1)} %param.11) | copy-start | bytes 196612
  47.2 1.4 %collective-permute-start.17 = (f32[256,128]{1,0:T(8,128)S(1)}, f32[256,128]{1,0:T(8,128)S(1)}, u32[]{:S(2)}, u32[]{:S(2)}) collective-permute-start(f32[256,128]{1,0:T(8,128)S(1)} %shard_map.66), channel_id=1, source_target_pairs={{0,1},{1,0},{2,3},{3,2},{4,5},{5,4},{6,7},{7,6},{8,9},{9,8},{10,11... | collective-permute-start | bytes 393224 | tf_op jit(solution)/shard_map/ppermute | solution.py:40

commit v8 on v6

--- a/solution.py
+++ b/solution.py
@@ -9,11 +9,14 @@
 from jax.sharding import PartitionSpec as P
 
 LEN = 1024
-LIMIT = 42
 NT = (((1,), (1,)), ((), ()))
 TN = (((0,), (0,)), ((), ()))
 VMEM = pl.BlockSpec(memory_space=pltpu.VMEM)
 HBM = pl.BlockSpec(memory_space=pltpu.HBM)
+
+
+def held(space, *arrays):
+    return [pltpu.with_memory_space_constraint(x, space) for x in arrays]
 
 
 def dot(a, b, dims):
@@ -40,69 +43,65 @@
     return lax.ppermute(x, "dp", [(i, i ^ bit) for i in range(n)])
 
 
-def gather_kernel(chips, a_width, act, grad, out, sems):
+def start_kernel(chips, act, grad, in_rows, out_rows, first, second, keep, send, sems):
     core = lax.axis_index("dp") & 1
-    copies = []
-    for chip in range(chips):
-        block = 2 * chip + core
-        for k, (ref, start, stop) in enumerate(((act, 0, a_width), (grad, a_width, out.shape[2]))):
-            width = stop - start
-            copies.append(
-                pltpu.make_async_copy(
-                    ref.at[:, pl.ds(pl.multiple_of(block * width, 128), width)],
-                    out.at[chip, :, pl.ds(start, width)],
-                    sems.at[chip, k],
-                )
-            )
+    a_width, g_width = in_rows.shape[1], out_rows.shape[1]
+    cut = first.shape[1]
+    pairs = [
+        (in_rows, first.at[:, pl.ds(0, a_width)]),
+        (out_rows.at[:, pl.ds(0, cut - a_width)], first.at[:, pl.ds(a_width, cut - a_width)]),
+        (out_rows.at[:, pl.ds(cut - a_width, second.shape[1])], second),
+    ]
+    for out, owner in ((send, 1 - core), (keep, core)):
+        for chip in range(chips):
+            block = 2 * chip + owner
+            for ref, at, width in ((act, 0, a_width), (grad, a_width, g_width)):
+                columns = pl.ds(pl.multiple_of(block * width, 128), width)
+                pairs.append((ref.at[:, columns], out.at[chip, :, pl.ds(at, width)]))
+    copies = [pltpu.make_async_copy(*pair, sems.at[i]) for i, pair in enumerate(pairs)]
     for copy in copies:
         copy.start()
     for copy in copies:
         copy.wait()
 
 
-def gather_columns(act, grad, a_width, width, chips):
+def start(act, grad, in_rows, out_rows, chips):
     rows = act.shape[0]
+    rank, width = in_rows.shape[0], in_rows.shape[1] + out_rows.shape[1]
+    cut = width // 256 * 128
+    shapes = [(rank, cut), (rank, width - cut)] + [(chips, rows, width)] * 2
     return pl.pallas_call(
-        functools.partial(gather_kernel, chips, a_width),
-        out_shape=jax.ShapeDtypeStruct((chips, rows, width), act.dtype),
-        in_specs=[HBM, HBM],
-        out_specs=VMEM,
-        scratch_shapes=[pltpu.SemaphoreType.DMA((chips, 2))],
-        compiler_params=pltpu.CompilerParams(vmem_limit_bytes=LIMIT * 2**20),
+        functools.partial(start_kernel, chips),
+        out_shape=[pltpu.VMEM(shape, act.dtype) for shape in shapes],
+        in_specs=[HBM] * 4,
+        out_specs=[VMEM] * 4,
+        scratch_shapes=[pltpu.SemaphoreType.DMA((3 + 4 * chips,))],
+        compiler_params=pltpu.CompilerParams(vmem_limit_bytes=16 * 2**20),
         cost_estimate=pl.CostEstimate(
-            flops=0, bytes_accessed=4 * chips * rows * width, transcendentals=0
+            flops=0, bytes_accessed=4 * (rank + 2 * chips * rows) * width, transcendentals=0
         ),
-    )(act, grad)
+    )(*held(pltpu.HBM, act, grad, in_rows, out_rows))
 
 
 def project_kernel(chips, offsets, a_width, carry, *refs):
-    mine, act, grad = refs[:3]
-    blocks, refs = refs[3 : 3 + 2 * len(offsets)], refs[3 + 2 * len(offsets) :]
+    keep, theirs = refs[:2]
+    blocks, refs = refs[2 : 2 + 2 * len(offsets)], refs[2 + 2 * len(offsets) :]
     out = refs[-1]
     rank, cut = blocks[0].shape
-    width = mine.shape[2]
-    g_width = width - a_width
-    core = lax.axis_index("dp") & 1
+    width = keep.shape[2]
     if carry:
         a_sum, g_sum = refs[0][:, :rank], refs[0][:, rank:]
     else:
         a_sum = g_sum = jnp.zeros((out.shape[0], rank), jnp.float32)
     for i, offset in enumerate(offsets):
         chip = chip_behind(offset, chips)
-        block = chip * 2 + core
-        a_at = pl.multiple_of(block * a_width, 128)
-        g_at = pl.multiple_of(block * g_width, 128)
-
-        def both(start, stop):
-            if stop <= a_width:
-                theirs = act[:, pl.ds(a_at + start, stop - start)]
-            else:
-                theirs = grad[:, pl.ds(g_at + start - a_width, stop - start)]
-            return jnp.concatenate([mine[chip, :, start:stop], theirs], axis=0)
-
-        a_sum += dot(both(0, a_width), blocks[2 * i][:, :a_width], NT)
-        g_sum += dot(both(a_width, cut), blocks[2 * i][:, a_width:], NT)
-        g_sum += dot(both(cut, width), blocks[2 * i + 1][...], NT)
+
+        def tokens(first, last):
+            return jnp.concatenate([ref[chip, :, first:last] for ref in (keep, theirs)], axis=0)
+
+        a_sum += dot(tokens(0, a_width), blocks[2 * i][:, :a_width], NT)
+        g_sum += dot(tokens(a_width, cut), blocks[2 * i][:, a_width:], NT)
+        g_sum += dot(tokens(cut, width), blocks[2 * i + 1][...], NT)
     out[:, :rank] = a_sum
     out[:, rank:] = g_sum
 
@@ -115,16 +114,16 @@
     carried = () if carry is None else (carry,)
     return pl.pallas_call(
         functools.partial(project_kernel, chips, offsets, a_width, carry is not None),
-        out_shape=jax.ShapeDtypeStruct((2 * rows, 2 * rank), jnp.float32),
-        in_specs=[VMEM] * (3 + len(flat) + len(carried)),
+        out_shape=pltpu.VMEM((2 * rows, 2 * rank), jnp.float32),
+        in_specs=[VMEM] * (2 + len(flat) + len(carried)),
         out_specs=VMEM,
-        compiler_params=pltpu.CompilerParams(vmem_limit_bytes=24 * 2**20),
+        compiler_params=pltpu.CompilerParams(vmem_limit_bytes=16 * 2**20),
         cost_estimate=pl.CostEstimate(
             flops=4 * count * rows * rank * width,
             bytes_accessed=count * (2 * rows + rank) * width * 2,
             transcendentals=0,
         ),
-    )(*tokens, *flat, *carried)
+    )(*held(pltpu.VMEM, *tokens, *flat, *carried))
 
 
 def to_all(x, groups):
@@ -139,24 +138,13 @@
     chips = n // 2
     split = LEN // rows
 
-    width = a_width + out_basis.shape[0]
-    cut = width // 256 * 128
-    in_rows, out_rows = in_basis.T, out_basis.T
-    own = (
-        jnp.concatenate([in_rows, out_rows[:, : cut - a_width]], axis=1),
-        out_rows[:, cut - a_width :],
-    )
-    activations_2 = swap(activations, 1, n)
-    out_grads_2 = swap(out_grads, 1, n)
+    *own, keep, send = start(activations, out_grads, in_basis.T, out_basis.T, chips)
+    tokens = (keep, swap(send, 1, n))
     up, down = [own], [own]
     for i in range(chips // 2 - 1):
-        if i == 1:
-            mine = gather_columns(activations, out_grads, a_width, width, chips)
-            first, activations_2, mine = lax.optimization_barrier((up[-1][0], activations_2, mine))
-            up[-1] = (first, up[-1][1])
         up.append(tuple(ring(x, 1, chips) for x in up[-1]))
         down.append(tuple(ring(x, -1, chips) for x in down[-1]))
-    run = functools.partial(project, (mine, activations_2, out_grads_2), a_width=a_width)
+    run = functools.partial(project, tokens, a_width=a_width)
     near, offsets = [own], [0]
     for i in range(1, chips // 2 - 1):
         near += [up[i], down[i]]

time: 62.1 us -> 58.6 us (0.944)
  starting transfers between devices: 19 us -> 15.4 us
  local copies, waits for them, and re-layouts: 3.74 us -> 0.23 us
  waiting for transfers between devices: 9.72 us -> 13.2 us
  Pallas kernels: 5.31 us -> 7.4 us
  blocking collectives: 21 us -> 20 us
  other arithmetic: 1.26 us -> 0.41 us
    ppermute x14, starting transfers between devices: 18.4 us -> 14.8 us  [ring(): return lax.ppermute(x, 'dp', pairs)]
    ppermute x14, waiting for transfers between devices: 8.38 us -> 11.9 us  [ring(): return lax.ppermute(x, 'dp', pairs)]
    pallas_call x1, Pallas kernels: 2.19 us -> 4.31 us  [start(): pl.pallas_call(functools.partial(start_kernel, chips), out_shape=[pltpu.V...]
    slice x2 -> x0, local copies, waits for them, and re-layouts: 1.92 us -> none  [the longest x1 1 us: local(): out_rows[:, :cut - a_width]]
    unnamed x6 -> x4, local copies, waits for them, and re-layouts: 1.6 us -> 0.01 us
    all_to_all x2, blocking collectives: 21 us -> 20 us  [to_all(): lax.all_to_all(copies, 'dp', 0, 0, axis_index_groups=groups, tiled=True)]
    concatenate x1 -> x0, other arithmetic: 0.85 us -> none  [local(): jnp.concatenate([in_rows, out_rows[:, :cut - a_width]], axis=1)]
    ppermute x3 -> x2, waiting for transfers between devices: 1.34 us -> 1.34 us  [swap(): return lax.ppermute(x, 'dp', [(i, i ^ bit) for i in range(n)])]
  transfers between devices with their start and end apart: 17 -> 16, of which waited for: 8 -> 9; matrix products, arithmetic and copies ran while one was open for 4% -> 0% of each run, Pallas kernels for 8% -> 4%
where the time goes in v8:
time: 58.6 us; the launch traced here: 58.4 us
  blocking collectives  20 us (34%)
  starting transfers between devices  15.4 us (26%)
  waiting for transfers between devices  13.2 us (23%)
  Pallas kernels  7.4 us (13%)
  matrix products  1.61 us (3%)
    all_to_all x2, blocking collectives, to_all(): lax.all_to_all(copies, 'dp', 0, 0, axis_index_groups=groups, tiled=True)  20 us
    ppermute x14, starting transfers between devices, ring(): return lax.ppermute(x, 'dp', pairs)  14.8 us
    ppermute x14, waiting for transfers between devices, ring(): return lax.ppermute(x, 'dp', pairs)  11.9 us
    pallas_call x1, Pallas kernels, start(): pl.pallas_call(functools.partial(start_kernel, chips), out_shape=[pltpu.V...  4.31 us
    pallas_call x3, Pallas kernels, project(): pl.pallas_call(functools.partial(project_kernel, chips, offsets, a_width,...  3.09 us
    dot_general x3, matrix products, dot(): return lax.dot_general(a, b, dims, preferred_element_type=jnp.float32)  1.61 us
    ppermute x2, waiting for transfers between devices, swap(): return lax.ppermute(x, 'dp', [(i, i ^ bit) for i in range(n)])  1.34 us
  transfers between devices with their start and end apart: 16, of which 9 were waited for; matrix products, arithmetic and copies ran while one was open for 0% of the time, Pallas kernels for 4%

profile of v8, /device:TPU:0, one launch (start us, length us, event | category | flops | bytes accessed | tf_op | source)
XLA Modules:
  0.0 58.4 jit_solution(5330737968191396803)
XLA Ops:
  0.0 4.3 %shard_map.64 = (bf16[64,1152]{1,0:T(8,128)(2,1)S(1)}, bf16[64,1152]{1,0:T(8,128)(2,1)S(1)}, bf16[8,128,2304]{2,1,0:T(8,128)(2,1)S(1)}, bf16[8,128,2304]{2,1,0:T(8,128)(2,1)S(1)}) custom-call(bf16[128,8192]{1,0:T(8,128)(2,1)} %act.1, bf16[128,28672]{1,0:T(8,128)(2,1)} %grad.1, bf16[64,512]{1,0:T(8,128)(2,1)} %bitcast.10, bf16[64,1792]{1,0:T(8,128)(2,1)} %bitcast.9), custom_call_target="tpu_custom_call" | custom-call | bytes 19464192 | tf_op jit(solution)/shard_map/pallas_call | solution.py:73
  4.8 2.6 %collective-permute-start.1 = (bf16[64,1152]{1,0:T(8,128)(2,1)S(1)}, bf16[64,1152]{1,0:T(8,128)(2,1)S(1)}, u32[]{:S(2)}, u32[]{:S(2)}) collective-permute-start(bf16[64,1152]{1,0:T(8,128)(2,1)S(1)} %get-tuple-element.14.refs_2_), channel_id=1, source_target_pairs={{0,4},{1,5},{4,8},{5,9},{8,12},{9,13},{12,14},{13,15},{14,10},{15,... | collective-permute-start | bytes 442376 | tf_op jit(solution)/shard_map/ppermute | solution.py:39
  7.5 2.0 %collective-permute-start.2 = (bf16[64,1152]{1,0:T(8,128)(2,1)S(1)}, bf16[64,1152]{1,0:T(8,128)(2,1)S(1)}, u32[]{:S(2)}, u32[]{:S(2)}) collective-permute-start(bf16[64,1152]{1,0:T(8,128)(2,1)S(1)} %get-tuple-element.15.refs_3_), channel_id=1, source_target_pairs={{0,4},{1,5},{4,8},{5,9},{8,12},{9,13},{12,14},{13,15},{14,10},{15,... | collective-permute-start | bytes 442376 | tf_op jit(solution)/shard_map/ppermute | solution.py:39
  9.5 2.6 %collective-permute-done.1.refs_4_ = bf16[64,1152]{1,0:T(8,128)(2,1)S(1)} collective-permute-done((bf16[64,1152]{1,0:T(8,128)(2,1)S(1)}, bf16[64,1152]{1,0:T(8,128)(2,1)S(1)}, u32[]{:S(2)}, u32[]{:S(2)}) %collective-permute-start.1) | collective-permute-done | bytes 147488 | tf_op jit(solution)/shard_map/ppermute | solution.py:39
  12.1 2.0 %collective-permute-start.5 = (bf16[64,1152]{1,0:T(8,128)(2,1)S(1)}, bf16[64,1152]{1,0:T(8,128)(2,1)S(1)}, u32[]{:S(2)}, u32[]{:S(2)}) collective-permute-start(bf16[64,1152]{1,0:T(8,128)(2,1)S(1)} %collective-permute-done.1.refs_4_), channel_id=1, source_target_pairs={{0,4},{1,5},{4,8},{5,9},{8,12},{9,13},{12,14},{13,15},{14,10},{15,... | collective-permute-start | bytes 442376 | tf_op jit(solution)/shard_map/ppermute | solution.py:39
  14.2 1.1 %collective-permute-done.2.refs_5_ = bf16[64,1152]{1,0:T(8,128)(2,1)S(1)} collective-permute-done((bf16[64,1152]{1,0:T(8,128)(2,1)S(1)}, bf16[64,1152]{1,0:T(8,128)(2,1)S(1)}, u32[]{:S(2)}, u32[]{:S(2)}) %collective-permute-start.2) | collective-permute-done | bytes 147488 | tf_op jit(solution)/shard_map/ppermute | solution.py:39
  15.3 2.0 %collective-permute-start.6 = (bf16[64,1152]{1,0:T(8,128)(2,1)S(1)}, bf16[64,1152]{1,0:T(8,128)(2,1)S(1)}, u32[]{:S(2)}, u32[]{:S(2)}) collective-permute-start(bf16[64,1152]{1,0:T(8,128)(2,1)S(1)} %collective-permute-done.2.refs_5_), channel_id=1, source_target_pairs={{0,4},{1,5},{4,8},{5,9},{8,12},{9,13},{12,14},{13,15},{14,10},{15,... | collective-permute-start | bytes 442376 | tf_op jit(solution)/shard_map/ppermute | solution.py:39
  17.3 1.5 %collective-permute-done.5.refs_8_ = bf16[64,1152]{1,0:T(8,128)(2,1)S(1)} collective-permute-done((bf16[64,1152]{1,0:T(8,128)(2,1)S(1)}, bf16[64,1152]{1,0:T(8,128)(2,1)S(1)}, u32[]{:S(2)}, u32[]{:S(2)}) %collective-permute-start.5) | collective-permute-done | bytes 147488 | tf_op jit(solution)/shard_map/ppermute | solution.py:39
  18.8 2.0 %collective-permute-start.9 = (bf16[64,1152]{1,0:T(8,128)(2,1)S(1)}, bf16[64,1152]{1,0:T(8,128)(2,1)S(1)}, u32[]{:S(2)}, u32[]{:S(2)}) collective-permute-start(bf16[64,1152]{1,0:T(8,128)(2,1)S(1)} %collective-permute-done.5.refs_8_), channel_id=1, source_target_pairs={{0,4},{1,5},{4,8},{5,9},{8,12},{9,13},{12,14},{13,15},{14,10},{15,... | collective-permute-start | bytes 442376 | tf_op jit(solution)/shard_map/ppermute | solution.py:39
  20.9 1.2 %collective-permute-done.6.refs_9_ = bf16[64,1152]{1,0:T(8,128)(2,1)S(1)} collective-permute-done((bf16[64,1152]{1,0:T(8,128)(2,1)S(1)}, bf16[64,1152]{1,0:T(8,128)(2,1)S(1)}, u32[]{:S(2)}, u32[]{:S(2)}) %collective-permute-start.6) | collective-permute-done | bytes 147488 | tf_op jit(solution)/shard_map/ppermute | solution.py:39
  22.0 2.0 %collective-permute-start.13 = (bf16[64,1152]{1,0:T(8,128)(2,1)S(1)}, bf16[64,1152]{1,0:T(8,128)(2,1)S(1)}, u32[]{:S(2)}, u32[]{:S(2)}) collective-permute-start(bf16[64,1152]{1,0:T(8,128)(2,1)S(1)} %collective-permute-done.6.refs_9_), channel_id=1, source_target_pairs={{0,4},{1,5},{4,8},{5,9},{8,12},{9,13},{12,14},{13,15},{14,10},{15,... | collective-permute-start | bytes 442376 | tf_op jit(solution)/shard_map/ppermute | solution.py:39
  24.1 1.7 %shard_map.65.refs_6_ = f32[256,128]{1,0:T(8,128)S(1)} custom-call(bf16[8,128,2304]{2,1,0:T(8,128)(2,1)S(1)} %get-tuple-element.12.refs_0_, bf16[8,128,2304]{2,1,0:T(8,128)(2,1)S(1)} %collective-permute-done.refs_1_, bf16[64,1152]{1,0:T(8,128)(2,1)S(1)} %get-tuple-element.14.refs_2_, bf16[64,1152]{1,0:T(8,128)(2,1)S(1)} %get-tuple-element.15.refs_3_, ...), custom_call_target="tpu_custom_call" | custom-call | flops 377487360 | bytes 7372800 | tf_op jit(solution)/shard_map/pallas_call | solution.py:115
  25.9 1.5 %collective-permute-done.10.refs_5_ = bf16[64,1152]{1,0:T(8,128)(2,1)S(1)} collective-permute-done((bf16[64,1152]{1,0:T(8,128)(2,1)S(1)}, bf16[64,1152]{1,0:T(8,128)(2,1)S(1)}, u32[]{:S(2)}, u32[]{:S(2)}) %collective-permute-start.10) | collective-permute-done | bytes 147488 | tf_op jit(solution)/shard_map/ppermute | solution.py:39
  27.4 1.6 %collective-permute-start.11 = (bf16[64,1152]{1,0:T(8,128)(2,1)S(1)}, bf16[64,1152]{1,0:T(8,128)(2,1)S(1)}, u32[]{:S(2)}, u32[]{:S(2)}) collective-permute-start(bf16[64,1152]{1,0:T(8,128)(2,1)S(1)} %collective-permute-done.9.refs_2_), channel_id=1, source_target_pairs={{0,4},{1,5},{4,8},{5,9},{8,12},{9,13},{12,14},{13,15},{14,10},{15,... | collective-permute-start | bytes 442376 | tf_op jit(solution)/shard_map/ppermute | solution.py:39
  29.4 0.7 %collective-permute-done.14.refs_4_ = bf16[64,1152]{1,0:T(8,128)(2,1)S(1)} collective-permute-done((bf16[64,1152]{1,0:T(8,128)(2,1)S(1)}, bf16[64,1152]{1,0:T(8,128)(2,1)S(1)}, u32[]{:S(2)}, u32[]{:S(2)}) %collective-permute-start.14) | collective-permute-done | bytes 147488 | tf_op jit(solution)/shard_map/ppermute | solution.py:39
  30.1 0.8 %shard_map.66.refs_4_ = f32[256,128]{1,0:T(8,128)S(1)} custom-call(bf16[8,128,2304]{2,1,0:T(8,128)(2,1)S(1)} %get-tuple-element.12.refs_0_, bf16[8,128,2304]{2,1,0:T(8,128)(2,1)S(1)} %collective-permute-done.refs_1_, bf16[64,1152]{1,0:T(8,128)(2,1)S(1)} %collective-permute-done.9.refs_2_, bf16[64,1152]{1,0:T(8,128)(2,1)S(1)} %collective-permute-done.13.refs_3_, ...), custom_call_target="tpu_custom_call" | custom-call | flops 150994944 | bytes 2949120 | tf_op jit(solution)/shard_map/pallas_call | solution.py:115
  30.9 1.6 %collective-permute-done.11.refs_2_ = bf16[64,1152]{1,0:T(8,128)(2,1)S(1)} collective-permute-done((bf16[64,1152]{1,0:T(8,128)(2,1)S(1)}, bf16[64,1152]{1,0:T(8,128)(2,1)S(1)}, u32[]{:S(2)}, u32[]{:S(2)}) %collective-permute-start.11) | collective-permute-done | bytes 147488 | tf_op jit(solution)/shard_map/ppermute | solution.py:39
  32.5 1.6 %collective-permute-done.12.refs_3_ = bf16[64,1152]{1,0:T(8,128)(2,1)S(1)} collective-permute-done((bf16[64,1152]{1,0:T(8,128)(2,1)S(1)}, bf16[64,1152]{1,0:T(8,128)(2,1)S(1)}, u32[]{:S(2)}, u32[]{:S(2)}) %collective-permute-start.12) | collective-permute-done | bytes 147488 | tf_op jit(solution)/shard_map/ppermute | solution.py:39
  34.1 0.5 shard_map.67
  34.7 1.3 %collective-permute-done.15 = f32[256,128]{1,0:T(8,128)S(1)} collective-permute-done((f32[256,128]{1,0:T(8,128)S(1)}, f32[256,128]{1,0:T(8,128)S(1)}, u32[]{:S(2)}, u32[]{:S(2)}) %collective-permute-start.15) | collective-permute-done | bytes 131104 | tf_op jit(solution)/shard_map/ppermute | solution.py:43
  36.5 11.0 %all_to_all.10 = f32[8,1,4096]{2,1,0:T(1,128)S(1)} all-to-all(f32[8,1,4096]{2,1,0:T(1,128)S(1)} %broadcast_in_dim.4), channel_id=1, replica_groups={{0,2,4,6,8,10,12,14},{1,3,5,7,9,11,13,15},{16,18,20,22,24,26,28,30},{17..., dimensions={0} | all-to-all | bytes 262144 | tf_op jit(solution)/shard_map/all_to_all | solution.py:131
  47.9 0.6 %convolution_convert_fusion = bf16[2,256]{1,0:T(2,128)(2,1)S(1)} fusion(bf16[256,4096]{1,0:T(8,128)(2,1)S(1)} %copy-done, bf16[2,4096]{1,0:T(2,128)(2,1)S(1)} %reduce_sum.9), kind=kOutput, calls=%fused_computation.1 | convolution fusion | flops 4194816 | bytes 2114560 | tf_op jit(solution)/shard_map/dot_general | solution.py:23
  48.6 9.1 %all_to_all.11 = bf16[16,2,256]{2,1,0:T(2,128)(2,1)S(1)} all-to-all(bf16[16,2,256]{2,1,0:T(2,128)(2,1)S(1)} %broadcast_in_dim.5), channel_id=1, replica_groups={{0,1,2,3,4,5,6,7,8,9,10,11,12,13,14,15},{16,17,18,19,20,21,22,23,24,25,..., dimensions={0} | all-to-all | bytes 32768 | tf_op jit(solution)/shard_map/all_to_all | solution.py:131
  57.7 0.7 %convolution_multiply_fusion.1 = f32[2,8]{1,0:T(2,128)} fusion(bf16[2,4096]{1,0:T(2,128)(2,1)S(1)} %bitcast.11, bf16[8,4096]{1,0:T(8,128)(2,1)S(1)} %copy-done.1), kind=kOutput, calls=%fused_computation.2 | convolution fusion | flops 131088 | bytes 81984 | tf_op jit(solution)/shard_map/dot_general | solution.py:23
  (29 shorter events, 2.1 us)
Async XLA Ops:
  0.0 47.9 %copy-start = (bf16[256,4096]{1,0:T(8,128)(2,1)S(1)}, bf16[256,4096]{1,0:T(8,128)(2,1)}, u32[]{:S(2)}) copy-start(bf16[256,4096]{1,0:T(8,128)(2,1)} %param.10) | copy-start | bytes 6291460
  4.3 19.8 %collective-permute-start = (bf16[8,128,2304]{2,1,0:T(8,128)(2,1)S(1)}, bf16[8,128,2304]{2,1,0:T(8,128)(2,1)S(1)}, u32[]{:S(2)}, u32[]{:S(2)}) collective-permute-start(bf16[8,128,2304]{2,1,0:T(8,128)(2,1)S(1)} %get-tuple-element.13), channel_id=1, source_target_pairs={{0,1},{1,0},{2,3},{3,2},{4,5},{5,4},{6,7},{7,6},{8,9},{9,8},{10,11... | collective-permute-start | bytes 14155784 | tf_op jit(solution)/shard_map/ppermute | solution.py:43
  4.8 7.3 %collective-permute-start.1 = (bf16[64,1152]{1,0:T(8,128)(2,1)S(1)}, bf16[64,1152]{1,0:T(8,128)(2,1)S(1)}, u32[]{:S(2)}, u32[]{:S(2)}) collective-permute-start(bf16[64,1152]{1,0:T(8,128)(2,1)S(1)} %get-tuple-element.14.refs_2_), channel_id=1, source_target_pairs={{0,4},{1,5},{4,8},{5,9},{8,12},{9,13},{12,14},{13,15},{14,10},{15,... | collective-permute-start | bytes 442376 | tf_op jit(solution)/shard_map/ppermute | solution.py:39
  7.5 6.7 %collective-permute-start.4 = (bf16[64,1152]{1,0:T(8,128)(2,1)S(1)}, bf16[64,1152]{1,0:T(8,128)(2,1)S(1)}, u32[]{:S(2)}, u32[]{:S(2)}) collective-permute-start(bf16[64,1152]{1,0:T(8,128)(2,1)S(1)} %get-tuple-element.15.refs_3_), channel_id=1, source_target_pairs={{0,2},{1,3},{4,0},{5,1},{8,4},{9,5},{12,8},{13,9},{14,12},{15,13},... | collective-permute-start | bytes 442376 | tf_op jit(solution)/shard_map/ppermute | solution.py:39
  7.5 7.8 %collective-permute-start.2 = (bf16[64,1152]{1,0:T(8,128)(2,1)S(1)}, bf16[64,1152]{1,0:T(8,128)(2,1)S(1)}, u32[]{:S(2)}, u32[]{:S(2)}) collective-permute-start(bf16[64,1152]{1,0:T(8,128)(2,1)S(1)} %get-tuple-element.15.refs_3_), channel_id=1, source_target_pairs={{0,4},{1,5},{4,8},{5,9},{8,12},{9,13},{12,14},{13,15},{14,10},{15,... | collective-permute-start | bytes 442376 | tf_op jit(solution)/shard_map/ppermute | solution.py:39
  9.5 7.8 %collective-permute-start.3 = (bf16[64,1152]{1,0:T(8,128)(2,1)S(1)}, bf16[64,1152]{1,0:T(8,128)(2,1)S(1)}, u32[]{:S(2)}, u32[]{:S(2)}) collective-permute-start(bf16[64,1152]{1,0:T(8,128)(2,1)S(1)} %get-tuple-element.14.refs_2_), channel_id=1, source_target_pairs={{0,2},{1,3},{4,0},{5,1},{8,4},{9,5},{12,8},{13,9},{14,12},{15,13},... | collective-permute-start | bytes 442376 | tf_op jit(solution)/shard_map/ppermute | solution.py:39
  12.1 6.7 %collective-permute-start.5 = (bf16[64,1152]{1,0:T(8,128)(2,1)S(1)}, bf16[64,1152]{1,0:T(8,128)(2,1)S(1)}, u32[]{:S(2)}, u32[]{:S(2)}) collective-permute-start(bf16[64,1152]{1,0:T(8,128)(2,1)S(1)} %collective-permute-done.1.refs_4_), channel_id=1, source_target_pairs={{0,4},{1,5},{4,8},{5,9},{8,12},{9,13},{12,14},{13,15},{14,10},{15,... | collective-permute-start | bytes 442376 | tf_op jit(solution)/shard_map/ppermute | solution.py:39
  14.2 6.7 %collective-permute-start.8 = (bf16[64,1152]{1,0:T(8,128)(2,1)S(1)}, bf16[64,1152]{1,0:T(8,128)(2,1)S(1)}, u32[]{:S(2)}, u32[]{:S(2)}) collective-permute-start(bf16[64,1152]{1,0:T(8,128)(2,1)S(1)} %collective-permute-done.4.refs_7_), channel_id=1, source_target_pairs={{0,2},{1,3},{4,0},{5,1},{8,4},{9,5},{12,8},{13,9},{14,12},{15,13},... | collective-permute-start | bytes 442376 | tf_op jit(solution)/shard_map/ppermute | solution.py:39
  15.3 6.8 %collective-permute-start.6 = (bf16[64,1152]{1,0:T(8,128)(2,1)S(1)}, bf16[64,1152]{1,0:T(8,128)(2,1)S(1)}, u32[]{:S(2)}, u32[]{:S(2)}) collective-permute-start(bf16[64,1152]{1,0:T(8,128)(2,1)S(1)} %collective-permute-done.2.refs_5_), channel_id=1, source_target_pairs={{0,4},{1,5},{4,8},{5,9},{8,12},{9,13},{12,14},{13,15},{14,10},{15,... | collective-permute-start | bytes 442376 | tf_op jit(solution)/shard_map/ppermute | solution.py:39
  17.3 6.8 %collective-permute-start.7 = (bf16[64,1152]{1,0:T(8,128)(2,1)S(1)}, bf16[64,1152]{1,0:T(8,128)(2,1)S(1)}, u32[]{:S(2)}, u32[]{:S(2)}) collective-permute-start(bf16[64,1152]{1,0:T(8,128)(2,1)S(1)} %collective-permute-done.3.refs_6_), channel_id=1, source_target_pairs={{0,2},{1,3},{4,0},{5,1},{8,4},{9,5},{12,8},{13,9},{14,12},{15,13},... | collective-permute-start | bytes 442376 | tf_op jit(solution)/shard_map/ppermute | solution.py:39
  18.8 7.0 %collective-permute-start.9 = (bf16[64,1152]{1,0:T(8,128)(2,1)S(1)}, bf16[64,1152]{1,0:T(8,128)(2,1)S(1)}, u32[]{:S(2)}, u32[]{:S(2)}) collective-permute-start(bf16[64,1152]{1,0:T(8,128)(2,1)S(1)} %collective-permute-done.5.refs_8_), channel_id=1, source_target_pairs={{0,4},{1,5},{4,8},{5,9},{8,12},{9,13},{12,14},{13,15},{14,10},{15,... | collective-permute-start | bytes 442376 | tf_op jit(solution)/shard_map/ppermute | solution.py:39
  20.8 6.6 %collective-permute-start.10 = (bf16[64,1152]{1,0:T(8,128)(2,1)S(1)}, bf16[64,1152]{1,0:T(8,128)(2,1)S(1)}, u32[]{:S(2)}, u32[]{:S(2)}) collective-permute-start(bf16[64,1152]{1,0:T(8,128)(2,1)S(1)} %collective-permute-done.8.refs_11_), channel_id=1, source_target_pairs={{0,2},{1,3},{4,0},{5,1},{8,4},{9,5},{12,8},{13,9},{14,12},{15,13},... | collective-permute-start | bytes 442376 | tf_op jit(solution)/shard_map/ppermute | solution.py:39
  22.0 7.4 %collective-permute-start.13 = (bf16[64,1152]{1,0:T(8,128)(2,1)S(1)}, bf16[64,1152]{1,0:T(8,128)(2,1)S(1)}, u32[]{:S(2)}, u32[]{:S(2)}) collective-permute-start(bf16[64,1152]{1,0:T(8,128)(2,1)S(1)} %collective-permute-done.6.refs_9_), channel_id=1, source_target_pairs={{0,4},{1,5},{4,8},{5,9},{8,12},{9,13},{12,14},{13,15},{14,10},{15,... | collective-permute-start | bytes 442376 | tf_op jit(solution)/shard_map/ppermute | solution.py:39
  24.1 6.0 %collective-permute-start.14 = (bf16[64,1152]{1,0:T(8,128)(2,1)S(1)}, bf16[64,1152]{1,0:T(8,128)(2,1)S(1)}, u32[]{:S(2)}, u32[]{:S(2)}) collective-permute-start(bf16[64,1152]{1,0:T(8,128)(2,1)S(1)} %collective-permute-done.7.refs_10_), channel_id=1, source_target_pairs={{0,2},{1,3},{4,0},{5,1},{8,4},{9,5},{12,8},{13,9},{14,12},{15,13},... | collective-permute-start | bytes 442376 | tf_op jit(solution)/shard_map/ppermute | solution.py:39
  27.4 5.1 %collective-permute-start.11 = (bf16[64,1152]{1,0:T(8,128)(2,1)S(1)}, bf16[64,1152]{1,0:T(8,128)(2,1)S(1)}, u32[]{:S(2)}, u32[]{:S(2)}) collective-permute-start(bf16[64,1152]{1,0:T(8,128)(2,1)S(1)} %collective-permute-done.9.refs_2_), channel_id=1, source_target_pairs={{0,4},{1,5},{4,8},{5,9},{8,12},{9,13},{12,14},{13,15},{14,10},{15,... | collective-permute-start | bytes 442376 | tf_op jit(solution)/shard_map/ppermute | solution.py:39
  29.0 5.1 %collective-permute-start.12 = (bf16[64,1152]{1,0:T(8,128)(2,1)S(1)}, bf16[64,1152]{1,0:T(8,128)(2,1)S(1)}, u32[]{:S(2)}, u32[]{:S(2)}) collective-permute-start(bf16[64,1152]{1,0:T(8,128)(2,1)S(1)} %collective-permute-done.10.refs_5_), channel_id=1, source_target_pairs={{0,2},{1,3},{4,0},{5,1},{8,4},{9,5},{12,8},{13,9},{14,12},{15,13},... | collective-permute-start | bytes 442376 | tf_op jit(solution)/shard_map/ppermute | solution.py:39
  34.6 23.0 %copy-start.1 = (bf16[8,4096]{1,0:T(8,128)(2,1)S(1)}, bf16[8,4096]{1,0:T(8,128)(2,1)}, u32[]{:S(2)}) copy-start(bf16[8,4096]{1,0:T(8,128)(2,1)} %param.11) | copy-start | bytes 196612
  34.7 1.4 %collective-permute-start.15 = (f32[256,128]{1,0:T(8,128)S(1)}, f32[256,128]{1,0:T(8,128)S(1)}, u32[]{:S(2)}, u32[]{:S(2)}) collective-permute-start(f32[256,128]{1,0:T(8,128)S(1)} %shard_map.67), channel_id=1, source_target_pairs={{0,1},{1,0},{2,3},{3,2},{4,5},{5,4},{6,7},{7,6},{8,9},{9,8},{10,11... | collective-permute-start | bytes 393224 | tf_op jit(solution)/shard_map/ppermute | solution.py:43

commit v9 on v8

--- a/solution.py
+++ b/solution.py
@@ -43,44 +43,78 @@
     return lax.ppermute(x, "dp", [(i, i ^ bit) for i in range(n)])
 
 
-def start_kernel(chips, act, grad, in_rows, out_rows, first, second, keep, send, sems):
+def column_copies(chips, core, act, grad, out, sems):
+    a_width = act.shape[1] // (2 * chips)
+    g_width = grad.shape[1] // (2 * chips)
+    copies = []
+    for chip in range(chips):
+        block = 2 * chip + core
+        for k, (ref, at, width) in enumerate(((act, 0, a_width), (grad, a_width, g_width))):
+            columns = pl.ds(pl.multiple_of(block * width, 128), width)
+            copies.append(
+                pltpu.make_async_copy(
+                    ref.at[:, columns], out.at[chip, :, pl.ds(at, width)], sems.at[chip, k]
+                )
+            )
+    return copies
+
+
+def run_copies(copies):
+    for copy in copies:
+        copy.start()
+    for copy in copies:
+        copy.wait()
+
+
+def start_kernel(chips, act, grad, in_rows, out_rows, first, second, send, sems, send_sems):
     core = lax.axis_index("dp") & 1
-    a_width, g_width = in_rows.shape[1], out_rows.shape[1]
+    a_width = in_rows.shape[1]
     cut = first.shape[1]
     pairs = [
         (in_rows, first.at[:, pl.ds(0, a_width)]),
         (out_rows.at[:, pl.ds(0, cut - a_width)], first.at[:, pl.ds(a_width, cut - a_width)]),
         (out_rows.at[:, pl.ds(cut - a_width, second.shape[1])], second),
     ]
-    for out, owner in ((send, 1 - core), (keep, core)):
-        for chip in range(chips):
-            block = 2 * chip + owner
-            for ref, at, width in ((act, 0, a_width), (grad, a_width, g_width)):
-                columns = pl.ds(pl.multiple_of(block * width, 128), width)
-                pairs.append((ref.at[:, columns], out.at[chip, :, pl.ds(at, width)]))
     copies = [pltpu.make_async_copy(*pair, sems.at[i]) for i, pair in enumerate(pairs)]
-    for copy in copies:
-        copy.start()
-    for copy in copies:
-        copy.wait()
+    run_copies(copies + column_copies(chips, 1 - core, act, grad, send, send_sems))
 
 
 def start(act, grad, in_rows, out_rows, chips):
     rows = act.shape[0]
     rank, width = in_rows.shape[0], in_rows.shape[1] + out_rows.shape[1]
     cut = width // 256 * 128
-    shapes = [(rank, cut), (rank, width - cut)] + [(chips, rows, width)] * 2
+    shapes = (rank, cut), (rank, width - cut), (chips, rows, width)
     return pl.pallas_call(
         functools.partial(start_kernel, chips),
         out_shape=[pltpu.VMEM(shape, act.dtype) for shape in shapes],
         in_specs=[HBM] * 4,
-        out_specs=[VMEM] * 4,
-        scratch_shapes=[pltpu.SemaphoreType.DMA((3 + 4 * chips,))],
+        out_specs=[VMEM] * 3,
+        scratch_shapes=[pltpu.SemaphoreType.DMA((3,)), pltpu.SemaphoreType.DMA((chips, 2))],
         compiler_params=pltpu.CompilerParams(vmem_limit_bytes=16 * 2**20),
         cost_estimate=pl.CostEstimate(
-            flops=0, bytes_accessed=4 * (rank + 2 * chips * rows) * width, transcendentals=0
+            flops=0, bytes_accessed=4 * (rank + chips * rows) * width, transcendentals=0
         ),
     )(*held(pltpu.HBM, act, grad, in_rows, out_rows))
+
+
+def keep_kernel(chips, act, grad, keep, sems):
+    core = lax.axis_index("dp") & 1
+    run_copies(column_copies(chips, core, act, grad, keep, sems))
+
+
+def keep_columns(act, grad, chips):
+    rows, width = act.shape[0], (act.shape[1] + grad.shape[1]) // (2 * chips)
+    return pl.pallas_call(
+        functools.partial(keep_kernel, chips),
+        out_shape=pltpu.VMEM((chips, rows, width), act.dtype),
+        in_specs=[HBM] * 2,
+        out_specs=VMEM,
+        scratch_shapes=[pltpu.SemaphoreType.DMA((chips, 2))],
+        compiler_params=pltpu.CompilerParams(vmem_limit_bytes=16 * 2**20),
+        cost_estimate=pl.CostEstimate(
+            flops=0, bytes_accessed=4 * chips * rows * width, transcendentals=0
+        ),
+    )(*held(pltpu.HBM, act, grad))
 
 
 def project_kernel(chips, offsets, a_width, carry, *refs):
@@ -138,21 +172,23 @@
     chips = n // 2
     split = LEN // rows
 
-    *own, keep, send = start(activations, out_grads, in_basis.T, out_basis.T, chips)
-    tokens = (keep, swap(send, 1, n))
+    *own, send = start(activations, out_grads, in_basis.T, out_basis.T, chips)
+    theirs = swap(send, 1, n)
     up, down = [own], [own]
-    for i in range(chips // 2 - 1):
-        up.append(tuple(ring(x, 1, chips) for x in up[-1]))
-        down.append(tuple(ring(x, -1, chips) for x in down[-1]))
-    run = functools.partial(project, tokens, a_width=a_width)
+    for _ in range(chips // 2 - 1):
+        up.append([ring(x, 1, chips) for x in up[-1]])
+        down.append([ring(x, -1, chips) for x in down[-1]])
+    last = chips // 2 - 1
+    keep = keep_columns(activations, out_grads, chips)
+    keep, far_up, far_down = lax.optimization_barrier((keep, up[last][0], down[last][1]))
+    far = (ring(far_up, 1, chips), ring(far_down, -1, chips))
+
+    run = functools.partial(project, (keep, theirs), a_width=a_width)
     near, offsets = [own], [0]
-    for i in range(1, chips // 2 - 1):
+    for i in range(1, last):
         near += [up[i], down[i]]
         offsets += [i, -i]
     total = run(near, offsets)
-    total, far_up, far_down = lax.optimization_barrier((total, up[-1][0], down[-1][1]))
-    far = (ring(far_up, 1, chips), ring(far_down, -1, chips))
-    last = chips // 2 - 1
     total = run([up[last], down[last]], [last, -last], carry=total)
     total = run([far], [chips // 2], carry=total)
     theirs = swap(total, 1, n)

time: 58.6 us -> 57.8 us (0.986)
  waiting for transfers between devices: 13.2 us -> 10.7 us
  Pallas kernels: 7.4 us -> 8.31 us
  blocking collectives: 20 us -> 20.8 us
    ppermute x14, waiting for transfers between devices: 11.9 us -> 9.39 us  [ring(): return lax.ppermute(x, 'dp', pairs)]
    pallas_call x0 -> x1, Pallas kernels: none -> 2.49 us  [keep_columns(): pl.pallas_call(functools.partial(keep_kernel, chips), out_shape=pltpu.VME...]
    pallas_call x1, Pallas kernels: 4.31 us -> 2.74 us  [start(): pl.pallas_call(functools.partial(start_kernel, chips), out_shape=[pltpu.V...]
    all_to_all x2, blocking collectives: 20 us -> 20.8 us  [to_all(): lax.all_to_all(copies, 'dp', 0, 0, axis_index_groups=groups, tiled=True)]
  transfers between devices with their start and end apart: 16 -> 16, of which waited for: 9 -> 8; matrix products, arithmetic and copies ran while one was open for 0% -> 0% of each run, Pallas kernels for 4% -> 9%
where the time goes in v9:
time: 57.8 us; the launch traced here: 57.6 us
  blocking collectives  20.8 us (36%)
  starting transfers between devices  15.4 us (27%)
  waiting for transfers between devices  10.7 us (19%)
  Pallas kernels  8.31 us (14%)
  matrix products  1.61 us (3%)
    all_to_all x2, blocking collectives, to_all(): lax.all_to_all(copies, 'dp', 0, 0, axis_index_groups=groups, tiled=True)  20.8 us
    ppermute x14, starting transfers between devices, ring(): return lax.ppermute(x, 'dp', pairs)  14.8 us
    ppermute x14, waiting for transfers between devices, ring(): return lax.ppermute(x, 'dp', pairs)  9.39 us
    pallas_call x3, Pallas kernels, project(): pl.pallas_call(functools.partial(project_kernel, chips, offsets, a_width,...  3.08 us
    pallas_call x1, Pallas kernels, start(): pl.pallas_call(functools.partial(start_kernel, chips), out_shape=[pltpu.V...  2.74 us
    pallas_call x1, Pallas kernels, keep_columns(): pl.pallas_call(functools.partial(keep_kernel, chips), out_shape=pltpu.VME...  2.49 us
    dot_general x3, matrix products, dot(): return lax.dot_general(a, b, dims, preferred_element_type=jnp.float32)  1.61 us
    ppermute x2, waiting for transfers between devices, swap(): return lax.ppermute(x, 'dp', [(i, i ^ bit) for i in range(n)])  1.34 us
  transfers between devices with their start and end apart: 16, of which 8 were waited for; matrix products, arithmetic and copies ran while one was open for 0% of the time, Pallas kernels for 9%

profile of v9, /device:TPU:0, one launch (start us, length us, event | category | flops | bytes accessed | tf_op | source)
XLA Modules:
  0.0 57.6 jit_solution(15519314618770106883)
XLA Ops:
  0.0 2.7 %shard_map.65 = (bf16[64,1152]{1,0:T(8,128)(2,1)S(1)}, bf16[64,1152]{1,0:T(8,128)(2,1)S(1)}, bf16[8,128,2304]{2,1,0:T(8,128)(2,1)S(1)}) custom-call(bf16[128,8192]{1,0:T(8,128)(2,1)} %act.3, bf16[128,28672]{1,0:T(8,128)(2,1)} %grad.3, bf16[64,512]{1,0:T(8,128)(2,1)} %bitcast.10, bf16[64,1792]{1,0:T(8,128)(2,1)} %bitcast.9), custom_call_target="tpu_custom_call" | custom-call | bytes 10027008 | tf_op jit(solution)/shard_map/pallas_call | solution.py:87
  2.8 0.5 collective-permute-start.6
  3.3 2.6 %collective-permute-start = (bf16[64,1152]{1,0:T(8,128)(2,1)S(1)}, bf16[64,1152]{1,0:T(8,128)(2,1)S(1)}, u32[]{:S(2)}, u32[]{:S(2)}) collective-permute-start(bf16[64,1152]{1,0:T(8,128)(2,1)S(1)} %get-tuple-element.11.refs_2_), channel_id=1, source_target_pairs={{0,4},{1,5},{4,8},{5,9},{8,12},{9,13},{12,14},{13,15},{14,10},{15,... | collective-permute-start | bytes 442376 | tf_op jit(solution)/shard_map/ppermute | solution.py:39
  5.9 2.0 %collective-permute-start.9 = (bf16[64,1152]{1,0:T(8,128)(2,1)S(1)}, bf16[64,1152]{1,0:T(8,128)(2,1)S(1)}, u32[]{:S(2)}, u32[]{:S(2)}) collective-permute-start(bf16[64,1152]{1,0:T(8,128)(2,1)S(1)} %get-tuple-element.12.refs_3_), channel_id=1, source_target_pairs={{0,4},{1,5},{4,8},{5,9},{8,12},{9,13},{12,14},{13,15},{14,10},{15,... | collective-permute-start | bytes 442376 | tf_op jit(solution)/shard_map/ppermute | solution.py:39
  8.0 2.6 %collective-permute-done.refs_4_ = bf16[64,1152]{1,0:T(8,128)(2,1)S(1)} collective-permute-done((bf16[64,1152]{1,0:T(8,128)(2,1)S(1)}, bf16[64,1152]{1,0:T(8,128)(2,1)S(1)}, u32[]{:S(2)}, u32[]{:S(2)}) %collective-permute-start) | collective-permute-done | bytes 147488 | tf_op jit(solution)/shard_map/ppermute | solution.py:39
  10.6 2.0 %collective-permute-start.1 = (bf16[64,1152]{1,0:T(8,128)(2,1)S(1)}, bf16[64,1152]{1,0:T(8,128)(2,1)S(1)}, u32[]{:S(2)}, u32[]{:S(2)}) collective-permute-start(bf16[64,1152]{1,0:T(8,128)(2,1)S(1)} %collective-permute-done.refs_4_), channel_id=1, source_target_pairs={{0,4},{1,5},{4,8},{5,9},{8,12},{9,13},{12,14},{13,15},{14,10},{15,... | collective-permute-start | bytes 442376 | tf_op jit(solution)/shard_map/ppermute | solution.py:39
  12.6 1.1 %collective-permute-done.9.refs_5_ = bf16[64,1152]{1,0:T(8,128)(2,1)S(1)} collective-permute-done((bf16[64,1152]{1,0:T(8,128)(2,1)S(1)}, bf16[64,1152]{1,0:T(8,128)(2,1)S(1)}, u32[]{:S(2)}, u32[]{:S(2)}) %collective-permute-start.9) | collective-permute-done | bytes 147488 | tf_op jit(solution)/shard_map/ppermute | solution.py:39
  13.7 2.0 %collective-permute-start.10 = (bf16[64,1152]{1,0:T(8,128)(2,1)S(1)}, bf16[64,1152]{1,0:T(8,128)(2,1)S(1)}, u32[]{:S(2)}, u32[]{:S(2)}) collective-permute-start(bf16[64,1152]{1,0:T(8,128)(2,1)S(1)} %collective-permute-done.9.refs_5_), channel_id=1, source_target_pairs={{0,4},{1,5},{4,8},{5,9},{8,12},{9,13},{12,14},{13,15},{14,10},{15,... | collective-permute-start | bytes 442376 | tf_op jit(solution)/shard_map/ppermute | solution.py:39
  15.8 1.5 %collective-permute-done.1.refs_8_ = bf16[64,1152]{1,0:T(8,128)(2,1)S(1)} collective-permute-done((bf16[64,1152]{1,0:T(8,128)(2,1)S(1)}, bf16[64,1152]{1,0:T(8,128)(2,1)S(1)}, u32[]{:S(2)}, u32[]{:S(2)}) %collective-permute-start.1) | collective-permute-done | bytes 147488 | tf_op jit(solution)/shard_map/ppermute | solution.py:39
  17.3 2.0 %collective-permute-start.2 = (bf16[64,1152]{1,0:T(8,128)(2,1)S(1)}, bf16[64,1152]{1,0:T(8,128)(2,1)S(1)}, u32[]{:S(2)}, u32[]{:S(2)}) collective-permute-start(bf16[64,1152]{1,0:T(8,128)(2,1)S(1)} %collective-permute-done.1.refs_8_), channel_id=1, source_target_pairs={{0,4},{1,5},{4,8},{5,9},{8,12},{9,13},{12,14},{13,15},{14,10},{15,... | collective-permute-start | bytes 442376 | tf_op jit(solution)/shard_map/ppermute | solution.py:39
  19.3 1.2 %collective-permute-done.10.refs_9_ = bf16[64,1152]{1,0:T(8,128)(2,1)S(1)} collective-permute-done((bf16[64,1152]{1,0:T(8,128)(2,1)S(1)}, bf16[64,1152]{1,0:T(8,128)(2,1)S(1)}, u32[]{:S(2)}, u32[]{:S(2)}) %collective-permute-start.10) | collective-permute-done | bytes 147488 | tf_op jit(solution)/shard_map/ppermute | solution.py:39
  20.5 2.0 %collective-permute-start.11 = (bf16[64,1152]{1,0:T(8,128)(2,1)S(1)}, bf16[64,1152]{1,0:T(8,128)(2,1)S(1)}, u32[]{:S(2)}, u32[]{:S(2)}) collective-permute-start(bf16[64,1152]{1,0:T(8,128)(2,1)S(1)} %collective-permute-done.10.refs_9_), channel_id=1, source_target_pairs={{0,4},{1,5},{4,8},{5,9},{8,12},{9,13},{12,14},{13,15},{14,10},{15,... | collective-permute-start | bytes 442376 | tf_op jit(solution)/shard_map/ppermute | solution.py:39
  22.5 2.5 %shard_map.64.refs_0_ = bf16[8,128,2304]{2,1,0:T(8,128)(2,1)S(1)} custom-call(bf16[128,8192]{1,0:T(8,128)(2,1)} %act.3, bf16[128,28672]{1,0:T(8,128)(2,1)} %grad.3), custom_call_target="tpu_custom_call" | custom-call | bytes 9437184 | tf_op jit(solution)/shard_map/pallas_call | solution.py:107
  25.1 0.8 %collective-permute-done.5.refs_5_ = bf16[64,1152]{1,0:T(8,128)(2,1)S(1)} collective-permute-done((bf16[64,1152]{1,0:T(8,128)(2,1)S(1)}, bf16[64,1152]{1,0:T(8,128)(2,1)S(1)}, u32[]{:S(2)}, u32[]{:S(2)}) %collective-permute-start.5) | collective-permute-done | bytes 147488 | tf_op jit(solution)/shard_map/ppermute | solution.py:39
  25.8 1.6 %collective-permute-start.7 = (bf16[64,1152]{1,0:T(8,128)(2,1)S(1)}, bf16[64,1152]{1,0:T(8,128)(2,1)S(1)}, u32[]{:S(2)}, u32[]{:S(2)}) collective-permute-start(bf16[64,1152]{1,0:T(8,128)(2,1)S(1)} %collective-permute-done.2.refs_2_), channel_id=1, source_target_pairs={{0,4},{1,5},{4,8},{5,9},{8,12},{9,13},{12,14},{13,15},{14,10},{15,... | collective-permute-start | bytes 442376 | tf_op jit(solution)/shard_map/ppermute | solution.py:39
  27.9 1.7 %shard_map.66.refs_6_ = f32[256,128]{1,0:T(8,128)S(1)} custom-call(bf16[8,128,2304]{2,1,0:T(8,128)(2,1)S(1)} %shard_map.64.refs_0_, bf16[8,128,2304]{2,1,0:T(8,128)(2,1)S(1)} %collective-permute-done.6.refs_1_, bf16[64,1152]{1,0:T(8,128)(2,1)S(1)} %get-tuple-element.11.refs_2_, bf16[64,1152]{1,0:T(8,128)(2,1)S(1)} %get-tuple-element.12.refs_3_, ...), custom_call_target="tpu_custom_call" | custom-call | flops 377487360 | bytes 7372800 | tf_op jit(solution)/shard_map/pallas_call | solution.py:149
  29.6 0.8 %shard_map.67.refs_4_ = f32[256,128]{1,0:T(8,128)S(1)} custom-call(bf16[8,128,2304]{2,1,0:T(8,128)(2,1)S(1)} %shard_map.64.refs_0_, bf16[8,128,2304]{2,1,0:T(8,128)(2,1)S(1)} %collective-permute-done.6.refs_1_, bf16[64,1152]{1,0:T(8,128)(2,1)S(1)} %collective-permute-done.2.refs_2_, bf16[64,1152]{1,0:T(8,128)(2,1)S(1)} %collective-permute-done.11.refs_3_, ...), custom_call_target="tpu_custom_call" | custom-call | flops 150994944 | bytes 2949120 | tf_op jit(solution)/shard_map/pallas_call | solution.py:149
  30.5 0.5 collective-permute-done.7.refs_2_
  31.0 1.6 %collective-permute-done.8.refs_3_ = bf16[64,1152]{1,0:T(8,128)(2,1)S(1)} collective-permute-done((bf16[64,1152]{1,0:T(8,128)(2,1)S(1)}, bf16[64,1152]{1,0:T(8,128)(2,1)S(1)}, u32[]{:S(2)}, u32[]{:S(2)}) %collective-permute-start.8) | collective-permute-done | bytes 147488 | tf_op jit(solution)/shard_map/ppermute | solution.py:39
  33.2 1.3 %collective-permute-done.15 = f32[256,128]{1,0:T(8,128)S(1)} collective-permute-done((f32[256,128]{1,0:T(8,128)S(1)}, f32[256,128]{1,0:T(8,128)S(1)}, u32[]{:S(2)}, u32[]{:S(2)}) %collective-permute-start.15) | collective-permute-done | bytes 131104 | tf_op jit(solution)/shard_map/ppermute | solution.py:43
  34.9 11.7 %all_to_all.10 = f32[8,1,4096]{2,1,0:T(1,128)S(1)} all-to-all(f32[8,1,4096]{2,1,0:T(1,128)S(1)} %broadcast_in_dim.4), channel_id=1, replica_groups={{0,2,4,6,8,10,12,14},{1,3,5,7,9,11,13,15},{16,18,20,22,24,26,28,30},{17..., dimensions={0} | all-to-all | bytes 262144 | tf_op jit(solution)/shard_map/all_to_all | solution.py:165
  47.1 0.6 %convolution_convert_fusion = bf16[2,256]{1,0:T(2,128)(2,1)S(1)} fusion(bf16[256,4096]{1,0:T(8,128)(2,1)S(1)} %copy-done, bf16[2,4096]{1,0:T(2,128)(2,1)S(1)} %reduce_sum.9), kind=kOutput, calls=%fused_computation.1 | convolution fusion | flops 4194816 | bytes 2114560 | tf_op jit(solution)/shard_map/dot_general | solution.py:23
  47.8 9.1 %all_to_all.11 = bf16[16,2,256]{2,1,0:T(2,128)(2,1)S(1)} all-to-all(bf16[16,2,256]{2,1,0:T(2,128)(2,1)S(1)} %broadcast_in_dim.5), channel_id=1, replica_groups={{0,1,2,3,4,5,6,7,8,9,10,11,12,13,14,15},{16,17,18,19,20,21,22,23,24,25,..., dimensions={0} | all-to-all | bytes 32768 | tf_op jit(solution)/shard_map/all_to_all | solution.py:165
  56.9 0.7 %convolution_multiply_fusion.1 = f32[2,8]{1,0:T(2,128)} fusion(bf16[2,4096]{1,0:T(2,128)(2,1)S(1)} %bitcast.11, bf16[8,4096]{1,0:T(8,128)(2,1)S(1)} %copy-done.1), kind=kOutput, calls=%fused_computation.2 | convolution fusion | flops 131088 | bytes 81984 | tf_op jit(solution)/shard_map/dot_general | solution.py:23
  (30 shorter events, 2.1 us)
Async XLA Ops:
  0.0 47.1 %copy-start = (bf16[256,4096]{1,0:T(8,128)(2,1)S(1)}, bf16[256,4096]{1,0:T(8,128)(2,1)}, u32[]{:S(2)}) copy-start(bf16[256,4096]{1,0:T(8,128)(2,1)} %param.10) | copy-start | bytes 6291460
  2.8 25.1 %collective-permute-start.6 = (bf16[8,128,2304]{2,1,0:T(8,128)(2,1)S(1)}, bf16[8,128,2304]{2,1,0:T(8,128)(2,1)S(1)}, u32[]{:S(2)}, u32[]{:S(2)}) collective-permute-start(bf16[8,128,2304]{2,1,0:T(8,128)(2,1)S(1)} %get-tuple-element.14), channel_id=1, source_target_pairs={{0,1},{1,0},{2,3},{3,2},{4,5},{5,4},{6,7},{7,6},{8,9},{9,8},{10,11... | collective-permute-start | bytes 14155784 | tf_op jit(solution)/shard_map/ppermute | solution.py:43
  3.3 7.3 %collective-permute-start = (bf16[64,1152]{1,0:T(8,128)(2,1)S(1)}, bf16[64,1152]{1,0:T(8,128)(2,1)S(1)}, u32[]{:S(2)}, u32[]{:S(2)}) collective-permute-start(bf16[64,1152]{1,0:T(8,128)(2,1)S(1)} %get-tuple-element.11.refs_2_), channel_id=1, source_target_pairs={{0,4},{1,5},{4,8},{5,9},{8,12},{9,13},{12,14},{13,15},{14,10},{15,... | collective-permute-start | bytes 442376 | tf_op jit(solution)/shard_map/ppermute | solution.py:39
  5.9 6.7 %collective-permute-start.3 = (bf16[64,1152]{1,0:T(8,128)(2,1)S(1)}, bf16[64,1152]{1,0:T(8,128)(2,1)S(1)}, u32[]{:S(2)}, u32[]{:S(2)}) collective-permute-start(bf16[64,1152]{1,0:T(8,128)(2,1)S(1)} %get-tuple-element.12.refs_3_), channel_id=1, source_target_pairs={{0,2},{1,3},{4,0},{5,1},{8,4},{9,5},{12,8},{13,9},{14,12},{15,13},... | collective-permute-start | bytes 442376 | tf_op jit(solution)/shard_map/ppermute | solution.py:39
  5.9 7.8 %collective-permute-start.9 = (bf16[64,1152]{1,0:T(8,128)(2,1)S(1)}, bf16[64,1152]{1,0:T(8,128)(2,1)S(1)}, u32[]{:S(2)}, u32[]{:S(2)}) collective-permute-start(bf16[64,1152]{1,0:T(8,128)(2,1)S(1)} %get-tuple-element.12.refs_3_), channel_id=1, source_target_pairs={{0,4},{1,5},{4,8},{5,9},{8,12},{9,13},{12,14},{13,15},{14,10},{15,... | collective-permute-start | bytes 442376 | tf_op jit(solution)/shard_map/ppermute | solution.py:39
  7.9 7.8 %collective-permute-start.12 = (bf16[64,1152]{1,0:T(8,128)(2,1)S(1)}, bf16[64,1152]{1,0:T(8,128)(2,1)S(1)}, u32[]{:S(2)}, u32[]{:S(2)}) collective-permute-start(bf16[64,1152]{1,0:T(8,128)(2,1)S(1)} %get-tuple-element.11.refs_2_), channel_id=1, source_target_pairs={{0,2},{1,3},{4,0},{5,1},{8,4},{9,5},{12,8},{13,9},{14,12},{15,13},... | collective-permute-start | bytes 442376 | tf_op jit(solution)/shard_map/ppermute | solution.py:39
  10.6 6.7 %collective-permute-start.1 = (bf16[64,1152]{1,0:T(8,128)(2,1)S(1)}, bf16[64,1152]{1,0:T(8,128)(2,1)S(1)}, u32[]{:S(2)}, u32[]{:S(2)}) collective-permute-start(bf16[64,1152]{1,0:T(8,128)(2,1)S(1)} %collective-permute-done.refs_4_), channel_id=1, source_target_pairs={{0,4},{1,5},{4,8},{5,9},{8,12},{9,13},{12,14},{13,15},{14,10},{15,... | collective-permute-start | bytes 442376 | tf_op jit(solution)/shard_map/ppermute | solution.py:39
  12.6 6.7 %collective-permute-start.4 = (bf16[64,1152]{1,0:T(8,128)(2,1)S(1)}, bf16[64,1152]{1,0:T(8,128)(2,1)S(1)}, u32[]{:S(2)}, u32[]{:S(2)}) collective-permute-start(bf16[64,1152]{1,0:T(8,128)(2,1)S(1)} %collective-permute-done.3.refs_7_), channel_id=1, source_target_pairs={{0,2},{1,3},{4,0},{5,1},{8,4},{9,5},{12,8},{13,9},{14,12},{15,13},... | collective-permute-start | bytes 442376 | tf_op jit(solution)/shard_map/ppermute | solution.py:39
  13.7 6.8 %collective-permute-start.10 = (bf16[64,1152]{1,0:T(8,128)(2,1)S(1)}, bf16[64,1152]{1,0:T(8,128)(2,1)S(1)}, u32[]{:S(2)}, u32[]{:S(2)}) collective-permute-start(bf16[64,1152]{1,0:T(8,128)(2,1)S(1)} %collective-permute-done.9.refs_5_), channel_id=1, source_target_pairs={{0,4},{1,5},{4,8},{5,9},{8,12},{9,13},{12,14},{13,15},{14,10},{15,... | collective-permute-start | bytes 442376 | tf_op jit(solution)/shard_map/ppermute | solution.py:39
  15.8 6.8 %collective-permute-start.13 = (bf16[64,1152]{1,0:T(8,128)(2,1)S(1)}, bf16[64,1152]{1,0:T(8,128)(2,1)S(1)}, u32[]{:S(2)}, u32[]{:S(2)}) collective-permute-start(bf16[64,1152]{1,0:T(8,128)(2,1)S(1)} %collective-permute-done.12.refs_6_), channel_id=1, source_target_pairs={{0,2},{1,3},{4,0},{5,1},{8,4},{9,5},{12,8},{13,9},{14,12},{15,13},... | collective-permute-start | bytes 442376 | tf_op jit(solution)/shard_map/ppermute | solution.py:39
  17.3 7.8 %collective-permute-start.2 = (bf16[64,1152]{1,0:T(8,128)(2,1)S(1)}, bf16[64,1152]{1,0:T(8,128)(2,1)S(1)}, u32[]{:S(2)}, u32[]{:S(2)}) collective-permute-start(bf16[64,1152]{1,0:T(8,128)(2,1)S(1)} %collective-permute-done.1.refs_8_), channel_id=1, source_target_pairs={{0,4},{1,5},{4,8},{5,9},{8,12},{9,13},{12,14},{13,15},{14,10},{15,... | collective-permute-start | bytes 442376 | tf_op jit(solution)/shard_map/ppermute | solution.py:39
  19.3 6.6 %collective-permute-start.5 = (bf16[64,1152]{1,0:T(8,128)(2,1)S(1)}, bf16[64,1152]{1,0:T(8,128)(2,1)S(1)}, u32[]{:S(2)}, u32[]{:S(2)}) collective-permute-start(bf16[64,1152]{1,0:T(8,128)(2,1)S(1)} %collective-permute-done.4.refs_11_), channel_id=1, source_target_pairs={{0,2},{1,3},{4,0},{5,1},{8,4},{9,5},{12,8},{13,9},{14,12},{15,13},... | collective-permute-start | bytes 442376 | tf_op jit(solution)/shard_map/ppermute | solution.py:39
  20.5 9.1 %collective-permute-start.11 = (bf16[64,1152]{1,0:T(8,128)(2,1)S(1)}, bf16[64,1152]{1,0:T(8,128)(2,1)S(1)}, u32[]{:S(2)}, u32[]{:S(2)}) collective-permute-start(bf16[64,1152]{1,0:T(8,128)(2,1)S(1)} %collective-permute-done.10.refs_9_), channel_id=1, source_target_pairs={{0,4},{1,5},{4,8},{5,9},{8,12},{9,13},{12,14},{13,15},{14,10},{15,... | collective-permute-start | bytes 442376 | tf_op jit(solution)/shard_map/ppermute | solution.py:39
  22.5 7.1 %collective-permute-start.14 = (bf16[64,1152]{1,0:T(8,128)(2,1)S(1)}, bf16[64,1152]{1,0:T(8,128)(2,1)S(1)}, u32[]{:S(2)}, u32[]{:S(2)}) collective-permute-start(bf16[64,1152]{1,0:T(8,128)(2,1)S(1)} %collective-permute-done.13.refs_10_), channel_id=1, source_target_pairs={{0,2},{1,3},{4,0},{5,1},{8,4},{9,5},{12,8},{13,9},{14,12},{15,13},... | collective-permute-start | bytes 442376 | tf_op jit(solution)/shard_map/ppermute | solution.py:39
  25.8 5.1 %collective-permute-start.7 = (bf16[64,1152]{1,0:T(8,128)(2,1)S(1)}, bf16[64,1152]{1,0:T(8,128)(2,1)S(1)}, u32[]{:S(2)}, u32[]{:S(2)}) collective-permute-start(bf16[64,1152]{1,0:T(8,128)(2,1)S(1)} %collective-permute-done.2.refs_2_), channel_id=1, source_target_pairs={{0,4},{1,5},{4,8},{5,9},{8,12},{9,13},{12,14},{13,15},{14,10},{15,... | collective-permute-start | bytes 442376 | tf_op jit(solution)/shard_map/ppermute | solution.py:39
  27.4 5.1 %collective-permute-start.8 = (bf16[64,1152]{1,0:T(8,128)(2,1)S(1)}, bf16[64,1152]{1,0:T(8,128)(2,1)S(1)}, u32[]{:S(2)}, u32[]{:S(2)}) collective-permute-start(bf16[64,1152]{1,0:T(8,128)(2,1)S(1)} %collective-permute-done.5.refs_5_), channel_id=1, source_target_pairs={{0,2},{1,3},{4,0},{5,1},{8,4},{9,5},{12,8},{13,9},{14,12},{15,13},... | collective-permute-start | bytes 442376 | tf_op jit(solution)/shard_map/ppermute | solution.py:39
  33.1 23.8 %copy-start.1 = (bf16[8,4096]{1,0:T(8,128)(2,1)S(1)}, bf16[8,4096]{1,0:T(8,128)(2,1)}, u32[]{:S(2)}) copy-start(bf16[8,4096]{1,0:T(8,128)(2,1)} %param.11) | copy-start | bytes 196612
  33.1 1.4 %collective-permute-start.15 = (f32[256,128]{1,0:T(8,128)S(1)}, f32[256,128]{1,0:T(8,128)S(1)}, u32[]{:S(2)}, u32[]{:S(2)}) collective-permute-start(f32[256,128]{1,0:T(8,128)S(1)} %shard_map.68), channel_id=1, source_target_pairs={{0,1},{1,0},{2,3},{3,2},{4,5},{5,4},{6,7},{7,6},{8,9},{9,8},{10,11... | collective-permute-start | bytes 393224 | tf_op jit(solution)/shard_map/ppermute | solution.py:43

commit v10 on v9

--- a/solution.py
+++ b/solution.py
@@ -117,47 +117,67 @@
     )(*held(pltpu.HBM, act, grad))
 
 
-def project_kernel(chips, offsets, a_width, carry, *refs):
+def project_kernel(chips, offsets, parts, a_width, cut, carry, *refs):
     keep, theirs = refs[:2]
-    blocks, refs = refs[2 : 2 + 2 * len(offsets)], refs[2 + 2 * len(offsets) :]
+    chunks, refs = refs[2 : 2 + len(parts)], refs[2 + len(parts) :]
     out = refs[-1]
-    rank, cut = blocks[0].shape
+    rank = chunks[0].shape[0]
     width = keep.shape[2]
     if carry:
         a_sum, g_sum = refs[0][:, :rank], refs[0][:, rank:]
     else:
         a_sum = g_sum = jnp.zeros((out.shape[0], rank), jnp.float32)
-    for i, offset in enumerate(offsets):
+    for offset, part, chunk in zip(offsets, parts, chunks):
         chip = chip_behind(offset, chips)
 
         def tokens(first, last):
             return jnp.concatenate([ref[chip, :, first:last] for ref in (keep, theirs)], axis=0)
 
-        a_sum += dot(tokens(0, a_width), blocks[2 * i][:, :a_width], NT)
-        g_sum += dot(tokens(a_width, cut), blocks[2 * i][:, a_width:], NT)
-        g_sum += dot(tokens(cut, width), blocks[2 * i + 1][...], NT)
+        if part == 0:
+            a_sum += dot(tokens(0, a_width), chunk[:, :a_width], NT)
+            g_sum += dot(tokens(a_width, cut), chunk[:, a_width:], NT)
+        else:
+            g_sum += dot(tokens(cut, width), chunk[...], NT)
     out[:, :rank] = a_sum
     out[:, rank:] = g_sum
 
 
-def project(tokens, blocks, offsets, a_width, carry=None):
+def project(tokens, chunks, a_width, cut, carry=None):
     chips, rows, width = tokens[0].shape
-    count = len(offsets)
-    rank = blocks[0][0].shape[0]
-    flat = [x for block in blocks for x in block]
+    offsets, parts, flat = zip(*chunks)
+    rank = flat[0].shape[0]
     carried = () if carry is None else (carry,)
-    return pl.pallas_call(
-        functools.partial(project_kernel, chips, offsets, a_width, carry is not None),
+    columns = sum(x.shape[1] for x in flat)
+    return pl.pallas_call(
+        functools.partial(project_kernel, chips, offsets, parts, a_width, cut, carry is not None),
         out_shape=pltpu.VMEM((2 * rows, 2 * rank), jnp.float32),
         in_specs=[VMEM] * (2 + len(flat) + len(carried)),
         out_specs=VMEM,
         compiler_params=pltpu.CompilerParams(vmem_limit_bytes=16 * 2**20),
         cost_estimate=pl.CostEstimate(
-            flops=4 * count * rows * rank * width,
-            bytes_accessed=count * (2 * rows + rank) * width * 2,
+            flops=4 * rows * rank * columns,
+            bytes_accessed=(2 * rows + rank) * columns * 2,
             transcendentals=0,
         ),
     )(*held(pltpu.VMEM, *tokens, *flat, *carried))
+
+
+def score_kernel(scale, conditioned, queries, out):
+    width = conditioned.shape[2]
+    total = jnp.zeros(out.shape, jnp.float32)
+    for i in range(conditioned.shape[0]):
+        total += dot(conditioned[i], queries[:, i * width : (i + 1) * width], NT)
+    out[...] = total * scale
+
+
+def score(conditioned, queries, scale):
+    return pl.pallas_call(
+        functools.partial(score_kernel, scale),
+        out_shape=jax.ShapeDtypeStruct((conditioned.shape[1], queries.shape[0]), jnp.float32),
+        in_specs=[VMEM] * 2,
+        out_specs=VMEM,
+        compiler_params=pltpu.CompilerParams(vmem_limit_bytes=16 * 2**20),
+    )(*held(pltpu.VMEM, conditioned, queries))
 
 
 def to_all(x, groups):
@@ -183,27 +203,31 @@
     keep, far_up, far_down = lax.optimization_barrier((keep, up[last][0], down[last][1]))
     far = (ring(far_up, 1, chips), ring(far_down, -1, chips))
 
-    run = functools.partial(project, (keep, theirs), a_width=a_width)
-    near, offsets = [own], [0]
+    cut = own[0].shape[1]
+    run = functools.partial(project, (keep, theirs), a_width=a_width, cut=cut)
+
+    def both(block, offset):
+        return [(offset, part, x) for part, x in enumerate(block)]
+
+    near = both(own, 0)
     for i in range(1, last):
-        near += [up[i], down[i]]
-        offsets += [i, -i]
-    total = run(near, offsets)
-    total = run([up[last], down[last]], [last, -last], carry=total)
-    total = run([far], [chips // 2], carry=total)
+        near += both(up[i], i) + both(down[i], -i)
+    total = run(near)
+    total = run(both(up[last], last) + both(down[last], -last), carry=total)
+    for part, x in enumerate(far):
+        total = run([(chips // 2, part, x)], carry=total)
     theirs = swap(total, 1, n)
     total = (total + jnp.concatenate([theirs[rows:], theirs[:rows]], axis=0)).astype(jnp.bfloat16)
 
     raw = dot(total[:, rank:], total[:, :rank], TN)
-    raw = raw.reshape(1, rank * rank) * (1.0 / math.sqrt(LEN))
+    raw = (raw * (1.0 / math.sqrt(LEN))).reshape(-1, 128)
     planes = [[2 * i + c for i in range(chips)] for c in range(2)]
-    raw = to_all(raw, planes).reshape(-1, split // 2, rank * rank)
-    features = raw.sum(axis=1).astype(jnp.bfloat16)
+    raw = to_all(raw, planes)
+    features = raw.reshape((-1, split // 2) + raw.shape[1:]).sum(axis=1)
+    features = features.astype(jnp.bfloat16).reshape(-1, rank * rank)
 
     conditioned = dot(features, preconditioner, NT).astype(jnp.bfloat16)
-    conditioned = to_all(conditioned, [list(range(n))])
-    conditioned = conditioned.transpose(1, 0, 2).reshape(-1, queries.shape[1])
-    return dot(conditioned, queries, NT) * (1.0 / rank)
+    return score(to_all(conditioned, [list(range(n))]), queries, 1.0 / rank)
 
 
 def local_gathered(activations, out_grads, in_basis, out_basis, preconditioner, queries):

time: 57.8 us -> 57.1 us (0.988)
  Pallas kernels: 8.31 us -> 9.26 us
  matrix products: 1.61 us -> 0.89 us
    pallas_call x3 -> x5, Pallas kernels: 3.08 us -> 4.03 us  [the longest x4 3.29 us: project(): pl.pallas_call(functools.partial(project_kernel, chips, offsets, parts, a...]
    dot_general x3 -> x2, matrix products: 1.61 us -> 0.89 us  [dot(): return lax.dot_general(a, b, dims, preferred_element_type=jnp.float32)]
  transfers between devices with their start and end apart: 16 -> 16, of which waited for: 8 -> 8; matrix products, arithmetic and copies ran while one was open for 0% -> 0% of each run, Pallas kernels for 9% -> 10%
where the time goes in v10:
time: 57.1 us; the launch traced here: 56.9 us
  blocking collectives  20.8 us (36%)
  starting transfers between devices  15.4 us (27%)
  waiting for transfers between devices  10.4 us (18%)
  Pallas kernels  9.26 us (16%)
  matrix products  0.89 us (2%)
    all_to_all x2, blocking collectives, to_all(): lax.all_to_all(copies, 'dp', 0, 0, axis_index_groups=groups, tiled=True)  20.8 us
    ppermute x14, starting transfers between devices, ring(): return lax.ppermute(x, 'dp', pairs)  14.8 us
    ppermute x14, waiting for transfers between devices, ring(): return lax.ppermute(x, 'dp', pairs)  9.02 us
    pallas_call x4, Pallas kernels, project(): pl.pallas_call(functools.partial(project_kernel, chips, offsets, parts, a...  3.29 us
    pallas_call x1, Pallas kernels, start(): pl.pallas_call(functools.partial(start_kernel, chips), out_shape=[pltpu.V...  2.74 us
    pallas_call x1, Pallas kernels, keep_columns(): pl.pallas_call(functools.partial(keep_kernel, chips), out_shape=pltpu.VME...  2.49 us
    ppermute x2, waiting for transfers between devices, swap(): return lax.ppermute(x, 'dp', [(i, i ^ bit) for i in range(n)])  1.34 us
  transfers between devices with their start and end apart: 16, of which 8 were waited for; matrix products, arithmetic and copies ran while one was open for 0% of the time, Pallas kernels for 10%

profile of v10, /device:TPU:0, one launch (start us, length us, event | category | flops | bytes accessed | tf_op | source)
XLA Modules:
  0.0 56.9 jit_solution(1340882311830870945)
XLA Ops:
  0.0 2.7 %shard_map.65 = (bf16[64,1152]{1,0:T(8,128)(2,1)S(1)}, bf16[64,1152]{1,0:T(8,128)(2,1)S(1)}, bf16[8,128,2304]{2,1,0:T(8,128)(2,1)S(1)}) custom-call(bf16[128,8192]{1,0:T(8,128)(2,1)} %act.3, bf16[128,28672]{1,0:T(8,128)(2,1)} %grad.3, bf16[64,512]{1,0:T(8,128)(2,1)} %bitcast.12, bf16[64,1792]{1,0:T(8,128)(2,1)} %bitcast.11), custom_call_target="tpu_custom_call" | custom-call | bytes 10027008 | tf_op jit(solution)/shard_map/pallas_call | solution.py:87
  2.8 0.5 collective-permute-start.6
  3.3 2.6 %collective-permute-start = (bf16[64,1152]{1,0:T(8,128)(2,1)S(1)}, bf16[64,1152]{1,0:T(8,128)(2,1)S(1)}, u32[]{:S(2)}, u32[]{:S(2)}) collective-permute-start(bf16[64,1152]{1,0:T(8,128)(2,1)S(1)} %get-tuple-element.11.refs_2_), channel_id=1, source_target_pairs={{0,4},{1,5},{4,8},{5,9},{8,12},{9,13},{12,14},{13,15},{14,10},{15,... | collective-permute-start | bytes 442376 | tf_op jit(solution)/shard_map/ppermute | solution.py:39
  5.9 2.0 %collective-permute-start.9 = (bf16[64,1152]{1,0:T(8,128)(2,1)S(1)}, bf16[64,1152]{1,0:T(8,128)(2,1)S(1)}, u32[]{:S(2)}, u32[]{:S(2)}) collective-permute-start(bf16[64,1152]{1,0:T(8,128)(2,1)S(1)} %get-tuple-element.12.refs_3_), channel_id=1, source_target_pairs={{0,4},{1,5},{4,8},{5,9},{8,12},{9,13},{12,14},{13,15},{14,10},{15,... | collective-permute-start | bytes 442376 | tf_op jit(solution)/shard_map/ppermute | solution.py:39
  8.0 2.6 %collective-permute-done.refs_4_ = bf16[64,1152]{1,0:T(8,128)(2,1)S(1)} collective-permute-done((bf16[64,1152]{1,0:T(8,128)(2,1)S(1)}, bf16[64,1152]{1,0:T(8,128)(2,1)S(1)}, u32[]{:S(2)}, u32[]{:S(2)}) %collective-permute-start) | collective-permute-done | bytes 147488 | tf_op jit(solution)/shard_map/ppermute | solution.py:39
  10.6 2.0 %collective-permute-start.1 = (bf16[64,1152]{1,0:T(8,128)(2,1)S(1)}, bf16[64,1152]{1,0:T(8,128)(2,1)S(1)}, u32[]{:S(2)}, u32[]{:S(2)}) collective-permute-start(bf16[64,1152]{1,0:T(8,128)(2,1)S(1)} %collective-permute-done.refs_4_), channel_id=1, source_target_pairs={{0,4},{1,5},{4,8},{5,9},{8,12},{9,13},{12,14},{13,15},{14,10},{15,... | collective-permute-start | bytes 442376 | tf_op jit(solution)/shard_map/ppermute | solution.py:39
  12.6 1.1 %collective-permute-done.9.refs_5_ = bf16[64,1152]{1,0:T(8,128)(2,1)S(1)} collective-permute-done((bf16[64,1152]{1,0:T(8,128)(2,1)S(1)}, bf16[64,1152]{1,0:T(8,128)(2,1)S(1)}, u32[]{:S(2)}, u32[]{:S(2)}) %collective-permute-start.9) | collective-permute-done | bytes 147488 | tf_op jit(solution)/shard_map/ppermute | solution.py:39
  13.7 2.0 %collective-permute-start.10 = (bf16[64,1152]{1,0:T(8,128)(2,1)S(1)}, bf16[64,1152]{1,0:T(8,128)(2,1)S(1)}, u32[]{:S(2)}, u32[]{:S(2)}) collective-permute-start(bf16[64,1152]{1,0:T(8,128)(2,1)S(1)} %collective-permute-done.9.refs_5_), channel_id=1, source_target_pairs={{0,4},{1,5},{4,8},{5,9},{8,12},{9,13},{12,14},{13,15},{14,10},{15,... | collective-permute-start | bytes 442376 | tf_op jit(solution)/shard_map/ppermute | solution.py:39
  15.8 1.5 %collective-permute-done.1.refs_8_ = bf16[64,1152]{1,0:T(8,128)(2,1)S(1)} collective-permute-done((bf16[64,1152]{1,0:T(8,128)(2,1)S(1)}, bf16[64,1152]{1,0:T(8,128)(2,1)S(1)}, u32[]{:S(2)}, u32[]{:S(2)}) %collective-permute-start.1) | collective-permute-done | bytes 147488 | tf_op jit(solution)/shard_map/ppermute | solution.py:39
  17.3 2.0 %collective-permute-start.2 = (bf16[64,1152]{1,0:T(8,128)(2,1)S(1)}, bf16[64,1152]{1,0:T(8,128)(2,1)S(1)}, u32[]{:S(2)}, u32[]{:S(2)}) collective-permute-start(bf16[64,1152]{1,0:T(8,128)(2,1)S(1)} %collective-permute-done.1.refs_8_), channel_id=1, source_target_pairs={{0,4},{1,5},{4,8},{5,9},{8,12},{9,13},{12,14},{13,15},{14,10},{15,... | collective-permute-start | bytes 442376 | tf_op jit(solution)/shard_map/ppermute | solution.py:39
  19.3 1.2 %collective-permute-done.10.refs_9_ = bf16[64,1152]{1,0:T(8,128)(2,1)S(1)} collective-permute-done((bf16[64,1152]{1,0:T(8,128)(2,1)S(1)}, bf16[64,1152]{1,0:T(8,128)(2,1)S(1)}, u32[]{:S(2)}, u32[]{:S(2)}) %collective-permute-start.10) | collective-permute-done | bytes 147488 | tf_op jit(solution)/shard_map/ppermute | solution.py:39
  20.5 2.0 %collective-permute-start.11 = (bf16[64,1152]{1,0:T(8,128)(2,1)S(1)}, bf16[64,1152]{1,0:T(8,128)(2,1)S(1)}, u32[]{:S(2)}, u32[]{:S(2)}) collective-permute-start(bf16[64,1152]{1,0:T(8,128)(2,1)S(1)} %collective-permute-done.10.refs_9_), channel_id=1, source_target_pairs={{0,4},{1,5},{4,8},{5,9},{8,12},{9,13},{12,14},{13,15},{14,10},{15,... | collective-permute-start | bytes 442376 | tf_op jit(solution)/shard_map/ppermute | solution.py:39
  22.5 2.5 %shard_map.64.refs_0_ = bf16[8,128,2304]{2,1,0:T(8,128)(2,1)S(1)} custom-call(bf16[128,8192]{1,0:T(8,128)(2,1)} %act.3, bf16[128,28672]{1,0:T(8,128)(2,1)} %grad.3), custom_call_target="tpu_custom_call" | custom-call | bytes 9437184 | tf_op jit(solution)/shard_map/pallas_call | solution.py:107
  25.1 0.8 %collective-permute-done.5.refs_5_ = bf16[64,1152]{1,0:T(8,128)(2,1)S(1)} collective-permute-done((bf16[64,1152]{1,0:T(8,128)(2,1)S(1)}, bf16[64,1152]{1,0:T(8,128)(2,1)S(1)}, u32[]{:S(2)}, u32[]{:S(2)}) %collective-permute-start.5) | collective-permute-done | bytes 147488 | tf_op jit(solution)/shard_map/ppermute | solution.py:39
  25.8 1.6 %collective-permute-start.8 = (bf16[64,1152]{1,0:T(8,128)(2,1)S(1)}, bf16[64,1152]{1,0:T(8,128)(2,1)S(1)}, u32[]{:S(2)}, u32[]{:S(2)}) collective-permute-start(bf16[64,1152]{1,0:T(8,128)(2,1)S(1)} %collective-permute-done.2.refs_2_), channel_id=1, source_target_pairs={{0,4},{1,5},{4,8},{5,9},{8,12},{9,13},{12,14},{13,15},{14,10},{15,... | collective-permute-start | bytes 442376 | tf_op jit(solution)/shard_map/ppermute | solution.py:39
  27.9 1.7 %shard_map.66.refs_6_ = f32[256,128]{1,0:T(8,128)S(1)} custom-call(bf16[8,128,2304]{2,1,0:T(8,128)(2,1)S(1)} %shard_map.64.refs_0_, bf16[8,128,2304]{2,1,0:T(8,128)(2,1)S(1)} %collective-permute-done.6.refs_1_, bf16[64,1152]{1,0:T(8,128)(2,1)S(1)} %get-tuple-element.11.refs_2_, bf16[64,1152]{1,0:T(8,128)(2,1)S(1)} %get-tuple-element.12.refs_3_, ...), custom_call_target="tpu_custom_call" | custom-call | flops 377487360 | bytes 7372800 | tf_op jit(solution)/shard_map/pallas_call | solution.py:151
  29.6 0.8 %shard_map.67.refs_3_ = f32[256,128]{1,0:T(8,128)S(1)} custom-call(bf16[8,128,2304]{2,1,0:T(8,128)(2,1)S(1)} %shard_map.64.refs_0_, bf16[8,128,2304]{2,1,0:T(8,128)(2,1)S(1)} %collective-permute-done.6.refs_1_, bf16[64,1152]{1,0:T(8,128)(2,1)S(1)} %collective-permute-done.2.refs_2_, bf16[64,1152]{1,0:T(8,128)(2,1)S(1)} %collective-permute-done.11.refs_3_, ...), custom_call_target="tpu_custom_call" | custom-call | flops 150994944 | bytes 2949120 | tf_op jit(solution)/shard_map/pallas_call | solution.py:151
  30.5 0.5 collective-permute-done.8.refs_2_
  31.4 1.2 %collective-permute-done.7.refs_2_ = bf16[64,1152]{1,0:T(8,128)(2,1)S(1)} collective-permute-done((bf16[64,1152]{1,0:T(8,128)(2,1)S(1)}, bf16[64,1152]{1,0:T(8,128)(2,1)S(1)}, u32[]{:S(2)}, u32[]{:S(2)}) %collective-permute-start.7) | collective-permute-done | bytes 147488 | tf_op jit(solution)/shard_map/ppermute | solution.py:39
  33.0 1.3 %collective-permute-done.15 = f32[256,128]{1,0:T(8,128)S(1)} collective-permute-done((f32[256,128]{1,0:T(8,128)S(1)}, f32[256,128]{1,0:T(8,128)S(1)}, u32[]{:S(2)}, u32[]{:S(2)}) %collective-permute-start.15) | collective-permute-done | bytes 131104 | tf_op jit(solution)/shard_map/ppermute | solution.py:43
  34.7 11.7 %all_to_all.10 = f32[8,32,128]{2,1,0:T(8,128)S(1)} all-to-all(f32[8,32,128]{2,1,0:T(8,128)S(1)} %broadcast_in_dim.14), channel_id=1, replica_groups={{0,2,4,6,8,10,12,14},{1,3,5,7,9,11,13,15},{16,18,20,22,24,26,28,30},{17..., dimensions={0} | all-to-all | bytes 262144 | tf_op jit(solution)/shard_map/all_to_all | solution.py:185
  46.5 0.6 %convolution_convert_fusion = bf16[2,256]{1,0:T(2,128)(2,1)S(1)} fusion(bf16[256,4096]{1,0:T(8,128)(2,1)S(1)} %copy-done, bf16[1,2,32,128]{3,2,1,0:T(8,128)(2,1)S(1)} %bitcast.13), kind=kOutput, calls=%fused_computation.1 | convolution fusion | flops 4194816 | bytes 2114560 | tf_op jit(solution)/shard_map/dot_general | solution.py:23
  47.1 9.1 %all_to_all.11.conditioned = bf16[16,2,256]{2,1,0:T(2,128)(2,1)S(1)} all-to-all(bf16[16,2,256]{2,1,0:T(2,128)(2,1)S(1)} %broadcast_in_dim.15), channel_id=1, replica_groups={{0,1,2,3,4,5,6,7,8,9,10,11,12,13,14,15},{16,17,18,19,20,21,22,23,24,25,..., dimensions={0} | all-to-all | bytes 32768 | tf_op jit(solution)/shard_map/all_to_all | solution.py:185
  56.2 0.7 %shard_map.70 = f32[2,8]{1,0:T(2,128)} custom-call(bf16[16,2,256]{2,1,0:T(2,128)(2,1)S(1)} %all_to_all.11.conditioned, bf16[8,4096]{1,0:T(8,128)(2,1)S(1)} %copy-done.1), custom_call_target="tpu_custom_call" | custom-call | tf_op jit(solution)/shard_map/pallas_call | solution.py:174
  (29 shorter events, 1.9 us)
Async XLA Ops:
  0.0 46.4 %copy-start = (bf16[256,4096]{1,0:T(8,128)(2,1)S(1)}, bf16[256,4096]{1,0:T(8,128)(2,1)}, u32[]{:S(2)}) copy-start(bf16[256,4096]{1,0:T(8,128)(2,1)} %param.10) | copy-start | bytes 6291460
  2.8 25.1 %collective-permute-start.6 = (bf16[8,128,2304]{2,1,0:T(8,128)(2,1)S(1)}, bf16[8,128,2304]{2,1,0:T(8,128)(2,1)S(1)}, u32[]{:S(2)}, u32[]{:S(2)}) collective-permute-start(bf16[8,128,2304]{2,1,0:T(8,128)(2,1)S(1)} %get-tuple-element.14), channel_id=1, source_target_pairs={{0,1},{1,0},{2,3},{3,2},{4,5},{5,4},{6,7},{7,6},{8,9},{9,8},{10,11... | collective-permute-start | bytes 14155784 | tf_op jit(solution)/shard_map/ppermute | solution.py:43
  3.3 7.3 %collective-permute-start = (bf16[64,1152]{1,0:T(8,128)(2,1)S(1)}, bf16[64,1152]{1,0:T(8,128)(2,1)S(1)}, u32[]{:S(2)}, u32[]{:S(2)}) collective-permute-start(bf16[64,1152]{1,0:T(8,128)(2,1)S(1)} %get-tuple-element.11.refs_2_), channel_id=1, source_target_pairs={{0,4},{1,5},{4,8},{5,9},{8,12},{9,13},{12,14},{13,15},{14,10},{15,... | collective-permute-start | bytes 442376 | tf_op jit(solution)/shard_map/ppermute | solution.py:39
  5.9 6.7 %collective-permute-start.3 = (bf16[64,1152]{1,0:T(8,128)(2,1)S(1)}, bf16[64,1152]{1,0:T(8,128)(2,1)S(1)}, u32[]{:S(2)}, u32[]{:S(2)}) collective-permute-start(bf16[64,1152]{1,0:T(8,128)(2,1)S(1)} %get-tuple-element.12.refs_3_), channel_id=1, source_target_pairs={{0,2},{1,3},{4,0},{5,1},{8,4},{9,5},{12,8},{13,9},{14,12},{15,13},... | collective-permute-start | bytes 442376 | tf_op jit(solution)/shard_map/ppermute | solution.py:39
  5.9 7.8 %collective-permute-start.9 = (bf16[64,1152]{1,0:T(8,128)(2,1)S(1)}, bf16[64,1152]{1,0:T(8,128)(2,1)S(1)}, u32[]{:S(2)}, u32[]{:S(2)}) collective-permute-start(bf16[64,1152]{1,0:T(8,128)(2,1)S(1)} %get-tuple-element.12.refs_3_), channel_id=1, source_target_pairs={{0,4},{1,5},{4,8},{5,9},{8,12},{9,13},{12,14},{13,15},{14,10},{15,... | collective-permute-start | bytes 442376 | tf_op jit(solution)/shard_map/ppermute | solution.py:39
  7.9 7.8 %collective-permute-start.12 = (bf16[64,1152]{1,0:T(8,128)(2,1)S(1)}, bf16[64,1152]{1,0:T(8,128)(2,1)S(1)}, u32[]{:S(2)}, u32[]{:S(2)}) collective-permute-start(bf16[64,1152]{1,0:T(8,128)(2,1)S(1)} %get-tuple-element.11.refs_2_), channel_id=1, source_target_pairs={{0,2},{1,3},{4,0},{5,1},{8,4},{9,5},{12,8},{13,9},{14,12},{15,13},... | collective-permute-start | bytes 442376 | tf_op jit(solution)/shard_map/ppermute | solution.py:39
  10.6 6.7 %collective-permute-start.1 = (bf16[64,1152]{1,0:T(8,128)(2,1)S(1)}, bf16[64,1152]{1,0:T(8,128)(2,1)S(1)}, u32[]{:S(2)}, u32[]{:S(2)}) collective-permute-start(bf16[64,1152]{1,0:T(8,128)(2,1)S(1)} %collective-permute-done.refs_4_), channel_id=1, source_target_pairs={{0,4},{1,5},{4,8},{5,9},{8,12},{9,13},{12,14},{13,15},{14,10},{15,... | collective-permute-start | bytes 442376 | tf_op jit(solution)/shard_map/ppermute | solution.py:39
  12.6 6.7 %collective-permute-start.4 = (bf16[64,1152]{1,0:T(8,128)(2,1)S(1)}, bf16[64,1152]{1,0:T(8,128)(2,1)S(1)}, u32[]{:S(2)}, u32[]{:S(2)}) collective-permute-start(bf16[64,1152]{1,0:T(8,128)(2,1)S(1)} %collective-permute-done.3.refs_7_), channel_id=1, source_target_pairs={{0,2},{1,3},{4,0},{5,1},{8,4},{9,5},{12,8},{13,9},{14,12},{15,13},... | collective-permute-start | bytes 442376 | tf_op jit(solution)/shard_map/ppermute | solution.py:39
  13.7 6.8 %collective-permute-start.10 = (bf16[64,1152]{1,0:T(8,128)(2,1)S(1)}, bf16[64,1152]{1,0:T(8,128)(2,1)S(1)}, u32[]{:S(2)}, u32[]{:S(2)}) collective-permute-start(bf16[64,1152]{1,0:T(8,128)(2,1)S(1)} %collective-permute-done.9.refs_5_), channel_id=1, source_target_pairs={{0,4},{1,5},{4,8},{5,9},{8,12},{9,13},{12,14},{13,15},{14,10},{15,... | collective-permute-start | bytes 442376 | tf_op jit(solution)/shard_map/ppermute | solution.py:39
  15.8 6.8 %collective-permute-start.13 = (bf16[64,1152]{1,0:T(8,128)(2,1)S(1)}, bf16[64,1152]{1,0:T(8,128)(2,1)S(1)}, u32[]{:S(2)}, u32[]{:S(2)}) collective-permute-start(bf16[64,1152]{1,0:T(8,128)(2,1)S(1)} %collective-permute-done.12.refs_6_), channel_id=1, source_target_pairs={{0,2},{1,3},{4,0},{5,1},{8,4},{9,5},{12,8},{13,9},{14,12},{15,13},... | collective-permute-start | bytes 442376 | tf_op jit(solution)/shard_map/ppermute | solution.py:39
  17.3 7.8 %collective-permute-start.2 = (bf16[64,1152]{1,0:T(8,128)(2,1)S(1)}, bf16[64,1152]{1,0:T(8,128)(2,1)S(1)}, u32[]{:S(2)}, u32[]{:S(2)}) collective-permute-start(bf16[64,1152]{1,0:T(8,128)(2,1)S(1)} %collective-permute-done.1.refs_8_), channel_id=1, source_target_pairs={{0,4},{1,5},{4,8},{5,9},{8,12},{9,13},{12,14},{13,15},{14,10},{15,... | collective-permute-start | bytes 442376 | tf_op jit(solution)/shard_map/ppermute | solution.py:39
  19.3 6.6 %collective-permute-start.5 = (bf16[64,1152]{1,0:T(8,128)(2,1)S(1)}, bf16[64,1152]{1,0:T(8,128)(2,1)S(1)}, u32[]{:S(2)}, u32[]{:S(2)}) collective-permute-start(bf16[64,1152]{1,0:T(8,128)(2,1)S(1)} %collective-permute-done.4.refs_11_), channel_id=1, source_target_pairs={{0,2},{1,3},{4,0},{5,1},{8,4},{9,5},{12,8},{13,9},{14,12},{15,13},... | collective-permute-start | bytes 442376 | tf_op jit(solution)/shard_map/ppermute | solution.py:39
  20.5 9.1 %collective-permute-start.11 = (bf16[64,1152]{1,0:T(8,128)(2,1)S(1)}, bf16[64,1152]{1,0:T(8,128)(2,1)S(1)}, u32[]{:S(2)}, u32[]{:S(2)}) collective-permute-start(bf16[64,1152]{1,0:T(8,128)(2,1)S(1)} %collective-permute-done.10.refs_9_), channel_id=1, source_target_pairs={{0,4},{1,5},{4,8},{5,9},{8,12},{9,13},{12,14},{13,15},{14,10},{15,... | collective-permute-start | bytes 442376 | tf_op jit(solution)/shard_map/ppermute | solution.py:39
  22.5 7.1 %collective-permute-start.14 = (bf16[64,1152]{1,0:T(8,128)(2,1)S(1)}, bf16[64,1152]{1,0:T(8,128)(2,1)S(1)}, u32[]{:S(2)}, u32[]{:S(2)}) collective-permute-start(bf16[64,1152]{1,0:T(8,128)(2,1)S(1)} %collective-permute-done.13.refs_10_), channel_id=1, source_target_pairs={{0,2},{1,3},{4,0},{5,1},{8,4},{9,5},{12,8},{13,9},{14,12},{15,13},... | collective-permute-start | bytes 442376 | tf_op jit(solution)/shard_map/ppermute | solution.py:39
  25.8 5.1 %collective-permute-start.8 = (bf16[64,1152]{1,0:T(8,128)(2,1)S(1)}, bf16[64,1152]{1,0:T(8,128)(2,1)S(1)}, u32[]{:S(2)}, u32[]{:S(2)}) collective-permute-start(bf16[64,1152]{1,0:T(8,128)(2,1)S(1)} %collective-permute-done.2.refs_2_), channel_id=1, source_target_pairs={{0,4},{1,5},{4,8},{5,9},{8,12},{9,13},{12,14},{13,15},{14,10},{15,... | collective-permute-start | bytes 442376 | tf_op jit(solution)/shard_map/ppermute | solution.py:39
  27.4 5.1 %collective-permute-start.7 = (bf16[64,1152]{1,0:T(8,128)(2,1)S(1)}, bf16[64,1152]{1,0:T(8,128)(2,1)S(1)}, u32[]{:S(2)}, u32[]{:S(2)}) collective-permute-start(bf16[64,1152]{1,0:T(8,128)(2,1)S(1)} %collective-permute-done.5.refs_5_), channel_id=1, source_target_pairs={{0,2},{1,3},{4,0},{5,1},{8,4},{9,5},{12,8},{13,9},{14,12},{15,13},... | collective-permute-start | bytes 442376 | tf_op jit(solution)/shard_map/ppermute | solution.py:39
  32.9 23.3 %copy-start.1 = (bf16[8,4096]{1,0:T(8,128)(2,1)S(1)}, bf16[8,4096]{1,0:T(8,128)(2,1)}, u32[]{:S(2)}) copy-start(bf16[8,4096]{1,0:T(8,128)(2,1)} %queries.1) | copy-start | bytes 196612
  32.9 1.4 %collective-permute-start.15 = (f32[256,128]{1,0:T(8,128)S(1)}, f32[256,128]{1,0:T(8,128)S(1)}, u32[]{:S(2)}, u32[]{:S(2)}) collective-permute-start(f32[256,128]{1,0:T(8,128)S(1)} %shard_map.69), channel_id=1, source_target_pairs={{0,1},{1,0},{2,3},{3,2},{4,5},{5,4},{6,7},{7,6},{8,9},{9,8},{10,11... | collective-permute-start | bytes 393224 | tf_op jit(solution)/shard_map/ppermute | solution.py:43

commit v11 on v10

--- a/solution.py
+++ b/solution.py
@@ -34,7 +34,7 @@
     half = chips // 2
     chip = [2 * p if p < half else 2 * (chips - 1 - p) + 1 for p in range(chips)]
     pairs = [
-        (chip[p] * 2 + c, chip[(p + step) % chips] * 2 + c) for p in range(chips) for c in range(2)
+        (chip[p] * 2 + c, chip[(p + step) % chips] * 2 + 1 - c) for p in range(chips) for c in range(2)
     ]
     return lax.ppermute(x, "dp", pairs)
 
@@ -43,12 +43,17 @@
     return lax.ppermute(x, "dp", [(i, i ^ bit) for i in range(n)])
 
 
+def odd(chip):
+    return (chip ^ (chip >> 1)) & 1
+
+
 def column_copies(chips, core, act, grad, out, sems):
+    ring_of = core ^ odd(lax.axis_index("dp") >> 1)
     a_width = act.shape[1] // (2 * chips)
     g_width = grad.shape[1] // (2 * chips)
     copies = []
     for chip in range(chips):
-        block = 2 * chip + core
+        block = 2 * chip + (ring_of ^ odd(chip))
         for k, (ref, at, width) in enumerate(((act, 0, a_width), (grad, a_width, g_width))):
             columns = pl.ds(pl.multiple_of(block * width, 128), width)
             copies.append(

time: 57.1 us -> 57.3 us (level)
  waiting for transfers between devices: 10.4 us -> 9.41 us
  blocking collectives: 20.8 us -> 21.5 us
    ppermute x14, waiting for transfers between devices: 9.02 us -> 8.2 us  [ring(): return lax.ppermute(x, 'dp', pairs)]
    all_to_all x2, blocking collectives: 20.8 us -> 21.5 us  [to_all(): lax.all_to_all(copies, 'dp', 0, 0, axis_index_groups=groups, tiled=True)]
where the time goes in v11:
time: 57.3 us; the launch traced here: 57.1 us
  blocking collectives  21.5 us (38%)
  starting transfers between devices  15.7 us (27%)
  waiting for transfers between devices  9.41 us (16%)
  Pallas kernels  9.27 us (16%)
  matrix products  0.89 us (2%)
    all_to_all x2, blocking collectives, to_all(): lax.all_to_all(copies, 'dp', 0, 0, axis_index_groups=groups, tiled=True)  21.5 us
    ppermute x14, starting transfers between devices, ring(): return lax.ppermute(x, 'dp', pairs)  15 us
    ppermute x14, waiting for transfers between devices, ring(): return lax.ppermute(x, 'dp', pairs)  8.2 us
    pallas_call x4, Pallas kernels, project(): pl.pallas_call(functools.partial(project_kernel, chips, offsets, parts, a...  3.3 us
    pallas_call x1, Pallas kernels, start(): pl.pallas_call(functools.partial(start_kernel, chips), out_shape=[pltpu.V...  2.74 us
    pallas_call x1, Pallas kernels, keep_columns(): pl.pallas_call(functools.partial(keep_kernel, chips), out_shape=pltpu.VME...  2.49 us
    ppermute x2, waiting for transfers between devices, swap(): return lax.ppermute(x, 'dp', [(i, i ^ bit) for i in range(n)])  1.21 us
  transfers between devices with their start and end apart: 16, of which 8 were waited for; matrix products, arithmetic and copies ran while one was open for 0% of the time, Pallas kernels for 10%

profile of v11, /device:TPU:0, one launch (start us, length us, event | category | flops | bytes accessed | tf_op | source)
XLA Modules:
  0.0 57.1 jit_solution(12769034333129548222)
XLA Ops:
  0.0 2.7 %shard_map.65 = (bf16[64,1152]{1,0:T(8,128)(2,1)S(1)}, bf16[64,1152]{1,0:T(8,128)(2,1)S(1)}, bf16[8,128,2304]{2,1,0:T(8,128)(2,1)S(1)}) custom-call(bf16[128,8192]{1,0:T(8,128)(2,1)} %act.3, bf16[128,28672]{1,0:T(8,128)(2,1)} %grad.3, bf16[64,512]{1,0:T(8,128)(2,1)} %bitcast.12, bf16[64,1792]{1,0:T(8,128)(2,1)} %bitcast.11), custom_call_target="tpu_custom_call" | custom-call | bytes 10027008 | tf_op jit(solution)/shard_map/pallas_call | solution.py:92
  2.8 0.5 collective-permute-start.6
  3.3 2.7 %collective-permute-start = (bf16[64,1152]{1,0:T(8,128)(2,1)S(1)}, bf16[64,1152]{1,0:T(8,128)(2,1)S(1)}, u32[]{:S(2)}, u32[]{:S(2)}) collective-permute-start(bf16[64,1152]{1,0:T(8,128)(2,1)S(1)} %get-tuple-element.11.refs_2_), channel_id=1, source_target_pairs={{0,5},{1,4},{4,9},{5,8},{8,13},{9,12},{12,15},{13,14},{14,11},{15,... | collective-permute-start | bytes 442376 | tf_op jit(solution)/shard_map/ppermute | solution.py:39
  6.0 1.7 %collective-permute-start.9 = (bf16[64,1152]{1,0:T(8,128)(2,1)S(1)}, bf16[64,1152]{1,0:T(8,128)(2,1)S(1)}, u32[]{:S(2)}, u32[]{:S(2)}) collective-permute-start(bf16[64,1152]{1,0:T(8,128)(2,1)S(1)} %get-tuple-element.12.refs_3_), channel_id=1, source_target_pairs={{0,5},{1,4},{4,9},{5,8},{8,13},{9,12},{12,15},{13,14},{14,11},{15,... | collective-permute-start | bytes 442376 | tf_op jit(solution)/shard_map/ppermute | solution.py:39
  7.7 2.4 %collective-permute-done.refs_4_ = bf16[64,1152]{1,0:T(8,128)(2,1)S(1)} collective-permute-done((bf16[64,1152]{1,0:T(8,128)(2,1)S(1)}, bf16[64,1152]{1,0:T(8,128)(2,1)S(1)}, u32[]{:S(2)}, u32[]{:S(2)}) %collective-permute-start) | collective-permute-done | bytes 147488 | tf_op jit(solution)/shard_map/ppermute | solution.py:39
  10.1 2.2 %collective-permute-start.1 = (bf16[64,1152]{1,0:T(8,128)(2,1)S(1)}, bf16[64,1152]{1,0:T(8,128)(2,1)S(1)}, u32[]{:S(2)}, u32[]{:S(2)}) collective-permute-start(bf16[64,1152]{1,0:T(8,128)(2,1)S(1)} %collective-permute-done.refs_4_), channel_id=1, source_target_pairs={{0,5},{1,4},{4,9},{5,8},{8,13},{9,12},{12,15},{13,14},{14,11},{15,... | collective-permute-start | bytes 442376 | tf_op jit(solution)/shard_map/ppermute | solution.py:39
  12.4 0.9 %collective-permute-done.9.refs_5_ = bf16[64,1152]{1,0:T(8,128)(2,1)S(1)} collective-permute-done((bf16[64,1152]{1,0:T(8,128)(2,1)S(1)}, bf16[64,1152]{1,0:T(8,128)(2,1)S(1)}, u32[]{:S(2)}, u32[]{:S(2)}) %collective-permute-start.9) | collective-permute-done | bytes 147488 | tf_op jit(solution)/shard_map/ppermute | solution.py:39
  13.2 2.2 %collective-permute-start.10 = (bf16[64,1152]{1,0:T(8,128)(2,1)S(1)}, bf16[64,1152]{1,0:T(8,128)(2,1)S(1)}, u32[]{:S(2)}, u32[]{:S(2)}) collective-permute-start(bf16[64,1152]{1,0:T(8,128)(2,1)S(1)} %collective-permute-done.9.refs_5_), channel_id=1, source_target_pairs={{0,5},{1,4},{4,9},{5,8},{8,13},{9,12},{12,15},{13,14},{14,11},{15,... | collective-permute-start | bytes 442376 | tf_op jit(solution)/shard_map/ppermute | solution.py:39
  15.4 1.1 %collective-permute-done.1.refs_8_ = bf16[64,1152]{1,0:T(8,128)(2,1)S(1)} collective-permute-done((bf16[64,1152]{1,0:T(8,128)(2,1)S(1)}, bf16[64,1152]{1,0:T(8,128)(2,1)S(1)}, u32[]{:S(2)}, u32[]{:S(2)}) %collective-permute-start.1) | collective-permute-done | bytes 147488 | tf_op jit(solution)/shard_map/ppermute | solution.py:39
  16.5 2.2 %collective-permute-start.2 = (bf16[64,1152]{1,0:T(8,128)(2,1)S(1)}, bf16[64,1152]{1,0:T(8,128)(2,1)S(1)}, u32[]{:S(2)}, u32[]{:S(2)}) collective-permute-start(bf16[64,1152]{1,0:T(8,128)(2,1)S(1)} %collective-permute-done.1.refs_8_), channel_id=1, source_target_pairs={{0,5},{1,4},{4,9},{5,8},{8,13},{9,12},{12,15},{13,14},{14,11},{15,... | collective-permute-start | bytes 442376 | tf_op jit(solution)/shard_map/ppermute | solution.py:39
  18.7 0.9 %collective-permute-done.10.refs_9_ = bf16[64,1152]{1,0:T(8,128)(2,1)S(1)} collective-permute-done((bf16[64,1152]{1,0:T(8,128)(2,1)S(1)}, bf16[64,1152]{1,0:T(8,128)(2,1)S(1)}, u32[]{:S(2)}, u32[]{:S(2)}) %collective-permute-start.10) | collective-permute-done | bytes 147488 | tf_op jit(solution)/shard_map/ppermute | solution.py:39
  19.5 2.2 %collective-permute-start.11 = (bf16[64,1152]{1,0:T(8,128)(2,1)S(1)}, bf16[64,1152]{1,0:T(8,128)(2,1)S(1)}, u32[]{:S(2)}, u32[]{:S(2)}) collective-permute-start(bf16[64,1152]{1,0:T(8,128)(2,1)S(1)} %collective-permute-done.10.refs_9_), channel_id=1, source_target_pairs={{0,5},{1,4},{4,9},{5,8},{8,13},{9,12},{12,15},{13,14},{14,11},{15,... | collective-permute-start | bytes 442376 | tf_op jit(solution)/shard_map/ppermute | solution.py:39
  21.8 2.5 %shard_map.64.refs_0_ = bf16[8,128,2304]{2,1,0:T(8,128)(2,1)S(1)} custom-call(bf16[128,8192]{1,0:T(8,128)(2,1)} %act.3, bf16[128,28672]{1,0:T(8,128)(2,1)} %grad.3), custom_call_target="tpu_custom_call" | custom-call | bytes 9437184 | tf_op jit(solution)/shard_map/pallas_call | solution.py:112
  24.6 1.5 %collective-permute-start.8 = (bf16[64,1152]{1,0:T(8,128)(2,1)S(1)}, bf16[64,1152]{1,0:T(8,128)(2,1)S(1)}, u32[]{:S(2)}, u32[]{:S(2)}) collective-permute-start(bf16[64,1152]{1,0:T(8,128)(2,1)S(1)} %collective-permute-done.2.refs_2_), channel_id=1, source_target_pairs={{0,5},{1,4},{4,9},{5,8},{8,13},{9,12},{12,15},{13,14},{14,11},{15,... | collective-permute-start | bytes 442376 | tf_op jit(solution)/shard_map/ppermute | solution.py:39
  26.4 1.7 %shard_map.66.refs_6_ = f32[256,128]{1,0:T(8,128)S(1)} custom-call(bf16[8,128,2304]{2,1,0:T(8,128)(2,1)S(1)} %shard_map.64.refs_0_, bf16[8,128,2304]{2,1,0:T(8,128)(2,1)S(1)} %collective-permute-done.6.refs_1_, bf16[64,1152]{1,0:T(8,128)(2,1)S(1)} %get-tuple-element.11.refs_2_, bf16[64,1152]{1,0:T(8,128)(2,1)S(1)} %get-tuple-element.12.refs_3_, ...), custom_call_target="tpu_custom_call" | custom-call | flops 377487360 | bytes 7372800 | tf_op jit(solution)/shard_map/pallas_call | solution.py:156
  28.1 0.8 %shard_map.67.refs_3_ = f32[256,128]{1,0:T(8,128)S(1)} custom-call(bf16[8,128,2304]{2,1,0:T(8,128)(2,1)S(1)} %shard_map.64.refs_0_, bf16[8,128,2304]{2,1,0:T(8,128)(2,1)S(1)} %collective-permute-done.6.refs_1_, bf16[64,1152]{1,0:T(8,128)(2,1)S(1)} %collective-permute-done.2.refs_2_, bf16[64,1152]{1,0:T(8,128)(2,1)S(1)} %collective-permute-done.11.refs_3_, ...), custom_call_target="tpu_custom_call" | custom-call | flops 150994944 | bytes 2949120 | tf_op jit(solution)/shard_map/pallas_call | solution.py:156
  29.0 1.4 %collective-permute-done.8.refs_2_ = bf16[64,1152]{1,0:T(8,128)(2,1)S(1)} collective-permute-done((bf16[64,1152]{1,0:T(8,128)(2,1)S(1)}, bf16[64,1152]{1,0:T(8,128)(2,1)S(1)}, u32[]{:S(2)}, u32[]{:S(2)}) %collective-permute-start.8) | collective-permute-done | bytes 147488 | tf_op jit(solution)/shard_map/ppermute | solution.py:39
  30.7 1.2 %collective-permute-done.7.refs_2_ = bf16[64,1152]{1,0:T(8,128)(2,1)S(1)} collective-permute-done((bf16[64,1152]{1,0:T(8,128)(2,1)S(1)}, bf16[64,1152]{1,0:T(8,128)(2,1)S(1)}, u32[]{:S(2)}, u32[]{:S(2)}) %collective-permute-start.7) | collective-permute-done | bytes 147488 | tf_op jit(solution)/shard_map/ppermute | solution.py:39
  31.9 0.4 shard_map.69
  32.5 1.2 %collective-permute-done.15 = f32[256,128]{1,0:T(8,128)S(1)} collective-permute-done((f32[256,128]{1,0:T(8,128)S(1)}, f32[256,128]{1,0:T(8,128)S(1)}, u32[]{:S(2)}, u32[]{:S(2)}) %collective-permute-start.15) | collective-permute-done | bytes 131104 | tf_op jit(solution)/shard_map/ppermute | solution.py:43
  34.1 12.4 %all_to_all.10 = f32[8,32,128]{2,1,0:T(8,128)S(1)} all-to-all(f32[8,32,128]{2,1,0:T(8,128)S(1)} %broadcast_in_dim.14), channel_id=1, replica_groups={{0,2,4,6,8,10,12,14},{1,3,5,7,9,11,13,15},{16,18,20,22,24,26,28,30},{17..., dimensions={0} | all-to-all | bytes 262144 | tf_op jit(solution)/shard_map/all_to_all | solution.py:190
  46.6 0.6 %convolution_convert_fusion = bf16[2,256]{1,0:T(2,128)(2,1)S(1)} fusion(bf16[256,4096]{1,0:T(8,128)(2,1)S(1)} %copy-done, bf16[1,2,32,128]{3,2,1,0:T(8,128)(2,1)S(1)} %bitcast.13), kind=kOutput, calls=%fused_computation.1 | convolution fusion | flops 4194816 | bytes 2114560 | tf_op jit(solution)/shard_map/dot_general | solution.py:23
  47.3 9.1 %all_to_all.11.conditioned = bf16[16,2,256]{2,1,0:T(2,128)(2,1)S(1)} all-to-all(bf16[16,2,256]{2,1,0:T(2,128)(2,1)S(1)} %broadcast_in_dim.15), channel_id=1, replica_groups={{0,1,2,3,4,5,6,7,8,9,10,11,12,13,14,15},{16,17,18,19,20,21,22,23,24,25,..., dimensions={0} | all-to-all | bytes 32768 | tf_op jit(solution)/shard_map/all_to_all | solution.py:190
  56.3 0.7 %shard_map.70 = f32[2,8]{1,0:T(2,128)} custom-call(bf16[16,2,256]{2,1,0:T(2,128)(2,1)S(1)} %all_to_all.11.conditioned, bf16[8,4096]{1,0:T(8,128)(2,1)S(1)} %copy-done.1), custom_call_target="tpu_custom_call" | custom-call | tf_op jit(solution)/shard_map/pallas_call | solution.py:179
  (29 shorter events, 1.7 us)
Async XLA Ops:
  0.0 46.6 %copy-start = (bf16[256,4096]{1,0:T(8,128)(2,1)S(1)}, bf16[256,4096]{1,0:T(8,128)(2,1)}, u32[]{:S(2)}) copy-start(bf16[256,4096]{1,0:T(8,128)(2,1)} %param.10) | copy-start | bytes 6291460
  2.8 23.6 %collective-permute-start.6 = (bf16[8,128,2304]{2,1,0:T(8,128)(2,1)S(1)}, bf16[8,128,2304]{2,1,0:T(8,128)(2,1)S(1)}, u32[]{:S(2)}, u32[]{:S(2)}) collective-permute-start(bf16[8,128,2304]{2,1,0:T(8,128)(2,1)S(1)} %get-tuple-element.14), channel_id=1, source_target_pairs={{0,1},{1,0},{2,3},{3,2},{4,5},{5,4},{6,7},{7,6},{8,9},{9,8},{10,11... | collective-permute-start | bytes 14155784 | tf_op jit(solution)/shard_map/ppermute | solution.py:43
  3.3 6.9 %collective-permute-start = (bf16[64,1152]{1,0:T(8,128)(2,1)S(1)}, bf16[64,1152]{1,0:T(8,128)(2,1)S(1)}, u32[]{:S(2)}, u32[]{:S(2)}) collective-permute-start(bf16[64,1152]{1,0:T(8,128)(2,1)S(1)} %get-tuple-element.11.refs_2_), channel_id=1, source_target_pairs={{0,5},{1,4},{4,9},{5,8},{8,13},{9,12},{12,15},{13,14},{14,11},{15,... | collective-permute-start | bytes 442376 | tf_op jit(solution)/shard_map/ppermute | solution.py:39
  6.0 6.4 %collective-permute-start.3 = (bf16[64,1152]{1,0:T(8,128)(2,1)S(1)}, bf16[64,1152]{1,0:T(8,128)(2,1)S(1)}, u32[]{:S(2)}, u32[]{:S(2)}) collective-permute-start(bf16[64,1152]{1,0:T(8,128)(2,1)S(1)} %get-tuple-element.12.refs_3_), channel_id=1, source_target_pairs={{0,3},{1,2},{4,1},{5,0},{8,5},{9,4},{12,9},{13,8},{14,13},{15,12},... | collective-permute-start | bytes 442376 | tf_op jit(solution)/shard_map/ppermute | solution.py:39
  6.0 7.3 %collective-permute-start.9 = (bf16[64,1152]{1,0:T(8,128)(2,1)S(1)}, bf16[64,1152]{1,0:T(8,128)(2,1)S(1)}, u32[]{:S(2)}, u32[]{:S(2)}) collective-permute-start(bf16[64,1152]{1,0:T(8,128)(2,1)S(1)} %get-tuple-element.12.refs_3_), channel_id=1, source_target_pairs={{0,5},{1,4},{4,9},{5,8},{8,13},{9,12},{12,15},{13,14},{14,11},{15,... | collective-permute-start | bytes 442376 | tf_op jit(solution)/shard_map/ppermute | solution.py:39
  7.7 7.7 %collective-permute-start.12 = (bf16[64,1152]{1,0:T(8,128)(2,1)S(1)}, bf16[64,1152]{1,0:T(8,128)(2,1)S(1)}, u32[]{:S(2)}, u32[]{:S(2)}) collective-permute-start(bf16[64,1152]{1,0:T(8,128)(2,1)S(1)} %get-tuple-element.11.refs_2_), channel_id=1, source_target_pairs={{0,3},{1,2},{4,1},{5,0},{8,5},{9,4},{12,9},{13,8},{14,13},{15,12},... | collective-permute-start | bytes 442376 | tf_op jit(solution)/shard_map/ppermute | solution.py:39
  10.1 6.3 %collective-permute-start.1 = (bf16[64,1152]{1,0:T(8,128)(2,1)S(1)}, bf16[64,1152]{1,0:T(8,128)(2,1)S(1)}, u32[]{:S(2)}, u32[]{:S(2)}) collective-permute-start(bf16[64,1152]{1,0:T(8,128)(2,1)S(1)} %collective-permute-done.refs_4_), channel_id=1, source_target_pairs={{0,5},{1,4},{4,9},{5,8},{8,13},{9,12},{12,15},{13,14},{14,11},{15,... | collective-permute-start | bytes 442376 | tf_op jit(solution)/shard_map/ppermute | solution.py:39
  12.3 6.3 %collective-permute-start.4 = (bf16[64,1152]{1,0:T(8,128)(2,1)S(1)}, bf16[64,1152]{1,0:T(8,128)(2,1)S(1)}, u32[]{:S(2)}, u32[]{:S(2)}) collective-permute-start(bf16[64,1152]{1,0:T(8,128)(2,1)S(1)} %collective-permute-done.3.refs_7_), channel_id=1, source_target_pairs={{0,3},{1,2},{4,1},{5,0},{8,5},{9,4},{12,9},{13,8},{14,13},{15,12},... | collective-permute-start | bytes 442376 | tf_op jit(solution)/shard_map/ppermute | solution.py:39
  13.2 6.3 %collective-permute-start.10 = (bf16[64,1152]{1,0:T(8,128)(2,1)S(1)}, bf16[64,1152]{1,0:T(8,128)(2,1)S(1)}, u32[]{:S(2)}, u32[]{:S(2)}) collective-permute-start(bf16[64,1152]{1,0:T(8,128)(2,1)S(1)} %collective-permute-done.9.refs_5_), channel_id=1, source_target_pairs={{0,5},{1,4},{4,9},{5,8},{8,13},{9,12},{12,15},{13,14},{14,11},{15,... | collective-permute-start | bytes 442376 | tf_op jit(solution)/shard_map/ppermute | solution.py:39
  15.4 6.4 %collective-permute-start.13 = (bf16[64,1152]{1,0:T(8,128)(2,1)S(1)}, bf16[64,1152]{1,0:T(8,128)(2,1)S(1)}, u32[]{:S(2)}, u32[]{:S(2)}) collective-permute-start(bf16[64,1152]{1,0:T(8,128)(2,1)S(1)} %collective-permute-done.12.refs_6_), channel_id=1, source_target_pairs={{0,3},{1,2},{4,1},{5,0},{8,5},{9,4},{12,9},{13,8},{14,13},{15,12},... | collective-permute-start | bytes 442376 | tf_op jit(solution)/shard_map/ppermute | solution.py:39
  16.5 7.8 %collective-permute-start.2 = (bf16[64,1152]{1,0:T(8,128)(2,1)S(1)}, bf16[64,1152]{1,0:T(8,128)(2,1)S(1)}, u32[]{:S(2)}, u32[]{:S(2)}) collective-permute-start(bf16[64,1152]{1,0:T(8,128)(2,1)S(1)} %collective-permute-done.1.refs_8_), channel_id=1, source_target_pairs={{0,5},{1,4},{4,9},{5,8},{8,13},{9,12},{12,15},{13,14},{14,11},{15,... | collective-permute-start | bytes 442376 | tf_op jit(solution)/shard_map/ppermute | solution.py:39
  18.7 6.0 %collective-permute-start.5 = (bf16[64,1152]{1,0:T(8,128)(2,1)S(1)}, bf16[64,1152]{1,0:T(8,128)(2,1)S(1)}, u32[]{:S(2)}, u32[]{:S(2)}) collective-permute-start(bf16[64,1152]{1,0:T(8,128)(2,1)S(1)} %collective-permute-done.4.refs_11_), channel_id=1, source_target_pairs={{0,3},{1,2},{4,1},{5,0},{8,5},{9,4},{12,9},{13,8},{14,13},{15,12},... | collective-permute-start | bytes 442376 | tf_op jit(solution)/shard_map/ppermute | solution.py:39
  19.5 8.6 %collective-permute-start.11 = (bf16[64,1152]{1,0:T(8,128)(2,1)S(1)}, bf16[64,1152]{1,0:T(8,128)(2,1)S(1)}, u32[]{:S(2)}, u32[]{:S(2)}) collective-permute-start(bf16[64,1152]{1,0:T(8,128)(2,1)S(1)} %collective-permute-done.10.refs_9_), channel_id=1, source_target_pairs={{0,5},{1,4},{4,9},{5,8},{8,13},{9,12},{12,15},{13,14},{14,11},{15,... | collective-permute-start | bytes 442376 | tf_op jit(solution)/shard_map/ppermute | solution.py:39
  21.8 6.4 %collective-permute-start.14 = (bf16[64,1152]{1,0:T(8,128)(2,1)S(1)}, bf16[64,1152]{1,0:T(8,128)(2,1)S(1)}, u32[]{:S(2)}, u32[]{:S(2)}) collective-permute-start(bf16[64,1152]{1,0:T(8,128)(2,1)S(1)} %collective-permute-done.13.refs_10_), channel_id=1, source_target_pairs={{0,3},{1,2},{4,1},{5,0},{8,5},{9,4},{12,9},{13,8},{14,13},{15,12},... | collective-permute-start | bytes 442376 | tf_op jit(solution)/shard_map/ppermute | solution.py:39
  24.6 5.7 %collective-permute-start.8 = (bf16[64,1152]{1,0:T(8,128)(2,1)S(1)}, bf16[64,1152]{1,0:T(8,128)(2,1)S(1)}, u32[]{:S(2)}, u32[]{:S(2)}) collective-permute-start(bf16[64,1152]{1,0:T(8,128)(2,1)S(1)} %collective-permute-done.2.refs_2_), channel_id=1, source_target_pairs={{0,5},{1,4},{4,9},{5,8},{8,13},{9,12},{12,15},{13,14},{14,11},{15,... | collective-permute-start | bytes 442376 | tf_op jit(solution)/shard_map/ppermute | solution.py:39
  26.1 5.8 %collective-permute-start.7 = (bf16[64,1152]{1,0:T(8,128)(2,1)S(1)}, bf16[64,1152]{1,0:T(8,128)(2,1)S(1)}, u32[]{:S(2)}, u32[]{:S(2)}) collective-permute-start(bf16[64,1152]{1,0:T(8,128)(2,1)S(1)} %collective-permute-done.5.refs_5_), channel_id=1, source_target_pairs={{0,3},{1,2},{4,1},{5,0},{8,5},{9,4},{12,9},{13,8},{14,13},{15,12},... | collective-permute-start | bytes 442376 | tf_op jit(solution)/shard_map/ppermute | solution.py:39
  32.3 24.0 %copy-start.1 = (bf16[8,4096]{1,0:T(8,128)(2,1)S(1)}, bf16[8,4096]{1,0:T(8,128)(2,1)}, u32[]{:S(2)}) copy-start(bf16[8,4096]{1,0:T(8,128)(2,1)} %queries.1) | copy-start | bytes 196612
  32.3 1.4 %collective-permute-start.15 = (f32[256,128]{1,0:T(8,128)S(1)}, f32[256,128]{1,0:T(8,128)S(1)}, u32[]{:S(2)}, u32[]{:S(2)}) collective-permute-start(f32[256,128]{1,0:T(8,128)S(1)} %shard_map.69), channel_id=1, source_target_pairs={{0,1},{1,0},{2,3},{3,2},{4,5},{5,4},{6,7},{7,6},{8,9},{9,8},{10,11... | collective-permute-start | bytes 393224 | tf_op jit(solution)/shard_map/ppermute | solution.py:43

commit v12 on v11

--- a/solution.py
+++ b/solution.py
@@ -204,9 +204,8 @@
         up.append([ring(x, 1, chips) for x in up[-1]])
         down.append([ring(x, -1, chips) for x in down[-1]])
     last = chips // 2 - 1
+    far = (ring(up[last][0], 1, chips), ring(down[last][1], -1, chips))
     keep = keep_columns(activations, out_grads, chips)
-    keep, far_up, far_down = lax.optimization_barrier((keep, up[last][0], down[last][1]))
-    far = (ring(far_up, 1, chips), ring(far_down, -1, chips))
 
     cut = own[0].shape[1]
     run = functools.partial(project, (keep, theirs), a_width=a_width, cut=cut)

time: 57.3 us -> 57.1 us (level)
  waiting for transfers between devices: 9.41 us -> 7.93 us
  blocking collectives: 21.5 us -> 22.4 us
    ppermute x14, waiting for transfers between devices: 8.2 us -> 6.69 us  [ring(): return lax.ppermute(x, 'dp', pairs)]
    all_to_all x2, blocking collectives: 21.5 us -> 22.4 us  [to_all(): lax.all_to_all(copies, 'dp', 0, 0, axis_index_groups=groups, tiled=True)]
  transfers between devices with their start and end apart: 16 -> 16, of which waited for: 8 -> 7; matrix products, arithmetic and copies ran while one was open for 0% -> 0% of each run, Pallas kernels for 10% -> 10%
where the time goes in v12:
time: 57.1 us; the launch traced here: 56.9 us
  blocking collectives  22.4 us (39%)
  starting transfers between devices  16.1 us (28%)
  Pallas kernels  9.28 us (16%)
  waiting for transfers between devices  7.93 us (14%)
  matrix products  0.89 us (2%)
    all_to_all x2, blocking collectives, to_all(): lax.all_to_all(copies, 'dp', 0, 0, axis_index_groups=groups, tiled=True)  22.4 us
    ppermute x14, starting transfers between devices, ring(): return lax.ppermute(x, 'dp', pairs)  15.4 us
    ppermute x14, waiting for transfers between devices, ring(): return lax.ppermute(x, 'dp', pairs)  6.69 us
    pallas_call x4, Pallas kernels, project(): pl.pallas_call(functools.partial(project_kernel, chips, offsets, parts, a...  3.31 us
    pallas_call x1, Pallas kernels, start(): pl.pallas_call(functools.partial(start_kernel, chips), out_shape=[pltpu.V...  2.74 us
    pallas_call x1, Pallas kernels, keep_columns(): pl.pallas_call(functools.partial(keep_kernel, chips), out_shape=pltpu.VME...  2.49 us
    ppermute x2, waiting for transfers between devices, swap(): return lax.ppermute(x, 'dp', [(i, i ^ bit) for i in range(n)])  1.24 us
  transfers between devices with their start and end apart: 16, of which 7 were waited for; matrix products, arithmetic and copies ran while one was open for 0% of the time, Pallas kernels for 10%

profile of v12, /device:TPU:0, one launch (start us, length us, event | category | flops | bytes accessed | tf_op | source)
XLA Modules:
  0.0 56.9 jit_solution(424133822422490863)
XLA Ops:
  0.0 2.7 %shard_map.65 = (bf16[64,1152]{1,0:T(8,128)(2,1)S(1)}, bf16[64,1152]{1,0:T(8,128)(2,1)S(1)}, bf16[8,128,2304]{2,1,0:T(8,128)(2,1)S(1)}) custom-call(bf16[128,8192]{1,0:T(8,128)(2,1)} %act.3, bf16[128,28672]{1,0:T(8,128)(2,1)} %grad.3, bf16[64,512]{1,0:T(8,128)(2,1)} %bitcast.12, bf16[64,1792]{1,0:T(8,128)(2,1)} %bitcast.11), custom_call_target="tpu_custom_call" | custom-call | bytes 10027008 | tf_op jit(solution)/shard_map/pallas_call | solution.py:92
  2.8 0.5 collective-permute-start
  3.3 2.7 %collective-permute-start.5 = (bf16[64,1152]{1,0:T(8,128)(2,1)S(1)}, bf16[64,1152]{1,0:T(8,128)(2,1)S(1)}, u32[]{:S(2)}, u32[]{:S(2)}) collective-permute-start(bf16[64,1152]{1,0:T(8,128)(2,1)S(1)} %get-tuple-element.10.refs_2_), channel_id=1, source_target_pairs={{0,5},{1,4},{4,9},{5,8},{8,13},{9,12},{12,15},{13,14},{14,11},{15,... | collective-permute-start | bytes 442376 | tf_op jit(solution)/shard_map/ppermute | solution.py:39
  6.0 1.7 %collective-permute-start.9 = (bf16[64,1152]{1,0:T(8,128)(2,1)S(1)}, bf16[64,1152]{1,0:T(8,128)(2,1)S(1)}, u32[]{:S(2)}, u32[]{:S(2)}) collective-permute-start(bf16[64,1152]{1,0:T(8,128)(2,1)S(1)} %get-tuple-element.9.refs_3_), channel_id=1, source_target_pairs={{0,5},{1,4},{4,9},{5,8},{8,13},{9,12},{12,15},{13,14},{14,11},{15,... | collective-permute-start | bytes 442376 | tf_op jit(solution)/shard_map/ppermute | solution.py:39
  7.7 2.4 %collective-permute-done.5.refs_4_ = bf16[64,1152]{1,0:T(8,128)(2,1)S(1)} collective-permute-done((bf16[64,1152]{1,0:T(8,128)(2,1)S(1)}, bf16[64,1152]{1,0:T(8,128)(2,1)S(1)}, u32[]{:S(2)}, u32[]{:S(2)}) %collective-permute-start.5) | collective-permute-done | bytes 147488 | tf_op jit(solution)/shard_map/ppermute | solution.py:39
  10.1 2.2 %collective-permute-start.6 = (bf16[64,1152]{1,0:T(8,128)(2,1)S(1)}, bf16[64,1152]{1,0:T(8,128)(2,1)S(1)}, u32[]{:S(2)}, u32[]{:S(2)}) collective-permute-start(bf16[64,1152]{1,0:T(8,128)(2,1)S(1)} %collective-permute-done.5.refs_4_), channel_id=1, source_target_pairs={{0,5},{1,4},{4,9},{5,8},{8,13},{9,12},{12,15},{13,14},{14,11},{15,... | collective-permute-start | bytes 442376 | tf_op jit(solution)/shard_map/ppermute | solution.py:39
  12.4 0.9 %collective-permute-done.9.refs_5_ = bf16[64,1152]{1,0:T(8,128)(2,1)S(1)} collective-permute-done((bf16[64,1152]{1,0:T(8,128)(2,1)S(1)}, bf16[64,1152]{1,0:T(8,128)(2,1)S(1)}, u32[]{:S(2)}, u32[]{:S(2)}) %collective-permute-start.9) | collective-permute-done | bytes 147488 | tf_op jit(solution)/shard_map/ppermute | solution.py:39
  13.2 2.2 %collective-permute-start.10 = (bf16[64,1152]{1,0:T(8,128)(2,1)S(1)}, bf16[64,1152]{1,0:T(8,128)(2,1)S(1)}, u32[]{:S(2)}, u32[]{:S(2)}) collective-permute-start(bf16[64,1152]{1,0:T(8,128)(2,1)S(1)} %collective-permute-done.9.refs_5_), channel_id=1, source_target_pairs={{0,5},{1,4},{4,9},{5,8},{8,13},{9,12},{12,15},{13,14},{14,11},{15,... | collective-permute-start | bytes 442376 | tf_op jit(solution)/shard_map/ppermute | solution.py:39
  15.4 1.1 %collective-permute-done.6.refs_8_ = bf16[64,1152]{1,0:T(8,128)(2,1)S(1)} collective-permute-done((bf16[64,1152]{1,0:T(8,128)(2,1)S(1)}, bf16[64,1152]{1,0:T(8,128)(2,1)S(1)}, u32[]{:S(2)}, u32[]{:S(2)}) %collective-permute-start.6) | collective-permute-done | bytes 147488 | tf_op jit(solution)/shard_map/ppermute | solution.py:39
  16.5 2.2 %collective-permute-start.7 = (bf16[64,1152]{1,0:T(8,128)(2,1)S(1)}, bf16[64,1152]{1,0:T(8,128)(2,1)S(1)}, u32[]{:S(2)}, u32[]{:S(2)}) collective-permute-start(bf16[64,1152]{1,0:T(8,128)(2,1)S(1)} %collective-permute-done.6.refs_8_), channel_id=1, source_target_pairs={{0,5},{1,4},{4,9},{5,8},{8,13},{9,12},{12,15},{13,14},{14,11},{15,... | collective-permute-start | bytes 442376 | tf_op jit(solution)/shard_map/ppermute | solution.py:39
  18.7 0.9 %collective-permute-done.10.refs_9_ = bf16[64,1152]{1,0:T(8,128)(2,1)S(1)} collective-permute-done((bf16[64,1152]{1,0:T(8,128)(2,1)S(1)}, bf16[64,1152]{1,0:T(8,128)(2,1)S(1)}, u32[]{:S(2)}, u32[]{:S(2)}) %collective-permute-start.10) | collective-permute-done | bytes 147488 | tf_op jit(solution)/shard_map/ppermute | solution.py:39
  19.5 2.2 %collective-permute-start.11 = (bf16[64,1152]{1,0:T(8,128)(2,1)S(1)}, bf16[64,1152]{1,0:T(8,128)(2,1)S(1)}, u32[]{:S(2)}, u32[]{:S(2)}) collective-permute-start(bf16[64,1152]{1,0:T(8,128)(2,1)S(1)} %collective-permute-done.10.refs_9_), channel_id=1, source_target_pairs={{0,5},{1,4},{4,9},{5,8},{8,13},{9,12},{12,15},{13,14},{14,11},{15,... | collective-permute-start | bytes 442376 | tf_op jit(solution)/shard_map/ppermute | solution.py:39
  21.8 1.0 %collective-permute-done.7.refs_2_ = bf16[64,1152]{1,0:T(8,128)(2,1)S(1)} collective-permute-done((bf16[64,1152]{1,0:T(8,128)(2,1)S(1)}, bf16[64,1152]{1,0:T(8,128)(2,1)S(1)}, u32[]{:S(2)}, u32[]{:S(2)}) %collective-permute-start.7) | collective-permute-done | bytes 147488 | tf_op jit(solution)/shard_map/ppermute | solution.py:39
  22.7 2.2 %collective-permute-start.8 = (bf16[64,1152]{1,0:T(8,128)(2,1)S(1)}, bf16[64,1152]{1,0:T(8,128)(2,1)S(1)}, u32[]{:S(2)}, u32[]{:S(2)}) collective-permute-start(bf16[64,1152]{1,0:T(8,128)(2,1)S(1)} %collective-permute-done.7.refs_2_), channel_id=1, source_target_pairs={{0,5},{1,4},{4,9},{5,8},{8,13},{9,12},{12,15},{13,14},{14,11},{15,... | collective-permute-start | bytes 442376 | tf_op jit(solution)/shard_map/ppermute | solution.py:39
  24.9 2.5 %shard_map.64.refs_0_ = bf16[8,128,2304]{2,1,0:T(8,128)(2,1)S(1)} custom-call(bf16[128,8192]{1,0:T(8,128)(2,1)} %act.3, bf16[128,28672]{1,0:T(8,128)(2,1)} %grad.3), custom_call_target="tpu_custom_call" | custom-call | bytes 9437184 | tf_op jit(solution)/shard_map/pallas_call | solution.py:112
  27.4 1.7 %shard_map.66.refs_6_ = f32[256,128]{1,0:T(8,128)S(1)} custom-call(bf16[8,128,2304]{2,1,0:T(8,128)(2,1)S(1)} %shard_map.64.refs_0_, bf16[8,128,2304]{2,1,0:T(8,128)(2,1)S(1)} %collective-permute-done.refs_1_, bf16[64,1152]{1,0:T(8,128)(2,1)S(1)} %get-tuple-element.10.refs_2_, bf16[64,1152]{1,0:T(8,128)(2,1)S(1)} %get-tuple-element.9.refs_3_, ...), custom_call_target="tpu_custom_call" | custom-call | flops 377487360 | bytes 7372800 | tf_op jit(solution)/shard_map/pallas_call | solution.py:156
  29.2 0.8 %shard_map.67.refs_3_ = f32[256,128]{1,0:T(8,128)S(1)} custom-call(bf16[8,128,2304]{2,1,0:T(8,128)(2,1)S(1)} %shard_map.64.refs_0_, bf16[8,128,2304]{2,1,0:T(8,128)(2,1)S(1)} %collective-permute-done.refs_1_, bf16[64,1152]{1,0:T(8,128)(2,1)S(1)} %collective-permute-done.7.refs_2_, bf16[64,1152]{1,0:T(8,128)(2,1)S(1)} %collective-permute-done.11.refs_3_, ...), custom_call_target="tpu_custom_call" | custom-call | flops 150994944 | bytes 2949120 | tf_op jit(solution)/shard_map/pallas_call | solution.py:156
  30.4 0.5 collective-permute-done.4.refs_2_
  30.9 0.4 shard_map.69
  31.5 1.2 %collective-permute-done.15 = f32[256,128]{1,0:T(8,128)S(1)} collective-permute-done((f32[256,128]{1,0:T(8,128)S(1)}, f32[256,128]{1,0:T(8,128)S(1)}, u32[]{:S(2)}, u32[]{:S(2)}) %collective-permute-start.15) | collective-permute-done | bytes 131104 | tf_op jit(solution)/shard_map/ppermute | solution.py:43
  33.1 13.2 %all_to_all.10 = f32[8,32,128]{2,1,0:T(8,128)S(1)} all-to-all(f32[8,32,128]{2,1,0:T(8,128)S(1)} %broadcast_in_dim.14), channel_id=1, replica_groups={{0,2,4,6,8,10,12,14},{1,3,5,7,9,11,13,15},{16,18,20,22,24,26,28,30},{17..., dimensions={0} | all-to-all | bytes 262144 | tf_op jit(solution)/shard_map/all_to_all | solution.py:190
  46.4 0.6 %convolution_convert_fusion = bf16[2,256]{1,0:T(2,128)(2,1)S(1)} fusion(bf16[256,4096]{1,0:T(8,128)(2,1)S(1)} %copy-done, bf16[1,2,32,128]{3,2,1,0:T(8,128)(2,1)S(1)} %bitcast.13), kind=kOutput, calls=%fused_computation.1 | convolution fusion | flops 4194816 | bytes 2114560 | tf_op jit(solution)/shard_map/dot_general | solution.py:23
  47.0 9.1 %all_to_all.11.conditioned = bf16[16,2,256]{2,1,0:T(2,128)(2,1)S(1)} all-to-all(bf16[16,2,256]{2,1,0:T(2,128)(2,1)S(1)} %broadcast_in_dim.15), channel_id=1, replica_groups={{0,1,2,3,4,5,6,7,8,9,10,11,12,13,14,15},{16,17,18,19,20,21,22,23,24,25,..., dimensions={0} | all-to-all | bytes 32768 | tf_op jit(solution)/shard_map/all_to_all | solution.py:190
  56.2 0.7 %shard_map.70 = f32[2,8]{1,0:T(2,128)} custom-call(bf16[16,2,256]{2,1,0:T(2,128)(2,1)S(1)} %all_to_all.11.conditioned, bf16[8,4096]{1,0:T(8,128)(2,1)S(1)} %copy-done.1), custom_call_target="tpu_custom_call" | custom-call | tf_op jit(solution)/shard_map/pallas_call | solution.py:179
  (29 shorter events, 1.0 us)
Async XLA Ops:
  0.0 46.4 %copy-start = (bf16[256,4096]{1,0:T(8,128)(2,1)S(1)}, bf16[256,4096]{1,0:T(8,128)(2,1)}, u32[]{:S(2)}) copy-start(bf16[256,4096]{1,0:T(8,128)(2,1)} %param.10) | copy-start | bytes 6291460
  2.8 24.7 %collective-permute-start = (bf16[8,128,2304]{2,1,0:T(8,128)(2,1)S(1)}, bf16[8,128,2304]{2,1,0:T(8,128)(2,1)S(1)}, u32[]{:S(2)}, u32[]{:S(2)}) collective-permute-start(bf16[8,128,2304]{2,1,0:T(8,128)(2,1)S(1)} %get-tuple-element.8), channel_id=1, source_target_pairs={{0,1},{1,0},{2,3},{3,2},{4,5},{5,4},{6,7},{7,6},{8,9},{9,8},{10,11... | collective-permute-start | bytes 14155784 | tf_op jit(solution)/shard_map/ppermute | solution.py:43
  3.3 6.9 %collective-permute-start.5 = (bf16[64,1152]{1,0:T(8,128)(2,1)S(1)}, bf16[64,1152]{1,0:T(8,128)(2,1)S(1)}, u32[]{:S(2)}, u32[]{:S(2)}) collective-permute-start(bf16[64,1152]{1,0:T(8,128)(2,1)S(1)} %get-tuple-element.10.refs_2_), channel_id=1, source_target_pairs={{0,5},{1,4},{4,9},{5,8},{8,13},{9,12},{12,15},{13,14},{14,11},{15,... | collective-permute-start | bytes 442376 | tf_op jit(solution)/shard_map/ppermute | solution.py:39
  6.0 6.4 %collective-permute-start.1 = (bf16[64,1152]{1,0:T(8,128)(2,1)S(1)}, bf16[64,1152]{1,0:T(8,128)(2,1)S(1)}, u32[]{:S(2)}, u32[]{:S(2)}) collective-permute-start(bf16[64,1152]{1,0:T(8,128)(2,1)S(1)} %get-tuple-element.9.refs_3_), channel_id=1, source_target_pairs={{0,3},{1,2},{4,1},{5,0},{8,5},{9,4},{12,9},{13,8},{14,13},{15,12},... | collective-permute-start | bytes 442376 | tf_op jit(solution)/shard_map/ppermute | solution.py:39
  6.0 7.3 %collective-permute-start.9 = (bf16[64,1152]{1,0:T(8,128)(2,1)S(1)}, bf16[64,1152]{1,0:T(8,128)(2,1)S(1)}, u32[]{:S(2)}, u32[]{:S(2)}) collective-permute-start(bf16[64,1152]{1,0:T(8,128)(2,1)S(1)} %get-tuple-element.9.refs_3_), channel_id=1, source_target_pairs={{0,5},{1,4},{4,9},{5,8},{8,13},{9,12},{12,15},{13,14},{14,11},{15,... | collective-permute-start | bytes 442376 | tf_op jit(solution)/shard_map/ppermute | solution.py:39
  7.7 7.7 %collective-permute-start.12 = (bf16[64,1152]{1,0:T(8,128)(2,1)S(1)}, bf16[64,1152]{1,0:T(8,128)(2,1)S(1)}, u32[]{:S(2)}, u32[]{:S(2)}) collective-permute-start(bf16[64,1152]{1,0:T(8,128)(2,1)S(1)} %get-tuple-element.10.refs_2_), channel_id=1, source_target_pairs={{0,3},{1,2},{4,1},{5,0},{8,5},{9,4},{12,9},{13,8},{14,13},{15,12},... | collective-permute-start | bytes 442376 | tf_op jit(solution)/shard_map/ppermute | solution.py:39
  10.1 6.3 %collective-permute-start.6 = (bf16[64,1152]{1,0:T(8,128)(2,1)S(1)}, bf16[64,1152]{1,0:T(8,128)(2,1)S(1)}, u32[]{:S(2)}, u32[]{:S(2)}) collective-permute-start(bf16[64,1152]{1,0:T(8,128)(2,1)S(1)} %collective-permute-done.5.refs_4_), channel_id=1, source_target_pairs={{0,5},{1,4},{4,9},{5,8},{8,13},{9,12},{12,15},{13,14},{14,11},{15,... | collective-permute-start | bytes 442376 | tf_op jit(solution)/shard_map/ppermute | solution.py:39
  12.3 6.3 %collective-permute-start.2 = (bf16[64,1152]{1,0:T(8,128)(2,1)S(1)}, bf16[64,1152]{1,0:T(8,128)(2,1)S(1)}, u32[]{:S(2)}, u32[]{:S(2)}) collective-permute-start(bf16[64,1152]{1,0:T(8,128)(2,1)S(1)} %collective-permute-done.1.refs_7_), channel_id=1, source_target_pairs={{0,3},{1,2},{4,1},{5,0},{8,5},{9,4},{12,9},{13,8},{14,13},{15,12},... | collective-permute-start | bytes 442376 | tf_op jit(solution)/shard_map/ppermute | solution.py:39
  13.2 6.3 %collective-permute-start.10 = (bf16[64,1152]{1,0:T(8,128)(2,1)S(1)}, bf16[64,1152]{1,0:T(8,128)(2,1)S(1)}, u32[]{:S(2)}, u32[]{:S(2)}) collective-permute-start(bf16[64,1152]{1,0:T(8,128)(2,1)S(1)} %collective-permute-done.9.refs_5_), channel_id=1, source_target_pairs={{0,5},{1,4},{4,9},{5,8},{8,13},{9,12},{12,15},{13,14},{14,11},{15,... | collective-permute-start | bytes 442376 | tf_op jit(solution)/shard_map/ppermute | solution.py:39
  15.4 6.4 %collective-permute-start.13 = (bf16[64,1152]{1,0:T(8,128)(2,1)S(1)}, bf16[64,1152]{1,0:T(8,128)(2,1)S(1)}, u32[]{:S(2)}, u32[]{:S(2)}) collective-permute-start(bf16[64,1152]{1,0:T(8,128)(2,1)S(1)} %collective-permute-done.12.refs_6_), channel_id=1, source_target_pairs={{0,3},{1,2},{4,1},{5,0},{8,5},{9,4},{12,9},{13,8},{14,13},{15,12},... | collective-permute-start | bytes 442376 | tf_op jit(solution)/shard_map/ppermute | solution.py:39
  16.5 6.3 %collective-permute-start.7 = (bf16[64,1152]{1,0:T(8,128)(2,1)S(1)}, bf16[64,1152]{1,0:T(8,128)(2,1)S(1)}, u32[]{:S(2)}, u32[]{:S(2)}) collective-permute-start(bf16[64,1152]{1,0:T(8,128)(2,1)S(1)} %collective-permute-done.6.refs_8_), channel_id=1, source_target_pairs={{0,5},{1,4},{4,9},{5,8},{8,13},{9,12},{12,15},{13,14},{14,11},{15,... | collective-permute-start | bytes 442376 | tf_op jit(solution)/shard_map/ppermute | solution.py:39
  18.7 6.3 %collective-permute-start.3 = (bf16[64,1152]{1,0:T(8,128)(2,1)S(1)}, bf16[64,1152]{1,0:T(8,128)(2,1)S(1)}, u32[]{:S(2)}, u32[]{:S(2)}) collective-permute-start(bf16[64,1152]{1,0:T(8,128)(2,1)S(1)} %collective-permute-done.2.refs_11_), channel_id=1, source_target_pairs={{0,3},{1,2},{4,1},{5,0},{8,5},{9,4},{12,9},{13,8},{14,13},{15,12},... | collective-permute-start | bytes 442376 | tf_op jit(solution)/shard_map/ppermute | solution.py:39
  19.5 9.6 %collective-permute-start.11 = (bf16[64,1152]{1,0:T(8,128)(2,1)S(1)}, bf16[64,1152]{1,0:T(8,128)(2,1)S(1)}, u32[]{:S(2)}, u32[]{:S(2)}) collective-permute-start(bf16[64,1152]{1,0:T(8,128)(2,1)S(1)} %collective-permute-done.10.refs_9_), channel_id=1, source_target_pairs={{0,5},{1,4},{4,9},{5,8},{8,13},{9,12},{12,15},{13,14},{14,11},{15,... | collective-permute-start | bytes 442376 | tf_op jit(solution)/shard_map/ppermute | solution.py:39
  21.8 7.4 %collective-permute-start.14 = (bf16[64,1152]{1,0:T(8,128)(2,1)S(1)}, bf16[64,1152]{1,0:T(8,128)(2,1)S(1)}, u32[]{:S(2)}, u32[]{:S(2)}) collective-permute-start(bf16[64,1152]{1,0:T(8,128)(2,1)S(1)} %collective-permute-done.13.refs_10_), channel_id=1, source_target_pairs={{0,3},{1,2},{4,1},{5,0},{8,5},{9,4},{12,9},{13,8},{14,13},{15,12},... | collective-permute-start | bytes 442376 | tf_op jit(solution)/shard_map/ppermute | solution.py:39
  22.7 7.3 %collective-permute-start.8 = (bf16[64,1152]{1,0:T(8,128)(2,1)S(1)}, bf16[64,1152]{1,0:T(8,128)(2,1)S(1)}, u32[]{:S(2)}, u32[]{:S(2)}) collective-permute-start(bf16[64,1152]{1,0:T(8,128)(2,1)S(1)} %collective-permute-done.7.refs_2_), channel_id=1, source_target_pairs={{0,5},{1,4},{4,9},{5,8},{8,13},{9,12},{12,15},{13,14},{14,11},{15,... | collective-permute-start | bytes 442376 | tf_op jit(solution)/shard_map/ppermute | solution.py:39
  24.9 6.0 %collective-permute-start.4 = (bf16[64,1152]{1,0:T(8,128)(2,1)S(1)}, bf16[64,1152]{1,0:T(8,128)(2,1)S(1)}, u32[]{:S(2)}, u32[]{:S(2)}) collective-permute-start(bf16[64,1152]{1,0:T(8,128)(2,1)S(1)} %collective-permute-done.3.refs_5_), channel_id=1, source_target_pairs={{0,3},{1,2},{4,1},{5,0},{8,5},{9,4},{12,9},{13,8},{14,13},{15,12},... | collective-permute-start | bytes 442376 | tf_op jit(solution)/shard_map/ppermute | solution.py:39
  31.3 24.9 %copy-start.1 = (bf16[8,4096]{1,0:T(8,128)(2,1)S(1)}, bf16[8,4096]{1,0:T(8,128)(2,1)}, u32[]{:S(2)}) copy-start(bf16[8,4096]{1,0:T(8,128)(2,1)} %queries.1) | copy-start | bytes 196612
  31.3 1.4 %collective-permute-start.15 = (f32[256,128]{1,0:T(8,128)S(1)}, f32[256,128]{1,0:T(8,128)S(1)}, u32[]{:S(2)}, u32[]{:S(2)}) collective-permute-start(f32[256,128]{1,0:T(8,128)S(1)} %shard_map.69), channel_id=1, source_target_pairs={{0,1},{1,0},{2,3},{3,2},{4,5},{5,4},{6,7},{7,6},{8,9},{9,8},{10,11... | collective-permute-start | bytes 393224 | tf_op jit(solution)/shard_map/ppermute | solution.py:43

commit v13 on v12

--- a/solution.py
+++ b/solution.py
@@ -225,10 +225,14 @@
 
     raw = dot(total[:, rank:], total[:, :rank], TN)
     raw = (raw * (1.0 / math.sqrt(LEN))).reshape(-1, 128)
-    planes = [[2 * i + c for i in range(chips)] for c in range(2)]
-    raw = to_all(raw, planes)
-    features = raw.reshape((-1, split // 2) + raw.shape[1:]).sum(axis=1)
-    features = features.astype(jnp.bfloat16).reshape(-1, rank * rank)
+    features = (raw + sum(swap(raw, i, n) for i in range(2, split, 2))).astype(jnp.bfloat16)[None]
+    bit = split
+    while bit < n:
+        pair = features, swap(features, bit, n)
+        first = (lax.axis_index("dp") & bit) == 0
+        features = jnp.where(first, jnp.concatenate(pair), jnp.concatenate(pair[::-1]))
+        bit *= 2
+    features = features.reshape(-1, rank * rank)
 
     conditioned = dot(features, preconditioner, NT).astype(jnp.bfloat16)
     return score(to_all(conditioned, [list(range(n))]), queries, 1.0 / rank)

time: 57.1 us -> 57.7 us (1.011)
  blocking collectives: 22.4 us -> 10.8 us
  starting transfers between devices: 16.1 us -> 22.6 us
  waiting for transfers between devices: 7.93 us -> 13.6 us
    all_to_all x2 -> x1, blocking collectives: 22.4 us -> 10.8 us  [to_all(): lax.all_to_all(copies, 'dp', 0, 0, axis_index_groups=groups, tiled=True)]
    ppermute x2 -> x6, starting transfers between devices: 0.7 us -> 7.16 us  [swap(): return lax.ppermute(x, 'dp', [(i, i ^ bit) for i in range(n)])]
    ppermute x2 -> x6, waiting for transfers between devices: 1.24 us -> 6.92 us  [swap(): return lax.ppermute(x, 'dp', [(i, i ^ bit) for i in range(n)])]
  transfers between devices with their start and end apart: 16 -> 20, of which waited for: 7 -> 11; matrix products, arithmetic and copies ran while one was open for 0% -> 0% of each run, Pallas kernels for 10% -> 9%
where the time goes in v13:
time: 57.7 us; the launch traced here: 57.5 us
  starting transfers between devices  22.6 us (39%)
  waiting for transfers between devices  13.6 us (24%)
  blocking collectives  10.8 us (19%)
  Pallas kernels  9.28 us (16%)
  matrix products  0.9 us (2%)
    ppermute x14, starting transfers between devices, ring(): return lax.ppermute(x, 'dp', pairs)  15.4 us
    all_to_all x1, blocking collectives, to_all(): lax.all_to_all(copies, 'dp', 0, 0, axis_index_groups=groups, tiled=True)  10.8 us
    ppermute x6, starting transfers between devices, swap(): return lax.ppermute(x, 'dp', [(i, i ^ bit) for i in range(n)])  7.16 us
    ppermute x6, waiting for transfers between devices, swap(): return lax.ppermute(x, 'dp', [(i, i ^ bit) for i in range(n)])  6.92 us
    ppermute x14, waiting for transfers between devices, ring(): return lax.ppermute(x, 'dp', pairs)  6.69 us
    pallas_call x4, Pallas kernels, project(): pl.pallas_call(functools.partial(project_kernel, chips, offsets, parts, a...  3.31 us
    pallas_call x1, Pallas kernels, start(): pl.pallas_call(functools.partial(start_kernel, chips), out_shape=[pltpu.V...  2.74 us
    pallas_call x1, Pallas kernels, keep_columns(): pl.pallas_call(functools.partial(keep_kernel, chips), out_shape=pltpu.VME...  2.49 us
  transfers between devices with their start and end apart: 20, of which 11 were waited for; matrix products, arithmetic and copies ran while one was open for 0% of the time, Pallas kernels for 9%

profile of v13, /device:TPU:0, one launch (start us, length us, event | category | flops | bytes accessed | tf_op | source)
XLA Modules:
  0.0 57.5 jit_solution(16075898287324401614)
XLA Ops:
  0.0 2.7 %shard_map.65 = (bf16[64,1152]{1,0:T(8,128)(2,1)S(1)}, bf16[64,1152]{1,0:T(8,128)(2,1)S(1)}, bf16[8,128,2304]{2,1,0:T(8,128)(2,1)S(1)}) custom-call(bf16[128,8192]{1,0:T(8,128)(2,1)} %act.3, bf16[128,28672]{1,0:T(8,128)(2,1)} %grad.3, bf16[64,512]{1,0:T(8,128)(2,1)} %bitcast.14, bf16[64,1792]{1,0:T(8,128)(2,1)} %bitcast.13), custom_call_target="tpu_custom_call" | custom-call | bytes 10027008 | tf_op jit(solution)/shard_map/pallas_call | solution.py:92
  3.3 2.7 %collective-permute-start.5 = (bf16[64,1152]{1,0:T(8,128)(2,1)S(1)}, bf16[64,1152]{1,0:T(8,128)(2,1)S(1)}, u32[]{:S(2)}, u32[]{:S(2)}) collective-permute-start(bf16[64,1152]{1,0:T(8,128)(2,1)S(1)} %get-tuple-element.10.refs_2_), channel_id=1, source_target_pairs={{0,5},{1,4},{4,9},{5,8},{8,13},{9,12},{12,15},{13,14},{14,11},{15,... | collective-permute-start | bytes 442376 | tf_op jit(solution)/shard_map/ppermute | solution.py:39
  6.0 1.7 %collective-permute-start.9 = (bf16[64,1152]{1,0:T(8,128)(2,1)S(1)}, bf16[64,1152]{1,0:T(8,128)(2,1)S(1)}, u32[]{:S(2)}, u32[]{:S(2)}) collective-permute-start(bf16[64,1152]{1,0:T(8,128)(2,1)S(1)} %get-tuple-element.9.refs_3_), channel_id=1, source_target_pairs={{0,5},{1,4},{4,9},{5,8},{8,13},{9,12},{12,15},{13,14},{14,11},{15,... | collective-permute-start | bytes 442376 | tf_op jit(solution)/shard_map/ppermute | solution.py:39
  7.7 2.4 %collective-permute-done.5.refs_4_ = bf16[64,1152]{1,0:T(8,128)(2,1)S(1)} collective-permute-done((bf16[64,1152]{1,0:T(8,128)(2,1)S(1)}, bf16[64,1152]{1,0:T(8,128)(2,1)S(1)}, u32[]{:S(2)}, u32[]{:S(2)}) %collective-permute-start.5) | collective-permute-done | bytes 147488 | tf_op jit(solution)/shard_map/ppermute | solution.py:39
  10.1 2.2 %collective-permute-start.6 = (bf16[64,1152]{1,0:T(8,128)(2,1)S(1)}, bf16[64,1152]{1,0:T(8,128)(2,1)S(1)}, u32[]{:S(2)}, u32[]{:S(2)}) collective-permute-start(bf16[64,1152]{1,0:T(8,128)(2,1)S(1)} %collective-permute-done.5.refs_4_), channel_id=1, source_target_pairs={{0,5},{1,4},{4,9},{5,8},{8,13},{9,12},{12,15},{13,14},{14,11},{15,... | collective-permute-start | bytes 442376 | tf_op jit(solution)/shard_map/ppermute | solution.py:39
  12.4 0.9 %collective-permute-done.9.refs_5_ = bf16[64,1152]{1,0:T(8,128)(2,1)S(1)} collective-permute-done((bf16[64,1152]{1,0:T(8,128)(2,1)S(1)}, bf16[64,1152]{1,0:T(8,128)(2,1)S(1)}, u32[]{:S(2)}, u32[]{:S(2)}) %collective-permute-start.9) | collective-permute-done | bytes 147488 | tf_op jit(solution)/shard_map/ppermute | solution.py:39
  13.2 2.2 %collective-permute-start.10 = (bf16[64,1152]{1,0:T(8,128)(2,1)S(1)}, bf16[64,1152]{1,0:T(8,128)(2,1)S(1)}, u32[]{:S(2)}, u32[]{:S(2)}) collective-permute-start(bf16[64,1152]{1,0:T(8,128)(2,1)S(1)} %collective-permute-done.9.refs_5_), channel_id=1, source_target_pairs={{0,5},{1,4},{4,9},{5,8},{8,13},{9,12},{12,15},{13,14},{14,11},{15,... | collective-permute-start | bytes 442376 | tf_op jit(solution)/shard_map/ppermute | solution.py:39
  15.4 1.1 %collective-permute-done.6.refs_8_ = bf16[64,1152]{1,0:T(8,128)(2,1)S(1)} collective-permute-done((bf16[64,1152]{1,0:T(8,128)(2,1)S(1)}, bf16[64,1152]{1,0:T(8,128)(2,1)S(1)}, u32[]{:S(2)}, u32[]{:S(2)}) %collective-permute-start.6) | collective-permute-done | bytes 147488 | tf_op jit(solution)/shard_map/ppermute | solution.py:39
  16.5 2.2 %collective-permute-start.7 = (bf16[64,1152]{1,0:T(8,128)(2,1)S(1)}, bf16[64,1152]{1,0:T(8,128)(2,1)S(1)}, u32[]{:S(2)}, u32[]{:S(2)}) collective-permute-start(bf16[64,1152]{1,0:T(8,128)(2,1)S(1)} %collective-permute-done.6.refs_8_), channel_id=1, source_target_pairs={{0,5},{1,4},{4,9},{5,8},{8,13},{9,12},{12,15},{13,14},{14,11},{15,... | collective-permute-start | bytes 442376 | tf_op jit(solution)/shard_map/ppermute | solution.py:39
  18.7 0.9 %collective-permute-done.10.refs_9_ = bf16[64,1152]{1,0:T(8,128)(2,1)S(1)} collective-permute-done((bf16[64,1152]{1,0:T(8,128)(2,1)S(1)}, bf16[64,1152]{1,0:T(8,128)(2,1)S(1)}, u32[]{:S(2)}, u32[]{:S(2)}) %collective-permute-start.10) | collective-permute-done | bytes 147488 | tf_op jit(solution)/shard_map/ppermute | solution.py:39
  19.5 2.2 %collective-permute-start.11 = (bf16[64,1152]{1,0:T(8,128)(2,1)S(1)}, bf16[64,1152]{1,0:T(8,128)(2,1)S(1)}, u32[]{:S(2)}, u32[]{:S(2)}) collective-permute-start(bf16[64,1152]{1,0:T(8,128)(2,1)S(1)} %collective-permute-done.10.refs_9_), channel_id=1, source_target_pairs={{0,5},{1,4},{4,9},{5,8},{8,13},{9,12},{12,15},{13,14},{14,11},{15,... | collective-permute-start | bytes 442376 | tf_op jit(solution)/shard_map/ppermute | solution.py:39
  21.8 1.0 %collective-permute-done.7.refs_2_ = bf16[64,1152]{1,0:T(8,128)(2,1)S(1)} collective-permute-done((bf16[64,1152]{1,0:T(8,128)(2,1)S(1)}, bf16[64,1152]{1,0:T(8,128)(2,1)S(1)}, u32[]{:S(2)}, u32[]{:S(2)}) %collective-permute-start.7) | collective-permute-done | bytes 147488 | tf_op jit(solution)/shard_map/ppermute | solution.py:39
  22.7 2.2 %collective-permute-start.8 = (bf16[64,1152]{1,0:T(8,128)(2,1)S(1)}, bf16[64,1152]{1,0:T(8,128)(2,1)S(1)}, u32[]{:S(2)}, u32[]{:S(2)}) collective-permute-start(bf16[64,1152]{1,0:T(8,128)(2,1)S(1)} %collective-permute-done.7.refs_2_), channel_id=1, source_target_pairs={{0,5},{1,4},{4,9},{5,8},{8,13},{9,12},{12,15},{13,14},{14,11},{15,... | collective-permute-start | bytes 442376 | tf_op jit(solution)/shard_map/ppermute | solution.py:39
  24.9 2.5 %shard_map.64.refs_0_ = bf16[8,128,2304]{2,1,0:T(8,128)(2,1)S(1)} custom-call(bf16[128,8192]{1,0:T(8,128)(2,1)} %act.3, bf16[128,28672]{1,0:T(8,128)(2,1)} %grad.3), custom_call_target="tpu_custom_call" | custom-call | bytes 9437184 | tf_op jit(solution)/shard_map/pallas_call | solution.py:112
  27.4 1.7 %shard_map.66.refs_6_ = f32[256,128]{1,0:T(8,128)S(1)} custom-call(bf16[8,128,2304]{2,1,0:T(8,128)(2,1)S(1)} %shard_map.64.refs_0_, bf16[8,128,2304]{2,1,0:T(8,128)(2,1)S(1)} %collective-permute-done.refs_1_, bf16[64,1152]{1,0:T(8,128)(2,1)S(1)} %get-tuple-element.10.refs_2_, bf16[64,1152]{1,0:T(8,128)(2,1)S(1)} %get-tuple-element.9.refs_3_, ...), custom_call_target="tpu_custom_call" | custom-call | flops 377487360 | bytes 7372800 | tf_op jit(solution)/shard_map/pallas_call | solution.py:156
  29.2 0.8 %shard_map.67.refs_3_ = f32[256,128]{1,0:T(8,128)S(1)} custom-call(bf16[8,128,2304]{2,1,0:T(8,128)(2,1)S(1)} %shard_map.64.refs_0_, bf16[8,128,2304]{2,1,0:T(8,128)(2,1)S(1)} %collective-permute-done.refs_1_, bf16[64,1152]{1,0:T(8,128)(2,1)S(1)} %collective-permute-done.7.refs_2_, bf16[64,1152]{1,0:T(8,128)(2,1)S(1)} %collective-permute-done.11.refs_3_, ...), custom_call_target="tpu_custom_call" | custom-call | flops 150994944 | bytes 2949120 | tf_op jit(solution)/shard_map/pallas_call | solution.py:156
  31.5 1.2 %collective-permute-done.15 = f32[256,128]{1,0:T(8,128)S(1)} collective-permute-done((f32[256,128]{1,0:T(8,128)S(1)}, f32[256,128]{1,0:T(8,128)S(1)}, u32[]{:S(2)}, u32[]{:S(2)}) %collective-permute-start.15) | collective-permute-done | bytes 131104 | tf_op jit(solution)/shard_map/ppermute | solution.py:43
  33.1 1.4 %collective-permute-start.16 = (f32[32,128]{1,0:T(8,128)S(1)}, f32[32,128]{1,0:T(8,128)S(1)}, u32[]{:S(2)}, u32[]{:S(2)}) collective-permute-start(f32[32,128]{1,0:T(8,128)S(1)} %reshape.11), channel_id=1, source_target_pairs={{0,2},{1,3},{2,0},{3,1},{4,6},{5,7},{6,4},{7,5},{8,10},{9,11},{10,... | collective-permute-start | bytes 49160 | tf_op jit(solution)/shard_map/ppermute | solution.py:43
  34.5 1.5 %collective-permute-start.17 = (f32[32,128]{1,0:T(8,128)S(1)}, f32[32,128]{1,0:T(8,128)S(1)}, u32[]{:S(2)}, u32[]{:S(2)}) collective-permute-start(f32[32,128]{1,0:T(8,128)S(1)} %reshape.11), channel_id=1, source_target_pairs={{0,4},{1,5},{2,6},{3,7},{4,0},{5,1},{6,2},{7,3},{8,12},{9,13},{10,... | collective-permute-start | bytes 49160 | tf_op jit(solution)/shard_map/ppermute | solution.py:43
  36.8 1.4 %collective-permute-done.17 = f32[32,128]{1,0:T(8,128)S(1)} collective-permute-done((f32[32,128]{1,0:T(8,128)S(1)}, f32[32,128]{1,0:T(8,128)S(1)}, u32[]{:S(2)}, u32[]{:S(2)}) %collective-permute-start.17) | collective-permute-done | bytes 16416 | tf_op jit(solution)/shard_map/ppermute | solution.py:43
  38.3 2.4 %collective-permute-done.18 = f32[32,128]{1,0:T(8,128)S(1)} collective-permute-done((f32[32,128]{1,0:T(8,128)S(1)}, f32[32,128]{1,0:T(8,128)S(1)}, u32[]{:S(2)}, u32[]{:S(2)}) %collective-permute-start.18) | collective-permute-done | bytes 16416 | tf_op jit(solution)/shard_map/ppermute | solution.py:43
  40.6 3.0 %collective-permute-start.19 = (bf16[1,32,128]{2,1,0:T(8,128)(2,1)S(1)}, bf16[1,32,128]{2,1,0:T(8,128)(2,1)S(1)}, u32[]{:S(2)}, u32[]{:S(2)}) collective-permute-start(bf16[1,32,128]{2,1,0:T(8,128)(2,1)S(1)} %bitcast.17), channel_id=1, source_target_pairs={{0,8},{1,9},{2,10},{3,11},{4,12},{5,13},{6,14},{7,15},{8,0},{9,1},... | collective-permute-start | bytes 24584 | tf_op jit(solution)/shard_map/ppermute | solution.py:43
  43.6 1.6 %collective-permute-done.19 = bf16[1,32,128]{2,1,0:T(8,128)(2,1)S(1)} collective-permute-done((bf16[1,32,128]{2,1,0:T(8,128)(2,1)S(1)}, bf16[1,32,128]{2,1,0:T(8,128)(2,1)S(1)}, u32[]{:S(2)}, u32[]{:S(2)}) %collective-permute-start.19) | collective-permute-done | bytes 8224 | tf_op jit(solution)/shard_map/ppermute | solution.py:43
  46.0 10.8 %all_to_all.5.conditioned = bf16[16,2,256]{2,1,0:T(2,128)(2,1)S(1)} all-to-all(bf16[16,2,256]{2,1,0:T(2,128)(2,1)S(1)} %broadcast_in_dim.10), channel_id=1, replica_groups={{0,1,2,3,4,5,6,7,8,9,10,11,12,13,14,15},{16,17,18,19,20,21,22,23,24,25,..., dimensions={0} | all-to-all | bytes 32768 | tf_op jit(solution)/shard_map/all_to_all | solution.py:190
  (37 shorter events, 4.6 us)
Async XLA Ops:
  0.0 45.3 %copy-start = (bf16[256,4096]{1,0:T(8,128)(2,1)S(1)}, bf16[256,4096]{1,0:T(8,128)(2,1)}, u32[]{:S(2)}) copy-start(bf16[256,4096]{1,0:T(8,128)(2,1)} %param.10) | copy-start | bytes 6291460
  2.8 24.7 %collective-permute-start = (bf16[8,128,2304]{2,1,0:T(8,128)(2,1)S(1)}, bf16[8,128,2304]{2,1,0:T(8,128)(2,1)S(1)}, u32[]{:S(2)}, u32[]{:S(2)}) collective-permute-start(bf16[8,128,2304]{2,1,0:T(8,128)(2,1)S(1)} %get-tuple-element.8), channel_id=1, source_target_pairs={{0,1},{1,0},{2,3},{3,2},{4,5},{5,4},{6,7},{7,6},{8,9},{9,8},{10,11... | collective-permute-start | bytes 14155784 | tf_op jit(solution)/shard_map/ppermute | solution.py:43
  3.3 6.9 %collective-permute-start.5 = (bf16[64,1152]{1,0:T(8,128)(2,1)S(1)}, bf16[64,1152]{1,0:T(8,128)(2,1)S(1)}, u32[]{:S(2)}, u32[]{:S(2)}) collective-permute-start(bf16[64,1152]{1,0:T(8,128)(2,1)S(1)} %get-tuple-element.10.refs_2_), channel_id=1, source_target_pairs={{0,5},{1,4},{4,9},{5,8},{8,13},{9,12},{12,15},{13,14},{14,11},{15,... | collective-permute-start | bytes 442376 | tf_op jit(solution)/shard_map/ppermute | solution.py:39
  6.0 6.4 %collective-permute-start.1 = (bf16[64,1152]{1,0:T(8,128)(2,1)S(1)}, bf16[64,1152]{1,0:T(8,128)(2,1)S(1)}, u32[]{:S(2)}, u32[]{:S(2)}) collective-permute-start(bf16[64,1152]{1,0:T(8,128)(2,1)S(1)} %get-tuple-element.9.refs_3_), channel_id=1, source_target_pairs={{0,3},{1,2},{4,1},{5,0},{8,5},{9,4},{12,9},{13,8},{14,13},{15,12},... | collective-permute-start | bytes 442376 | tf_op jit(solution)/shard_map/ppermute | solution.py:39
  6.0 7.3 %collective-permute-start.9 = (bf16[64,1152]{1,0:T(8,128)(2,1)S(1)}, bf16[64,1152]{1,0:T(8,128)(2,1)S(1)}, u32[]{:S(2)}, u32[]{:S(2)}) collective-permute-start(bf16[64,1152]{1,0:T(8,128)(2,1)S(1)} %get-tuple-element.9.refs_3_), channel_id=1, source_target_pairs={{0,5},{1,4},{4,9},{5,8},{8,13},{9,12},{12,15},{13,14},{14,11},{15,... | collective-permute-start | bytes 442376 | tf_op jit(solution)/shard_map/ppermute | solution.py:39
  7.7 7.7 %collective-permute-start.12 = (bf16[64,1152]{1,0:T(8,128)(2,1)S(1)}, bf16[64,1152]{1,0:T(8,128)(2,1)S(1)}, u32[]{:S(2)}, u32[]{:S(2)}) collective-permute-start(bf16[64,1152]{1,0:T(8,128)(2,1)S(1)} %get-tuple-element.10.refs_2_), channel_id=1, source_target_pairs={{0,3},{1,2},{4,1},{5,0},{8,5},{9,4},{12,9},{13,8},{14,13},{15,12},... | collective-permute-start | bytes 442376 | tf_op jit(solution)/shard_map/ppermute | solution.py:39
  10.1 6.3 %collective-permute-start.6 = (bf16[64,1152]{1,0:T(8,128)(2,1)S(1)}, bf16[64,1152]{1,0:T(8,128)(2,1)S(1)}, u32[]{:S(2)}, u32[]{:S(2)}) collective-permute-start(bf16[64,1152]{1,0:T(8,128)(2,1)S(1)} %collective-permute-done.5.refs_4_), channel_id=1, source_target_pairs={{0,5},{1,4},{4,9},{5,8},{8,13},{9,12},{12,15},{13,14},{14,11},{15,... | collective-permute-start | bytes 442376 | tf_op jit(solution)/shard_map/ppermute | solution.py:39
  12.3 6.3 %collective-permute-start.2 = (bf16[64,1152]{1,0:T(8,128)(2,1)S(1)}, bf16[64,1152]{1,0:T(8,128)(2,1)S(1)}, u32[]{:S(2)}, u32[]{:S(2)}) collective-permute-start(bf16[64,1152]{1,0:T(8,128)(2,1)S(1)} %collective-permute-done.1.refs_7_), channel_id=1, source_target_pairs={{0,3},{1,2},{4,1},{5,0},{8,5},{9,4},{12,9},{13,8},{14,13},{15,12},... | collective-permute-start | bytes 442376 | tf_op jit(solution)/shard_map/ppermute | solution.py:39
  13.2 6.3 %collective-permute-start.10 = (bf16[64,1152]{1,0:T(8,128)(2,1)S(1)}, bf16[64,1152]{1,0:T(8,128)(2,1)S(1)}, u32[]{:S(2)}, u32[]{:S(2)}) collective-permute-start(bf16[64,1152]{1,0:T(8,128)(2,1)S(1)} %collective-permute-done.9.refs_5_), channel_id=1, source_target_pairs={{0,5},{1,4},{4,9},{5,8},{8,13},{9,12},{12,15},{13,14},{14,11},{15,... | collective-permute-start | bytes 442376 | tf_op jit(solution)/shard_map/ppermute | solution.py:39
  15.4 6.4 %collective-permute-start.13 = (bf16[64,1152]{1,0:T(8,128)(2,1)S(1)}, bf16[64,1152]{1,0:T(8,128)(2,1)S(1)}, u32[]{:S(2)}, u32[]{:S(2)}) collective-permute-start(bf16[64,1152]{1,0:T(8,128)(2,1)S(1)} %collective-permute-done.12.refs_6_), channel_id=1, source_target_pairs={{0,3},{1,2},{4,1},{5,0},{8,5},{9,4},{12,9},{13,8},{14,13},{15,12},... | collective-permute-start | bytes 442376 | tf_op jit(solution)/shard_map/ppermute | solution.py:39
  16.5 6.3 %collective-permute-start.7 = (bf16[64,1152]{1,0:T(8,128)(2,1)S(1)}, bf16[64,1152]{1,0:T(8,128)(2,1)S(1)}, u32[]{:S(2)}, u32[]{:S(2)}) collective-permute-start(bf16[64,1152]{1,0:T(8,128)(2,1)S(1)} %collective-permute-done.6.refs_8_), channel_id=1, source_target_pairs={{0,5},{1,4},{4,9},{5,8},{8,13},{9,12},{12,15},{13,14},{14,11},{15,... | collective-permute-start | bytes 442376 | tf_op jit(solution)/shard_map/ppermute | solution.py:39
  18.7 6.3 %collective-permute-start.3 = (bf16[64,1152]{1,0:T(8,128)(2,1)S(1)}, bf16[64,1152]{1,0:T(8,128)(2,1)S(1)}, u32[]{:S(2)}, u32[]{:S(2)}) collective-permute-start(bf16[64,1152]{1,0:T(8,128)(2,1)S(1)} %collective-permute-done.2.refs_11_), channel_id=1, source_target_pairs={{0,3},{1,2},{4,1},{5,0},{8,5},{9,4},{12,9},{13,8},{14,13},{15,12},... | collective-permute-start | bytes 442376 | tf_op jit(solution)/shard_map/ppermute | solution.py:39
  19.5 9.6 %collective-permute-start.11 = (bf16[64,1152]{1,0:T(8,128)(2,1)S(1)}, bf16[64,1152]{1,0:T(8,128)(2,1)S(1)}, u32[]{:S(2)}, u32[]{:S(2)}) collective-permute-start(bf16[64,1152]{1,0:T(8,128)(2,1)S(1)} %collective-permute-done.10.refs_9_), channel_id=1, source_target_pairs={{0,5},{1,4},{4,9},{5,8},{8,13},{9,12},{12,15},{13,14},{14,11},{15,... | collective-permute-start | bytes 442376 | tf_op jit(solution)/shard_map/ppermute | solution.py:39
  21.8 7.4 %collective-permute-start.14 = (bf16[64,1152]{1,0:T(8,128)(2,1)S(1)}, bf16[64,1152]{1,0:T(8,128)(2,1)S(1)}, u32[]{:S(2)}, u32[]{:S(2)}) collective-permute-start(bf16[64,1152]{1,0:T(8,128)(2,1)S(1)} %collective-permute-done.13.refs_10_), channel_id=1, source_target_pairs={{0,3},{1,2},{4,1},{5,0},{8,5},{9,4},{12,9},{13,8},{14,13},{15,12},... | collective-permute-start | bytes 442376 | tf_op jit(solution)/shard_map/ppermute | solution.py:39
  22.7 7.3 %collective-permute-start.8 = (bf16[64,1152]{1,0:T(8,128)(2,1)S(1)}, bf16[64,1152]{1,0:T(8,128)(2,1)S(1)}, u32[]{:S(2)}, u32[]{:S(2)}) collective-permute-start(bf16[64,1152]{1,0:T(8,128)(2,1)S(1)} %collective-permute-done.7.refs_2_), channel_id=1, source_target_pairs={{0,5},{1,4},{4,9},{5,8},{8,13},{9,12},{12,15},{13,14},{14,11},{15,... | collective-permute-start | bytes 442376 | tf_op jit(solution)/shard_map/ppermute | solution.py:39
  24.9 6.0 %collective-permute-start.4 = (bf16[64,1152]{1,0:T(8,128)(2,1)S(1)}, bf16[64,1152]{1,0:T(8,128)(2,1)S(1)}, u32[]{:S(2)}, u32[]{:S(2)}) collective-permute-start(bf16[64,1152]{1,0:T(8,128)(2,1)S(1)} %collective-permute-done.3.refs_5_), channel_id=1, source_target_pairs={{0,3},{1,2},{4,1},{5,0},{8,5},{9,4},{12,9},{13,8},{14,13},{15,12},... | collective-permute-start | bytes 442376 | tf_op jit(solution)/shard_map/ppermute | solution.py:39
  31.3 25.5 %copy-start.1 = (bf16[8,4096]{1,0:T(8,128)(2,1)S(1)}, bf16[8,4096]{1,0:T(8,128)(2,1)}, u32[]{:S(2)}) copy-start(bf16[8,4096]{1,0:T(8,128)(2,1)} %queries.1) | copy-start | bytes 196612
  31.3 1.4 %collective-permute-start.15 = (f32[256,128]{1,0:T(8,128)S(1)}, f32[256,128]{1,0:T(8,128)S(1)}, u32[]{:S(2)}, u32[]{:S(2)}) collective-permute-start(f32[256,128]{1,0:T(8,128)S(1)} %shard_map.69), channel_id=1, source_target_pairs={{0,1},{1,0},{2,3},{3,2},{4,5},{5,4},{6,7},{7,6},{8,9},{9,8},{10,11... | collective-permute-start | bytes 393224 | tf_op jit(solution)/shard_map/ppermute | solution.py:43
  33.1 3.7 %collective-permute-start.16 = (f32[32,128]{1,0:T(8,128)S(1)}, f32[32,128]{1,0:T(8,128)S(1)}, u32[]{:S(2)}, u32[]{:S(2)}) collective-permute-start(f32[32,128]{1,0:T(8,128)S(1)} %reshape.11), channel_id=1, source_target_pairs={{0,2},{1,3},{2,0},{3,1},{4,6},{5,7},{6,4},{7,5},{8,10},{9,11},{10,... | collective-permute-start | bytes 49160 | tf_op jit(solution)/shard_map/ppermute | solution.py:43
  34.5 3.7 %collective-permute-start.17 = (f32[32,128]{1,0:T(8,128)S(1)}, f32[32,128]{1,0:T(8,128)S(1)}, u32[]{:S(2)}, u32[]{:S(2)}) collective-permute-start(f32[32,128]{1,0:T(8,128)S(1)} %reshape.11), channel_id=1, source_target_pairs={{0,4},{1,5},{2,6},{3,7},{4,0},{5,1},{6,2},{7,3},{8,12},{9,13},{10,... | collective-permute-start | bytes 49160 | tf_op jit(solution)/shard_map/ppermute | solution.py:43
  36.0 4.6 %collective-permute-start.18 = (f32[32,128]{1,0:T(8,128)S(1)}, f32[32,128]{1,0:T(8,128)S(1)}, u32[]{:S(2)}, u32[]{:S(2)}) collective-permute-start(f32[32,128]{1,0:T(8,128)S(1)} %reshape.11), channel_id=1, source_target_pairs={{0,6},{1,7},{2,4},{3,5},{4,2},{5,3},{6,0},{7,1},{8,14},{9,15},{10,... | collective-permute-start | bytes 49160 | tf_op jit(solution)/shard_map/ppermute | solution.py:43
  40.6 4.6 %collective-permute-start.19 = (bf16[1,32,128]{2,1,0:T(8,128)(2,1)S(1)}, bf16[1,32,128]{2,1,0:T(8,128)(2,1)S(1)}, u32[]{:S(2)}, u32[]{:S(2)}) collective-permute-start(bf16[1,32,128]{2,1,0:T(8,128)(2,1)S(1)} %bitcast.17), channel_id=1, source_target_pairs={{0,8},{1,9},{2,10},{3,11},{4,12},{5,13},{6,14},{7,15},{8,0},{9,1},... | collective-permute-start | bytes 24584 | tf_op jit(solution)/shard_map/ppermute | solution.py:43

commit v14 on v12

--- a/solution.py
+++ b/solution.py
@@ -47,21 +47,17 @@
     return (chip ^ (chip >> 1)) & 1
 
 
-def column_copies(chips, core, act, grad, out, sems):
-    ring_of = core ^ odd(lax.axis_index("dp") >> 1)
-    a_width = act.shape[1] // (2 * chips)
-    g_width = grad.shape[1] // (2 * chips)
-    copies = []
-    for chip in range(chips):
-        block = 2 * chip + (ring_of ^ odd(chip))
-        for k, (ref, at, width) in enumerate(((act, 0, a_width), (grad, a_width, g_width))):
-            columns = pl.ds(pl.multiple_of(block * width, 128), width)
-            copies.append(
-                pltpu.make_async_copy(
-                    ref.at[:, columns], out.at[chip, :, pl.ds(at, width)], sems.at[chip, k]
-                )
-            )
-    return copies
+def column_copies(chip, ring_core, act, grad, out, sems, chips):
+    block = 2 * chip + (ring_core ^ odd(lax.axis_index("dp") >> 1) ^ odd(chip))
+    a_width, g_width = (x.shape[1] // (2 * chips) for x in (act, grad))
+    return [
+        pltpu.make_async_copy(
+            ref.at[:, pl.ds(pl.multiple_of(block * width, 128), width)],
+            out.at[:, pl.ds(at, width)],
+            sems.at[k],
+        )
+        for k, (ref, at, width) in enumerate(((act, 0, a_width), (grad, a_width, g_width)))
+    ]
 
 
 def run_copies(copies):
@@ -81,7 +77,9 @@
         (out_rows.at[:, pl.ds(cut - a_width, second.shape[1])], second),
     ]
     copies = [pltpu.make_async_copy(*pair, sems.at[i]) for i, pair in enumerate(pairs)]
-    run_copies(copies + column_copies(chips, 1 - core, act, grad, send, send_sems))
+    for chip in range(chips):
+        copies += column_copies(chip, 1 - core, act, grad, send.at[chip], send_sems.at[chip], chips)
+    run_copies(copies)
 
 
 def start(act, grad, in_rows, out_rows, chips):
@@ -102,61 +100,90 @@
     )(*held(pltpu.HBM, act, grad, in_rows, out_rows))
 
 
-def keep_kernel(chips, act, grad, keep, sems):
+def add_products(sums, mine, theirs, part, chunk, a_width, cut):
+    a_sum, g_sum = sums
+
+    def tokens(first, last):
+        return jnp.concatenate([ref[:, first:last] for ref in (mine, theirs)], axis=0)
+
+    if part == 0:
+        a_sum += dot(tokens(0, a_width), chunk[:, :a_width], NT)
+        g_sum += dot(tokens(a_width, cut), chunk[:, a_width:], NT)
+    else:
+        g_sum += dot(tokens(cut, mine.shape[1]), chunk[...], NT)
+    return a_sum, g_sum
+
+
+def near_kernel(chips, offsets, later, a_width, act, grad, theirs, *refs):
+    chunks, (out, rest, buf, sems) = refs[:-4], refs[-4:]
+    rank, cut = chunks[0].shape
     core = lax.axis_index("dp") & 1
-    run_copies(column_copies(chips, core, act, grad, keep, sems))
-
-
-def keep_columns(act, grad, chips):
-    rows, width = act.shape[0], (act.shape[1] + grad.shape[1]) // (2 * chips)
+    where = [chip_behind(offset, chips) for offset in offsets + later]
+    spaces = [buf.at[i] for i in range(len(offsets))] + [rest.at[i] for i in range(len(later))]
+    copies = [
+        column_copies(chip, core, act, grad, space, sems.at[i], chips)
+        for i, (chip, space) in enumerate(zip(where, spaces))
+    ]
+    for pair in copies:
+        for copy in pair:
+            copy.start()
+    sums = (jnp.zeros((out.shape[0], rank), jnp.float32),) * 2
+    for i in range(len(offsets)):
+        for copy in copies[i]:
+            copy.wait()
+        for part in range(2):
+            chunk = chunks[2 * i + part]
+            sums = add_products(sums, spaces[i], theirs.at[where[i]], part, chunk, a_width, cut)
+    out[:, :rank], out[:, rank:] = sums
+    for pair in copies[len(offsets) :]:
+        for copy in pair:
+            copy.wait()
+
+
+def near_products(act, grad, theirs, blocks, offsets, later, a_width):
+    chips, rows, width = theirs.shape
+    rank = blocks[0][0].shape[0]
+    flat = [x for block in blocks for x in block]
+    count = len(offsets)
     return pl.pallas_call(
-        functools.partial(keep_kernel, chips),
-        out_shape=pltpu.VMEM((chips, rows, width), act.dtype),
-        in_specs=[HBM] * 2,
-        out_specs=VMEM,
-        scratch_shapes=[pltpu.SemaphoreType.DMA((chips, 2))],
+        functools.partial(near_kernel, chips, offsets, later, a_width),
+        out_shape=(
+            pltpu.VMEM((2 * rows, 2 * rank), jnp.float32),
+            pltpu.VMEM((len(later), rows, width), act.dtype),
+        ),
+        in_specs=[HBM] * 2 + [VMEM] * (1 + len(flat)),
+        out_specs=(VMEM, VMEM),
+        scratch_shapes=[
+            pltpu.VMEM((count, rows, width), act.dtype),
+            pltpu.SemaphoreType.DMA((count + len(later), 2)),
+        ],
         compiler_params=pltpu.CompilerParams(vmem_limit_bytes=16 * 2**20),
         cost_estimate=pl.CostEstimate(
-            flops=0, bytes_accessed=4 * chips * rows * width, transcendentals=0
-        ),
-    )(*held(pltpu.HBM, act, grad))
-
-
-def project_kernel(chips, offsets, parts, a_width, cut, carry, *refs):
-    keep, theirs = refs[:2]
-    chunks, refs = refs[2 : 2 + len(parts)], refs[2 + len(parts) :]
-    out = refs[-1]
+            flops=4 * count * rows * rank * width,
+            bytes_accessed=2 * (chips * rows + count * (rows + rank)) * width,
+            transcendentals=0,
+        ),
+    )(*held(pltpu.HBM, act, grad), *held(pltpu.VMEM, theirs, *flat))
+
+
+def later_kernel(chips, items, a_width, cut, rest, theirs, *refs):
+    chunks, (carried, out) = refs[:-2], refs[-2:]
     rank = chunks[0].shape[0]
-    width = keep.shape[2]
-    if carry:
-        a_sum, g_sum = refs[0][:, :rank], refs[0][:, rank:]
-    else:
-        a_sum = g_sum = jnp.zeros((out.shape[0], rank), jnp.float32)
-    for offset, part, chunk in zip(offsets, parts, chunks):
+    sums = carried[:, :rank], carried[:, rank:]
+    for (offset, place, part), chunk in zip(items, chunks):
         chip = chip_behind(offset, chips)
-
-        def tokens(first, last):
-            return jnp.concatenate([ref[chip, :, first:last] for ref in (keep, theirs)], axis=0)
-
-        if part == 0:
-            a_sum += dot(tokens(0, a_width), chunk[:, :a_width], NT)
-            g_sum += dot(tokens(a_width, cut), chunk[:, a_width:], NT)
-        else:
-            g_sum += dot(tokens(cut, width), chunk[...], NT)
-    out[:, :rank] = a_sum
-    out[:, rank:] = g_sum
-
-
-def project(tokens, chunks, a_width, cut, carry=None):
-    chips, rows, width = tokens[0].shape
-    offsets, parts, flat = zip(*chunks)
-    rank = flat[0].shape[0]
-    carried = () if carry is None else (carry,)
-    columns = sum(x.shape[1] for x in flat)
+        sums = add_products(sums, rest.at[place], theirs.at[chip], part, chunk, a_width, cut)
+    out[:, :rank], out[:, rank:] = sums
+
+
+def later_products(rest, theirs, items, chunks, a_width, cut, total):
+    chips, rows, _ = theirs.shape
+    rank = chunks[0].shape[0]
+    columns = sum(x.shape[1] for x in chunks)
     return pl.pallas_call(
-        functools.partial(project_kernel, chips, offsets, parts, a_width, cut, carry is not None),
-        out_shape=pltpu.VMEM((2 * rows, 2 * rank), jnp.float32),
-        in_specs=[VMEM] * (2 + len(flat) + len(carried)),
+        functools.partial(later_kernel, chips, items, a_width, cut),
+        out_shape=pltpu.VMEM(total.shape, total.dtype),
+        in_specs=[VMEM] * (3 + len(chunks)),
         out_specs=VMEM,
         compiler_params=pltpu.CompilerParams(vmem_limit_bytes=16 * 2**20),
         cost_estimate=pl.CostEstimate(
@@ -164,7 +191,7 @@
             bytes_accessed=(2 * rows + rank) * columns * 2,
             transcendentals=0,
         ),
-    )(*held(pltpu.VMEM, *tokens, *flat, *carried))
+    )(*held(pltpu.VMEM, rest, theirs, *chunks, total))
 
 
 def score_kernel(scale, conditioned, queries, out):
@@ -205,21 +232,20 @@
         down.append([ring(x, -1, chips) for x in down[-1]])
     last = chips // 2 - 1
     far = (ring(up[last][0], 1, chips), ring(down[last][1], -1, chips))
-    keep = keep_columns(activations, out_grads, chips)
-
-    cut = own[0].shape[1]
-    run = functools.partial(project, (keep, theirs), a_width=a_width, cut=cut)
-
-    def both(block, offset):
-        return [(offset, part, x) for part, x in enumerate(block)]
-
-    near = both(own, 0)
+
+    near, offsets = [own], [0]
     for i in range(1, last):
-        near += both(up[i], i) + both(down[i], -i)
-    total = run(near)
-    total = run(both(up[last], last) + both(down[last], -last), carry=total)
-    for part, x in enumerate(far):
-        total = run([(chips // 2, part, x)], carry=total)
+        near += [up[i], down[i]]
+        offsets += [i, -i]
+    later = [last, -last, chips // 2]
+    total, rest = near_products(
+        activations, out_grads, theirs, near, offsets, later, a_width
+    )
+    add = functools.partial(later_products, rest, theirs, a_width=a_width, cut=own[0].shape[1])
+    items = [(offset, place, part) for place, offset in enumerate(later) for part in range(2)]
+    total = add(items[:4], [*up[last], *down[last]], total=total)
+    for item, chunk in zip(items[4:], far):
+        total = add([item], [chunk], total=total)
     theirs = swap(total, 1, n)
     total = (total + jnp.concatenate([theirs[rows:], theirs[:rows]], axis=0)).astype(jnp.bfloat16)
 

time: 57.1 us -> 56.6 us (level)
  blocking collectives: 22.4 us -> 21.8 us
    pallas_call x5 -> x4, Pallas kernels: 5.8 us -> 5.33 us  [the longest x1 3.77 us: near_products(): pl.pallas_call(functools.partial(near_kernel, chips, offsets, later, a_wi...]
  transfers between devices with their start and end apart: 16 -> 16, of which waited for: 7 -> 7; matrix products, arithmetic and copies ran while one was open for 0% -> 0% of each run, Pallas kernels for 10% -> 9%
where the time goes in v14:
time: 56.6 us; the launch traced here: 56.4 us
  blocking collectives  21.8 us (39%)
  starting transfers between devices  16.1 us (28%)
  Pallas kernels  8.8 us (16%)
  waiting for transfers between devices  8.42 us (15%)
  matrix products  0.89 us (2%)
    all_to_all x2, blocking collectives, to_all(): lax.all_to_all(copies, 'dp', 0, 0, axis_index_groups=groups, tiled=True)  21.8 us
    ppermute x14, starting transfers between devices, ring(): return lax.ppermute(x, 'dp', pairs)  15.4 us
    ppermute x14, waiting for transfers between devices, ring(): return lax.ppermute(x, 'dp', pairs)  7.18 us
    pallas_call x1, Pallas kernels, near_products(): pl.pallas_call(functools.partial(near_kernel, chips, offsets, later, a_wi...  3.77 us
    pallas_call x1, Pallas kernels, start(): pl.pallas_call(functools.partial(start_kernel, chips), out_shape=[pltpu.V...  2.74 us
    pallas_call x3, Pallas kernels, later_products(): pl.pallas_call(functools.partial(later_kernel, chips, items, a_width, cut...  1.56 us
    ppermute x2, waiting for transfers between devices, swap(): return lax.ppermute(x, 'dp', [(i, i ^ bit) for i in range(n)])  1.24 us
  transfers between devices with their start and end apart: 16, of which 7 were waited for; matrix products, arithmetic and copies ran while one was open for 0% of the time, Pallas kernels for 9%

profile of v14, /device:TPU:0, one launch (start us, length us, event | category | flops | bytes accessed | tf_op | source)
XLA Modules:
  0.0 56.4 jit_solution(7681438572357840396)
XLA Ops:
  0.0 2.7 %shard_map.64 = (bf16[64,1152]{1,0:T(8,128)(2,1)S(1)}, bf16[64,1152]{1,0:T(8,128)(2,1)S(1)}, bf16[8,128,2304]{2,1,0:T(8,128)(2,1)S(1)}) custom-call(bf16[128,8192]{1,0:T(8,128)(2,1)} %act.3, bf16[128,28672]{1,0:T(8,128)(2,1)} %grad.3, bf16[64,512]{1,0:T(8,128)(2,1)} %bitcast.12, bf16[64,1792]{1,0:T(8,128)(2,1)} %bitcast.11), custom_call_target="tpu_custom_call" | custom-call | bytes 10027008 | tf_op jit(solution)/shard_map/pallas_call | solution.py:90
  2.8 0.5 collective-permute-start
  3.3 2.7 %collective-permute-start.1 = (bf16[64,1152]{1,0:T(8,128)(2,1)S(1)}, bf16[64,1152]{1,0:T(8,128)(2,1)S(1)}, u32[]{:S(2)}, u32[]{:S(2)}) collective-permute-start(bf16[64,1152]{1,0:T(8,128)(2,1)S(1)} %get-tuple-element.11.refs_0_), channel_id=1, source_target_pairs={{0,5},{1,4},{4,9},{5,8},{8,13},{9,12},{12,15},{13,14},{14,11},{15,... | collective-permute-start | bytes 442376 | tf_op jit(solution)/shard_map/ppermute | solution.py:39
  6.0 1.7 %collective-permute-start.2 = (bf16[64,1152]{1,0:T(8,128)(2,1)S(1)}, bf16[64,1152]{1,0:T(8,128)(2,1)S(1)}, u32[]{:S(2)}, u32[]{:S(2)}) collective-permute-start(bf16[64,1152]{1,0:T(8,128)(2,1)S(1)} %get-tuple-element.12.refs_1_), channel_id=1, source_target_pairs={{0,5},{1,4},{4,9},{5,8},{8,13},{9,12},{12,15},{13,14},{14,11},{15,... | collective-permute-start | bytes 442376 | tf_op jit(solution)/shard_map/ppermute | solution.py:39
  7.7 2.4 %collective-permute-done.1.refs_2_ = bf16[64,1152]{1,0:T(8,128)(2,1)S(1)} collective-permute-done((bf16[64,1152]{1,0:T(8,128)(2,1)S(1)}, bf16[64,1152]{1,0:T(8,128)(2,1)S(1)}, u32[]{:S(2)}, u32[]{:S(2)}) %collective-permute-start.1) | collective-permute-done | bytes 147488 | tf_op jit(solution)/shard_map/ppermute | solution.py:39
  10.1 2.2 %collective-permute-start.5 = (bf16[64,1152]{1,0:T(8,128)(2,1)S(1)}, bf16[64,1152]{1,0:T(8,128)(2,1)S(1)}, u32[]{:S(2)}, u32[]{:S(2)}) collective-permute-start(bf16[64,1152]{1,0:T(8,128)(2,1)S(1)} %collective-permute-done.1.refs_2_), channel_id=1, source_target_pairs={{0,5},{1,4},{4,9},{5,8},{8,13},{9,12},{12,15},{13,14},{14,11},{15,... | collective-permute-start | bytes 442376 | tf_op jit(solution)/shard_map/ppermute | solution.py:39
  12.4 0.9 %collective-permute-done.2.refs_3_ = bf16[64,1152]{1,0:T(8,128)(2,1)S(1)} collective-permute-done((bf16[64,1152]{1,0:T(8,128)(2,1)S(1)}, bf16[64,1152]{1,0:T(8,128)(2,1)S(1)}, u32[]{:S(2)}, u32[]{:S(2)}) %collective-permute-start.2) | collective-permute-done | bytes 147488 | tf_op jit(solution)/shard_map/ppermute | solution.py:39
  13.2 2.2 %collective-permute-start.6 = (bf16[64,1152]{1,0:T(8,128)(2,1)S(1)}, bf16[64,1152]{1,0:T(8,128)(2,1)S(1)}, u32[]{:S(2)}, u32[]{:S(2)}) collective-permute-start(bf16[64,1152]{1,0:T(8,128)(2,1)S(1)} %collective-permute-done.2.refs_3_), channel_id=1, source_target_pairs={{0,5},{1,4},{4,9},{5,8},{8,13},{9,12},{12,15},{13,14},{14,11},{15,... | collective-permute-start | bytes 442376 | tf_op jit(solution)/shard_map/ppermute | solution.py:39
  15.4 1.1 %collective-permute-done.5.refs_6_ = bf16[64,1152]{1,0:T(8,128)(2,1)S(1)} collective-permute-done((bf16[64,1152]{1,0:T(8,128)(2,1)S(1)}, bf16[64,1152]{1,0:T(8,128)(2,1)S(1)}, u32[]{:S(2)}, u32[]{:S(2)}) %collective-permute-start.5) | collective-permute-done | bytes 147488 | tf_op jit(solution)/shard_map/ppermute | solution.py:39
  16.5 2.2 %collective-permute-start.11 = (bf16[64,1152]{1,0:T(8,128)(2,1)S(1)}, bf16[64,1152]{1,0:T(8,128)(2,1)S(1)}, u32[]{:S(2)}, u32[]{:S(2)}) collective-permute-start(bf16[64,1152]{1,0:T(8,128)(2,1)S(1)} %collective-permute-done.5.refs_6_), channel_id=1, source_target_pairs={{0,5},{1,4},{4,9},{5,8},{8,13},{9,12},{12,15},{13,14},{14,11},{15,... | collective-permute-start | bytes 442376 | tf_op jit(solution)/shard_map/ppermute | solution.py:39
  18.7 0.9 %collective-permute-done.6.refs_7_ = bf16[64,1152]{1,0:T(8,128)(2,1)S(1)} collective-permute-done((bf16[64,1152]{1,0:T(8,128)(2,1)S(1)}, bf16[64,1152]{1,0:T(8,128)(2,1)S(1)}, u32[]{:S(2)}, u32[]{:S(2)}) %collective-permute-start.6) | collective-permute-done | bytes 147488 | tf_op jit(solution)/shard_map/ppermute | solution.py:39
  19.5 2.2 %collective-permute-start.13 = (bf16[64,1152]{1,0:T(8,128)(2,1)S(1)}, bf16[64,1152]{1,0:T(8,128)(2,1)S(1)}, u32[]{:S(2)}, u32[]{:S(2)}) collective-permute-start(bf16[64,1152]{1,0:T(8,128)(2,1)S(1)} %collective-permute-done.6.refs_7_), channel_id=1, source_target_pairs={{0,5},{1,4},{4,9},{5,8},{8,13},{9,12},{12,15},{13,14},{14,11},{15,... | collective-permute-start | bytes 442376 | tf_op jit(solution)/shard_map/ppermute | solution.py:39
  21.8 1.0 %collective-permute-done.11.refs_0_ = bf16[64,1152]{1,0:T(8,128)(2,1)S(1)} collective-permute-done((bf16[64,1152]{1,0:T(8,128)(2,1)S(1)}, bf16[64,1152]{1,0:T(8,128)(2,1)S(1)}, u32[]{:S(2)}, u32[]{:S(2)}) %collective-permute-start.11) | collective-permute-done | bytes 147488 | tf_op jit(solution)/shard_map/ppermute | solution.py:39
  22.7 2.2 %collective-permute-start.12 = (bf16[64,1152]{1,0:T(8,128)(2,1)S(1)}, bf16[64,1152]{1,0:T(8,128)(2,1)S(1)}, u32[]{:S(2)}, u32[]{:S(2)}) collective-permute-start(bf16[64,1152]{1,0:T(8,128)(2,1)S(1)} %collective-permute-done.11.refs_0_), channel_id=1, source_target_pairs={{0,5},{1,4},{4,9},{5,8},{8,13},{9,12},{12,15},{13,14},{14,11},{15,... | collective-permute-start | bytes 442376 | tf_op jit(solution)/shard_map/ppermute | solution.py:39
  24.9 3.8 %shard_map.65 = (f32[256,128]{1,0:T(8,128)S(1)}, bf16[3,128,2304]{2,1,0:T(8,128)(2,1)S(1)}) custom-call(bf16[128,8192]{1,0:T(8,128)(2,1)} %act.3, bf16[128,28672]{1,0:T(8,128)(2,1)} %grad.3, bf16[8,128,2304]{2,1,0:T(8,128)(2,1)S(1)} %collective-permute-done.theirs, bf16[64,1152]{1,0:T(8,128)(2,1)S(1)} %get-tuple-element.11.refs_0_, ...), custom_call_target="tpu_custom_call" | custom-call | flops 377487360 | bytes 9142272 | tf_op jit(solution)/shard_map/pallas_call | solution.py:148
  28.7 0.8 %shard_map.66.refs_1_ = f32[256,128]{1,0:T(8,128)S(1)} custom-call(bf16[3,128,2304]{2,1,0:T(8,128)(2,1)S(1)} %get-tuple-element.13.rest, bf16[8,128,2304]{2,1,0:T(8,128)(2,1)S(1)} %collective-permute-done.theirs, bf16[64,1152]{1,0:T(8,128)(2,1)S(1)} %collective-permute-done.11.refs_0_, bf16[64,1152]{1,0:T(8,128)(2,1)S(1)} %collective-permute-done.13.refs_1_, ...), custom_call_target="tpu_custom_call" | custom-call | flops 150994944 | bytes 2949120 | tf_op jit(solution)/shard_map/pallas_call | solution.py:183
  29.6 0.4 shard_map.67.refs_1_
  29.9 1.0 %collective-permute-done.10.refs_0_ = bf16[64,1152]{1,0:T(8,128)(2,1)S(1)} collective-permute-done((bf16[64,1152]{1,0:T(8,128)(2,1)S(1)}, bf16[64,1152]{1,0:T(8,128)(2,1)S(1)}, u32[]{:S(2)}, u32[]{:S(2)}) %collective-permute-start.10) | collective-permute-done | bytes 147488 | tf_op jit(solution)/shard_map/ppermute | solution.py:39
  30.9 0.4 shard_map.68
  31.5 1.2 %collective-permute-done.15 = f32[256,128]{1,0:T(8,128)S(1)} collective-permute-done((f32[256,128]{1,0:T(8,128)S(1)}, f32[256,128]{1,0:T(8,128)S(1)}, u32[]{:S(2)}, u32[]{:S(2)}) %collective-permute-start.15) | collective-permute-done | bytes 131104 | tf_op jit(solution)/shard_map/ppermute | solution.py:43
  33.1 12.7 %all_to_all.10 = f32[8,32,128]{2,1,0:T(8,128)S(1)} all-to-all(f32[8,32,128]{2,1,0:T(8,128)S(1)} %broadcast_in_dim.14), channel_id=1, replica_groups={{0,2,4,6,8,10,12,14},{1,3,5,7,9,11,13,15},{16,18,20,22,24,26,28,30},{17..., dimensions={0} | all-to-all | bytes 262144 | tf_op jit(solution)/shard_map/all_to_all | solution.py:217
  45.8 0.6 %convolution_convert_fusion = bf16[2,256]{1,0:T(2,128)(2,1)S(1)} fusion(bf16[256,4096]{1,0:T(8,128)(2,1)S(1)} %copy-done, bf16[1,2,32,128]{3,2,1,0:T(8,128)(2,1)S(1)} %bitcast.13), kind=kOutput, calls=%fused_computation.1 | convolution fusion | flops 4194816 | bytes 2114560 | tf_op jit(solution)/shard_map/dot_general | solution.py:23
  46.5 9.1 %all_to_all.11.conditioned = bf16[16,2,256]{2,1,0:T(2,128)(2,1)S(1)} all-to-all(bf16[16,2,256]{2,1,0:T(2,128)(2,1)S(1)} %broadcast_in_dim.15), channel_id=1, replica_groups={{0,1,2,3,4,5,6,7,8,9,10,11,12,13,14,15},{16,17,18,19,20,21,22,23,24,25,..., dimensions={0} | all-to-all | bytes 32768 | tf_op jit(solution)/shard_map/all_to_all | solution.py:217
  55.6 0.7 %shard_map.69 = f32[2,8]{1,0:T(2,128)} custom-call(bf16[16,2,256]{2,1,0:T(2,128)(2,1)S(1)} %all_to_all.11.conditioned, bf16[8,4096]{1,0:T(8,128)(2,1)S(1)} %copy-done.1), custom_call_target="tpu_custom_call" | custom-call | tf_op jit(solution)/shard_map/pallas_call | solution.py:206
  (28 shorter events, 0.7 us)
Async XLA Ops:
  0.0 45.8 %copy-start = (bf16[256,4096]{1,0:T(8,128)(2,1)S(1)}, bf16[256,4096]{1,0:T(8,128)(2,1)}, u32[]{:S(2)}) copy-start(bf16[256,4096]{1,0:T(8,128)(2,1)} %param.10) | copy-start | bytes 6291460
  2.8 22.2 %collective-permute-start = (bf16[8,128,2304]{2,1,0:T(8,128)(2,1)S(1)}, bf16[8,128,2304]{2,1,0:T(8,128)(2,1)S(1)}, u32[]{:S(2)}, u32[]{:S(2)}) collective-permute-start(bf16[8,128,2304]{2,1,0:T(8,128)(2,1)S(1)} %get-tuple-element.10), channel_id=1, source_target_pairs={{0,1},{1,0},{2,3},{3,2},{4,5},{5,4},{6,7},{7,6},{8,9},{9,8},{10,11... | collective-permute-start | bytes 14155784 | tf_op jit(solution)/shard_map/ppermute | solution.py:43
  3.3 6.9 %collective-permute-start.1 = (bf16[64,1152]{1,0:T(8,128)(2,1)S(1)}, bf16[64,1152]{1,0:T(8,128)(2,1)S(1)}, u32[]{:S(2)}, u32[]{:S(2)}) collective-permute-start(bf16[64,1152]{1,0:T(8,128)(2,1)S(1)} %get-tuple-element.11.refs_0_), channel_id=1, source_target_pairs={{0,5},{1,4},{4,9},{5,8},{8,13},{9,12},{12,15},{13,14},{14,11},{15,... | collective-permute-start | bytes 442376 | tf_op jit(solution)/shard_map/ppermute | solution.py:39
  6.0 6.4 %collective-permute-start.4 = (bf16[64,1152]{1,0:T(8,128)(2,1)S(1)}, bf16[64,1152]{1,0:T(8,128)(2,1)S(1)}, u32[]{:S(2)}, u32[]{:S(2)}) collective-permute-start(bf16[64,1152]{1,0:T(8,128)(2,1)S(1)} %get-tuple-element.12.refs_1_), channel_id=1, source_target_pairs={{0,3},{1,2},{4,1},{5,0},{8,5},{9,4},{12,9},{13,8},{14,13},{15,12},... | collective-permute-start | bytes 442376 | tf_op jit(solution)/shard_map/ppermute | solution.py:39
  6.0 7.3 %collective-permute-start.2 = (bf16[64,1152]{1,0:T(8,128)(2,1)S(1)}, bf16[64,1152]{1,0:T(8,128)(2,1)S(1)}, u32[]{:S(2)}, u32[]{:S(2)}) collective-permute-start(bf16[64,1152]{1,0:T(8,128)(2,1)S(1)} %get-tuple-element.12.refs_1_), channel_id=1, source_target_pairs={{0,5},{1,4},{4,9},{5,8},{8,13},{9,12},{12,15},{13,14},{14,11},{15,... | collective-permute-start | bytes 442376 | tf_op jit(solution)/shard_map/ppermute | solution.py:39
  7.7 7.7 %collective-permute-start.3 = (bf16[64,1152]{1,0:T(8,128)(2,1)S(1)}, bf16[64,1152]{1,0:T(8,128)(2,1)S(1)}, u32[]{:S(2)}, u32[]{:S(2)}) collective-permute-start(bf16[64,1152]{1,0:T(8,128)(2,1)S(1)} %get-tuple-element.11.refs_0_), channel_id=1, source_target_pairs={{0,3},{1,2},{4,1},{5,0},{8,5},{9,4},{12,9},{13,8},{14,13},{15,12},... | collective-permute-start | bytes 442376 | tf_op jit(solution)/shard_map/ppermute | solution.py:39
  10.1 6.3 %collective-permute-start.5 = (bf16[64,1152]{1,0:T(8,128)(2,1)S(1)}, bf16[64,1152]{1,0:T(8,128)(2,1)S(1)}, u32[]{:S(2)}, u32[]{:S(2)}) collective-permute-start(bf16[64,1152]{1,0:T(8,128)(2,1)S(1)} %collective-permute-done.1.refs_2_), channel_id=1, source_target_pairs={{0,5},{1,4},{4,9},{5,8},{8,13},{9,12},{12,15},{13,14},{14,11},{15,... | collective-permute-start | bytes 442376 | tf_op jit(solution)/shard_map/ppermute | solution.py:39
  12.3 6.3 %collective-permute-start.8 = (bf16[64,1152]{1,0:T(8,128)(2,1)S(1)}, bf16[64,1152]{1,0:T(8,128)(2,1)S(1)}, u32[]{:S(2)}, u32[]{:S(2)}) collective-permute-start(bf16[64,1152]{1,0:T(8,128)(2,1)S(1)} %collective-permute-done.4.refs_5_), channel_id=1, source_target_pairs={{0,3},{1,2},{4,1},{5,0},{8,5},{9,4},{12,9},{13,8},{14,13},{15,12},... | collective-permute-start | bytes 442376 | tf_op jit(solution)/shard_map/ppermute | solution.py:39
  13.2 6.3 %collective-permute-start.6 = (bf16[64,1152]{1,0:T(8,128)(2,1)S(1)}, bf16[64,1152]{1,0:T(8,128)(2,1)S(1)}, u32[]{:S(2)}, u32[]{:S(2)}) collective-permute-start(bf16[64,1152]{1,0:T(8,128)(2,1)S(1)} %collective-permute-done.2.refs_3_), channel_id=1, source_target_pairs={{0,5},{1,4},{4,9},{5,8},{8,13},{9,12},{12,15},{13,14},{14,11},{15,... | collective-permute-start | bytes 442376 | tf_op jit(solution)/shard_map/ppermute | solution.py:39
  15.4 6.4 %collective-permute-start.7 = (bf16[64,1152]{1,0:T(8,128)(2,1)S(1)}, bf16[64,1152]{1,0:T(8,128)(2,1)S(1)}, u32[]{:S(2)}, u32[]{:S(2)}) collective-permute-start(bf16[64,1152]{1,0:T(8,128)(2,1)S(1)} %collective-permute-done.3.refs_4_), channel_id=1, source_target_pairs={{0,3},{1,2},{4,1},{5,0},{8,5},{9,4},{12,9},{13,8},{14,13},{15,12},... | collective-permute-start | bytes 442376 | tf_op jit(solution)/shard_map/ppermute | solution.py:39
  16.5 6.3 %collective-permute-start.11 = (bf16[64,1152]{1,0:T(8,128)(2,1)S(1)}, bf16[64,1152]{1,0:T(8,128)(2,1)S(1)}, u32[]{:S(2)}, u32[]{:S(2)}) collective-permute-start(bf16[64,1152]{1,0:T(8,128)(2,1)S(1)} %collective-permute-done.5.refs_6_), channel_id=1, source_target_pairs={{0,5},{1,4},{4,9},{5,8},{8,13},{9,12},{12,15},{13,14},{14,11},{15,... | collective-permute-start | bytes 442376 | tf_op jit(solution)/shard_map/ppermute | solution.py:39
  18.7 6.3 %collective-permute-start.9 = (bf16[64,1152]{1,0:T(8,128)(2,1)S(1)}, bf16[64,1152]{1,0:T(8,128)(2,1)S(1)}, u32[]{:S(2)}, u32[]{:S(2)}) collective-permute-start(bf16[64,1152]{1,0:T(8,128)(2,1)S(1)} %collective-permute-done.8.refs_9_), channel_id=1, source_target_pairs={{0,3},{1,2},{4,1},{5,0},{8,5},{9,4},{12,9},{13,8},{14,13},{15,12},... | collective-permute-start | bytes 442376 | tf_op jit(solution)/shard_map/ppermute | solution.py:39
  19.5 9.2 %collective-permute-start.13 = (bf16[64,1152]{1,0:T(8,128)(2,1)S(1)}, bf16[64,1152]{1,0:T(8,128)(2,1)S(1)}, u32[]{:S(2)}, u32[]{:S(2)}) collective-permute-start(bf16[64,1152]{1,0:T(8,128)(2,1)S(1)} %collective-permute-done.6.refs_7_), channel_id=1, source_target_pairs={{0,5},{1,4},{4,9},{5,8},{8,13},{9,12},{12,15},{13,14},{14,11},{15,... | collective-permute-start | bytes 442376 | tf_op jit(solution)/shard_map/ppermute | solution.py:39
  21.8 7.0 %collective-permute-start.14 = (bf16[64,1152]{1,0:T(8,128)(2,1)S(1)}, bf16[64,1152]{1,0:T(8,128)(2,1)S(1)}, u32[]{:S(2)}, u32[]{:S(2)}) collective-permute-start(bf16[64,1152]{1,0:T(8,128)(2,1)S(1)} %collective-permute-done.7.refs_8_), channel_id=1, source_target_pairs={{0,3},{1,2},{4,1},{5,0},{8,5},{9,4},{12,9},{13,8},{14,13},{15,12},... | collective-permute-start | bytes 442376 | tf_op jit(solution)/shard_map/ppermute | solution.py:39
  22.7 6.8 %collective-permute-start.12 = (bf16[64,1152]{1,0:T(8,128)(2,1)S(1)}, bf16[64,1152]{1,0:T(8,128)(2,1)S(1)}, u32[]{:S(2)}, u32[]{:S(2)}) collective-permute-start(bf16[64,1152]{1,0:T(8,128)(2,1)S(1)} %collective-permute-done.11.refs_0_), channel_id=1, source_target_pairs={{0,5},{1,4},{4,9},{5,8},{8,13},{9,12},{12,15},{13,14},{14,11},{15,... | collective-permute-start | bytes 442376 | tf_op jit(solution)/shard_map/ppermute | solution.py:39
  24.9 6.0 %collective-permute-start.10 = (bf16[64,1152]{1,0:T(8,128)(2,1)S(1)}, bf16[64,1152]{1,0:T(8,128)(2,1)S(1)}, u32[]{:S(2)}, u32[]{:S(2)}) collective-permute-start(bf16[64,1152]{1,0:T(8,128)(2,1)S(1)} %collective-permute-done.9.refs_3_), channel_id=1, source_target_pairs={{0,3},{1,2},{4,1},{5,0},{8,5},{9,4},{12,9},{13,8},{14,13},{15,12},... | collective-permute-start | bytes 442376 | tf_op jit(solution)/shard_map/ppermute | solution.py:39
  31.3 24.4 %copy-start.1 = (bf16[8,4096]{1,0:T(8,128)(2,1)S(1)}, bf16[8,4096]{1,0:T(8,128)(2,1)}, u32[]{:S(2)}) copy-start(bf16[8,4096]{1,0:T(8,128)(2,1)} %queries.1) | copy-start | bytes 196612
  31.3 1.4 %collective-permute-start.15 = (f32[256,128]{1,0:T(8,128)S(1)}, f32[256,128]{1,0:T(8,128)S(1)}, u32[]{:S(2)}, u32[]{:S(2)}) collective-permute-start(f32[256,128]{1,0:T(8,128)S(1)} %shard_map.68), channel_id=1, source_target_pairs={{0,1},{1,0},{2,3},{3,2},{4,5},{5,4},{6,7},{7,6},{8,9},{9,8},{10,11... | collective-permute-start | bytes 393224 | tf_op jit(solution)/shard_map/ppermute | solution.py:43

commit v15 on v14

--- a/solution.py
+++ b/solution.py
@@ -115,11 +115,13 @@
 
 
 def near_kernel(chips, offsets, later, a_width, act, grad, theirs, *refs):
-    chunks, (out, rest, buf, sems) = refs[:-4], refs[-4:]
+    chunks, refs = refs[: 2 * len(offsets)], refs[2 * len(offsets) :]
+    carried = None if later == [] else refs[0]
+    out, *rest, buf, sems = refs[0 if later == [] else 1 :]
     rank, cut = chunks[0].shape
     core = lax.axis_index("dp") & 1
     where = [chip_behind(offset, chips) for offset in offsets + later]
-    spaces = [buf.at[i] for i in range(len(offsets))] + [rest.at[i] for i in range(len(later))]
+    spaces = [buf.at[i] for i in range(len(offsets))] + [rest[0].at[i] for i in range(len(later))]
     copies = [
         column_copies(chip, core, act, grad, space, sems.at[i], chips)
         for i, (chip, space) in enumerate(zip(where, spaces))
@@ -127,7 +129,10 @@
     for pair in copies:
         for copy in pair:
             copy.start()
-    sums = (jnp.zeros((out.shape[0], rank), jnp.float32),) * 2
+    if carried is None:
+        sums = (jnp.zeros((out.shape[0], rank), jnp.float32),) * 2
+    else:
+        sums = carried[:, :rank], carried[:, rank:]
     for i in range(len(offsets)):
         for copy in copies[i]:
             copy.wait()
@@ -140,19 +145,20 @@
             copy.wait()
 
 
-def near_products(act, grad, theirs, blocks, offsets, later, a_width):
+def near_products(act, grad, theirs, blocks, offsets, a_width, total=None, later=()):
     chips, rows, width = theirs.shape
     rank = blocks[0][0].shape[0]
     flat = [x for block in blocks for x in block]
+    carried = [] if total is None else [total]
     count = len(offsets)
+    out_shape = [pltpu.VMEM((2 * rows, 2 * rank), jnp.float32)]
+    if later:
+        out_shape.append(pltpu.VMEM((len(later), rows, width), act.dtype))
     return pl.pallas_call(
-        functools.partial(near_kernel, chips, offsets, later, a_width),
-        out_shape=(
-            pltpu.VMEM((2 * rows, 2 * rank), jnp.float32),
-            pltpu.VMEM((len(later), rows, width), act.dtype),
-        ),
-        in_specs=[HBM] * 2 + [VMEM] * (1 + len(flat)),
-        out_specs=(VMEM, VMEM),
+        functools.partial(near_kernel, chips, offsets, list(later), a_width),
+        out_shape=out_shape,
+        in_specs=[HBM] * 2 + [VMEM] * (1 + len(flat) + len(carried)),
+        out_specs=[VMEM] * len(out_shape),
         scratch_shapes=[
             pltpu.VMEM((count, rows, width), act.dtype),
             pltpu.SemaphoreType.DMA((count + len(later), 2)),
@@ -160,10 +166,10 @@
         compiler_params=pltpu.CompilerParams(vmem_limit_bytes=16 * 2**20),
         cost_estimate=pl.CostEstimate(
             flops=4 * count * rows * rank * width,
-            bytes_accessed=2 * (chips * rows + count * (rows + rank)) * width,
+            bytes_accessed=2 * ((count + len(later)) * rows + count * (rows + rank)) * width,
             transcendentals=0,
         ),
-    )(*held(pltpu.HBM, act, grad), *held(pltpu.VMEM, theirs, *flat))
+    )(*held(pltpu.HBM, act, grad), *held(pltpu.VMEM, theirs, *flat, *carried))
 
 
 def later_kernel(chips, items, a_width, cut, rest, theirs, *refs):
@@ -226,21 +232,23 @@
 
     *own, send = start(activations, out_grads, in_basis.T, out_basis.T, chips)
     theirs = swap(send, 1, n)
+    multiply = functools.partial(near_products, activations, out_grads, theirs, a_width=a_width)
+    last = chips // 2 - 1
     up, down = [own], [own]
-    for _ in range(chips // 2 - 1):
+    for i in range(last):
+        if i == last - 1:
+            (total,) = multiply([own, up[1], down[1]], [0, 1, -1])
+            total, up[i][0] = lax.optimization_barrier((total, up[i][0]))
         up.append([ring(x, 1, chips) for x in up[-1]])
         down.append([ring(x, -1, chips) for x in down[-1]])
-    last = chips // 2 - 1
     far = (ring(up[last][0], 1, chips), ring(down[last][1], -1, chips))
 
-    near, offsets = [own], [0]
-    for i in range(1, last):
+    near, offsets = [], []
+    for i in range(2, last):
         near += [up[i], down[i]]
         offsets += [i, -i]
     later = [last, -last, chips // 2]
-    total, rest = near_products(
-        activations, out_grads, theirs, near, offsets, later, a_width
-    )
+    total, rest = multiply(near, offsets, total=total, later=later)
     add = functools.partial(later_products, rest, theirs, a_width=a_width, cut=own[0].shape[1])
     items = [(offset, place, part) for place, offset in enumerate(later) for part in range(2)]
     total = add(items[:4], [*up[last], *down[last]], total=total)
@@ -291,7 +299,7 @@
     def body(activations, out_grads, in_basis, out_basis, preconditioner, queries):
         aligned = all(x.shape[0] % 128 == 0 for x in (in_basis, out_basis, preconditioner))
         split = LEN // activations.shape[0]
-        regular = aligned and n >= 8 and power_of_two(n) and power_of_two(split) and 4 <= split <= n
+        regular = aligned and n >= 16 and power_of_two(n) and power_of_two(split) and 4 <= split <= n
         form = local if regular else local_gathered
         return form(activations, out_grads, in_basis, out_basis, preconditioner, queries)
 

time: 56.6 us -> 57.4 us (1.014)
  Pallas kernels: 8.8 us -> 10 us
  waiting for transfers between devices: 8.42 us -> 9.41 us
  starting transfers between devices: 16.1 us -> 15.3 us
    pallas_call x1 -> x2, Pallas kernels: 3.77 us -> 5.01 us  [near_products(): pl.pallas_call(functools.partial(near_kernel, chips, offsets, list(later)...]
    ppermute x14, waiting for transfers between devices: 7.18 us -> 8.18 us  [ring(): return lax.ppermute(x, 'dp', pairs)]
    ppermute x14, starting transfers between devices: 15.4 us -> 14.6 us  [ring(): return lax.ppermute(x, 'dp', pairs)]
  transfers between devices with their start and end apart: 16 -> 16, of which waited for: 7 -> 7; matrix products, arithmetic and copies ran while one was open for 0% -> 0% of each run, Pallas kernels for 9% -> 11%
where the time goes in v15:
time: 57.4 us; the launch traced here: 57.2 us
  blocking collectives  21.3 us (37%)
  starting transfers between devices  15.3 us (27%)
  Pallas kernels  10 us (17%)
  waiting for transfers between devices  9.41 us (16%)
  matrix products  0.89 us (2%)
    all_to_all x2, blocking collectives, to_all(): lax.all_to_all(copies, 'dp', 0, 0, axis_index_groups=groups, tiled=True)  21.3 us
    ppermute x14, starting transfers between devices, ring(): return lax.ppermute(x, 'dp', pairs)  14.6 us
    ppermute x14, waiting for transfers between devices, ring(): return lax.ppermute(x, 'dp', pairs)  8.18 us
    pallas_call x2, Pallas kernels, near_products(): pl.pallas_call(functools.partial(near_kernel, chips, offsets, list(later)...  5.01 us
    pallas_call x1, Pallas kernels, start(): pl.pallas_call(functools.partial(start_kernel, chips), out_shape=[pltpu.V...  2.74 us
    pallas_call x3, Pallas kernels, later_products(): pl.pallas_call(functools.partial(later_kernel, chips, items, a_width, cut...  1.55 us
    ppermute x2, waiting for transfers between devices, swap(): return lax.ppermute(x, 'dp', [(i, i ^ bit) for i in range(n)])  1.23 us
  transfers between devices with their start and end apart: 16, of which 7 were waited for; matrix products, arithmetic and copies ran while one was open for 0% of the time, Pallas kernels for 11%

profile of v15, /device:TPU:0, one launch (start us, length us, event | category | flops | bytes accessed | tf_op | source)
XLA Modules:
  0.0 57.2 jit_solution(18131806050378639577)
XLA Ops:
  0.0 2.7 %shard_map.64 = (bf16[64,1152]{1,0:T(8,128)(2,1)S(1)}, bf16[64,1152]{1,0:T(8,128)(2,1)S(1)}, bf16[8,128,2304]{2,1,0:T(8,128)(2,1)S(1)}) custom-call(bf16[128,8192]{1,0:T(8,128)(2,1)} %act.5, bf16[128,28672]{1,0:T(8,128)(2,1)} %grad.5, bf16[64,512]{1,0:T(8,128)(2,1)} %bitcast.12, bf16[64,1792]{1,0:T(8,128)(2,1)} %bitcast.11), custom_call_target="tpu_custom_call" | custom-call | bytes 10027008 | tf_op jit(solution)/shard_map/pallas_call | solution.py:90
  2.8 0.5 collective-permute-start
  3.3 2.7 %collective-permute-start.1 = (bf16[64,1152]{1,0:T(8,128)(2,1)S(1)}, bf16[64,1152]{1,0:T(8,128)(2,1)S(1)}, u32[]{:S(2)}, u32[]{:S(2)}) collective-permute-start(bf16[64,1152]{1,0:T(8,128)(2,1)S(1)} %get-tuple-element.13.refs_0_), channel_id=1, source_target_pairs={{0,5},{1,4},{4,9},{5,8},{8,13},{9,12},{12,15},{13,14},{14,11},{15,... | collective-permute-start | bytes 442376 | tf_op jit(solution)/shard_map/ppermute | solution.py:39
  6.0 1.7 %collective-permute-start.2 = (bf16[64,1152]{1,0:T(8,128)(2,1)S(1)}, bf16[64,1152]{1,0:T(8,128)(2,1)S(1)}, u32[]{:S(2)}, u32[]{:S(2)}) collective-permute-start(bf16[64,1152]{1,0:T(8,128)(2,1)S(1)} %get-tuple-element.14.refs_1_), channel_id=1, source_target_pairs={{0,5},{1,4},{4,9},{5,8},{8,13},{9,12},{12,15},{13,14},{14,11},{15,... | collective-permute-start | bytes 442376 | tf_op jit(solution)/shard_map/ppermute | solution.py:39
  7.7 2.4 %collective-permute-done.1.refs_2_ = bf16[64,1152]{1,0:T(8,128)(2,1)S(1)} collective-permute-done((bf16[64,1152]{1,0:T(8,128)(2,1)S(1)}, bf16[64,1152]{1,0:T(8,128)(2,1)S(1)}, u32[]{:S(2)}, u32[]{:S(2)}) %collective-permute-start.1) | collective-permute-done | bytes 147488 | tf_op jit(solution)/shard_map/ppermute | solution.py:39
  10.1 2.2 %collective-permute-start.5 = (bf16[64,1152]{1,0:T(8,128)(2,1)S(1)}, bf16[64,1152]{1,0:T(8,128)(2,1)S(1)}, u32[]{:S(2)}, u32[]{:S(2)}) collective-permute-start(bf16[64,1152]{1,0:T(8,128)(2,1)S(1)} %collective-permute-done.1.refs_2_), channel_id=1, source_target_pairs={{0,5},{1,4},{4,9},{5,8},{8,13},{9,12},{12,15},{13,14},{14,11},{15,... | collective-permute-start | bytes 442376 | tf_op jit(solution)/shard_map/ppermute | solution.py:39
  12.4 0.9 %collective-permute-done.2.refs_3_ = bf16[64,1152]{1,0:T(8,128)(2,1)S(1)} collective-permute-done((bf16[64,1152]{1,0:T(8,128)(2,1)S(1)}, bf16[64,1152]{1,0:T(8,128)(2,1)S(1)}, u32[]{:S(2)}, u32[]{:S(2)}) %collective-permute-start.2) | collective-permute-done | bytes 147488 | tf_op jit(solution)/shard_map/ppermute | solution.py:39
  13.2 2.2 %collective-permute-start.6 = (bf16[64,1152]{1,0:T(8,128)(2,1)S(1)}, bf16[64,1152]{1,0:T(8,128)(2,1)S(1)}, u32[]{:S(2)}, u32[]{:S(2)}) collective-permute-start(bf16[64,1152]{1,0:T(8,128)(2,1)S(1)} %collective-permute-done.2.refs_3_), channel_id=1, source_target_pairs={{0,5},{1,4},{4,9},{5,8},{8,13},{9,12},{12,15},{13,14},{14,11},{15,... | collective-permute-start | bytes 442376 | tf_op jit(solution)/shard_map/ppermute | solution.py:39
  15.4 2.8 %shard_map.65.refs_4_ = f32[256,128]{1,0:T(8,128)S(1)} custom-call(bf16[128,8192]{1,0:T(8,128)(2,1)} %act.5, bf16[128,28672]{1,0:T(8,128)(2,1)} %grad.5, bf16[8,128,2304]{2,1,0:T(8,128)(2,1)S(1)} %collective-permute-done.theirs, bf16[64,1152]{1,0:T(8,128)(2,1)S(1)} %get-tuple-element.13.refs_0_, bf16[64,1152]{1,0:T(8,128)(2,1)S(1)} %get-tuple-element.14.refs_1_, ...), custom_call_target="tpu_custom_call" | custom-call | flops 226492416 | bytes 4423680 | tf_op jit(solution)/shard_map/pallas_call | solution.py:157
  18.2 1.8 %collective-permute-start.11 = (bf16[64,1152]{1,0:T(8,128)(2,1)S(1)}, bf16[64,1152]{1,0:T(8,128)(2,1)S(1)}, u32[]{:S(2)}, u32[]{:S(2)}) collective-permute-start(bf16[64,1152]{1,0:T(8,128)(2,1)S(1)} %collective-permute-done.5.refs_0_), channel_id=1, source_target_pairs={{0,5},{1,4},{4,9},{5,8},{8,13},{9,12},{12,15},{13,14},{14,11},{15,... | collective-permute-start | bytes 442376 | tf_op jit(solution)/shard_map/ppermute | solution.py:39
  20.0 1.7 %collective-permute-start.13 = (bf16[64,1152]{1,0:T(8,128)(2,1)S(1)}, bf16[64,1152]{1,0:T(8,128)(2,1)S(1)}, u32[]{:S(2)}, u32[]{:S(2)}) collective-permute-start(bf16[64,1152]{1,0:T(8,128)(2,1)S(1)} %collective-permute-done.6.refs_1_), channel_id=1, source_target_pairs={{0,5},{1,4},{4,9},{5,8},{8,13},{9,12},{12,15},{13,14},{14,11},{15,... | collective-permute-start | bytes 442376 | tf_op jit(solution)/shard_map/ppermute | solution.py:39
  21.8 2.4 %collective-permute-done.11.refs_0_ = bf16[64,1152]{1,0:T(8,128)(2,1)S(1)} collective-permute-done((bf16[64,1152]{1,0:T(8,128)(2,1)S(1)}, bf16[64,1152]{1,0:T(8,128)(2,1)S(1)}, u32[]{:S(2)}, u32[]{:S(2)}) %collective-permute-start.11) | collective-permute-done | bytes 147488 | tf_op jit(solution)/shard_map/ppermute | solution.py:39
  24.2 2.1 %collective-permute-start.12 = (bf16[64,1152]{1,0:T(8,128)(2,1)S(1)}, bf16[64,1152]{1,0:T(8,128)(2,1)S(1)}, u32[]{:S(2)}, u32[]{:S(2)}) collective-permute-start(bf16[64,1152]{1,0:T(8,128)(2,1)S(1)} %collective-permute-done.11.refs_0_), channel_id=1, source_target_pairs={{0,5},{1,4},{4,9},{5,8},{8,13},{9,12},{12,15},{13,14},{14,11},{15,... | collective-permute-start | bytes 442376 | tf_op jit(solution)/shard_map/ppermute | solution.py:39
  26.4 2.3 %shard_map.66 = (f32[256,128]{1,0:T(8,128)S(1)}, bf16[3,128,2304]{2,1,0:T(8,128)(2,1)S(1)}) custom-call(bf16[128,8192]{1,0:T(8,128)(2,1)} %act.5, bf16[128,28672]{1,0:T(8,128)(2,1)} %grad.5, bf16[8,128,2304]{2,1,0:T(8,128)(2,1)S(1)} %collective-permute-done.theirs, bf16[64,1152]{1,0:T(8,128)(2,1)S(1)} %collective-permute-done.5.refs_0_, ...), custom_call_target="tpu_custom_call" | custom-call | flops 150994944 | bytes 4718592 | tf_op jit(solution)/shard_map/pallas_call | solution.py:157
  28.6 0.4 collective-permute-done.14.refs_2_
  29.1 0.8 %shard_map.67.refs_1_ = f32[256,128]{1,0:T(8,128)S(1)} custom-call(bf16[3,128,2304]{2,1,0:T(8,128)(2,1)S(1)} %get-tuple-element.17.rest, bf16[8,128,2304]{2,1,0:T(8,128)(2,1)S(1)} %collective-permute-done.theirs, bf16[64,1152]{1,0:T(8,128)(2,1)S(1)} %collective-permute-done.11.refs_0_, bf16[64,1152]{1,0:T(8,128)(2,1)S(1)} %collective-permute-done.13.refs_1_, ...), custom_call_target="tpu_custom_call" | custom-call | flops 150994944 | bytes 2949120 | tf_op jit(solution)/shard_map/pallas_call | solution.py:189
  29.9 0.4 collective-permute-done.12.refs_0_
  30.3 0.4 shard_map.68.refs_1_
  30.7 1.6 %collective-permute-done.10.refs_0_ = bf16[64,1152]{1,0:T(8,128)(2,1)S(1)} collective-permute-done((bf16[64,1152]{1,0:T(8,128)(2,1)S(1)}, bf16[64,1152]{1,0:T(8,128)(2,1)S(1)}, u32[]{:S(2)}, u32[]{:S(2)}) %collective-permute-start.10) | collective-permute-done | bytes 147488 | tf_op jit(solution)/shard_map/ppermute | solution.py:39
  32.8 1.2 %collective-permute-done.15 = f32[256,128]{1,0:T(8,128)S(1)} collective-permute-done((f32[256,128]{1,0:T(8,128)S(1)}, f32[256,128]{1,0:T(8,128)S(1)}, u32[]{:S(2)}, u32[]{:S(2)}) %collective-permute-start.15) | collective-permute-done | bytes 131104 | tf_op jit(solution)/shard_map/ppermute | solution.py:43
  34.4 12.3 %all_to_all.10 = f32[8,32,128]{2,1,0:T(8,128)S(1)} all-to-all(f32[8,32,128]{2,1,0:T(8,128)S(1)} %broadcast_in_dim.14), channel_id=1, replica_groups={{0,2,4,6,8,10,12,14},{1,3,5,7,9,11,13,15},{16,18,20,22,24,26,28,30},{17..., dimensions={0} | all-to-all | bytes 262144 | tf_op jit(solution)/shard_map/all_to_all | solution.py:223
  46.7 0.6 %convolution_convert_fusion = bf16[2,256]{1,0:T(2,128)(2,1)S(1)} fusion(bf16[256,4096]{1,0:T(8,128)(2,1)S(1)} %copy-done, bf16[1,2,32,128]{3,2,1,0:T(8,128)(2,1)S(1)} %bitcast.13), kind=kOutput, calls=%fused_computation.1 | convolution fusion | flops 4194816 | bytes 2114560 | tf_op jit(solution)/shard_map/dot_general | solution.py:23
  47.4 9.1 %all_to_all.11.conditioned = bf16[16,2,256]{2,1,0:T(2,128)(2,1)S(1)} all-to-all(bf16[16,2,256]{2,1,0:T(2,128)(2,1)S(1)} %broadcast_in_dim.15), channel_id=1, replica_groups={{0,1,2,3,4,5,6,7,8,9,10,11,12,13,14,15},{16,17,18,19,20,21,22,23,24,25,..., dimensions={0} | all-to-all | bytes 32768 | tf_op jit(solution)/shard_map/all_to_all | solution.py:223
  56.5 0.7 %shard_map.70 = f32[2,8]{1,0:T(2,128)} custom-call(bf16[16,2,256]{2,1,0:T(2,128)(2,1)S(1)} %all_to_all.11.conditioned, bf16[8,4096]{1,0:T(8,128)(2,1)S(1)} %copy-done.1), custom_call_target="tpu_custom_call" | custom-call | tf_op jit(solution)/shard_map/pallas_call | solution.py:212
  (29 shorter events, 1.1 us)
Async XLA Ops:
  0.0 46.7 %copy-start = (bf16[256,4096]{1,0:T(8,128)(2,1)S(1)}, bf16[256,4096]{1,0:T(8,128)(2,1)}, u32[]{:S(2)}) copy-start(bf16[256,4096]{1,0:T(8,128)(2,1)} %param.10) | copy-start | bytes 6291460
  2.8 12.6 %collective-permute-start = (bf16[8,128,2304]{2,1,0:T(8,128)(2,1)S(1)}, bf16[8,128,2304]{2,1,0:T(8,128)(2,1)S(1)}, u32[]{:S(2)}, u32[]{:S(2)}) collective-permute-start(bf16[8,128,2304]{2,1,0:T(8,128)(2,1)S(1)} %get-tuple-element.12), channel_id=1, source_target_pairs={{0,1},{1,0},{2,3},{3,2},{4,5},{5,4},{6,7},{7,6},{8,9},{9,8},{10,11... | collective-permute-start | bytes 14155784 | tf_op jit(solution)/shard_map/ppermute | solution.py:43
  3.3 6.9 %collective-permute-start.1 = (bf16[64,1152]{1,0:T(8,128)(2,1)S(1)}, bf16[64,1152]{1,0:T(8,128)(2,1)S(1)}, u32[]{:S(2)}, u32[]{:S(2)}) collective-permute-start(bf16[64,1152]{1,0:T(8,128)(2,1)S(1)} %get-tuple-element.13.refs_0_), channel_id=1, source_target_pairs={{0,5},{1,4},{4,9},{5,8},{8,13},{9,12},{12,15},{13,14},{14,11},{15,... | collective-permute-start | bytes 442376 | tf_op jit(solution)/shard_map/ppermute | solution.py:39
  6.0 6.4 %collective-permute-start.4 = (bf16[64,1152]{1,0:T(8,128)(2,1)S(1)}, bf16[64,1152]{1,0:T(8,128)(2,1)S(1)}, u32[]{:S(2)}, u32[]{:S(2)}) collective-permute-start(bf16[64,1152]{1,0:T(8,128)(2,1)S(1)} %get-tuple-element.14.refs_1_), channel_id=1, source_target_pairs={{0,3},{1,2},{4,1},{5,0},{8,5},{9,4},{12,9},{13,8},{14,13},{15,12},... | collective-permute-start | bytes 442376 | tf_op jit(solution)/shard_map/ppermute | solution.py:39
  6.0 7.3 %collective-permute-start.2 = (bf16[64,1152]{1,0:T(8,128)(2,1)S(1)}, bf16[64,1152]{1,0:T(8,128)(2,1)S(1)}, u32[]{:S(2)}, u32[]{:S(2)}) collective-permute-start(bf16[64,1152]{1,0:T(8,128)(2,1)S(1)} %get-tuple-element.14.refs_1_), channel_id=1, source_target_pairs={{0,5},{1,4},{4,9},{5,8},{8,13},{9,12},{12,15},{13,14},{14,11},{15,... | collective-permute-start | bytes 442376 | tf_op jit(solution)/shard_map/ppermute | solution.py:39
  7.7 7.7 %collective-permute-start.3 = (bf16[64,1152]{1,0:T(8,128)(2,1)S(1)}, bf16[64,1152]{1,0:T(8,128)(2,1)S(1)}, u32[]{:S(2)}, u32[]{:S(2)}) collective-permute-start(bf16[64,1152]{1,0:T(8,128)(2,1)S(1)} %get-tuple-element.13.refs_0_), channel_id=1, source_target_pairs={{0,3},{1,2},{4,1},{5,0},{8,5},{9,4},{12,9},{13,8},{14,13},{15,12},... | collective-permute-start | bytes 442376 | tf_op jit(solution)/shard_map/ppermute | solution.py:39
  10.1 8.0 %collective-permute-start.5 = (bf16[64,1152]{1,0:T(8,128)(2,1)S(1)}, bf16[64,1152]{1,0:T(8,128)(2,1)S(1)}, u32[]{:S(2)}, u32[]{:S(2)}) collective-permute-start(bf16[64,1152]{1,0:T(8,128)(2,1)S(1)} %collective-permute-done.1.refs_2_), channel_id=1, source_target_pairs={{0,5},{1,4},{4,9},{5,8},{8,13},{9,12},{12,15},{13,14},{14,11},{15,... | collective-permute-start | bytes 442376 | tf_op jit(solution)/shard_map/ppermute | solution.py:39
  12.3 7.6 %collective-permute-start.8 = (bf16[64,1152]{1,0:T(8,128)(2,1)S(1)}, bf16[64,1152]{1,0:T(8,128)(2,1)S(1)}, u32[]{:S(2)}, u32[]{:S(2)}) collective-permute-start(bf16[64,1152]{1,0:T(8,128)(2,1)S(1)} %collective-permute-done.4.refs_5_), channel_id=1, source_target_pairs={{0,3},{1,2},{4,1},{5,0},{8,5},{9,4},{12,9},{13,8},{14,13},{15,12},... | collective-permute-start | bytes 442376 | tf_op jit(solution)/shard_map/ppermute | solution.py:39
  13.2 6.7 %collective-permute-start.6 = (bf16[64,1152]{1,0:T(8,128)(2,1)S(1)}, bf16[64,1152]{1,0:T(8,128)(2,1)S(1)}, u32[]{:S(2)}, u32[]{:S(2)}) collective-permute-start(bf16[64,1152]{1,0:T(8,128)(2,1)S(1)} %collective-permute-done.2.refs_3_), channel_id=1, source_target_pairs={{0,5},{1,4},{4,9},{5,8},{8,13},{9,12},{12,15},{13,14},{14,11},{15,... | collective-permute-start | bytes 442376 | tf_op jit(solution)/shard_map/ppermute | solution.py:39
  15.4 6.3 %collective-permute-start.7 = (bf16[64,1152]{1,0:T(8,128)(2,1)S(1)}, bf16[64,1152]{1,0:T(8,128)(2,1)S(1)}, u32[]{:S(2)}, u32[]{:S(2)}) collective-permute-start(bf16[64,1152]{1,0:T(8,128)(2,1)S(1)} %collective-permute-done.3.refs_4_), channel_id=1, source_target_pairs={{0,3},{1,2},{4,1},{5,0},{8,5},{9,4},{12,9},{13,8},{14,13},{15,12},... | collective-permute-start | bytes 442376 | tf_op jit(solution)/shard_map/ppermute | solution.py:39
  18.2 6.0 %collective-permute-start.11 = (bf16[64,1152]{1,0:T(8,128)(2,1)S(1)}, bf16[64,1152]{1,0:T(8,128)(2,1)S(1)}, u32[]{:S(2)}, u32[]{:S(2)}) collective-permute-start(bf16[64,1152]{1,0:T(8,128)(2,1)S(1)} %collective-permute-done.5.refs_0_), channel_id=1, source_target_pairs={{0,5},{1,4},{4,9},{5,8},{8,13},{9,12},{12,15},{13,14},{14,11},{15,... | collective-permute-start | bytes 442376 | tf_op jit(solution)/shard_map/ppermute | solution.py:39
  19.9 6.4 %collective-permute-start.9 = (bf16[64,1152]{1,0:T(8,128)(2,1)S(1)}, bf16[64,1152]{1,0:T(8,128)(2,1)S(1)}, u32[]{:S(2)}, u32[]{:S(2)}) collective-permute-start(bf16[64,1152]{1,0:T(8,128)(2,1)S(1)} %collective-permute-done.8.refs_3_), channel_id=1, source_target_pairs={{0,3},{1,2},{4,1},{5,0},{8,5},{9,4},{12,9},{13,8},{14,13},{15,12},... | collective-permute-start | bytes 442376 | tf_op jit(solution)/shard_map/ppermute | solution.py:39
  20.0 8.7 %collective-permute-start.13 = (bf16[64,1152]{1,0:T(8,128)(2,1)S(1)}, bf16[64,1152]{1,0:T(8,128)(2,1)S(1)}, u32[]{:S(2)}, u32[]{:S(2)}) collective-permute-start(bf16[64,1152]{1,0:T(8,128)(2,1)S(1)} %collective-permute-done.6.refs_1_), channel_id=1, source_target_pairs={{0,5},{1,4},{4,9},{5,8},{8,13},{9,12},{12,15},{13,14},{14,11},{15,... | collective-permute-start | bytes 442376 | tf_op jit(solution)/shard_map/ppermute | solution.py:39
  21.7 7.4 %collective-permute-start.14 = (bf16[64,1152]{1,0:T(8,128)(2,1)S(1)}, bf16[64,1152]{1,0:T(8,128)(2,1)S(1)}, u32[]{:S(2)}, u32[]{:S(2)}) collective-permute-start(bf16[64,1152]{1,0:T(8,128)(2,1)S(1)} %collective-permute-done.7.refs_2_), channel_id=1, source_target_pairs={{0,3},{1,2},{4,1},{5,0},{8,5},{9,4},{12,9},{13,8},{14,13},{15,12},... | collective-permute-start | bytes 442376 | tf_op jit(solution)/shard_map/ppermute | solution.py:39
  24.2 6.1 %collective-permute-start.12 = (bf16[64,1152]{1,0:T(8,128)(2,1)S(1)}, bf16[64,1152]{1,0:T(8,128)(2,1)S(1)}, u32[]{:S(2)}, u32[]{:S(2)}) collective-permute-start(bf16[64,1152]{1,0:T(8,128)(2,1)S(1)} %collective-permute-done.11.refs_0_), channel_id=1, source_target_pairs={{0,5},{1,4},{4,9},{5,8},{8,13},{9,12},{12,15},{13,14},{14,11},{15,... | collective-permute-start | bytes 442376 | tf_op jit(solution)/shard_map/ppermute | solution.py:39
  26.3 5.9 %collective-permute-start.10 = (bf16[64,1152]{1,0:T(8,128)(2,1)S(1)}, bf16[64,1152]{1,0:T(8,128)(2,1)S(1)}, u32[]{:S(2)}, u32[]{:S(2)}) collective-permute-start(bf16[64,1152]{1,0:T(8,128)(2,1)S(1)} %collective-permute-done.9.refs_3_), channel_id=1, source_target_pairs={{0,3},{1,2},{4,1},{5,0},{8,5},{9,4},{12,9},{13,8},{14,13},{15,12},... | collective-permute-start | bytes 442376 | tf_op jit(solution)/shard_map/ppermute | solution.py:39
  32.6 23.8 %copy-start.1 = (bf16[8,4096]{1,0:T(8,128)(2,1)S(1)}, bf16[8,4096]{1,0:T(8,128)(2,1)}, u32[]{:S(2)}) copy-start(bf16[8,4096]{1,0:T(8,128)(2,1)} %queries.1) | copy-start | bytes 196612
  32.6 1.4 %collective-permute-start.15 = (f32[256,128]{1,0:T(8,128)S(1)}, f32[256,128]{1,0:T(8,128)S(1)}, u32[]{:S(2)}, u32[]{:S(2)}) collective-permute-start(f32[256,128]{1,0:T(8,128)S(1)} %shard_map.69), channel_id=1, source_target_pairs={{0,1},{1,0},{2,3},{3,2},{4,5},{5,4},{6,7},{7,6},{8,9},{9,8},{10,11... | collective-permute-start | bytes 393224 | tf_op jit(solution)/shard_map/ppermute | solution.py:43

commit v16 on v14

--- a/solution.py
+++ b/solution.py
@@ -124,20 +124,19 @@
         column_copies(chip, core, act, grad, space, sems.at[i], chips)
         for i, (chip, space) in enumerate(zip(where, spaces))
     ]
-    for pair in copies:
+    for pair in copies[:3]:
         for copy in pair:
             copy.start()
     sums = (jnp.zeros((out.shape[0], rank), jnp.float32),) * 2
-    for i in range(len(offsets)):
+    for i in range(len(copies)):
         for copy in copies[i]:
             copy.wait()
-        for part in range(2):
+        for copy in sum(copies[i + 3 : i + 4], []):
+            copy.start()
+        for part in range(2) if i < len(offsets) else ():
             chunk = chunks[2 * i + part]
             sums = add_products(sums, spaces[i], theirs.at[where[i]], part, chunk, a_width, cut)
     out[:, :rank], out[:, rank:] = sums
-    for pair in copies[len(offsets) :]:
-        for copy in pair:
-            copy.wait()
 
 
 def near_products(act, grad, theirs, blocks, offsets, later, a_width):

time: 56.6 us -> 57.6 us (1.018)
  waiting for transfers between devices: 8.42 us -> 7.31 us
  Pallas kernels: 8.8 us -> 9.8 us
  blocking collectives: 21.8 us -> 22.8 us
    pallas_call x1, Pallas kernels: 3.77 us -> 4.76 us  [near_products(): pl.pallas_call(functools.partial(near_kernel, chips, offsets, later, a_wi...]
    ppermute x14, waiting for transfers between devices: 7.18 us -> 6.21 us  [ring(): return lax.ppermute(x, 'dp', pairs)]
    all_to_all x2, blocking collectives: 21.8 us -> 22.8 us  [to_all(): lax.all_to_all(copies, 'dp', 0, 0, axis_index_groups=groups, tiled=True)]
  transfers between devices with their start and end apart: 16 -> 16, of which waited for: 7 -> 6; matrix products, arithmetic and copies ran while one was open for 0% -> 0% of each run, Pallas kernels for 9% -> 10%
where the time goes in v16:
time: 57.6 us; the launch traced here: 57.4 us
  blocking collectives  22.8 us (40%)
  starting transfers between devices  16.3 us (28%)
  Pallas kernels  9.8 us (17%)
  waiting for transfers between devices  7.31 us (13%)
  matrix products  0.89 us (2%)
    all_to_all x2, blocking collectives, to_all(): lax.all_to_all(copies, 'dp', 0, 0, axis_index_groups=groups, tiled=True)  22.8 us
    ppermute x14, starting transfers between devices, ring(): return lax.ppermute(x, 'dp', pairs)  15.4 us
    ppermute x14, waiting for transfers between devices, ring(): return lax.ppermute(x, 'dp', pairs)  6.21 us
    pallas_call x1, Pallas kernels, near_products(): pl.pallas_call(functools.partial(near_kernel, chips, offsets, later, a_wi...  4.76 us
    pallas_call x1, Pallas kernels, start(): pl.pallas_call(functools.partial(start_kernel, chips), out_shape=[pltpu.V...  2.74 us
    pallas_call x3, Pallas kernels, later_products(): pl.pallas_call(functools.partial(later_kernel, chips, items, a_width, cut...  1.57 us
  transfers between devices with their start and end apart: 16, of which 6 were waited for; matrix products, arithmetic and copies ran while one was open for 0% of the time, Pallas kernels for 10%

profile of v16, /device:TPU:0, one launch (start us, length us, event | category | flops | bytes accessed | tf_op | source)
XLA Modules:
  0.0 57.4 jit_solution(852156955544733730)
XLA Ops:
  0.0 2.7 %shard_map.64 = (bf16[64,1152]{1,0:T(8,128)(2,1)S(1)}, bf16[64,1152]{1,0:T(8,128)(2,1)S(1)}, bf16[8,128,2304]{2,1,0:T(8,128)(2,1)S(1)}) custom-call(bf16[128,8192]{1,0:T(8,128)(2,1)} %act.3, bf16[128,28672]{1,0:T(8,128)(2,1)} %grad.3, bf16[64,512]{1,0:T(8,128)(2,1)} %bitcast.12, bf16[64,1792]{1,0:T(8,128)(2,1)} %bitcast.11), custom_call_target="tpu_custom_call" | custom-call | bytes 10027008 | tf_op jit(solution)/shard_map/pallas_call | solution.py:90
  2.8 0.5 collective-permute-start
  3.3 2.7 %collective-permute-start.1 = (bf16[64,1152]{1,0:T(8,128)(2,1)S(1)}, bf16[64,1152]{1,0:T(8,128)(2,1)S(1)}, u32[]{:S(2)}, u32[]{:S(2)}) collective-permute-start(bf16[64,1152]{1,0:T(8,128)(2,1)S(1)} %get-tuple-element.11.refs_0_), channel_id=1, source_target_pairs={{0,5},{1,4},{4,9},{5,8},{8,13},{9,12},{12,15},{13,14},{14,11},{15,... | collective-permute-start | bytes 442376 | tf_op jit(solution)/shard_map/ppermute | solution.py:39
  6.0 1.7 %collective-permute-start.2 = (bf16[64,1152]{1,0:T(8,128)(2,1)S(1)}, bf16[64,1152]{1,0:T(8,128)(2,1)S(1)}, u32[]{:S(2)}, u32[]{:S(2)}) collective-permute-start(bf16[64,1152]{1,0:T(8,128)(2,1)S(1)} %get-tuple-element.12.refs_1_), channel_id=1, source_target_pairs={{0,5},{1,4},{4,9},{5,8},{8,13},{9,12},{12,15},{13,14},{14,11},{15,... | collective-permute-start | bytes 442376 | tf_op jit(solution)/shard_map/ppermute | solution.py:39
  7.7 2.4 %collective-permute-done.1.refs_2_ = bf16[64,1152]{1,0:T(8,128)(2,1)S(1)} collective-permute-done((bf16[64,1152]{1,0:T(8,128)(2,1)S(1)}, bf16[64,1152]{1,0:T(8,128)(2,1)S(1)}, u32[]{:S(2)}, u32[]{:S(2)}) %collective-permute-start.1) | collective-permute-done | bytes 147488 | tf_op jit(solution)/shard_map/ppermute | solution.py:39
  10.1 2.2 %collective-permute-start.5 = (bf16[64,1152]{1,0:T(8,128)(2,1)S(1)}, bf16[64,1152]{1,0:T(8,128)(2,1)S(1)}, u32[]{:S(2)}, u32[]{:S(2)}) collective-permute-start(bf16[64,1152]{1,0:T(8,128)(2,1)S(1)} %collective-permute-done.1.refs_2_), channel_id=1, source_target_pairs={{0,5},{1,4},{4,9},{5,8},{8,13},{9,12},{12,15},{13,14},{14,11},{15,... | collective-permute-start | bytes 442376 | tf_op jit(solution)/shard_map/ppermute | solution.py:39
  12.4 0.9 %collective-permute-done.2.refs_3_ = bf16[64,1152]{1,0:T(8,128)(2,1)S(1)} collective-permute-done((bf16[64,1152]{1,0:T(8,128)(2,1)S(1)}, bf16[64,1152]{1,0:T(8,128)(2,1)S(1)}, u32[]{:S(2)}, u32[]{:S(2)}) %collective-permute-start.2) | collective-permute-done | bytes 147488 | tf_op jit(solution)/shard_map/ppermute | solution.py:39
  13.2 2.2 %collective-permute-start.6 = (bf16[64,1152]{1,0:T(8,128)(2,1)S(1)}, bf16[64,1152]{1,0:T(8,128)(2,1)S(1)}, u32[]{:S(2)}, u32[]{:S(2)}) collective-permute-start(bf16[64,1152]{1,0:T(8,128)(2,1)S(1)} %collective-permute-done.2.refs_3_), channel_id=1, source_target_pairs={{0,5},{1,4},{4,9},{5,8},{8,13},{9,12},{12,15},{13,14},{14,11},{15,... | collective-permute-start | bytes 442376 | tf_op jit(solution)/shard_map/ppermute | solution.py:39
  15.4 1.1 %collective-permute-done.5.refs_6_ = bf16[64,1152]{1,0:T(8,128)(2,1)S(1)} collective-permute-done((bf16[64,1152]{1,0:T(8,128)(2,1)S(1)}, bf16[64,1152]{1,0:T(8,128)(2,1)S(1)}, u32[]{:S(2)}, u32[]{:S(2)}) %collective-permute-start.5) | collective-permute-done | bytes 147488 | tf_op jit(solution)/shard_map/ppermute | solution.py:39
  16.5 2.2 %collective-permute-start.11 = (bf16[64,1152]{1,0:T(8,128)(2,1)S(1)}, bf16[64,1152]{1,0:T(8,128)(2,1)S(1)}, u32[]{:S(2)}, u32[]{:S(2)}) collective-permute-start(bf16[64,1152]{1,0:T(8,128)(2,1)S(1)} %collective-permute-done.5.refs_6_), channel_id=1, source_target_pairs={{0,5},{1,4},{4,9},{5,8},{8,13},{9,12},{12,15},{13,14},{14,11},{15,... | collective-permute-start | bytes 442376 | tf_op jit(solution)/shard_map/ppermute | solution.py:39
  18.7 0.9 %collective-permute-done.6.refs_7_ = bf16[64,1152]{1,0:T(8,128)(2,1)S(1)} collective-permute-done((bf16[64,1152]{1,0:T(8,128)(2,1)S(1)}, bf16[64,1152]{1,0:T(8,128)(2,1)S(1)}, u32[]{:S(2)}, u32[]{:S(2)}) %collective-permute-start.6) | collective-permute-done | bytes 147488 | tf_op jit(solution)/shard_map/ppermute | solution.py:39
  19.5 2.2 %collective-permute-start.13 = (bf16[64,1152]{1,0:T(8,128)(2,1)S(1)}, bf16[64,1152]{1,0:T(8,128)(2,1)S(1)}, u32[]{:S(2)}, u32[]{:S(2)}) collective-permute-start(bf16[64,1152]{1,0:T(8,128)(2,1)S(1)} %collective-permute-done.6.refs_7_), channel_id=1, source_target_pairs={{0,5},{1,4},{4,9},{5,8},{8,13},{9,12},{12,15},{13,14},{14,11},{15,... | collective-permute-start | bytes 442376 | tf_op jit(solution)/shard_map/ppermute | solution.py:39
  21.8 1.0 %collective-permute-done.11.refs_0_ = bf16[64,1152]{1,0:T(8,128)(2,1)S(1)} collective-permute-done((bf16[64,1152]{1,0:T(8,128)(2,1)S(1)}, bf16[64,1152]{1,0:T(8,128)(2,1)S(1)}, u32[]{:S(2)}, u32[]{:S(2)}) %collective-permute-start.11) | collective-permute-done | bytes 147488 | tf_op jit(solution)/shard_map/ppermute | solution.py:39
  22.7 2.2 %collective-permute-start.12 = (bf16[64,1152]{1,0:T(8,128)(2,1)S(1)}, bf16[64,1152]{1,0:T(8,128)(2,1)S(1)}, u32[]{:S(2)}, u32[]{:S(2)}) collective-permute-start(bf16[64,1152]{1,0:T(8,128)(2,1)S(1)} %collective-permute-done.11.refs_0_), channel_id=1, source_target_pairs={{0,5},{1,4},{4,9},{5,8},{8,13},{9,12},{12,15},{13,14},{14,11},{15,... | collective-permute-start | bytes 442376 | tf_op jit(solution)/shard_map/ppermute | solution.py:39
  24.9 4.8 %shard_map.65 = (f32[256,128]{1,0:T(8,128)S(1)}, bf16[3,128,2304]{2,1,0:T(8,128)(2,1)S(1)}) custom-call(bf16[128,8192]{1,0:T(8,128)(2,1)} %act.3, bf16[128,28672]{1,0:T(8,128)(2,1)} %grad.3, bf16[8,128,2304]{2,1,0:T(8,128)(2,1)S(1)} %collective-permute-done.theirs, bf16[64,1152]{1,0:T(8,128)(2,1)S(1)} %get-tuple-element.11.refs_0_, ...), custom_call_target="tpu_custom_call" | custom-call | flops 377487360 | bytes 9142272 | tf_op jit(solution)/shard_map/pallas_call | solution.py:147
  29.7 0.8 %shard_map.66.refs_1_ = f32[256,128]{1,0:T(8,128)S(1)} custom-call(bf16[3,128,2304]{2,1,0:T(8,128)(2,1)S(1)} %get-tuple-element.13.rest, bf16[8,128,2304]{2,1,0:T(8,128)(2,1)S(1)} %collective-permute-done.theirs, bf16[64,1152]{1,0:T(8,128)(2,1)S(1)} %collective-permute-done.11.refs_0_, bf16[64,1152]{1,0:T(8,128)(2,1)S(1)} %collective-permute-done.13.refs_1_, ...), custom_call_target="tpu_custom_call" | custom-call | flops 150994944 | bytes 2949120 | tf_op jit(solution)/shard_map/pallas_call | solution.py:182
  30.5 0.4 shard_map.67.refs_1_
  30.9 0.4 shard_map.68
  31.3 0.3 collective-permute-start.15
  31.7 1.1 %collective-permute-done.15 = f32[256,128]{1,0:T(8,128)S(1)} collective-permute-done((f32[256,128]{1,0:T(8,128)S(1)}, f32[256,128]{1,0:T(8,128)S(1)}, u32[]{:S(2)}, u32[]{:S(2)}) %collective-permute-start.15) | collective-permute-done | bytes 131104 | tf_op jit(solution)/shard_map/ppermute | solution.py:43
  33.1 13.7 %all_to_all.10 = f32[8,32,128]{2,1,0:T(8,128)S(1)} all-to-all(f32[8,32,128]{2,1,0:T(8,128)S(1)} %broadcast_in_dim.14), channel_id=1, replica_groups={{0,2,4,6,8,10,12,14},{1,3,5,7,9,11,13,15},{16,18,20,22,24,26,28,30},{17..., dimensions={0} | all-to-all | bytes 262144 | tf_op jit(solution)/shard_map/all_to_all | solution.py:216
  46.8 0.6 %convolution_convert_fusion = bf16[2,256]{1,0:T(2,128)(2,1)S(1)} fusion(bf16[256,4096]{1,0:T(8,128)(2,1)S(1)} %copy-done, bf16[1,2,32,128]{3,2,1,0:T(8,128)(2,1)S(1)} %bitcast.13), kind=kOutput, calls=%fused_computation.1 | convolution fusion | flops 4194816 | bytes 2114560 | tf_op jit(solution)/shard_map/dot_general | solution.py:23
  47.5 9.1 %all_to_all.11.conditioned = bf16[16,2,256]{2,1,0:T(2,128)(2,1)S(1)} all-to-all(bf16[16,2,256]{2,1,0:T(2,128)(2,1)S(1)} %broadcast_in_dim.15), channel_id=1, replica_groups={{0,1,2,3,4,5,6,7,8,9,10,11,12,13,14,15},{16,17,18,19,20,21,22,23,24,25,..., dimensions={0} | all-to-all | bytes 32768 | tf_op jit(solution)/shard_map/all_to_all | solution.py:216
  56.6 0.7 %shard_map.69 = f32[2,8]{1,0:T(2,128)} custom-call(bf16[16,2,256]{2,1,0:T(2,128)(2,1)S(1)} %all_to_all.11.conditioned, bf16[8,4096]{1,0:T(8,128)(2,1)S(1)} %copy-done.1), custom_call_target="tpu_custom_call" | custom-call | tf_op jit(solution)/shard_map/pallas_call | solution.py:205
  (28 shorter events, 0.5 us)
Async XLA Ops:
  0.0 46.8 %copy-start = (bf16[256,4096]{1,0:T(8,128)(2,1)S(1)}, bf16[256,4096]{1,0:T(8,128)(2,1)}, u32[]{:S(2)}) copy-start(bf16[256,4096]{1,0:T(8,128)(2,1)} %param.10) | copy-start | bytes 6291460
  2.8 22.2 %collective-permute-start = (bf16[8,128,2304]{2,1,0:T(8,128)(2,1)S(1)}, bf16[8,128,2304]{2,1,0:T(8,128)(2,1)S(1)}, u32[]{:S(2)}, u32[]{:S(2)}) collective-permute-start(bf16[8,128,2304]{2,1,0:T(8,128)(2,1)S(1)} %get-tuple-element.10), channel_id=1, source_target_pairs={{0,1},{1,0},{2,3},{3,2},{4,5},{5,4},{6,7},{7,6},{8,9},{9,8},{10,11... | collective-permute-start | bytes 14155784 | tf_op jit(solution)/shard_map/ppermute | solution.py:43
  3.3 6.9 %collective-permute-start.1 = (bf16[64,1152]{1,0:T(8,128)(2,1)S(1)}, bf16[64,1152]{1,0:T(8,128)(2,1)S(1)}, u32[]{:S(2)}, u32[]{:S(2)}) collective-permute-start(bf16[64,1152]{1,0:T(8,128)(2,1)S(1)} %get-tuple-element.11.refs_0_), channel_id=1, source_target_pairs={{0,5},{1,4},{4,9},{5,8},{8,13},{9,12},{12,15},{13,14},{14,11},{15,... | collective-permute-start | bytes 442376 | tf_op jit(solution)/shard_map/ppermute | solution.py:39
  6.0 6.4 %collective-permute-start.4 = (bf16[64,1152]{1,0:T(8,128)(2,1)S(1)}, bf16[64,1152]{1,0:T(8,128)(2,1)S(1)}, u32[]{:S(2)}, u32[]{:S(2)}) collective-permute-start(bf16[64,1152]{1,0:T(8,128)(2,1)S(1)} %get-tuple-element.12.refs_1_), channel_id=1, source_target_pairs={{0,3},{1,2},{4,1},{5,0},{8,5},{9,4},{12,9},{13,8},{14,13},{15,12},... | collective-permute-start | bytes 442376 | tf_op jit(solution)/shard_map/ppermute | solution.py:39
  6.0 7.3 %collective-permute-start.2 = (bf16[64,1152]{1,0:T(8,128)(2,1)S(1)}, bf16[64,1152]{1,0:T(8,128)(2,1)S(1)}, u32[]{:S(2)}, u32[]{:S(2)}) collective-permute-start(bf16[64,1152]{1,0:T(8,128)(2,1)S(1)} %get-tuple-element.12.refs_1_), channel_id=1, source_target_pairs={{0,5},{1,4},{4,9},{5,8},{8,13},{9,12},{12,15},{13,14},{14,11},{15,... | collective-permute-start | bytes 442376 | tf_op jit(solution)/shard_map/ppermute | solution.py:39
  7.7 7.7 %collective-permute-start.3 = (bf16[64,1152]{1,0:T(8,128)(2,1)S(1)}, bf16[64,1152]{1,0:T(8,128)(2,1)S(1)}, u32[]{:S(2)}, u32[]{:S(2)}) collective-permute-start(bf16[64,1152]{1,0:T(8,128)(2,1)S(1)} %get-tuple-element.11.refs_0_), channel_id=1, source_target_pairs={{0,3},{1,2},{4,1},{5,0},{8,5},{9,4},{12,9},{13,8},{14,13},{15,12},... | collective-permute-start | bytes 442376 | tf_op jit(solution)/shard_map/ppermute | solution.py:39
  10.1 6.3 %collective-permute-start.5 = (bf16[64,1152]{1,0:T(8,128)(2,1)S(1)}, bf16[64,1152]{1,0:T(8,128)(2,1)S(1)}, u32[]{:S(2)}, u32[]{:S(2)}) collective-permute-start(bf16[64,1152]{1,0:T(8,128)(2,1)S(1)} %collective-permute-done.1.refs_2_), channel_id=1, source_target_pairs={{0,5},{1,4},{4,9},{5,8},{8,13},{9,12},{12,15},{13,14},{14,11},{15,... | collective-permute-start | bytes 442376 | tf_op jit(solution)/shard_map/ppermute | solution.py:39
  12.3 6.3 %collective-permute-start.8 = (bf16[64,1152]{1,0:T(8,128)(2,1)S(1)}, bf16[64,1152]{1,0:T(8,128)(2,1)S(1)}, u32[]{:S(2)}, u32[]{:S(2)}) collective-permute-start(bf16[64,1152]{1,0:T(8,128)(2,1)S(1)} %collective-permute-done.4.refs_5_), channel_id=1, source_target_pairs={{0,3},{1,2},{4,1},{5,0},{8,5},{9,4},{12,9},{13,8},{14,13},{15,12},... | collective-permute-start | bytes 442376 | tf_op jit(solution)/shard_map/ppermute | solution.py:39
  13.2 6.3 %collective-permute-start.6 = (bf16[64,1152]{1,0:T(8,128)(2,1)S(1)}, bf16[64,1152]{1,0:T(8,128)(2,1)S(1)}, u32[]{:S(2)}, u32[]{:S(2)}) collective-permute-start(bf16[64,1152]{1,0:T(8,128)(2,1)S(1)} %collective-permute-done.2.refs_3_), channel_id=1, source_target_pairs={{0,5},{1,4},{4,9},{5,8},{8,13},{9,12},{12,15},{13,14},{14,11},{15,... | collective-permute-start | bytes 442376 | tf_op jit(solution)/shard_map/ppermute | solution.py:39
  15.4 6.4 %collective-permute-start.7 = (bf16[64,1152]{1,0:T(8,128)(2,1)S(1)}, bf16[64,1152]{1,0:T(8,128)(2,1)S(1)}, u32[]{:S(2)}, u32[]{:S(2)}) collective-permute-start(bf16[64,1152]{1,0:T(8,128)(2,1)S(1)} %collective-permute-done.3.refs_4_), channel_id=1, source_target_pairs={{0,3},{1,2},{4,1},{5,0},{8,5},{9,4},{12,9},{13,8},{14,13},{15,12},... | collective-permute-start | bytes 442376 | tf_op jit(solution)/shard_map/ppermute | solution.py:39
  16.5 6.3 %collective-permute-start.11 = (bf16[64,1152]{1,0:T(8,128)(2,1)S(1)}, bf16[64,1152]{1,0:T(8,128)(2,1)S(1)}, u32[]{:S(2)}, u32[]{:S(2)}) collective-permute-start(bf16[64,1152]{1,0:T(8,128)(2,1)S(1)} %collective-permute-done.5.refs_6_), channel_id=1, source_target_pairs={{0,5},{1,4},{4,9},{5,8},{8,13},{9,12},{12,15},{13,14},{14,11},{15,... | collective-permute-start | bytes 442376 | tf_op jit(solution)/shard_map/ppermute | solution.py:39
  18.7 6.3 %collective-permute-start.9 = (bf16[64,1152]{1,0:T(8,128)(2,1)S(1)}, bf16[64,1152]{1,0:T(8,128)(2,1)S(1)}, u32[]{:S(2)}, u32[]{:S(2)}) collective-permute-start(bf16[64,1152]{1,0:T(8,128)(2,1)S(1)} %collective-permute-done.8.refs_9_), channel_id=1, source_target_pairs={{0,3},{1,2},{4,1},{5,0},{8,5},{9,4},{12,9},{13,8},{14,13},{15,12},... | collective-permute-start | bytes 442376 | tf_op jit(solution)/shard_map/ppermute | solution.py:39
  19.5 10.1 %collective-permute-start.13 = (bf16[64,1152]{1,0:T(8,128)(2,1)S(1)}, bf16[64,1152]{1,0:T(8,128)(2,1)S(1)}, u32[]{:S(2)}, u32[]{:S(2)}) collective-permute-start(bf16[64,1152]{1,0:T(8,128)(2,1)S(1)} %collective-permute-done.6.refs_7_), channel_id=1, source_target_pairs={{0,5},{1,4},{4,9},{5,8},{8,13},{9,12},{12,15},{13,14},{14,11},{15,... | collective-permute-start | bytes 442376 | tf_op jit(solution)/shard_map/ppermute | solution.py:39
  21.8 7.9 %collective-permute-start.14 = (bf16[64,1152]{1,0:T(8,128)(2,1)S(1)}, bf16[64,1152]{1,0:T(8,128)(2,1)S(1)}, u32[]{:S(2)}, u32[]{:S(2)}) collective-permute-start(bf16[64,1152]{1,0:T(8,128)(2,1)S(1)} %collective-permute-done.7.refs_8_), channel_id=1, source_target_pairs={{0,3},{1,2},{4,1},{5,0},{8,5},{9,4},{12,9},{13,8},{14,13},{15,12},... | collective-permute-start | bytes 442376 | tf_op jit(solution)/shard_map/ppermute | solution.py:39
  22.7 7.8 %collective-permute-start.12 = (bf16[64,1152]{1,0:T(8,128)(2,1)S(1)}, bf16[64,1152]{1,0:T(8,128)(2,1)S(1)}, u32[]{:S(2)}, u32[]{:S(2)}) collective-permute-start(bf16[64,1152]{1,0:T(8,128)(2,1)S(1)} %collective-permute-done.11.refs_0_), channel_id=1, source_target_pairs={{0,5},{1,4},{4,9},{5,8},{8,13},{9,12},{12,15},{13,14},{14,11},{15,... | collective-permute-start | bytes 442376 | tf_op jit(solution)/shard_map/ppermute | solution.py:39
  24.9 6.0 %collective-permute-start.10 = (bf16[64,1152]{1,0:T(8,128)(2,1)S(1)}, bf16[64,1152]{1,0:T(8,128)(2,1)S(1)}, u32[]{:S(2)}, u32[]{:S(2)}) collective-permute-start(bf16[64,1152]{1,0:T(8,128)(2,1)S(1)} %collective-permute-done.9.refs_3_), channel_id=1, source_target_pairs={{0,3},{1,2},{4,1},{5,0},{8,5},{9,4},{12,9},{13,8},{14,13},{15,12},... | collective-permute-start | bytes 442376 | tf_op jit(solution)/shard_map/ppermute | solution.py:39
  31.3 25.3 %copy-start.1 = (bf16[8,4096]{1,0:T(8,128)(2,1)S(1)}, bf16[8,4096]{1,0:T(8,128)(2,1)}, u32[]{:S(2)}) copy-start(bf16[8,4096]{1,0:T(8,128)(2,1)} %queries.1) | copy-start | bytes 196612
  31.3 1.4 %collective-permute-start.15 = (f32[256,128]{1,0:T(8,128)S(1)}, f32[256,128]{1,0:T(8,128)S(1)}, u32[]{:S(2)}, u32[]{:S(2)}) collective-permute-start(f32[256,128]{1,0:T(8,128)S(1)} %shard_map.68), channel_id=1, source_target_pairs={{0,1},{1,0},{2,3},{3,2},{4,5},{5,4},{6,7},{7,6},{8,9},{9,8},{10,11... | collective-permute-start | bytes 393224 | tf_op jit(solution)/shard_map/ppermute | solution.py:43

commit v17 on v12

--- a/solution.py
+++ b/solution.py
@@ -47,21 +47,17 @@
     return (chip ^ (chip >> 1)) & 1
 
 
-def column_copies(chips, core, act, grad, out, sems):
-    ring_of = core ^ odd(lax.axis_index("dp") >> 1)
-    a_width = act.shape[1] // (2 * chips)
-    g_width = grad.shape[1] // (2 * chips)
-    copies = []
-    for chip in range(chips):
-        block = 2 * chip + (ring_of ^ odd(chip))
-        for k, (ref, at, width) in enumerate(((act, 0, a_width), (grad, a_width, g_width))):
-            columns = pl.ds(pl.multiple_of(block * width, 128), width)
-            copies.append(
-                pltpu.make_async_copy(
-                    ref.at[:, columns], out.at[chip, :, pl.ds(at, width)], sems.at[chip, k]
-                )
-            )
-    return copies
+def column_copies(chip, ring_core, act, grad, out, sems, chips):
+    block = 2 * chip + (ring_core ^ odd(lax.axis_index("dp") >> 1) ^ odd(chip))
+    a_width, g_width = (x.shape[1] // (2 * chips) for x in (act, grad))
+    return [
+        pltpu.make_async_copy(
+            ref.at[:, pl.ds(pl.multiple_of(block * width, 128), width)],
+            out.at[:, pl.ds(at, width)],
+            sems.at[k],
+        )
+        for k, (ref, at, width) in enumerate(((act, 0, a_width), (grad, a_width, g_width)))
+    ]
 
 
 def run_copies(copies):
@@ -81,7 +77,9 @@
         (out_rows.at[:, pl.ds(cut - a_width, second.shape[1])], second),
     ]
     copies = [pltpu.make_async_copy(*pair, sems.at[i]) for i, pair in enumerate(pairs)]
-    run_copies(copies + column_copies(chips, 1 - core, act, grad, send, send_sems))
+    for chip in range(chips):
+        copies += column_copies(chip, 1 - core, act, grad, send.at[chip], send_sems.at[chip], chips)
+    run_copies(copies)
 
 
 def start(act, grad, in_rows, out_rows, chips):
@@ -102,61 +100,44 @@
     )(*held(pltpu.HBM, act, grad, in_rows, out_rows))
 
 
-def keep_kernel(chips, act, grad, keep, sems):
-    core = lax.axis_index("dp") & 1
-    run_copies(column_copies(chips, core, act, grad, keep, sems))
-
-
-def keep_columns(act, grad, chips):
-    rows, width = act.shape[0], (act.shape[1] + grad.shape[1]) // (2 * chips)
-    return pl.pallas_call(
-        functools.partial(keep_kernel, chips),
-        out_shape=pltpu.VMEM((chips, rows, width), act.dtype),
-        in_specs=[HBM] * 2,
-        out_specs=VMEM,
-        scratch_shapes=[pltpu.SemaphoreType.DMA((chips, 2))],
-        compiler_params=pltpu.CompilerParams(vmem_limit_bytes=16 * 2**20),
-        cost_estimate=pl.CostEstimate(
-            flops=0, bytes_accessed=4 * chips * rows * width, transcendentals=0
-        ),
-    )(*held(pltpu.HBM, act, grad))
-
-
-def project_kernel(chips, offsets, parts, a_width, cut, carry, *refs):
-    keep, theirs = refs[:2]
-    chunks, refs = refs[2 : 2 + len(parts)], refs[2 + len(parts) :]
+def project_kernel(chips, items, a_width, cut, carry, act, grad, theirs, *refs):
+    chunks, refs = refs[: len(items)], refs[len(items) :]
     out = refs[-1]
     rank = chunks[0].shape[0]
-    width = keep.shape[2]
+    g_width = theirs.shape[2] - a_width
+    me = lax.axis_index("dp")
     if carry:
         a_sum, g_sum = refs[0][:, :rank], refs[0][:, rank:]
     else:
         a_sum = g_sum = jnp.zeros((out.shape[0], rank), jnp.float32)
-    for offset, part, chunk in zip(offsets, parts, chunks):
+    for (offset, part), chunk in zip(items, chunks):
         chip = chip_behind(offset, chips)
-
-        def tokens(first, last):
-            return jnp.concatenate([ref[chip, :, first:last] for ref in (keep, theirs)], axis=0)
+        block = 2 * chip + ((me & 1) ^ odd(me >> 1) ^ odd(chip))
+
+        def tokens(ref, width, skip, first, last):
+            at = pl.multiple_of(block * width, 128) + (first - skip)
+            return jnp.concatenate(
+                [ref[:, pl.ds(at, last - first)], theirs[chip, :, first:last]], axis=0
+            )
 
         if part == 0:
-            a_sum += dot(tokens(0, a_width), chunk[:, :a_width], NT)
-            g_sum += dot(tokens(a_width, cut), chunk[:, a_width:], NT)
+            a_sum += dot(tokens(act, a_width, 0, 0, a_width), chunk[:, :a_width], NT)
+            g_sum += dot(tokens(grad, g_width, a_width, a_width, cut), chunk[:, a_width:], NT)
         else:
-            g_sum += dot(tokens(cut, width), chunk[...], NT)
+            g_sum += dot(tokens(grad, g_width, a_width, cut, theirs.shape[2]), chunk[...], NT)
     out[:, :rank] = a_sum
     out[:, rank:] = g_sum
 
 
-def project(tokens, chunks, a_width, cut, carry=None):
-    chips, rows, width = tokens[0].shape
-    offsets, parts, flat = zip(*chunks)
-    rank = flat[0].shape[0]
-    carried = () if carry is None else (carry,)
-    columns = sum(x.shape[1] for x in flat)
+def project(tokens, items, chunks, a_width, cut, total=None):
+    chips, rows, _ = tokens[2].shape
+    rank = chunks[0].shape[0]
+    columns = sum(x.shape[1] for x in chunks)
+    carried = [] if total is None else [total]
     return pl.pallas_call(
-        functools.partial(project_kernel, chips, offsets, parts, a_width, cut, carry is not None),
+        functools.partial(project_kernel, chips, items, a_width, cut, total is not None),
         out_shape=pltpu.VMEM((2 * rows, 2 * rank), jnp.float32),
-        in_specs=[VMEM] * (2 + len(flat) + len(carried)),
+        in_specs=[VMEM] * (3 + len(chunks) + len(carried)),
         out_specs=VMEM,
         compiler_params=pltpu.CompilerParams(vmem_limit_bytes=16 * 2**20),
         cost_estimate=pl.CostEstimate(
@@ -164,7 +145,7 @@
             bytes_accessed=(2 * rows + rank) * columns * 2,
             transcendentals=0,
         ),
-    )(*held(pltpu.VMEM, *tokens, *flat, *carried))
+    )(*held(pltpu.VMEM, *tokens, *chunks, *carried))
 
 
 def score_kernel(scale, conditioned, queries, out):
@@ -205,21 +186,18 @@
         down.append([ring(x, -1, chips) for x in down[-1]])
     last = chips // 2 - 1
     far = (ring(up[last][0], 1, chips), ring(down[last][1], -1, chips))
-    keep = keep_columns(activations, out_grads, chips)
-
-    cut = own[0].shape[1]
-    run = functools.partial(project, (keep, theirs), a_width=a_width, cut=cut)
-
-    def both(block, offset):
-        return [(offset, part, x) for part, x in enumerate(block)]
-
-    near = both(own, 0)
+
+    tokens = activations, out_grads, theirs
+    run = functools.partial(project, tokens, a_width=a_width, cut=own[0].shape[1])
+    near, items = [*own], [(0, 0), (0, 1)]
     for i in range(1, last):
-        near += both(up[i], i) + both(down[i], -i)
-    total = run(near)
-    total = run(both(up[last], last) + both(down[last], -last), carry=total)
-    for part, x in enumerate(far):
-        total = run([(chips // 2, part, x)], carry=total)
+        near += [*up[i], *down[i]]
+        items += [(offset, part) for offset in (i, -i) for part in range(2)]
+    total = run(items, near)
+    items = [(offset, part) for offset in (last, -last) for part in range(2)]
+    total = run(items, [*up[last], *down[last]], total=total)
+    for part, chunk in enumerate(far):
+        total = run([(chips // 2, part)], [chunk], total=total)
     theirs = swap(total, 1, n)
     total = (total + jnp.concatenate([theirs[rows:], theirs[:rows]], axis=0)).astype(jnp.bfloat16)
 

time: 57.1 us -> 56.2 us (0.984)
  waiting for transfers between devices: 7.93 us -> 10.4 us
  Pallas kernels: 9.28 us -> 6.81 us
  blocking collectives: 22.4 us -> 21.5 us
    ppermute x14, waiting for transfers between devices: 6.69 us -> 9.17 us  [ring(): return lax.ppermute(x, 'dp', pairs)]
    pallas_call x5 -> x4, Pallas kernels: 5.8 us -> 3.34 us  [project(): pl.pallas_call(functools.partial(project_kernel, chips, items, a_width, c...]
    all_to_all x2, blocking collectives: 22.4 us -> 21.5 us  [to_all(): lax.all_to_all(copies, 'dp', 0, 0, axis_index_groups=groups, tiled=True)]
  transfers between devices with their start and end apart: 16 -> 16, of which waited for: 7 -> 9; matrix products, arithmetic and copies ran while one was open for 0% -> 0% of each run, Pallas kernels for 10% -> 5%
where the time goes in v17:
time: 56.2 us; the launch traced here: 56 us
  blocking collectives  21.5 us (38%)
  starting transfers between devices  16.1 us (29%)
  waiting for transfers between devices  10.4 us (19%)
  Pallas kernels  6.81 us (12%)
  matrix products  0.89 us (2%)
    all_to_all x2, blocking collectives, to_all(): lax.all_to_all(copies, 'dp', 0, 0, axis_index_groups=groups, tiled=True)  21.5 us
    ppermute x14, starting transfers between devices, ring(): return lax.ppermute(x, 'dp', pairs)  15.4 us
    ppermute x14, waiting for transfers between devices, ring(): return lax.ppermute(x, 'dp', pairs)  9.17 us
    pallas_call x4, Pallas kernels, project(): pl.pallas_call(functools.partial(project_kernel, chips, items, a_width, c...  3.34 us
    pallas_call x1, Pallas kernels, start(): pl.pallas_call(functools.partial(start_kernel, chips), out_shape=[pltpu.V...  2.74 us
    ppermute x2, waiting for transfers between devices, swap(): return lax.ppermute(x, 'dp', [(i, i ^ bit) for i in range(n)])  1.24 us
  transfers between devices with their start and end apart: 16, of which 9 were waited for; matrix products, arithmetic and copies ran while one was open for 0% of the time, Pallas kernels for 5%

profile of v17, /device:TPU:0, one launch (start us, length us, event | category | flops | bytes accessed | tf_op | source)
XLA Modules:
  0.0 56.0 jit_solution(9788470735068854535)
XLA Ops:
  0.0 2.7 %shard_map.64 = (bf16[64,1152]{1,0:T(8,128)(2,1)S(1)}, bf16[64,1152]{1,0:T(8,128)(2,1)S(1)}, bf16[8,128,2304]{2,1,0:T(8,128)(2,1)S(1)}) custom-call(bf16[128,8192]{1,0:T(8,128)(2,1)} %act.9, bf16[128,28672]{1,0:T(8,128)(2,1)} %grad.9, bf16[64,512]{1,0:T(8,128)(2,1)} %bitcast.12, bf16[64,1792]{1,0:T(8,128)(2,1)} %bitcast.11), custom_call_target="tpu_custom_call" | custom-call | bytes 10027008 | tf_op jit(solution)/shard_map/pallas_call | solution.py:90
  2.8 0.5 collective-permute-start
  3.3 2.7 %collective-permute-start.5 = (bf16[64,1152]{1,0:T(8,128)(2,1)S(1)}, bf16[64,1152]{1,0:T(8,128)(2,1)S(1)}, u32[]{:S(2)}, u32[]{:S(2)}) collective-permute-start(bf16[64,1152]{1,0:T(8,128)(2,1)S(1)} %get-tuple-element.10.refs_0_), channel_id=1, source_target_pairs={{0,5},{1,4},{4,9},{5,8},{8,13},{9,12},{12,15},{13,14},{14,11},{15,... | collective-permute-start | bytes 442376 | tf_op jit(solution)/shard_map/ppermute | solution.py:39
  6.0 1.7 %collective-permute-start.9 = (bf16[64,1152]{1,0:T(8,128)(2,1)S(1)}, bf16[64,1152]{1,0:T(8,128)(2,1)S(1)}, u32[]{:S(2)}, u32[]{:S(2)}) collective-permute-start(bf16[64,1152]{1,0:T(8,128)(2,1)S(1)} %get-tuple-element.9.refs_1_), channel_id=1, source_target_pairs={{0,5},{1,4},{4,9},{5,8},{8,13},{9,12},{12,15},{13,14},{14,11},{15,... | collective-permute-start | bytes 442376 | tf_op jit(solution)/shard_map/ppermute | solution.py:39
  7.7 2.4 %collective-permute-done.5.refs_2_ = bf16[64,1152]{1,0:T(8,128)(2,1)S(1)} collective-permute-done((bf16[64,1152]{1,0:T(8,128)(2,1)S(1)}, bf16[64,1152]{1,0:T(8,128)(2,1)S(1)}, u32[]{:S(2)}, u32[]{:S(2)}) %collective-permute-start.5) | collective-permute-done | bytes 147488 | tf_op jit(solution)/shard_map/ppermute | solution.py:39
  10.2 2.2 %collective-permute-start.6 = (bf16[64,1152]{1,0:T(8,128)(2,1)S(1)}, bf16[64,1152]{1,0:T(8,128)(2,1)S(1)}, u32[]{:S(2)}, u32[]{:S(2)}) collective-permute-start(bf16[64,1152]{1,0:T(8,128)(2,1)S(1)} %collective-permute-done.5.refs_2_), channel_id=1, source_target_pairs={{0,5},{1,4},{4,9},{5,8},{8,13},{9,12},{12,15},{13,14},{14,11},{15,... | collective-permute-start | bytes 442376 | tf_op jit(solution)/shard_map/ppermute | solution.py:39
  12.4 0.9 %collective-permute-done.9.refs_3_ = bf16[64,1152]{1,0:T(8,128)(2,1)S(1)} collective-permute-done((bf16[64,1152]{1,0:T(8,128)(2,1)S(1)}, bf16[64,1152]{1,0:T(8,128)(2,1)S(1)}, u32[]{:S(2)}, u32[]{:S(2)}) %collective-permute-start.9) | collective-permute-done | bytes 147488 | tf_op jit(solution)/shard_map/ppermute | solution.py:39
  13.2 2.2 %collective-permute-start.10 = (bf16[64,1152]{1,0:T(8,128)(2,1)S(1)}, bf16[64,1152]{1,0:T(8,128)(2,1)S(1)}, u32[]{:S(2)}, u32[]{:S(2)}) collective-permute-start(bf16[64,1152]{1,0:T(8,128)(2,1)S(1)} %collective-permute-done.9.refs_3_), channel_id=1, source_target_pairs={{0,5},{1,4},{4,9},{5,8},{8,13},{9,12},{12,15},{13,14},{14,11},{15,... | collective-permute-start | bytes 442376 | tf_op jit(solution)/shard_map/ppermute | solution.py:39
  15.4 1.1 %collective-permute-done.6.refs_6_ = bf16[64,1152]{1,0:T(8,128)(2,1)S(1)} collective-permute-done((bf16[64,1152]{1,0:T(8,128)(2,1)S(1)}, bf16[64,1152]{1,0:T(8,128)(2,1)S(1)}, u32[]{:S(2)}, u32[]{:S(2)}) %collective-permute-start.6) | collective-permute-done | bytes 147488 | tf_op jit(solution)/shard_map/ppermute | solution.py:39
  16.5 2.2 %collective-permute-start.7 = (bf16[64,1152]{1,0:T(8,128)(2,1)S(1)}, bf16[64,1152]{1,0:T(8,128)(2,1)S(1)}, u32[]{:S(2)}, u32[]{:S(2)}) collective-permute-start(bf16[64,1152]{1,0:T(8,128)(2,1)S(1)} %collective-permute-done.6.refs_6_), channel_id=1, source_target_pairs={{0,5},{1,4},{4,9},{5,8},{8,13},{9,12},{12,15},{13,14},{14,11},{15,... | collective-permute-start | bytes 442376 | tf_op jit(solution)/shard_map/ppermute | solution.py:39
  18.7 0.9 %collective-permute-done.10.refs_7_ = bf16[64,1152]{1,0:T(8,128)(2,1)S(1)} collective-permute-done((bf16[64,1152]{1,0:T(8,128)(2,1)S(1)}, bf16[64,1152]{1,0:T(8,128)(2,1)S(1)}, u32[]{:S(2)}, u32[]{:S(2)}) %collective-permute-start.10) | collective-permute-done | bytes 147488 | tf_op jit(solution)/shard_map/ppermute | solution.py:39
  19.6 2.2 %collective-permute-start.11 = (bf16[64,1152]{1,0:T(8,128)(2,1)S(1)}, bf16[64,1152]{1,0:T(8,128)(2,1)S(1)}, u32[]{:S(2)}, u32[]{:S(2)}) collective-permute-start(bf16[64,1152]{1,0:T(8,128)(2,1)S(1)} %collective-permute-done.10.refs_7_), channel_id=1, source_target_pairs={{0,5},{1,4},{4,9},{5,8},{8,13},{9,12},{12,15},{13,14},{14,11},{15,... | collective-permute-start | bytes 442376 | tf_op jit(solution)/shard_map/ppermute | solution.py:39
  21.8 1.0 %collective-permute-done.7.refs_0_ = bf16[64,1152]{1,0:T(8,128)(2,1)S(1)} collective-permute-done((bf16[64,1152]{1,0:T(8,128)(2,1)S(1)}, bf16[64,1152]{1,0:T(8,128)(2,1)S(1)}, u32[]{:S(2)}, u32[]{:S(2)}) %collective-permute-start.7) | collective-permute-done | bytes 147488 | tf_op jit(solution)/shard_map/ppermute | solution.py:39
  22.7 2.2 %collective-permute-start.8 = (bf16[64,1152]{1,0:T(8,128)(2,1)S(1)}, bf16[64,1152]{1,0:T(8,128)(2,1)S(1)}, u32[]{:S(2)}, u32[]{:S(2)}) collective-permute-start(bf16[64,1152]{1,0:T(8,128)(2,1)S(1)} %collective-permute-done.7.refs_0_), channel_id=1, source_target_pairs={{0,5},{1,4},{4,9},{5,8},{8,13},{9,12},{12,15},{13,14},{14,11},{15,... | collective-permute-start | bytes 442376 | tf_op jit(solution)/shard_map/ppermute | solution.py:39
  25.0 1.8 %shard_map.65.refs_4_ = f32[256,128]{1,0:T(8,128)S(1)} custom-call(bf16[128,8192]{1,0:T(8,128)(2,1)S(1)} %copy-done.2, bf16[128,28672]{1,0:T(8,128)(2,1)S(1)} %copy-done.1, bf16[8,128,2304]{2,1,0:T(8,128)(2,1)S(1)} %collective-permute-done.theirs, bf16[64,1152]{1,0:T(8,128)(2,1)S(1)} %get-tuple-element.10.refs_0_, ...), custom_call_target="tpu_custom_call" | custom-call | flops 377487360 | bytes 7372800 | tf_op jit(solution)/shard_map/pallas_call | solution.py:137
  26.7 1.1 %collective-permute-done.14.refs_2_ = bf16[64,1152]{1,0:T(8,128)(2,1)S(1)} collective-permute-done((bf16[64,1152]{1,0:T(8,128)(2,1)S(1)}, bf16[64,1152]{1,0:T(8,128)(2,1)S(1)}, u32[]{:S(2)}, u32[]{:S(2)}) %collective-permute-start.14) | collective-permute-done | bytes 147488 | tf_op jit(solution)/shard_map/ppermute | solution.py:39
  27.9 0.8 %shard_map.66.refs_1_ = f32[256,128]{1,0:T(8,128)S(1)} custom-call(bf16[128,8192]{1,0:T(8,128)(2,1)S(1)} %copy-done.2, bf16[128,28672]{1,0:T(8,128)(2,1)S(1)} %copy-done.1, bf16[8,128,2304]{2,1,0:T(8,128)(2,1)S(1)} %collective-permute-done.theirs, bf16[64,1152]{1,0:T(8,128)(2,1)S(1)} %collective-permute-done.7.refs_0_, ...), custom_call_target="tpu_custom_call" | custom-call | flops 150994944 | bytes 2949120 | tf_op jit(solution)/shard_map/pallas_call | solution.py:137
  28.8 0.4 shard_map.67.refs_1_
  29.2 1.7 %collective-permute-done.4.refs_0_ = bf16[64,1152]{1,0:T(8,128)(2,1)S(1)} collective-permute-done((bf16[64,1152]{1,0:T(8,128)(2,1)S(1)}, bf16[64,1152]{1,0:T(8,128)(2,1)S(1)}, u32[]{:S(2)}, u32[]{:S(2)}) %collective-permute-start.4) | collective-permute-done | bytes 147488 | tf_op jit(solution)/shard_map/ppermute | solution.py:39
  31.5 1.2 %collective-permute-done.15 = f32[256,128]{1,0:T(8,128)S(1)} collective-permute-done((f32[256,128]{1,0:T(8,128)S(1)}, f32[256,128]{1,0:T(8,128)S(1)}, u32[]{:S(2)}, u32[]{:S(2)}) %collective-permute-start.15) | collective-permute-done | bytes 131104 | tf_op jit(solution)/shard_map/ppermute | solution.py:43
  33.1 12.4 %all_to_all.10 = f32[8,32,128]{2,1,0:T(8,128)S(1)} all-to-all(f32[8,32,128]{2,1,0:T(8,128)S(1)} %broadcast_in_dim.14), channel_id=1, replica_groups={{0,2,4,6,8,10,12,14},{1,3,5,7,9,11,13,15},{16,18,20,22,24,26,28,30},{17..., dimensions={0} | all-to-all | bytes 262144 | tf_op jit(solution)/shard_map/all_to_all | solution.py:171
  45.6 0.6 %convolution_convert_fusion = bf16[2,256]{1,0:T(2,128)(2,1)S(1)} fusion(bf16[256,4096]{1,0:T(8,128)(2,1)S(1)} %copy-done, bf16[1,2,32,128]{3,2,1,0:T(8,128)(2,1)S(1)} %bitcast.13), kind=kOutput, calls=%fused_computation.1 | convolution fusion | flops 4194816 | bytes 2114560 | tf_op jit(solution)/shard_map/dot_general | solution.py:23
  46.2 9.1 %all_to_all.11.conditioned = bf16[16,2,256]{2,1,0:T(2,128)(2,1)S(1)} all-to-all(bf16[16,2,256]{2,1,0:T(2,128)(2,1)S(1)} %broadcast_in_dim.15), channel_id=1, replica_groups={{0,1,2,3,4,5,6,7,8,9,10,11,12,13,14,15},{16,17,18,19,20,21,22,23,24,25,..., dimensions={0} | all-to-all | bytes 32768 | tf_op jit(solution)/shard_map/all_to_all | solution.py:171
  55.3 0.7 %shard_map.69 = f32[2,8]{1,0:T(2,128)} custom-call(bf16[16,2,256]{2,1,0:T(2,128)(2,1)S(1)} %all_to_all.11.conditioned, bf16[8,4096]{1,0:T(8,128)(2,1)S(1)} %copy-done.3), custom_call_target="tpu_custom_call" | custom-call | tf_op jit(solution)/shard_map/pallas_call | solution.py:160
  (32 shorter events, 1.1 us)
Async XLA Ops:
  0.0 45.5 %copy-start = (bf16[256,4096]{1,0:T(8,128)(2,1)S(1)}, bf16[256,4096]{1,0:T(8,128)(2,1)}, u32[]{:S(2)}) copy-start(bf16[256,4096]{1,0:T(8,128)(2,1)} %param.10) | copy-start | bytes 6291460
  0.0 24.9 %copy-start.1 = (bf16[128,28672]{1,0:T(8,128)(2,1)S(1)}, bf16[128,28672]{1,0:T(8,128)(2,1)}, u32[]{:S(2)}) copy-start(bf16[128,28672]{1,0:T(8,128)(2,1)} %grad.9) | copy-start | bytes 22020100
  0.0 24.9 %copy-start.2 = (bf16[128,8192]{1,0:T(8,128)(2,1)S(1)}, bf16[128,8192]{1,0:T(8,128)(2,1)}, u32[]{:S(2)}) copy-start(bf16[128,8192]{1,0:T(8,128)(2,1)} %act.9) | copy-start | bytes 6291460
  2.8 22.2 %collective-permute-start = (bf16[8,128,2304]{2,1,0:T(8,128)(2,1)S(1)}, bf16[8,128,2304]{2,1,0:T(8,128)(2,1)S(1)}, u32[]{:S(2)}, u32[]{:S(2)}) collective-permute-start(bf16[8,128,2304]{2,1,0:T(8,128)(2,1)S(1)} %get-tuple-element.8), channel_id=1, source_target_pairs={{0,1},{1,0},{2,3},{3,2},{4,5},{5,4},{6,7},{7,6},{8,9},{9,8},{10,11... | collective-permute-start | bytes 14155784 | tf_op jit(solution)/shard_map/ppermute | solution.py:43
  3.3 6.9 %collective-permute-start.5 = (bf16[64,1152]{1,0:T(8,128)(2,1)S(1)}, bf16[64,1152]{1,0:T(8,128)(2,1)S(1)}, u32[]{:S(2)}, u32[]{:S(2)}) collective-permute-start(bf16[64,1152]{1,0:T(8,128)(2,1)S(1)} %get-tuple-element.10.refs_0_), channel_id=1, source_target_pairs={{0,5},{1,4},{4,9},{5,8},{8,13},{9,12},{12,15},{13,14},{14,11},{15,... | collective-permute-start | bytes 442376 | tf_op jit(solution)/shard_map/ppermute | solution.py:39
  6.0 6.4 %collective-permute-start.1 = (bf16[64,1152]{1,0:T(8,128)(2,1)S(1)}, bf16[64,1152]{1,0:T(8,128)(2,1)S(1)}, u32[]{:S(2)}, u32[]{:S(2)}) collective-permute-start(bf16[64,1152]{1,0:T(8,128)(2,1)S(1)} %get-tuple-element.9.refs_1_), channel_id=1, source_target_pairs={{0,3},{1,2},{4,1},{5,0},{8,5},{9,4},{12,9},{13,8},{14,13},{15,12},... | collective-permute-start | bytes 442376 | tf_op jit(solution)/shard_map/ppermute | solution.py:39
  6.0 7.3 %collective-permute-start.9 = (bf16[64,1152]{1,0:T(8,128)(2,1)S(1)}, bf16[64,1152]{1,0:T(8,128)(2,1)S(1)}, u32[]{:S(2)}, u32[]{:S(2)}) collective-permute-start(bf16[64,1152]{1,0:T(8,128)(2,1)S(1)} %get-tuple-element.9.refs_1_), channel_id=1, source_target_pairs={{0,5},{1,4},{4,9},{5,8},{8,13},{9,12},{12,15},{13,14},{14,11},{15,... | collective-permute-start | bytes 442376 | tf_op jit(solution)/shard_map/ppermute | solution.py:39
  7.7 7.7 %collective-permute-start.12 = (bf16[64,1152]{1,0:T(8,128)(2,1)S(1)}, bf16[64,1152]{1,0:T(8,128)(2,1)S(1)}, u32[]{:S(2)}, u32[]{:S(2)}) collective-permute-start(bf16[64,1152]{1,0:T(8,128)(2,1)S(1)} %get-tuple-element.10.refs_0_), channel_id=1, source_target_pairs={{0,3},{1,2},{4,1},{5,0},{8,5},{9,4},{12,9},{13,8},{14,13},{15,12},... | collective-permute-start | bytes 442376 | tf_op jit(solution)/shard_map/ppermute | solution.py:39
  10.2 6.3 %collective-permute-start.6 = (bf16[64,1152]{1,0:T(8,128)(2,1)S(1)}, bf16[64,1152]{1,0:T(8,128)(2,1)S(1)}, u32[]{:S(2)}, u32[]{:S(2)}) collective-permute-start(bf16[64,1152]{1,0:T(8,128)(2,1)S(1)} %collective-permute-done.5.refs_2_), channel_id=1, source_target_pairs={{0,5},{1,4},{4,9},{5,8},{8,13},{9,12},{12,15},{13,14},{14,11},{15,... | collective-permute-start | bytes 442376 | tf_op jit(solution)/shard_map/ppermute | solution.py:39
  12.4 6.3 %collective-permute-start.2 = (bf16[64,1152]{1,0:T(8,128)(2,1)S(1)}, bf16[64,1152]{1,0:T(8,128)(2,1)S(1)}, u32[]{:S(2)}, u32[]{:S(2)}) collective-permute-start(bf16[64,1152]{1,0:T(8,128)(2,1)S(1)} %collective-permute-done.1.refs_5_), channel_id=1, source_target_pairs={{0,3},{1,2},{4,1},{5,0},{8,5},{9,4},{12,9},{13,8},{14,13},{15,12},... | collective-permute-start | bytes 442376 | tf_op jit(solution)/shard_map/ppermute | solution.py:39
  13.2 6.3 %collective-permute-start.10 = (bf16[64,1152]{1,0:T(8,128)(2,1)S(1)}, bf16[64,1152]{1,0:T(8,128)(2,1)S(1)}, u32[]{:S(2)}, u32[]{:S(2)}) collective-permute-start(bf16[64,1152]{1,0:T(8,128)(2,1)S(1)} %collective-permute-done.9.refs_3_), channel_id=1, source_target_pairs={{0,5},{1,4},{4,9},{5,8},{8,13},{9,12},{12,15},{13,14},{14,11},{15,... | collective-permute-start | bytes 442376 | tf_op jit(solution)/shard_map/ppermute | solution.py:39
  15.4 6.4 %collective-permute-start.13 = (bf16[64,1152]{1,0:T(8,128)(2,1)S(1)}, bf16[64,1152]{1,0:T(8,128)(2,1)S(1)}, u32[]{:S(2)}, u32[]{:S(2)}) collective-permute-start(bf16[64,1152]{1,0:T(8,128)(2,1)S(1)} %collective-permute-done.12.refs_4_), channel_id=1, source_target_pairs={{0,3},{1,2},{4,1},{5,0},{8,5},{9,4},{12,9},{13,8},{14,13},{15,12},... | collective-permute-start | bytes 442376 | tf_op jit(solution)/shard_map/ppermute | solution.py:39
  16.5 6.3 %collective-permute-start.7 = (bf16[64,1152]{1,0:T(8,128)(2,1)S(1)}, bf16[64,1152]{1,0:T(8,128)(2,1)S(1)}, u32[]{:S(2)}, u32[]{:S(2)}) collective-permute-start(bf16[64,1152]{1,0:T(8,128)(2,1)S(1)} %collective-permute-done.6.refs_6_), channel_id=1, source_target_pairs={{0,5},{1,4},{4,9},{5,8},{8,13},{9,12},{12,15},{13,14},{14,11},{15,... | collective-permute-start | bytes 442376 | tf_op jit(solution)/shard_map/ppermute | solution.py:39
  18.7 6.3 %collective-permute-start.3 = (bf16[64,1152]{1,0:T(8,128)(2,1)S(1)}, bf16[64,1152]{1,0:T(8,128)(2,1)S(1)}, u32[]{:S(2)}, u32[]{:S(2)}) collective-permute-start(bf16[64,1152]{1,0:T(8,128)(2,1)S(1)} %collective-permute-done.2.refs_9_), channel_id=1, source_target_pairs={{0,3},{1,2},{4,1},{5,0},{8,5},{9,4},{12,9},{13,8},{14,13},{15,12},... | collective-permute-start | bytes 442376 | tf_op jit(solution)/shard_map/ppermute | solution.py:39
  19.6 7.2 %collective-permute-start.11 = (bf16[64,1152]{1,0:T(8,128)(2,1)S(1)}, bf16[64,1152]{1,0:T(8,128)(2,1)S(1)}, u32[]{:S(2)}, u32[]{:S(2)}) collective-permute-start(bf16[64,1152]{1,0:T(8,128)(2,1)S(1)} %collective-permute-done.10.refs_7_), channel_id=1, source_target_pairs={{0,5},{1,4},{4,9},{5,8},{8,13},{9,12},{12,15},{13,14},{14,11},{15,... | collective-permute-start | bytes 442376 | tf_op jit(solution)/shard_map/ppermute | solution.py:39
  21.8 6.1 %collective-permute-start.14 = (bf16[64,1152]{1,0:T(8,128)(2,1)S(1)}, bf16[64,1152]{1,0:T(8,128)(2,1)S(1)}, u32[]{:S(2)}, u32[]{:S(2)}) collective-permute-start(bf16[64,1152]{1,0:T(8,128)(2,1)S(1)} %collective-permute-done.13.refs_8_), channel_id=1, source_target_pairs={{0,3},{1,2},{4,1},{5,0},{8,5},{9,4},{12,9},{13,8},{14,13},{15,12},... | collective-permute-start | bytes 442376 | tf_op jit(solution)/shard_map/ppermute | solution.py:39
  22.7 6.1 %collective-permute-start.8 = (bf16[64,1152]{1,0:T(8,128)(2,1)S(1)}, bf16[64,1152]{1,0:T(8,128)(2,1)S(1)}, u32[]{:S(2)}, u32[]{:S(2)}) collective-permute-start(bf16[64,1152]{1,0:T(8,128)(2,1)S(1)} %collective-permute-done.7.refs_0_), channel_id=1, source_target_pairs={{0,5},{1,4},{4,9},{5,8},{8,13},{9,12},{12,15},{13,14},{14,11},{15,... | collective-permute-start | bytes 442376 | tf_op jit(solution)/shard_map/ppermute | solution.py:39
  24.9 6.0 %collective-permute-start.4 = (bf16[64,1152]{1,0:T(8,128)(2,1)S(1)}, bf16[64,1152]{1,0:T(8,128)(2,1)S(1)}, u32[]{:S(2)}, u32[]{:S(2)}) collective-permute-start(bf16[64,1152]{1,0:T(8,128)(2,1)S(1)} %collective-permute-done.3.refs_3_), channel_id=1, source_target_pairs={{0,3},{1,2},{4,1},{5,0},{8,5},{9,4},{12,9},{13,8},{14,13},{15,12},... | collective-permute-start | bytes 442376 | tf_op jit(solution)/shard_map/ppermute | solution.py:39
  31.3 24.0 %copy-start.3 = (bf16[8,4096]{1,0:T(8,128)(2,1)S(1)}, bf16[8,4096]{1,0:T(8,128)(2,1)}, u32[]{:S(2)}) copy-start(bf16[8,4096]{1,0:T(8,128)(2,1)} %queries.1) | copy-start | bytes 196612
  31.3 1.4 %collective-permute-start.15 = (f32[256,128]{1,0:T(8,128)S(1)}, f32[256,128]{1,0:T(8,128)S(1)}, u32[]{:S(2)}, u32[]{:S(2)}) collective-permute-start(f32[256,128]{1,0:T(8,128)S(1)} %shard_map.68), channel_id=1, source_target_pairs={{0,1},{1,0},{2,3},{3,2},{4,5},{5,4},{6,7},{7,6},{8,9},{9,8},{10,11... | collective-permute-start | bytes 393224 | tf_op jit(solution)/shard_map/ppermute | solution.py:43

commit v18 on v17

--- a/solution.py
+++ b/solution.py
@@ -203,8 +203,8 @@
 
     raw = dot(total[:, rank:], total[:, :rank], TN)
     raw = (raw * (1.0 / math.sqrt(LEN))).reshape(-1, 128)
-    planes = [[2 * i + c for i in range(chips)] for c in range(2)]
-    raw = to_all(raw, planes)
+    groups = [[2 * i + (c ^ (i & 1)) for i in range(chips)] for c in range(2)]
+    raw = to_all(raw, groups)
     features = raw.reshape((-1, split // 2) + raw.shape[1:]).sum(axis=1)
     features = features.astype(jnp.bfloat16).reshape(-1, rank * rank)
 

time: 56.2 us -> 56.7 us (level)
  no operation moved by 1% of the time
where the time goes in v18:
time: 56.7 us; the launch traced here: 56.6 us
  blocking collectives  22 us (39%)
  starting transfers between devices  16.1 us (28%)
  waiting for transfers between devices  10.4 us (18%)
  Pallas kernels  6.81 us (12%)
  matrix products  0.89 us (2%)
    all_to_all x2, blocking collectives, to_all(): lax.all_to_all(copies, 'dp', 0, 0, axis_index_groups=groups, tiled=True)  22 us
    ppermute x14, starting transfers between devices, ring(): return lax.ppermute(x, 'dp', pairs)  15.4 us
    ppermute x14, waiting for transfers between devices, ring(): return lax.ppermute(x, 'dp', pairs)  9.17 us
    pallas_call x4, Pallas kernels, project(): pl.pallas_call(functools.partial(project_kernel, chips, items, a_width, c...  3.34 us
    pallas_call x1, Pallas kernels, start(): pl.pallas_call(functools.partial(start_kernel, chips), out_shape=[pltpu.V...  2.74 us
    ppermute x2, waiting for transfers between devices, swap(): return lax.ppermute(x, 'dp', [(i, i ^ bit) for i in range(n)])  1.24 us
  transfers between devices with their start and end apart: 16, of which 9 were waited for; matrix products, arithmetic and copies ran while one was open for 0% of the time, Pallas kernels for 5%

profile of v18, /device:TPU:0, one launch (start us, length us, event | category | flops | bytes accessed | tf_op | source)
XLA Modules:
  0.0 56.6 jit_solution(7034845867263625753)
XLA Ops:
  0.0 2.7 %shard_map.64 = (bf16[64,1152]{1,0:T(8,128)(2,1)S(1)}, bf16[64,1152]{1,0:T(8,128)(2,1)S(1)}, bf16[8,128,2304]{2,1,0:T(8,128)(2,1)S(1)}) custom-call(bf16[128,8192]{1,0:T(8,128)(2,1)} %act.9, bf16[128,28672]{1,0:T(8,128)(2,1)} %grad.9, bf16[64,512]{1,0:T(8,128)(2,1)} %bitcast.12, bf16[64,1792]{1,0:T(8,128)(2,1)} %bitcast.11), custom_call_target="tpu_custom_call" | custom-call | bytes 10027008 | tf_op jit(solution)/shard_map/pallas_call | solution.py:90
  2.8 0.5 collective-permute-start
  3.3 2.7 %collective-permute-start.5 = (bf16[64,1152]{1,0:T(8,128)(2,1)S(1)}, bf16[64,1152]{1,0:T(8,128)(2,1)S(1)}, u32[]{:S(2)}, u32[]{:S(2)}) collective-permute-start(bf16[64,1152]{1,0:T(8,128)(2,1)S(1)} %get-tuple-element.10.refs_0_), channel_id=1, source_target_pairs={{0,5},{1,4},{4,9},{5,8},{8,13},{9,12},{12,15},{13,14},{14,11},{15,... | collective-permute-start | bytes 442376 | tf_op jit(solution)/shard_map/ppermute | solution.py:39
  6.0 1.7 %collective-permute-start.9 = (bf16[64,1152]{1,0:T(8,128)(2,1)S(1)}, bf16[64,1152]{1,0:T(8,128)(2,1)S(1)}, u32[]{:S(2)}, u32[]{:S(2)}) collective-permute-start(bf16[64,1152]{1,0:T(8,128)(2,1)S(1)} %get-tuple-element.9.refs_1_), channel_id=1, source_target_pairs={{0,5},{1,4},{4,9},{5,8},{8,13},{9,12},{12,15},{13,14},{14,11},{15,... | collective-permute-start | bytes 442376 | tf_op jit(solution)/shard_map/ppermute | solution.py:39
  7.7 2.4 %collective-permute-done.5.refs_2_ = bf16[64,1152]{1,0:T(8,128)(2,1)S(1)} collective-permute-done((bf16[64,1152]{1,0:T(8,128)(2,1)S(1)}, bf16[64,1152]{1,0:T(8,128)(2,1)S(1)}, u32[]{:S(2)}, u32[]{:S(2)}) %collective-permute-start.5) | collective-permute-done | bytes 147488 | tf_op jit(solution)/shard_map/ppermute | solution.py:39
  10.2 2.2 %collective-permute-start.6 = (bf16[64,1152]{1,0:T(8,128)(2,1)S(1)}, bf16[64,1152]{1,0:T(8,128)(2,1)S(1)}, u32[]{:S(2)}, u32[]{:S(2)}) collective-permute-start(bf16[64,1152]{1,0:T(8,128)(2,1)S(1)} %collective-permute-done.5.refs_2_), channel_id=1, source_target_pairs={{0,5},{1,4},{4,9},{5,8},{8,13},{9,12},{12,15},{13,14},{14,11},{15,... | collective-permute-start | bytes 442376 | tf_op jit(solution)/shard_map/ppermute | solution.py:39
  12.4 0.9 %collective-permute-done.9.refs_3_ = bf16[64,1152]{1,0:T(8,128)(2,1)S(1)} collective-permute-done((bf16[64,1152]{1,0:T(8,128)(2,1)S(1)}, bf16[64,1152]{1,0:T(8,128)(2,1)S(1)}, u32[]{:S(2)}, u32[]{:S(2)}) %collective-permute-start.9) | collective-permute-done | bytes 147488 | tf_op jit(solution)/shard_map/ppermute | solution.py:39
  13.2 2.2 %collective-permute-start.10 = (bf16[64,1152]{1,0:T(8,128)(2,1)S(1)}, bf16[64,1152]{1,0:T(8,128)(2,1)S(1)}, u32[]{:S(2)}, u32[]{:S(2)}) collective-permute-start(bf16[64,1152]{1,0:T(8,128)(2,1)S(1)} %collective-permute-done.9.refs_3_), channel_id=1, source_target_pairs={{0,5},{1,4},{4,9},{5,8},{8,13},{9,12},{12,15},{13,14},{14,11},{15,... | collective-permute-start | bytes 442376 | tf_op jit(solution)/shard_map/ppermute | solution.py:39
  15.4 1.1 %collective-permute-done.6.refs_6_ = bf16[64,1152]{1,0:T(8,128)(2,1)S(1)} collective-permute-done((bf16[64,1152]{1,0:T(8,128)(2,1)S(1)}, bf16[64,1152]{1,0:T(8,128)(2,1)S(1)}, u32[]{:S(2)}, u32[]{:S(2)}) %collective-permute-start.6) | collective-permute-done | bytes 147488 | tf_op jit(solution)/shard_map/ppermute | solution.py:39
  16.5 2.2 %collective-permute-start.7 = (bf16[64,1152]{1,0:T(8,128)(2,1)S(1)}, bf16[64,1152]{1,0:T(8,128)(2,1)S(1)}, u32[]{:S(2)}, u32[]{:S(2)}) collective-permute-start(bf16[64,1152]{1,0:T(8,128)(2,1)S(1)} %collective-permute-done.6.refs_6_), channel_id=1, source_target_pairs={{0,5},{1,4},{4,9},{5,8},{8,13},{9,12},{12,15},{13,14},{14,11},{15,... | collective-permute-start | bytes 442376 | tf_op jit(solution)/shard_map/ppermute | solution.py:39
  18.7 0.9 %collective-permute-done.10.refs_7_ = bf16[64,1152]{1,0:T(8,128)(2,1)S(1)} collective-permute-done((bf16[64,1152]{1,0:T(8,128)(2,1)S(1)}, bf16[64,1152]{1,0:T(8,128)(2,1)S(1)}, u32[]{:S(2)}, u32[]{:S(2)}) %collective-permute-start.10) | collective-permute-done | bytes 147488 | tf_op jit(solution)/shard_map/ppermute | solution.py:39
  19.6 2.2 %collective-permute-start.11 = (bf16[64,1152]{1,0:T(8,128)(2,1)S(1)}, bf16[64,1152]{1,0:T(8,128)(2,1)S(1)}, u32[]{:S(2)}, u32[]{:S(2)}) collective-permute-start(bf16[64,1152]{1,0:T(8,128)(2,1)S(1)} %collective-permute-done.10.refs_7_), channel_id=1, source_target_pairs={{0,5},{1,4},{4,9},{5,8},{8,13},{9,12},{12,15},{13,14},{14,11},{15,... | collective-permute-start | bytes 442376 | tf_op jit(solution)/shard_map/ppermute | solution.py:39
  21.8 1.0 %collective-permute-done.7.refs_0_ = bf16[64,1152]{1,0:T(8,128)(2,1)S(1)} collective-permute-done((bf16[64,1152]{1,0:T(8,128)(2,1)S(1)}, bf16[64,1152]{1,0:T(8,128)(2,1)S(1)}, u32[]{:S(2)}, u32[]{:S(2)}) %collective-permute-start.7) | collective-permute-done | bytes 147488 | tf_op jit(solution)/shard_map/ppermute | solution.py:39
  22.7 2.2 %collective-permute-start.8 = (bf16[64,1152]{1,0:T(8,128)(2,1)S(1)}, bf16[64,1152]{1,0:T(8,128)(2,1)S(1)}, u32[]{:S(2)}, u32[]{:S(2)}) collective-permute-start(bf16[64,1152]{1,0:T(8,128)(2,1)S(1)} %collective-permute-done.7.refs_0_), channel_id=1, source_target_pairs={{0,5},{1,4},{4,9},{5,8},{8,13},{9,12},{12,15},{13,14},{14,11},{15,... | collective-permute-start | bytes 442376 | tf_op jit(solution)/shard_map/ppermute | solution.py:39
  25.0 1.8 %shard_map.65.refs_4_ = f32[256,128]{1,0:T(8,128)S(1)} custom-call(bf16[128,8192]{1,0:T(8,128)(2,1)S(1)} %copy-done.2, bf16[128,28672]{1,0:T(8,128)(2,1)S(1)} %copy-done.1, bf16[8,128,2304]{2,1,0:T(8,128)(2,1)S(1)} %collective-permute-done.theirs, bf16[64,1152]{1,0:T(8,128)(2,1)S(1)} %get-tuple-element.10.refs_0_, ...), custom_call_target="tpu_custom_call" | custom-call | flops 377487360 | bytes 7372800 | tf_op jit(solution)/shard_map/pallas_call | solution.py:137
  26.7 1.1 %collective-permute-done.14.refs_2_ = bf16[64,1152]{1,0:T(8,128)(2,1)S(1)} collective-permute-done((bf16[64,1152]{1,0:T(8,128)(2,1)S(1)}, bf16[64,1152]{1,0:T(8,128)(2,1)S(1)}, u32[]{:S(2)}, u32[]{:S(2)}) %collective-permute-start.14) | collective-permute-done | bytes 147488 | tf_op jit(solution)/shard_map/ppermute | solution.py:39
  27.9 0.8 %shard_map.66.refs_1_ = f32[256,128]{1,0:T(8,128)S(1)} custom-call(bf16[128,8192]{1,0:T(8,128)(2,1)S(1)} %copy-done.2, bf16[128,28672]{1,0:T(8,128)(2,1)S(1)} %copy-done.1, bf16[8,128,2304]{2,1,0:T(8,128)(2,1)S(1)} %collective-permute-done.theirs, bf16[64,1152]{1,0:T(8,128)(2,1)S(1)} %collective-permute-done.7.refs_0_, ...), custom_call_target="tpu_custom_call" | custom-call | flops 150994944 | bytes 2949120 | tf_op jit(solution)/shard_map/pallas_call | solution.py:137
  28.8 0.4 shard_map.67.refs_1_
  29.2 1.7 %collective-permute-done.4.refs_0_ = bf16[64,1152]{1,0:T(8,128)(2,1)S(1)} collective-permute-done((bf16[64,1152]{1,0:T(8,128)(2,1)S(1)}, bf16[64,1152]{1,0:T(8,128)(2,1)S(1)}, u32[]{:S(2)}, u32[]{:S(2)}) %collective-permute-start.4) | collective-permute-done | bytes 147488 | tf_op jit(solution)/shard_map/ppermute | solution.py:39
  31.5 1.2 %collective-permute-done.15 = f32[256,128]{1,0:T(8,128)S(1)} collective-permute-done((f32[256,128]{1,0:T(8,128)S(1)}, f32[256,128]{1,0:T(8,128)S(1)}, u32[]{:S(2)}, u32[]{:S(2)}) %collective-permute-start.15) | collective-permute-done | bytes 131104 | tf_op jit(solution)/shard_map/ppermute | solution.py:43
  33.1 12.7 %all_to_all.10 = f32[8,32,128]{2,1,0:T(8,128)S(1)} all-to-all(f32[8,32,128]{2,1,0:T(8,128)S(1)} %broadcast_in_dim.14), channel_id=1, replica_groups={{0,3,4,7,8,11,12,15},{1,2,5,6,9,10,13,14},{16,19,20,23,24,27,28,31},{17..., dimensions={0} | all-to-all | bytes 262144 | tf_op jit(solution)/shard_map/all_to_all | solution.py:171
  45.8 0.6 %convolution_convert_fusion = bf16[2,256]{1,0:T(2,128)(2,1)S(1)} fusion(bf16[256,4096]{1,0:T(8,128)(2,1)S(1)} %copy-done, bf16[1,2,32,128]{3,2,1,0:T(8,128)(2,1)S(1)} %bitcast.13), kind=kOutput, calls=%fused_computation.1 | convolution fusion | flops 4194816 | bytes 2114560 | tf_op jit(solution)/shard_map/dot_general | solution.py:23
  46.5 9.3 %all_to_all.11.conditioned = bf16[16,2,256]{2,1,0:T(2,128)(2,1)S(1)} all-to-all(bf16[16,2,256]{2,1,0:T(2,128)(2,1)S(1)} %broadcast_in_dim.15), channel_id=1, replica_groups={{0,1,2,3,4,5,6,7,8,9,10,11,12,13,14,15},{16,17,18,19,20,21,22,23,24,25,..., dimensions={0} | all-to-all | bytes 32768 | tf_op jit(solution)/shard_map/all_to_all | solution.py:171
  55.8 0.7 %shard_map.69 = f32[2,8]{1,0:T(2,128)} custom-call(bf16[16,2,256]{2,1,0:T(2,128)(2,1)S(1)} %all_to_all.11.conditioned, bf16[8,4096]{1,0:T(8,128)(2,1)S(1)} %copy-done.3), custom_call_target="tpu_custom_call" | custom-call | tf_op jit(solution)/shard_map/pallas_call | solution.py:160
  (32 shorter events, 1.1 us)
Async XLA Ops:
  0.0 45.8 %copy-start = (bf16[256,4096]{1,0:T(8,128)(2,1)S(1)}, bf16[256,4096]{1,0:T(8,128)(2,1)}, u32[]{:S(2)}) copy-start(bf16[256,4096]{1,0:T(8,128)(2,1)} %param.10) | copy-start | bytes 6291460
  0.0 24.9 %copy-start.1 = (bf16[128,28672]{1,0:T(8,128)(2,1)S(1)}, bf16[128,28672]{1,0:T(8,128)(2,1)}, u32[]{:S(2)}) copy-start(bf16[128,28672]{1,0:T(8,128)(2,1)} %grad.9) | copy-start | bytes 22020100
  0.0 24.9 %copy-start.2 = (bf16[128,8192]{1,0:T(8,128)(2,1)S(1)}, bf16[128,8192]{1,0:T(8,128)(2,1)}, u32[]{:S(2)}) copy-start(bf16[128,8192]{1,0:T(8,128)(2,1)} %act.9) | copy-start | bytes 6291460
  2.8 22.2 %collective-permute-start = (bf16[8,128,2304]{2,1,0:T(8,128)(2,1)S(1)}, bf16[8,128,2304]{2,1,0:T(8,128)(2,1)S(1)}, u32[]{:S(2)}, u32[]{:S(2)}) collective-permute-start(bf16[8,128,2304]{2,1,0:T(8,128)(2,1)S(1)} %get-tuple-element.8), channel_id=1, source_target_pairs={{0,1},{1,0},{2,3},{3,2},{4,5},{5,4},{6,7},{7,6},{8,9},{9,8},{10,11... | collective-permute-start | bytes 14155784 | tf_op jit(solution)/shard_map/ppermute | solution.py:43
  3.3 6.9 %collective-permute-start.5 = (bf16[64,1152]{1,0:T(8,128)(2,1)S(1)}, bf16[64,1152]{1,0:T(8,128)(2,1)S(1)}, u32[]{:S(2)}, u32[]{:S(2)}) collective-permute-start(bf16[64,1152]{1,0:T(8,128)(2,1)S(1)} %get-tuple-element.10.refs_0_), channel_id=1, source_target_pairs={{0,5},{1,4},{4,9},{5,8},{8,13},{9,12},{12,15},{13,14},{14,11},{15,... | collective-permute-start | bytes 442376 | tf_op jit(solution)/shard_map/ppermute | solution.py:39
  6.0 6.4 %collective-permute-start.1 = (bf16[64,1152]{1,0:T(8,128)(2,1)S(1)}, bf16[64,1152]{1,0:T(8,128)(2,1)S(1)}, u32[]{:S(2)}, u32[]{:S(2)}) collective-permute-start(bf16[64,1152]{1,0:T(8,128)(2,1)S(1)} %get-tuple-element.9.refs_1_), channel_id=1, source_target_pairs={{0,3},{1,2},{4,1},{5,0},{8,5},{9,4},{12,9},{13,8},{14,13},{15,12},... | collective-permute-start | bytes 442376 | tf_op jit(solution)/shard_map/ppermute | solution.py:39
  6.0 7.3 %collective-permute-start.9 = (bf16[64,1152]{1,0:T(8,128)(2,1)S(1)}, bf16[64,1152]{1,0:T(8,128)(2,1)S(1)}, u32[]{:S(2)}, u32[]{:S(2)}) collective-permute-start(bf16[64,1152]{1,0:T(8,128)(2,1)S(1)} %get-tuple-element.9.refs_1_), channel_id=1, source_target_pairs={{0,5},{1,4},{4,9},{5,8},{8,13},{9,12},{12,15},{13,14},{14,11},{15,... | collective-permute-start | bytes 442376 | tf_op jit(solution)/shard_map/ppermute | solution.py:39
  7.7 7.7 %collective-permute-start.12 = (bf16[64,1152]{1,0:T(8,128)(2,1)S(1)}, bf16[64,1152]{1,0:T(8,128)(2,1)S(1)}, u32[]{:S(2)}, u32[]{:S(2)}) collective-permute-start(bf16[64,1152]{1,0:T(8,128)(2,1)S(1)} %get-tuple-element.10.refs_0_), channel_id=1, source_target_pairs={{0,3},{1,2},{4,1},{5,0},{8,5},{9,4},{12,9},{13,8},{14,13},{15,12},... | collective-permute-start | bytes 442376 | tf_op jit(solution)/shard_map/ppermute | solution.py:39
  10.2 6.3 %collective-permute-start.6 = (bf16[64,1152]{1,0:T(8,128)(2,1)S(1)}, bf16[64,1152]{1,0:T(8,128)(2,1)S(1)}, u32[]{:S(2)}, u32[]{:S(2)}) collective-permute-start(bf16[64,1152]{1,0:T(8,128)(2,1)S(1)} %collective-permute-done.5.refs_2_), channel_id=1, source_target_pairs={{0,5},{1,4},{4,9},{5,8},{8,13},{9,12},{12,15},{13,14},{14,11},{15,... | collective-permute-start | bytes 442376 | tf_op jit(solution)/shard_map/ppermute | solution.py:39
  12.4 6.3 %collective-permute-start.2 = (bf16[64,1152]{1,0:T(8,128)(2,1)S(1)}, bf16[64,1152]{1,0:T(8,128)(2,1)S(1)}, u32[]{:S(2)}, u32[]{:S(2)}) collective-permute-start(bf16[64,1152]{1,0:T(8,128)(2,1)S(1)} %collective-permute-done.1.refs_5_), channel_id=1, source_target_pairs={{0,3},{1,2},{4,1},{5,0},{8,5},{9,4},{12,9},{13,8},{14,13},{15,12},... | collective-permute-start | bytes 442376 | tf_op jit(solution)/shard_map/ppermute | solution.py:39
  13.2 6.3 %collective-permute-start.10 = (bf16[64,1152]{1,0:T(8,128)(2,1)S(1)}, bf16[64,1152]{1,0:T(8,128)(2,1)S(1)}, u32[]{:S(2)}, u32[]{:S(2)}) collective-permute-start(bf16[64,1152]{1,0:T(8,128)(2,1)S(1)} %collective-permute-done.9.refs_3_), channel_id=1, source_target_pairs={{0,5},{1,4},{4,9},{5,8},{8,13},{9,12},{12,15},{13,14},{14,11},{15,... | collective-permute-start | bytes 442376 | tf_op jit(solution)/shard_map/ppermute | solution.py:39
  15.4 6.4 %collective-permute-start.13 = (bf16[64,1152]{1,0:T(8,128)(2,1)S(1)}, bf16[64,1152]{1,0:T(8,128)(2,1)S(1)}, u32[]{:S(2)}, u32[]{:S(2)}) collective-permute-start(bf16[64,1152]{1,0:T(8,128)(2,1)S(1)} %collective-permute-done.12.refs_4_), channel_id=1, source_target_pairs={{0,3},{1,2},{4,1},{5,0},{8,5},{9,4},{12,9},{13,8},{14,13},{15,12},... | collective-permute-start | bytes 442376 | tf_op jit(solution)/shard_map/ppermute | solution.py:39
  16.5 6.3 %collective-permute-start.7 = (bf16[64,1152]{1,0:T(8,128)(2,1)S(1)}, bf16[64,1152]{1,0:T(8,128)(2,1)S(1)}, u32[]{:S(2)}, u32[]{:S(2)}) collective-permute-start(bf16[64,1152]{1,0:T(8,128)(2,1)S(1)} %collective-permute-done.6.refs_6_), channel_id=1, source_target_pairs={{0,5},{1,4},{4,9},{5,8},{8,13},{9,12},{12,15},{13,14},{14,11},{15,... | collective-permute-start | bytes 442376 | tf_op jit(solution)/shard_map/ppermute | solution.py:39
  18.7 6.3 %collective-permute-start.3 = (bf16[64,1152]{1,0:T(8,128)(2,1)S(1)}, bf16[64,1152]{1,0:T(8,128)(2,1)S(1)}, u32[]{:S(2)}, u32[]{:S(2)}) collective-permute-start(bf16[64,1152]{1,0:T(8,128)(2,1)S(1)} %collective-permute-done.2.refs_9_), channel_id=1, source_target_pairs={{0,3},{1,2},{4,1},{5,0},{8,5},{9,4},{12,9},{13,8},{14,13},{15,12},... | collective-permute-start | bytes 442376 | tf_op jit(solution)/shard_map/ppermute | solution.py:39
  19.6 7.2 %collective-permute-start.11 = (bf16[64,1152]{1,0:T(8,128)(2,1)S(1)}, bf16[64,1152]{1,0:T(8,128)(2,1)S(1)}, u32[]{:S(2)}, u32[]{:S(2)}) collective-permute-start(bf16[64,1152]{1,0:T(8,128)(2,1)S(1)} %collective-permute-done.10.refs_7_), channel_id=1, source_target_pairs={{0,5},{1,4},{4,9},{5,8},{8,13},{9,12},{12,15},{13,14},{14,11},{15,... | collective-permute-start | bytes 442376 | tf_op jit(solution)/shard_map/ppermute | solution.py:39
  21.8 6.1 %collective-permute-start.14 = (bf16[64,1152]{1,0:T(8,128)(2,1)S(1)}, bf16[64,1152]{1,0:T(8,128)(2,1)S(1)}, u32[]{:S(2)}, u32[]{:S(2)}) collective-permute-start(bf16[64,1152]{1,0:T(8,128)(2,1)S(1)} %collective-permute-done.13.refs_8_), channel_id=1, source_target_pairs={{0,3},{1,2},{4,1},{5,0},{8,5},{9,4},{12,9},{13,8},{14,13},{15,12},... | collective-permute-start | bytes 442376 | tf_op jit(solution)/shard_map/ppermute | solution.py:39
  22.7 6.1 %collective-permute-start.8 = (bf16[64,1152]{1,0:T(8,128)(2,1)S(1)}, bf16[64,1152]{1,0:T(8,128)(2,1)S(1)}, u32[]{:S(2)}, u32[]{:S(2)}) collective-permute-start(bf16[64,1152]{1,0:T(8,128)(2,1)S(1)} %collective-permute-done.7.refs_0_), channel_id=1, source_target_pairs={{0,5},{1,4},{4,9},{5,8},{8,13},{9,12},{12,15},{13,14},{14,11},{15,... | collective-permute-start | bytes 442376 | tf_op jit(solution)/shard_map/ppermute | solution.py:39
  24.9 6.0 %collective-permute-start.4 = (bf16[64,1152]{1,0:T(8,128)(2,1)S(1)}, bf16[64,1152]{1,0:T(8,128)(2,1)S(1)}, u32[]{:S(2)}, u32[]{:S(2)}) collective-permute-start(bf16[64,1152]{1,0:T(8,128)(2,1)S(1)} %collective-permute-done.3.refs_3_), channel_id=1, source_target_pairs={{0,3},{1,2},{4,1},{5,0},{8,5},{9,4},{12,9},{13,8},{14,13},{15,12},... | collective-permute-start | bytes 442376 | tf_op jit(solution)/shard_map/ppermute | solution.py:39
  31.3 24.5 %copy-start.3 = (bf16[8,4096]{1,0:T(8,128)(2,1)S(1)}, bf16[8,4096]{1,0:T(8,128)(2,1)}, u32[]{:S(2)}) copy-start(bf16[8,4096]{1,0:T(8,128)(2,1)} %queries.1) | copy-start | bytes 196612
  31.3 1.4 %collective-permute-start.15 = (f32[256,128]{1,0:T(8,128)S(1)}, f32[256,128]{1,0:T(8,128)S(1)}, u32[]{:S(2)}, u32[]{:S(2)}) collective-permute-start(f32[256,128]{1,0:T(8,128)S(1)} %shard_map.68), channel_id=1, source_target_pairs={{0,1},{1,0},{2,3},{3,2},{4,5},{5,4},{6,7},{7,6},{8,9},{9,8},{10,11... | collective-permute-start | bytes 393224 | tf_op jit(solution)/shard_map/ppermute | solution.py:43

commit v19 on v17

--- a/solution.py
+++ b/solution.py
@@ -47,17 +47,15 @@
     return (chip ^ (chip >> 1)) & 1
 
 
-def column_copies(chip, ring_core, act, grad, out, sems, chips):
-    block = 2 * chip + (ring_core ^ odd(lax.axis_index("dp") >> 1) ^ odd(chip))
-    a_width, g_width = (x.shape[1] // (2 * chips) for x in (act, grad))
-    return [
-        pltpu.make_async_copy(
-            ref.at[:, pl.ds(pl.multiple_of(block * width, 128), width)],
-            out.at[:, pl.ds(at, width)],
-            sems.at[k],
-        )
-        for k, (ref, at, width) in enumerate(((act, 0, a_width), (grad, a_width, g_width)))
-    ]
+def gradient_runs(chips):
+    runs = []
+    for chip in range(chips):
+        block = 2 * chip + odd(chip)
+        if runs and sum(runs[-1]) == block:
+            runs[-1] = (runs[-1][0], runs[-1][1] + 1)
+        else:
+            runs.append((block, 1))
+    return runs
 
 
 def run_copies(copies):
@@ -67,35 +65,41 @@
         copy.wait()
 
 
-def start_kernel(chips, act, grad, in_rows, out_rows, first, second, send, sems, send_sems):
-    core = lax.axis_index("dp") & 1
-    a_width = in_rows.shape[1]
+def start_kernel(chips, act, grad, in_rows, out_rows, first, second, send, sems):
+    me = lax.axis_index("dp")
+    ring_of = 1 ^ (me & 1) ^ odd(me >> 1)
+    a_width, g_width = in_rows.shape[1], out_rows.shape[1]
     cut = first.shape[1]
     pairs = [
         (in_rows, first.at[:, pl.ds(0, a_width)]),
         (out_rows.at[:, pl.ds(0, cut - a_width)], first.at[:, pl.ds(a_width, cut - a_width)]),
         (out_rows.at[:, pl.ds(cut - a_width, second.shape[1])], second),
+        (act, send.at[:, pl.ds(0, act.shape[1])]),
     ]
-    copies = [pltpu.make_async_copy(*pair, sems.at[i]) for i, pair in enumerate(pairs)]
-    for chip in range(chips):
-        copies += column_copies(chip, 1 - core, act, grad, send.at[chip], send_sems.at[chip], chips)
-    run_copies(copies)
+    to = act.shape[1]
+    for block, length in gradient_runs(chips):
+        at = pl.multiple_of(((block + 4 * ring_of) & (2 * chips - 1)) * g_width, 128)
+        width = length * g_width
+        pairs.append((grad.at[:, pl.ds(at, width)], send.at[:, pl.ds(to, width)]))
+        to += width
+    run_copies([pltpu.make_async_copy(*pair, sems.at[i]) for i, pair in enumerate(pairs)])
 
 
 def start(act, grad, in_rows, out_rows, chips):
     rows = act.shape[0]
     rank, width = in_rows.shape[0], in_rows.shape[1] + out_rows.shape[1]
     cut = width // 256 * 128
-    shapes = (rank, cut), (rank, width - cut), (chips, rows, width)
+    columns = act.shape[1] + grad.shape[1] // 2
+    shapes = (rank, cut), (rank, width - cut), (rows, columns)
     return pl.pallas_call(
         functools.partial(start_kernel, chips),
         out_shape=[pltpu.VMEM(shape, act.dtype) for shape in shapes],
         in_specs=[HBM] * 4,
         out_specs=[VMEM] * 3,
-        scratch_shapes=[pltpu.SemaphoreType.DMA((3,)), pltpu.SemaphoreType.DMA((chips, 2))],
+        scratch_shapes=[pltpu.SemaphoreType.DMA((4 + len(gradient_runs(chips)),))],
         compiler_params=pltpu.CompilerParams(vmem_limit_bytes=16 * 2**20),
         cost_estimate=pl.CostEstimate(
-            flops=0, bytes_accessed=4 * (rank + chips * rows) * width, transcendentals=0
+            flops=0, bytes_accessed=4 * (rank * width + rows * columns), transcendentals=0
         ),
     )(*held(pltpu.HBM, act, grad, in_rows, out_rows))
 
@@ -104,33 +108,38 @@
     chunks, refs = refs[: len(items)], refs[len(items) :]
     out = refs[-1]
     rank = chunks[0].shape[0]
-    g_width = theirs.shape[2] - a_width
+    g_width = grad.shape[1] // (2 * chips)
     me = lax.axis_index("dp")
+    ring_of = (me & 1) ^ odd(me >> 1)
     if carry:
         a_sum, g_sum = refs[0][:, :rank], refs[0][:, rank:]
     else:
         a_sum = g_sum = jnp.zeros((out.shape[0], rank), jnp.float32)
     for (offset, part), chunk in zip(items, chunks):
         chip = chip_behind(offset, chips)
-        block = 2 * chip + ((me & 1) ^ odd(me >> 1) ^ odd(chip))
-
-        def tokens(ref, width, skip, first, last):
-            at = pl.multiple_of(block * width, 128) + (first - skip)
-            return jnp.concatenate(
-                [ref[:, pl.ds(at, last - first)], theirs[chip, :, first:last]], axis=0
-            )
+        block = 2 * chip + (ring_of ^ odd(chip))
+        place = (chip - 2 * ring_of) & (chips - 1)
+        a_at = pl.ds(pl.multiple_of(block * a_width, 128), a_width)
+        mine_at = pl.multiple_of(block * g_width, 128)
+        theirs_at = pl.multiple_of(act.shape[1] + place * g_width, 128)
+
+        def gradients(first, last):
+            columns = [pl.ds(at + first, last - first) for at in (mine_at, theirs_at)]
+            return jnp.concatenate([grad[:, columns[0]], theirs[:, columns[1]]], axis=0)
 
         if part == 0:
-            a_sum += dot(tokens(act, a_width, 0, 0, a_width), chunk[:, :a_width], NT)
-            g_sum += dot(tokens(grad, g_width, a_width, a_width, cut), chunk[:, a_width:], NT)
+            a_tokens = jnp.concatenate([act[:, a_at], theirs[:, a_at]], axis=0)
+            a_sum += dot(a_tokens, chunk[:, :a_width], NT)
+            g_sum += dot(gradients(0, cut - a_width), chunk[:, a_width:], NT)
         else:
-            g_sum += dot(tokens(grad, g_width, a_width, cut, theirs.shape[2]), chunk[...], NT)
+            g_sum += dot(gradients(cut - a_width, g_width), chunk[...], NT)
     out[:, :rank] = a_sum
     out[:, rank:] = g_sum
 
 
 def project(tokens, items, chunks, a_width, cut, total=None):
-    chips, rows, _ = tokens[2].shape
+    rows = tokens[0].shape[0]
+    chips = tokens[0].shape[1] // (2 * a_width)
     rank = chunks[0].shape[0]
     columns = sum(x.shape[1] for x in chunks)
     carried = [] if total is None else [total]

time: 56.2 us -> 56.5 us (level)
  no operation moved by 1% of the time
where the time goes in v19:
time: 56.5 us; the launch traced here: 56.3 us
  blocking collectives  21.5 us (38%)
  starting transfers between devices  16.1 us (28%)
  waiting for transfers between devices  10.4 us (18%)
  Pallas kernels  7.09 us (13%)
  matrix products  0.89 us (2%)
    all_to_all x2, blocking collectives, to_all(): lax.all_to_all(copies, 'dp', 0, 0, axis_index_groups=groups, tiled=True)  21.5 us
    ppermute x14, starting transfers between devices, ring(): return lax.ppermute(x, 'dp', pairs)  15.4 us
    ppermute x14, waiting for transfers between devices, ring(): return lax.ppermute(x, 'dp', pairs)  9.17 us
    pallas_call x4, Pallas kernels, project(): pl.pallas_call(functools.partial(project_kernel, chips, items, a_width, c...  3.34 us
    pallas_call x1, Pallas kernels, start(): pl.pallas_call(functools.partial(start_kernel, chips), out_shape=[pltpu.V...  3.02 us
    ppermute x2, waiting for transfers between devices, swap(): return lax.ppermute(x, 'dp', [(i, i ^ bit) for i in range(n)])  1.23 us
  transfers between devices with their start and end apart: 16, of which 9 were waited for; matrix products, arithmetic and copies ran while one was open for 0% of the time, Pallas kernels for 5%

profile of v19, /device:TPU:0, one launch (start us, length us, event | category | flops | bytes accessed | tf_op | source)
XLA Modules:
  0.0 56.3 jit_solution(7539082016866189318)
XLA Ops:
  0.0 3.0 %shard_map.64 = (bf16[64,1152]{1,0:T(8,128)(2,1)S(1)}, bf16[64,1152]{1,0:T(8,128)(2,1)S(1)}, bf16[128,22528]{1,0:T(8,128)(2,1)S(1)}) custom-call(bf16[128,8192]{1,0:T(8,128)(2,1)} %act.9, bf16[128,28672]{1,0:T(8,128)(2,1)} %grad.9, bf16[64,512]{1,0:T(8,128)(2,1)} %bitcast.12, bf16[64,1792]{1,0:T(8,128)(2,1)} %bitcast.11), custom_call_target="tpu_custom_call" | custom-call | bytes 12124160 | tf_op jit(solution)/shard_map/pallas_call | solution.py:94
  3.0 0.5 collective-permute-start
  3.6 2.7 %collective-permute-start.5 = (bf16[64,1152]{1,0:T(8,128)(2,1)S(1)}, bf16[64,1152]{1,0:T(8,128)(2,1)S(1)}, u32[]{:S(2)}, u32[]{:S(2)}) collective-permute-start(bf16[64,1152]{1,0:T(8,128)(2,1)S(1)} %get-tuple-element.10.refs_0_), channel_id=1, source_target_pairs={{0,5},{1,4},{4,9},{5,8},{8,13},{9,12},{12,15},{13,14},{14,11},{15,... | collective-permute-start | bytes 442376 | tf_op jit(solution)/shard_map/ppermute | solution.py:39
  6.2 1.7 %collective-permute-start.9 = (bf16[64,1152]{1,0:T(8,128)(2,1)S(1)}, bf16[64,1152]{1,0:T(8,128)(2,1)S(1)}, u32[]{:S(2)}, u32[]{:S(2)}) collective-permute-start(bf16[64,1152]{1,0:T(8,128)(2,1)S(1)} %get-tuple-element.9.refs_1_), channel_id=1, source_target_pairs={{0,5},{1,4},{4,9},{5,8},{8,13},{9,12},{12,15},{13,14},{14,11},{15,... | collective-permute-start | bytes 442376 | tf_op jit(solution)/shard_map/ppermute | solution.py:39
  8.0 2.4 %collective-permute-done.5.refs_2_ = bf16[64,1152]{1,0:T(8,128)(2,1)S(1)} collective-permute-done((bf16[64,1152]{1,0:T(8,128)(2,1)S(1)}, bf16[64,1152]{1,0:T(8,128)(2,1)S(1)}, u32[]{:S(2)}, u32[]{:S(2)}) %collective-permute-start.5) | collective-permute-done | bytes 147488 | tf_op jit(solution)/shard_map/ppermute | solution.py:39
  10.4 2.2 %collective-permute-start.6 = (bf16[64,1152]{1,0:T(8,128)(2,1)S(1)}, bf16[64,1152]{1,0:T(8,128)(2,1)S(1)}, u32[]{:S(2)}, u32[]{:S(2)}) collective-permute-start(bf16[64,1152]{1,0:T(8,128)(2,1)S(1)} %collective-permute-done.5.refs_2_), channel_id=1, source_target_pairs={{0,5},{1,4},{4,9},{5,8},{8,13},{9,12},{12,15},{13,14},{14,11},{15,... | collective-permute-start | bytes 442376 | tf_op jit(solution)/shard_map/ppermute | solution.py:39
  12.6 0.9 %collective-permute-done.9.refs_3_ = bf16[64,1152]{1,0:T(8,128)(2,1)S(1)} collective-permute-done((bf16[64,1152]{1,0:T(8,128)(2,1)S(1)}, bf16[64,1152]{1,0:T(8,128)(2,1)S(1)}, u32[]{:S(2)}, u32[]{:S(2)}) %collective-permute-start.9) | collective-permute-done | bytes 147488 | tf_op jit(solution)/shard_map/ppermute | solution.py:39
  13.5 2.2 %collective-permute-start.10 = (bf16[64,1152]{1,0:T(8,128)(2,1)S(1)}, bf16[64,1152]{1,0:T(8,128)(2,1)S(1)}, u32[]{:S(2)}, u32[]{:S(2)}) collective-permute-start(bf16[64,1152]{1,0:T(8,128)(2,1)S(1)} %collective-permute-done.9.refs_3_), channel_id=1, source_target_pairs={{0,5},{1,4},{4,9},{5,8},{8,13},{9,12},{12,15},{13,14},{14,11},{15,... | collective-permute-start | bytes 442376 | tf_op jit(solution)/shard_map/ppermute | solution.py:39
  15.7 1.1 %collective-permute-done.6.refs_6_ = bf16[64,1152]{1,0:T(8,128)(2,1)S(1)} collective-permute-done((bf16[64,1152]{1,0:T(8,128)(2,1)S(1)}, bf16[64,1152]{1,0:T(8,128)(2,1)S(1)}, u32[]{:S(2)}, u32[]{:S(2)}) %collective-permute-start.6) | collective-permute-done | bytes 147488 | tf_op jit(solution)/shard_map/ppermute | solution.py:39
  16.7 2.2 %collective-permute-start.7 = (bf16[64,1152]{1,0:T(8,128)(2,1)S(1)}, bf16[64,1152]{1,0:T(8,128)(2,1)S(1)}, u32[]{:S(2)}, u32[]{:S(2)}) collective-permute-start(bf16[64,1152]{1,0:T(8,128)(2,1)S(1)} %collective-permute-done.6.refs_6_), channel_id=1, source_target_pairs={{0,5},{1,4},{4,9},{5,8},{8,13},{9,12},{12,15},{13,14},{14,11},{15,... | collective-permute-start | bytes 442376 | tf_op jit(solution)/shard_map/ppermute | solution.py:39
  18.9 0.9 %collective-permute-done.10.refs_7_ = bf16[64,1152]{1,0:T(8,128)(2,1)S(1)} collective-permute-done((bf16[64,1152]{1,0:T(8,128)(2,1)S(1)}, bf16[64,1152]{1,0:T(8,128)(2,1)S(1)}, u32[]{:S(2)}, u32[]{:S(2)}) %collective-permute-start.10) | collective-permute-done | bytes 147488 | tf_op jit(solution)/shard_map/ppermute | solution.py:39
  19.8 2.2 %collective-permute-start.11 = (bf16[64,1152]{1,0:T(8,128)(2,1)S(1)}, bf16[64,1152]{1,0:T(8,128)(2,1)S(1)}, u32[]{:S(2)}, u32[]{:S(2)}) collective-permute-start(bf16[64,1152]{1,0:T(8,128)(2,1)S(1)} %collective-permute-done.10.refs_7_), channel_id=1, source_target_pairs={{0,5},{1,4},{4,9},{5,8},{8,13},{9,12},{12,15},{13,14},{14,11},{15,... | collective-permute-start | bytes 442376 | tf_op jit(solution)/shard_map/ppermute | solution.py:39
  22.0 1.0 %collective-permute-done.7.refs_0_ = bf16[64,1152]{1,0:T(8,128)(2,1)S(1)} collective-permute-done((bf16[64,1152]{1,0:T(8,128)(2,1)S(1)}, bf16[64,1152]{1,0:T(8,128)(2,1)S(1)}, u32[]{:S(2)}, u32[]{:S(2)}) %collective-permute-start.7) | collective-permute-done | bytes 147488 | tf_op jit(solution)/shard_map/ppermute | solution.py:39
  23.0 2.2 %collective-permute-start.8 = (bf16[64,1152]{1,0:T(8,128)(2,1)S(1)}, bf16[64,1152]{1,0:T(8,128)(2,1)S(1)}, u32[]{:S(2)}, u32[]{:S(2)}) collective-permute-start(bf16[64,1152]{1,0:T(8,128)(2,1)S(1)} %collective-permute-done.7.refs_0_), channel_id=1, source_target_pairs={{0,5},{1,4},{4,9},{5,8},{8,13},{9,12},{12,15},{13,14},{14,11},{15,... | collective-permute-start | bytes 442376 | tf_op jit(solution)/shard_map/ppermute | solution.py:39
  25.2 1.8 %shard_map.65.refs_4_ = f32[256,128]{1,0:T(8,128)S(1)} custom-call(bf16[128,8192]{1,0:T(8,128)(2,1)S(1)} %copy-done.2, bf16[128,28672]{1,0:T(8,128)(2,1)S(1)} %copy-done.1, bf16[128,22528]{1,0:T(8,128)(2,1)S(1)} %collective-permute-done.theirs, bf16[64,1152]{1,0:T(8,128)(2,1)S(1)} %get-tuple-element.10.refs_0_, ...), custom_call_target="tpu_custom_call" | custom-call | flops 377487360 | bytes 7372800 | tf_op jit(solution)/shard_map/pallas_call | solution.py:146
  27.0 1.1 %collective-permute-done.14.refs_2_ = bf16[64,1152]{1,0:T(8,128)(2,1)S(1)} collective-permute-done((bf16[64,1152]{1,0:T(8,128)(2,1)S(1)}, bf16[64,1152]{1,0:T(8,128)(2,1)S(1)}, u32[]{:S(2)}, u32[]{:S(2)}) %collective-permute-start.14) | collective-permute-done | bytes 147488 | tf_op jit(solution)/shard_map/ppermute | solution.py:39
  28.1 0.8 %shard_map.66.refs_1_ = f32[256,128]{1,0:T(8,128)S(1)} custom-call(bf16[128,8192]{1,0:T(8,128)(2,1)S(1)} %copy-done.2, bf16[128,28672]{1,0:T(8,128)(2,1)S(1)} %copy-done.1, bf16[128,22528]{1,0:T(8,128)(2,1)S(1)} %collective-permute-done.theirs, bf16[64,1152]{1,0:T(8,128)(2,1)S(1)} %collective-permute-done.7.refs_0_, ...), custom_call_target="tpu_custom_call" | custom-call | flops 150994944 | bytes 2949120 | tf_op jit(solution)/shard_map/pallas_call | solution.py:146
  29.1 0.4 shard_map.67.refs_1_
  29.5 1.7 %collective-permute-done.4.refs_0_ = bf16[64,1152]{1,0:T(8,128)(2,1)S(1)} collective-permute-done((bf16[64,1152]{1,0:T(8,128)(2,1)S(1)}, bf16[64,1152]{1,0:T(8,128)(2,1)S(1)}, u32[]{:S(2)}, u32[]{:S(2)}) %collective-permute-start.4) | collective-permute-done | bytes 147488 | tf_op jit(solution)/shard_map/ppermute | solution.py:39
  31.8 1.2 %collective-permute-done.15 = f32[256,128]{1,0:T(8,128)S(1)} collective-permute-done((f32[256,128]{1,0:T(8,128)S(1)}, f32[256,128]{1,0:T(8,128)S(1)}, u32[]{:S(2)}, u32[]{:S(2)}) %collective-permute-start.15) | collective-permute-done | bytes 131104 | tf_op jit(solution)/shard_map/ppermute | solution.py:43
  33.4 12.4 %all_to_all.10 = f32[8,32,128]{2,1,0:T(8,128)S(1)} all-to-all(f32[8,32,128]{2,1,0:T(8,128)S(1)} %broadcast_in_dim.14), channel_id=1, replica_groups={{0,2,4,6,8,10,12,14},{1,3,5,7,9,11,13,15},{16,18,20,22,24,26,28,30},{17..., dimensions={0} | all-to-all | bytes 262144 | tf_op jit(solution)/shard_map/all_to_all | solution.py:180
  45.8 0.6 %convolution_convert_fusion = bf16[2,256]{1,0:T(2,128)(2,1)S(1)} fusion(bf16[256,4096]{1,0:T(8,128)(2,1)S(1)} %copy-done, bf16[1,2,32,128]{3,2,1,0:T(8,128)(2,1)S(1)} %bitcast.13), kind=kOutput, calls=%fused_computation.1 | convolution fusion | flops 4194816 | bytes 2114560 | tf_op jit(solution)/shard_map/dot_general | solution.py:23
  46.5 9.1 %all_to_all.11.conditioned = bf16[16,2,256]{2,1,0:T(2,128)(2,1)S(1)} all-to-all(bf16[16,2,256]{2,1,0:T(2,128)(2,1)S(1)} %broadcast_in_dim.15), channel_id=1, replica_groups={{0,1,2,3,4,5,6,7,8,9,10,11,12,13,14,15},{16,17,18,19,20,21,22,23,24,25,..., dimensions={0} | all-to-all | bytes 32768 | tf_op jit(solution)/shard_map/all_to_all | solution.py:180
  55.6 0.7 %shard_map.69 = f32[2,8]{1,0:T(2,128)} custom-call(bf16[16,2,256]{2,1,0:T(2,128)(2,1)S(1)} %all_to_all.11.conditioned, bf16[8,4096]{1,0:T(8,128)(2,1)S(1)} %copy-done.3), custom_call_target="tpu_custom_call" | custom-call | tf_op jit(solution)/shard_map/pallas_call | solution.py:169
  (32 shorter events, 1.1 us)
Async XLA Ops:
  0.0 45.8 %copy-start = (bf16[256,4096]{1,0:T(8,128)(2,1)S(1)}, bf16[256,4096]{1,0:T(8,128)(2,1)}, u32[]{:S(2)}) copy-start(bf16[256,4096]{1,0:T(8,128)(2,1)} %param.10) | copy-start | bytes 6291460
  0.0 25.2 %copy-start.1 = (bf16[128,28672]{1,0:T(8,128)(2,1)S(1)}, bf16[128,28672]{1,0:T(8,128)(2,1)}, u32[]{:S(2)}) copy-start(bf16[128,28672]{1,0:T(8,128)(2,1)} %grad.9) | copy-start | bytes 22020100
  0.0 25.2 %copy-start.2 = (bf16[128,8192]{1,0:T(8,128)(2,1)S(1)}, bf16[128,8192]{1,0:T(8,128)(2,1)}, u32[]{:S(2)}) copy-start(bf16[128,8192]{1,0:T(8,128)(2,1)} %act.9) | copy-start | bytes 6291460
  3.0 22.2 %collective-permute-start = (bf16[128,22528]{1,0:T(8,128)(2,1)S(1)}, bf16[128,22528]{1,0:T(8,128)(2,1)S(1)}, u32[]{:S(2)}, u32[]{:S(2)}) collective-permute-start(bf16[128,22528]{1,0:T(8,128)(2,1)S(1)} %get-tuple-element.8), channel_id=1, source_target_pairs={{0,1},{1,0},{2,3},{3,2},{4,5},{5,4},{6,7},{7,6},{8,9},{9,8},{10,11... | collective-permute-start | bytes 17301512 | tf_op jit(solution)/shard_map/ppermute | solution.py:43
  3.6 6.9 %collective-permute-start.5 = (bf16[64,1152]{1,0:T(8,128)(2,1)S(1)}, bf16[64,1152]{1,0:T(8,128)(2,1)S(1)}, u32[]{:S(2)}, u32[]{:S(2)}) collective-permute-start(bf16[64,1152]{1,0:T(8,128)(2,1)S(1)} %get-tuple-element.10.refs_0_), channel_id=1, source_target_pairs={{0,5},{1,4},{4,9},{5,8},{8,13},{9,12},{12,15},{13,14},{14,11},{15,... | collective-permute-start | bytes 442376 | tf_op jit(solution)/shard_map/ppermute | solution.py:39
  6.2 6.4 %collective-permute-start.1 = (bf16[64,1152]{1,0:T(8,128)(2,1)S(1)}, bf16[64,1152]{1,0:T(8,128)(2,1)S(1)}, u32[]{:S(2)}, u32[]{:S(2)}) collective-permute-start(bf16[64,1152]{1,0:T(8,128)(2,1)S(1)} %get-tuple-element.9.refs_1_), channel_id=1, source_target_pairs={{0,3},{1,2},{4,1},{5,0},{8,5},{9,4},{12,9},{13,8},{14,13},{15,12},... | collective-permute-start | bytes 442376 | tf_op jit(solution)/shard_map/ppermute | solution.py:39
  6.2 7.3 %collective-permute-start.9 = (bf16[64,1152]{1,0:T(8,128)(2,1)S(1)}, bf16[64,1152]{1,0:T(8,128)(2,1)S(1)}, u32[]{:S(2)}, u32[]{:S(2)}) collective-permute-start(bf16[64,1152]{1,0:T(8,128)(2,1)S(1)} %get-tuple-element.9.refs_1_), channel_id=1, source_target_pairs={{0,5},{1,4},{4,9},{5,8},{8,13},{9,12},{12,15},{13,14},{14,11},{15,... | collective-permute-start | bytes 442376 | tf_op jit(solution)/shard_map/ppermute | solution.py:39
  8.0 7.7 %collective-permute-start.12 = (bf16[64,1152]{1,0:T(8,128)(2,1)S(1)}, bf16[64,1152]{1,0:T(8,128)(2,1)S(1)}, u32[]{:S(2)}, u32[]{:S(2)}) collective-permute-start(bf16[64,1152]{1,0:T(8,128)(2,1)S(1)} %get-tuple-element.10.refs_0_), channel_id=1, source_target_pairs={{0,3},{1,2},{4,1},{5,0},{8,5},{9,4},{12,9},{13,8},{14,13},{15,12},... | collective-permute-start | bytes 442376 | tf_op jit(solution)/shard_map/ppermute | solution.py:39
  10.4 6.3 %collective-permute-start.6 = (bf16[64,1152]{1,0:T(8,128)(2,1)S(1)}, bf16[64,1152]{1,0:T(8,128)(2,1)S(1)}, u32[]{:S(2)}, u32[]{:S(2)}) collective-permute-start(bf16[64,1152]{1,0:T(8,128)(2,1)S(1)} %collective-permute-done.5.refs_2_), channel_id=1, source_target_pairs={{0,5},{1,4},{4,9},{5,8},{8,13},{9,12},{12,15},{13,14},{14,11},{15,... | collective-permute-start | bytes 442376 | tf_op jit(solution)/shard_map/ppermute | solution.py:39
  12.6 6.3 %collective-permute-start.2 = (bf16[64,1152]{1,0:T(8,128)(2,1)S(1)}, bf16[64,1152]{1,0:T(8,128)(2,1)S(1)}, u32[]{:S(2)}, u32[]{:S(2)}) collective-permute-start(bf16[64,1152]{1,0:T(8,128)(2,1)S(1)} %collective-permute-done.1.refs_5_), channel_id=1, source_target_pairs={{0,3},{1,2},{4,1},{5,0},{8,5},{9,4},{12,9},{13,8},{14,13},{15,12},... | collective-permute-start | bytes 442376 | tf_op jit(solution)/shard_map/ppermute | solution.py:39
  13.5 6.3 %collective-permute-start.10 = (bf16[64,1152]{1,0:T(8,128)(2,1)S(1)}, bf16[64,1152]{1,0:T(8,128)(2,1)S(1)}, u32[]{:S(2)}, u32[]{:S(2)}) collective-permute-start(bf16[64,1152]{1,0:T(8,128)(2,1)S(1)} %collective-permute-done.9.refs_3_), channel_id=1, source_target_pairs={{0,5},{1,4},{4,9},{5,8},{8,13},{9,12},{12,15},{13,14},{14,11},{15,... | collective-permute-start | bytes 442376 | tf_op jit(solution)/shard_map/ppermute | solution.py:39
  15.7 6.4 %collective-permute-start.13 = (bf16[64,1152]{1,0:T(8,128)(2,1)S(1)}, bf16[64,1152]{1,0:T(8,128)(2,1)S(1)}, u32[]{:S(2)}, u32[]{:S(2)}) collective-permute-start(bf16[64,1152]{1,0:T(8,128)(2,1)S(1)} %collective-permute-done.12.refs_4_), channel_id=1, source_target_pairs={{0,3},{1,2},{4,1},{5,0},{8,5},{9,4},{12,9},{13,8},{14,13},{15,12},... | collective-permute-start | bytes 442376 | tf_op jit(solution)/shard_map/ppermute | solution.py:39
  16.7 6.3 %collective-permute-start.7 = (bf16[64,1152]{1,0:T(8,128)(2,1)S(1)}, bf16[64,1152]{1,0:T(8,128)(2,1)S(1)}, u32[]{:S(2)}, u32[]{:S(2)}) collective-permute-start(bf16[64,1152]{1,0:T(8,128)(2,1)S(1)} %collective-permute-done.6.refs_6_), channel_id=1, source_target_pairs={{0,5},{1,4},{4,9},{5,8},{8,13},{9,12},{12,15},{13,14},{14,11},{15,... | collective-permute-start | bytes 442376 | tf_op jit(solution)/shard_map/ppermute | solution.py:39
  18.9 6.3 %collective-permute-start.3 = (bf16[64,1152]{1,0:T(8,128)(2,1)S(1)}, bf16[64,1152]{1,0:T(8,128)(2,1)S(1)}, u32[]{:S(2)}, u32[]{:S(2)}) collective-permute-start(bf16[64,1152]{1,0:T(8,128)(2,1)S(1)} %collective-permute-done.2.refs_9_), channel_id=1, source_target_pairs={{0,3},{1,2},{4,1},{5,0},{8,5},{9,4},{12,9},{13,8},{14,13},{15,12},... | collective-permute-start | bytes 442376 | tf_op jit(solution)/shard_map/ppermute | solution.py:39
  19.8 7.2 %collective-permute-start.11 = (bf16[64,1152]{1,0:T(8,128)(2,1)S(1)}, bf16[64,1152]{1,0:T(8,128)(2,1)S(1)}, u32[]{:S(2)}, u32[]{:S(2)}) collective-permute-start(bf16[64,1152]{1,0:T(8,128)(2,1)S(1)} %collective-permute-done.10.refs_7_), channel_id=1, source_target_pairs={{0,5},{1,4},{4,9},{5,8},{8,13},{9,12},{12,15},{13,14},{14,11},{15,... | collective-permute-start | bytes 442376 | tf_op jit(solution)/shard_map/ppermute | solution.py:39
  22.0 6.1 %collective-permute-start.14 = (bf16[64,1152]{1,0:T(8,128)(2,1)S(1)}, bf16[64,1152]{1,0:T(8,128)(2,1)S(1)}, u32[]{:S(2)}, u32[]{:S(2)}) collective-permute-start(bf16[64,1152]{1,0:T(8,128)(2,1)S(1)} %collective-permute-done.13.refs_8_), channel_id=1, source_target_pairs={{0,3},{1,2},{4,1},{5,0},{8,5},{9,4},{12,9},{13,8},{14,13},{15,12},... | collective-permute-start | bytes 442376 | tf_op jit(solution)/shard_map/ppermute | solution.py:39
  23.0 6.1 %collective-permute-start.8 = (bf16[64,1152]{1,0:T(8,128)(2,1)S(1)}, bf16[64,1152]{1,0:T(8,128)(2,1)S(1)}, u32[]{:S(2)}, u32[]{:S(2)}) collective-permute-start(bf16[64,1152]{1,0:T(8,128)(2,1)S(1)} %collective-permute-done.7.refs_0_), channel_id=1, source_target_pairs={{0,5},{1,4},{4,9},{5,8},{8,13},{9,12},{12,15},{13,14},{14,11},{15,... | collective-permute-start | bytes 442376 | tf_op jit(solution)/shard_map/ppermute | solution.py:39
  25.2 6.0 %collective-permute-start.4 = (bf16[64,1152]{1,0:T(8,128)(2,1)S(1)}, bf16[64,1152]{1,0:T(8,128)(2,1)S(1)}, u32[]{:S(2)}, u32[]{:S(2)}) collective-permute-start(bf16[64,1152]{1,0:T(8,128)(2,1)S(1)} %collective-permute-done.3.refs_3_), channel_id=1, source_target_pairs={{0,3},{1,2},{4,1},{5,0},{8,5},{9,4},{12,9},{13,8},{14,13},{15,12},... | collective-permute-start | bytes 442376 | tf_op jit(solution)/shard_map/ppermute | solution.py:39
  31.6 24.0 %copy-start.3 = (bf16[8,4096]{1,0:T(8,128)(2,1)S(1)}, bf16[8,4096]{1,0:T(8,128)(2,1)}, u32[]{:S(2)}) copy-start(bf16[8,4096]{1,0:T(8,128)(2,1)} %queries.1) | copy-start | bytes 196612
  31.6 1.4 %collective-permute-start.15 = (f32[256,128]{1,0:T(8,128)S(1)}, f32[256,128]{1,0:T(8,128)S(1)}, u32[]{:S(2)}, u32[]{:S(2)}) collective-permute-start(f32[256,128]{1,0:T(8,128)S(1)} %shard_map.68), channel_id=1, source_target_pairs={{0,1},{1,0},{2,3},{3,2},{4,5},{5,4},{6,7},{7,6},{8,9},{9,8},{10,11... | collective-permute-start | bytes 393224 | tf_op jit(solution)/shard_map/ppermute | solution.py:43

commit v20 on v17

--- a/solution.py
+++ b/solution.py
@@ -9,6 +9,7 @@
 from jax.sharding import PartitionSpec as P
 
 LEN = 1024
+HIDE = 10**11
 NT = (((1,), (1,)), ((), ()))
 TN = (((0,), (0,)), ((), ()))
 VMEM = pl.BlockSpec(memory_space=pltpu.VMEM)
@@ -67,8 +68,7 @@
         copy.wait()
 
 
-def start_kernel(chips, act, grad, in_rows, out_rows, first, second, send, sems, send_sems):
-    core = lax.axis_index("dp") & 1
+def chunk_kernel(in_rows, out_rows, first, second, sems):
     a_width = in_rows.shape[1]
     cut = first.shape[1]
     pairs = [
@@ -76,76 +76,106 @@
         (out_rows.at[:, pl.ds(0, cut - a_width)], first.at[:, pl.ds(a_width, cut - a_width)]),
         (out_rows.at[:, pl.ds(cut - a_width, second.shape[1])], second),
     ]
-    copies = [pltpu.make_async_copy(*pair, sems.at[i]) for i, pair in enumerate(pairs)]
-    for chip in range(chips):
-        copies += column_copies(chip, 1 - core, act, grad, send.at[chip], send_sems.at[chip], chips)
-    run_copies(copies)
-
-
-def start(act, grad, in_rows, out_rows, chips):
-    rows = act.shape[0]
+    run_copies([pltpu.make_async_copy(*pair, sems.at[i]) for i, pair in enumerate(pairs)])
+
+
+def chunks_of(in_rows, out_rows):
     rank, width = in_rows.shape[0], in_rows.shape[1] + out_rows.shape[1]
     cut = width // 256 * 128
-    shapes = (rank, cut), (rank, width - cut), (chips, rows, width)
-    return pl.pallas_call(
-        functools.partial(start_kernel, chips),
-        out_shape=[pltpu.VMEM(shape, act.dtype) for shape in shapes],
-        in_specs=[HBM] * 4,
-        out_specs=[VMEM] * 3,
-        scratch_shapes=[pltpu.SemaphoreType.DMA((3,)), pltpu.SemaphoreType.DMA((chips, 2))],
+    return pl.pallas_call(
+        chunk_kernel,
+        out_shape=[pltpu.VMEM((rank, w), in_rows.dtype) for w in (cut, width - cut)],
+        in_specs=[HBM] * 2,
+        out_specs=[VMEM] * 2,
+        scratch_shapes=[pltpu.SemaphoreType.DMA((3,))],
         compiler_params=pltpu.CompilerParams(vmem_limit_bytes=16 * 2**20),
         cost_estimate=pl.CostEstimate(
-            flops=0, bytes_accessed=4 * (rank + chips * rows) * width, transcendentals=0
-        ),
-    )(*held(pltpu.HBM, act, grad, in_rows, out_rows))
-
-
-def project_kernel(chips, items, a_width, cut, carry, act, grad, theirs, *refs):
+            flops=0, bytes_accessed=4 * rank * width, transcendentals=0
+        ),
+    )(*held(pltpu.HBM, in_rows, out_rows))
+
+
+def pack_kernel(chips, act, grad, send, sems):
+    core = lax.axis_index("dp") & 1
+    copies = []
+    for chip in range(chips):
+        copies += column_copies(chip, 1 - core, act, grad, send.at[chip], sems.at[chip], chips)
+    run_copies(copies)
+
+
+def pack(act, grad, chips):
+    rows, width = act.shape[0], (act.shape[1] + grad.shape[1]) // (2 * chips)
+    return pl.pallas_call(
+        functools.partial(pack_kernel, chips),
+        out_shape=pltpu.VMEM((chips, rows, width), act.dtype),
+        in_specs=[HBM] * 2,
+        out_specs=VMEM,
+        scratch_shapes=[pltpu.SemaphoreType.DMA((chips, 2))],
+        compiler_params=pltpu.CompilerParams(vmem_limit_bytes=16 * 2**20),
+        cost_estimate=pl.CostEstimate(
+            flops=0, bytes_accessed=4 * chips * rows * width, transcendentals=0
+        ),
+    )(*held(pltpu.HBM, act, grad))
+
+
+def project_kernel(chips, items, a_width, cut, carry, act, grad, *refs):
+    theirs = None
+    if carry:
+        theirs, refs = refs[0], refs[1:]
     chunks, refs = refs[: len(items)], refs[len(items) :]
     out = refs[-1]
-    rank = chunks[0].shape[0]
-    g_width = theirs.shape[2] - a_width
+    rows, rank = act.shape[0], chunks[0].shape[0]
+    g_width = grad.shape[1] // (2 * chips)
     me = lax.axis_index("dp")
     if carry:
         a_sum, g_sum = refs[0][:, :rank], refs[0][:, rank:]
     else:
-        a_sum = g_sum = jnp.zeros((out.shape[0], rank), jnp.float32)
-    for (offset, part), chunk in zip(items, chunks):
+        a_sum = g_sum = jnp.zeros((2 * rows, rank), jnp.float32)
+    for (offset, part, whose), chunk in zip(items, chunks):
         chip = chip_behind(offset, chips)
         block = 2 * chip + ((me & 1) ^ odd(me >> 1) ^ odd(chip))
 
-        def tokens(ref, width, skip, first, last):
+        def product(ref, width, skip, first, last, basis):
             at = pl.multiple_of(block * width, 128) + (first - skip)
-            return jnp.concatenate(
-                [ref[:, pl.ds(at, last - first)], theirs[chip, :, first:last]], axis=0
-            )
+            tokens = []
+            if whose != 1:
+                tokens.append(ref[:, pl.ds(at, last - first)])
+            if whose != 0:
+                tokens.append(theirs[chip, :, first:last])
+            value = dot(jnp.concatenate(tokens, axis=0), basis, NT)
+            if whose == 2:
+                return value
+            none = jnp.zeros((rows, rank), jnp.float32)
+            return jnp.concatenate([none, value] if whose == 1 else [value, none], axis=0)
 
         if part == 0:
-            a_sum += dot(tokens(act, a_width, 0, 0, a_width), chunk[:, :a_width], NT)
-            g_sum += dot(tokens(grad, g_width, a_width, a_width, cut), chunk[:, a_width:], NT)
+            a_sum += product(act, a_width, 0, 0, a_width, chunk[:, :a_width])
+            g_sum += product(grad, g_width, a_width, a_width, cut, chunk[:, a_width:])
         else:
-            g_sum += dot(tokens(grad, g_width, a_width, cut, theirs.shape[2]), chunk[...], NT)
+            g_sum += product(grad, g_width, a_width, cut, a_width + g_width, chunk[...])
     out[:, :rank] = a_sum
     out[:, rank:] = g_sum
 
 
-def project(tokens, items, chunks, a_width, cut, total=None):
-    chips, rows, _ = tokens[2].shape
+def project(tokens, items, chunks, a_width, cut, total=None, hide=0):
+    rows = tokens[0].shape[0]
+    chips = tokens[0].shape[1] // (2 * a_width)
     rank = chunks[0].shape[0]
     columns = sum(x.shape[1] for x in chunks)
     carried = [] if total is None else [total]
+    operands = [*tokens, *chunks, *carried]
     return pl.pallas_call(
         functools.partial(project_kernel, chips, items, a_width, cut, total is not None),
         out_shape=pltpu.VMEM((2 * rows, 2 * rank), jnp.float32),
-        in_specs=[VMEM] * (3 + len(chunks) + len(carried)),
+        in_specs=[VMEM] * len(operands),
         out_specs=VMEM,
         compiler_params=pltpu.CompilerParams(vmem_limit_bytes=16 * 2**20),
         cost_estimate=pl.CostEstimate(
-            flops=4 * rows * rank * columns,
+            flops=4 * rows * rank * columns + hide,
             bytes_accessed=(2 * rows + rank) * columns * 2,
             transcendentals=0,
         ),
-    )(*held(pltpu.VMEM, *tokens, *chunks, *carried))
+    )(*held(pltpu.VMEM, *operands))
 
 
 def score_kernel(scale, conditioned, queries, out):
@@ -178,26 +208,30 @@
     chips = n // 2
     split = LEN // rows
 
-    *own, send = start(activations, out_grads, in_basis.T, out_basis.T, chips)
-    theirs = swap(send, 1, n)
+    own = list(chunks_of(in_basis.T, out_basis.T))
+    theirs = swap(pack(activations, out_grads, chips), 1, n)
+    run = functools.partial(project, a_width=a_width, cut=own[0].shape[1])
+    mine = activations, out_grads
+    last = chips // 2 - 1
     up, down = [own], [own]
-    for _ in range(chips // 2 - 1):
+    for i in range(last):
+        if i == 1:
+            total = run(mine, [(0, 0, 0), (0, 1, 0)], own, hide=HIDE)
+            total, up[i][0] = lax.optimization_barrier((total, up[i][0]))
         up.append([ring(x, 1, chips) for x in up[-1]])
         down.append([ring(x, -1, chips) for x in down[-1]])
-    last = chips // 2 - 1
     far = (ring(up[last][0], 1, chips), ring(down[last][1], -1, chips))
 
-    tokens = activations, out_grads, theirs
-    run = functools.partial(project, tokens, a_width=a_width, cut=own[0].shape[1])
-    near, items = [*own], [(0, 0), (0, 1)]
+    run = functools.partial(run, (*mine, theirs))
+    near, items = [*own], [(0, 0, 1), (0, 1, 1)]
     for i in range(1, last):
         near += [*up[i], *down[i]]
-        items += [(offset, part) for offset in (i, -i) for part in range(2)]
-    total = run(items, near)
-    items = [(offset, part) for offset in (last, -last) for part in range(2)]
+        items += [(offset, part, 2) for offset in (i, -i) for part in range(2)]
+    total = run(items, near, total=total)
+    items = [(offset, part, 2) for offset in (last, -last) for part in range(2)]
     total = run(items, [*up[last], *down[last]], total=total)
     for part, chunk in enumerate(far):
-        total = run([(chips // 2, part)], [chunk], total=total)
+        total = run([(chips // 2, part, 2)], [chunk], total=total)
     theirs = swap(total, 1, n)
     total = (total + jnp.concatenate([theirs[rows:], theirs[:rows]], axis=0)).astype(jnp.bfloat16)
 

time: 56.2 us -> 57.6 us (1.025)
  Pallas kernels: 6.81 us -> 8.71 us
  waiting for transfers between devices: 10.4 us -> 9.2 us
  starting transfers between devices: 16.1 us -> 16.8 us
    pallas_call x1 -> x2, Pallas kernels: 2.74 us -> 4.4 us  [the longest x1 3.25 us: pack(): pl.pallas_call(functools.partial(pack_kernel, chips), out_shape=pltpu.VME...]
    ppermute x14, waiting for transfers between devices: 9.17 us -> 7.96 us  [ring(): return lax.ppermute(x, 'dp', pairs)]
    ppermute x14, starting transfers between devices: 15.4 us -> 16 us  [ring(): return lax.ppermute(x, 'dp', pairs)]
    pallas_call x4 -> x5, Pallas kernels: 3.34 us -> 3.58 us  [project(): pl.pallas_call(functools.partial(project_kernel, chips, items, a_width, c...]
  transfers between devices with their start and end apart: 16 -> 16, of which waited for: 9 -> 8; matrix products, arithmetic and copies ran while one was open for 0% -> 0% of each run, Pallas kernels for 5% -> 11%
where the time goes in v20:
time: 57.6 us; the launch traced here: 57.4 us
  blocking collectives  21.4 us (37%)
  starting transfers between devices  16.8 us (29%)
  waiting for transfers between devices  9.2 us (16%)
  Pallas kernels  8.71 us (15%)
  matrix products  0.89 us (2%)
    all_to_all x2, blocking collectives, to_all(): lax.all_to_all(copies, 'dp', 0, 0, axis_index_groups=groups, tiled=True)  21.4 us
    ppermute x14, starting transfers between devices, ring(): return lax.ppermute(x, 'dp', pairs)  16 us
    ppermute x14, waiting for transfers between devices, ring(): return lax.ppermute(x, 'dp', pairs)  7.96 us
    pallas_call x5, Pallas kernels, project(): pl.pallas_call(functools.partial(project_kernel, chips, items, a_width, c...  3.58 us
    pallas_call x1, Pallas kernels, pack(): pl.pallas_call(functools.partial(pack_kernel, chips), out_shape=pltpu.VME...  3.25 us
    ppermute x2, waiting for transfers between devices, swap(): return lax.ppermute(x, 'dp', [(i, i ^ bit) for i in range(n)])  1.24 us
    pallas_call x1, Pallas kernels, chunks_of(): pl.pallas_call(chunk_kernel, out_shape=[pltpu.VMEM((rank, w), in_rows.dty...  1.16 us
  transfers between devices with their start and end apart: 16, of which 8 were waited for; matrix products, arithmetic and copies ran while one was open for 0% of the time, Pallas kernels for 11%

profile of v20, /device:TPU:0, one launch (start us, length us, event | category | flops | bytes accessed | tf_op | source)
XLA Modules:
  0.0 57.4 jit_solution(12553386793954200879)
XLA Ops:
  0.0 1.2 %shard_map.65 = (bf16[64,1152]{1,0:T(8,128)(2,1)S(1)}, bf16[64,1152]{1,0:T(8,128)(2,1)S(1)}) custom-call(bf16[64,512]{1,0:T(8,128)(2,1)} %bitcast.15, bf16[64,1792]{1,0:T(8,128)(2,1)} %bitcast.13), custom_call_target="tpu_custom_call" | custom-call | bytes 589824 | tf_op jit(solution)/shard_map/pallas_call | solution.py:85
  1.2 2.5 %collective-permute-start.1 = (bf16[64,1152]{1,0:T(8,128)(2,1)S(1)}, bf16[64,1152]{1,0:T(8,128)(2,1)S(1)}, u32[]{:S(2)}, u32[]{:S(2)}) collective-permute-start(bf16[64,1152]{1,0:T(8,128)(2,1)S(1)} %get-tuple-element.9.refs_1_.refs_2_), channel_id=1, source_target_pairs={{0,3},{1,2},{4,1},{5,0},{8,5},{9,4},{12,9},{13,8},{14,13},{15,12},... | collective-permute-start | bytes 442376 | tf_op jit(solution)/shard_map/ppermute | solution.py:40
  3.8 1.9 %collective-permute-start.5 = (bf16[64,1152]{1,0:T(8,128)(2,1)S(1)}, bf16[64,1152]{1,0:T(8,128)(2,1)S(1)}, u32[]{:S(2)}, u32[]{:S(2)}) collective-permute-start(bf16[64,1152]{1,0:T(8,128)(2,1)S(1)} %get-tuple-element.10.refs_0_.refs_1_), channel_id=1, source_target_pairs={{0,5},{1,4},{4,9},{5,8},{8,13},{9,12},{12,15},{13,14},{14,11},{15,... | collective-permute-start | bytes 442376 | tf_op jit(solution)/shard_map/ppermute | solution.py:40
  5.6 3.2 %shard_map.64 = bf16[8,128,2304]{2,1,0:T(8,128)(2,1)S(1)} custom-call(bf16[128,8192]{1,0:T(8,128)(2,1)} %act.11, bf16[128,28672]{1,0:T(8,128)(2,1)} %grad.11), custom_call_target="tpu_custom_call" | custom-call | bytes 9437184 | tf_op jit(solution)/shard_map/pallas_call | solution.py:108
  8.9 0.6 %collective-permute-start = (bf16[8,128,2304]{2,1,0:T(8,128)(2,1)S(1)}, bf16[8,128,2304]{2,1,0:T(8,128)(2,1)S(1)}, u32[]{:S(2)}, u32[]{:S(2)}) collective-permute-start(bf16[8,128,2304]{2,1,0:T(8,128)(2,1)S(1)} %shard_map.64), channel_id=1, source_target_pairs={{0,1},{1,0},{2,3},{3,2},{4,5},{5,4},{6,7},{7,6},{8,9},{9,8},{10,11... | collective-permute-start | bytes 14155784 | tf_op jit(solution)/shard_map/ppermute | solution.py:44
  9.9 2.4 %collective-permute-done.5.refs_3_ = bf16[64,1152]{1,0:T(8,128)(2,1)S(1)} collective-permute-done((bf16[64,1152]{1,0:T(8,128)(2,1)S(1)}, bf16[64,1152]{1,0:T(8,128)(2,1)S(1)}, u32[]{:S(2)}, u32[]{:S(2)}) %collective-permute-start.5) | collective-permute-done | bytes 147488 | tf_op jit(solution)/shard_map/ppermute | solution.py:40
  12.3 1.0 %collective-permute-start.6 = (bf16[64,1152]{1,0:T(8,128)(2,1)S(1)}, bf16[64,1152]{1,0:T(8,128)(2,1)S(1)}, u32[]{:S(2)}, u32[]{:S(2)}) collective-permute-start(bf16[64,1152]{1,0:T(8,128)(2,1)S(1)} %collective-permute-done.5.refs_3_), channel_id=1, source_target_pairs={{0,5},{1,4},{4,9},{5,8},{8,13},{9,12},{12,15},{13,14},{14,11},{15,... | collective-permute-start | bytes 442376 | tf_op jit(solution)/shard_map/ppermute | solution.py:40
  13.3 0.8 %collective-permute-start.2 = (bf16[64,1152]{1,0:T(8,128)(2,1)S(1)}, bf16[64,1152]{1,0:T(8,128)(2,1)S(1)}, u32[]{:S(2)}, u32[]{:S(2)}) collective-permute-start(bf16[64,1152]{1,0:T(8,128)(2,1)S(1)} %collective-permute-done.1.refs_6_), channel_id=1, source_target_pairs={{0,3},{1,2},{4,1},{5,0},{8,5},{9,4},{12,9},{13,8},{14,13},{15,12},... | collective-permute-start | bytes 442376 | tf_op jit(solution)/shard_map/ppermute | solution.py:40
  14.1 1.0 %collective-permute-start.10 = (bf16[64,1152]{1,0:T(8,128)(2,1)S(1)}, bf16[64,1152]{1,0:T(8,128)(2,1)S(1)}, u32[]{:S(2)}, u32[]{:S(2)}) collective-permute-start(bf16[64,1152]{1,0:T(8,128)(2,1)S(1)} %collective-permute-done.9.refs_4_), channel_id=1, source_target_pairs={{0,5},{1,4},{4,9},{5,8},{8,13},{9,12},{12,15},{13,14},{14,11},{15,... | collective-permute-start | bytes 442376 | tf_op jit(solution)/shard_map/ppermute | solution.py:40
  15.1 0.8 %collective-permute-start.13 = (bf16[64,1152]{1,0:T(8,128)(2,1)S(1)}, bf16[64,1152]{1,0:T(8,128)(2,1)S(1)}, u32[]{:S(2)}, u32[]{:S(2)}) collective-permute-start(bf16[64,1152]{1,0:T(8,128)(2,1)S(1)} %collective-permute-done.12.refs_5_), channel_id=1, source_target_pairs={{0,3},{1,2},{4,1},{5,0},{8,5},{9,4},{12,9},{13,8},{14,13},{15,12},... | collective-permute-start | bytes 442376 | tf_op jit(solution)/shard_map/ppermute | solution.py:40
  15.9 2.0 %collective-permute-done.6.refs_7_ = bf16[64,1152]{1,0:T(8,128)(2,1)S(1)} collective-permute-done((bf16[64,1152]{1,0:T(8,128)(2,1)S(1)}, bf16[64,1152]{1,0:T(8,128)(2,1)S(1)}, u32[]{:S(2)}, u32[]{:S(2)}) %collective-permute-start.6) | collective-permute-done | bytes 147488 | tf_op jit(solution)/shard_map/ppermute | solution.py:40
  17.8 1.9 %collective-permute-start.7 = (bf16[64,1152]{1,0:T(8,128)(2,1)S(1)}, bf16[64,1152]{1,0:T(8,128)(2,1)S(1)}, u32[]{:S(2)}, u32[]{:S(2)}) collective-permute-start(bf16[64,1152]{1,0:T(8,128)(2,1)S(1)} %collective-permute-done.6.refs_7_), channel_id=1, source_target_pairs={{0,5},{1,4},{4,9},{5,8},{8,13},{9,12},{12,15},{13,14},{14,11},{15,... | collective-permute-start | bytes 442376 | tf_op jit(solution)/shard_map/ppermute | solution.py:40
  19.8 0.8 %collective-permute-start.3 = (bf16[64,1152]{1,0:T(8,128)(2,1)S(1)}, bf16[64,1152]{1,0:T(8,128)(2,1)S(1)}, u32[]{:S(2)}, u32[]{:S(2)}) collective-permute-start(bf16[64,1152]{1,0:T(8,128)(2,1)S(1)} %collective-permute-done.2.refs_10_), channel_id=1, source_target_pairs={{0,3},{1,2},{4,1},{5,0},{8,5},{9,4},{12,9},{13,8},{14,13},{15,12},... | collective-permute-start | bytes 442376 | tf_op jit(solution)/shard_map/ppermute | solution.py:40
  21.0 1.9 %collective-permute-start.11 = (bf16[64,1152]{1,0:T(8,128)(2,1)S(1)}, bf16[64,1152]{1,0:T(8,128)(2,1)S(1)}, u32[]{:S(2)}, u32[]{:S(2)}) collective-permute-start(bf16[64,1152]{1,0:T(8,128)(2,1)S(1)} %collective-permute-done.10.refs_8_), channel_id=1, source_target_pairs={{0,5},{1,4},{4,9},{5,8},{8,13},{9,12},{12,15},{13,14},{14,11},{15,... | collective-permute-start | bytes 442376 | tf_op jit(solution)/shard_map/ppermute | solution.py:40
  24.1 2.0 %collective-permute-start.8 = (bf16[64,1152]{1,0:T(8,128)(2,1)S(1)}, bf16[64,1152]{1,0:T(8,128)(2,1)S(1)}, u32[]{:S(2)}, u32[]{:S(2)}) collective-permute-start(bf16[64,1152]{1,0:T(8,128)(2,1)S(1)} %collective-permute-done.7.refs_1_), channel_id=1, source_target_pairs={{0,5},{1,4},{4,9},{5,8},{8,13},{9,12},{12,15},{13,14},{14,11},{15,... | collective-permute-start | bytes 442376 | tf_op jit(solution)/shard_map/ppermute | solution.py:40
  26.2 0.8 %collective-permute-start.4 = (bf16[64,1152]{1,0:T(8,128)(2,1)S(1)}, bf16[64,1152]{1,0:T(8,128)(2,1)S(1)}, u32[]{:S(2)}, u32[]{:S(2)}) collective-permute-start(bf16[64,1152]{1,0:T(8,128)(2,1)S(1)} %collective-permute-done.3.refs_4_), channel_id=1, source_target_pairs={{0,3},{1,2},{4,1},{5,0},{8,5},{9,4},{12,9},{13,8},{14,13},{15,12},... | collective-permute-start | bytes 442376 | tf_op jit(solution)/shard_map/ppermute | solution.py:40
  27.0 1.6 %shard_map.67.refs_5_ = f32[256,128]{1,0:T(8,128)S(1)} custom-call(bf16[128,8192]{1,0:T(8,128)(2,1)S(1)} %copy-done.1, bf16[128,28672]{1,0:T(8,128)(2,1)S(1)} %bitcast.12, bf16[8,128,2304]{2,1,0:T(8,128)(2,1)S(1)} %collective-permute-done.refs_0_, bf16[64,1152]{1,0:T(8,128)(2,1)S(1)} %get-tuple-element.10.refs_0_.refs_1_, ...), custom_call_target="tpu_custom_call" | custom-call | flops 377487360 | bytes 7372800 | tf_op jit(solution)/shard_map/pallas_call | solution.py:167
  29.1 0.8 %shard_map.68.refs_2_ = f32[256,128]{1,0:T(8,128)S(1)} custom-call(bf16[128,8192]{1,0:T(8,128)(2,1)S(1)} %copy-done.1, bf16[128,28672]{1,0:T(8,128)(2,1)S(1)} %bitcast.12, bf16[8,128,2304]{2,1,0:T(8,128)(2,1)S(1)} %collective-permute-done.refs_0_, bf16[64,1152]{1,0:T(8,128)(2,1)S(1)} %collective-permute-done.7.refs_1_, ...), custom_call_target="tpu_custom_call" | custom-call | flops 150994944 | bytes 2949120 | tf_op jit(solution)/shard_map/pallas_call | solution.py:167
  30.9 1.4 %collective-permute-done.4.refs_1_ = bf16[64,1152]{1,0:T(8,128)(2,1)S(1)} collective-permute-done((bf16[64,1152]{1,0:T(8,128)(2,1)S(1)}, bf16[64,1152]{1,0:T(8,128)(2,1)S(1)}, u32[]{:S(2)}, u32[]{:S(2)}) %collective-permute-start.4) | collective-permute-done | bytes 147488 | tf_op jit(solution)/shard_map/ppermute | solution.py:40
  32.9 1.2 %collective-permute-done.15 = f32[256,128]{1,0:T(8,128)S(1)} collective-permute-done((f32[256,128]{1,0:T(8,128)S(1)}, f32[256,128]{1,0:T(8,128)S(1)}, u32[]{:S(2)}, u32[]{:S(2)}) %collective-permute-start.15) | collective-permute-done | bytes 131104 | tf_op jit(solution)/shard_map/ppermute | solution.py:44
  34.5 12.4 %all_to_all.10 = f32[8,32,128]{2,1,0:T(8,128)S(1)} all-to-all(f32[8,32,128]{2,1,0:T(8,128)S(1)} %broadcast_in_dim.14), channel_id=1, replica_groups={{0,2,4,6,8,10,12,14},{1,3,5,7,9,11,13,15},{16,18,20,22,24,26,28,30},{17..., dimensions={0} | all-to-all | bytes 262144 | tf_op jit(solution)/shard_map/all_to_all | solution.py:201
  46.9 0.6 %convolution_convert_fusion = bf16[2,256]{1,0:T(2,128)(2,1)S(1)} fusion(bf16[256,4096]{1,0:T(8,128)(2,1)S(1)} %copy-done, bf16[1,2,32,128]{3,2,1,0:T(8,128)(2,1)S(1)} %bitcast.14), kind=kOutput, calls=%fused_computation.1 | convolution fusion | flops 4194816 | bytes 2114560 | tf_op jit(solution)/shard_map/dot_general | solution.py:24
  47.6 9.1 %all_to_all.11.conditioned = bf16[16,2,256]{2,1,0:T(2,128)(2,1)S(1)} all-to-all(bf16[16,2,256]{2,1,0:T(2,128)(2,1)S(1)} %broadcast_in_dim.15), channel_id=1, replica_groups={{0,1,2,3,4,5,6,7,8,9,10,11,12,13,14,15},{16,17,18,19,20,21,22,23,24,25,..., dimensions={0} | all-to-all | bytes 32768 | tf_op jit(solution)/shard_map/all_to_all | solution.py:201
  56.6 0.7 %shard_map.71 = f32[2,8]{1,0:T(2,128)} custom-call(bf16[16,2,256]{2,1,0:T(2,128)(2,1)S(1)} %all_to_all.11.conditioned, bf16[8,4096]{1,0:T(8,128)(2,1)S(1)} %copy-done.2), custom_call_target="tpu_custom_call" | custom-call | tf_op jit(solution)/shard_map/pallas_call | solution.py:190
  (37 shorter events, 4.6 us)
Async XLA Ops:
  0.0 46.9 %copy-start = (bf16[256,4096]{1,0:T(8,128)(2,1)S(1)}, bf16[256,4096]{1,0:T(8,128)(2,1)}, u32[]{:S(2)}) copy-start(bf16[256,4096]{1,0:T(8,128)(2,1)} %param.10) | copy-start | bytes 6291460
  1.2 12.2 %collective-permute-start.1 = (bf16[64,1152]{1,0:T(8,128)(2,1)S(1)}, bf16[64,1152]{1,0:T(8,128)(2,1)S(1)}, u32[]{:S(2)}, u32[]{:S(2)}) collective-permute-start(bf16[64,1152]{1,0:T(8,128)(2,1)S(1)} %get-tuple-element.9.refs_1_.refs_2_), channel_id=1, source_target_pairs={{0,3},{1,2},{4,1},{5,0},{8,5},{9,4},{12,9},{13,8},{14,13},{15,12},... | collective-permute-start | bytes 442376 | tf_op jit(solution)/shard_map/ppermute | solution.py:40
  3.6 10.5 %collective-permute-start.9 = (bf16[64,1152]{1,0:T(8,128)(2,1)S(1)}, bf16[64,1152]{1,0:T(8,128)(2,1)S(1)}, u32[]{:S(2)}, u32[]{:S(2)}) collective-permute-start(bf16[64,1152]{1,0:T(8,128)(2,1)S(1)} %get-tuple-element.9.refs_1_.refs_2_), channel_id=1, source_target_pairs={{0,5},{1,4},{4,9},{5,8},{8,13},{9,12},{12,15},{13,14},{14,11},{15,... | collective-permute-start | bytes 442376 | tf_op jit(solution)/shard_map/ppermute | solution.py:40
  3.7 5.8 %slice-start = ((s8[7340032]{0:T(1024)(128)(4,1)}), s8[4194304]{0:T(1024)(128)(4,1)S(1)}, s32[]{:S(2)}) async-start(s8[7340032]{0:T(1024)(128)(4,1)} %bitcast.11), calls=%async_computation.2 | async-start | bytes 8388608
  3.8 5.8 %slice-start.1 = ((s8[7340032]{0:T(1024)(128)(4,1)}), s8[3145728]{0:T(1024)(128)(4,1)S(1)}, s32[]{:S(2)}) async-start(s8[7340032]{0:T(1024)(128)(4,1)} %bitcast.11), calls=%async_computation.3 | async-start | bytes 6291456
  3.8 5.8 %copy-start.1 = (bf16[128,8192]{1,0:T(8,128)(2,1)S(1)}, bf16[128,8192]{1,0:T(8,128)(2,1)}, u32[]{:S(2)}) copy-start(bf16[128,8192]{1,0:T(8,128)(2,1)} %act.11) | copy-start | bytes 6291460
  3.8 8.6 %collective-permute-start.5 = (bf16[64,1152]{1,0:T(8,128)(2,1)S(1)}, bf16[64,1152]{1,0:T(8,128)(2,1)S(1)}, u32[]{:S(2)}, u32[]{:S(2)}) collective-permute-start(bf16[64,1152]{1,0:T(8,128)(2,1)S(1)} %get-tuple-element.10.refs_0_.refs_1_), channel_id=1, source_target_pairs={{0,5},{1,4},{4,9},{5,8},{8,13},{9,12},{12,15},{13,14},{14,11},{15,... | collective-permute-start | bytes 442376 | tf_op jit(solution)/shard_map/ppermute | solution.py:40
  5.6 9.5 %collective-permute-start.12 = (bf16[64,1152]{1,0:T(8,128)(2,1)S(1)}, bf16[64,1152]{1,0:T(8,128)(2,1)S(1)}, u32[]{:S(2)}, u32[]{:S(2)}) collective-permute-start(bf16[64,1152]{1,0:T(8,128)(2,1)S(1)} %get-tuple-element.10.refs_0_.refs_1_), channel_id=1, source_target_pairs={{0,3},{1,2},{4,1},{5,0},{8,5},{9,4},{12,9},{13,8},{14,13},{15,12},... | collective-permute-start | bytes 442376 | tf_op jit(solution)/shard_map/ppermute | solution.py:40
  8.9 18.1 %collective-permute-start = (bf16[8,128,2304]{2,1,0:T(8,128)(2,1)S(1)}, bf16[8,128,2304]{2,1,0:T(8,128)(2,1)S(1)}, u32[]{:S(2)}, u32[]{:S(2)}) collective-permute-start(bf16[8,128,2304]{2,1,0:T(8,128)(2,1)S(1)} %shard_map.64), channel_id=1, source_target_pairs={{0,1},{1,0},{2,3},{3,2},{4,5},{5,4},{6,7},{7,6},{8,9},{9,8},{10,11... | collective-permute-start | bytes 14155784 | tf_op jit(solution)/shard_map/ppermute | solution.py:44
  12.3 5.5 %collective-permute-start.6 = (bf16[64,1152]{1,0:T(8,128)(2,1)S(1)}, bf16[64,1152]{1,0:T(8,128)(2,1)S(1)}, u32[]{:S(2)}, u32[]{:S(2)}) collective-permute-start(bf16[64,1152]{1,0:T(8,128)(2,1)S(1)} %collective-permute-done.5.refs_3_), channel_id=1, source_target_pairs={{0,5},{1,4},{4,9},{5,8},{8,13},{9,12},{12,15},{13,14},{14,11},{15,... | collective-permute-start | bytes 442376 | tf_op jit(solution)/shard_map/ppermute | solution.py:40
  13.3 6.4 %collective-permute-start.2 = (bf16[64,1152]{1,0:T(8,128)(2,1)S(1)}, bf16[64,1152]{1,0:T(8,128)(2,1)S(1)}, u32[]{:S(2)}, u32[]{:S(2)}) collective-permute-start(bf16[64,1152]{1,0:T(8,128)(2,1)S(1)} %collective-permute-done.1.refs_6_), channel_id=1, source_target_pairs={{0,3},{1,2},{4,1},{5,0},{8,5},{9,4},{12,9},{13,8},{14,13},{15,12},... | collective-permute-start | bytes 442376 | tf_op jit(solution)/shard_map/ppermute | solution.py:40
  14.1 6.9 %collective-permute-start.10 = (bf16[64,1152]{1,0:T(8,128)(2,1)S(1)}, bf16[64,1152]{1,0:T(8,128)(2,1)S(1)}, u32[]{:S(2)}, u32[]{:S(2)}) collective-permute-start(bf16[64,1152]{1,0:T(8,128)(2,1)S(1)} %collective-permute-done.9.refs_4_), channel_id=1, source_target_pairs={{0,5},{1,4},{4,9},{5,8},{8,13},{9,12},{12,15},{13,14},{14,11},{15,... | collective-permute-start | bytes 442376 | tf_op jit(solution)/shard_map/ppermute | solution.py:40
  15.1 7.8 %collective-permute-start.13 = (bf16[64,1152]{1,0:T(8,128)(2,1)S(1)}, bf16[64,1152]{1,0:T(8,128)(2,1)S(1)}, u32[]{:S(2)}, u32[]{:S(2)}) collective-permute-start(bf16[64,1152]{1,0:T(8,128)(2,1)S(1)} %collective-permute-done.12.refs_5_), channel_id=1, source_target_pairs={{0,3},{1,2},{4,1},{5,0},{8,5},{9,4},{12,9},{13,8},{14,13},{15,12},... | collective-permute-start | bytes 442376 | tf_op jit(solution)/shard_map/ppermute | solution.py:40
  17.8 6.3 %collective-permute-start.7 = (bf16[64,1152]{1,0:T(8,128)(2,1)S(1)}, bf16[64,1152]{1,0:T(8,128)(2,1)S(1)}, u32[]{:S(2)}, u32[]{:S(2)}) collective-permute-start(bf16[64,1152]{1,0:T(8,128)(2,1)S(1)} %collective-permute-done.6.refs_7_), channel_id=1, source_target_pairs={{0,5},{1,4},{4,9},{5,8},{8,13},{9,12},{12,15},{13,14},{14,11},{15,... | collective-permute-start | bytes 442376 | tf_op jit(solution)/shard_map/ppermute | solution.py:40
  19.8 6.4 %collective-permute-start.3 = (bf16[64,1152]{1,0:T(8,128)(2,1)S(1)}, bf16[64,1152]{1,0:T(8,128)(2,1)S(1)}, u32[]{:S(2)}, u32[]{:S(2)}) collective-permute-start(bf16[64,1152]{1,0:T(8,128)(2,1)S(1)} %collective-permute-done.2.refs_10_), channel_id=1, source_target_pairs={{0,3},{1,2},{4,1},{5,0},{8,5},{9,4},{12,9},{13,8},{14,13},{15,12},... | collective-permute-start | bytes 442376 | tf_op jit(solution)/shard_map/ppermute | solution.py:40
  21.0 7.6 %collective-permute-start.11 = (bf16[64,1152]{1,0:T(8,128)(2,1)S(1)}, bf16[64,1152]{1,0:T(8,128)(2,1)S(1)}, u32[]{:S(2)}, u32[]{:S(2)}) collective-permute-start(bf16[64,1152]{1,0:T(8,128)(2,1)S(1)} %collective-permute-done.10.refs_8_), channel_id=1, source_target_pairs={{0,5},{1,4},{4,9},{5,8},{8,13},{9,12},{12,15},{13,14},{14,11},{15,... | collective-permute-start | bytes 442376 | tf_op jit(solution)/shard_map/ppermute | solution.py:40
  22.9 6.2 %collective-permute-start.14 = (bf16[64,1152]{1,0:T(8,128)(2,1)S(1)}, bf16[64,1152]{1,0:T(8,128)(2,1)S(1)}, u32[]{:S(2)}, u32[]{:S(2)}) collective-permute-start(bf16[64,1152]{1,0:T(8,128)(2,1)S(1)} %collective-permute-done.13.refs_9_), channel_id=1, source_target_pairs={{0,3},{1,2},{4,1},{5,0},{8,5},{9,4},{12,9},{13,8},{14,13},{15,12},... | collective-permute-start | bytes 442376 | tf_op jit(solution)/shard_map/ppermute | solution.py:40
  24.1 6.3 %collective-permute-start.8 = (bf16[64,1152]{1,0:T(8,128)(2,1)S(1)}, bf16[64,1152]{1,0:T(8,128)(2,1)S(1)}, u32[]{:S(2)}, u32[]{:S(2)}) collective-permute-start(bf16[64,1152]{1,0:T(8,128)(2,1)S(1)} %collective-permute-done.7.refs_1_), channel_id=1, source_target_pairs={{0,5},{1,4},{4,9},{5,8},{8,13},{9,12},{12,15},{13,14},{14,11},{15,... | collective-permute-start | bytes 442376 | tf_op jit(solution)/shard_map/ppermute | solution.py:40
  26.2 6.1 %collective-permute-start.4 = (bf16[64,1152]{1,0:T(8,128)(2,1)S(1)}, bf16[64,1152]{1,0:T(8,128)(2,1)S(1)}, u32[]{:S(2)}, u32[]{:S(2)}) collective-permute-start(bf16[64,1152]{1,0:T(8,128)(2,1)S(1)} %collective-permute-done.3.refs_4_), channel_id=1, source_target_pairs={{0,3},{1,2},{4,1},{5,0},{8,5},{9,4},{12,9},{13,8},{14,13},{15,12},... | collective-permute-start | bytes 442376 | tf_op jit(solution)/shard_map/ppermute | solution.py:40
  32.7 24.0 %copy-start.2 = (bf16[8,4096]{1,0:T(8,128)(2,1)S(1)}, bf16[8,4096]{1,0:T(8,128)(2,1)}, u32[]{:S(2)}) copy-start(bf16[8,4096]{1,0:T(8,128)(2,1)} %queries.1) | copy-start | bytes 196612
  32.7 1.4 %collective-permute-start.15 = (f32[256,128]{1,0:T(8,128)S(1)}, f32[256,128]{1,0:T(8,128)S(1)}, u32[]{:S(2)}, u32[]{:S(2)}) collective-permute-start(f32[256,128]{1,0:T(8,128)S(1)} %shard_map.70), channel_id=1, source_target_pairs={{0,1},{1,0},{2,3},{3,2},{4,5},{5,4},{6,7},{7,6},{8,9},{9,8},{10,11... | collective-permute-start | bytes 393224 | tf_op jit(solution)/shard_map/ppermute | solution.py:44

commit v21 on v18

--- a/solution.py
+++ b/solution.py
@@ -202,14 +202,14 @@
     total = (total + jnp.concatenate([theirs[rows:], theirs[:rows]], axis=0)).astype(jnp.bfloat16)
 
     raw = dot(total[:, rank:], total[:, :rank], TN)
-    raw = (raw * (1.0 / math.sqrt(LEN))).reshape(-1, 128)
-    groups = [[2 * i + (c ^ (i & 1)) for i in range(chips)] for c in range(2)]
-    raw = to_all(raw, groups)
-    features = raw.reshape((-1, split // 2) + raw.shape[1:]).sum(axis=1)
-    features = features.astype(jnp.bfloat16).reshape(-1, rank * rank)
+    raw = (raw * (1.0 / math.sqrt(LEN))).reshape(2, -1, 128)
+    half = lax.dynamic_index_in_dim(raw, lax.axis_index("dp") & 1, keepdims=False)
+    everyone = [list(range(n))]
+    raw = to_all(half, everyone).reshape((-1, split // 2) + raw.shape)
+    features = raw.sum(axis=1).astype(jnp.bfloat16).reshape(-1, rank * rank)
 
     conditioned = dot(features, preconditioner, NT).astype(jnp.bfloat16)
-    return score(to_all(conditioned, [list(range(n))]), queries, 1.0 / rank)
+    return score(to_all(conditioned, everyone), queries, 1.0 / rank)
 
 
 def local_gathered(activations, out_grads, in_basis, out_basis, preconditioner, queries):

time: 56.7 us -> 57 us (level)
  no operation moved by 1% of the time
where the time goes in v21:
time: 57 us; the launch traced here: 56.7 us
  blocking collectives  22.2 us (39%)
  starting transfers between devices  16.1 us (28%)
  waiting for transfers between devices  10.4 us (18%)
  Pallas kernels  6.81 us (12%)
  matrix products  0.89 us (2%)
    all_to_all x2, blocking collectives, to_all(): lax.all_to_all(copies, 'dp', 0, 0, axis_index_groups=groups, tiled=True)  22.2 us
    ppermute x14, starting transfers between devices, ring(): return lax.ppermute(x, 'dp', pairs)  15.4 us
    ppermute x14, waiting for transfers between devices, ring(): return lax.ppermute(x, 'dp', pairs)  9.17 us
    pallas_call x4, Pallas kernels, project(): pl.pallas_call(functools.partial(project_kernel, chips, items, a_width, c...  3.34 us
    pallas_call x1, Pallas kernels, start(): pl.pallas_call(functools.partial(start_kernel, chips), out_shape=[pltpu.V...  2.74 us
    ppermute x2, waiting for transfers between devices, swap(): return lax.ppermute(x, 'dp', [(i, i ^ bit) for i in range(n)])  1.24 us
  transfers between devices with their start and end apart: 16, of which 9 were waited for; matrix products, arithmetic and copies ran while one was open for 0% of the time, Pallas kernels for 5%

profile of v21, /device:TPU:0, one launch (start us, length us, event | category | flops | bytes accessed | tf_op | source)
XLA Modules:
  0.0 56.7 jit_solution(12355058888580546842)
XLA Ops:
  0.0 2.7 %shard_map.64 = (bf16[64,1152]{1,0:T(8,128)(2,1)S(1)}, bf16[64,1152]{1,0:T(8,128)(2,1)S(1)}, bf16[8,128,2304]{2,1,0:T(8,128)(2,1)S(1)}) custom-call(bf16[128,8192]{1,0:T(8,128)(2,1)} %act.9, bf16[128,28672]{1,0:T(8,128)(2,1)} %grad.9, bf16[64,512]{1,0:T(8,128)(2,1)} %bitcast.13, bf16[64,1792]{1,0:T(8,128)(2,1)} %bitcast.12), custom_call_target="tpu_custom_call" | custom-call | bytes 10027008 | tf_op jit(solution)/shard_map/pallas_call | solution.py:90
  2.8 0.5 collective-permute-start
  3.3 2.7 %collective-permute-start.5 = (bf16[64,1152]{1,0:T(8,128)(2,1)S(1)}, bf16[64,1152]{1,0:T(8,128)(2,1)S(1)}, u32[]{:S(2)}, u32[]{:S(2)}) collective-permute-start(bf16[64,1152]{1,0:T(8,128)(2,1)S(1)} %get-tuple-element.10.refs_0_), channel_id=1, source_target_pairs={{0,5},{1,4},{4,9},{5,8},{8,13},{9,12},{12,15},{13,14},{14,11},{15,... | collective-permute-start | bytes 442376 | tf_op jit(solution)/shard_map/ppermute | solution.py:39
  6.0 1.7 %collective-permute-start.9 = (bf16[64,1152]{1,0:T(8,128)(2,1)S(1)}, bf16[64,1152]{1,0:T(8,128)(2,1)S(1)}, u32[]{:S(2)}, u32[]{:S(2)}) collective-permute-start(bf16[64,1152]{1,0:T(8,128)(2,1)S(1)} %get-tuple-element.9.refs_1_), channel_id=1, source_target_pairs={{0,5},{1,4},{4,9},{5,8},{8,13},{9,12},{12,15},{13,14},{14,11},{15,... | collective-permute-start | bytes 442376 | tf_op jit(solution)/shard_map/ppermute | solution.py:39
  7.7 2.4 %collective-permute-done.5.refs_2_ = bf16[64,1152]{1,0:T(8,128)(2,1)S(1)} collective-permute-done((bf16[64,1152]{1,0:T(8,128)(2,1)S(1)}, bf16[64,1152]{1,0:T(8,128)(2,1)S(1)}, u32[]{:S(2)}, u32[]{:S(2)}) %collective-permute-start.5) | collective-permute-done | bytes 147488 | tf_op jit(solution)/shard_map/ppermute | solution.py:39
  10.2 2.2 %collective-permute-start.6 = (bf16[64,1152]{1,0:T(8,128)(2,1)S(1)}, bf16[64,1152]{1,0:T(8,128)(2,1)S(1)}, u32[]{:S(2)}, u32[]{:S(2)}) collective-permute-start(bf16[64,1152]{1,0:T(8,128)(2,1)S(1)} %collective-permute-done.5.refs_2_), channel_id=1, source_target_pairs={{0,5},{1,4},{4,9},{5,8},{8,13},{9,12},{12,15},{13,14},{14,11},{15,... | collective-permute-start | bytes 442376 | tf_op jit(solution)/shard_map/ppermute | solution.py:39
  12.4 0.9 %collective-permute-done.9.refs_3_ = bf16[64,1152]{1,0:T(8,128)(2,1)S(1)} collective-permute-done((bf16[64,1152]{1,0:T(8,128)(2,1)S(1)}, bf16[64,1152]{1,0:T(8,128)(2,1)S(1)}, u32[]{:S(2)}, u32[]{:S(2)}) %collective-permute-start.9) | collective-permute-done | bytes 147488 | tf_op jit(solution)/shard_map/ppermute | solution.py:39
  13.2 2.2 %collective-permute-start.10 = (bf16[64,1152]{1,0:T(8,128)(2,1)S(1)}, bf16[64,1152]{1,0:T(8,128)(2,1)S(1)}, u32[]{:S(2)}, u32[]{:S(2)}) collective-permute-start(bf16[64,1152]{1,0:T(8,128)(2,1)S(1)} %collective-permute-done.9.refs_3_), channel_id=1, source_target_pairs={{0,5},{1,4},{4,9},{5,8},{8,13},{9,12},{12,15},{13,14},{14,11},{15,... | collective-permute-start | bytes 442376 | tf_op jit(solution)/shard_map/ppermute | solution.py:39
  15.4 1.1 %collective-permute-done.6.refs_6_ = bf16[64,1152]{1,0:T(8,128)(2,1)S(1)} collective-permute-done((bf16[64,1152]{1,0:T(8,128)(2,1)S(1)}, bf16[64,1152]{1,0:T(8,128)(2,1)S(1)}, u32[]{:S(2)}, u32[]{:S(2)}) %collective-permute-start.6) | collective-permute-done | bytes 147488 | tf_op jit(solution)/shard_map/ppermute | solution.py:39
  16.5 2.2 %collective-permute-start.7 = (bf16[64,1152]{1,0:T(8,128)(2,1)S(1)}, bf16[64,1152]{1,0:T(8,128)(2,1)S(1)}, u32[]{:S(2)}, u32[]{:S(2)}) collective-permute-start(bf16[64,1152]{1,0:T(8,128)(2,1)S(1)} %collective-permute-done.6.refs_6_), channel_id=1, source_target_pairs={{0,5},{1,4},{4,9},{5,8},{8,13},{9,12},{12,15},{13,14},{14,11},{15,... | collective-permute-start | bytes 442376 | tf_op jit(solution)/shard_map/ppermute | solution.py:39
  18.7 0.9 %collective-permute-done.10.refs_7_ = bf16[64,1152]{1,0:T(8,128)(2,1)S(1)} collective-permute-done((bf16[64,1152]{1,0:T(8,128)(2,1)S(1)}, bf16[64,1152]{1,0:T(8,128)(2,1)S(1)}, u32[]{:S(2)}, u32[]{:S(2)}) %collective-permute-start.10) | collective-permute-done | bytes 147488 | tf_op jit(solution)/shard_map/ppermute | solution.py:39
  19.6 2.2 %collective-permute-start.11 = (bf16[64,1152]{1,0:T(8,128)(2,1)S(1)}, bf16[64,1152]{1,0:T(8,128)(2,1)S(1)}, u32[]{:S(2)}, u32[]{:S(2)}) collective-permute-start(bf16[64,1152]{1,0:T(8,128)(2,1)S(1)} %collective-permute-done.10.refs_7_), channel_id=1, source_target_pairs={{0,5},{1,4},{4,9},{5,8},{8,13},{9,12},{12,15},{13,14},{14,11},{15,... | collective-permute-start | bytes 442376 | tf_op jit(solution)/shard_map/ppermute | solution.py:39
  21.8 1.0 %collective-permute-done.7.refs_0_ = bf16[64,1152]{1,0:T(8,128)(2,1)S(1)} collective-permute-done((bf16[64,1152]{1,0:T(8,128)(2,1)S(1)}, bf16[64,1152]{1,0:T(8,128)(2,1)S(1)}, u32[]{:S(2)}, u32[]{:S(2)}) %collective-permute-start.7) | collective-permute-done | bytes 147488 | tf_op jit(solution)/shard_map/ppermute | solution.py:39
  22.7 2.2 %collective-permute-start.8 = (bf16[64,1152]{1,0:T(8,128)(2,1)S(1)}, bf16[64,1152]{1,0:T(8,128)(2,1)S(1)}, u32[]{:S(2)}, u32[]{:S(2)}) collective-permute-start(bf16[64,1152]{1,0:T(8,128)(2,1)S(1)} %collective-permute-done.7.refs_0_), channel_id=1, source_target_pairs={{0,5},{1,4},{4,9},{5,8},{8,13},{9,12},{12,15},{13,14},{14,11},{15,... | collective-permute-start | bytes 442376 | tf_op jit(solution)/shard_map/ppermute | solution.py:39
  25.0 1.8 %shard_map.65.refs_4_ = f32[256,128]{1,0:T(8,128)S(1)} custom-call(bf16[128,8192]{1,0:T(8,128)(2,1)S(1)} %copy-done.2, bf16[128,28672]{1,0:T(8,128)(2,1)S(1)} %copy-done.1, bf16[8,128,2304]{2,1,0:T(8,128)(2,1)S(1)} %collective-permute-done.theirs, bf16[64,1152]{1,0:T(8,128)(2,1)S(1)} %get-tuple-element.10.refs_0_, ...), custom_call_target="tpu_custom_call" | custom-call | flops 377487360 | bytes 7372800 | tf_op jit(solution)/shard_map/pallas_call | solution.py:137
  26.7 1.1 %collective-permute-done.14.refs_2_ = bf16[64,1152]{1,0:T(8,128)(2,1)S(1)} collective-permute-done((bf16[64,1152]{1,0:T(8,128)(2,1)S(1)}, bf16[64,1152]{1,0:T(8,128)(2,1)S(1)}, u32[]{:S(2)}, u32[]{:S(2)}) %collective-permute-start.14) | collective-permute-done | bytes 147488 | tf_op jit(solution)/shard_map/ppermute | solution.py:39
  27.9 0.8 %shard_map.66.refs_1_ = f32[256,128]{1,0:T(8,128)S(1)} custom-call(bf16[128,8192]{1,0:T(8,128)(2,1)S(1)} %copy-done.2, bf16[128,28672]{1,0:T(8,128)(2,1)S(1)} %copy-done.1, bf16[8,128,2304]{2,1,0:T(8,128)(2,1)S(1)} %collective-permute-done.theirs, bf16[64,1152]{1,0:T(8,128)(2,1)S(1)} %collective-permute-done.7.refs_0_, ...), custom_call_target="tpu_custom_call" | custom-call | flops 150994944 | bytes 2949120 | tf_op jit(solution)/shard_map/pallas_call | solution.py:137
  28.8 0.4 shard_map.67.refs_1_
  29.2 1.7 %collective-permute-done.4.refs_0_ = bf16[64,1152]{1,0:T(8,128)(2,1)S(1)} collective-permute-done((bf16[64,1152]{1,0:T(8,128)(2,1)S(1)}, bf16[64,1152]{1,0:T(8,128)(2,1)S(1)}, u32[]{:S(2)}, u32[]{:S(2)}) %collective-permute-start.4) | collective-permute-done | bytes 147488 | tf_op jit(solution)/shard_map/ppermute | solution.py:39
  31.5 1.2 %collective-permute-done.15 = f32[256,128]{1,0:T(8,128)S(1)} collective-permute-done((f32[256,128]{1,0:T(8,128)S(1)}, f32[256,128]{1,0:T(8,128)S(1)}, u32[]{:S(2)}, u32[]{:S(2)}) %collective-permute-start.15) | collective-permute-done | bytes 131104 | tf_op jit(solution)/shard_map/ppermute | solution.py:43
  33.1 13.1 %all_to_all.10 = f32[16,16,128]{2,1,0:T(8,128)S(1)} all-to-all(f32[16,16,128]{2,1,0:T(8,128)S(1)} %broadcast_in_dim.7), channel_id=1, replica_groups={{0,1,2,3,4,5,6,7,8,9,10,11,12,13,14,15},{16,17,18,19,20,21,22,23,24,25,..., dimensions={0} | all-to-all | bytes 262144 | tf_op jit(solution)/shard_map/all_to_all | solution.py:171
  46.3 0.6 %convolution_convert_fusion = bf16[2,256]{1,0:T(2,128)(2,1)S(1)} fusion(bf16[256,4096]{1,0:T(8,128)(2,1)S(1)} %copy-done, bf16[1,2,32,128]{3,2,1,0:T(8,128)(2,1)S(1)} %bitcast.14), kind=kOutput, calls=%fused_computation.1 | convolution fusion | flops 4194816 | bytes 2114560 | tf_op jit(solution)/shard_map/dot_general | solution.py:23
  46.9 9.1 %all_to_all.11.conditioned = bf16[16,2,256]{2,1,0:T(2,128)(2,1)S(1)} all-to-all(bf16[16,2,256]{2,1,0:T(2,128)(2,1)S(1)} %broadcast_in_dim.16), channel_id=1, replica_groups={{0,1,2,3,4,5,6,7,8,9,10,11,12,13,14,15},{16,17,18,19,20,21,22,23,24,25,..., dimensions={0} | all-to-all | bytes 32768 | tf_op jit(solution)/shard_map/all_to_all | solution.py:171
  56.0 0.7 %shard_map.69 = f32[2,8]{1,0:T(2,128)} custom-call(bf16[16,2,256]{2,1,0:T(2,128)(2,1)S(1)} %all_to_all.11.conditioned, bf16[8,4096]{1,0:T(8,128)(2,1)S(1)} %copy-done.3), custom_call_target="tpu_custom_call" | custom-call | tf_op jit(solution)/shard_map/pallas_call | solution.py:160
  (33 shorter events, 1.1 us)
Async XLA Ops:
  0.0 46.3 %copy-start = (bf16[256,4096]{1,0:T(8,128)(2,1)S(1)}, bf16[256,4096]{1,0:T(8,128)(2,1)}, u32[]{:S(2)}) copy-start(bf16[256,4096]{1,0:T(8,128)(2,1)} %param.10) | copy-start | bytes 6291460
  0.0 24.9 %copy-start.1 = (bf16[128,28672]{1,0:T(8,128)(2,1)S(1)}, bf16[128,28672]{1,0:T(8,128)(2,1)}, u32[]{:S(2)}) copy-start(bf16[128,28672]{1,0:T(8,128)(2,1)} %grad.9) | copy-start | bytes 22020100
  0.0 24.9 %copy-start.2 = (bf16[128,8192]{1,0:T(8,128)(2,1)S(1)}, bf16[128,8192]{1,0:T(8,128)(2,1)}, u32[]{:S(2)}) copy-start(bf16[128,8192]{1,0:T(8,128)(2,1)} %act.9) | copy-start | bytes 6291460
  2.8 22.2 %collective-permute-start = (bf16[8,128,2304]{2,1,0:T(8,128)(2,1)S(1)}, bf16[8,128,2304]{2,1,0:T(8,128)(2,1)S(1)}, u32[]{:S(2)}, u32[]{:S(2)}) collective-permute-start(bf16[8,128,2304]{2,1,0:T(8,128)(2,1)S(1)} %get-tuple-element.8), channel_id=1, source_target_pairs={{0,1},{1,0},{2,3},{3,2},{4,5},{5,4},{6,7},{7,6},{8,9},{9,8},{10,11... | collective-permute-start | bytes 14155784 | tf_op jit(solution)/shard_map/ppermute | solution.py:43
  3.3 6.9 %collective-permute-start.5 = (bf16[64,1152]{1,0:T(8,128)(2,1)S(1)}, bf16[64,1152]{1,0:T(8,128)(2,1)S(1)}, u32[]{:S(2)}, u32[]{:S(2)}) collective-permute-start(bf16[64,1152]{1,0:T(8,128)(2,1)S(1)} %get-tuple-element.10.refs_0_), channel_id=1, source_target_pairs={{0,5},{1,4},{4,9},{5,8},{8,13},{9,12},{12,15},{13,14},{14,11},{15,... | collective-permute-start | bytes 442376 | tf_op jit(solution)/shard_map/ppermute | solution.py:39
  6.0 6.4 %collective-permute-start.1 = (bf16[64,1152]{1,0:T(8,128)(2,1)S(1)}, bf16[64,1152]{1,0:T(8,128)(2,1)S(1)}, u32[]{:S(2)}, u32[]{:S(2)}) collective-permute-start(bf16[64,1152]{1,0:T(8,128)(2,1)S(1)} %get-tuple-element.9.refs_1_), channel_id=1, source_target_pairs={{0,3},{1,2},{4,1},{5,0},{8,5},{9,4},{12,9},{13,8},{14,13},{15,12},... | collective-permute-start | bytes 442376 | tf_op jit(solution)/shard_map/ppermute | solution.py:39
  6.0 7.3 %collective-permute-start.9 = (bf16[64,1152]{1,0:T(8,128)(2,1)S(1)}, bf16[64,1152]{1,0:T(8,128)(2,1)S(1)}, u32[]{:S(2)}, u32[]{:S(2)}) collective-permute-start(bf16[64,1152]{1,0:T(8,128)(2,1)S(1)} %get-tuple-element.9.refs_1_), channel_id=1, source_target_pairs={{0,5},{1,4},{4,9},{5,8},{8,13},{9,12},{12,15},{13,14},{14,11},{15,... | collective-permute-start | bytes 442376 | tf_op jit(solution)/shard_map/ppermute | solution.py:39
  7.7 7.7 %collective-permute-start.12 = (bf16[64,1152]{1,0:T(8,128)(2,1)S(1)}, bf16[64,1152]{1,0:T(8,128)(2,1)S(1)}, u32[]{:S(2)}, u32[]{:S(2)}) collective-permute-start(bf16[64,1152]{1,0:T(8,128)(2,1)S(1)} %get-tuple-element.10.refs_0_), channel_id=1, source_target_pairs={{0,3},{1,2},{4,1},{5,0},{8,5},{9,4},{12,9},{13,8},{14,13},{15,12},... | collective-permute-start | bytes 442376 | tf_op jit(solution)/shard_map/ppermute | solution.py:39
  10.2 6.3 %collective-permute-start.6 = (bf16[64,1152]{1,0:T(8,128)(2,1)S(1)}, bf16[64,1152]{1,0:T(8,128)(2,1)S(1)}, u32[]{:S(2)}, u32[]{:S(2)}) collective-permute-start(bf16[64,1152]{1,0:T(8,128)(2,1)S(1)} %collective-permute-done.5.refs_2_), channel_id=1, source_target_pairs={{0,5},{1,4},{4,9},{5,8},{8,13},{9,12},{12,15},{13,14},{14,11},{15,... | collective-permute-start | bytes 442376 | tf_op jit(solution)/shard_map/ppermute | solution.py:39
  12.4 6.3 %collective-permute-start.2 = (bf16[64,1152]{1,0:T(8,128)(2,1)S(1)}, bf16[64,1152]{1,0:T(8,128)(2,1)S(1)}, u32[]{:S(2)}, u32[]{:S(2)}) collective-permute-start(bf16[64,1152]{1,0:T(8,128)(2,1)S(1)} %collective-permute-done.1.refs_5_), channel_id=1, source_target_pairs={{0,3},{1,2},{4,1},{5,0},{8,5},{9,4},{12,9},{13,8},{14,13},{15,12},... | collective-permute-start | bytes 442376 | tf_op jit(solution)/shard_map/ppermute | solution.py:39
  13.2 6.3 %collective-permute-start.10 = (bf16[64,1152]{1,0:T(8,128)(2,1)S(1)}, bf16[64,1152]{1,0:T(8,128)(2,1)S(1)}, u32[]{:S(2)}, u32[]{:S(2)}) collective-permute-start(bf16[64,1152]{1,0:T(8,128)(2,1)S(1)} %collective-permute-done.9.refs_3_), channel_id=1, source_target_pairs={{0,5},{1,4},{4,9},{5,8},{8,13},{9,12},{12,15},{13,14},{14,11},{15,... | collective-permute-start | bytes 442376 | tf_op jit(solution)/shard_map/ppermute | solution.py:39
  15.4 6.4 %collective-permute-start.13 = (bf16[64,1152]{1,0:T(8,128)(2,1)S(1)}, bf16[64,1152]{1,0:T(8,128)(2,1)S(1)}, u32[]{:S(2)}, u32[]{:S(2)}) collective-permute-start(bf16[64,1152]{1,0:T(8,128)(2,1)S(1)} %collective-permute-done.12.refs_4_), channel_id=1, source_target_pairs={{0,3},{1,2},{4,1},{5,0},{8,5},{9,4},{12,9},{13,8},{14,13},{15,12},... | collective-permute-start | bytes 442376 | tf_op jit(solution)/shard_map/ppermute | solution.py:39
  16.5 6.3 %collective-permute-start.7 = (bf16[64,1152]{1,0:T(8,128)(2,1)S(1)}, bf16[64,1152]{1,0:T(8,128)(2,1)S(1)}, u32[]{:S(2)}, u32[]{:S(2)}) collective-permute-start(bf16[64,1152]{1,0:T(8,128)(2,1)S(1)} %collective-permute-done.6.refs_6_), channel_id=1, source_target_pairs={{0,5},{1,4},{4,9},{5,8},{8,13},{9,12},{12,15},{13,14},{14,11},{15,... | collective-permute-start | bytes 442376 | tf_op jit(solution)/shard_map/ppermute | solution.py:39
  18.7 6.3 %collective-permute-start.3 = (bf16[64,1152]{1,0:T(8,128)(2,1)S(1)}, bf16[64,1152]{1,0:T(8,128)(2,1)S(1)}, u32[]{:S(2)}, u32[]{:S(2)}) collective-permute-start(bf16[64,1152]{1,0:T(8,128)(2,1)S(1)} %collective-permute-done.2.refs_9_), channel_id=1, source_target_pairs={{0,3},{1,2},{4,1},{5,0},{8,5},{9,4},{12,9},{13,8},{14,13},{15,12},... | collective-permute-start | bytes 442376 | tf_op jit(solution)/shard_map/ppermute | solution.py:39
  19.6 7.2 %collective-permute-start.11 = (bf16[64,1152]{1,0:T(8,128)(2,1)S(1)}, bf16[64,1152]{1,0:T(8,128)(2,1)S(1)}, u32[]{:S(2)}, u32[]{:S(2)}) collective-permute-start(bf16[64,1152]{1,0:T(8,128)(2,1)S(1)} %collective-permute-done.10.refs_7_), channel_id=1, source_target_pairs={{0,5},{1,4},{4,9},{5,8},{8,13},{9,12},{12,15},{13,14},{14,11},{15,... | collective-permute-start | bytes 442376 | tf_op jit(solution)/shard_map/ppermute | solution.py:39
  21.8 6.1 %collective-permute-start.14 = (bf16[64,1152]{1,0:T(8,128)(2,1)S(1)}, bf16[64,1152]{1,0:T(8,128)(2,1)S(1)}, u32[]{:S(2)}, u32[]{:S(2)}) collective-permute-start(bf16[64,1152]{1,0:T(8,128)(2,1)S(1)} %collective-permute-done.13.refs_8_), channel_id=1, source_target_pairs={{0,3},{1,2},{4,1},{5,0},{8,5},{9,4},{12,9},{13,8},{14,13},{15,12},... | collective-permute-start | bytes 442376 | tf_op jit(solution)/shard_map/ppermute | solution.py:39
  22.7 6.1 %collective-permute-start.8 = (bf16[64,1152]{1,0:T(8,128)(2,1)S(1)}, bf16[64,1152]{1,0:T(8,128)(2,1)S(1)}, u32[]{:S(2)}, u32[]{:S(2)}) collective-permute-start(bf16[64,1152]{1,0:T(8,128)(2,1)S(1)} %collective-permute-done.7.refs_0_), channel_id=1, source_target_pairs={{0,5},{1,4},{4,9},{5,8},{8,13},{9,12},{12,15},{13,14},{14,11},{15,... | collective-permute-start | bytes 442376 | tf_op jit(solution)/shard_map/ppermute | solution.py:39
  24.9 6.0 %collective-permute-start.4 = (bf16[64,1152]{1,0:T(8,128)(2,1)S(1)}, bf16[64,1152]{1,0:T(8,128)(2,1)S(1)}, u32[]{:S(2)}, u32[]{:S(2)}) collective-permute-start(bf16[64,1152]{1,0:T(8,128)(2,1)S(1)} %collective-permute-done.3.refs_3_), channel_id=1, source_target_pairs={{0,3},{1,2},{4,1},{5,0},{8,5},{9,4},{12,9},{13,8},{14,13},{15,12},... | collective-permute-start | bytes 442376 | tf_op jit(solution)/shard_map/ppermute | solution.py:39
  31.3 24.7 %copy-start.3 = (bf16[8,4096]{1,0:T(8,128)(2,1)S(1)}, bf16[8,4096]{1,0:T(8,128)(2,1)}, u32[]{:S(2)}) copy-start(bf16[8,4096]{1,0:T(8,128)(2,1)} %queries.1) | copy-start | bytes 196612
  31.3 1.4 %collective-permute-start.15 = (f32[256,128]{1,0:T(8,128)S(1)}, f32[256,128]{1,0:T(8,128)S(1)}, u32[]{:S(2)}, u32[]{:S(2)}) collective-permute-start(f32[256,128]{1,0:T(8,128)S(1)} %shard_map.68), channel_id=1, source_target_pairs={{0,1},{1,0},{2,3},{3,2},{4,5},{5,4},{6,7},{7,6},{8,9},{9,8},{10,11... | collective-permute-start | bytes 393224 | tf_op jit(solution)/shard_map/ppermute | solution.py:43

commit v22 on v18

--- a/solution.py
+++ b/solution.py
@@ -203,9 +203,10 @@
 
     raw = dot(total[:, rank:], total[:, :rank], TN)
     raw = (raw * (1.0 / math.sqrt(LEN))).reshape(-1, 128)
-    groups = [[2 * i + (c ^ (i & 1)) for i in range(chips)] for c in range(2)]
-    raw = to_all(raw, groups)
-    features = raw.reshape((-1, split // 2) + raw.shape[1:]).sum(axis=1)
+    me = lax.axis_index("dp")
+    sequence = lax.broadcasted_iota(jnp.int32, (n // split, 1, 1), 0)
+    gives = (sequence == me // split) & ((me & 1) == 0)
+    features = lax.psum(jnp.where(gives, raw[None], 0.0), "dp")
     features = features.astype(jnp.bfloat16).reshape(-1, rank * rank)
 
     conditioned = dot(features, preconditioner, NT).astype(jnp.bfloat16)

time: 56.7 us -> 105 us (1.85)
  blocking collectives: 22 us -> 69.8 us
    psum x0 -> x1, blocking collectives: none -> 60.7 us  [local(): features = lax.psum(jnp.where(gives, raw[None], 0.0), 'dp')]
    all_to_all x2 -> x1, blocking collectives: 22 us -> 9.07 us  [to_all(): lax.all_to_all(copies, 'dp', 0, 0, axis_index_groups=groups, tiled=True)]
  transfers between devices with their start and end apart: 16 -> 16, of which waited for: 9 -> 9; matrix products, arithmetic and copies ran while one was open for 0% -> 0% of each run, Pallas kernels for 5% -> 3%
where the time goes in v22:
time: 105 us; the launch traced here: 104 us
  blocking collectives  69.8 us (66%)
  starting transfers between devices  16.1 us (15%)
  waiting for transfers between devices  10.4 us (10%)
  Pallas kernels  6.81 us (6%)
    psum x1, blocking collectives, local(): features = lax.psum(jnp.where(gives, raw[None], 0.0), 'dp')  60.7 us
    ppermute x14, starting transfers between devices, ring(): return lax.ppermute(x, 'dp', pairs)  15.4 us
    ppermute x14, waiting for transfers between devices, ring(): return lax.ppermute(x, 'dp', pairs)  9.17 us
    all_to_all x1, blocking collectives, to_all(): lax.all_to_all(copies, 'dp', 0, 0, axis_index_groups=groups, tiled=True)  9.07 us
    pallas_call x4, Pallas kernels, project(): pl.pallas_call(functools.partial(project_kernel, chips, items, a_width, c...  3.34 us
    pallas_call x1, Pallas kernels, start(): pl.pallas_call(functools.partial(start_kernel, chips), out_shape=[pltpu.V...  2.74 us
  transfers between devices with their start and end apart: 16, of which 9 were waited for; matrix products, arithmetic and copies ran while one was open for 0% of the time, Pallas kernels for 3%

profile of v22, /device:TPU:0, one launch (start us, length us, event | category | flops | bytes accessed | tf_op | source)
XLA Modules:
  0.0 104.4 jit_solution(3421754359281430608)
XLA Ops:
  0.0 2.7 %shard_map.64 = (bf16[64,1152]{1,0:T(8,128)(2,1)S(1)}, bf16[64,1152]{1,0:T(8,128)(2,1)S(1)}, bf16[8,128,2304]{2,1,0:T(8,128)(2,1)S(1)}) custom-call(bf16[128,8192]{1,0:T(8,128)(2,1)} %act.9, bf16[128,28672]{1,0:T(8,128)(2,1)} %grad.9, bf16[64,512]{1,0:T(8,128)(2,1)} %bitcast.10, bf16[64,1792]{1,0:T(8,128)(2,1)} %bitcast.9), custom_call_target="tpu_custom_call" | custom-call | bytes 10027008 | tf_op jit(solution)/shard_map/pallas_call | solution.py:90
  2.8 0.5 collective-permute-start
  3.3 2.7 %collective-permute-start.5 = (bf16[64,1152]{1,0:T(8,128)(2,1)S(1)}, bf16[64,1152]{1,0:T(8,128)(2,1)S(1)}, u32[]{:S(2)}, u32[]{:S(2)}) collective-permute-start(bf16[64,1152]{1,0:T(8,128)(2,1)S(1)} %get-tuple-element.10.refs_0_), channel_id=1, source_target_pairs={{0,5},{1,4},{4,9},{5,8},{8,13},{9,12},{12,15},{13,14},{14,11},{15,... | collective-permute-start | bytes 442376 | tf_op jit(solution)/shard_map/ppermute | solution.py:39
  6.0 1.7 %collective-permute-start.9 = (bf16[64,1152]{1,0:T(8,128)(2,1)S(1)}, bf16[64,1152]{1,0:T(8,128)(2,1)S(1)}, u32[]{:S(2)}, u32[]{:S(2)}) collective-permute-start(bf16[64,1152]{1,0:T(8,128)(2,1)S(1)} %get-tuple-element.9.refs_1_), channel_id=1, source_target_pairs={{0,5},{1,4},{4,9},{5,8},{8,13},{9,12},{12,15},{13,14},{14,11},{15,... | collective-permute-start | bytes 442376 | tf_op jit(solution)/shard_map/ppermute | solution.py:39
  7.7 2.4 %collective-permute-done.5.refs_2_ = bf16[64,1152]{1,0:T(8,128)(2,1)S(1)} collective-permute-done((bf16[64,1152]{1,0:T(8,128)(2,1)S(1)}, bf16[64,1152]{1,0:T(8,128)(2,1)S(1)}, u32[]{:S(2)}, u32[]{:S(2)}) %collective-permute-start.5) | collective-permute-done | bytes 147488 | tf_op jit(solution)/shard_map/ppermute | solution.py:39
  10.2 2.2 %collective-permute-start.6 = (bf16[64,1152]{1,0:T(8,128)(2,1)S(1)}, bf16[64,1152]{1,0:T(8,128)(2,1)S(1)}, u32[]{:S(2)}, u32[]{:S(2)}) collective-permute-start(bf16[64,1152]{1,0:T(8,128)(2,1)S(1)} %collective-permute-done.5.refs_2_), channel_id=1, source_target_pairs={{0,5},{1,4},{4,9},{5,8},{8,13},{9,12},{12,15},{13,14},{14,11},{15,... | collective-permute-start | bytes 442376 | tf_op jit(solution)/shard_map/ppermute | solution.py:39
  12.4 0.9 collective-permute-done.9.refs_3_
  13.2 2.2 %collective-permute-start.10 = (bf16[64,1152]{1,0:T(8,128)(2,1)S(1)}, bf16[64,1152]{1,0:T(8,128)(2,1)S(1)}, u32[]{:S(2)}, u32[]{:S(2)}) collective-permute-start(bf16[64,1152]{1,0:T(8,128)(2,1)S(1)} %collective-permute-done.9.refs_3_), channel_id=1, source_target_pairs={{0,5},{1,4},{4,9},{5,8},{8,13},{9,12},{12,15},{13,14},{14,11},{15,... | collective-permute-start | bytes 442376 | tf_op jit(solution)/shard_map/ppermute | solution.py:39
  15.4 1.1 %collective-permute-done.6.refs_6_ = bf16[64,1152]{1,0:T(8,128)(2,1)S(1)} collective-permute-done((bf16[64,1152]{1,0:T(8,128)(2,1)S(1)}, bf16[64,1152]{1,0:T(8,128)(2,1)S(1)}, u32[]{:S(2)}, u32[]{:S(2)}) %collective-permute-start.6) | collective-permute-done | bytes 147488 | tf_op jit(solution)/shard_map/ppermute | solution.py:39
  16.5 2.2 %collective-permute-start.7 = (bf16[64,1152]{1,0:T(8,128)(2,1)S(1)}, bf16[64,1152]{1,0:T(8,128)(2,1)S(1)}, u32[]{:S(2)}, u32[]{:S(2)}) collective-permute-start(bf16[64,1152]{1,0:T(8,128)(2,1)S(1)} %collective-permute-done.6.refs_6_), channel_id=1, source_target_pairs={{0,5},{1,4},{4,9},{5,8},{8,13},{9,12},{12,15},{13,14},{14,11},{15,... | collective-permute-start | bytes 442376 | tf_op jit(solution)/shard_map/ppermute | solution.py:39
  18.7 0.9 collective-permute-done.10.refs_7_
  19.6 2.2 %collective-permute-start.11 = (bf16[64,1152]{1,0:T(8,128)(2,1)S(1)}, bf16[64,1152]{1,0:T(8,128)(2,1)S(1)}, u32[]{:S(2)}, u32[]{:S(2)}) collective-permute-start(bf16[64,1152]{1,0:T(8,128)(2,1)S(1)} %collective-permute-done.10.refs_7_), channel_id=1, source_target_pairs={{0,5},{1,4},{4,9},{5,8},{8,13},{9,12},{12,15},{13,14},{14,11},{15,... | collective-permute-start | bytes 442376 | tf_op jit(solution)/shard_map/ppermute | solution.py:39
  21.8 1.0 collective-permute-done.7.refs_0_
  22.7 2.2 %collective-permute-start.8 = (bf16[64,1152]{1,0:T(8,128)(2,1)S(1)}, bf16[64,1152]{1,0:T(8,128)(2,1)S(1)}, u32[]{:S(2)}, u32[]{:S(2)}) collective-permute-start(bf16[64,1152]{1,0:T(8,128)(2,1)S(1)} %collective-permute-done.7.refs_0_), channel_id=1, source_target_pairs={{0,5},{1,4},{4,9},{5,8},{8,13},{9,12},{12,15},{13,14},{14,11},{15,... | collective-permute-start | bytes 442376 | tf_op jit(solution)/shard_map/ppermute | solution.py:39
  25.0 1.8 %shard_map.65.refs_4_ = f32[256,128]{1,0:T(8,128)S(1)} custom-call(bf16[128,8192]{1,0:T(8,128)(2,1)S(1)} %copy-done.2, bf16[128,28672]{1,0:T(8,128)(2,1)S(1)} %copy-done.1, bf16[8,128,2304]{2,1,0:T(8,128)(2,1)S(1)} %collective-permute-done.theirs, bf16[64,1152]{1,0:T(8,128)(2,1)S(1)} %get-tuple-element.10.refs_0_, ...), custom_call_target="tpu_custom_call" | custom-call | flops 377487360 | bytes 7372800 | tf_op jit(solution)/shard_map/pallas_call | solution.py:137
  26.7 1.1 %collective-permute-done.14.refs_2_ = bf16[64,1152]{1,0:T(8,128)(2,1)S(1)} collective-permute-done((bf16[64,1152]{1,0:T(8,128)(2,1)S(1)}, bf16[64,1152]{1,0:T(8,128)(2,1)S(1)}, u32[]{:S(2)}, u32[]{:S(2)}) %collective-permute-start.14) | collective-permute-done | bytes 147488 | tf_op jit(solution)/shard_map/ppermute | solution.py:39
  27.9 0.8 shard_map.66.refs_1_
  28.8 0.4 shard_map.67.refs_1_
  29.2 1.7 %collective-permute-done.4.refs_0_ = bf16[64,1152]{1,0:T(8,128)(2,1)S(1)} collective-permute-done((bf16[64,1152]{1,0:T(8,128)(2,1)S(1)}, bf16[64,1152]{1,0:T(8,128)(2,1)S(1)}, u32[]{:S(2)}, u32[]{:S(2)}) %collective-permute-start.4) | collective-permute-done | bytes 147488 | tf_op jit(solution)/shard_map/ppermute | solution.py:39
  31.5 1.2 %collective-permute-done.15 = f32[256,128]{1,0:T(8,128)S(1)} collective-permute-done((f32[256,128]{1,0:T(8,128)S(1)}, f32[256,128]{1,0:T(8,128)S(1)}, u32[]{:S(2)}, u32[]{:S(2)}) %collective-permute-start.15) | collective-permute-done | bytes 131104 | tf_op jit(solution)/shard_map/ppermute | solution.py:43
  33.2 60.7 %psum.7 = bf16[2,32,128]{2,1,0:T(8,128)(2,1)S(1)} all-reduce(f32[2,32,128]{2,1,0:T(8,128)S(1)} %broadcast_select_fusion), channel_id=1, replica_groups=mesh['parts'=2,'dp'=16] {'dp'}, use_global_device_ids=true, to_apply=%region_0.1 | all-reduce | flops 8192 | bytes 49152 | tf_op jit(solution)/shard_map/psum | solution.py:209
  93.9 0.6 convolution_convert_fusion
  94.6 9.1 %all_to_all.5.conditioned = bf16[16,2,256]{2,1,0:T(2,128)(2,1)S(1)} all-to-all(bf16[16,2,256]{2,1,0:T(2,128)(2,1)S(1)} %broadcast_in_dim.32), channel_id=1, replica_groups={{0,1,2,3,4,5,6,7,8,9,10,11,12,13,14,15},{16,17,18,19,20,21,22,23,24,25,..., dimensions={0} | all-to-all | bytes 32768 | tf_op jit(solution)/shard_map/all_to_all | solution.py:171
  103.6 0.7 shard_map.69
  (32 shorter events, 1.2 us)
Async XLA Ops:
  0.0 93.9 %copy-start = (bf16[256,4096]{1,0:T(8,128)(2,1)S(1)}, bf16[256,4096]{1,0:T(8,128)(2,1)}, u32[]{:S(2)}) copy-start(bf16[256,4096]{1,0:T(8,128)(2,1)} %param.10) | copy-start | bytes 6291460
  0.0 24.9 %copy-start.1 = (bf16[128,28672]{1,0:T(8,128)(2,1)S(1)}, bf16[128,28672]{1,0:T(8,128)(2,1)}, u32[]{:S(2)}) copy-start(bf16[128,28672]{1,0:T(8,128)(2,1)} %grad.9) | copy-start | bytes 22020100
  0.0 24.9 %copy-start.2 = (bf16[128,8192]{1,0:T(8,128)(2,1)S(1)}, bf16[128,8192]{1,0:T(8,128)(2,1)}, u32[]{:S(2)}) copy-start(bf16[128,8192]{1,0:T(8,128)(2,1)} %act.9) | copy-start | bytes 6291460
  2.8 22.2 %collective-permute-start = (bf16[8,128,2304]{2,1,0:T(8,128)(2,1)S(1)}, bf16[8,128,2304]{2,1,0:T(8,128)(2,1)S(1)}, u32[]{:S(2)}, u32[]{:S(2)}) collective-permute-start(bf16[8,128,2304]{2,1,0:T(8,128)(2,1)S(1)} %get-tuple-element.8), channel_id=1, source_target_pairs={{0,1},{1,0},{2,3},{3,2},{4,5},{5,4},{6,7},{7,6},{8,9},{9,8},{10,11... | collective-permute-start | bytes 14155784 | tf_op jit(solution)/shard_map/ppermute | solution.py:43
  3.3 6.9 %collective-permute-start.5 = (bf16[64,1152]{1,0:T(8,128)(2,1)S(1)}, bf16[64,1152]{1,0:T(8,128)(2,1)S(1)}, u32[]{:S(2)}, u32[]{:S(2)}) collective-permute-start(bf16[64,1152]{1,0:T(8,128)(2,1)S(1)} %get-tuple-element.10.refs_0_), channel_id=1, source_target_pairs={{0,5},{1,4},{4,9},{5,8},{8,13},{9,12},{12,15},{13,14},{14,11},{15,... | collective-permute-start | bytes 442376 | tf_op jit(solution)/shard_map/ppermute | solution.py:39
  6.0 6.4 %collective-permute-start.1 = (bf16[64,1152]{1,0:T(8,128)(2,1)S(1)}, bf16[64,1152]{1,0:T(8,128)(2,1)S(1)}, u32[]{:S(2)}, u32[]{:S(2)}) collective-permute-start(bf16[64,1152]{1,0:T(8,128)(2,1)S(1)} %get-tuple-element.9.refs_1_), channel_id=1, source_target_pairs={{0,3},{1,2},{4,1},{5,0},{8,5},{9,4},{12,9},{13,8},{14,13},{15,12},... | collective-permute-start | bytes 442376 | tf_op jit(solution)/shard_map/ppermute | solution.py:39
  6.0 7.3 %collective-permute-start.9 = (bf16[64,1152]{1,0:T(8,128)(2,1)S(1)}, bf16[64,1152]{1,0:T(8,128)(2,1)S(1)}, u32[]{:S(2)}, u32[]{:S(2)}) collective-permute-start(bf16[64,1152]{1,0:T(8,128)(2,1)S(1)} %get-tuple-element.9.refs_1_), channel_id=1, source_target_pairs={{0,5},{1,4},{4,9},{5,8},{8,13},{9,12},{12,15},{13,14},{14,11},{15,... | collective-permute-start | bytes 442376 | tf_op jit(solution)/shard_map/ppermute | solution.py:39
  7.7 7.7 %collective-permute-start.12 = (bf16[64,1152]{1,0:T(8,128)(2,1)S(1)}, bf16[64,1152]{1,0:T(8,128)(2,1)S(1)}, u32[]{:S(2)}, u32[]{:S(2)}) collective-permute-start(bf16[64,1152]{1,0:T(8,128)(2,1)S(1)} %get-tuple-element.10.refs_0_), channel_id=1, source_target_pairs={{0,3},{1,2},{4,1},{5,0},{8,5},{9,4},{12,9},{13,8},{14,13},{15,12},... | collective-permute-start | bytes 442376 | tf_op jit(solution)/shard_map/ppermute | solution.py:39
  10.2 6.3 %collective-permute-start.6 = (bf16[64,1152]{1,0:T(8,128)(2,1)S(1)}, bf16[64,1152]{1,0:T(8,128)(2,1)S(1)}, u32[]{:S(2)}, u32[]{:S(2)}) collective-permute-start(bf16[64,1152]{1,0:T(8,128)(2,1)S(1)} %collective-permute-done.5.refs_2_), channel_id=1, source_target_pairs={{0,5},{1,4},{4,9},{5,8},{8,13},{9,12},{12,15},{13,14},{14,11},{15,... | collective-permute-start | bytes 442376 | tf_op jit(solution)/shard_map/ppermute | solution.py:39
  12.4 6.3 %collective-permute-start.2 = (bf16[64,1152]{1,0:T(8,128)(2,1)S(1)}, bf16[64,1152]{1,0:T(8,128)(2,1)S(1)}, u32[]{:S(2)}, u32[]{:S(2)}) collective-permute-start(bf16[64,1152]{1,0:T(8,128)(2,1)S(1)} %collective-permute-done.1.refs_5_), channel_id=1, source_target_pairs={{0,3},{1,2},{4,1},{5,0},{8,5},{9,4},{12,9},{13,8},{14,13},{15,12},... | collective-permute-start | bytes 442376 | tf_op jit(solution)/shard_map/ppermute | solution.py:39
  13.2 6.3 %collective-permute-start.10 = (bf16[64,1152]{1,0:T(8,128)(2,1)S(1)}, bf16[64,1152]{1,0:T(8,128)(2,1)S(1)}, u32[]{:S(2)}, u32[]{:S(2)}) collective-permute-start(bf16[64,1152]{1,0:T(8,128)(2,1)S(1)} %collective-permute-done.9.refs_3_), channel_id=1, source_target_pairs={{0,5},{1,4},{4,9},{5,8},{8,13},{9,12},{12,15},{13,14},{14,11},{15,... | collective-permute-start | bytes 442376 | tf_op jit(solution)/shard_map/ppermute | solution.py:39
  15.4 6.4 %collective-permute-start.13 = (bf16[64,1152]{1,0:T(8,128)(2,1)S(1)}, bf16[64,1152]{1,0:T(8,128)(2,1)S(1)}, u32[]{:S(2)}, u32[]{:S(2)}) collective-permute-start(bf16[64,1152]{1,0:T(8,128)(2,1)S(1)} %collective-permute-done.12.refs_4_), channel_id=1, source_target_pairs={{0,3},{1,2},{4,1},{5,0},{8,5},{9,4},{12,9},{13,8},{14,13},{15,12},... | collective-permute-start | bytes 442376 | tf_op jit(solution)/shard_map/ppermute | solution.py:39
  16.5 6.3 %collective-permute-start.7 = (bf16[64,1152]{1,0:T(8,128)(2,1)S(1)}, bf16[64,1152]{1,0:T(8,128)(2,1)S(1)}, u32[]{:S(2)}, u32[]{:S(2)}) collective-permute-start(bf16[64,1152]{1,0:T(8,128)(2,1)S(1)} %collective-permute-done.6.refs_6_), channel_id=1, source_target_pairs={{0,5},{1,4},{4,9},{5,8},{8,13},{9,12},{12,15},{13,14},{14,11},{15,... | collective-permute-start | bytes 442376 | tf_op jit(solution)/shard_map/ppermute | solution.py:39
  18.7 6.3 %collective-permute-start.3 = (bf16[64,1152]{1,0:T(8,128)(2,1)S(1)}, bf16[64,1152]{1,0:T(8,128)(2,1)S(1)}, u32[]{:S(2)}, u32[]{:S(2)}) collective-permute-start(bf16[64,1152]{1,0:T(8,128)(2,1)S(1)} %collective-permute-done.2.refs_9_), channel_id=1, source_target_pairs={{0,3},{1,2},{4,1},{5,0},{8,5},{9,4},{12,9},{13,8},{14,13},{15,12},... | collective-permute-start | bytes 442376 | tf_op jit(solution)/shard_map/ppermute | solution.py:39
  19.6 7.2 %collective-permute-start.11 = (bf16[64,1152]{1,0:T(8,128)(2,1)S(1)}, bf16[64,1152]{1,0:T(8,128)(2,1)S(1)}, u32[]{:S(2)}, u32[]{:S(2)}) collective-permute-start(bf16[64,1152]{1,0:T(8,128)(2,1)S(1)} %collective-permute-done.10.refs_7_), channel_id=1, source_target_pairs={{0,5},{1,4},{4,9},{5,8},{8,13},{9,12},{12,15},{13,14},{14,11},{15,... | collective-permute-start | bytes 442376 | tf_op jit(solution)/shard_map/ppermute | solution.py:39
  21.8 6.1 %collective-permute-start.14 = (bf16[64,1152]{1,0:T(8,128)(2,1)S(1)}, bf16[64,1152]{1,0:T(8,128)(2,1)S(1)}, u32[]{:S(2)}, u32[]{:S(2)}) collective-permute-start(bf16[64,1152]{1,0:T(8,128)(2,1)S(1)} %collective-permute-done.13.refs_8_), channel_id=1, source_target_pairs={{0,3},{1,2},{4,1},{5,0},{8,5},{9,4},{12,9},{13,8},{14,13},{15,12},... | collective-permute-start | bytes 442376 | tf_op jit(solution)/shard_map/ppermute | solution.py:39
  22.7 6.1 %collective-permute-start.8 = (bf16[64,1152]{1,0:T(8,128)(2,1)S(1)}, bf16[64,1152]{1,0:T(8,128)(2,1)S(1)}, u32[]{:S(2)}, u32[]{:S(2)}) collective-permute-start(bf16[64,1152]{1,0:T(8,128)(2,1)S(1)} %collective-permute-done.7.refs_0_), channel_id=1, source_target_pairs={{0,5},{1,4},{4,9},{5,8},{8,13},{9,12},{12,15},{13,14},{14,11},{15,... | collective-permute-start | bytes 442376 | tf_op jit(solution)/shard_map/ppermute | solution.py:39
  24.9 6.0 %collective-permute-start.4 = (bf16[64,1152]{1,0:T(8,128)(2,1)S(1)}, bf16[64,1152]{1,0:T(8,128)(2,1)S(1)}, u32[]{:S(2)}, u32[]{:S(2)}) collective-permute-start(bf16[64,1152]{1,0:T(8,128)(2,1)S(1)} %collective-permute-done.3.refs_3_), channel_id=1, source_target_pairs={{0,3},{1,2},{4,1},{5,0},{8,5},{9,4},{12,9},{13,8},{14,13},{15,12},... | collective-permute-start | bytes 442376 | tf_op jit(solution)/shard_map/ppermute | solution.py:39
  31.3 72.3 %copy-start.3 = (bf16[8,4096]{1,0:T(8,128)(2,1)S(1)}, bf16[8,4096]{1,0:T(8,128)(2,1)}, u32[]{:S(2)}) copy-start(bf16[8,4096]{1,0:T(8,128)(2,1)} %queries.1) | copy-start | bytes 196612
  31.3 1.4 %collective-permute-start.15 = (f32[256,128]{1,0:T(8,128)S(1)}, f32[256,128]{1,0:T(8,128)S(1)}, u32[]{:S(2)}, u32[]{:S(2)}) collective-permute-start(f32[256,128]{1,0:T(8,128)S(1)} %shard_map.68), channel_id=1, source_target_pairs={{0,1},{1,0},{2,3},{3,2},{4,5},{5,4},{6,7},{7,6},{8,9},{9,8},{10,11... | collective-permute-start | bytes 393224 | tf_op jit(solution)/shard_map/ppermute | solution.py:43

commit v23 on v17

--- a/solution.py
+++ b/solution.py
@@ -202,9 +202,9 @@
     total = (total + jnp.concatenate([theirs[rows:], theirs[:rows]], axis=0)).astype(jnp.bfloat16)
 
     raw = dot(total[:, rank:], total[:, :rank], TN)
-    raw = (raw * (1.0 / math.sqrt(LEN))).reshape(-1, 128)
+    raw = (raw * (1.0 / math.sqrt(LEN))).astype(jnp.bfloat16).reshape(-1, 128)
     planes = [[2 * i + c for i in range(chips)] for c in range(2)]
-    raw = to_all(raw, planes)
+    raw = to_all(raw, planes).astype(jnp.float32)
     features = raw.reshape((-1, split // 2) + raw.shape[1:]).sum(axis=1)
     features = features.astype(jnp.bfloat16).reshape(-1, rank * rank)
 

time: 56.2 us -> 55.8 us (level)
  no operation moved by 1% of the time
where the time goes in v23:
time: 55.8 us; the launch traced here: 55.6 us
  blocking collectives  21 us (38%)
  starting transfers between devices  16.1 us (29%)
  waiting for transfers between devices  10.4 us (19%)
  Pallas kernels  6.81 us (12%)
  matrix products  0.89 us (2%)
    all_to_all x2, blocking collectives, to_all(): lax.all_to_all(copies, 'dp', 0, 0, axis_index_groups=groups, tiled=True)  21 us
    ppermute x14, starting transfers between devices, ring(): return lax.ppermute(x, 'dp', pairs)  15.4 us
    ppermute x14, waiting for transfers between devices, ring(): return lax.ppermute(x, 'dp', pairs)  9.17 us
    pallas_call x4, Pallas kernels, project(): pl.pallas_call(functools.partial(project_kernel, chips, items, a_width, c...  3.34 us
    pallas_call x1, Pallas kernels, start(): pl.pallas_call(functools.partial(start_kernel, chips), out_shape=[pltpu.V...  2.74 us
    ppermute x2, waiting for transfers between devices, swap(): return lax.ppermute(x, 'dp', [(i, i ^ bit) for i in range(n)])  1.24 us
  transfers between devices with their start and end apart: 16, of which 9 were waited for; matrix products, arithmetic and copies ran while one was open for 0% of the time, Pallas kernels for 5%

profile of v23, /device:TPU:0, one launch (start us, length us, event | category | flops | bytes accessed | tf_op | source)
XLA Modules:
  0.0 55.6 jit_solution(1120957669409582677)
XLA Ops:
  0.0 2.7 %shard_map.64 = (bf16[64,1152]{1,0:T(8,128)(2,1)S(1)}, bf16[64,1152]{1,0:T(8,128)(2,1)S(1)}, bf16[8,128,2304]{2,1,0:T(8,128)(2,1)S(1)}) custom-call(bf16[128,8192]{1,0:T(8,128)(2,1)} %act.9, bf16[128,28672]{1,0:T(8,128)(2,1)} %grad.9, bf16[64,512]{1,0:T(8,128)(2,1)} %bitcast.10, bf16[64,1792]{1,0:T(8,128)(2,1)} %bitcast.9), custom_call_target="tpu_custom_call" | custom-call | bytes 10027008 | tf_op jit(solution)/shard_map/pallas_call | solution.py:90
  2.8 0.5 collective-permute-start
  3.3 2.7 %collective-permute-start.5 = (bf16[64,1152]{1,0:T(8,128)(2,1)S(1)}, bf16[64,1152]{1,0:T(8,128)(2,1)S(1)}, u32[]{:S(2)}, u32[]{:S(2)}) collective-permute-start(bf16[64,1152]{1,0:T(8,128)(2,1)S(1)} %get-tuple-element.10.refs_0_), channel_id=1, source_target_pairs={{0,5},{1,4},{4,9},{5,8},{8,13},{9,12},{12,15},{13,14},{14,11},{15,... | collective-permute-start | bytes 442376 | tf_op jit(solution)/shard_map/ppermute | solution.py:39
  6.0 1.7 %collective-permute-start.9 = (bf16[64,1152]{1,0:T(8,128)(2,1)S(1)}, bf16[64,1152]{1,0:T(8,128)(2,1)S(1)}, u32[]{:S(2)}, u32[]{:S(2)}) collective-permute-start(bf16[64,1152]{1,0:T(8,128)(2,1)S(1)} %get-tuple-element.9.refs_1_), channel_id=1, source_target_pairs={{0,5},{1,4},{4,9},{5,8},{8,13},{9,12},{12,15},{13,14},{14,11},{15,... | collective-permute-start | bytes 442376 | tf_op jit(solution)/shard_map/ppermute | solution.py:39
  7.7 2.4 %collective-permute-done.5.refs_2_ = bf16[64,1152]{1,0:T(8,128)(2,1)S(1)} collective-permute-done((bf16[64,1152]{1,0:T(8,128)(2,1)S(1)}, bf16[64,1152]{1,0:T(8,128)(2,1)S(1)}, u32[]{:S(2)}, u32[]{:S(2)}) %collective-permute-start.5) | collective-permute-done | bytes 147488 | tf_op jit(solution)/shard_map/ppermute | solution.py:39
  10.2 2.2 %collective-permute-start.6 = (bf16[64,1152]{1,0:T(8,128)(2,1)S(1)}, bf16[64,1152]{1,0:T(8,128)(2,1)S(1)}, u32[]{:S(2)}, u32[]{:S(2)}) collective-permute-start(bf16[64,1152]{1,0:T(8,128)(2,1)S(1)} %collective-permute-done.5.refs_2_), channel_id=1, source_target_pairs={{0,5},{1,4},{4,9},{5,8},{8,13},{9,12},{12,15},{13,14},{14,11},{15,... | collective-permute-start | bytes 442376 | tf_op jit(solution)/shard_map/ppermute | solution.py:39
  12.4 0.9 %collective-permute-done.9.refs_3_ = bf16[64,1152]{1,0:T(8,128)(2,1)S(1)} collective-permute-done((bf16[64,1152]{1,0:T(8,128)(2,1)S(1)}, bf16[64,1152]{1,0:T(8,128)(2,1)S(1)}, u32[]{:S(2)}, u32[]{:S(2)}) %collective-permute-start.9) | collective-permute-done | bytes 147488 | tf_op jit(solution)/shard_map/ppermute | solution.py:39
  13.2 2.2 %collective-permute-start.10 = (bf16[64,1152]{1,0:T(8,128)(2,1)S(1)}, bf16[64,1152]{1,0:T(8,128)(2,1)S(1)}, u32[]{:S(2)}, u32[]{:S(2)}) collective-permute-start(bf16[64,1152]{1,0:T(8,128)(2,1)S(1)} %collective-permute-done.9.refs_3_), channel_id=1, source_target_pairs={{0,5},{1,4},{4,9},{5,8},{8,13},{9,12},{12,15},{13,14},{14,11},{15,... | collective-permute-start | bytes 442376 | tf_op jit(solution)/shard_map/ppermute | solution.py:39
  15.4 1.1 %collective-permute-done.6.refs_6_ = bf16[64,1152]{1,0:T(8,128)(2,1)S(1)} collective-permute-done((bf16[64,1152]{1,0:T(8,128)(2,1)S(1)}, bf16[64,1152]{1,0:T(8,128)(2,1)S(1)}, u32[]{:S(2)}, u32[]{:S(2)}) %collective-permute-start.6) | collective-permute-done | bytes 147488 | tf_op jit(solution)/shard_map/ppermute | solution.py:39
  16.5 2.2 %collective-permute-start.7 = (bf16[64,1152]{1,0:T(8,128)(2,1)S(1)}, bf16[64,1152]{1,0:T(8,128)(2,1)S(1)}, u32[]{:S(2)}, u32[]{:S(2)}) collective-permute-start(bf16[64,1152]{1,0:T(8,128)(2,1)S(1)} %collective-permute-done.6.refs_6_), channel_id=1, source_target_pairs={{0,5},{1,4},{4,9},{5,8},{8,13},{9,12},{12,15},{13,14},{14,11},{15,... | collective-permute-start | bytes 442376 | tf_op jit(solution)/shard_map/ppermute | solution.py:39
  18.7 0.9 %collective-permute-done.10.refs_7_ = bf16[64,1152]{1,0:T(8,128)(2,1)S(1)} collective-permute-done((bf16[64,1152]{1,0:T(8,128)(2,1)S(1)}, bf16[64,1152]{1,0:T(8,128)(2,1)S(1)}, u32[]{:S(2)}, u32[]{:S(2)}) %collective-permute-start.10) | collective-permute-done | bytes 147488 | tf_op jit(solution)/shard_map/ppermute | solution.py:39
  19.6 2.2 %collective-permute-start.11 = (bf16[64,1152]{1,0:T(8,128)(2,1)S(1)}, bf16[64,1152]{1,0:T(8,128)(2,1)S(1)}, u32[]{:S(2)}, u32[]{:S(2)}) collective-permute-start(bf16[64,1152]{1,0:T(8,128)(2,1)S(1)} %collective-permute-done.10.refs_7_), channel_id=1, source_target_pairs={{0,5},{1,4},{4,9},{5,8},{8,13},{9,12},{12,15},{13,14},{14,11},{15,... | collective-permute-start | bytes 442376 | tf_op jit(solution)/shard_map/ppermute | solution.py:39
  21.8 1.0 %collective-permute-done.7.refs_0_ = bf16[64,1152]{1,0:T(8,128)(2,1)S(1)} collective-permute-done((bf16[64,1152]{1,0:T(8,128)(2,1)S(1)}, bf16[64,1152]{1,0:T(8,128)(2,1)S(1)}, u32[]{:S(2)}, u32[]{:S(2)}) %collective-permute-start.7) | collective-permute-done | bytes 147488 | tf_op jit(solution)/shard_map/ppermute | solution.py:39
  22.7 2.2 %collective-permute-start.8 = (bf16[64,1152]{1,0:T(8,128)(2,1)S(1)}, bf16[64,1152]{1,0:T(8,128)(2,1)S(1)}, u32[]{:S(2)}, u32[]{:S(2)}) collective-permute-start(bf16[64,1152]{1,0:T(8,128)(2,1)S(1)} %collective-permute-done.7.refs_0_), channel_id=1, source_target_pairs={{0,5},{1,4},{4,9},{5,8},{8,13},{9,12},{12,15},{13,14},{14,11},{15,... | collective-permute-start | bytes 442376 | tf_op jit(solution)/shard_map/ppermute | solution.py:39
  25.0 1.8 %shard_map.65.refs_4_ = f32[256,128]{1,0:T(8,128)S(1)} custom-call(bf16[128,8192]{1,0:T(8,128)(2,1)S(1)} %copy-done.2, bf16[128,28672]{1,0:T(8,128)(2,1)S(1)} %copy-done.1, bf16[8,128,2304]{2,1,0:T(8,128)(2,1)S(1)} %collective-permute-done.theirs, bf16[64,1152]{1,0:T(8,128)(2,1)S(1)} %get-tuple-element.10.refs_0_, ...), custom_call_target="tpu_custom_call" | custom-call | flops 377487360 | bytes 7372800 | tf_op jit(solution)/shard_map/pallas_call | solution.py:137
  26.7 1.1 %collective-permute-done.14.refs_2_ = bf16[64,1152]{1,0:T(8,128)(2,1)S(1)} collective-permute-done((bf16[64,1152]{1,0:T(8,128)(2,1)S(1)}, bf16[64,1152]{1,0:T(8,128)(2,1)S(1)}, u32[]{:S(2)}, u32[]{:S(2)}) %collective-permute-start.14) | collective-permute-done | bytes 147488 | tf_op jit(solution)/shard_map/ppermute | solution.py:39
  27.9 0.8 %shard_map.66.refs_1_ = f32[256,128]{1,0:T(8,128)S(1)} custom-call(bf16[128,8192]{1,0:T(8,128)(2,1)S(1)} %copy-done.2, bf16[128,28672]{1,0:T(8,128)(2,1)S(1)} %copy-done.1, bf16[8,128,2304]{2,1,0:T(8,128)(2,1)S(1)} %collective-permute-done.theirs, bf16[64,1152]{1,0:T(8,128)(2,1)S(1)} %collective-permute-done.7.refs_0_, ...), custom_call_target="tpu_custom_call" | custom-call | flops 150994944 | bytes 2949120 | tf_op jit(solution)/shard_map/pallas_call | solution.py:137
  28.8 0.4 shard_map.67.refs_1_
  29.2 1.7 %collective-permute-done.4.refs_0_ = bf16[64,1152]{1,0:T(8,128)(2,1)S(1)} collective-permute-done((bf16[64,1152]{1,0:T(8,128)(2,1)S(1)}, bf16[64,1152]{1,0:T(8,128)(2,1)S(1)}, u32[]{:S(2)}, u32[]{:S(2)}) %collective-permute-start.4) | collective-permute-done | bytes 147488 | tf_op jit(solution)/shard_map/ppermute | solution.py:39
  31.5 1.2 %collective-permute-done.15 = f32[256,128]{1,0:T(8,128)S(1)} collective-permute-done((f32[256,128]{1,0:T(8,128)S(1)}, f32[256,128]{1,0:T(8,128)S(1)}, u32[]{:S(2)}, u32[]{:S(2)}) %collective-permute-start.15) | collective-permute-done | bytes 131104 | tf_op jit(solution)/shard_map/ppermute | solution.py:43
  33.1 12.0 %all_to_all.10 = bf16[8,32,128]{2,1,0:T(8,128)(2,1)S(1)} all-to-all(bf16[8,32,128]{2,1,0:T(8,128)(2,1)S(1)} %broadcast_in_dim.14), channel_id=1, replica_groups={{0,2,4,6,8,10,12,14},{1,3,5,7,9,11,13,15},{16,18,20,22,24,26,28,30},{17..., dimensions={0} | all-to-all | bytes 131072 | tf_op jit(solution)/shard_map/all_to_all | solution.py:171
  45.1 0.6 %convolution_convert_fusion = bf16[2,256]{1,0:T(2,128)(2,1)S(1)} fusion(bf16[256,4096]{1,0:T(8,128)(2,1)S(1)} %copy-done, bf16[1,2,32,128]{3,2,1,0:T(8,128)(2,1)S(1)} %bitcast.11), kind=kOutput, calls=%fused_computation.2 | convolution fusion | flops 4194816 | bytes 2114560 | tf_op jit(solution)/shard_map/dot_general | solution.py:23
  45.8 9.1 %all_to_all.11.conditioned = bf16[16,2,256]{2,1,0:T(2,128)(2,1)S(1)} all-to-all(bf16[16,2,256]{2,1,0:T(2,128)(2,1)S(1)} %broadcast_in_dim.15), channel_id=1, replica_groups={{0,1,2,3,4,5,6,7,8,9,10,11,12,13,14,15},{16,17,18,19,20,21,22,23,24,25,..., dimensions={0} | all-to-all | bytes 32768 | tf_op jit(solution)/shard_map/all_to_all | solution.py:171
  54.9 0.7 %shard_map.69 = f32[2,8]{1,0:T(2,128)} custom-call(bf16[16,2,256]{2,1,0:T(2,128)(2,1)S(1)} %all_to_all.11.conditioned, bf16[8,4096]{1,0:T(8,128)(2,1)S(1)} %copy-done.3), custom_call_target="tpu_custom_call" | custom-call | tf_op jit(solution)/shard_map/pallas_call | solution.py:160
  (32 shorter events, 1.1 us)
Async XLA Ops:
  0.0 45.1 %copy-start = (bf16[256,4096]{1,0:T(8,128)(2,1)S(1)}, bf16[256,4096]{1,0:T(8,128)(2,1)}, u32[]{:S(2)}) copy-start(bf16[256,4096]{1,0:T(8,128)(2,1)} %param.10) | copy-start | bytes 6291460
  0.0 24.9 %copy-start.1 = (bf16[128,28672]{1,0:T(8,128)(2,1)S(1)}, bf16[128,28672]{1,0:T(8,128)(2,1)}, u32[]{:S(2)}) copy-start(bf16[128,28672]{1,0:T(8,128)(2,1)} %grad.9) | copy-start | bytes 22020100
  0.0 24.9 %copy-start.2 = (bf16[128,8192]{1,0:T(8,128)(2,1)S(1)}, bf16[128,8192]{1,0:T(8,128)(2,1)}, u32[]{:S(2)}) copy-start(bf16[128,8192]{1,0:T(8,128)(2,1)} %act.9) | copy-start | bytes 6291460
  2.8 22.2 %collective-permute-start = (bf16[8,128,2304]{2,1,0:T(8,128)(2,1)S(1)}, bf16[8,128,2304]{2,1,0:T(8,128)(2,1)S(1)}, u32[]{:S(2)}, u32[]{:S(2)}) collective-permute-start(bf16[8,128,2304]{2,1,0:T(8,128)(2,1)S(1)} %get-tuple-element.8), channel_id=1, source_target_pairs={{0,1},{1,0},{2,3},{3,2},{4,5},{5,4},{6,7},{7,6},{8,9},{9,8},{10,11... | collective-permute-start | bytes 14155784 | tf_op jit(solution)/shard_map/ppermute | solution.py:43
  3.3 6.9 %collective-permute-start.5 = (bf16[64,1152]{1,0:T(8,128)(2,1)S(1)}, bf16[64,1152]{1,0:T(8,128)(2,1)S(1)}, u32[]{:S(2)}, u32[]{:S(2)}) collective-permute-start(bf16[64,1152]{1,0:T(8,128)(2,1)S(1)} %get-tuple-element.10.refs_0_), channel_id=1, source_target_pairs={{0,5},{1,4},{4,9},{5,8},{8,13},{9,12},{12,15},{13,14},{14,11},{15,... | collective-permute-start | bytes 442376 | tf_op jit(solution)/shard_map/ppermute | solution.py:39
  6.0 6.4 %collective-permute-start.1 = (bf16[64,1152]{1,0:T(8,128)(2,1)S(1)}, bf16[64,1152]{1,0:T(8,128)(2,1)S(1)}, u32[]{:S(2)}, u32[]{:S(2)}) collective-permute-start(bf16[64,1152]{1,0:T(8,128)(2,1)S(1)} %get-tuple-element.9.refs_1_), channel_id=1, source_target_pairs={{0,3},{1,2},{4,1},{5,0},{8,5},{9,4},{12,9},{13,8},{14,13},{15,12},... | collective-permute-start | bytes 442376 | tf_op jit(solution)/shard_map/ppermute | solution.py:39
  6.0 7.3 %collective-permute-start.9 = (bf16[64,1152]{1,0:T(8,128)(2,1)S(1)}, bf16[64,1152]{1,0:T(8,128)(2,1)S(1)}, u32[]{:S(2)}, u32[]{:S(2)}) collective-permute-start(bf16[64,1152]{1,0:T(8,128)(2,1)S(1)} %get-tuple-element.9.refs_1_), channel_id=1, source_target_pairs={{0,5},{1,4},{4,9},{5,8},{8,13},{9,12},{12,15},{13,14},{14,11},{15,... | collective-permute-start | bytes 442376 | tf_op jit(solution)/shard_map/ppermute | solution.py:39
  7.7 7.7 %collective-permute-start.12 = (bf16[64,1152]{1,0:T(8,128)(2,1)S(1)}, bf16[64,1152]{1,0:T(8,128)(2,1)S(1)}, u32[]{:S(2)}, u32[]{:S(2)}) collective-permute-start(bf16[64,1152]{1,0:T(8,128)(2,1)S(1)} %get-tuple-element.10.refs_0_), channel_id=1, source_target_pairs={{0,3},{1,2},{4,1},{5,0},{8,5},{9,4},{12,9},{13,8},{14,13},{15,12},... | collective-permute-start | bytes 442376 | tf_op jit(solution)/shard_map/ppermute | solution.py:39
  10.2 6.3 %collective-permute-start.6 = (bf16[64,1152]{1,0:T(8,128)(2,1)S(1)}, bf16[64,1152]{1,0:T(8,128)(2,1)S(1)}, u32[]{:S(2)}, u32[]{:S(2)}) collective-permute-start(bf16[64,1152]{1,0:T(8,128)(2,1)S(1)} %collective-permute-done.5.refs_2_), channel_id=1, source_target_pairs={{0,5},{1,4},{4,9},{5,8},{8,13},{9,12},{12,15},{13,14},{14,11},{15,... | collective-permute-start | bytes 442376 | tf_op jit(solution)/shard_map/ppermute | solution.py:39
  12.4 6.3 %collective-permute-start.2 = (bf16[64,1152]{1,0:T(8,128)(2,1)S(1)}, bf16[64,1152]{1,0:T(8,128)(2,1)S(1)}, u32[]{:S(2)}, u32[]{:S(2)}) collective-permute-start(bf16[64,1152]{1,0:T(8,128)(2,1)S(1)} %collective-permute-done.1.refs_5_), channel_id=1, source_target_pairs={{0,3},{1,2},{4,1},{5,0},{8,5},{9,4},{12,9},{13,8},{14,13},{15,12},... | collective-permute-start | bytes 442376 | tf_op jit(solution)/shard_map/ppermute | solution.py:39
  13.2 6.3 %collective-permute-start.10 = (bf16[64,1152]{1,0:T(8,128)(2,1)S(1)}, bf16[64,1152]{1,0:T(8,128)(2,1)S(1)}, u32[]{:S(2)}, u32[]{:S(2)}) collective-permute-start(bf16[64,1152]{1,0:T(8,128)(2,1)S(1)} %collective-permute-done.9.refs_3_), channel_id=1, source_target_pairs={{0,5},{1,4},{4,9},{5,8},{8,13},{9,12},{12,15},{13,14},{14,11},{15,... | collective-permute-start | bytes 442376 | tf_op jit(solution)/shard_map/ppermute | solution.py:39
  15.4 6.4 %collective-permute-start.13 = (bf16[64,1152]{1,0:T(8,128)(2,1)S(1)}, bf16[64,1152]{1,0:T(8,128)(2,1)S(1)}, u32[]{:S(2)}, u32[]{:S(2)}) collective-permute-start(bf16[64,1152]{1,0:T(8,128)(2,1)S(1)} %collective-permute-done.12.refs_4_), channel_id=1, source_target_pairs={{0,3},{1,2},{4,1},{5,0},{8,5},{9,4},{12,9},{13,8},{14,13},{15,12},... | collective-permute-start | bytes 442376 | tf_op jit(solution)/shard_map/ppermute | solution.py:39
  16.5 6.3 %collective-permute-start.7 = (bf16[64,1152]{1,0:T(8,128)(2,1)S(1)}, bf16[64,1152]{1,0:T(8,128)(2,1)S(1)}, u32[]{:S(2)}, u32[]{:S(2)}) collective-permute-start(bf16[64,1152]{1,0:T(8,128)(2,1)S(1)} %collective-permute-done.6.refs_6_), channel_id=1, source_target_pairs={{0,5},{1,4},{4,9},{5,8},{8,13},{9,12},{12,15},{13,14},{14,11},{15,... | collective-permute-start | bytes 442376 | tf_op jit(solution)/shard_map/ppermute | solution.py:39
  18.7 6.3 %collective-permute-start.3 = (bf16[64,1152]{1,0:T(8,128)(2,1)S(1)}, bf16[64,1152]{1,0:T(8,128)(2,1)S(1)}, u32[]{:S(2)}, u32[]{:S(2)}) collective-permute-start(bf16[64,1152]{1,0:T(8,128)(2,1)S(1)} %collective-permute-done.2.refs_9_), channel_id=1, source_target_pairs={{0,3},{1,2},{4,1},{5,0},{8,5},{9,4},{12,9},{13,8},{14,13},{15,12},... | collective-permute-start | bytes 442376 | tf_op jit(solution)/shard_map/ppermute | solution.py:39
  19.6 7.2 %collective-permute-start.11 = (bf16[64,1152]{1,0:T(8,128)(2,1)S(1)}, bf16[64,1152]{1,0:T(8,128)(2,1)S(1)}, u32[]{:S(2)}, u32[]{:S(2)}) collective-permute-start(bf16[64,1152]{1,0:T(8,128)(2,1)S(1)} %collective-permute-done.10.refs_7_), channel_id=1, source_target_pairs={{0,5},{1,4},{4,9},{5,8},{8,13},{9,12},{12,15},{13,14},{14,11},{15,... | collective-permute-start | bytes 442376 | tf_op jit(solution)/shard_map/ppermute | solution.py:39
  21.8 6.1 %collective-permute-start.14 = (bf16[64,1152]{1,0:T(8,128)(2,1)S(1)}, bf16[64,1152]{1,0:T(8,128)(2,1)S(1)}, u32[]{:S(2)}, u32[]{:S(2)}) collective-permute-start(bf16[64,1152]{1,0:T(8,128)(2,1)S(1)} %collective-permute-done.13.refs_8_), channel_id=1, source_target_pairs={{0,3},{1,2},{4,1},{5,0},{8,5},{9,4},{12,9},{13,8},{14,13},{15,12},... | collective-permute-start | bytes 442376 | tf_op jit(solution)/shard_map/ppermute | solution.py:39
  22.7 6.1 %collective-permute-start.8 = (bf16[64,1152]{1,0:T(8,128)(2,1)S(1)}, bf16[64,1152]{1,0:T(8,128)(2,1)S(1)}, u32[]{:S(2)}, u32[]{:S(2)}) collective-permute-start(bf16[64,1152]{1,0:T(8,128)(2,1)S(1)} %collective-permute-done.7.refs_0_), channel_id=1, source_target_pairs={{0,5},{1,4},{4,9},{5,8},{8,13},{9,12},{12,15},{13,14},{14,11},{15,... | collective-permute-start | bytes 442376 | tf_op jit(solution)/shard_map/ppermute | solution.py:39
  24.9 6.0 %collective-permute-start.4 = (bf16[64,1152]{1,0:T(8,128)(2,1)S(1)}, bf16[64,1152]{1,0:T(8,128)(2,1)S(1)}, u32[]{:S(2)}, u32[]{:S(2)}) collective-permute-start(bf16[64,1152]{1,0:T(8,128)(2,1)S(1)} %collective-permute-done.3.refs_3_), channel_id=1, source_target_pairs={{0,3},{1,2},{4,1},{5,0},{8,5},{9,4},{12,9},{13,8},{14,13},{15,12},... | collective-permute-start | bytes 442376 | tf_op jit(solution)/shard_map/ppermute | solution.py:39
  31.3 23.6 %copy-start.3 = (bf16[8,4096]{1,0:T(8,128)(2,1)S(1)}, bf16[8,4096]{1,0:T(8,128)(2,1)}, u32[]{:S(2)}) copy-start(bf16[8,4096]{1,0:T(8,128)(2,1)} %queries.1) | copy-start | bytes 196612
  31.3 1.4 %collective-permute-start.15 = (f32[256,128]{1,0:T(8,128)S(1)}, f32[256,128]{1,0:T(8,128)S(1)}, u32[]{:S(2)}, u32[]{:S(2)}) collective-permute-start(f32[256,128]{1,0:T(8,128)S(1)} %shard_map.68), channel_id=1, source_target_pairs={{0,1},{1,0},{2,3},{3,2},{4,5},{5,4},{6,7},{7,6},{8,9},{9,8},{10,11... | collective-permute-start | bytes 393224 | tf_op jit(solution)/shard_map/ppermute | solution.py:43

commit v24 on v17

--- a/solution.py
+++ b/solution.py
@@ -85,7 +85,7 @@
 def start(act, grad, in_rows, out_rows, chips):
     rows = act.shape[0]
     rank, width = in_rows.shape[0], in_rows.shape[1] + out_rows.shape[1]
-    cut = width // 256 * 128
+    cut = (width // 256 + 1) * 128
     shapes = (rank, cut), (rank, width - cut), (chips, rows, width)
     return pl.pallas_call(
         functools.partial(start_kernel, chips),

time: 56.2 us -> 59.3 us (1.055)
  starting transfers between devices: 16.1 us -> 17.6 us
  waiting for transfers between devices: 10.4 us -> 11.9 us
    ppermute x14, waiting for transfers between devices: 9.17 us -> 10.9 us  [ring(): return lax.ppermute(x, 'dp', pairs)]
    ppermute x14, starting transfers between devices: 15.4 us -> 16.7 us  [ring(): return lax.ppermute(x, 'dp', pairs)]
where the time goes in v24:
time: 59.3 us; the launch traced here: 59.1 us
  blocking collectives  21.6 us (36%)
  starting transfers between devices  17.6 us (30%)
  waiting for transfers between devices  11.9 us (20%)
  Pallas kernels  6.8 us (11%)
  matrix products  0.89 us (2%)
    all_to_all x2, blocking collectives, to_all(): lax.all_to_all(copies, 'dp', 0, 0, axis_index_groups=groups, tiled=True)  21.6 us
    ppermute x14, starting transfers between devices, ring(): return lax.ppermute(x, 'dp', pairs)  16.7 us
    ppermute x14, waiting for transfers between devices, ring(): return lax.ppermute(x, 'dp', pairs)  10.9 us
    pallas_call x4, Pallas kernels, project(): pl.pallas_call(functools.partial(project_kernel, chips, items, a_width, c...  3.33 us
    pallas_call x1, Pallas kernels, start(): pl.pallas_call(functools.partial(start_kernel, chips), out_shape=[pltpu.V...  2.74 us
  transfers between devices with their start and end apart: 16, of which 9 were waited for; matrix products, arithmetic and copies ran while one was open for 0% of the time, Pallas kernels for 5%

profile of v24, /device:TPU:0, one launch (start us, length us, event | category | flops | bytes accessed | tf_op | source)
XLA Modules:
  0.0 59.1 jit_solution(784225966719490124)
XLA Ops:
  0.0 2.7 %shard_map.64 = (bf16[64,1280]{1,0:T(8,128)(2,1)S(1)}, bf16[64,1024]{1,0:T(8,128)(2,1)S(1)}, bf16[8,128,2304]{2,1,0:T(8,128)(2,1)S(1)}) custom-call(bf16[128,8192]{1,0:T(8,128)(2,1)} %act.9, bf16[128,28672]{1,0:T(8,128)(2,1)} %grad.9, bf16[64,512]{1,0:T(8,128)(2,1)} %bitcast.12, bf16[64,1792]{1,0:T(8,128)(2,1)} %bitcast.11), custom_call_target="tpu_custom_call" | custom-call | bytes 10027008 | tf_op jit(solution)/shard_map/pallas_call | solution.py:90
  3.3 2.7 %collective-permute-start.5 = (bf16[64,1280]{1,0:T(8,128)(2,1)S(1)}, bf16[64,1280]{1,0:T(8,128)(2,1)S(1)}, u32[]{:S(2)}, u32[]{:S(2)}) collective-permute-start(bf16[64,1280]{1,0:T(8,128)(2,1)S(1)} %get-tuple-element.10.refs_0_), channel_id=1, source_target_pairs={{0,5},{1,4},{4,9},{5,8},{8,13},{9,12},{12,15},{13,14},{14,11},{15,... | collective-permute-start | bytes 491528 | tf_op jit(solution)/shard_map/ppermute | solution.py:39
  6.0 1.7 %collective-permute-start.12 = (bf16[64,1280]{1,0:T(8,128)(2,1)S(1)}, bf16[64,1280]{1,0:T(8,128)(2,1)S(1)}, u32[]{:S(2)}, u32[]{:S(2)}) collective-permute-start(bf16[64,1280]{1,0:T(8,128)(2,1)S(1)} %get-tuple-element.10.refs_0_), channel_id=1, source_target_pairs={{0,3},{1,2},{4,1},{5,0},{8,5},{9,4},{12,9},{13,8},{14,13},{15,12},... | collective-permute-start | bytes 491528 | tf_op jit(solution)/shard_map/ppermute | solution.py:39
  7.7 2.8 %collective-permute-done.5.refs_2_ = bf16[64,1280]{1,0:T(8,128)(2,1)S(1)} collective-permute-done((bf16[64,1280]{1,0:T(8,128)(2,1)S(1)}, bf16[64,1280]{1,0:T(8,128)(2,1)S(1)}, u32[]{:S(2)}, u32[]{:S(2)}) %collective-permute-start.5) | collective-permute-done | bytes 163872 | tf_op jit(solution)/shard_map/ppermute | solution.py:39
  10.4 1.7 %collective-permute-start.6 = (bf16[64,1280]{1,0:T(8,128)(2,1)S(1)}, bf16[64,1280]{1,0:T(8,128)(2,1)S(1)}, u32[]{:S(2)}, u32[]{:S(2)}) collective-permute-start(bf16[64,1280]{1,0:T(8,128)(2,1)S(1)} %collective-permute-done.5.refs_2_), channel_id=1, source_target_pairs={{0,5},{1,4},{4,9},{5,8},{8,13},{9,12},{12,15},{13,14},{14,11},{15,... | collective-permute-start | bytes 491528 | tf_op jit(solution)/shard_map/ppermute | solution.py:39
  12.1 1.0 %collective-permute-start.9 = (bf16[64,1024]{1,0:T(8,128)(2,1)S(1)}, bf16[64,1024]{1,0:T(8,128)(2,1)S(1)}, u32[]{:S(2)}, u32[]{:S(2)}) collective-permute-start(bf16[64,1024]{1,0:T(8,128)(2,1)S(1)} %get-tuple-element.9.refs_1_), channel_id=1, source_target_pairs={{0,5},{1,4},{4,9},{5,8},{8,13},{9,12},{12,15},{13,14},{14,11},{15,... | collective-permute-start | bytes 393224 | tf_op jit(solution)/shard_map/ppermute | solution.py:39
  13.2 0.7 %collective-permute-start.2 = (bf16[64,1024]{1,0:T(8,128)(2,1)S(1)}, bf16[64,1024]{1,0:T(8,128)(2,1)S(1)}, u32[]{:S(2)}, u32[]{:S(2)}) collective-permute-start(bf16[64,1024]{1,0:T(8,128)(2,1)S(1)} %collective-permute-done.1.refs_5_), channel_id=1, source_target_pairs={{0,3},{1,2},{4,1},{5,0},{8,5},{9,4},{12,9},{13,8},{14,13},{15,12},... | collective-permute-start | bytes 393224 | tf_op jit(solution)/shard_map/ppermute | solution.py:39
  13.9 1.1 %collective-permute-done.12.refs_4_ = bf16[64,1280]{1,0:T(8,128)(2,1)S(1)} collective-permute-done((bf16[64,1280]{1,0:T(8,128)(2,1)S(1)}, bf16[64,1280]{1,0:T(8,128)(2,1)S(1)}, u32[]{:S(2)}, u32[]{:S(2)}) %collective-permute-start.12) | collective-permute-done | bytes 163872 | tf_op jit(solution)/shard_map/ppermute | solution.py:39
  15.0 1.7 %collective-permute-done.6.refs_6_ = bf16[64,1280]{1,0:T(8,128)(2,1)S(1)} collective-permute-done((bf16[64,1280]{1,0:T(8,128)(2,1)S(1)}, bf16[64,1280]{1,0:T(8,128)(2,1)S(1)}, u32[]{:S(2)}, u32[]{:S(2)}) %collective-permute-start.6) | collective-permute-done | bytes 163872 | tf_op jit(solution)/shard_map/ppermute | solution.py:39
  16.7 2.2 %collective-permute-start.7 = (bf16[64,1280]{1,0:T(8,128)(2,1)S(1)}, bf16[64,1280]{1,0:T(8,128)(2,1)S(1)}, u32[]{:S(2)}, u32[]{:S(2)}) collective-permute-start(bf16[64,1280]{1,0:T(8,128)(2,1)S(1)} %collective-permute-done.6.refs_6_), channel_id=1, source_target_pairs={{0,5},{1,4},{4,9},{5,8},{8,13},{9,12},{12,15},{13,14},{14,11},{15,... | collective-permute-start | bytes 491528 | tf_op jit(solution)/shard_map/ppermute | solution.py:39
  19.3 1.6 %collective-permute-start.10 = (bf16[64,1024]{1,0:T(8,128)(2,1)S(1)}, bf16[64,1024]{1,0:T(8,128)(2,1)S(1)}, u32[]{:S(2)}, u32[]{:S(2)}) collective-permute-start(bf16[64,1024]{1,0:T(8,128)(2,1)S(1)} %collective-permute-done.9.refs_3_), channel_id=1, source_target_pairs={{0,5},{1,4},{4,9},{5,8},{8,13},{9,12},{12,15},{13,14},{14,11},{15,... | collective-permute-start | bytes 393224 | tf_op jit(solution)/shard_map/ppermute | solution.py:39
  21.0 0.9 %collective-permute-done.13.refs_8_ = bf16[64,1280]{1,0:T(8,128)(2,1)S(1)} collective-permute-done((bf16[64,1280]{1,0:T(8,128)(2,1)S(1)}, bf16[64,1280]{1,0:T(8,128)(2,1)S(1)}, u32[]{:S(2)}, u32[]{:S(2)}) %collective-permute-start.13) | collective-permute-done | bytes 163872 | tf_op jit(solution)/shard_map/ppermute | solution.py:39
  21.9 0.9 %collective-permute-start.14 = (bf16[64,1280]{1,0:T(8,128)(2,1)S(1)}, bf16[64,1280]{1,0:T(8,128)(2,1)S(1)}, u32[]{:S(2)}, u32[]{:S(2)}) collective-permute-start(bf16[64,1280]{1,0:T(8,128)(2,1)S(1)} %collective-permute-done.13.refs_8_), channel_id=1, source_target_pairs={{0,3},{1,2},{4,1},{5,0},{8,5},{9,4},{12,9},{13,8},{14,13},{15,12},... | collective-permute-start | bytes 491528 | tf_op jit(solution)/shard_map/ppermute | solution.py:39
  22.8 0.8 %collective-permute-done.7.refs_0_ = bf16[64,1280]{1,0:T(8,128)(2,1)S(1)} collective-permute-done((bf16[64,1280]{1,0:T(8,128)(2,1)S(1)}, bf16[64,1280]{1,0:T(8,128)(2,1)S(1)}, u32[]{:S(2)}, u32[]{:S(2)}) %collective-permute-start.7) | collective-permute-done | bytes 163872 | tf_op jit(solution)/shard_map/ppermute | solution.py:39
  23.5 2.2 %collective-permute-start.8 = (bf16[64,1280]{1,0:T(8,128)(2,1)S(1)}, bf16[64,1280]{1,0:T(8,128)(2,1)S(1)}, u32[]{:S(2)}, u32[]{:S(2)}) collective-permute-start(bf16[64,1280]{1,0:T(8,128)(2,1)S(1)} %collective-permute-done.7.refs_0_), channel_id=1, source_target_pairs={{0,5},{1,4},{4,9},{5,8},{8,13},{9,12},{12,15},{13,14},{14,11},{15,... | collective-permute-start | bytes 491528 | tf_op jit(solution)/shard_map/ppermute | solution.py:39
  25.9 1.5 %collective-permute-start.11 = (bf16[64,1024]{1,0:T(8,128)(2,1)S(1)}, bf16[64,1024]{1,0:T(8,128)(2,1)S(1)}, u32[]{:S(2)}, u32[]{:S(2)}) collective-permute-start(bf16[64,1024]{1,0:T(8,128)(2,1)S(1)} %collective-permute-done.10.refs_7_), channel_id=1, source_target_pairs={{0,5},{1,4},{4,9},{5,8},{8,13},{9,12},{12,15},{13,14},{14,11},{15,... | collective-permute-start | bytes 393224 | tf_op jit(solution)/shard_map/ppermute | solution.py:39
  27.7 1.7 %shard_map.65.refs_4_ = f32[256,128]{1,0:T(8,128)S(1)} custom-call(bf16[128,8192]{1,0:T(8,128)(2,1)S(1)} %copy-done.2, bf16[128,28672]{1,0:T(8,128)(2,1)S(1)} %copy-done.1, bf16[8,128,2304]{2,1,0:T(8,128)(2,1)S(1)} %collective-permute-done.theirs, bf16[64,1280]{1,0:T(8,128)(2,1)S(1)} %get-tuple-element.10.refs_0_, ...), custom_call_target="tpu_custom_call" | custom-call | flops 377487360 | bytes 7372800 | tf_op jit(solution)/shard_map/pallas_call | solution.py:137
  29.5 3.2 %collective-permute-done.11.refs_1_ = bf16[64,1024]{1,0:T(8,128)(2,1)S(1)} collective-permute-done((bf16[64,1024]{1,0:T(8,128)(2,1)S(1)}, bf16[64,1024]{1,0:T(8,128)(2,1)S(1)}, u32[]{:S(2)}, u32[]{:S(2)}) %collective-permute-start.11) | collective-permute-done | bytes 131104 | tf_op jit(solution)/shard_map/ppermute | solution.py:39
  32.7 0.8 %shard_map.66.refs_1_ = f32[256,128]{1,0:T(8,128)S(1)} custom-call(bf16[128,8192]{1,0:T(8,128)(2,1)S(1)} %copy-done.2, bf16[128,28672]{1,0:T(8,128)(2,1)S(1)} %copy-done.1, bf16[8,128,2304]{2,1,0:T(8,128)(2,1)S(1)} %collective-permute-done.theirs, bf16[64,1280]{1,0:T(8,128)(2,1)S(1)} %collective-permute-done.7.refs_0_, ...), custom_call_target="tpu_custom_call" | custom-call | flops 150994944 | bytes 2949120 | tf_op jit(solution)/shard_map/pallas_call | solution.py:137
  34.7 1.0 %collective-permute-done.15 = f32[256,128]{1,0:T(8,128)S(1)} collective-permute-done((f32[256,128]{1,0:T(8,128)S(1)}, f32[256,128]{1,0:T(8,128)S(1)}, u32[]{:S(2)}, u32[]{:S(2)}) %collective-permute-start.15) | collective-permute-done | bytes 131104 | tf_op jit(solution)/shard_map/ppermute | solution.py:43
  36.1 12.5 %all_to_all.10 = f32[8,32,128]{2,1,0:T(8,128)S(1)} all-to-all(f32[8,32,128]{2,1,0:T(8,128)S(1)} %broadcast_in_dim.14), channel_id=1, replica_groups={{0,2,4,6,8,10,12,14},{1,3,5,7,9,11,13,15},{16,18,20,22,24,26,28,30},{17..., dimensions={0} | all-to-all | bytes 262144 | tf_op jit(solution)/shard_map/all_to_all | solution.py:171
  48.6 0.6 %convolution_convert_fusion = bf16[2,256]{1,0:T(2,128)(2,1)S(1)} fusion(bf16[256,4096]{1,0:T(8,128)(2,1)S(1)} %copy-done, bf16[1,2,32,128]{3,2,1,0:T(8,128)(2,1)S(1)} %bitcast.13), kind=kOutput, calls=%fused_computation.1 | convolution fusion | flops 4194816 | bytes 2114560 | tf_op jit(solution)/shard_map/dot_general | solution.py:23
  49.3 9.1 %all_to_all.11.conditioned = bf16[16,2,256]{2,1,0:T(2,128)(2,1)S(1)} all-to-all(bf16[16,2,256]{2,1,0:T(2,128)(2,1)S(1)} %broadcast_in_dim.15), channel_id=1, replica_groups={{0,1,2,3,4,5,6,7,8,9,10,11,12,13,14,15},{16,17,18,19,20,21,22,23,24,25,..., dimensions={0} | all-to-all | bytes 32768 | tf_op jit(solution)/shard_map/all_to_all | solution.py:171
  58.4 0.7 %shard_map.69 = f32[2,8]{1,0:T(2,128)} custom-call(bf16[16,2,256]{2,1,0:T(2,128)(2,1)S(1)} %all_to_all.11.conditioned, bf16[8,4096]{1,0:T(8,128)(2,1)S(1)} %copy-done.3), custom_call_target="tpu_custom_call" | custom-call | tf_op jit(solution)/shard_map/pallas_call | solution.py:160
  (32 shorter events, 3.1 us)
Async XLA Ops:
  0.0 48.6 %copy-start = (bf16[256,4096]{1,0:T(8,128)(2,1)S(1)}, bf16[256,4096]{1,0:T(8,128)(2,1)}, u32[]{:S(2)}) copy-start(bf16[256,4096]{1,0:T(8,128)(2,1)} %param.10) | copy-start | bytes 6291460
  0.0 27.7 %copy-start.1 = (bf16[128,28672]{1,0:T(8,128)(2,1)S(1)}, bf16[128,28672]{1,0:T(8,128)(2,1)}, u32[]{:S(2)}) copy-start(bf16[128,28672]{1,0:T(8,128)(2,1)} %grad.9) | copy-start | bytes 22020100
  0.0 27.7 %copy-start.2 = (bf16[128,8192]{1,0:T(8,128)(2,1)S(1)}, bf16[128,8192]{1,0:T(8,128)(2,1)}, u32[]{:S(2)}) copy-start(bf16[128,8192]{1,0:T(8,128)(2,1)} %act.9) | copy-start | bytes 6291460
  2.8 25.0 %collective-permute-start = (bf16[8,128,2304]{2,1,0:T(8,128)(2,1)S(1)}, bf16[8,128,2304]{2,1,0:T(8,128)(2,1)S(1)}, u32[]{:S(2)}, u32[]{:S(2)}) collective-permute-start(bf16[8,128,2304]{2,1,0:T(8,128)(2,1)S(1)} %get-tuple-element.8), channel_id=1, source_target_pairs={{0,1},{1,0},{2,3},{3,2},{4,5},{5,4},{6,7},{7,6},{8,9},{9,8},{10,11... | collective-permute-start | bytes 14155784 | tf_op jit(solution)/shard_map/ppermute | solution.py:43
  3.3 7.1 %collective-permute-start.5 = (bf16[64,1280]{1,0:T(8,128)(2,1)S(1)}, bf16[64,1280]{1,0:T(8,128)(2,1)S(1)}, u32[]{:S(2)}, u32[]{:S(2)}) collective-permute-start(bf16[64,1280]{1,0:T(8,128)(2,1)S(1)} %get-tuple-element.10.refs_0_), channel_id=1, source_target_pairs={{0,5},{1,4},{4,9},{5,8},{8,13},{9,12},{12,15},{13,14},{14,11},{15,... | collective-permute-start | bytes 491528 | tf_op jit(solution)/shard_map/ppermute | solution.py:39
  6.0 7.2 %collective-permute-start.1 = (bf16[64,1024]{1,0:T(8,128)(2,1)S(1)}, bf16[64,1024]{1,0:T(8,128)(2,1)S(1)}, u32[]{:S(2)}, u32[]{:S(2)}) collective-permute-start(bf16[64,1024]{1,0:T(8,128)(2,1)S(1)} %get-tuple-element.9.refs_1_), channel_id=1, source_target_pairs={{0,3},{1,2},{4,1},{5,0},{8,5},{9,4},{12,9},{13,8},{14,13},{15,12},... | collective-permute-start | bytes 393224 | tf_op jit(solution)/shard_map/ppermute | solution.py:39
  6.0 9.1 %collective-permute-start.12 = (bf16[64,1280]{1,0:T(8,128)(2,1)S(1)}, bf16[64,1280]{1,0:T(8,128)(2,1)S(1)}, u32[]{:S(2)}, u32[]{:S(2)}) collective-permute-start(bf16[64,1280]{1,0:T(8,128)(2,1)S(1)} %get-tuple-element.10.refs_0_), channel_id=1, source_target_pairs={{0,3},{1,2},{4,1},{5,0},{8,5},{9,4},{12,9},{13,8},{14,13},{15,12},... | collective-permute-start | bytes 491528 | tf_op jit(solution)/shard_map/ppermute | solution.py:39
  10.4 6.3 %collective-permute-start.6 = (bf16[64,1280]{1,0:T(8,128)(2,1)S(1)}, bf16[64,1280]{1,0:T(8,128)(2,1)S(1)}, u32[]{:S(2)}, u32[]{:S(2)}) collective-permute-start(bf16[64,1280]{1,0:T(8,128)(2,1)S(1)} %collective-permute-done.5.refs_2_), channel_id=1, source_target_pairs={{0,5},{1,4},{4,9},{5,8},{8,13},{9,12},{12,15},{13,14},{14,11},{15,... | collective-permute-start | bytes 491528 | tf_op jit(solution)/shard_map/ppermute | solution.py:39
  12.1 7.1 %collective-permute-start.9 = (bf16[64,1024]{1,0:T(8,128)(2,1)S(1)}, bf16[64,1024]{1,0:T(8,128)(2,1)S(1)}, u32[]{:S(2)}, u32[]{:S(2)}) collective-permute-start(bf16[64,1024]{1,0:T(8,128)(2,1)S(1)} %get-tuple-element.9.refs_1_), channel_id=1, source_target_pairs={{0,5},{1,4},{4,9},{5,8},{8,13},{9,12},{12,15},{13,14},{14,11},{15,... | collective-permute-start | bytes 393224 | tf_op jit(solution)/shard_map/ppermute | solution.py:39
  13.2 7.7 %collective-permute-start.2 = (bf16[64,1024]{1,0:T(8,128)(2,1)S(1)}, bf16[64,1024]{1,0:T(8,128)(2,1)S(1)}, u32[]{:S(2)}, u32[]{:S(2)}) collective-permute-start(bf16[64,1024]{1,0:T(8,128)(2,1)S(1)} %collective-permute-done.1.refs_5_), channel_id=1, source_target_pairs={{0,3},{1,2},{4,1},{5,0},{8,5},{9,4},{12,9},{13,8},{14,13},{15,12},... | collective-permute-start | bytes 393224 | tf_op jit(solution)/shard_map/ppermute | solution.py:39
  15.0 6.8 %collective-permute-start.13 = (bf16[64,1280]{1,0:T(8,128)(2,1)S(1)}, bf16[64,1280]{1,0:T(8,128)(2,1)S(1)}, u32[]{:S(2)}, u32[]{:S(2)}) collective-permute-start(bf16[64,1280]{1,0:T(8,128)(2,1)S(1)} %collective-permute-done.12.refs_4_), channel_id=1, source_target_pairs={{0,3},{1,2},{4,1},{5,0},{8,5},{9,4},{12,9},{13,8},{14,13},{15,12},... | collective-permute-start | bytes 491528 | tf_op jit(solution)/shard_map/ppermute | solution.py:39
  16.7 6.8 %collective-permute-start.7 = (bf16[64,1280]{1,0:T(8,128)(2,1)S(1)}, bf16[64,1280]{1,0:T(8,128)(2,1)S(1)}, u32[]{:S(2)}, u32[]{:S(2)}) collective-permute-start(bf16[64,1280]{1,0:T(8,128)(2,1)S(1)} %collective-permute-done.6.refs_6_), channel_id=1, source_target_pairs={{0,5},{1,4},{4,9},{5,8},{8,13},{9,12},{12,15},{13,14},{14,11},{15,... | collective-permute-start | bytes 491528 | tf_op jit(solution)/shard_map/ppermute | solution.py:39
  19.3 6.6 %collective-permute-start.10 = (bf16[64,1024]{1,0:T(8,128)(2,1)S(1)}, bf16[64,1024]{1,0:T(8,128)(2,1)S(1)}, u32[]{:S(2)}, u32[]{:S(2)}) collective-permute-start(bf16[64,1024]{1,0:T(8,128)(2,1)S(1)} %collective-permute-done.9.refs_3_), channel_id=1, source_target_pairs={{0,5},{1,4},{4,9},{5,8},{8,13},{9,12},{12,15},{13,14},{14,11},{15,... | collective-permute-start | bytes 393224 | tf_op jit(solution)/shard_map/ppermute | solution.py:39
  20.9 6.5 %collective-permute-start.3 = (bf16[64,1024]{1,0:T(8,128)(2,1)S(1)}, bf16[64,1024]{1,0:T(8,128)(2,1)S(1)}, u32[]{:S(2)}, u32[]{:S(2)}) collective-permute-start(bf16[64,1024]{1,0:T(8,128)(2,1)S(1)} %collective-permute-done.2.refs_9_), channel_id=1, source_target_pairs={{0,3},{1,2},{4,1},{5,0},{8,5},{9,4},{12,9},{13,8},{14,13},{15,12},... | collective-permute-start | bytes 393224 | tf_op jit(solution)/shard_map/ppermute | solution.py:39
  21.9 10.8 %collective-permute-start.14 = (bf16[64,1280]{1,0:T(8,128)(2,1)S(1)}, bf16[64,1280]{1,0:T(8,128)(2,1)S(1)}, u32[]{:S(2)}, u32[]{:S(2)}) collective-permute-start(bf16[64,1280]{1,0:T(8,128)(2,1)S(1)} %collective-permute-done.13.refs_8_), channel_id=1, source_target_pairs={{0,3},{1,2},{4,1},{5,0},{8,5},{9,4},{12,9},{13,8},{14,13},{15,12},... | collective-permute-start | bytes 491528 | tf_op jit(solution)/shard_map/ppermute | solution.py:39
  23.5 10.0 %collective-permute-start.8 = (bf16[64,1280]{1,0:T(8,128)(2,1)S(1)}, bf16[64,1280]{1,0:T(8,128)(2,1)S(1)}, u32[]{:S(2)}, u32[]{:S(2)}) collective-permute-start(bf16[64,1280]{1,0:T(8,128)(2,1)S(1)} %collective-permute-done.7.refs_0_), channel_id=1, source_target_pairs={{0,5},{1,4},{4,9},{5,8},{8,13},{9,12},{12,15},{13,14},{14,11},{15,... | collective-permute-start | bytes 491528 | tf_op jit(solution)/shard_map/ppermute | solution.py:39
  25.9 6.8 %collective-permute-start.11 = (bf16[64,1024]{1,0:T(8,128)(2,1)S(1)}, bf16[64,1024]{1,0:T(8,128)(2,1)S(1)}, u32[]{:S(2)}, u32[]{:S(2)}) collective-permute-start(bf16[64,1024]{1,0:T(8,128)(2,1)S(1)} %collective-permute-done.10.refs_7_), channel_id=1, source_target_pairs={{0,5},{1,4},{4,9},{5,8},{8,13},{9,12},{12,15},{13,14},{14,11},{15,... | collective-permute-start | bytes 393224 | tf_op jit(solution)/shard_map/ppermute | solution.py:39
  27.4 6.5 %collective-permute-start.4 = (bf16[64,1024]{1,0:T(8,128)(2,1)S(1)}, bf16[64,1024]{1,0:T(8,128)(2,1)S(1)}, u32[]{:S(2)}, u32[]{:S(2)}) collective-permute-start(bf16[64,1024]{1,0:T(8,128)(2,1)S(1)} %collective-permute-done.3.refs_3_), channel_id=1, source_target_pairs={{0,3},{1,2},{4,1},{5,0},{8,5},{9,4},{12,9},{13,8},{14,13},{15,12},... | collective-permute-start | bytes 393224 | tf_op jit(solution)/shard_map/ppermute | solution.py:39
  34.3 24.1 %copy-start.3 = (bf16[8,4096]{1,0:T(8,128)(2,1)S(1)}, bf16[8,4096]{1,0:T(8,128)(2,1)}, u32[]{:S(2)}) copy-start(bf16[8,4096]{1,0:T(8,128)(2,1)} %queries.1) | copy-start | bytes 196612
  34.3 1.4 %collective-permute-start.15 = (f32[256,128]{1,0:T(8,128)S(1)}, f32[256,128]{1,0:T(8,128)S(1)}, u32[]{:S(2)}, u32[]{:S(2)}) collective-permute-start(f32[256,128]{1,0:T(8,128)S(1)} %shard_map.68), channel_id=1, source_target_pairs={{0,1},{1,0},{2,3},{3,2},{4,5},{5,4},{6,7},{7,6},{8,9},{9,8},{10,11... | collective-permute-start | bytes 393224 | tf_op jit(solution)/shard_map/ppermute | solution.py:43

commit v25 on v20

--- a/solution.py
+++ b/solution.py
@@ -68,7 +68,8 @@
         copy.wait()
 
 
-def chunk_kernel(in_rows, out_rows, first, second, sems):
+def start_kernel(chips, act, grad, in_rows, out_rows, first, second, send, sems, send_sems):
+    core = lax.axis_index("dp") & 1
     a_width = in_rows.shape[1]
     cut = first.shape[1]
     pairs = [
@@ -76,46 +77,28 @@
         (out_rows.at[:, pl.ds(0, cut - a_width)], first.at[:, pl.ds(a_width, cut - a_width)]),
         (out_rows.at[:, pl.ds(cut - a_width, second.shape[1])], second),
     ]
-    run_copies([pltpu.make_async_copy(*pair, sems.at[i]) for i, pair in enumerate(pairs)])
-
-
-def chunks_of(in_rows, out_rows):
+    copies = [pltpu.make_async_copy(*pair, sems.at[i]) for i, pair in enumerate(pairs)]
+    for chip in range(chips):
+        copies += column_copies(chip, 1 - core, act, grad, send.at[chip], send_sems.at[chip], chips)
+    run_copies(copies)
+
+
+def start(act, grad, in_rows, out_rows, chips):
+    rows = act.shape[0]
     rank, width = in_rows.shape[0], in_rows.shape[1] + out_rows.shape[1]
     cut = width // 256 * 128
+    shapes = (rank, cut), (rank, width - cut), (chips, rows, width)
     return pl.pallas_call(
-        chunk_kernel,
-        out_shape=[pltpu.VMEM((rank, w), in_rows.dtype) for w in (cut, width - cut)],
-        in_specs=[HBM] * 2,
-        out_specs=[VMEM] * 2,
-        scratch_shapes=[pltpu.SemaphoreType.DMA((3,))],
+        functools.partial(start_kernel, chips),
+        out_shape=[pltpu.VMEM(shape, act.dtype) for shape in shapes],
+        in_specs=[HBM] * 4,
+        out_specs=[VMEM] * 3,
+        scratch_shapes=[pltpu.SemaphoreType.DMA((3,)), pltpu.SemaphoreType.DMA((chips, 2))],
         compiler_params=pltpu.CompilerParams(vmem_limit_bytes=16 * 2**20),
         cost_estimate=pl.CostEstimate(
-            flops=0, bytes_accessed=4 * rank * width, transcendentals=0
+            flops=0, bytes_accessed=4 * (rank + chips * rows) * width, transcendentals=0
         ),
-    )(*held(pltpu.HBM, in_rows, out_rows))
-
-
-def pack_kernel(chips, act, grad, send, sems):
-    core = lax.axis_index("dp") & 1
-    copies = []
-    for chip in range(chips):
-        copies += column_copies(chip, 1 - core, act, grad, send.at[chip], sems.at[chip], chips)
-    run_copies(copies)
-
-
-def pack(act, grad, chips):
-    rows, width = act.shape[0], (act.shape[1] + grad.shape[1]) // (2 * chips)
-    return pl.pallas_call(
-        functools.partial(pack_kernel, chips),
-        out_shape=pltpu.VMEM((chips, rows, width), act.dtype),
-        in_specs=[HBM] * 2,
-        out_specs=VMEM,
-        scratch_shapes=[pltpu.SemaphoreType.DMA((chips, 2))],
-        compiler_params=pltpu.CompilerParams(vmem_limit_bytes=16 * 2**20),
-        cost_estimate=pl.CostEstimate(
-            flops=0, bytes_accessed=4 * chips * rows * width, transcendentals=0
-        ),
-    )(*held(pltpu.HBM, act, grad))
+    )(*held(pltpu.HBM, act, grad, in_rows, out_rows))
 
 
 def project_kernel(chips, items, a_width, cut, carry, act, grad, *refs):
@@ -208,8 +191,8 @@
     chips = n // 2
     split = LEN // rows
 
-    own = list(chunks_of(in_basis.T, out_basis.T))
-    theirs = swap(pack(activations, out_grads, chips), 1, n)
+    *own, send = start(activations, out_grads, in_basis.T, out_basis.T, chips)
+    theirs = swap(send, 1, n)
     run = functools.partial(project, a_width=a_width, cut=own[0].shape[1])
     mine = activations, out_grads
     last = chips // 2 - 1
@@ -217,7 +200,7 @@
     for i in range(last):
         if i == 1:
             total = run(mine, [(0, 0, 0), (0, 1, 0)], own, hide=HIDE)
-            total, up[i][0] = lax.optimization_barrier((total, up[i][0]))
+            total, up[i][1] = lax.optimization_barrier((total, up[i][1]))
         up.append([ring(x, 1, chips) for x in up[-1]])
         down.append([ring(x, -1, chips) for x in down[-1]])
     far = (ring(up[last][0], 1, chips), ring(down[last][1], -1, chips))

time: 57.6 us -> 56.2 us (0.976)
  Pallas kernels: 8.71 us -> 7.04 us
    pallas_call x2 -> x1, Pallas kernels: 4.4 us -> 2.74 us  [start(): pl.pallas_call(functools.partial(start_kernel, chips), out_shape=[pltpu.V...]
  transfers between devices with their start and end apart: 16 -> 16, of which waited for: 8 -> 8; matrix products, arithmetic and copies ran while one was open for 0% -> 0% of each run, Pallas kernels for 11% -> 6%
where the time goes in v25:
time: 56.2 us; the launch traced here: 56 us
  blocking collectives  21.9 us (39%)
  starting transfers between devices  17.1 us (30%)
  waiting for transfers between devices  8.75 us (16%)
  Pallas kernels  7.04 us (13%)
  matrix products  0.89 us (2%)
    all_to_all x2, blocking collectives, to_all(): lax.all_to_all(copies, 'dp', 0, 0, axis_index_groups=groups, tiled=True)  21.9 us
    ppermute x14, starting transfers between devices, ring(): return lax.ppermute(x, 'dp', pairs)  16.1 us
    ppermute x14, waiting for transfers between devices, ring(): return lax.ppermute(x, 'dp', pairs)  7.76 us
    pallas_call x5, Pallas kernels, project(): pl.pallas_call(functools.partial(project_kernel, chips, items, a_width, c...  3.57 us
    pallas_call x1, Pallas kernels, start(): pl.pallas_call(functools.partial(start_kernel, chips), out_shape=[pltpu.V...  2.74 us
  transfers between devices with their start and end apart: 16, of which 8 were waited for; matrix products, arithmetic and copies ran while one was open for 0% of the time, Pallas kernels for 6%

profile of v25, /device:TPU:0, one launch (start us, length us, event | category | flops | bytes accessed | tf_op | source)
XLA Modules:
  0.0 56.0 jit_solution(14062448651233950646)
XLA Ops:
  0.0 2.7 %shard_map.64 = (bf16[64,1152]{1,0:T(8,128)(2,1)S(1)}, bf16[64,1152]{1,0:T(8,128)(2,1)S(1)}, bf16[8,128,2304]{2,1,0:T(8,128)(2,1)S(1)}) custom-call(bf16[128,8192]{1,0:T(8,128)(2,1)} %act.11, bf16[128,28672]{1,0:T(8,128)(2,1)} %grad.11, bf16[64,512]{1,0:T(8,128)(2,1)} %bitcast.12, bf16[64,1792]{1,0:T(8,128)(2,1)} %bitcast.11), custom_call_target="tpu_custom_call" | custom-call | bytes 10027008 | tf_op jit(solution)/shard_map/pallas_call | solution.py:91
  2.8 2.5 %collective-permute-start.1 = (bf16[64,1152]{1,0:T(8,128)(2,1)S(1)}, bf16[64,1152]{1,0:T(8,128)(2,1)S(1)}, u32[]{:S(2)}, u32[]{:S(2)}) collective-permute-start(bf16[64,1152]{1,0:T(8,128)(2,1)S(1)} %get-tuple-element.11.refs_1_.refs_2_), channel_id=1, source_target_pairs={{0,3},{1,2},{4,1},{5,0},{8,5},{9,4},{12,9},{13,8},{14,13},{15,12},... | collective-permute-start | bytes 442376 | tf_op jit(solution)/shard_map/ppermute | solution.py:40
  5.4 1.9 %collective-permute-start.9 = (bf16[64,1152]{1,0:T(8,128)(2,1)S(1)}, bf16[64,1152]{1,0:T(8,128)(2,1)S(1)}, u32[]{:S(2)}, u32[]{:S(2)}) collective-permute-start(bf16[64,1152]{1,0:T(8,128)(2,1)S(1)} %get-tuple-element.11.refs_1_.refs_2_), channel_id=1, source_target_pairs={{0,5},{1,4},{4,9},{5,8},{8,13},{9,12},{12,15},{13,14},{14,11},{15,... | collective-permute-start | bytes 442376 | tf_op jit(solution)/shard_map/ppermute | solution.py:40
  7.8 1.7 %collective-permute-done.1.refs_6_ = bf16[64,1152]{1,0:T(8,128)(2,1)S(1)} collective-permute-done((bf16[64,1152]{1,0:T(8,128)(2,1)S(1)}, bf16[64,1152]{1,0:T(8,128)(2,1)S(1)}, u32[]{:S(2)}, u32[]{:S(2)}) %collective-permute-start.1) | collective-permute-done | bytes 147488 | tf_op jit(solution)/shard_map/ppermute | solution.py:40
  9.5 2.2 %collective-permute-start.2 = (bf16[64,1152]{1,0:T(8,128)(2,1)S(1)}, bf16[64,1152]{1,0:T(8,128)(2,1)S(1)}, u32[]{:S(2)}, u32[]{:S(2)}) collective-permute-start(bf16[64,1152]{1,0:T(8,128)(2,1)S(1)} %collective-permute-done.1.refs_6_), channel_id=1, source_target_pairs={{0,3},{1,2},{4,1},{5,0},{8,5},{9,4},{12,9},{13,8},{14,13},{15,12},... | collective-permute-start | bytes 442376 | tf_op jit(solution)/shard_map/ppermute | solution.py:40
  12.2 1.7 %collective-permute-done.9.refs_4_ = bf16[64,1152]{1,0:T(8,128)(2,1)S(1)} collective-permute-done((bf16[64,1152]{1,0:T(8,128)(2,1)S(1)}, bf16[64,1152]{1,0:T(8,128)(2,1)S(1)}, u32[]{:S(2)}, u32[]{:S(2)}) %collective-permute-start.9) | collective-permute-done | bytes 147488 | tf_op jit(solution)/shard_map/ppermute | solution.py:40
  13.9 1.0 %collective-permute-start.10 = (bf16[64,1152]{1,0:T(8,128)(2,1)S(1)}, bf16[64,1152]{1,0:T(8,128)(2,1)S(1)}, u32[]{:S(2)}, u32[]{:S(2)}) collective-permute-start(bf16[64,1152]{1,0:T(8,128)(2,1)S(1)} %collective-permute-done.9.refs_4_), channel_id=1, source_target_pairs={{0,5},{1,4},{4,9},{5,8},{8,13},{9,12},{12,15},{13,14},{14,11},{15,... | collective-permute-start | bytes 442376 | tf_op jit(solution)/shard_map/ppermute | solution.py:40
  15.0 1.0 %collective-permute-start.13 = (bf16[64,1152]{1,0:T(8,128)(2,1)S(1)}, bf16[64,1152]{1,0:T(8,128)(2,1)S(1)}, u32[]{:S(2)}, u32[]{:S(2)}) collective-permute-start(bf16[64,1152]{1,0:T(8,128)(2,1)S(1)} %collective-permute-done.12.refs_5_), channel_id=1, source_target_pairs={{0,3},{1,2},{4,1},{5,0},{8,5},{9,4},{12,9},{13,8},{14,13},{15,12},... | collective-permute-start | bytes 442376 | tf_op jit(solution)/shard_map/ppermute | solution.py:40
  16.0 1.2 %collective-permute-done.6.refs_7_ = bf16[64,1152]{1,0:T(8,128)(2,1)S(1)} collective-permute-done((bf16[64,1152]{1,0:T(8,128)(2,1)S(1)}, bf16[64,1152]{1,0:T(8,128)(2,1)S(1)}, u32[]{:S(2)}, u32[]{:S(2)}) %collective-permute-start.6) | collective-permute-done | bytes 147488 | tf_op jit(solution)/shard_map/ppermute | solution.py:40
  17.2 1.0 %collective-permute-start.7 = (bf16[64,1152]{1,0:T(8,128)(2,1)S(1)}, bf16[64,1152]{1,0:T(8,128)(2,1)S(1)}, u32[]{:S(2)}, u32[]{:S(2)}) collective-permute-start(bf16[64,1152]{1,0:T(8,128)(2,1)S(1)} %collective-permute-done.6.refs_7_), channel_id=1, source_target_pairs={{0,5},{1,4},{4,9},{5,8},{8,13},{9,12},{12,15},{13,14},{14,11},{15,... | collective-permute-start | bytes 442376 | tf_op jit(solution)/shard_map/ppermute | solution.py:40
  18.2 1.6 %collective-permute-start.3 = (bf16[64,1152]{1,0:T(8,128)(2,1)S(1)}, bf16[64,1152]{1,0:T(8,128)(2,1)S(1)}, u32[]{:S(2)}, u32[]{:S(2)}) collective-permute-start(bf16[64,1152]{1,0:T(8,128)(2,1)S(1)} %collective-permute-done.2.refs_10_), channel_id=1, source_target_pairs={{0,3},{1,2},{4,1},{5,0},{8,5},{9,4},{12,9},{13,8},{14,13},{15,12},... | collective-permute-start | bytes 442376 | tf_op jit(solution)/shard_map/ppermute | solution.py:40
  20.4 0.9 %collective-permute-start.11 = (bf16[64,1152]{1,0:T(8,128)(2,1)S(1)}, bf16[64,1152]{1,0:T(8,128)(2,1)S(1)}, u32[]{:S(2)}, u32[]{:S(2)}) collective-permute-start(bf16[64,1152]{1,0:T(8,128)(2,1)S(1)} %collective-permute-done.10.refs_8_), channel_id=1, source_target_pairs={{0,5},{1,4},{4,9},{5,8},{8,13},{9,12},{12,15},{13,14},{14,11},{15,... | collective-permute-start | bytes 442376 | tf_op jit(solution)/shard_map/ppermute | solution.py:40
  21.3 0.9 %collective-permute-start.14 = (bf16[64,1152]{1,0:T(8,128)(2,1)S(1)}, bf16[64,1152]{1,0:T(8,128)(2,1)S(1)}, u32[]{:S(2)}, u32[]{:S(2)}) collective-permute-start(bf16[64,1152]{1,0:T(8,128)(2,1)S(1)} %collective-permute-done.13.refs_9_), channel_id=1, source_target_pairs={{0,3},{1,2},{4,1},{5,0},{8,5},{9,4},{12,9},{13,8},{14,13},{15,12},... | collective-permute-start | bytes 442376 | tf_op jit(solution)/shard_map/ppermute | solution.py:40
  22.2 1.3 %collective-permute-done.7.refs_1_ = bf16[64,1152]{1,0:T(8,128)(2,1)S(1)} collective-permute-done((bf16[64,1152]{1,0:T(8,128)(2,1)S(1)}, bf16[64,1152]{1,0:T(8,128)(2,1)S(1)}, u32[]{:S(2)}, u32[]{:S(2)}) %collective-permute-start.7) | collective-permute-done | bytes 147488 | tf_op jit(solution)/shard_map/ppermute | solution.py:40
  23.5 1.2 %collective-permute-start.8 = (bf16[64,1152]{1,0:T(8,128)(2,1)S(1)}, bf16[64,1152]{1,0:T(8,128)(2,1)S(1)}, u32[]{:S(2)}, u32[]{:S(2)}) collective-permute-start(bf16[64,1152]{1,0:T(8,128)(2,1)S(1)} %collective-permute-done.7.refs_1_), channel_id=1, source_target_pairs={{0,5},{1,4},{4,9},{5,8},{8,13},{9,12},{12,15},{13,14},{14,11},{15,... | collective-permute-start | bytes 442376 | tf_op jit(solution)/shard_map/ppermute | solution.py:40
  24.7 1.6 %collective-permute-start.4 = (bf16[64,1152]{1,0:T(8,128)(2,1)S(1)}, bf16[64,1152]{1,0:T(8,128)(2,1)S(1)}, u32[]{:S(2)}, u32[]{:S(2)}) collective-permute-start(bf16[64,1152]{1,0:T(8,128)(2,1)S(1)} %collective-permute-done.3.refs_4_), channel_id=1, source_target_pairs={{0,3},{1,2},{4,1},{5,0},{8,5},{9,4},{12,9},{13,8},{14,13},{15,12},... | collective-permute-start | bytes 442376 | tf_op jit(solution)/shard_map/ppermute | solution.py:40
  26.3 1.6 %shard_map.66.refs_5_ = f32[256,128]{1,0:T(8,128)S(1)} custom-call(bf16[128,8192]{1,0:T(8,128)(2,1)S(1)} %copy-done.2, bf16[128,28672]{1,0:T(8,128)(2,1)S(1)} %copy-done.1, bf16[8,128,2304]{2,1,0:T(8,128)(2,1)S(1)} %collective-permute-done.refs_0_, bf16[64,1152]{1,0:T(8,128)(2,1)S(1)} %get-tuple-element.12.refs_0_.refs_1_, ...), custom_call_target="tpu_custom_call" | custom-call | flops 377487360 | bytes 7372800 | tf_op jit(solution)/shard_map/pallas_call | solution.py:150
  27.9 0.8 %shard_map.67.refs_2_ = f32[256,128]{1,0:T(8,128)S(1)} custom-call(bf16[128,8192]{1,0:T(8,128)(2,1)S(1)} %copy-done.2, bf16[128,28672]{1,0:T(8,128)(2,1)S(1)} %copy-done.1, bf16[8,128,2304]{2,1,0:T(8,128)(2,1)S(1)} %collective-permute-done.refs_0_, bf16[64,1152]{1,0:T(8,128)(2,1)S(1)} %collective-permute-done.7.refs_1_, ...), custom_call_target="tpu_custom_call" | custom-call | flops 150994944 | bytes 2949120 | tf_op jit(solution)/shard_map/pallas_call | solution.py:150
  28.8 1.1 %collective-permute-done.8.refs_1_ = bf16[64,1152]{1,0:T(8,128)(2,1)S(1)} collective-permute-done((bf16[64,1152]{1,0:T(8,128)(2,1)S(1)}, bf16[64,1152]{1,0:T(8,128)(2,1)S(1)}, u32[]{:S(2)}, u32[]{:S(2)}) %collective-permute-start.8) | collective-permute-done | bytes 147488 | tf_op jit(solution)/shard_map/ppermute | solution.py:40
  31.3 1.0 %collective-permute-done.15 = f32[256,128]{1,0:T(8,128)S(1)} collective-permute-done((f32[256,128]{1,0:T(8,128)S(1)}, f32[256,128]{1,0:T(8,128)S(1)}, u32[]{:S(2)}, u32[]{:S(2)}) %collective-permute-start.15) | collective-permute-done | bytes 131104 | tf_op jit(solution)/shard_map/ppermute | solution.py:44
  32.7 12.8 %all_to_all.10 = f32[8,32,128]{2,1,0:T(8,128)S(1)} all-to-all(f32[8,32,128]{2,1,0:T(8,128)S(1)} %broadcast_in_dim.14), channel_id=1, replica_groups={{0,2,4,6,8,10,12,14},{1,3,5,7,9,11,13,15},{16,18,20,22,24,26,28,30},{17..., dimensions={0} | all-to-all | bytes 262144 | tf_op jit(solution)/shard_map/all_to_all | solution.py:184
  45.5 0.6 %convolution_convert_fusion = bf16[2,256]{1,0:T(2,128)(2,1)S(1)} fusion(bf16[256,4096]{1,0:T(8,128)(2,1)S(1)} %copy-done, bf16[1,2,32,128]{3,2,1,0:T(8,128)(2,1)S(1)} %bitcast.13), kind=kOutput, calls=%fused_computation.1 | convolution fusion | flops 4194816 | bytes 2114560 | tf_op jit(solution)/shard_map/dot_general | solution.py:24
  46.2 9.1 %all_to_all.11.conditioned = bf16[16,2,256]{2,1,0:T(2,128)(2,1)S(1)} all-to-all(bf16[16,2,256]{2,1,0:T(2,128)(2,1)S(1)} %broadcast_in_dim.15), channel_id=1, replica_groups={{0,1,2,3,4,5,6,7,8,9,10,11,12,13,14,15},{16,17,18,19,20,21,22,23,24,25,..., dimensions={0} | all-to-all | bytes 32768 | tf_op jit(solution)/shard_map/all_to_all | solution.py:184
  55.3 0.7 %shard_map.70 = f32[2,8]{1,0:T(2,128)} custom-call(bf16[16,2,256]{2,1,0:T(2,128)(2,1)S(1)} %all_to_all.11.conditioned, bf16[8,4096]{1,0:T(8,128)(2,1)S(1)} %copy-done.3), custom_call_target="tpu_custom_call" | custom-call | tf_op jit(solution)/shard_map/pallas_call | solution.py:173
  (33 shorter events, 3.6 us)
Async XLA Ops:
  0.0 45.5 %copy-start = (bf16[256,4096]{1,0:T(8,128)(2,1)S(1)}, bf16[256,4096]{1,0:T(8,128)(2,1)}, u32[]{:S(2)}) copy-start(bf16[256,4096]{1,0:T(8,128)(2,1)} %param.10) | copy-start | bytes 6291460
  0.0 11.9 %copy-start.1 = (bf16[128,28672]{1,0:T(8,128)(2,1)S(1)}, bf16[128,28672]{1,0:T(8,128)(2,1)}, u32[]{:S(2)}) copy-start(bf16[128,28672]{1,0:T(8,128)(2,1)} %grad.11) | copy-start | bytes 22020100
  0.0 11.9 %copy-start.2 = (bf16[128,8192]{1,0:T(8,128)(2,1)S(1)}, bf16[128,8192]{1,0:T(8,128)(2,1)}, u32[]{:S(2)}) copy-start(bf16[128,8192]{1,0:T(8,128)(2,1)} %act.11) | copy-start | bytes 6291460
  2.8 6.7 %collective-permute-start.1 = (bf16[64,1152]{1,0:T(8,128)(2,1)S(1)}, bf16[64,1152]{1,0:T(8,128)(2,1)S(1)}, u32[]{:S(2)}, u32[]{:S(2)}) collective-permute-start(bf16[64,1152]{1,0:T(8,128)(2,1)S(1)} %get-tuple-element.11.refs_1_.refs_2_), channel_id=1, source_target_pairs={{0,3},{1,2},{4,1},{5,0},{8,5},{9,4},{12,9},{13,8},{14,13},{15,12},... | collective-permute-start | bytes 442376 | tf_op jit(solution)/shard_map/ppermute | solution.py:40
  5.2 6.4 %collective-permute-start.5 = (bf16[64,1152]{1,0:T(8,128)(2,1)S(1)}, bf16[64,1152]{1,0:T(8,128)(2,1)S(1)}, u32[]{:S(2)}, u32[]{:S(2)}) collective-permute-start(bf16[64,1152]{1,0:T(8,128)(2,1)S(1)} %get-tuple-element.12.refs_0_.refs_1_), channel_id=1, source_target_pairs={{0,5},{1,4},{4,9},{5,8},{8,13},{9,12},{12,15},{13,14},{14,11},{15,... | collective-permute-start | bytes 442376 | tf_op jit(solution)/shard_map/ppermute | solution.py:40
  5.4 8.6 %collective-permute-start.9 = (bf16[64,1152]{1,0:T(8,128)(2,1)S(1)}, bf16[64,1152]{1,0:T(8,128)(2,1)S(1)}, u32[]{:S(2)}, u32[]{:S(2)}) collective-permute-start(bf16[64,1152]{1,0:T(8,128)(2,1)S(1)} %get-tuple-element.11.refs_1_.refs_2_), channel_id=1, source_target_pairs={{0,5},{1,4},{4,9},{5,8},{8,13},{9,12},{12,15},{13,14},{14,11},{15,... | collective-permute-start | bytes 442376 | tf_op jit(solution)/shard_map/ppermute | solution.py:40
  7.2 7.7 %collective-permute-start.12 = (bf16[64,1152]{1,0:T(8,128)(2,1)S(1)}, bf16[64,1152]{1,0:T(8,128)(2,1)S(1)}, u32[]{:S(2)}, u32[]{:S(2)}) collective-permute-start(bf16[64,1152]{1,0:T(8,128)(2,1)S(1)} %get-tuple-element.12.refs_0_.refs_1_), channel_id=1, source_target_pairs={{0,3},{1,2},{4,1},{5,0},{8,5},{9,4},{12,9},{13,8},{14,13},{15,12},... | collective-permute-start | bytes 442376 | tf_op jit(solution)/shard_map/ppermute | solution.py:40
  7.2 19.1 %collective-permute-start = (bf16[8,128,2304]{2,1,0:T(8,128)(2,1)S(1)}, bf16[8,128,2304]{2,1,0:T(8,128)(2,1)S(1)}, u32[]{:S(2)}, u32[]{:S(2)}) collective-permute-start(bf16[8,128,2304]{2,1,0:T(8,128)(2,1)S(1)} %get-tuple-element.10), channel_id=1, source_target_pairs={{0,1},{1,0},{2,3},{3,2},{4,5},{5,4},{6,7},{7,6},{8,9},{9,8},{10,11... | collective-permute-start | bytes 14155784 | tf_op jit(solution)/shard_map/ppermute | solution.py:44
  9.5 8.8 %collective-permute-start.2 = (bf16[64,1152]{1,0:T(8,128)(2,1)S(1)}, bf16[64,1152]{1,0:T(8,128)(2,1)S(1)}, u32[]{:S(2)}, u32[]{:S(2)}) collective-permute-start(bf16[64,1152]{1,0:T(8,128)(2,1)S(1)} %collective-permute-done.1.refs_6_), channel_id=1, source_target_pairs={{0,3},{1,2},{4,1},{5,0},{8,5},{9,4},{12,9},{13,8},{14,13},{15,12},... | collective-permute-start | bytes 442376 | tf_op jit(solution)/shard_map/ppermute | solution.py:40
  11.7 5.5 %collective-permute-start.6 = (bf16[64,1152]{1,0:T(8,128)(2,1)S(1)}, bf16[64,1152]{1,0:T(8,128)(2,1)S(1)}, u32[]{:S(2)}, u32[]{:S(2)}) collective-permute-start(bf16[64,1152]{1,0:T(8,128)(2,1)S(1)} %collective-permute-done.5.refs_3_), channel_id=1, source_target_pairs={{0,5},{1,4},{4,9},{5,8},{8,13},{9,12},{12,15},{13,14},{14,11},{15,... | collective-permute-start | bytes 442376 | tf_op jit(solution)/shard_map/ppermute | solution.py:40
  13.9 6.4 %collective-permute-start.10 = (bf16[64,1152]{1,0:T(8,128)(2,1)S(1)}, bf16[64,1152]{1,0:T(8,128)(2,1)S(1)}, u32[]{:S(2)}, u32[]{:S(2)}) collective-permute-start(bf16[64,1152]{1,0:T(8,128)(2,1)S(1)} %collective-permute-done.9.refs_4_), channel_id=1, source_target_pairs={{0,5},{1,4},{4,9},{5,8},{8,13},{9,12},{12,15},{13,14},{14,11},{15,... | collective-permute-start | bytes 442376 | tf_op jit(solution)/shard_map/ppermute | solution.py:40
  15.0 6.3 %collective-permute-start.13 = (bf16[64,1152]{1,0:T(8,128)(2,1)S(1)}, bf16[64,1152]{1,0:T(8,128)(2,1)S(1)}, u32[]{:S(2)}, u32[]{:S(2)}) collective-permute-start(bf16[64,1152]{1,0:T(8,128)(2,1)S(1)} %collective-permute-done.12.refs_5_), channel_id=1, source_target_pairs={{0,3},{1,2},{4,1},{5,0},{8,5},{9,4},{12,9},{13,8},{14,13},{15,12},... | collective-permute-start | bytes 442376 | tf_op jit(solution)/shard_map/ppermute | solution.py:40
  17.2 6.3 %collective-permute-start.7 = (bf16[64,1152]{1,0:T(8,128)(2,1)S(1)}, bf16[64,1152]{1,0:T(8,128)(2,1)S(1)}, u32[]{:S(2)}, u32[]{:S(2)}) collective-permute-start(bf16[64,1152]{1,0:T(8,128)(2,1)S(1)} %collective-permute-done.6.refs_7_), channel_id=1, source_target_pairs={{0,5},{1,4},{4,9},{5,8},{8,13},{9,12},{12,15},{13,14},{14,11},{15,... | collective-permute-start | bytes 442376 | tf_op jit(solution)/shard_map/ppermute | solution.py:40
  18.2 6.4 %collective-permute-start.3 = (bf16[64,1152]{1,0:T(8,128)(2,1)S(1)}, bf16[64,1152]{1,0:T(8,128)(2,1)S(1)}, u32[]{:S(2)}, u32[]{:S(2)}) collective-permute-start(bf16[64,1152]{1,0:T(8,128)(2,1)S(1)} %collective-permute-done.2.refs_10_), channel_id=1, source_target_pairs={{0,3},{1,2},{4,1},{5,0},{8,5},{9,4},{12,9},{13,8},{14,13},{15,12},... | collective-permute-start | bytes 442376 | tf_op jit(solution)/shard_map/ppermute | solution.py:40
  20.4 7.5 %collective-permute-start.11 = (bf16[64,1152]{1,0:T(8,128)(2,1)S(1)}, bf16[64,1152]{1,0:T(8,128)(2,1)S(1)}, u32[]{:S(2)}, u32[]{:S(2)}) collective-permute-start(bf16[64,1152]{1,0:T(8,128)(2,1)S(1)} %collective-permute-done.10.refs_8_), channel_id=1, source_target_pairs={{0,5},{1,4},{4,9},{5,8},{8,13},{9,12},{12,15},{13,14},{14,11},{15,... | collective-permute-start | bytes 442376 | tf_op jit(solution)/shard_map/ppermute | solution.py:40
  21.3 6.6 %collective-permute-start.14 = (bf16[64,1152]{1,0:T(8,128)(2,1)S(1)}, bf16[64,1152]{1,0:T(8,128)(2,1)S(1)}, u32[]{:S(2)}, u32[]{:S(2)}) collective-permute-start(bf16[64,1152]{1,0:T(8,128)(2,1)S(1)} %collective-permute-done.13.refs_9_), channel_id=1, source_target_pairs={{0,3},{1,2},{4,1},{5,0},{8,5},{9,4},{12,9},{13,8},{14,13},{15,12},... | collective-permute-start | bytes 442376 | tf_op jit(solution)/shard_map/ppermute | solution.py:40
  23.5 6.4 %collective-permute-start.8 = (bf16[64,1152]{1,0:T(8,128)(2,1)S(1)}, bf16[64,1152]{1,0:T(8,128)(2,1)S(1)}, u32[]{:S(2)}, u32[]{:S(2)}) collective-permute-start(bf16[64,1152]{1,0:T(8,128)(2,1)S(1)} %collective-permute-done.7.refs_1_), channel_id=1, source_target_pairs={{0,5},{1,4},{4,9},{5,8},{8,13},{9,12},{12,15},{13,14},{14,11},{15,... | collective-permute-start | bytes 442376 | tf_op jit(solution)/shard_map/ppermute | solution.py:40
  24.7 5.8 %collective-permute-start.4 = (bf16[64,1152]{1,0:T(8,128)(2,1)S(1)}, bf16[64,1152]{1,0:T(8,128)(2,1)S(1)}, u32[]{:S(2)}, u32[]{:S(2)}) collective-permute-start(bf16[64,1152]{1,0:T(8,128)(2,1)S(1)} %collective-permute-done.3.refs_4_), channel_id=1, source_target_pairs={{0,3},{1,2},{4,1},{5,0},{8,5},{9,4},{12,9},{13,8},{14,13},{15,12},... | collective-permute-start | bytes 442376 | tf_op jit(solution)/shard_map/ppermute | solution.py:40
  30.8 24.5 %copy-start.3 = (bf16[8,4096]{1,0:T(8,128)(2,1)S(1)}, bf16[8,4096]{1,0:T(8,128)(2,1)}, u32[]{:S(2)}) copy-start(bf16[8,4096]{1,0:T(8,128)(2,1)} %queries.1) | copy-start | bytes 196612
  30.8 1.5 %collective-permute-start.15 = (f32[256,128]{1,0:T(8,128)S(1)}, f32[256,128]{1,0:T(8,128)S(1)}, u32[]{:S(2)}, u32[]{:S(2)}) collective-permute-start(f32[256,128]{1,0:T(8,128)S(1)} %shard_map.69), channel_id=1, source_target_pairs={{0,1},{1,0},{2,3},{3,2},{4,5},{5,4},{6,7},{7,6},{8,9},{9,8},{10,11... | collective-permute-start | bytes 393224 | tf_op jit(solution)/shard_map/ppermute | solution.py:44

commit v26 on v20

--- a/solution.py
+++ b/solution.py
@@ -217,7 +217,7 @@
     for i in range(last):
         if i == 1:
             total = run(mine, [(0, 0, 0), (0, 1, 0)], own, hide=HIDE)
-            total, up[i][0] = lax.optimization_barrier((total, up[i][0]))
+            total, up[i][1] = lax.optimization_barrier((total, up[i][1]))
         up.append([ring(x, 1, chips) for x in up[-1]])
         down.append([ring(x, -1, chips) for x in down[-1]])
     far = (ring(up[last][0], 1, chips), ring(down[last][1], -1, chips))

time: 57.6 us -> 55.2 us (0.958)
  waiting for transfers between devices: 9.2 us -> 7.99 us
  starting transfers between devices: 16.8 us -> 15.9 us
    ppermute x14, waiting for transfers between devices: 7.96 us -> 6.76 us  [ring(): return lax.ppermute(x, 'dp', pairs)]
    ppermute x14, starting transfers between devices: 16 us -> 15.1 us  [ring(): return lax.ppermute(x, 'dp', pairs)]
  transfers between devices with their start and end apart: 16 -> 16, of which waited for: 8 -> 8; matrix products, arithmetic and copies ran while one was open for 0% -> 0% of each run, Pallas kernels for 11% -> 12%
where the time goes in v26:
time: 55.2 us; the launch traced here: 55 us
  blocking collectives  21.3 us (39%)
  starting transfers between devices  15.9 us (29%)
  Pallas kernels  8.68 us (16%)
  waiting for transfers between devices  7.99 us (14%)
  matrix products  0.89 us (2%)
    all_to_all x2, blocking collectives, to_all(): lax.all_to_all(copies, 'dp', 0, 0, axis_index_groups=groups, tiled=True)  21.3 us
    ppermute x14, starting transfers between devices, ring(): return lax.ppermute(x, 'dp', pairs)  15.1 us
    ppermute x14, waiting for transfers between devices, ring(): return lax.ppermute(x, 'dp', pairs)  6.76 us
    pallas_call x5, Pallas kernels, project(): pl.pallas_call(functools.partial(project_kernel, chips, items, a_width, c...  3.57 us
    pallas_call x1, Pallas kernels, pack(): pl.pallas_call(functools.partial(pack_kernel, chips), out_shape=pltpu.VME...  3.22 us
    ppermute x2, waiting for transfers between devices, swap(): return lax.ppermute(x, 'dp', [(i, i ^ bit) for i in range(n)])  1.23 us
    pallas_call x1, Pallas kernels, chunks_of(): pl.pallas_call(chunk_kernel, out_shape=[pltpu.VMEM((rank, w), in_rows.dty...  1.16 us
  transfers between devices with their start and end apart: 16, of which 8 were waited for; matrix products, arithmetic and copies ran while one was open for 0% of the time, Pallas kernels for 12%

profile of v26, /device:TPU:0, one launch (start us, length us, event | category | flops | bytes accessed | tf_op | source)
XLA Modules:
  0.0 55.0 jit_solution(7225981057312646406)
XLA Ops:
  0.0 1.2 %shard_map.65 = (bf16[64,1152]{1,0:T(8,128)(2,1)S(1)}, bf16[64,1152]{1,0:T(8,128)(2,1)S(1)}) custom-call(bf16[64,512]{1,0:T(8,128)(2,1)} %bitcast.15, bf16[64,1792]{1,0:T(8,128)(2,1)} %bitcast.13), custom_call_target="tpu_custom_call" | custom-call | bytes 589824 | tf_op jit(solution)/shard_map/pallas_call | solution.py:85
  1.2 2.5 %collective-permute-start.1 = (bf16[64,1152]{1,0:T(8,128)(2,1)S(1)}, bf16[64,1152]{1,0:T(8,128)(2,1)S(1)}, u32[]{:S(2)}, u32[]{:S(2)}) collective-permute-start(bf16[64,1152]{1,0:T(8,128)(2,1)S(1)} %get-tuple-element.9.refs_1_.refs_2_), channel_id=1, source_target_pairs={{0,3},{1,2},{4,1},{5,0},{8,5},{9,4},{12,9},{13,8},{14,13},{15,12},... | collective-permute-start | bytes 442376 | tf_op jit(solution)/shard_map/ppermute | solution.py:40
  3.8 1.9 %collective-permute-start.9 = (bf16[64,1152]{1,0:T(8,128)(2,1)S(1)}, bf16[64,1152]{1,0:T(8,128)(2,1)S(1)}, u32[]{:S(2)}, u32[]{:S(2)}) collective-permute-start(bf16[64,1152]{1,0:T(8,128)(2,1)S(1)} %get-tuple-element.9.refs_1_.refs_2_), channel_id=1, source_target_pairs={{0,5},{1,4},{4,9},{5,8},{8,13},{9,12},{12,15},{13,14},{14,11},{15,... | collective-permute-start | bytes 442376 | tf_op jit(solution)/shard_map/ppermute | solution.py:40
  5.6 3.2 %shard_map.64 = bf16[8,128,2304]{2,1,0:T(8,128)(2,1)S(1)} custom-call(bf16[128,8192]{1,0:T(8,128)(2,1)} %act.11, bf16[128,28672]{1,0:T(8,128)(2,1)} %grad.11), custom_call_target="tpu_custom_call" | custom-call | bytes 9437184 | tf_op jit(solution)/shard_map/pallas_call | solution.py:108
  9.5 1.2 %collective-permute-start.2 = (bf16[64,1152]{1,0:T(8,128)(2,1)S(1)}, bf16[64,1152]{1,0:T(8,128)(2,1)S(1)}, u32[]{:S(2)}, u32[]{:S(2)}) collective-permute-start(bf16[64,1152]{1,0:T(8,128)(2,1)S(1)} %collective-permute-done.1.refs_6_), channel_id=1, source_target_pairs={{0,3},{1,2},{4,1},{5,0},{8,5},{9,4},{12,9},{13,8},{14,13},{15,12},... | collective-permute-start | bytes 442376 | tf_op jit(solution)/shard_map/ppermute | solution.py:40
  12.3 1.0 %collective-permute-start.10 = (bf16[64,1152]{1,0:T(8,128)(2,1)S(1)}, bf16[64,1152]{1,0:T(8,128)(2,1)S(1)}, u32[]{:S(2)}, u32[]{:S(2)}) collective-permute-start(bf16[64,1152]{1,0:T(8,128)(2,1)S(1)} %collective-permute-done.9.refs_4_), channel_id=1, source_target_pairs={{0,5},{1,4},{4,9},{5,8},{8,13},{9,12},{12,15},{13,14},{14,11},{15,... | collective-permute-start | bytes 442376 | tf_op jit(solution)/shard_map/ppermute | solution.py:40
  13.4 1.0 %collective-permute-start.13 = (bf16[64,1152]{1,0:T(8,128)(2,1)S(1)}, bf16[64,1152]{1,0:T(8,128)(2,1)S(1)}, u32[]{:S(2)}, u32[]{:S(2)}) collective-permute-start(bf16[64,1152]{1,0:T(8,128)(2,1)S(1)} %collective-permute-done.12.refs_5_), channel_id=1, source_target_pairs={{0,3},{1,2},{4,1},{5,0},{8,5},{9,4},{12,9},{13,8},{14,13},{15,12},... | collective-permute-start | bytes 442376 | tf_op jit(solution)/shard_map/ppermute | solution.py:40
  14.4 1.9 %collective-permute-done.6.refs_7_ = bf16[64,1152]{1,0:T(8,128)(2,1)S(1)} collective-permute-done((bf16[64,1152]{1,0:T(8,128)(2,1)S(1)}, bf16[64,1152]{1,0:T(8,128)(2,1)S(1)}, u32[]{:S(2)}, u32[]{:S(2)}) %collective-permute-start.6) | collective-permute-done | bytes 147488 | tf_op jit(solution)/shard_map/ppermute | solution.py:40
  16.3 1.4 %collective-permute-start.7 = (bf16[64,1152]{1,0:T(8,128)(2,1)S(1)}, bf16[64,1152]{1,0:T(8,128)(2,1)S(1)}, u32[]{:S(2)}, u32[]{:S(2)}) collective-permute-start(bf16[64,1152]{1,0:T(8,128)(2,1)S(1)} %collective-permute-done.6.refs_7_), channel_id=1, source_target_pairs={{0,5},{1,4},{4,9},{5,8},{8,13},{9,12},{12,15},{13,14},{14,11},{15,... | collective-permute-start | bytes 442376 | tf_op jit(solution)/shard_map/ppermute | solution.py:40
  17.6 1.1 %collective-permute-start.3 = (bf16[64,1152]{1,0:T(8,128)(2,1)S(1)}, bf16[64,1152]{1,0:T(8,128)(2,1)S(1)}, u32[]{:S(2)}, u32[]{:S(2)}) collective-permute-start(bf16[64,1152]{1,0:T(8,128)(2,1)S(1)} %collective-permute-done.2.refs_10_), channel_id=1, source_target_pairs={{0,3},{1,2},{4,1},{5,0},{8,5},{9,4},{12,9},{13,8},{14,13},{15,12},... | collective-permute-start | bytes 442376 | tf_op jit(solution)/shard_map/ppermute | solution.py:40
  18.7 0.7 %collective-permute-done.10.refs_8_ = bf16[64,1152]{1,0:T(8,128)(2,1)S(1)} collective-permute-done((bf16[64,1152]{1,0:T(8,128)(2,1)S(1)}, bf16[64,1152]{1,0:T(8,128)(2,1)S(1)}, u32[]{:S(2)}, u32[]{:S(2)}) %collective-permute-start.10) | collective-permute-done | bytes 147488 | tf_op jit(solution)/shard_map/ppermute | solution.py:40
  19.4 0.9 %collective-permute-start.11 = (bf16[64,1152]{1,0:T(8,128)(2,1)S(1)}, bf16[64,1152]{1,0:T(8,128)(2,1)S(1)}, u32[]{:S(2)}, u32[]{:S(2)}) collective-permute-start(bf16[64,1152]{1,0:T(8,128)(2,1)S(1)} %collective-permute-done.10.refs_8_), channel_id=1, source_target_pairs={{0,5},{1,4},{4,9},{5,8},{8,13},{9,12},{12,15},{13,14},{14,11},{15,... | collective-permute-start | bytes 442376 | tf_op jit(solution)/shard_map/ppermute | solution.py:40
  20.3 0.9 %collective-permute-start.14 = (bf16[64,1152]{1,0:T(8,128)(2,1)S(1)}, bf16[64,1152]{1,0:T(8,128)(2,1)S(1)}, u32[]{:S(2)}, u32[]{:S(2)}) collective-permute-start(bf16[64,1152]{1,0:T(8,128)(2,1)S(1)} %collective-permute-done.13.refs_9_), channel_id=1, source_target_pairs={{0,3},{1,2},{4,1},{5,0},{8,5},{9,4},{12,9},{13,8},{14,13},{15,12},... | collective-permute-start | bytes 442376 | tf_op jit(solution)/shard_map/ppermute | solution.py:40
  21.2 1.3 %collective-permute-done.7.refs_1_ = bf16[64,1152]{1,0:T(8,128)(2,1)S(1)} collective-permute-done((bf16[64,1152]{1,0:T(8,128)(2,1)S(1)}, bf16[64,1152]{1,0:T(8,128)(2,1)S(1)}, u32[]{:S(2)}, u32[]{:S(2)}) %collective-permute-start.7) | collective-permute-done | bytes 147488 | tf_op jit(solution)/shard_map/ppermute | solution.py:40
  22.5 1.5 %collective-permute-start.8 = (bf16[64,1152]{1,0:T(8,128)(2,1)S(1)}, bf16[64,1152]{1,0:T(8,128)(2,1)S(1)}, u32[]{:S(2)}, u32[]{:S(2)}) collective-permute-start(bf16[64,1152]{1,0:T(8,128)(2,1)S(1)} %collective-permute-done.7.refs_1_), channel_id=1, source_target_pairs={{0,5},{1,4},{4,9},{5,8},{8,13},{9,12},{12,15},{13,14},{14,11},{15,... | collective-permute-start | bytes 442376 | tf_op jit(solution)/shard_map/ppermute | solution.py:40
  24.1 1.1 %collective-permute-start.4 = (bf16[64,1152]{1,0:T(8,128)(2,1)S(1)}, bf16[64,1152]{1,0:T(8,128)(2,1)S(1)}, u32[]{:S(2)}, u32[]{:S(2)}) collective-permute-start(bf16[64,1152]{1,0:T(8,128)(2,1)S(1)} %collective-permute-done.3.refs_4_), channel_id=1, source_target_pairs={{0,3},{1,2},{4,1},{5,0},{8,5},{9,4},{12,9},{13,8},{14,13},{15,12},... | collective-permute-start | bytes 442376 | tf_op jit(solution)/shard_map/ppermute | solution.py:40
  25.2 1.6 %shard_map.67.refs_5_ = f32[256,128]{1,0:T(8,128)S(1)} custom-call(bf16[128,8192]{1,0:T(8,128)(2,1)S(1)} %copy-done.1, bf16[128,28672]{1,0:T(8,128)(2,1)S(1)} %bitcast.12, bf16[8,128,2304]{2,1,0:T(8,128)(2,1)S(1)} %collective-permute-done.refs_0_, bf16[64,1152]{1,0:T(8,128)(2,1)S(1)} %get-tuple-element.10.refs_0_.refs_1_, ...), custom_call_target="tpu_custom_call" | custom-call | flops 377487360 | bytes 7372800 | tf_op jit(solution)/shard_map/pallas_call | solution.py:167
  26.9 0.8 %shard_map.68.refs_2_ = f32[256,128]{1,0:T(8,128)S(1)} custom-call(bf16[128,8192]{1,0:T(8,128)(2,1)S(1)} %copy-done.1, bf16[128,28672]{1,0:T(8,128)(2,1)S(1)} %bitcast.12, bf16[8,128,2304]{2,1,0:T(8,128)(2,1)S(1)} %collective-permute-done.refs_0_, bf16[64,1152]{1,0:T(8,128)(2,1)S(1)} %collective-permute-done.7.refs_1_, ...), custom_call_target="tpu_custom_call" | custom-call | flops 150994944 | bytes 2949120 | tf_op jit(solution)/shard_map/pallas_call | solution.py:167
  27.7 0.9 %collective-permute-done.8.refs_1_ = bf16[64,1152]{1,0:T(8,128)(2,1)S(1)} collective-permute-done((bf16[64,1152]{1,0:T(8,128)(2,1)S(1)}, bf16[64,1152]{1,0:T(8,128)(2,1)S(1)}, u32[]{:S(2)}, u32[]{:S(2)}) %collective-permute-start.8) | collective-permute-done | bytes 147488 | tf_op jit(solution)/shard_map/ppermute | solution.py:40
  29.1 1.0 %collective-permute-done.4.refs_1_ = bf16[64,1152]{1,0:T(8,128)(2,1)S(1)} collective-permute-done((bf16[64,1152]{1,0:T(8,128)(2,1)S(1)}, bf16[64,1152]{1,0:T(8,128)(2,1)S(1)}, u32[]{:S(2)}, u32[]{:S(2)}) %collective-permute-start.4) | collective-permute-done | bytes 147488 | tf_op jit(solution)/shard_map/ppermute | solution.py:40
  30.7 1.2 %collective-permute-done.15 = f32[256,128]{1,0:T(8,128)S(1)} collective-permute-done((f32[256,128]{1,0:T(8,128)S(1)}, f32[256,128]{1,0:T(8,128)S(1)}, u32[]{:S(2)}, u32[]{:S(2)}) %collective-permute-start.15) | collective-permute-done | bytes 131104 | tf_op jit(solution)/shard_map/ppermute | solution.py:44
  32.3 12.2 %all_to_all.10 = f32[8,32,128]{2,1,0:T(8,128)S(1)} all-to-all(f32[8,32,128]{2,1,0:T(8,128)S(1)} %broadcast_in_dim.14), channel_id=1, replica_groups={{0,2,4,6,8,10,12,14},{1,3,5,7,9,11,13,15},{16,18,20,22,24,26,28,30},{17..., dimensions={0} | all-to-all | bytes 262144 | tf_op jit(solution)/shard_map/all_to_all | solution.py:201
  45.2 9.1 %all_to_all.11.conditioned = bf16[16,2,256]{2,1,0:T(2,128)(2,1)S(1)} all-to-all(bf16[16,2,256]{2,1,0:T(2,128)(2,1)S(1)} %broadcast_in_dim.15), channel_id=1, replica_groups={{0,1,2,3,4,5,6,7,8,9,10,11,12,13,14,15},{16,17,18,19,20,21,22,23,24,25,..., dimensions={0} | all-to-all | bytes 32768 | tf_op jit(solution)/shard_map/all_to_all | solution.py:201
  54.3 0.7 %shard_map.71 = f32[2,8]{1,0:T(2,128)} custom-call(bf16[16,2,256]{2,1,0:T(2,128)(2,1)S(1)} %all_to_all.11.conditioned, bf16[8,4096]{1,0:T(8,128)(2,1)S(1)} %copy-done.2), custom_call_target="tpu_custom_call" | custom-call | tf_op jit(solution)/shard_map/pallas_call | solution.py:190
  (37 shorter events, 4.5 us)
Async XLA Ops:
  0.0 44.5 %copy-start = (bf16[256,4096]{1,0:T(8,128)(2,1)S(1)}, bf16[256,4096]{1,0:T(8,128)(2,1)}, u32[]{:S(2)}) copy-start(bf16[256,4096]{1,0:T(8,128)(2,1)} %param.10) | copy-start | bytes 6291460
  1.2 8.3 %collective-permute-start.1 = (bf16[64,1152]{1,0:T(8,128)(2,1)S(1)}, bf16[64,1152]{1,0:T(8,128)(2,1)S(1)}, u32[]{:S(2)}, u32[]{:S(2)}) collective-permute-start(bf16[64,1152]{1,0:T(8,128)(2,1)S(1)} %get-tuple-element.9.refs_1_.refs_2_), channel_id=1, source_target_pairs={{0,3},{1,2},{4,1},{5,0},{8,5},{9,4},{12,9},{13,8},{14,13},{15,12},... | collective-permute-start | bytes 442376 | tf_op jit(solution)/shard_map/ppermute | solution.py:40
  3.6 7.6 %slice-start = ((s8[7340032]{0:T(1024)(128)(4,1)}), s8[4194304]{0:T(1024)(128)(4,1)S(1)}, s32[]{:S(2)}) async-start(s8[7340032]{0:T(1024)(128)(4,1)} %bitcast.11), calls=%async_computation.2 | async-start | bytes 8388608
  3.6 7.6 %slice-start.1 = ((s8[7340032]{0:T(1024)(128)(4,1)}), s8[3145728]{0:T(1024)(128)(4,1)S(1)}, s32[]{:S(2)}) async-start(s8[7340032]{0:T(1024)(128)(4,1)} %bitcast.11), calls=%async_computation.3 | async-start | bytes 6291456
  3.6 7.6 %copy-start.1 = (bf16[128,8192]{1,0:T(8,128)(2,1)S(1)}, bf16[128,8192]{1,0:T(8,128)(2,1)}, u32[]{:S(2)}) copy-start(bf16[128,8192]{1,0:T(8,128)(2,1)} %act.11) | copy-start | bytes 6291460
  3.6 7.1 %collective-permute-start.5 = (bf16[64,1152]{1,0:T(8,128)(2,1)S(1)}, bf16[64,1152]{1,0:T(8,128)(2,1)S(1)}, u32[]{:S(2)}, u32[]{:S(2)}) collective-permute-start(bf16[64,1152]{1,0:T(8,128)(2,1)S(1)} %get-tuple-element.10.refs_0_.refs_1_), channel_id=1, source_target_pairs={{0,5},{1,4},{4,9},{5,8},{8,13},{9,12},{12,15},{13,14},{14,11},{15,... | collective-permute-start | bytes 442376 | tf_op jit(solution)/shard_map/ppermute | solution.py:40
  3.8 8.6 %collective-permute-start.9 = (bf16[64,1152]{1,0:T(8,128)(2,1)S(1)}, bf16[64,1152]{1,0:T(8,128)(2,1)S(1)}, u32[]{:S(2)}, u32[]{:S(2)}) collective-permute-start(bf16[64,1152]{1,0:T(8,128)(2,1)S(1)} %get-tuple-element.9.refs_1_.refs_2_), channel_id=1, source_target_pairs={{0,5},{1,4},{4,9},{5,8},{8,13},{9,12},{12,15},{13,14},{14,11},{15,... | collective-permute-start | bytes 442376 | tf_op jit(solution)/shard_map/ppermute | solution.py:40
  5.6 7.7 %collective-permute-start.12 = (bf16[64,1152]{1,0:T(8,128)(2,1)S(1)}, bf16[64,1152]{1,0:T(8,128)(2,1)S(1)}, u32[]{:S(2)}, u32[]{:S(2)}) collective-permute-start(bf16[64,1152]{1,0:T(8,128)(2,1)S(1)} %get-tuple-element.10.refs_0_.refs_1_), channel_id=1, source_target_pairs={{0,3},{1,2},{4,1},{5,0},{8,5},{9,4},{12,9},{13,8},{14,13},{15,12},... | collective-permute-start | bytes 442376 | tf_op jit(solution)/shard_map/ppermute | solution.py:40
  8.9 16.3 %collective-permute-start = (bf16[8,128,2304]{2,1,0:T(8,128)(2,1)S(1)}, bf16[8,128,2304]{2,1,0:T(8,128)(2,1)S(1)}, u32[]{:S(2)}, u32[]{:S(2)}) collective-permute-start(bf16[8,128,2304]{2,1,0:T(8,128)(2,1)S(1)} %shard_map.64), channel_id=1, source_target_pairs={{0,1},{1,0},{2,3},{3,2},{4,5},{5,4},{6,7},{7,6},{8,9},{9,8},{10,11... | collective-permute-start | bytes 14155784 | tf_op jit(solution)/shard_map/ppermute | solution.py:44
  9.5 8.1 %collective-permute-start.2 = (bf16[64,1152]{1,0:T(8,128)(2,1)S(1)}, bf16[64,1152]{1,0:T(8,128)(2,1)S(1)}, u32[]{:S(2)}, u32[]{:S(2)}) collective-permute-start(bf16[64,1152]{1,0:T(8,128)(2,1)S(1)} %collective-permute-done.1.refs_6_), channel_id=1, source_target_pairs={{0,3},{1,2},{4,1},{5,0},{8,5},{9,4},{12,9},{13,8},{14,13},{15,12},... | collective-permute-start | bytes 442376 | tf_op jit(solution)/shard_map/ppermute | solution.py:40
  10.7 5.6 %collective-permute-start.6 = (bf16[64,1152]{1,0:T(8,128)(2,1)S(1)}, bf16[64,1152]{1,0:T(8,128)(2,1)S(1)}, u32[]{:S(2)}, u32[]{:S(2)}) collective-permute-start(bf16[64,1152]{1,0:T(8,128)(2,1)S(1)} %collective-permute-done.5.refs_3_), channel_id=1, source_target_pairs={{0,5},{1,4},{4,9},{5,8},{8,13},{9,12},{12,15},{13,14},{14,11},{15,... | collective-permute-start | bytes 442376 | tf_op jit(solution)/shard_map/ppermute | solution.py:40
  12.3 7.1 %collective-permute-start.10 = (bf16[64,1152]{1,0:T(8,128)(2,1)S(1)}, bf16[64,1152]{1,0:T(8,128)(2,1)S(1)}, u32[]{:S(2)}, u32[]{:S(2)}) collective-permute-start(bf16[64,1152]{1,0:T(8,128)(2,1)S(1)} %collective-permute-done.9.refs_4_), channel_id=1, source_target_pairs={{0,5},{1,4},{4,9},{5,8},{8,13},{9,12},{12,15},{13,14},{14,11},{15,... | collective-permute-start | bytes 442376 | tf_op jit(solution)/shard_map/ppermute | solution.py:40
  13.4 6.9 %collective-permute-start.13 = (bf16[64,1152]{1,0:T(8,128)(2,1)S(1)}, bf16[64,1152]{1,0:T(8,128)(2,1)S(1)}, u32[]{:S(2)}, u32[]{:S(2)}) collective-permute-start(bf16[64,1152]{1,0:T(8,128)(2,1)S(1)} %collective-permute-done.12.refs_5_), channel_id=1, source_target_pairs={{0,3},{1,2},{4,1},{5,0},{8,5},{9,4},{12,9},{13,8},{14,13},{15,12},... | collective-permute-start | bytes 442376 | tf_op jit(solution)/shard_map/ppermute | solution.py:40
  16.3 6.2 %collective-permute-start.7 = (bf16[64,1152]{1,0:T(8,128)(2,1)S(1)}, bf16[64,1152]{1,0:T(8,128)(2,1)S(1)}, u32[]{:S(2)}, u32[]{:S(2)}) collective-permute-start(bf16[64,1152]{1,0:T(8,128)(2,1)S(1)} %collective-permute-done.6.refs_7_), channel_id=1, source_target_pairs={{0,5},{1,4},{4,9},{5,8},{8,13},{9,12},{12,15},{13,14},{14,11},{15,... | collective-permute-start | bytes 442376 | tf_op jit(solution)/shard_map/ppermute | solution.py:40
  17.6 6.4 %collective-permute-start.3 = (bf16[64,1152]{1,0:T(8,128)(2,1)S(1)}, bf16[64,1152]{1,0:T(8,128)(2,1)S(1)}, u32[]{:S(2)}, u32[]{:S(2)}) collective-permute-start(bf16[64,1152]{1,0:T(8,128)(2,1)S(1)} %collective-permute-done.2.refs_10_), channel_id=1, source_target_pairs={{0,3},{1,2},{4,1},{5,0},{8,5},{9,4},{12,9},{13,8},{14,13},{15,12},... | collective-permute-start | bytes 442376 | tf_op jit(solution)/shard_map/ppermute | solution.py:40
  19.4 7.3 %collective-permute-start.11 = (bf16[64,1152]{1,0:T(8,128)(2,1)S(1)}, bf16[64,1152]{1,0:T(8,128)(2,1)S(1)}, u32[]{:S(2)}, u32[]{:S(2)}) collective-permute-start(bf16[64,1152]{1,0:T(8,128)(2,1)S(1)} %collective-permute-done.10.refs_8_), channel_id=1, source_target_pairs={{0,5},{1,4},{4,9},{5,8},{8,13},{9,12},{12,15},{13,14},{14,11},{15,... | collective-permute-start | bytes 442376 | tf_op jit(solution)/shard_map/ppermute | solution.py:40
  20.3 6.6 %collective-permute-start.14 = (bf16[64,1152]{1,0:T(8,128)(2,1)S(1)}, bf16[64,1152]{1,0:T(8,128)(2,1)S(1)}, u32[]{:S(2)}, u32[]{:S(2)}) collective-permute-start(bf16[64,1152]{1,0:T(8,128)(2,1)S(1)} %collective-permute-done.13.refs_9_), channel_id=1, source_target_pairs={{0,3},{1,2},{4,1},{5,0},{8,5},{9,4},{12,9},{13,8},{14,13},{15,12},... | collective-permute-start | bytes 442376 | tf_op jit(solution)/shard_map/ppermute | solution.py:40
  22.5 6.2 %collective-permute-start.8 = (bf16[64,1152]{1,0:T(8,128)(2,1)S(1)}, bf16[64,1152]{1,0:T(8,128)(2,1)S(1)}, u32[]{:S(2)}, u32[]{:S(2)}) collective-permute-start(bf16[64,1152]{1,0:T(8,128)(2,1)S(1)} %collective-permute-done.7.refs_1_), channel_id=1, source_target_pairs={{0,5},{1,4},{4,9},{5,8},{8,13},{9,12},{12,15},{13,14},{14,11},{15,... | collective-permute-start | bytes 442376 | tf_op jit(solution)/shard_map/ppermute | solution.py:40
  24.1 6.1 %collective-permute-start.4 = (bf16[64,1152]{1,0:T(8,128)(2,1)S(1)}, bf16[64,1152]{1,0:T(8,128)(2,1)S(1)}, u32[]{:S(2)}, u32[]{:S(2)}) collective-permute-start(bf16[64,1152]{1,0:T(8,128)(2,1)S(1)} %collective-permute-done.3.refs_4_), channel_id=1, source_target_pairs={{0,3},{1,2},{4,1},{5,0},{8,5},{9,4},{12,9},{13,8},{14,13},{15,12},... | collective-permute-start | bytes 442376 | tf_op jit(solution)/shard_map/ppermute | solution.py:40
  30.5 23.8 %copy-start.2 = (bf16[8,4096]{1,0:T(8,128)(2,1)S(1)}, bf16[8,4096]{1,0:T(8,128)(2,1)}, u32[]{:S(2)}) copy-start(bf16[8,4096]{1,0:T(8,128)(2,1)} %queries.1) | copy-start | bytes 196612
  30.5 1.4 %collective-permute-start.15 = (f32[256,128]{1,0:T(8,128)S(1)}, f32[256,128]{1,0:T(8,128)S(1)}, u32[]{:S(2)}, u32[]{:S(2)}) collective-permute-start(f32[256,128]{1,0:T(8,128)S(1)} %shard_map.70), channel_id=1, source_target_pairs={{0,1},{1,0},{2,3},{3,2},{4,5},{5,4},{6,7},{7,6},{8,9},{9,8},{10,11... | collective-permute-start | bytes 393224 | tf_op jit(solution)/shard_map/ppermute | solution.py:44

commit v27 on v26

--- a/solution.py
+++ b/solution.py
@@ -236,9 +236,9 @@
     total = (total + jnp.concatenate([theirs[rows:], theirs[:rows]], axis=0)).astype(jnp.bfloat16)
 
     raw = dot(total[:, rank:], total[:, :rank], TN)
-    raw = (raw * (1.0 / math.sqrt(LEN))).reshape(-1, 128)
+    raw = (raw * (1.0 / math.sqrt(LEN))).astype(jnp.bfloat16).reshape(-1, 128)
     planes = [[2 * i + c for i in range(chips)] for c in range(2)]
-    raw = to_all(raw, planes)
+    raw = to_all(raw, planes).astype(jnp.float32)
     features = raw.reshape((-1, split // 2) + raw.shape[1:]).sum(axis=1)
     features = features.astype(jnp.bfloat16).reshape(-1, rank * rank)
 

time: 55.2 us -> 54.8 us (level)
  no operation moved by 1% of the time
where the time goes in v27:
time: 54.8 us; the launch traced here: 54.6 us
  blocking collectives  20.8 us (38%)
  starting transfers between devices  15.9 us (29%)
  Pallas kernels  8.68 us (16%)
  waiting for transfers between devices  7.99 us (15%)
  matrix products  0.89 us (2%)
    all_to_all x2, blocking collectives, to_all(): lax.all_to_all(copies, 'dp', 0, 0, axis_index_groups=groups, tiled=True)  20.8 us
    ppermute x14, starting transfers between devices, ring(): return lax.ppermute(x, 'dp', pairs)  15.1 us
    ppermute x14, waiting for transfers between devices, ring(): return lax.ppermute(x, 'dp', pairs)  6.76 us
    pallas_call x5, Pallas kernels, project(): pl.pallas_call(functools.partial(project_kernel, chips, items, a_width, c...  3.57 us
    pallas_call x1, Pallas kernels, pack(): pl.pallas_call(functools.partial(pack_kernel, chips), out_shape=pltpu.VME...  3.22 us
    ppermute x2, waiting for transfers between devices, swap(): return lax.ppermute(x, 'dp', [(i, i ^ bit) for i in range(n)])  1.23 us
    pallas_call x1, Pallas kernels, chunks_of(): pl.pallas_call(chunk_kernel, out_shape=[pltpu.VMEM((rank, w), in_rows.dty...  1.16 us
  transfers between devices with their start and end apart: 16, of which 8 were waited for; matrix products, arithmetic and copies ran while one was open for 0% of the time, Pallas kernels for 12%

profile of v27, /device:TPU:0, one launch (start us, length us, event | category | flops | bytes accessed | tf_op | source)
XLA Modules:
  0.0 54.6 jit_solution(16396520978743433945)
XLA Ops:
  0.0 1.2 %shard_map.65 = (bf16[64,1152]{1,0:T(8,128)(2,1)S(1)}, bf16[64,1152]{1,0:T(8,128)(2,1)S(1)}) custom-call(bf16[64,512]{1,0:T(8,128)(2,1)} %bitcast.13, bf16[64,1792]{1,0:T(8,128)(2,1)} %bitcast.11), custom_call_target="tpu_custom_call" | custom-call | bytes 589824 | tf_op jit(solution)/shard_map/pallas_call | solution.py:85
  1.2 2.5 %collective-permute-start.1 = (bf16[64,1152]{1,0:T(8,128)(2,1)S(1)}, bf16[64,1152]{1,0:T(8,128)(2,1)S(1)}, u32[]{:S(2)}, u32[]{:S(2)}) collective-permute-start(bf16[64,1152]{1,0:T(8,128)(2,1)S(1)} %get-tuple-element.9.refs_1_.refs_2_), channel_id=1, source_target_pairs={{0,3},{1,2},{4,1},{5,0},{8,5},{9,4},{12,9},{13,8},{14,13},{15,12},... | collective-permute-start | bytes 442376 | tf_op jit(solution)/shard_map/ppermute | solution.py:40
  3.8 1.9 %collective-permute-start.9 = (bf16[64,1152]{1,0:T(8,128)(2,1)S(1)}, bf16[64,1152]{1,0:T(8,128)(2,1)S(1)}, u32[]{:S(2)}, u32[]{:S(2)}) collective-permute-start(bf16[64,1152]{1,0:T(8,128)(2,1)S(1)} %get-tuple-element.9.refs_1_.refs_2_), channel_id=1, source_target_pairs={{0,5},{1,4},{4,9},{5,8},{8,13},{9,12},{12,15},{13,14},{14,11},{15,... | collective-permute-start | bytes 442376 | tf_op jit(solution)/shard_map/ppermute | solution.py:40
  5.6 3.2 %shard_map.64 = bf16[8,128,2304]{2,1,0:T(8,128)(2,1)S(1)} custom-call(bf16[128,8192]{1,0:T(8,128)(2,1)} %act.11, bf16[128,28672]{1,0:T(8,128)(2,1)} %grad.11), custom_call_target="tpu_custom_call" | custom-call | bytes 9437184 | tf_op jit(solution)/shard_map/pallas_call | solution.py:108
  9.5 1.2 %collective-permute-start.2 = (bf16[64,1152]{1,0:T(8,128)(2,1)S(1)}, bf16[64,1152]{1,0:T(8,128)(2,1)S(1)}, u32[]{:S(2)}, u32[]{:S(2)}) collective-permute-start(bf16[64,1152]{1,0:T(8,128)(2,1)S(1)} %collective-permute-done.1.refs_6_), channel_id=1, source_target_pairs={{0,3},{1,2},{4,1},{5,0},{8,5},{9,4},{12,9},{13,8},{14,13},{15,12},... | collective-permute-start | bytes 442376 | tf_op jit(solution)/shard_map/ppermute | solution.py:40
  12.3 1.0 %collective-permute-start.10 = (bf16[64,1152]{1,0:T(8,128)(2,1)S(1)}, bf16[64,1152]{1,0:T(8,128)(2,1)S(1)}, u32[]{:S(2)}, u32[]{:S(2)}) collective-permute-start(bf16[64,1152]{1,0:T(8,128)(2,1)S(1)} %collective-permute-done.9.refs_4_), channel_id=1, source_target_pairs={{0,5},{1,4},{4,9},{5,8},{8,13},{9,12},{12,15},{13,14},{14,11},{15,... | collective-permute-start | bytes 442376 | tf_op jit(solution)/shard_map/ppermute | solution.py:40
  13.4 1.0 %collective-permute-start.13 = (bf16[64,1152]{1,0:T(8,128)(2,1)S(1)}, bf16[64,1152]{1,0:T(8,128)(2,1)S(1)}, u32[]{:S(2)}, u32[]{:S(2)}) collective-permute-start(bf16[64,1152]{1,0:T(8,128)(2,1)S(1)} %collective-permute-done.12.refs_5_), channel_id=1, source_target_pairs={{0,3},{1,2},{4,1},{5,0},{8,5},{9,4},{12,9},{13,8},{14,13},{15,12},... | collective-permute-start | bytes 442376 | tf_op jit(solution)/shard_map/ppermute | solution.py:40
  14.4 1.9 %collective-permute-done.6.refs_7_ = bf16[64,1152]{1,0:T(8,128)(2,1)S(1)} collective-permute-done((bf16[64,1152]{1,0:T(8,128)(2,1)S(1)}, bf16[64,1152]{1,0:T(8,128)(2,1)S(1)}, u32[]{:S(2)}, u32[]{:S(2)}) %collective-permute-start.6) | collective-permute-done | bytes 147488 | tf_op jit(solution)/shard_map/ppermute | solution.py:40
  16.3 1.4 %collective-permute-start.7 = (bf16[64,1152]{1,0:T(8,128)(2,1)S(1)}, bf16[64,1152]{1,0:T(8,128)(2,1)S(1)}, u32[]{:S(2)}, u32[]{:S(2)}) collective-permute-start(bf16[64,1152]{1,0:T(8,128)(2,1)S(1)} %collective-permute-done.6.refs_7_), channel_id=1, source_target_pairs={{0,5},{1,4},{4,9},{5,8},{8,13},{9,12},{12,15},{13,14},{14,11},{15,... | collective-permute-start | bytes 442376 | tf_op jit(solution)/shard_map/ppermute | solution.py:40
  17.6 1.1 %collective-permute-start.3 = (bf16[64,1152]{1,0:T(8,128)(2,1)S(1)}, bf16[64,1152]{1,0:T(8,128)(2,1)S(1)}, u32[]{:S(2)}, u32[]{:S(2)}) collective-permute-start(bf16[64,1152]{1,0:T(8,128)(2,1)S(1)} %collective-permute-done.2.refs_10_), channel_id=1, source_target_pairs={{0,3},{1,2},{4,1},{5,0},{8,5},{9,4},{12,9},{13,8},{14,13},{15,12},... | collective-permute-start | bytes 442376 | tf_op jit(solution)/shard_map/ppermute | solution.py:40
  18.7 0.7 %collective-permute-done.10.refs_8_ = bf16[64,1152]{1,0:T(8,128)(2,1)S(1)} collective-permute-done((bf16[64,1152]{1,0:T(8,128)(2,1)S(1)}, bf16[64,1152]{1,0:T(8,128)(2,1)S(1)}, u32[]{:S(2)}, u32[]{:S(2)}) %collective-permute-start.10) | collective-permute-done | bytes 147488 | tf_op jit(solution)/shard_map/ppermute | solution.py:40
  19.4 0.9 %collective-permute-start.11 = (bf16[64,1152]{1,0:T(8,128)(2,1)S(1)}, bf16[64,1152]{1,0:T(8,128)(2,1)S(1)}, u32[]{:S(2)}, u32[]{:S(2)}) collective-permute-start(bf16[64,1152]{1,0:T(8,128)(2,1)S(1)} %collective-permute-done.10.refs_8_), channel_id=1, source_target_pairs={{0,5},{1,4},{4,9},{5,8},{8,13},{9,12},{12,15},{13,14},{14,11},{15,... | collective-permute-start | bytes 442376 | tf_op jit(solution)/shard_map/ppermute | solution.py:40
  20.3 0.9 %collective-permute-start.14 = (bf16[64,1152]{1,0:T(8,128)(2,1)S(1)}, bf16[64,1152]{1,0:T(8,128)(2,1)S(1)}, u32[]{:S(2)}, u32[]{:S(2)}) collective-permute-start(bf16[64,1152]{1,0:T(8,128)(2,1)S(1)} %collective-permute-done.13.refs_9_), channel_id=1, source_target_pairs={{0,3},{1,2},{4,1},{5,0},{8,5},{9,4},{12,9},{13,8},{14,13},{15,12},... | collective-permute-start | bytes 442376 | tf_op jit(solution)/shard_map/ppermute | solution.py:40
  21.2 1.3 %collective-permute-done.7.refs_1_ = bf16[64,1152]{1,0:T(8,128)(2,1)S(1)} collective-permute-done((bf16[64,1152]{1,0:T(8,128)(2,1)S(1)}, bf16[64,1152]{1,0:T(8,128)(2,1)S(1)}, u32[]{:S(2)}, u32[]{:S(2)}) %collective-permute-start.7) | collective-permute-done | bytes 147488 | tf_op jit(solution)/shard_map/ppermute | solution.py:40
  22.5 1.5 %collective-permute-start.8 = (bf16[64,1152]{1,0:T(8,128)(2,1)S(1)}, bf16[64,1152]{1,0:T(8,128)(2,1)S(1)}, u32[]{:S(2)}, u32[]{:S(2)}) collective-permute-start(bf16[64,1152]{1,0:T(8,128)(2,1)S(1)} %collective-permute-done.7.refs_1_), channel_id=1, source_target_pairs={{0,5},{1,4},{4,9},{5,8},{8,13},{9,12},{12,15},{13,14},{14,11},{15,... | collective-permute-start | bytes 442376 | tf_op jit(solution)/shard_map/ppermute | solution.py:40
  24.1 1.1 %collective-permute-start.4 = (bf16[64,1152]{1,0:T(8,128)(2,1)S(1)}, bf16[64,1152]{1,0:T(8,128)(2,1)S(1)}, u32[]{:S(2)}, u32[]{:S(2)}) collective-permute-start(bf16[64,1152]{1,0:T(8,128)(2,1)S(1)} %collective-permute-done.3.refs_4_), channel_id=1, source_target_pairs={{0,3},{1,2},{4,1},{5,0},{8,5},{9,4},{12,9},{13,8},{14,13},{15,12},... | collective-permute-start | bytes 442376 | tf_op jit(solution)/shard_map/ppermute | solution.py:40
  25.2 1.6 %shard_map.67.refs_5_ = f32[256,128]{1,0:T(8,128)S(1)} custom-call(bf16[128,8192]{1,0:T(8,128)(2,1)S(1)} %copy-done.1, bf16[128,28672]{1,0:T(8,128)(2,1)S(1)} %bitcast.10, bf16[8,128,2304]{2,1,0:T(8,128)(2,1)S(1)} %collective-permute-done.refs_0_, bf16[64,1152]{1,0:T(8,128)(2,1)S(1)} %get-tuple-element.10.refs_0_.refs_1_, ...), custom_call_target="tpu_custom_call" | custom-call | flops 377487360 | bytes 7372800 | tf_op jit(solution)/shard_map/pallas_call | solution.py:167
  26.9 0.8 %shard_map.68.refs_2_ = f32[256,128]{1,0:T(8,128)S(1)} custom-call(bf16[128,8192]{1,0:T(8,128)(2,1)S(1)} %copy-done.1, bf16[128,28672]{1,0:T(8,128)(2,1)S(1)} %bitcast.10, bf16[8,128,2304]{2,1,0:T(8,128)(2,1)S(1)} %collective-permute-done.refs_0_, bf16[64,1152]{1,0:T(8,128)(2,1)S(1)} %collective-permute-done.7.refs_1_, ...), custom_call_target="tpu_custom_call" | custom-call | flops 150994944 | bytes 2949120 | tf_op jit(solution)/shard_map/pallas_call | solution.py:167
  27.7 0.9 %collective-permute-done.8.refs_1_ = bf16[64,1152]{1,0:T(8,128)(2,1)S(1)} collective-permute-done((bf16[64,1152]{1,0:T(8,128)(2,1)S(1)}, bf16[64,1152]{1,0:T(8,128)(2,1)S(1)}, u32[]{:S(2)}, u32[]{:S(2)}) %collective-permute-start.8) | collective-permute-done | bytes 147488 | tf_op jit(solution)/shard_map/ppermute | solution.py:40
  29.1 1.0 %collective-permute-done.4.refs_1_ = bf16[64,1152]{1,0:T(8,128)(2,1)S(1)} collective-permute-done((bf16[64,1152]{1,0:T(8,128)(2,1)S(1)}, bf16[64,1152]{1,0:T(8,128)(2,1)S(1)}, u32[]{:S(2)}, u32[]{:S(2)}) %collective-permute-start.4) | collective-permute-done | bytes 147488 | tf_op jit(solution)/shard_map/ppermute | solution.py:40
  30.7 1.2 %collective-permute-done.15 = f32[256,128]{1,0:T(8,128)S(1)} collective-permute-done((f32[256,128]{1,0:T(8,128)S(1)}, f32[256,128]{1,0:T(8,128)S(1)}, u32[]{:S(2)}, u32[]{:S(2)}) %collective-permute-start.15) | collective-permute-done | bytes 131104 | tf_op jit(solution)/shard_map/ppermute | solution.py:44
  32.3 11.7 %all_to_all.10 = bf16[8,32,128]{2,1,0:T(8,128)(2,1)S(1)} all-to-all(bf16[8,32,128]{2,1,0:T(8,128)(2,1)S(1)} %broadcast_in_dim.14), channel_id=1, replica_groups={{0,2,4,6,8,10,12,14},{1,3,5,7,9,11,13,15},{16,18,20,22,24,26,28,30},{17..., dimensions={0} | all-to-all | bytes 131072 | tf_op jit(solution)/shard_map/all_to_all | solution.py:201
  44.8 9.1 %all_to_all.11.conditioned = bf16[16,2,256]{2,1,0:T(2,128)(2,1)S(1)} all-to-all(bf16[16,2,256]{2,1,0:T(2,128)(2,1)S(1)} %broadcast_in_dim.15), channel_id=1, replica_groups={{0,1,2,3,4,5,6,7,8,9,10,11,12,13,14,15},{16,17,18,19,20,21,22,23,24,25,..., dimensions={0} | all-to-all | bytes 32768 | tf_op jit(solution)/shard_map/all_to_all | solution.py:201
  53.8 0.7 %shard_map.71 = f32[2,8]{1,0:T(2,128)} custom-call(bf16[16,2,256]{2,1,0:T(2,128)(2,1)S(1)} %all_to_all.11.conditioned, bf16[8,4096]{1,0:T(8,128)(2,1)S(1)} %copy-done.2), custom_call_target="tpu_custom_call" | custom-call | tf_op jit(solution)/shard_map/pallas_call | solution.py:190
  (37 shorter events, 4.5 us)
Async XLA Ops:
  0.0 44.1 %copy-start = (bf16[256,4096]{1,0:T(8,128)(2,1)S(1)}, bf16[256,4096]{1,0:T(8,128)(2,1)}, u32[]{:S(2)}) copy-start(bf16[256,4096]{1,0:T(8,128)(2,1)} %param.10) | copy-start | bytes 6291460
  1.2 8.3 %collective-permute-start.1 = (bf16[64,1152]{1,0:T(8,128)(2,1)S(1)}, bf16[64,1152]{1,0:T(8,128)(2,1)S(1)}, u32[]{:S(2)}, u32[]{:S(2)}) collective-permute-start(bf16[64,1152]{1,0:T(8,128)(2,1)S(1)} %get-tuple-element.9.refs_1_.refs_2_), channel_id=1, source_target_pairs={{0,3},{1,2},{4,1},{5,0},{8,5},{9,4},{12,9},{13,8},{14,13},{15,12},... | collective-permute-start | bytes 442376 | tf_op jit(solution)/shard_map/ppermute | solution.py:40
  3.6 7.6 %slice-start = ((s8[7340032]{0:T(1024)(128)(4,1)}), s8[4194304]{0:T(1024)(128)(4,1)S(1)}, s32[]{:S(2)}) async-start(s8[7340032]{0:T(1024)(128)(4,1)} %bitcast.9), calls=%async_computation.2 | async-start | bytes 8388608
  3.6 7.6 %slice-start.1 = ((s8[7340032]{0:T(1024)(128)(4,1)}), s8[3145728]{0:T(1024)(128)(4,1)S(1)}, s32[]{:S(2)}) async-start(s8[7340032]{0:T(1024)(128)(4,1)} %bitcast.9), calls=%async_computation.3 | async-start | bytes 6291456
  3.6 7.6 %copy-start.1 = (bf16[128,8192]{1,0:T(8,128)(2,1)S(1)}, bf16[128,8192]{1,0:T(8,128)(2,1)}, u32[]{:S(2)}) copy-start(bf16[128,8192]{1,0:T(8,128)(2,1)} %act.11) | copy-start | bytes 6291460
  3.6 7.1 %collective-permute-start.5 = (bf16[64,1152]{1,0:T(8,128)(2,1)S(1)}, bf16[64,1152]{1,0:T(8,128)(2,1)S(1)}, u32[]{:S(2)}, u32[]{:S(2)}) collective-permute-start(bf16[64,1152]{1,0:T(8,128)(2,1)S(1)} %get-tuple-element.10.refs_0_.refs_1_), channel_id=1, source_target_pairs={{0,5},{1,4},{4,9},{5,8},{8,13},{9,12},{12,15},{13,14},{14,11},{15,... | collective-permute-start | bytes 442376 | tf_op jit(solution)/shard_map/ppermute | solution.py:40
  3.8 8.6 %collective-permute-start.9 = (bf16[64,1152]{1,0:T(8,128)(2,1)S(1)}, bf16[64,1152]{1,0:T(8,128)(2,1)S(1)}, u32[]{:S(2)}, u32[]{:S(2)}) collective-permute-start(bf16[64,1152]{1,0:T(8,128)(2,1)S(1)} %get-tuple-element.9.refs_1_.refs_2_), channel_id=1, source_target_pairs={{0,5},{1,4},{4,9},{5,8},{8,13},{9,12},{12,15},{13,14},{14,11},{15,... | collective-permute-start | bytes 442376 | tf_op jit(solution)/shard_map/ppermute | solution.py:40
  5.6 7.7 %collective-permute-start.12 = (bf16[64,1152]{1,0:T(8,128)(2,1)S(1)}, bf16[64,1152]{1,0:T(8,128)(2,1)S(1)}, u32[]{:S(2)}, u32[]{:S(2)}) collective-permute-start(bf16[64,1152]{1,0:T(8,128)(2,1)S(1)} %get-tuple-element.10.refs_0_.refs_1_), channel_id=1, source_target_pairs={{0,3},{1,2},{4,1},{5,0},{8,5},{9,4},{12,9},{13,8},{14,13},{15,12},... | collective-permute-start | bytes 442376 | tf_op jit(solution)/shard_map/ppermute | solution.py:40
  8.9 16.3 %collective-permute-start = (bf16[8,128,2304]{2,1,0:T(8,128)(2,1)S(1)}, bf16[8,128,2304]{2,1,0:T(8,128)(2,1)S(1)}, u32[]{:S(2)}, u32[]{:S(2)}) collective-permute-start(bf16[8,128,2304]{2,1,0:T(8,128)(2,1)S(1)} %shard_map.64), channel_id=1, source_target_pairs={{0,1},{1,0},{2,3},{3,2},{4,5},{5,4},{6,7},{7,6},{8,9},{9,8},{10,11... | collective-permute-start | bytes 14155784 | tf_op jit(solution)/shard_map/ppermute | solution.py:44
  9.5 8.1 %collective-permute-start.2 = (bf16[64,1152]{1,0:T(8,128)(2,1)S(1)}, bf16[64,1152]{1,0:T(8,128)(2,1)S(1)}, u32[]{:S(2)}, u32[]{:S(2)}) collective-permute-start(bf16[64,1152]{1,0:T(8,128)(2,1)S(1)} %collective-permute-done.1.refs_6_), channel_id=1, source_target_pairs={{0,3},{1,2},{4,1},{5,0},{8,5},{9,4},{12,9},{13,8},{14,13},{15,12},... | collective-permute-start | bytes 442376 | tf_op jit(solution)/shard_map/ppermute | solution.py:40
  10.7 5.6 %collective-permute-start.6 = (bf16[64,1152]{1,0:T(8,128)(2,1)S(1)}, bf16[64,1152]{1,0:T(8,128)(2,1)S(1)}, u32[]{:S(2)}, u32[]{:S(2)}) collective-permute-start(bf16[64,1152]{1,0:T(8,128)(2,1)S(1)} %collective-permute-done.5.refs_3_), channel_id=1, source_target_pairs={{0,5},{1,4},{4,9},{5,8},{8,13},{9,12},{12,15},{13,14},{14,11},{15,... | collective-permute-start | bytes 442376 | tf_op jit(solution)/shard_map/ppermute | solution.py:40
  12.3 7.1 %collective-permute-start.10 = (bf16[64,1152]{1,0:T(8,128)(2,1)S(1)}, bf16[64,1152]{1,0:T(8,128)(2,1)S(1)}, u32[]{:S(2)}, u32[]{:S(2)}) collective-permute-start(bf16[64,1152]{1,0:T(8,128)(2,1)S(1)} %collective-permute-done.9.refs_4_), channel_id=1, source_target_pairs={{0,5},{1,4},{4,9},{5,8},{8,13},{9,12},{12,15},{13,14},{14,11},{15,... | collective-permute-start | bytes 442376 | tf_op jit(solution)/shard_map/ppermute | solution.py:40
  13.4 6.9 %collective-permute-start.13 = (bf16[64,1152]{1,0:T(8,128)(2,1)S(1)}, bf16[64,1152]{1,0:T(8,128)(2,1)S(1)}, u32[]{:S(2)}, u32[]{:S(2)}) collective-permute-start(bf16[64,1152]{1,0:T(8,128)(2,1)S(1)} %collective-permute-done.12.refs_5_), channel_id=1, source_target_pairs={{0,3},{1,2},{4,1},{5,0},{8,5},{9,4},{12,9},{13,8},{14,13},{15,12},... | collective-permute-start | bytes 442376 | tf_op jit(solution)/shard_map/ppermute | solution.py:40
  16.3 6.2 %collective-permute-start.7 = (bf16[64,1152]{1,0:T(8,128)(2,1)S(1)}, bf16[64,1152]{1,0:T(8,128)(2,1)S(1)}, u32[]{:S(2)}, u32[]{:S(2)}) collective-permute-start(bf16[64,1152]{1,0:T(8,128)(2,1)S(1)} %collective-permute-done.6.refs_7_), channel_id=1, source_target_pairs={{0,5},{1,4},{4,9},{5,8},{8,13},{9,12},{12,15},{13,14},{14,11},{15,... | collective-permute-start | bytes 442376 | tf_op jit(solution)/shard_map/ppermute | solution.py:40
  17.6 6.4 %collective-permute-start.3 = (bf16[64,1152]{1,0:T(8,128)(2,1)S(1)}, bf16[64,1152]{1,0:T(8,128)(2,1)S(1)}, u32[]{:S(2)}, u32[]{:S(2)}) collective-permute-start(bf16[64,1152]{1,0:T(8,128)(2,1)S(1)} %collective-permute-done.2.refs_10_), channel_id=1, source_target_pairs={{0,3},{1,2},{4,1},{5,0},{8,5},{9,4},{12,9},{13,8},{14,13},{15,12},... | collective-permute-start | bytes 442376 | tf_op jit(solution)/shard_map/ppermute | solution.py:40
  19.4 7.3 %collective-permute-start.11 = (bf16[64,1152]{1,0:T(8,128)(2,1)S(1)}, bf16[64,1152]{1,0:T(8,128)(2,1)S(1)}, u32[]{:S(2)}, u32[]{:S(2)}) collective-permute-start(bf16[64,1152]{1,0:T(8,128)(2,1)S(1)} %collective-permute-done.10.refs_8_), channel_id=1, source_target_pairs={{0,5},{1,4},{4,9},{5,8},{8,13},{9,12},{12,15},{13,14},{14,11},{15,... | collective-permute-start | bytes 442376 | tf_op jit(solution)/shard_map/ppermute | solution.py:40
  20.3 6.6 %collective-permute-start.14 = (bf16[64,1152]{1,0:T(8,128)(2,1)S(1)}, bf16[64,1152]{1,0:T(8,128)(2,1)S(1)}, u32[]{:S(2)}, u32[]{:S(2)}) collective-permute-start(bf16[64,1152]{1,0:T(8,128)(2,1)S(1)} %collective-permute-done.13.refs_9_), channel_id=1, source_target_pairs={{0,3},{1,2},{4,1},{5,0},{8,5},{9,4},{12,9},{13,8},{14,13},{15,12},... | collective-permute-start | bytes 442376 | tf_op jit(solution)/shard_map/ppermute | solution.py:40
  22.5 6.2 %collective-permute-start.8 = (bf16[64,1152]{1,0:T(8,128)(2,1)S(1)}, bf16[64,1152]{1,0:T(8,128)(2,1)S(1)}, u32[]{:S(2)}, u32[]{:S(2)}) collective-permute-start(bf16[64,1152]{1,0:T(8,128)(2,1)S(1)} %collective-permute-done.7.refs_1_), channel_id=1, source_target_pairs={{0,5},{1,4},{4,9},{5,8},{8,13},{9,12},{12,15},{13,14},{14,11},{15,... | collective-permute-start | bytes 442376 | tf_op jit(solution)/shard_map/ppermute | solution.py:40
  24.1 6.1 %collective-permute-start.4 = (bf16[64,1152]{1,0:T(8,128)(2,1)S(1)}, bf16[64,1152]{1,0:T(8,128)(2,1)S(1)}, u32[]{:S(2)}, u32[]{:S(2)}) collective-permute-start(bf16[64,1152]{1,0:T(8,128)(2,1)S(1)} %collective-permute-done.3.refs_4_), channel_id=1, source_target_pairs={{0,3},{1,2},{4,1},{5,0},{8,5},{9,4},{12,9},{13,8},{14,13},{15,12},... | collective-permute-start | bytes 442376 | tf_op jit(solution)/shard_map/ppermute | solution.py:40
  30.5 23.4 %copy-start.2 = (bf16[8,4096]{1,0:T(8,128)(2,1)S(1)}, bf16[8,4096]{1,0:T(8,128)(2,1)}, u32[]{:S(2)}) copy-start(bf16[8,4096]{1,0:T(8,128)(2,1)} %queries.1) | copy-start | bytes 196612
  30.5 1.4 %collective-permute-start.15 = (f32[256,128]{1,0:T(8,128)S(1)}, f32[256,128]{1,0:T(8,128)S(1)}, u32[]{:S(2)}, u32[]{:S(2)}) collective-permute-start(f32[256,128]{1,0:T(8,128)S(1)} %shard_map.70), channel_id=1, source_target_pairs={{0,1},{1,0},{2,3},{3,2},{4,5},{5,4},{6,7},{7,6},{8,9},{9,8},{10,11... | collective-permute-start | bytes 393224 | tf_op jit(solution)/shard_map/ppermute | solution.py:44
